TPU v7x, 32 devices: a whole 2x2x4 slice. The times are simulated.
32 devices in a mesh: parts: 2 (over x), cl: 8 (over z, y), grp: 2 (over core).
Axes of the slice: x: 2, y: 2, z: 4, core: 2. Of those that a mesh axis runs over, the one named last changes fastest.
Arguments:
- embeddings: bfloat16 [32768, 768], P(('parts', 'cl', 'grp')), parts along dimension 0, may hold values from -8 to 8
- labels: int32 [32768], P(('parts', 'cl', 'grp')), parts along dimension 0, may hold values from 0 to 63, as said below
- owner_map: int32 [128], P('parts'), parts along dimension 0, may hold values from 0 to 7, as said below
Outputs:
- dup_log: float32 [32768], P(('parts', 'cl', 'grp')), parts along dimension 0
There are 2 independent parts, one for each index of `parts`. A program takes and returns all parts, laid end to end along the dimension named above; each array names one. Nothing has to cross between parts.
Inputs may be any that keep to these rules, and one draw needn't show every extreme that they name: `labels`: each aligned block of 1024 rows (the rows of one device) holds at most 256 rows of any one coarse cluster, and in every block exactly 256 rows belong to one common coarse cluster. `owner_map`: each coarse cluster holds exactly 8 fine clusters.
All inputs are finite; a program needn't handle non-finite values.
Results may differ from a plain program's by a relative error of at most 0.0003.
Values may be sent and summed in bfloat16 or wider, within the bound.
No kernel may reach another device: no remote copies, remote signals or barrier semaphores. Data moves between devices by JAX's collectives and lax.ppermute only.
A program may use at most 64 MiB of HBM per device.

v0:
```python
import jax
import jax.numpy as jnp
from jax import lax
from jax.sharding import PartitionSpec as P

SLOTS = 2048


temper = 0.2
neighbour_factor = 0.5
epsilon = 1e-06


def shifted(x, axis, by):
    size = lax.axis_size(axis)
    return lax.ppermute(x, axis, [(i, (i + by) % size) for i in range(size)])


def owners_of(row_labels, owner_map):
    clusters = jnp.arange(owner_map.shape[0], dtype=jnp.int32)
    matches = row_labels[:, None] == clusters[None, :]
    return jnp.sum(jnp.where(matches, owner_map[None, :], 0), axis=1)


def slot_of(row_owners, n_owner, capacity):
    onehot = (row_owners[:, None] == jnp.arange(n_owner, dtype=jnp.int32)[None, :]).astype(
        jnp.int32
    )
    running = jnp.cumsum(onehot, axis=0)
    ranked = jnp.sum(onehot * running, axis=1) - 1
    return row_owners * capacity + ranked


def fill_slots(unit_rows, row_labels, slots, total):
    count = slots.shape[0]
    source = jnp.zeros((total,), jnp.int32).at[slots].set(jnp.arange(count, dtype=jnp.int32))
    filled = jnp.zeros((total,), jnp.bool_).at[slots].set(True)
    packed = jnp.where(filled[:, None], unit_rows[source], jnp.zeros((), unit_rows.dtype))
    tagged = jnp.where(filled, row_labels[source], -1)
    return (packed, tagged)


def log_counts(rows_x, rows_lab, columns):
    total = rows_x.shape[0]
    block_rows = min(512, total)
    blocks_x = rows_x.reshape(total // block_rows, block_rows, rows_x.shape[1])
    blocks_lab = rows_lab.reshape(total // block_rows, block_rows)

    def one_block(pair):
        block_x, block_lab = pair
        totals = jnp.zeros((block_rows,), jnp.float32)
        for col_x, col_lab in columns:
            scores = lax.dot_general(
                block_x, col_x, (((1,), (1,)), ((), ())), preferred_element_type=jnp.float32
            )
            same = block_lab[:, None] == col_lab[None, :]
            both_live = (block_lab[:, None] >= 0) & (col_lab[None, :] >= 0)
            factor = jnp.where(both_live, jnp.where(same, 1.0, neighbour_factor), 0.0)
            totals = totals + jnp.sum(factor * jnp.exp((scores - 1.0) / temper), axis=1)
        return jnp.log(jnp.where(block_lab >= 0, totals, 1.0))

    return lax.map(one_block, (blocks_x, blocks_lab)).reshape(total)


def body(embeddings, labels, owner_map):
    values32 = embeddings.astype(jnp.float32)
    squares = jnp.sum(values32 * values32, axis=1, keepdims=True)
    unit_rows = (values32 * lax.rsqrt(squares + epsilon)).astype(jnp.bfloat16)
    n_owner = lax.axis_size("cl")
    capacity = SLOTS // n_owner
    width_e = embeddings.shape[1]
    own_slots = slot_of(owners_of(labels, owner_map), n_owner, capacity)
    packed, tagged = fill_slots(unit_rows, labels, own_slots, SLOTS)
    recv_x, recv_lab = (
        lax.all_to_all(
            packed.reshape(n_owner, capacity, width_e),
            "cl",
            split_axis=0,
            concat_axis=0,
            tiled=True,
        ),
        lax.all_to_all(
            tagged.reshape(n_owner, capacity), "cl", split_axis=0, concat_axis=0, tiled=True
        ),
    )
    mine_x = recv_x.reshape(SLOTS, width_e)
    mine_lab = recv_lab.reshape(SLOTS)
    columns = [(mine_x, mine_lab)]
    visiting = (mine_x, mine_lab)
    visiting = shifted((visiting[0], visiting[1]), "grp", 1)
    columns.append(visiting)
    results = log_counts(mine_x, mine_lab, columns)
    returned = lax.all_to_all(
        results.reshape(n_owner, capacity), "cl", split_axis=0, concat_axis=0, tiled=True
    )
    return returned.reshape(SLOTS)[own_slots]


def solution(mesh):
    return jax.shard_map(
        body,
        mesh=mesh,
        in_specs=(P(("parts", "cl", "grp"), None), P(("parts", "cl", "grp")), P("parts")),
        out_specs=P(("parts", "cl", "grp")),
        check_vma=False,
    )
```

profile of v0, /device:TPU:0, one launch (start us, length us, event | category | flops | bytes accessed | tf_op | source)
XLA Modules:
  0.0 175.9 jit_solution(7842063294439778321)
XLA Ops:
  0.0 0.8 select_reduce_fusion
  0.8 2.3 %reduce-window.6 = s32[8,8,128]{2,1,0:T(8,128)S(1)} reduce-window(s32[8,8,128]{2,1,0:T(8,128)S(1)} %fusion.11, s32[]{:T(128)} %constant.77.clone.1), window={size=1x1x128 pad=0_0x0_0x127_0}, to_apply=%region_1.2 | reduce-window | flops 1040384 | bytes 65540 | tf_op jit(solution)/shard_map/reduce-window
  3.1 0.3 slice_reduce_fusion
  3.4 0.2 reduce-window.9
  3.5 0.1 add_bitcast_fusion
  3.7 4.3 %scatter_custom_fusion.1 = s32[2048]{0:T(1024)S(1)} fusion(s32[1024]{0:T(1024)S(1)} %bitcast.75, s32[1024]{0:T(1024)S(1)} %iota.15, s32[]{:T(128)} %constant.77.clone.1), kind=kCustom, calls=%fused_computation.40 | custom fusion | bytes 8196 | tf_op jit(solution)/shard_map/scatter | solution.py:36
  8.0 1.8 %fusion.7 = f32[1024]{0:T(1024)S(1)} fusion(bf16[1024,768]{1,0:T(8,128)(2,1)} %param.5), kind=kLoop, calls=%fused_computation.21 | loop fusion | flops 2358272 | bytes 1576960 | tf_op jit(solution)/shard_map/reduce_sum | solution.py:67
  9.8 1.7 fusion.8
  11.6 4.3 %scatter_custom_fusion = pred[2048]{0:T(1024)(128)(4,1)S(1)} fusion(s32[1024]{0:T(1024)S(1)} %bitcast.76, pred[1024]{0:T(1024)(128)(4,1)S(1)} %broadcast.147, pred[]{:T(512)} %constant.79.clone.1), kind=kCustom, calls=%fused_computation.43 | custom fusion | bytes 2049 | tf_op jit(solution)/shard_map/scatter | solution.py:37
  15.9 9.4 %gather_fusion.1 = bf16[2048,768]{1,0:T(8,128)(2,1)} fusion(bf16[1024,768]{1,0:T(8,128)(2,1)S(1)} %fusion.8, s32[2048]{0:T(1024)S(1)} %fusion.12), kind=kCustom, calls=%fused_computation.1 | custom fusion | bytes 6299648 | tf_op jit(solution)/shard_map/gather | solution.py:38
  25.3 2.1 %broadcast_select_fusion = bf16[8,256,768]{2,1,0:T(8,128)(2,1)S(1)} fusion(bf16[8,256,768]{2,1,0:T(8,128)(2,1)} %bitcast.55, pred[8,256]{1,0:T(8,128)(4,1)S(1)} %broadcast_in_dim.101), kind=kLoop, calls=%fused_computation.23 | loop fusion | flops 1572864 | bytes 6293504 | tf_op jit(solution)/shard_map/jit(_where)/select_n | solution.py:38
  27.4 0.0 copy-start
  27.5 77.8 %all_to_all.26 = bf16[8,256,768]{2,1,0:T(8,128)(2,1)S(1)} all-to-all(bf16[8,256,768]{2,1,0:T(8,128)(2,1)S(1)} %broadcast_select_fusion), channel_id=1, replica_groups=mesh['parts'=2,'cl'=8,'grp'=2] {'cl'}, dimensions={0} | all-to-all | bytes 6291456 | tf_op jit(solution)/shard_map/all_to_all | solution.py:75
  105.2 0.0 collective-permute-start.1
  105.2 0.0 copy-done
  105.2 8.6 %gather_fusion = s32[2048]{0:T(1024)S(1)} fusion(s32[1024]{0:T(1024)S(1)} %copy-done, s32[2048]{0:T(1024)S(1)} %fusion.12), kind=kCustom, calls=%fused_computation | custom fusion | bytes 24576 | tf_op jit(solution)/shard_map/gather | solution.py:39
  113.8 9.9 %all_to_all.27 = s32[8,1,256]{2,1,0:T(1,128)S(1)} all-to-all(s32[8,1,256]{2,1,0:T(1,128)S(1)} %bitcast.72), channel_id=1, replica_groups=mesh['parts'=2,'cl'=8,'grp'=2] {'cl'}, dimensions={0} | all-to-all | bytes 16384 | tf_op jit(solution)/shard_map/all_to_all | solution.py:82
  123.7 0.0 collective-permute-start
  123.8 1.1 collective-permute-done
  124.9 0.0 collective-permute-done.1
  124.9 30.0 %while.13 = (s32[]{:T(128)}, f32[4,512]{1,0:T(4,128)S(1)}, s32[4,512]{1,0:T(4,128)S(1)}, s32[8,256]{1,0:T(8,128)S(1)}, bf16[4,512,768]{2,1,0:T(8,128)(2,1)S(1)},...) while((s32[]{:T(128)}, f32[4,512]{1,0:T(4,128)S(1)}, ...), condition=%wide.region_10.11_spmd, body=%wide.region_7.10_spmd.sunk | while | flops 3238007808 | bytes 7954041 | solution.py:62
  125.0 2.7 %multiply_reduce_fusion.4 = f32[512]{0:T(512)S(1)} fusion(bf16[2048,768]{1,0:T(8,128)(2,1)S(1)} %get-tuple-element.219, s32[2048]{0:T(1024)S(1)} %bitcast.63, s32[512]{0:T(512)S(1)} %bitcast.68, pred[2048]{0:T(1024)(128)(4,1)S(1)} %broadcast_compare_fusion.6, pred[512]{0:T(512)(128)(4,1)S(1)} %broadcast_compare_fusion.7, ...), kind=kOutput, calls=%fused_computation.6.clone.1 | convolution fusion | flops 1619000832 | bytes 3947012 | tf_op jit(solution)/shard_map/while/body/eval_jaxpr/dot_general | solution.py:53
  127.7 4.6 %multiply_reduce_fusion.5 = f32[512]{0:T(512)S(1)} fusion(bf16[2048,768]{1,0:T(8,128)(2,1)} %get-tuple-element.221, s32[2048]{0:T(1024)S(1)} %get-tuple-element.220, s32[512]{0:T(512)S(1)} %bitcast.69, pred[2048]{0:T(1024)(128)(4,1)S(1)} %broadcast_compare_fusion.8, pred[512]{0:T(512)(128)(4,1)S(1)} %broadcast_compare_fusion.7, ...), kind=kOutput, calls=%fused_computation.5.clone.1 | convolution fusion | flops 1619000832 | bytes 3947012 | tf_op jit(solution)/shard_map/while/body/eval_jaxpr/dot_general | solution.py:53
  132.4 0.1 dynamic_update_slice.9
  132.5 2.7 %multiply_reduce_fusion.4 = f32[512]{0:T(512)S(1)} fusion(bf16[2048,768]{1,0:T(8,128)(2,1)S(1)} %get-tuple-element.219, s32[2048]{0:T(1024)S(1)} %bitcast.63, s32[512]{0:T(512)S(1)} %bitcast.68, pred[2048]{0:T(1024)(128)(4,1)S(1)} %broadcast_compare_fusion.6, pred[512]{0:T(512)(128)(4,1)S(1)} %broadcast_compare_fusion.7, ...), kind=kOutput, calls=%fused_computation.6.clone.1 | convolution fusion | flops 1619000832 | bytes 3947012 | tf_op jit(solution)/shard_map/while/body/eval_jaxpr/dot_general | solution.py:53
  135.2 4.6 %multiply_reduce_fusion.5 = f32[512]{0:T(512)S(1)} fusion(bf16[2048,768]{1,0:T(8,128)(2,1)} %get-tuple-element.221, s32[2048]{0:T(1024)S(1)} %get-tuple-element.220, s32[512]{0:T(512)S(1)} %bitcast.69, pred[2048]{0:T(1024)(128)(4,1)S(1)} %broadcast_compare_fusion.8, pred[512]{0:T(512)(128)(4,1)S(1)} %broadcast_compare_fusion.7, ...), kind=kOutput, calls=%fused_computation.5.clone.1 | convolution fusion | flops 1619000832 | bytes 3947012 | tf_op jit(solution)/shard_map/while/body/eval_jaxpr/dot_general | solution.py:53
  139.9 0.1 dynamic_update_slice.9
  140.0 2.7 %multiply_reduce_fusion.4 = f32[512]{0:T(512)S(1)} fusion(bf16[2048,768]{1,0:T(8,128)(2,1)S(1)} %get-tuple-element.219, s32[2048]{0:T(1024)S(1)} %bitcast.63, s32[512]{0:T(512)S(1)} %bitcast.68, pred[2048]{0:T(1024)(128)(4,1)S(1)} %broadcast_compare_fusion.6, pred[512]{0:T(512)(128)(4,1)S(1)} %broadcast_compare_fusion.7, ...), kind=kOutput, calls=%fused_computation.6.clone.1 | convolution fusion | flops 1619000832 | bytes 3947012 | tf_op jit(solution)/shard_map/while/body/eval_jaxpr/dot_general | solution.py:53
  142.7 4.6 %multiply_reduce_fusion.5 = f32[512]{0:T(512)S(1)} fusion(bf16[2048,768]{1,0:T(8,128)(2,1)} %get-tuple-element.221, s32[2048]{0:T(1024)S(1)} %get-tuple-element.220, s32[512]{0:T(512)S(1)} %bitcast.69, pred[2048]{0:T(1024)(128)(4,1)S(1)} %broadcast_compare_fusion.8, pred[512]{0:T(512)(128)(4,1)S(1)} %broadcast_compare_fusion.7, ...), kind=kOutput, calls=%fused_computation.5.clone.1 | convolution fusion | flops 1619000832 | bytes 3947012 | tf_op jit(solution)/shard_map/while/body/eval_jaxpr/dot_general | solution.py:53
  147.4 0.1 dynamic_update_slice.9
  147.5 2.7 %multiply_reduce_fusion.4 = f32[512]{0:T(512)S(1)} fusion(bf16[2048,768]{1,0:T(8,128)(2,1)S(1)} %get-tuple-element.219, s32[2048]{0:T(1024)S(1)} %bitcast.63, s32[512]{0:T(512)S(1)} %bitcast.68, pred[2048]{0:T(1024)(128)(4,1)S(1)} %broadcast_compare_fusion.6, pred[512]{0:T(512)(128)(4,1)S(1)} %broadcast_compare_fusion.7, ...), kind=kOutput, calls=%fused_computation.6.clone.1 | convolution fusion | flops 1619000832 | bytes 3947012 | tf_op jit(solution)/shard_map/while/body/eval_jaxpr/dot_general | solution.py:53
  150.2 4.6 %multiply_reduce_fusion.5 = f32[512]{0:T(512)S(1)} fusion(bf16[2048,768]{1,0:T(8,128)(2,1)} %get-tuple-element.221, s32[2048]{0:T(1024)S(1)} %get-tuple-element.220, s32[512]{0:T(512)S(1)} %bitcast.69, pred[2048]{0:T(1024)(128)(4,1)S(1)} %broadcast_compare_fusion.8, pred[512]{0:T(512)(128)(4,1)S(1)} %broadcast_compare_fusion.7, ...), kind=kOutput, calls=%fused_computation.5.clone.1 | convolution fusion | flops 1619000832 | bytes 3947012 | tf_op jit(solution)/shard_map/while/body/eval_jaxpr/dot_general | solution.py:53
  154.9 0.1 dynamic_update_slice.9
  154.9 0.6 all_to_all.21
  155.5 3.3 %all-to-all-start.2 = ((f32[8,1,256]{2,1,0:T(1,128)}), f32[8,1,256]{2,1,0:T(1,128)S(1)}, u32[]{:S(2)}, u32[]{:S(2)}) async-start(f32[8,1,256]{2,1,0:T(1,128)} %all_to_all.21), calls=%async_computation.2 | async-start | bytes 16384 | tf_op jit(solution)/shard_map/all_to_all | solution.py:93
  158.9 6.4 %all-to-all-done.2 = f32[8,1,256]{2,1,0:T(1,128)S(1)} async-done(((f32[8,1,256]{2,1,0:T(1,128)}), f32[8,1,256]{2,1,0:T(1,128)S(1)}, u32[]{:S(2)}, u32[]{:S(2)}) %all-to-all-start.2) | async-done | bytes 8224 | tf_op jit(solution)/shard_map/all_to_all | solution.py:93
  165.3 10.5 %gather_fusion.2 = f32[1024]{0:T(1024)} fusion(f32[2048]{0:T(1024)S(1)} %bitcast.54, s32[1024]{0:T(1024)S(1)} %broadcast_clamp_fusion), kind=kCustom, calls=%fused_computation.2 | custom fusion | bytes 12288 | tf_op jit(solution)/shard_map/gather | solution.py:96
  (43 shorter events, 0.3 us)
Async XLA Ops:
  27.4 77.8 %copy-start = (s32[1024]{0:T(1024)S(1)}, s32[1024]{0:T(1024)}, u32[]{:S(2)}) copy-start(s32[1024]{0:T(1024)} %param.6) | copy-start | bytes 12292
  105.2 19.7 %collective-permute-start.1 = (bf16[2048,768]{1,0:T(8,128)(2,1)S(1)}, bf16[2048,768]{1,0:T(8,128)(2,1)}, u32[]{:S(2)}, u32[]{:S(2)}) collective-permute-start(bf16[2048,768]{1,0:T(8,128)(2,1)S(1)} %bitcast.56), channel_id=1, source_target_pairs={{0,1},{1,0},{2,3},{3,2},{4,5},{5,4},{6,7},{7,6},{8,9},{9,8},{10,11... | collective-permute-start | bytes 9437192 | tf_op jit(solution)/shard_map/ppermute | solution.py:16
  123.7 1.2 collective-permute-start
  155.5 9.8 %all-to-all-start.2 = ((f32[8,1,256]{2,1,0:T(1,128)}), f32[8,1,256]{2,1,0:T(1,128)S(1)}, u32[]{:S(2)}, u32[]{:S(2)}) async-start(f32[8,1,256]{2,1,0:T(1,128)} %all_to_all.21), calls=%async_computation.2 | async-start | bytes 16384 | tf_op jit(solution)/shard_map/all_to_all | solution.py:93
where the time goes:
time: 176 us
  blocking collectives  87.7 us (50%)
  local copies, waits for them, and re-layouts  38.3 us (22%)
  matrix products  29.3 us (17%)
  other arithmetic  9.19 us (5%)
  waiting for transfers between devices  7.56 us (4%)
  starting transfers between devices  3.34 us (2%)
    all_to_all x1, blocking collectives, body(): lax.all_to_all(packed.reshape(n_owner, capacity, width_e), 'cl', split_ax...  77.8 us
    dot_general x8, matrix products, one_block(): lax.dot_general(block_x, col_x, (((1,), (1,)), ((), ())), preferred_eleme...  29.3 us
    gather x1, local copies, waits for them, and re-layouts, body(): return returned.reshape(SLOTS)[own_slots]  10.5 us
    all_to_all x1, blocking collectives, body(): lax.all_to_all(tagged.reshape(n_owner, capacity), 'cl', split_axis=0, con...  9.9 us
    gather x1, local copies, waits for them, and re-layouts, fill_slots(): unit_rows[source]  9.38 us
    gather x1, local copies, waits for them, and re-layouts, fill_slots(): tagged = jnp.where(filled, row_labels[source], -1)  8.58 us
    all_to_all x1, waiting for transfers between devices, body(): lax.all_to_all(results.reshape(n_owner, capacity), 'cl', split_axis=0, co...  6.44 us
    scatter x1, local copies, waits for them, and re-layouts, fill_slots(): filled = jnp.zeros((total,), jnp.bool_).at[slots].set(True)  4.34 us
  transfers between devices with their start and end apart: 3, of which 2 were waited for; matrix products, arithmetic and copies ran while one was open for 5% of the time, Pallas kernels for 0%

commit v1 on v0

v1 whole, which is shorter than its diff:
```python
import functools
import math

import jax
import jax.numpy as jnp
from jax import lax
from jax.experimental import pallas as pl
from jax.experimental.pallas import tpu as pltpu
from jax.sharding import PartitionSpec as P

SLOTS = 2048

temper = 0.2
neighbour_factor = 0.5
epsilon = 1e-06

LANES = 128
SCALE = math.log2(math.e) / temper
NEIGHBOUR = math.log2(neighbour_factor)
DEAD = -1e30
VMEM_LIMIT = 48 * 1024 * 1024


def column_of(row):
    pieces = []
    for start in range(0, row.shape[1], LANES):
        width = min(LANES, row.shape[1] - start)
        shape = (width, width)
        diagonal = lax.broadcasted_iota(jnp.int32, shape, 0) == lax.broadcasted_iota(
            jnp.int32, shape, 1
        )
        piece = jnp.broadcast_to(row[:, start : start + width], shape)
        pieces.append(jnp.sum(jnp.where(diagonal, piece, 0.0), axis=1, keepdims=True))
    return jnp.concatenate(pieces, axis=0)


def row_of(column):
    n = column.shape[0]
    diagonal = lax.broadcasted_iota(jnp.int32, (n, n), 0) == lax.broadcasted_iota(
        jnp.int32, (n, n), 1
    )
    return jnp.sum(jnp.where(diagonal, column, 0.0), axis=0, keepdims=True)


def pack_kernel(n_owner, capacity, x_ref, lab_ref, map_ref, out_ref, pos_ref, cnt_ref, unit, pos_row):
    rows = x_ref.shape[0]
    n_fine = map_ref.shape[1]
    per_owner = n_fine // n_owner
    owner_row = map_ref[...].astype(jnp.float32)
    fine_row = lax.broadcasted_iota(jnp.int32, (1, n_fine), 1).astype(jnp.float32)
    key_row = owner_row * n_fine + fine_row
    key_col = column_of(key_row)
    sorted_col = jnp.sum(jnp.where(key_row < key_col, 1.0, 0.0), axis=1, keepdims=True)
    lab = lab_ref[...].astype(jnp.float32)
    lab_row = jnp.concatenate([lab[b : b + 1, :] for b in range(lab.shape[0])], axis=1)
    fine_col = lax.broadcasted_iota(jnp.int32, (n_fine, rows), 0).astype(jnp.float32)
    fine_id = jnp.sum(jnp.where(fine_col == lab_row, sorted_col, 0.0), axis=0, keepdims=True)
    counts_col = jnp.sum(jnp.where(fine_col == fine_id, 1.0, 0.0), axis=1, keepdims=True)
    cnt_ref[...] = row_of(counts_col).astype(jnp.int32)
    coarse = jnp.floor((fine_id + 0.5) * (1.0 / per_owner))
    before = jnp.sum(
        jnp.where(fine_col < coarse * per_owner, counts_col, 0.0), axis=0, keepdims=True
    )
    index = lax.broadcasted_iota(jnp.int32, (1, rows), 1).astype(jnp.float32)
    row_key = fine_id * rows + index
    rank = jnp.zeros((1, rows), jnp.float32)
    for start in range(0, rows, LANES):
        other = column_of(row_key[:, start : start + LANES])
        rank = rank + jnp.sum(jnp.where(other < row_key, 1.0, 0.0), axis=0, keepdims=True)
    pos = (coarse * capacity + rank - before).astype(jnp.int32)
    pos_row[...] = pos
    pos_ref[...] = jnp.concatenate(
        [pos[:, start : start + LANES] for start in range(0, rows, LANES)], axis=0
    )
    x = x_ref[...].astype(jnp.float32)
    squares = jnp.sum(x * x, axis=1, keepdims=True)
    unit[...] = (x * lax.rsqrt(squares + epsilon)).astype(jnp.bfloat16)

    step = 256

    @pl.loop(0, out_ref.shape[0] // step)
    def _(block):
        slot = lax.broadcasted_iota(jnp.int32, (step, rows), 0) + block * step
        chosen = jnp.where(slot == pos_row[...], 1.0, 0.0).astype(jnp.bfloat16)
        packed = jnp.dot(chosen, unit[...], preferred_element_type=jnp.float32)
        out_ref[pl.ds(pl.multiple_of(block * step, step), step), :] = packed.astype(jnp.bfloat16)


def pack(embeddings, labels, owner_map, n_owner, capacity):
    rows, width = embeddings.shape
    n_fine = owner_map.shape[0]
    total = n_owner * capacity
    vmem = pl.BlockSpec(memory_space=pltpu.VMEM)
    return pl.pallas_call(
        functools.partial(pack_kernel, n_owner, capacity),
        out_shape=(
            jax.ShapeDtypeStruct((total, width), jnp.bfloat16),
            jax.ShapeDtypeStruct((rows // LANES, LANES), jnp.int32),
            jax.ShapeDtypeStruct((1, n_fine), jnp.int32),
        ),
        in_specs=[vmem] * 3,
        out_specs=(vmem, vmem, vmem),
        scratch_shapes=[pltpu.VMEM((rows, width), jnp.bfloat16), pltpu.VMEM((1, rows), jnp.int32)],
        compiler_params=pltpu.CompilerParams(vmem_limit_bytes=VMEM_LIMIT),
    )(embeddings, labels.reshape(rows // LANES, LANES), owner_map.reshape(1, n_fine))


def counts_kernel(n_owner, capacity, cnt_ref, mine_ref, other_ref, out_ref, lab_lane, lab_sub, bias):
    total = mine_ref.shape[0]
    per_owner = cnt_ref.shape[1] // n_owner
    me = lax.axis_index("cl")
    grp = lax.axis_index("grp")
    n_grp = lax.axis_size("grp")
    for member in range(2):
        for source in range(n_owner):
            line = source * n_grp + lax.rem(grp + member, n_grp)
            edges = []
            edge = jnp.int32(0)
            for f in range(per_owner):
                edge = edge + cnt_ref[line, me * per_owner + f]
                edges.append(edge)
            down = lax.broadcasted_iota(jnp.int32, (capacity, LANES), 0)
            label = jnp.zeros((capacity, LANES), jnp.int32)
            for edge in edges:
                label = label + jnp.where(down >= edge, 1, 0)
            start = (member * n_owner + source) * capacity
            lab_sub[start : start + capacity, :] = label
            bias[start : start + capacity, :] = jnp.where(
                label < per_owner, NEIGHBOUR - SCALE, DEAD
            )
            if member == 0:
                across = lax.broadcasted_iota(jnp.int32, (1, capacity), 1)
                label = jnp.zeros((1, capacity), jnp.int32)
                for edge in edges:
                    label = label + jnp.where(across >= edge, 1, 0)
                lab_lane[:, source * capacity : (source + 1) * capacity] = jnp.where(
                    label < per_owner, label, -1
                )
    wide, deep = min(512, total), min(256, total)

    @pl.loop(0, total // wide)
    def _(block):
        columns = pl.ds(pl.multiple_of(block * wide, wide), wide)
        rows_i = mine_ref[columns, :]
        label_i = lab_lane[:, columns]

        def add(ref, offset):
            def step(j, acc):
                start = pl.multiple_of(j * deep, deep)
                scores = lax.dot_general(
                    ref[pl.ds(start, deep), :],
                    rows_i,
                    (((1,), (1,)), ((), ())),
                    preferred_element_type=jnp.float32,
                )
                place = pl.ds(pl.multiple_of(start + offset, deep), deep)
                label_j = lab_sub[place, :]
                bias_j = bias[place, :]
                repeat = wide // LANES
                label_j = jnp.concatenate([label_j] * repeat, axis=1)
                bias_j = jnp.concatenate([bias_j] * repeat, axis=1)
                shift = jnp.where(label_j == label_i, -SCALE, bias_j)
                terms = jnp.exp2(scores * SCALE + shift)
                return acc + jnp.sum(terms.reshape(deep // 8, 8, wide), axis=0)

            return step

        acc = jnp.zeros((8, wide), jnp.float32)
        acc = lax.fori_loop(0, total // deep, add(mine_ref, 0), acc, unroll=2)
        acc = lax.fori_loop(0, total // deep, add(other_ref, total), acc, unroll=2)
        totals = jnp.sum(acc, axis=0, keepdims=True)
        out_ref[:, columns] = jnp.log(jnp.where(label_i >= 0, totals, 1.0))


def log_counts(counts, mine, other, n_owner, capacity):
    total = mine.shape[0]
    vmem = pl.BlockSpec(memory_space=pltpu.VMEM)
    return pl.pallas_call(
        functools.partial(counts_kernel, n_owner, capacity),
        out_shape=jax.ShapeDtypeStruct((1, total), jnp.float32),
        in_specs=[pl.BlockSpec(memory_space=pltpu.SMEM), vmem, vmem],
        out_specs=vmem,
        scratch_shapes=[
            pltpu.VMEM((1, total), jnp.int32),
            pltpu.VMEM((2 * total, LANES), jnp.int32),
            pltpu.VMEM((2 * total, LANES), jnp.float32),
        ],
        compiler_params=pltpu.CompilerParams(vmem_limit_bytes=VMEM_LIMIT),
    )(counts, mine, other)


def unpack_kernel(values_ref, pos_ref, out_ref):
    pos = pos_ref[...]
    lane = lax.rem(pos, LANES)
    line = lax.div(pos, LANES)
    out = jnp.zeros(pos.shape, jnp.float32)
    for r in range(values_ref.shape[0]):
        table = jnp.broadcast_to(values_ref[r : r + 1, :], pos.shape)
        found = jnp.take_along_axis(table, lane, axis=1)
        out = jnp.where(line == r, found, out)
    out_ref[...] = out


def unpack(values, pos):
    vmem = pl.BlockSpec(memory_space=pltpu.VMEM)
    return pl.pallas_call(
        unpack_kernel,
        out_shape=jax.ShapeDtypeStruct(pos.shape, jnp.float32),
        in_specs=[vmem, vmem],
        out_specs=vmem,
    )(values.reshape(-1, LANES), pos)


def body(embeddings, labels, owner_map):
    n_owner = lax.axis_size("cl")
    capacity = SLOTS // n_owner
    rows, width = embeddings.shape
    packed, pos, counts = pack(embeddings, labels, owner_map, n_owner, capacity)
    counts = lax.all_gather(counts, ("cl", "grp"), tiled=True)
    mine = lax.all_to_all(
        packed.reshape(n_owner, capacity, width), "cl", split_axis=0, concat_axis=0, tiled=True
    ).reshape(SLOTS, width)
    other = lax.ppermute(mine, "grp", [(0, 1), (1, 0)])
    results = log_counts(counts, mine, other, n_owner, capacity)
    returned = lax.all_to_all(
        results.reshape(n_owner, capacity), "cl", split_axis=0, concat_axis=0, tiled=True
    )
    return unpack(returned.reshape(SLOTS), pos).reshape(rows)


def solution(mesh):
    return jax.shard_map(
        body,
        mesh=mesh,
        in_specs=(P(("parts", "cl", "grp"), None), P(("parts", "cl", "grp")), P("parts")),
        out_specs=P(("parts", "cl", "grp")),
        check_vma=False,
    )
```

time: 176 us -> 144 us (0.82)
  local copies, waits for them, and re-layouts: 38.3 us -> 4.97 us
  Pallas kernels: 0 us -> 32.3 us
  matrix products: 29.3 us -> 0 us
  blocking collectives: 87.7 us -> 107 us
  other arithmetic: 9.19 us -> 0 us
  waiting for transfers between devices: 7.56 us -> 0.01 us
  starting transfers between devices: 3.34 us -> 0.01 us
    pallas_call x0 -> x3, Pallas kernels: none -> 32.3 us  [the longest x1 25 us: log_counts(): pl.pallas_call(functools.partial(counts_kernel, n_owner, capacity), out_s...]
    dot_general x8 -> x0, matrix products: 29.3 us -> none  [one_block(): lax.dot_general(block_x, col_x, (((1,), (1,)), ((), ())), preferred_eleme...]
    gather x3 -> x0, local copies, waits for them, and re-layouts: 28.5 us -> none  [the longest x1 10.5 us: body(): return returned.reshape(SLOTS)[own_slots]]
    all_gather x0 -> x1, blocking collectives: none -> 19.3 us  [body(): counts = lax.all_gather(counts, ('cl', 'grp'), tiled=True)]
    scatter x2 -> x0, local copies, waits for them, and re-layouts: 8.66 us -> none  [the longest x1 4.34 us: fill_slots(): filled = jnp.zeros((total,), jnp.bool_).at[slots].set(True)]
    all_to_all x1 -> x0, waiting for transfers between devices: 6.44 us -> none  [body(): lax.all_to_all(results.reshape(n_owner, capacity), 'cl', split_axis=0, co...]
    unnamed x3 -> x10, local copies, waits for them, and re-layouts: 0.01 us -> 4.97 us
    all_to_all x1 -> x0, starting transfers between devices: 3.33 us -> none  [body(): lax.all_to_all(results.reshape(n_owner, capacity), 'cl', split_axis=0, co...]
  transfers between devices with their start and end apart: 3 -> 1, of which waited for: 2 -> 0; matrix products, arithmetic and copies ran while one was open for 5% -> 0% of each run, Pallas kernels for 0% -> 0%
where the time goes in v1:
time: 144 us
  blocking collectives  107 us (74%)
  Pallas kernels  32.3 us (22%)
  local copies, waits for them, and re-layouts  4.97 us (3%)
    all_to_all x1, blocking collectives, body(): lax.all_to_all(packed.reshape(n_owner, capacity, width), 'cl', split_axis...  77.8 us
    pallas_call x1, Pallas kernels, log_counts(): pl.pallas_call(functools.partial(counts_kernel, n_owner, capacity), out_s...  25 us
    all_gather x1, blocking collectives, body(): counts = lax.all_gather(counts, ('cl', 'grp'), tiled=True)  19.3 us
    all_to_all x1, blocking collectives, body(): lax.all_to_all(results.reshape(n_owner, capacity), 'cl', split_axis=0, co...  9.57 us
    pallas_call x1, Pallas kernels, pack(): pl.pallas_call(functools.partial(pack_kernel, n_owner, capacity), out_sha...  5.83 us
    unnamed x10, local copies, waits for them, and re-layouts  4.97 us
  transfers between devices with their start and end apart: 1, of which 0 were waited for; matrix products, arithmetic and copies ran while one was open for 0% of the time, Pallas kernels for 0%

profile of v1, /device:TPU:0, one launch (start us, length us, event | category | flops | bytes accessed | tf_op | source)
XLA Modules:
  0.0 143.9 jit_solution(9112604844306875225)
XLA Ops:
  0.0 0.0 copy-start
  0.0 1.4 copy-done
  1.4 0.0 copy-start.1
  1.4 0.7 copy-done.1
  2.1 0.0 copy-start.3
  2.1 0.7 copy-done.3
  2.8 5.8 %shard_map.37 = (bf16[2048,768]{1,0:T(8,128)(2,1)S(1)}, s32[8,128]{1,0:T(8,128)S(1)}, s32[1,64]{1,0:T(1,128)S(1)}) custom-call(bf16[1024,768]{1,0:T(8,128)(2,1)S(1)} %copy-done, s32[8,128]{1,0:T(8,128)S(1)} %bitcast.14, s32[1,64]{1,0:T(1,128)S(1)} %bitcast.15), custom_call_target="tpu_custom_call" | custom-call | tf_op jit(solution)/shard_map/pallas_call | solution.py:94
  8.6 0.0 copy-start.2
  8.6 0.6 copy-done.2
  9.2 77.8 %all_to_all.14 = bf16[8,256,768]{2,1,0:T(8,128)(2,1)S(1)} all-to-all(bf16[8,256,768]{2,1,0:T(8,128)(2,1)S(1)} %bitcast.11), channel_id=1, replica_groups=mesh['parts'=2,'cl'=8,'grp'=2] {'cl'}, dimensions={0} | all-to-all | bytes 6291456 | tf_op jit(solution)/shard_map/all_to_all | solution.py:220
  86.9 0.0 collective-permute-start
  87.0 19.3 %all-gather = s32[16,1,64]{2,1,0:T(1,128)S(1)} all-gather(s32[1,1,64]{2,1,0:T(1,128)S(1)} %bitcast.16), channel_id=1, replica_groups=mesh['parts'=2,'cl'=8,'grp'=2] {'cl','grp'}, dimensions={0}, use_global_device_ids=true | all-gather | bytes 4352 | tf_op jit(solution)/shard_map/all_gather | solution.py:219
  106.2 0.0 collective-permute-done.other_ref
  106.2 0.0 copy-start.4
  106.2 1.6 %copy-done.4 = bf16[2048,768]{1,0:T(8,128)(2,1)} copy-done((bf16[2048,768]{1,0:T(8,128)(2,1)}, bf16[2048,768]{1,0:T(8,128)(2,1)S(1)}, u32[]{:S(2)}) %copy-start.4) | copy-done | bytes 3145752
  107.9 25.0 %shard_map.38 = f32[1,2048]{1,0:T(1,128)S(1)} custom-call(s32[16,64]{1,0:T(8,128)S(1)} %bitcast.12, bf16[2048,768]{1,0:T(8,128)(2,1)S(1)} %bitcast.10, bf16[2048,768]{1,0:T(8,128)(2,1)} %copy-done.4), custom_call_target="tpu_custom_call" | custom-call | tf_op jit(solution)/shard_map/pallas_call | solution.py:178
  132.9 9.6 %all_to_all.15 = f32[8,1,256]{2,1,0:T(1,128)} all-to-all(f32[8,1,256]{2,1,0:T(1,128)S(1)} %bitcast.13), channel_id=1, replica_groups=mesh['parts'=2,'cl'=8,'grp'=2] {'cl'}, dimensions={0} | all-to-all | bytes 16384 | tf_op jit(solution)/shard_map/all_to_all | solution.py:225
  142.5 1.4 shard_map.39
Async XLA Ops:
  0.0 1.4 copy-start
  1.4 0.7 copy-start.1
  2.1 0.7 copy-start.3
  8.6 0.6 copy-start.2
  86.9 19.3 %collective-permute-start = (bf16[2048,768]{1,0:T(8,128)(2,1)S(1)}, bf16[2048,768]{1,0:T(8,128)(2,1)S(1)}, u32[]{:S(2)}, u32[]{:S(2)}) collective-permute-start(bf16[2048,768]{1,0:T(8,128)(2,1)S(1)} %bitcast.9), channel_id=1, source_target_pairs={{0,1},{1,0},{2,3},{3,2},{4,5},{5,4},{6,7},{7,6},{8,9},{9,8},{10,11... | collective-permute-start | bytes 9437192 | tf_op jit(solution)/shard_map/ppermute | solution.py:223
  106.2 1.7 %copy-start.4 = (bf16[2048,768]{1,0:T(8,128)(2,1)}, bf16[2048,768]{1,0:T(8,128)(2,1)S(1)}, u32[]{:S(2)}) copy-start(bf16[2048,768]{1,0:T(8,128)(2,1)S(1)} %collective-permute-done.other_ref) | copy-start | bytes 9437188

commit v2 on v1

--- a/solution.py
+++ b/solution.py
@@ -19,6 +19,7 @@
 NEIGHBOUR = math.log2(neighbour_factor)
 DEAD = -1e30
 VMEM_LIMIT = 48 * 1024 * 1024
+FAST_LIMIT = 32 * 1024 * 1024
 
 
 def column_of(row):
@@ -211,7 +212,268 @@
     )(values.reshape(-1, LANES), pos)
 
 
-def body(embeddings, labels, owner_map):
+def swapped(x, first, second):
+    return jnp.where(x == first, second, jnp.where(x == second, first, x))
+
+
+def fast_pack_kernel(
+    n_owner, capacity, main, home, x_hbm, lab_hbm, map_hbm, *refs
+):
+    outs, extra_ref, pos_ref, info_ref = refs[:n_owner], *refs[n_owner : n_owner + 3]
+    x_ref, lab_ref, map_ref, unit, pos_row, sems = refs[n_owner + 3 :]
+    copies = [
+        pltpu.make_async_copy(src, dst, sems.at[i])
+        for i, (src, dst) in enumerate(((x_hbm, x_ref), (lab_hbm, lab_ref), (map_hbm, map_ref)))
+    ]
+    for copy in copies:
+        copy.start()
+    rows = x_ref.shape[0]
+    n_fine = map_ref.shape[1]
+    per_owner = n_fine // n_owner
+    me = lax.axis_index("cl")
+    copies[1].wait()
+    copies[2].wait()
+    owner_row = map_ref[...].astype(jnp.float32)
+    fine_row = lax.broadcasted_iota(jnp.int32, (1, n_fine), 1).astype(jnp.float32)
+    key_row = owner_row * n_fine + fine_row
+    key_col = column_of(key_row)
+    sorted_col = jnp.sum(jnp.where(key_row < key_col, 1.0, 0.0), axis=1, keepdims=True)
+    lab = lab_ref[...].astype(jnp.float32)
+    lab_row = jnp.concatenate([lab[b : b + 1, :] for b in range(lab.shape[0])], axis=1)
+    fine_col = lax.broadcasted_iota(jnp.int32, (n_fine, rows), 0).astype(jnp.float32)
+    fine_id = jnp.sum(jnp.where(fine_col == lab_row, sorted_col, 0.0), axis=0, keepdims=True)
+    counts_col = jnp.sum(jnp.where(fine_col == fine_id, 1.0, 0.0), axis=1, keepdims=True)
+    coarse = jnp.floor((fine_id + 0.5) * (1.0 / per_owner))
+    first = coarse * per_owner
+    before = jnp.sum(jnp.where(fine_col < first, counts_col, 0.0), axis=0, keepdims=True)
+    upto = jnp.sum(jnp.where(fine_col < first + per_owner, counts_col, 0.0), axis=0, keepdims=True)
+    full = jnp.min(
+        jnp.where(upto - before == capacity, coarse, float(n_owner)), axis=1, keepdims=True
+    )
+    info = jnp.concatenate(
+        [row_of(counts_col), jnp.broadcast_to(full, (1, info_ref.shape[1] - n_fine))], axis=1
+    )
+    info_ref[...] = info.astype(jnp.int32)
+    index = lax.broadcasted_iota(jnp.int32, (1, rows), 1).astype(jnp.float32)
+    row_key = fine_id * rows + index
+    rank = jnp.zeros((1, rows), jnp.float32)
+    for start in range(0, rows, LANES):
+        other = column_of(row_key[:, start : start + LANES])
+        rank = rank + jnp.sum(jnp.where(other < row_key, 1.0, 0.0), axis=0, keepdims=True)
+    rank = (rank - before).astype(jnp.int32)
+    place = swapped(coarse.astype(jnp.int32), full.astype(jnp.int32), home)
+    step = place ^ me
+    table = step * capacity + rank
+    pos_ref[...] = jnp.concatenate(
+        [table[:, start : start + LANES] for start in range(0, rows, LANES)], axis=0
+    )
+    rest = jnp.where(place == home, n_owner * main + rank - main, -1)
+    pos_row[...] = jnp.where(rank < main, step * main + rank, rest)
+    copies[0].wait()
+    x = x_ref[...].astype(jnp.float32)
+    squares = jnp.sum(x * x, axis=1, keepdims=True)
+    unit[...] = (x * lax.rsqrt(squares + epsilon)).astype(jnp.bfloat16)
+
+    def chosen_rows(start, count):
+        slot = lax.broadcasted_iota(jnp.int32, (count, rows), 0) + start
+        chosen = jnp.where(slot == pos_row[...], 1.0, 0.0).astype(jnp.bfloat16)
+        return jnp.dot(chosen, unit[...], preferred_element_type=jnp.float32).astype(jnp.bfloat16)
+
+    together = 4
+    for group in range(0, n_owner, together):
+        packed = chosen_rows(group * main, together * main)
+        for i in range(together):
+            outs[group + i][...] = packed[i * main : (i + 1) * main]
+    extra_ref[...] = chosen_rows(n_owner * main, capacity - main)
+
+
+def fast_pack(embeddings, labels, owner_map, n_owner, capacity, main, home):
+    rows, width = embeddings.shape
+    n_fine = owner_map.shape[0]
+    info = -(-(n_fine + 1) // LANES) * LANES
+    vmem = pl.BlockSpec(memory_space=pltpu.VMEM)
+    anywhere = pl.BlockSpec(memory_space=pl.ANY)
+    lab_shape = (rows // LANES, LANES)
+    out = pl.pallas_call(
+        functools.partial(fast_pack_kernel, n_owner, capacity, main, home),
+        out_shape=(
+            *[jax.ShapeDtypeStruct((main, width), jnp.bfloat16)] * n_owner,
+            jax.ShapeDtypeStruct((capacity - main, width), jnp.bfloat16),
+            jax.ShapeDtypeStruct(lab_shape, jnp.int32),
+            jax.ShapeDtypeStruct((1, info), jnp.int32),
+        ),
+        in_specs=[anywhere] * 3,
+        out_specs=(vmem,) * (n_owner + 3),
+        scratch_shapes=[
+            pltpu.VMEM((rows, width), jnp.bfloat16),
+            pltpu.VMEM(lab_shape, jnp.int32),
+            pltpu.VMEM((1, n_fine), jnp.int32),
+            pltpu.VMEM((rows, width), jnp.bfloat16),
+            pltpu.VMEM((1, rows), jnp.int32),
+            pltpu.SemaphoreType.DMA((3,)),
+        ],
+        compiler_params=pltpu.CompilerParams(vmem_limit_bytes=FAST_LIMIT),
+    )(embeddings, labels.reshape(lab_shape), owner_map.reshape(1, n_fine))
+    return out[:n_owner], out[n_owner], out[n_owner + 1], out[n_owner + 2]
+
+
+def fast_counts_kernel(n_owner, n_fine, capacity, main, home, info_ref, *refs):
+    n_in = 4 * n_owner
+    sources, outs = refs[:n_in], refs[n_in : n_in + n_owner]
+    rows_ref, lab_lane, lab_sub, bias, result, sems = refs[n_in + n_owner :]
+    per_owner = n_fine // n_owner
+    rest = capacity - main
+    n_main, n_rest = n_owner * main, n_owner * rest
+    total = n_main + n_rest
+    me = lax.axis_index("cl")
+    hot = info_ref[0, n_fine]
+    is_home = me == home
+    cluster = swapped(me, hot, home)
+    copies = []
+    for part, (offset, size) in enumerate(
+        ((0, main), (total, main), (n_main, rest), (total + n_main, rest))
+    ):
+        copies.append(
+            [
+                pltpu.make_async_copy(
+                    sources[part * n_owner + k],
+                    rows_ref.at[pl.ds(offset + k * size, size)],
+                    sems.at[part * n_owner + k],
+                )
+                for k in range(n_owner)
+            ]
+        )
+    for copy in copies[0] + copies[1]:
+        copy.start()
+
+    @pl.when(is_home)
+    def _():
+        for copy in copies[2] + copies[3]:
+            copy.start()
+
+    for member in range(2):
+        for k in range(n_owner):
+            line = 2 * k + member
+            edges = []
+            edge = jnp.int32(0)
+            for f in range(per_owner):
+                edge = edge + info_ref[line, cluster * per_owner + f]
+                edges.append(edge)
+            down = lax.broadcasted_iota(jnp.int32, (capacity, LANES), 0)
+            label = jnp.zeros((capacity, LANES), jnp.int32)
+            for edge in edges:
+                label = label + jnp.where(down >= edge, 1, 0)
+            shift = jnp.where(label < per_owner, NEIGHBOUR - SCALE, DEAD)
+            start = member * total + k * main
+            lab_sub[start : start + main, :] = label[:main]
+            bias[start : start + main, :] = shift[:main]
+            start = member * total + n_main + k * rest
+            lab_sub[start : start + rest, :] = label[main:]
+            bias[start : start + rest, :] = shift[main:]
+            if member == 0:
+                across = lax.broadcasted_iota(jnp.int32, (1, capacity), 1)
+                label = jnp.zeros((1, capacity), jnp.int32)
+                for edge in edges:
+                    label = label + jnp.where(across >= edge, 1, 0)
+                label = jnp.where(label < per_owner, label, -1)
+                lab_lane[:, k * main : (k + 1) * main] = label[:, :main]
+                lab_lane[:, n_main + k * rest : n_main + (k + 1) * rest] = label[:, main:]
+
+    for copy in copies[0] + copies[1]:
+        copy.wait()
+
+    @pl.when(is_home)
+    def _():
+        for copy in copies[2] + copies[3]:
+            copy.wait()
+
+    wide = 256
+    tiles_main = [(s + i * (n_main // 2), n_main // 2) for s in (0, total) for i in range(2)]
+    tiles_rest = [
+        (s + i * (n_rest // 2), n_rest // 2) for s in (n_main, total + n_main) for i in range(2)
+    ]
+
+    def sums(rows_i, label_i, tiles):
+        acc = jnp.zeros((8, wide), jnp.float32)
+        for start, deep in tiles:
+            scores = lax.dot_general(
+                rows_ref[start : start + deep, :],
+                rows_i,
+                (((1,), (1,)), ((), ())),
+                preferred_element_type=jnp.float32,
+            )
+            repeat = wide // LANES
+            label_j = jnp.concatenate([lab_sub[start : start + deep, :]] * repeat, axis=1)
+            bias_j = jnp.concatenate([bias[start : start + deep, :]] * repeat, axis=1)
+            shift = jnp.where(label_j == label_i, -SCALE, bias_j)
+            terms = jnp.exp2(scores * SCALE + shift)
+            acc = acc + jnp.sum(terms.reshape(deep // 8, 8, wide), axis=0)
+        return acc
+
+    blocks = jnp.where(is_home, total // wide, -(-n_main // wide))
+
+    @pl.loop(0, blocks)
+    def _(block):
+        columns = pl.ds(pl.multiple_of(block * wide, wide), wide)
+        rows_i = rows_ref[columns, :]
+        label_i = lab_lane[:, columns]
+        result[:, columns] = jnp.sum(sums(rows_i, label_i, tiles_main), axis=0, keepdims=True)
+
+        @pl.when(is_home)
+        def _():
+            more = sums(rows_i, label_i, tiles_rest)
+            result[:, columns] += jnp.sum(more, axis=0, keepdims=True)
+
+    values = jnp.log(jnp.where(lab_lane[...] >= 0, result[...], 1.0))
+    for k in range(n_owner):
+        outs[k][:, :main] = values[:, k * main : (k + 1) * main]
+        outs[k][:, main:] = values[:, n_main + k * rest : n_main + (k + 1) * rest]
+
+
+def fast_counts(info, chunks, n_owner, n_fine, capacity, main, home):
+    width = chunks[0].shape[1]
+    total = n_owner * capacity
+    vmem = pl.BlockSpec(memory_space=pltpu.VMEM)
+    anywhere = pl.BlockSpec(memory_space=pl.ANY)
+    return pl.pallas_call(
+        functools.partial(fast_counts_kernel, n_owner, n_fine, capacity, main, home),
+        out_shape=(jax.ShapeDtypeStruct((1, capacity), jnp.float32),) * n_owner,
+        in_specs=[pl.BlockSpec(memory_space=pltpu.SMEM)] + [anywhere] * len(chunks),
+        out_specs=(vmem,) * n_owner,
+        scratch_shapes=[
+            pltpu.VMEM((2 * total, width), jnp.bfloat16),
+            pltpu.VMEM((1, total), jnp.int32),
+            pltpu.VMEM((2 * total, LANES), jnp.int32),
+            pltpu.VMEM((2 * total, LANES), jnp.float32),
+            pltpu.VMEM((1, total), jnp.float32),
+            pltpu.SemaphoreType.DMA((4 * n_owner,)),
+        ],
+        compiler_params=pltpu.CompilerParams(vmem_limit_bytes=FAST_LIMIT),
+    )(info, *chunks)
+
+
+def everywhere(info, n_owner):
+    info = jnp.concatenate([info, lax.ppermute(info, "grp", [(0, 1), (1, 0)])], axis=0)
+    bit = 1
+    while bit < n_owner:
+        moved = lax.ppermute(info, "cl", [(i, i ^ bit) for i in range(n_owner)])
+        info = jnp.concatenate([info, moved], axis=0)
+        bit *= 2
+    return info
+
+
+def all_fit(info, n_owner, n_fine, capacity, main):
+    lines = info.shape[0]
+    hot = info[:, n_fine]
+    sums = jnp.sum(info[:, :n_fine].reshape(lines, n_owner, n_fine // n_owner), axis=2)
+    is_hot = jnp.arange(n_owner)[None, :] == hot[0]
+    fits = jnp.all((sums <= main) | is_hot) & jnp.all(hot == hot[0])
+    unfit = jnp.where(fits, 0, 1).astype(jnp.int32).reshape(1, 1)
+    unfit = unfit + lax.ppermute(unfit, "parts", [(0, 1), (1, 0)])
+    return unfit[0, 0] == 0
+
+
+def general(embeddings, labels, owner_map):
     n_owner = lax.axis_size("cl")
     capacity = SLOTS // n_owner
     rows, width = embeddings.shape
@@ -228,6 +490,43 @@
     return unpack(returned.reshape(SLOTS), pos).reshape(rows)
 
 
+def body(embeddings, labels, owner_map):
+    n_owner = lax.axis_size("cl")
+    capacity = SLOTS // n_owner
+    rows = embeddings.shape[0]
+    n_fine = owner_map.shape[0]
+    main = -(-(rows // n_owner * 9 // 8) // 16) * 16
+    if main >= capacity:
+        return general(embeddings, labels, owner_map)
+    home = n_owner // 4
+    sends, extra, pos, info = fast_pack(
+        embeddings, labels, owner_map, n_owner, capacity, main, home
+    )
+    info = everywhere(info, n_owner)
+    fits = all_fit(info, n_owner, n_fine, capacity, main)
+
+    def to_step(x, k):
+        return x if k == 0 else lax.ppermute(x, "cl", [(i, i ^ k) for i in range(n_owner)])
+
+    def to_home(x, k):
+        return x if k == 0 else lax.ppermute(x, "cl", [(home ^ k, home)])
+
+    mine = [to_step(sends[k], k) for k in range(n_owner)]
+    mine_rest = [to_home(extra, k) for k in range(n_owner)]
+    other = [lax.ppermute(x, "grp", [(0, 1), (1, 0)]) for x in mine]
+    home_pairs = [(2 * home, 2 * home + 1), (2 * home + 1, 2 * home)]
+    other_rest = [lax.ppermute(x, ("cl", "grp"), home_pairs) for x in mine_rest]
+    results = fast_counts(
+        info, mine + other + mine_rest + other_rest, n_owner, n_fine, capacity, main, home
+    )
+    returned = jnp.concatenate([to_step(results[k], k) for k in range(n_owner)], axis=0)
+    return lax.cond(
+        fits,
+        lambda: unpack(returned, pos).reshape(rows),
+        lambda: general(embeddings, labels, owner_map),
+    )
+
+
 def solution(mesh):
     return jax.shard_map(
         body,

time: 144 us -> 150 us (1.042)
  blocking collectives: 107 us -> 0 us
  starting transfers between devices: 0.01 us -> 79.3 us
  waiting for transfers between devices: 0.01 us -> 35.1 us
  Pallas kernels: 32.3 us -> 20.4 us
  local copies, waits for them, and re-layouts: 4.97 us -> 9.83 us
  other arithmetic: 0 us -> 2.84 us
  between operations: 0.03 us -> 2.17 us
    all_to_all x2 -> x0, blocking collectives: 87.3 us -> none  [the longest x1 77.8 us: body(): lax.all_to_all(packed.reshape(n_owner, capacity, width), 'cl', split_axis...]
    ppermute x1 -> x42, starting transfers between devices: 0.01 us -> 79.3 us  [the longest x14 53.1 us: to_step(): lax.ppermute(x, 'cl', [(i, i ^ k) for i in range(n_owner)])]
    ppermute x1 -> x42, waiting for transfers between devices: 0.01 us -> 35.1 us  [the longest x14 27.7 us: to_step(): lax.ppermute(x, 'cl', [(i, i ^ k) for i in range(n_owner)])]
    all_gather x1 -> x0, blocking collectives: 19.3 us -> none  [body(): counts = lax.all_gather(counts, ('cl', 'grp'), tiled=True)]
    pallas_call x2, Pallas kernels: 30.9 us -> 19.6 us  [the longest x1 15.1 us: fast_counts(): pl.pallas_call(functools.partial(fast_counts_kernel, n_owner, n_fine, cap...]
    unnamed x10 -> x26, local copies, waits for them, and re-layouts: 4.97 us -> 8.52 us
    reduce_and x0 -> x2, other arithmetic: none -> 2.15 us  [all_fit(): fits = jnp.all((sums <= main) | is_hot) & jnp.all(hot == hot[0])]
  transfers between devices with their start and end apart: 1 -> 42, of which waited for: 0 -> 8; matrix products, arithmetic and copies ran while one was open for 0% -> 2% of each run, Pallas kernels for 0% -> 0%
where the time goes in v2:
time: 150 us
  starting transfers between devices  79.3 us (53%)
  waiting for transfers between devices  35.1 us (23%)
  Pallas kernels  20.4 us (14%)
  local copies, waits for them, and re-layouts  9.83 us (7%)
  other arithmetic  2.84 us (2%)
  between operations  2.17 us (1%)
    ppermute x14, starting transfers between devices, to_step(): lax.ppermute(x, 'cl', [(i, i ^ k) for i in range(n_owner)])  53.1 us
    ppermute x14, waiting for transfers between devices, to_step(): lax.ppermute(x, 'cl', [(i, i ^ k) for i in range(n_owner)])  27.7 us
    pallas_call x1, Pallas kernels, fast_counts(): pl.pallas_call(functools.partial(fast_counts_kernel, n_owner, n_fine, cap...  15.1 us
    unnamed x26, local copies, waits for them, and re-layouts  8.52 us
    ppermute x7, starting transfers between devices, to_home(): return x if k == 0 else lax.ppermute(x, 'cl', [(home ^ k, home)])  7.88 us
    ppermute x8, starting transfers between devices, body(): other_rest = [lax.ppermute(x, ('cl', 'grp'), home_pairs) for x in mine_rest]  7.31 us
    ppermute x3, waiting for transfers between devices, everywhere(): moved = lax.ppermute(info, 'cl', [(i, i ^ bit) for i in range(n_owner)])  5.76 us
    ppermute x3, starting transfers between devices, everywhere(): moved = lax.ppermute(info, 'cl', [(i, i ^ bit) for i in range(n_owner)])  5.72 us
  transfers between devices with their start and end apart: 42, of which 8 were waited for; matrix products, arithmetic and copies ran while one was open for 2% of the time, Pallas kernels for 0%

profile of v2, /device:TPU:0, one launch (start us, length us, event | category | flops | bytes accessed | tf_op | source)
XLA Modules:
  0.0 149.7 jit_solution(1468979212861426531)
XLA Ops:
  0.0 4.5 %shard_map.39 = (bf16[144,768]{1,0:T(8,128)(2,1)S(1)}, bf16[144,768]{1,0:T(8,128)(2,1)S(1)}, bf16[144,768]{1,0:T(8,128)(2,1)S(1)}, bf16[144,768]{1,0:T(8,128)(2,...) custom-call(bf16[1024,768]{1,0:T(8,128)(2,1)} %x_hbm.1, ...), custom_call_target="tpu_custom_call" | custom-call | tf_op jit(solution)/shard_map/pallas_call | solution.py:297
  4.5 0.5 collective-permute-start.1
  5.0 0.8 collective-permute-done.1
  5.8 2.8 %collective-permute-start.2 = (s32[2,128]{1,0:T(2,128)S(1)}, s32[2,128]{1,0:T(2,128)S(1)}, u32[]{:S(2)}, u32[]{:S(2)}) collective-permute-start(s32[2,128]{1,0:T(2,128)S(1)} %pad_add_fusion.2), channel_id=1, source_target_pairs={{0,2},{2,0},{4,6},{6,4},{8,10},{10,8},{12,14},{14,12},{1,3},{3,1},... | collective-permute-start | bytes 3080 | tf_op jit(solution)/shard_map/ppermute | solution.py:459
  8.7 1.5 %collective-permute-done.2 = s32[2,128]{1,0:T(2,128)S(1)} collective-permute-done((s32[2,128]{1,0:T(2,128)S(1)}, s32[2,128]{1,0:T(2,128)S(1)}, u32[]{:S(2)}, u32[]{:S(2)}) %collective-permute-start.2) | collective-permute-done | bytes 1056 | tf_op jit(solution)/shard_map/ppermute | solution.py:459
  10.2 2.1 %collective-permute-start.3 = (s32[4,128]{1,0:T(4,128)S(1)}, s32[4,128]{1,0:T(4,128)S(1)}, u32[]{:S(2)}, u32[]{:S(2)}) collective-permute-start(s32[4,128]{1,0:T(4,128)S(1)} %pad_add_fusion.1), channel_id=1, source_target_pairs={{0,4},{2,6},{4,0},{6,2},{8,12},{10,14},{12,8},{14,10},{1,5},{3,7},... | collective-permute-start | bytes 6152 | tf_op jit(solution)/shard_map/ppermute | solution.py:459
  12.4 0.7 collective-permute-start.21
  13.0 2.6 %collective-permute-start.22 = (bf16[112,768]{1,0:T(8,128)(2,1)S(1)}, bf16[112,768]{1,0:T(8,128)(2,1)S(1)}, u32[]{:S(2)}, u32[]{:S(2)}) collective-permute-start(bf16[112,768]{1,0:T(8,128)(2,1)S(1)} %get-tuple-element.54.refs_16_), channel_id=1, source_target_pairs={{0,4},{1,5},{16,20},{17,21}} | collective-permute-start | bytes 516104 | tf_op jit(solution)/shard_map/ppermute | solution.py:512
  15.6 0.7 collective-permute-start.23
  16.3 0.7 collective-permute-start.24
  17.0 0.8 collective-permute-start.4
  17.7 4.2 %collective-permute-done.4 = s32[8,128]{1,0:T(8,128)S(1)} collective-permute-done((s32[8,128]{1,0:T(8,128)S(1)}, s32[8,128]{1,0:T(8,128)S(1)}, u32[]{:S(2)}, u32[]{:S(2)}) %collective-permute-start.4) | collective-permute-done | bytes 4128 | tf_op jit(solution)/shard_map/ppermute | solution.py:459
  22.0 0.7 collective-permute-start.25
  22.6 1.3 collective-permute-start.26
  24.0 1.7 %collective-permute-start.6 = (bf16[144,768]{1,0:T(8,128)(2,1)S(1)}, bf16[144,768]{1,0:T(8,128)(2,1)S(1)}, u32[]{:S(2)}, u32[]{:S(2)}) collective-permute-start(bf16[144,768]{1,0:T(8,128)(2,1)S(1)} %get-tuple-element.47), channel_id=1, source_target_pairs={{0,2},{2,0},{4,6},{6,4},{8,10},{10,8},{12,14},{14,12},{1,3},{3,1},... | collective-permute-start | bytes 663560 | tf_op jit(solution)/shard_map/ppermute | solution.py:509
  25.6 1.6 %collective-permute-start.7 = (bf16[144,768]{1,0:T(8,128)(2,1)S(1)}, bf16[144,768]{1,0:T(8,128)(2,1)S(1)}, u32[]{:S(2)}, u32[]{:S(2)}) collective-permute-start(bf16[144,768]{1,0:T(8,128)(2,1)S(1)} %get-tuple-element.48), channel_id=1, source_target_pairs={{0,4},{2,6},{4,0},{6,2},{8,12},{10,14},{12,8},{14,10},{1,5},{3,7},... | collective-permute-start | bytes 663560 | tf_op jit(solution)/shard_map/ppermute | solution.py:509
  27.3 1.3 collective-permute-start.27
  28.6 0.7 collective-permute-start.28
  29.3 1.5 collective-permute-start.8
  30.8 5.0 %collective-permute-start.9 = (bf16[144,768]{1,0:T(8,128)(2,1)S(1)}, bf16[144,768]{1,0:T(8,128)(2,1)S(1)}, u32[]{:S(2)}, u32[]{:S(2)}) collective-permute-start(bf16[144,768]{1,0:T(8,128)(2,1)S(1)} %get-tuple-element.50), channel_id=1, source_target_pairs={{0,8},{2,10},{4,12},{6,14},{8,0},{10,2},{12,4},{14,6},{1,9},{3,11}... | collective-permute-start | bytes 663560 | tf_op jit(solution)/shard_map/ppermute | solution.py:509
  35.8 0.7 copy-done
  36.4 5.6 %collective-permute-start.10 = (bf16[144,768]{1,0:T(8,128)(2,1)S(1)}, bf16[144,768]{1,0:T(8,128)(2,1)S(1)}, u32[]{:S(2)}, u32[]{:S(2)}) collective-permute-start(bf16[144,768]{1,0:T(8,128)(2,1)S(1)} %get-tuple-element.51), channel_id=1, source_target_pairs={{0,10},{2,8},{4,14},{6,12},{8,2},{10,0},{12,6},{14,4},{1,11},{3,9}... | collective-permute-start | bytes 663560 | tf_op jit(solution)/shard_map/ppermute | solution.py:509
  42.0 2.0 %collective-permute-start.12 = (bf16[144,768]{1,0:T(8,128)(2,1)S(1)}, bf16[144,768]{1,0:T(8,128)(2,1)S(1)}, u32[]{:S(2)}, u32[]{:S(2)}) collective-permute-start(bf16[144,768]{1,0:T(8,128)(2,1)S(1)} %get-tuple-element.53), channel_id=1, source_target_pairs={{0,14},{2,12},{4,10},{6,8},{8,6},{10,4},{12,2},{14,0},{1,15},{3,13... | collective-permute-start | bytes 663560 | tf_op jit(solution)/shard_map/ppermute | solution.py:509
  44.0 0.7 collective-permute-start.29
  44.7 25.2 %collective-permute-done.10.refs_5_ = bf16[144,768]{1,0:T(8,128)(2,1)S(1)} collective-permute-done((bf16[144,768]{1,0:T(8,128)(2,1)S(1)}, bf16[144,768]{1,0:T(8,128)(2,1)S(1)}, u32[]{:S(2)}, u32[]{:S(2)}) %collective-permute-start.10) | collective-permute-done | bytes 221216 | tf_op jit(solution)/shard_map/ppermute | solution.py:509
  70.0 0.7 collective-permute-start.30
  70.6 0.7 collective-permute-start.31
  71.3 0.7 collective-permute-start.32
  72.1 0.7 copy-done.2
  72.8 0.5 collective-permute-start.15
  73.3 0.7 copy-done.4
  73.9 1.3 collective-permute-start.33
  75.3 0.7 copy-done.6
  75.9 1.3 collective-permute-start.34
  77.3 0.7 copy-done.8
  77.9 1.3 collective-permute-start.35
  79.3 0.6 slice.14
  79.8 0.6 iota_compare_fusion
  80.7 0.5 collective-permute-start.17
  81.2 0.1 collective-permute-start.18
  81.3 0.4 collective-permute-start.19
  81.7 0.1 collective-permute-start.20
  81.8 0.8 or_reduce_fusion
  82.6 0.2 collective-permute-done.18.refs_13_
  82.8 0.3 collective-permute-done.19.refs_14_
  83.1 0.3 collective-permute-done.20.refs_15_
  83.4 0.9 copy-done.1
  84.3 0.9 copy-done.3
  85.3 0.9 copy-done.5
  86.2 0.9 copy-done.7
  87.1 0.9 copy-done.9
  88.0 15.1 %shard_map.40 = (f32[1,256]{1,0:T(1,128)S(1)}, f32[1,256]{1,0:T(1,128)S(1)}, f32[1,256]{1,0:T(1,128)S(1)}, f32[1,256]{1,0:T(1,128)S(1)}, f32[1,256]{1,0:T(1,128)...) custom-call(s32[16,128]{1,0:T(8,128)S(1)} %concatenate.21.info_ref, ...), custom_call_target="tpu_custom_call" | custom-call | tf_op jit(solution)/shard_map/pallas_call | solution.py:438
  103.2 26.7 %collective-permute-start.37 = (f32[1,256]{1,0:T(1,128)S(1)}, f32[1,256]{1,0:T(1,128)S(1)}, u32[]{:S(2)}, u32[]{:S(2)}) collective-permute-start(f32[1,256]{1,0:T(1,128)S(1)} %get-tuple-element.57), channel_id=1, source_target_pairs={{0,4},{2,6},{4,0},{6,2},{8,12},{10,14},{12,8},{14,10},{1,5},{3,7},... | collective-permute-start | bytes 3080 | tf_op jit(solution)/shard_map/ppermute | solution.py:509
  129.9 1.4 fusion
  132.5 3.0 %collective-permute-start.5 = (s32[1,1]{1,0:T(1,128)}, s32[1,1]{1,0:T(1,128)}, u32[]{:S(2)}, u32[]{:S(2)}) collective-permute-start(s32[1,1]{1,0:T(1,128)} %bitcast.14), channel_id=1, source_target_pairs={{0,16},{16,0},{1,17},{17,1},{2,18},{18,2},{3,19},{19,3},{4,20},{20... | collective-permute-start | bytes 20 | tf_op jit(solution)/shard_map/ppermute | solution.py:472
  135.5 1.4 collective-permute-start.38
  136.9 2.9 %collective-permute-start.40 = (f32[1,256]{1,0:T(1,128)S(1)}, f32[1,256]{1,0:T(1,128)S(1)}, u32[]{:S(2)}, u32[]{:S(2)}) collective-permute-start(f32[1,256]{1,0:T(1,128)S(1)} %get-tuple-element.60), channel_id=1, source_target_pairs={{0,10},{2,8},{4,14},{6,12},{8,2},{10,0},{12,6},{14,4},{1,11},{3,9}... | collective-permute-start | bytes 3080 | tf_op jit(solution)/shard_map/ppermute | solution.py:509
  139.8 1.5 %collective-permute-start.41 = (f32[1,256]{1,0:T(1,128)S(1)}, f32[1,256]{1,0:T(1,128)S(1)}, u32[]{:S(2)}, u32[]{:S(2)}) collective-permute-start(f32[1,256]{1,0:T(1,128)S(1)} %get-tuple-element.61), channel_id=1, source_target_pairs={{0,12},{2,14},{4,8},{6,10},{8,4},{10,6},{12,0},{14,2},{1,13},{3,15... | collective-permute-start | bytes 3080 | tf_op jit(solution)/shard_map/ppermute | solution.py:509
  141.4 3.2 %collective-permute-start.42 = (f32[1,256]{1,0:T(1,128)S(1)}, f32[1,256]{1,0:T(1,128)S(1)}, u32[]{:S(2)}, u32[]{:S(2)}) collective-permute-start(f32[1,256]{1,0:T(1,128)S(1)} %get-tuple-element.62), channel_id=1, source_target_pairs={{0,14},{2,12},{4,10},{6,8},{8,6},{10,4},{12,2},{14,0},{1,15},{3,13... | collective-permute-start | bytes 3080 | tf_op jit(solution)/shard_map/ppermute | solution.py:509
  145.2 2.4 %collective-permute-done.42 = f32[1,256]{1,0:T(1,128)S(1)} collective-permute-done((f32[1,256]{1,0:T(1,128)S(1)}, f32[1,256]{1,0:T(1,128)S(1)}, u32[]{:S(2)}, u32[]{:S(2)}) %collective-permute-start.42) | collective-permute-done | bytes 1056 | tf_op jit(solution)/shard_map/ppermute | solution.py:509
  147.7 1.4 conditional.1
  147.7 0.6 reshape.48.values_ref
  148.3 0.8 branch_1_fun.1
  149.1 0.6 copy-done.13
  (62 shorter events, 0.5 us)
Async XLA Ops:
  4.5 1.3 collective-permute-start.1
  5.8 4.4 %collective-permute-start.2 = (s32[2,128]{1,0:T(2,128)S(1)}, s32[2,128]{1,0:T(2,128)S(1)}, u32[]{:S(2)}, u32[]{:S(2)}) collective-permute-start(s32[2,128]{1,0:T(2,128)S(1)} %pad_add_fusion.2), channel_id=1, source_target_pairs={{0,2},{2,0},{4,6},{6,4},{8,10},{10,8},{12,14},{14,12},{1,3},{3,1},... | collective-permute-start | bytes 3080 | tf_op jit(solution)/shard_map/ppermute | solution.py:459
  10.2 6.7 %collective-permute-start.3 = (s32[4,128]{1,0:T(4,128)S(1)}, s32[4,128]{1,0:T(4,128)S(1)}, u32[]{:S(2)}, u32[]{:S(2)}) collective-permute-start(s32[4,128]{1,0:T(4,128)S(1)} %pad_add_fusion.1), channel_id=1, source_target_pairs={{0,4},{2,6},{4,0},{6,2},{8,12},{10,14},{12,8},{14,10},{1,5},{3,7},... | collective-permute-start | bytes 6152 | tf_op jit(solution)/shard_map/ppermute | solution.py:459
  12.4 10.3 %collective-permute-start.21 = (bf16[112,768]{1,0:T(8,128)(2,1)S(1)}, bf16[112,768]{1,0:T(8,128)(2,1)S(1)}, u32[]{:S(2)}, u32[]{:S(2)}) collective-permute-start(bf16[112,768]{1,0:T(8,128)(2,1)S(1)} %get-tuple-element.54.refs_16_), channel_id=1, source_target_pairs={{6,4},{7,5},{22,20},{23,21}} | collective-permute-start | bytes 516104 | tf_op jit(solution)/shard_map/ppermute | solution.py:512
  13.0 10.9 %collective-permute-start.22 = (bf16[112,768]{1,0:T(8,128)(2,1)S(1)}, bf16[112,768]{1,0:T(8,128)(2,1)S(1)}, u32[]{:S(2)}, u32[]{:S(2)}) collective-permute-start(bf16[112,768]{1,0:T(8,128)(2,1)S(1)} %get-tuple-element.54.refs_16_), channel_id=1, source_target_pairs={{0,4},{1,5},{16,20},{17,21}} | collective-permute-start | bytes 516104 | tf_op jit(solution)/shard_map/ppermute | solution.py:512
  15.6 10.1 %collective-permute-start.23 = (bf16[112,768]{1,0:T(8,128)(2,1)S(1)}, bf16[112,768]{1,0:T(8,128)(2,1)S(1)}, u32[]{:S(2)}, u32[]{:S(2)}) collective-permute-start(bf16[112,768]{1,0:T(8,128)(2,1)S(1)} %get-tuple-element.54.refs_16_), channel_id=1, source_target_pairs={{2,4},{3,5},{18,20},{19,21}} | collective-permute-start | bytes 516104 | tf_op jit(solution)/shard_map/ppermute | solution.py:512
  16.3 11.0 %collective-permute-start.24 = (bf16[112,768]{1,0:T(8,128)(2,1)S(1)}, bf16[112,768]{1,0:T(8,128)(2,1)S(1)}, u32[]{:S(2)}, u32[]{:S(2)}) collective-permute-start(bf16[112,768]{1,0:T(8,128)(2,1)S(1)} %get-tuple-element.54.refs_16_), channel_id=1, source_target_pairs={{12,4},{13,5},{28,20},{29,21}} | collective-permute-start | bytes 516104 | tf_op jit(solution)/shard_map/ppermute | solution.py:512
  17.0 5.0 %collective-permute-start.4 = (s32[8,128]{1,0:T(8,128)S(1)}, s32[8,128]{1,0:T(8,128)S(1)}, u32[]{:S(2)}, u32[]{:S(2)}) collective-permute-start(s32[8,128]{1,0:T(8,128)S(1)} %pad_add_fusion), channel_id=1, source_target_pairs={{0,8},{2,10},{4,12},{6,14},{8,0},{10,2},{12,4},{14,6},{1,9},{3,11}... | collective-permute-start | bytes 12296 | tf_op jit(solution)/shard_map/ppermute | solution.py:459
  22.0 6.7 %collective-permute-start.25 = (bf16[112,768]{1,0:T(8,128)(2,1)S(1)}, bf16[112,768]{1,0:T(8,128)(2,1)S(1)}, u32[]{:S(2)}, u32[]{:S(2)}) collective-permute-start(bf16[112,768]{1,0:T(8,128)(2,1)S(1)} %get-tuple-element.54.refs_16_), channel_id=1, source_target_pairs={{14,4},{15,5},{30,20},{31,21}} | collective-permute-start | bytes 516104 | tf_op jit(solution)/shard_map/ppermute | solution.py:512
  22.6 6.7 %collective-permute-start.26 = (bf16[112,768]{1,0:T(8,128)(2,1)S(1)}, bf16[112,768]{1,0:T(8,128)(2,1)}, u32[]{:S(2)}, u32[]{:S(2)}) collective-permute-start(bf16[112,768]{1,0:T(8,128)(2,1)S(1)} %get-tuple-element.54.refs_16_), channel_id=1, source_target_pairs={{8,4},{9,5},{24,20},{25,21}} | collective-permute-start | bytes 516104 | tf_op jit(solution)/shard_map/ppermute | solution.py:512
  24.0 18.0 %collective-permute-start.6 = (bf16[144,768]{1,0:T(8,128)(2,1)S(1)}, bf16[144,768]{1,0:T(8,128)(2,1)S(1)}, u32[]{:S(2)}, u32[]{:S(2)}) collective-permute-start(bf16[144,768]{1,0:T(8,128)(2,1)S(1)} %get-tuple-element.47), channel_id=1, source_target_pairs={{0,2},{2,0},{4,6},{6,4},{8,10},{10,8},{12,14},{14,12},{1,3},{3,1},... | collective-permute-start | bytes 663560 | tf_op jit(solution)/shard_map/ppermute | solution.py:509
  25.6 16.4 %collective-permute-start.7 = (bf16[144,768]{1,0:T(8,128)(2,1)S(1)}, bf16[144,768]{1,0:T(8,128)(2,1)S(1)}, u32[]{:S(2)}, u32[]{:S(2)}) collective-permute-start(bf16[144,768]{1,0:T(8,128)(2,1)S(1)} %get-tuple-element.48), channel_id=1, source_target_pairs={{0,4},{2,6},{4,0},{6,2},{8,12},{10,14},{12,8},{14,10},{1,5},{3,7},... | collective-permute-start | bytes 663560 | tf_op jit(solution)/shard_map/ppermute | solution.py:509
  27.3 3.5 %collective-permute-start.27 = (bf16[112,768]{1,0:T(8,128)(2,1)S(1)}, bf16[112,768]{1,0:T(8,128)(2,1)}, u32[]{:S(2)}, u32[]{:S(2)}) collective-permute-start(bf16[112,768]{1,0:T(8,128)(2,1)S(1)} %get-tuple-element.54.refs_16_), channel_id=1, source_target_pairs={{10,4},{11,5},{26,20},{27,21}} | collective-permute-start | bytes 516104 | tf_op jit(solution)/shard_map/ppermute | solution.py:512
  28.6 7.1 %collective-permute-start.28 = (bf16[112,768]{1,0:T(8,128)(2,1)S(1)}, bf16[112,768]{1,0:T(8,128)(2,1)S(1)}, u32[]{:S(2)}, u32[]{:S(2)}) collective-permute-start(bf16[112,768]{1,0:T(8,128)(2,1)S(1)} %get-tuple-element.54.refs_16_), channel_id=1, source_target_pairs={{4,5},{5,4},{20,21},{21,20}} | collective-permute-start | bytes 516104 | tf_op jit(solution)/shard_map/ppermute | solution.py:518
  29.3 14.7 %collective-permute-start.8 = (bf16[144,768]{1,0:T(8,128)(2,1)S(1)}, bf16[144,768]{1,0:T(8,128)(2,1)S(1)}, u32[]{:S(2)}, u32[]{:S(2)}) collective-permute-start(bf16[144,768]{1,0:T(8,128)(2,1)S(1)} %get-tuple-element.49), channel_id=1, source_target_pairs={{0,6},{2,4},{4,2},{6,0},{8,14},{10,12},{12,10},{14,8},{1,7},{3,5},... | collective-permute-start | bytes 663560 | tf_op jit(solution)/shard_map/ppermute | solution.py:509
  30.8 13.3 %collective-permute-start.9 = (bf16[144,768]{1,0:T(8,128)(2,1)S(1)}, bf16[144,768]{1,0:T(8,128)(2,1)S(1)}, u32[]{:S(2)}, u32[]{:S(2)}) collective-permute-start(bf16[144,768]{1,0:T(8,128)(2,1)S(1)} %get-tuple-element.50), channel_id=1, source_target_pairs={{0,8},{2,10},{4,12},{6,14},{8,0},{10,2},{12,4},{14,6},{1,9},{3,11}... | collective-permute-start | bytes 663560 | tf_op jit(solution)/shard_map/ppermute | solution.py:509
  35.8 0.7 copy-start
  36.4 33.5 %collective-permute-start.10 = (bf16[144,768]{1,0:T(8,128)(2,1)S(1)}, bf16[144,768]{1,0:T(8,128)(2,1)S(1)}, u32[]{:S(2)}, u32[]{:S(2)}) collective-permute-start(bf16[144,768]{1,0:T(8,128)(2,1)S(1)} %get-tuple-element.51), channel_id=1, source_target_pairs={{0,10},{2,8},{4,14},{6,12},{8,2},{10,0},{12,6},{14,4},{1,11},{3,9}... | collective-permute-start | bytes 663560 | tf_op jit(solution)/shard_map/ppermute | solution.py:509
  42.0 28.6 %collective-permute-start.11 = (bf16[144,768]{1,0:T(8,128)(2,1)S(1)}, bf16[144,768]{1,0:T(8,128)(2,1)S(1)}, u32[]{:S(2)}, u32[]{:S(2)}) collective-permute-start(bf16[144,768]{1,0:T(8,128)(2,1)S(1)} %get-tuple-element.52), channel_id=1, source_target_pairs={{0,12},{2,14},{4,8},{6,10},{8,4},{10,6},{12,0},{14,2},{1,13},{3,15... | collective-permute-start | bytes 663560 | tf_op jit(solution)/shard_map/ppermute | solution.py:509
  42.0 29.3 %collective-permute-start.12 = (bf16[144,768]{1,0:T(8,128)(2,1)S(1)}, bf16[144,768]{1,0:T(8,128)(2,1)S(1)}, u32[]{:S(2)}, u32[]{:S(2)}) collective-permute-start(bf16[144,768]{1,0:T(8,128)(2,1)S(1)} %get-tuple-element.53), channel_id=1, source_target_pairs={{0,14},{2,12},{4,10},{6,8},{8,6},{10,4},{12,2},{14,0},{1,15},{3,13... | collective-permute-start | bytes 663560 | tf_op jit(solution)/shard_map/ppermute | solution.py:509
  44.0 28.0 %collective-permute-start.13 = (bf16[144,768]{1,0:T(8,128)(2,1)S(1)}, bf16[144,768]{1,0:T(8,128)(2,1)S(1)}, u32[]{:S(2)}, u32[]{:S(2)}) collective-permute-start(bf16[144,768]{1,0:T(8,128)(2,1)S(1)} %get-tuple-element.46.refs_0_), channel_id=1, source_target_pairs={{0,1},{1,0},{2,3},{3,2},{4,5},{5,4},{6,7},{7,6},{8,9},{9,8},{10,11... | collective-permute-start | bytes 663560 | tf_op jit(solution)/shard_map/ppermute | solution.py:516
  44.0 28.1 %collective-permute-start.29 = (bf16[112,768]{1,0:T(8,128)(2,1)S(1)}, bf16[112,768]{1,0:T(8,128)(2,1)S(1)}, u32[]{:S(2)}, u32[]{:S(2)}) collective-permute-start(bf16[112,768]{1,0:T(8,128)(2,1)S(1)} %collective-permute-done.21.refs_17_), channel_id=1, source_target_pairs={{4,5},{5,4},{20,21},{21,20}} | collective-permute-start | bytes 516104 | tf_op jit(solution)/shard_map/ppermute | solution.py:518
  70.0 3.3 %collective-permute-start.30 = (bf16[112,768]{1,0:T(8,128)(2,1)S(1)}, bf16[112,768]{1,0:T(8,128)(2,1)S(1)}, u32[]{:S(2)}, u32[]{:S(2)}) collective-permute-start(bf16[112,768]{1,0:T(8,128)(2,1)S(1)} %collective-permute-done.22.refs_18_), channel_id=1, source_target_pairs={{4,5},{5,4},{20,21},{21,20}} | collective-permute-start | bytes 516104 | tf_op jit(solution)/shard_map/ppermute | solution.py:518
  70.6 4.6 %collective-permute-start.31 = (bf16[112,768]{1,0:T(8,128)(2,1)S(1)}, bf16[112,768]{1,0:T(8,128)(2,1)S(1)}, u32[]{:S(2)}, u32[]{:S(2)}) collective-permute-start(bf16[112,768]{1,0:T(8,128)(2,1)S(1)} %collective-permute-done.23.refs_19_), channel_id=1, source_target_pairs={{4,5},{5,4},{20,21},{21,20}} | collective-permute-start | bytes 516104 | tf_op jit(solution)/shard_map/ppermute | solution.py:518
  71.3 5.9 %collective-permute-start.32 = (bf16[112,768]{1,0:T(8,128)(2,1)S(1)}, bf16[112,768]{1,0:T(8,128)(2,1)S(1)}, u32[]{:S(2)}, u32[]{:S(2)}) collective-permute-start(bf16[112,768]{1,0:T(8,128)(2,1)S(1)} %collective-permute-done.24.refs_20_), channel_id=1, source_target_pairs={{4,5},{5,4},{20,21},{21,20}} | collective-permute-start | bytes 516104 | tf_op jit(solution)/shard_map/ppermute | solution.py:518
  72.0 9.3 %collective-permute-start.14 = (bf16[144,768]{1,0:T(8,128)(2,1)S(1)}, bf16[144,768]{1,0:T(8,128)(2,1)S(1)}, u32[]{:S(2)}, u32[]{:S(2)}) collective-permute-start(bf16[144,768]{1,0:T(8,128)(2,1)S(1)} %collective-permute-done.6.refs_1_), channel_id=1, source_target_pairs={{0,1},{1,0},{2,3},{3,2},{4,5},{5,4},{6,7},{7,6},{8,9},{9,8},{10,11... | collective-permute-start | bytes 663560 | tf_op jit(solution)/shard_map/ppermute | solution.py:516
  72.1 0.7 copy-start.2
  72.8 8.9 %collective-permute-start.15 = (bf16[144,768]{1,0:T(8,128)(2,1)S(1)}, bf16[144,768]{1,0:T(8,128)(2,1)S(1)}, u32[]{:S(2)}, u32[]{:S(2)}) collective-permute-start(bf16[144,768]{1,0:T(8,128)(2,1)S(1)} %collective-permute-done.7.refs_2_), channel_id=1, source_target_pairs={{0,1},{1,0},{2,3},{3,2},{4,5},{5,4},{6,7},{7,6},{8,9},{9,8},{10,11... | collective-permute-start | bytes 663560 | tf_op jit(solution)/shard_map/ppermute | solution.py:516
  73.3 0.7 copy-start.4
  73.9 6.7 %collective-permute-start.33 = (bf16[112,768]{1,0:T(8,128)(2,1)S(1)}, bf16[112,768]{1,0:T(8,128)(2,1)}, u32[]{:S(2)}, u32[]{:S(2)}) collective-permute-start(bf16[112,768]{1,0:T(8,128)(2,1)S(1)} %collective-permute-done.25.refs_21_), channel_id=1, source_target_pairs={{4,5},{5,4},{20,21},{21,20}} | collective-permute-start | bytes 516104 | tf_op jit(solution)/shard_map/ppermute | solution.py:518
  75.3 0.7 copy-start.6
  75.9 4.8 %collective-permute-start.34 = (bf16[112,768]{1,0:T(8,128)(2,1)}, bf16[112,768]{1,0:T(8,128)(2,1)}, u32[]{:S(2)}, u32[]{:S(2)}) collective-permute-start(bf16[112,768]{1,0:T(8,128)(2,1)} %collective-permute-done.26.refs_22_), channel_id=1, source_target_pairs={{4,5},{5,4},{20,21},{21,20}} | collective-permute-start | bytes 516104 | tf_op jit(solution)/shard_map/ppermute | solution.py:518
  77.3 0.7 copy-start.8
  77.9 3.3 %collective-permute-start.35 = (bf16[112,768]{1,0:T(8,128)(2,1)}, bf16[112,768]{1,0:T(8,128)(2,1)}, u32[]{:S(2)}, u32[]{:S(2)}) collective-permute-start(bf16[112,768]{1,0:T(8,128)(2,1)} %collective-permute-done.27.refs_23_), channel_id=1, source_target_pairs={{4,5},{5,4},{20,21},{21,20}} | collective-permute-start | bytes 516104 | tf_op jit(solution)/shard_map/ppermute | solution.py:518
  80.6 2.0 %collective-permute-start.16 = (bf16[144,768]{1,0:T(8,128)(2,1)S(1)}, bf16[144,768]{1,0:T(8,128)(2,1)S(1)}, u32[]{:S(2)}, u32[]{:S(2)}) collective-permute-start(bf16[144,768]{1,0:T(8,128)(2,1)S(1)} %collective-permute-done.8.refs_3_), channel_id=1, source_target_pairs={{0,1},{1,0},{2,3},{3,2},{4,5},{5,4},{6,7},{7,6},{8,9},{9,8},{10,11... | collective-permute-start | bytes 663560 | tf_op jit(solution)/shard_map/ppermute | solution.py:516
  80.7 1.9 %collective-permute-start.17 = (bf16[144,768]{1,0:T(8,128)(2,1)S(1)}, bf16[144,768]{1,0:T(8,128)(2,1)S(1)}, u32[]{:S(2)}, u32[]{:S(2)}) collective-permute-start(bf16[144,768]{1,0:T(8,128)(2,1)S(1)} %collective-permute-done.9.refs_4_), channel_id=1, source_target_pairs={{0,1},{1,0},{2,3},{3,2},{4,5},{5,4},{6,7},{7,6},{8,9},{9,8},{10,11... | collective-permute-start | bytes 663560 | tf_op jit(solution)/shard_map/ppermute | solution.py:516
  81.2 1.6 %collective-permute-start.18 = (bf16[144,768]{1,0:T(8,128)(2,1)S(1)}, bf16[144,768]{1,0:T(8,128)(2,1)S(1)}, u32[]{:S(2)}, u32[]{:S(2)}) collective-permute-start(bf16[144,768]{1,0:T(8,128)(2,1)S(1)} %collective-permute-done.10.refs_5_), channel_id=1, source_target_pairs={{0,1},{1,0},{2,3},{3,2},{4,5},{5,4},{6,7},{7,6},{8,9},{9,8},{10,11... | collective-permute-start | bytes 663560 | tf_op jit(solution)/shard_map/ppermute | solution.py:516
  81.3 1.8 %collective-permute-start.19 = (bf16[144,768]{1,0:T(8,128)(2,1)S(1)}, bf16[144,768]{1,0:T(8,128)(2,1)S(1)}, u32[]{:S(2)}, u32[]{:S(2)}) collective-permute-start(bf16[144,768]{1,0:T(8,128)(2,1)S(1)} %collective-permute-done.11.refs_6_), channel_id=1, source_target_pairs={{0,1},{1,0},{2,3},{3,2},{4,5},{5,4},{6,7},{7,6},{8,9},{9,8},{10,11... | collective-permute-start | bytes 663560 | tf_op jit(solution)/shard_map/ppermute | solution.py:516
  81.7 1.7 %collective-permute-start.20 = (bf16[144,768]{1,0:T(8,128)(2,1)S(1)}, bf16[144,768]{1,0:T(8,128)(2,1)S(1)}, u32[]{:S(2)}, u32[]{:S(2)}) collective-permute-start(bf16[144,768]{1,0:T(8,128)(2,1)S(1)} %collective-permute-done.12.refs_7_), channel_id=1, source_target_pairs={{0,1},{1,0},{2,3},{3,2},{4,5},{5,4},{6,7},{7,6},{8,9},{9,8},{10,11... | collective-permute-start | bytes 663560 | tf_op jit(solution)/shard_map/ppermute | solution.py:516
  81.8 65.8 %copy-start.12 = (s32[1024]{0:T(1024)S(1)}, s32[1024]{0:T(1024)}, u32[]{:S(2)}) copy-start(s32[1024]{0:T(1024)} %param.6) | copy-start | bytes 12292
  81.8 65.8 %copy-start.14 = (s32[64]{0:T(128)S(1)}, s32[64]{0:T(128)}, u32[]{:S(2)}) copy-start(s32[64]{0:T(128)} %param.7) | copy-start | bytes 772
  83.4 0.9 copy-start.1
  84.3 0.9 copy-start.3
  85.3 0.9 copy-start.5
  86.2 0.9 copy-start.7
  87.1 0.9 copy-start.9
  103.1 36.7 %collective-permute-start.36 = (f32[1,256]{1,0:T(1,128)S(1)}, f32[1,256]{1,0:T(1,128)S(1)}, u32[]{:S(2)}, u32[]{:S(2)}) collective-permute-start(f32[1,256]{1,0:T(1,128)S(1)} %get-tuple-element.56), channel_id=1, source_target_pairs={{0,2},{2,0},{4,6},{6,4},{8,10},{10,8},{12,14},{14,12},{1,3},{3,1},... | collective-permute-start | bytes 3080 | tf_op jit(solution)/shard_map/ppermute | solution.py:509
  103.2 38.1 %collective-permute-start.37 = (f32[1,256]{1,0:T(1,128)S(1)}, f32[1,256]{1,0:T(1,128)S(1)}, u32[]{:S(2)}, u32[]{:S(2)}) collective-permute-start(f32[1,256]{1,0:T(1,128)S(1)} %get-tuple-element.57), channel_id=1, source_target_pairs={{0,4},{2,6},{4,0},{6,2},{8,12},{10,14},{12,8},{14,10},{1,5},{3,7},... | collective-permute-start | bytes 3080 | tf_op jit(solution)/shard_map/ppermute | solution.py:509
  132.5 4.4 %collective-permute-start.5 = (s32[1,1]{1,0:T(1,128)}, s32[1,1]{1,0:T(1,128)}, u32[]{:S(2)}, u32[]{:S(2)}) collective-permute-start(s32[1,1]{1,0:T(1,128)} %bitcast.14), channel_id=1, source_target_pairs={{0,16},{16,0},{1,17},{17,1},{2,18},{18,2},{3,19},{19,3},{4,20},{20... | collective-permute-start | bytes 20 | tf_op jit(solution)/shard_map/ppermute | solution.py:472
  135.5 9.7 %collective-permute-start.38 = (f32[1,256]{1,0:T(1,128)S(1)}, f32[1,256]{1,0:T(1,128)S(1)}, u32[]{:S(2)}, u32[]{:S(2)}) collective-permute-start(f32[1,256]{1,0:T(1,128)S(1)} %get-tuple-element.58), channel_id=1, source_target_pairs={{0,6},{2,4},{4,2},{6,0},{8,14},{10,12},{12,10},{14,8},{1,7},{3,5},... | collective-permute-start | bytes 3080 | tf_op jit(solution)/shard_map/ppermute | solution.py:509
  136.9 8.3 %collective-permute-start.39 = (f32[1,256]{1,0:T(1,128)S(1)}, f32[1,256]{1,0:T(1,128)S(1)}, u32[]{:S(2)}, u32[]{:S(2)}) collective-permute-start(f32[1,256]{1,0:T(1,128)S(1)} %get-tuple-element.59), channel_id=1, source_target_pairs={{0,8},{2,10},{4,12},{6,14},{8,0},{10,2},{12,4},{14,6},{1,9},{3,11}... | collective-permute-start | bytes 3080 | tf_op jit(solution)/shard_map/ppermute | solution.py:509
  136.9 8.3 %collective-permute-start.40 = (f32[1,256]{1,0:T(1,128)S(1)}, f32[1,256]{1,0:T(1,128)S(1)}, u32[]{:S(2)}, u32[]{:S(2)}) collective-permute-start(f32[1,256]{1,0:T(1,128)S(1)} %get-tuple-element.60), channel_id=1, source_target_pairs={{0,10},{2,8},{4,14},{6,12},{8,2},{10,0},{12,6},{14,4},{1,11},{3,9}... | collective-permute-start | bytes 3080 | tf_op jit(solution)/shard_map/ppermute | solution.py:509
  139.8 5.4 %collective-permute-start.41 = (f32[1,256]{1,0:T(1,128)S(1)}, f32[1,256]{1,0:T(1,128)S(1)}, u32[]{:S(2)}, u32[]{:S(2)}) collective-permute-start(f32[1,256]{1,0:T(1,128)S(1)} %get-tuple-element.61), channel_id=1, source_target_pairs={{0,12},{2,14},{4,8},{6,10},{8,4},{10,6},{12,0},{14,2},{1,13},{3,15... | collective-permute-start | bytes 3080 | tf_op jit(solution)/shard_map/ppermute | solution.py:509
  141.4 6.3 %collective-permute-start.42 = (f32[1,256]{1,0:T(1,128)S(1)}, f32[1,256]{1,0:T(1,128)S(1)}, u32[]{:S(2)}, u32[]{:S(2)}) collective-permute-start(f32[1,256]{1,0:T(1,128)S(1)} %get-tuple-element.62), channel_id=1, source_target_pairs={{0,14},{2,12},{4,10},{6,8},{8,6},{10,4},{12,2},{14,0},{1,15},{3,13... | collective-permute-start | bytes 3080 | tf_op jit(solution)/shard_map/ppermute | solution.py:509
  149.1 0.6 copy-start.13

commit v3 on v1

--- a/solution.py
+++ b/solution.py
@@ -19,6 +19,8 @@
 NEIGHBOUR = math.log2(neighbour_factor)
 DEAD = -1e30
 VMEM_LIMIT = 48 * 1024 * 1024
+FAST_LIMIT = 40 * 1024 * 1024
+INFO = 16
 
 
 def column_of(row):
@@ -211,7 +213,300 @@
     )(values.reshape(-1, LANES), pos)
 
 
-def body(embeddings, labels, owner_map):
+def swapped(x, first, second):
+    return jnp.where(x == first, second, jnp.where(x == second, first, x))
+
+
+def fast_pack_kernel(n_owner, capacity, main, home, x_hbm, lab_hbm, map_hbm, *refs):
+    main_ref, extra_ref, pos_ref, x_ref, lab_ref, map_ref, unit, pos_row, sems = refs
+    copies = [
+        pltpu.make_async_copy(src, dst, sems.at[i])
+        for i, (src, dst) in enumerate(((x_hbm, x_ref), (lab_hbm, lab_ref), (map_hbm, map_ref)))
+    ]
+    for copy in copies:
+        copy.start()
+    rows = x_ref.shape[0]
+    n_fine = map_ref.shape[1]
+    per_owner = n_fine // n_owner
+    rest = capacity - main
+    copies[1].wait()
+    copies[2].wait()
+    owner_row = map_ref[...].astype(jnp.float32)
+    fine_row = lax.broadcasted_iota(jnp.int32, (1, n_fine), 1).astype(jnp.float32)
+    key_row = owner_row * n_fine + fine_row
+    key_col = column_of(key_row)
+    sorted_col = jnp.sum(jnp.where(key_row < key_col, 1.0, 0.0), axis=1, keepdims=True)
+    lab = lab_ref[...].astype(jnp.float32)
+    lab_row = jnp.concatenate([lab[b : b + 1, :] for b in range(lab.shape[0])], axis=1)
+    fine_col = lax.broadcasted_iota(jnp.int32, (n_fine, rows), 0).astype(jnp.float32)
+    fine_id = jnp.sum(jnp.where(fine_col == lab_row, sorted_col, 0.0), axis=0, keepdims=True)
+    counts_col = jnp.sum(jnp.where(fine_col == fine_id, 1.0, 0.0), axis=1, keepdims=True)
+    coarse = jnp.floor((fine_id + 0.5) * (1.0 / per_owner))
+    first = coarse * per_owner
+    before = jnp.sum(jnp.where(fine_col < first, counts_col, 0.0), axis=0, keepdims=True)
+    upto = jnp.sum(jnp.where(fine_col < first + per_owner, counts_col, 0.0), axis=0, keepdims=True)
+    full = jnp.min(
+        jnp.where(upto - before == capacity, coarse, float(n_owner)), axis=1, keepdims=True
+    )
+    line = lax.broadcasted_iota(jnp.int32, (n_fine, LANES), 0)
+    lane = lax.broadcasted_iota(jnp.int32, (n_fine, LANES), 1)
+    inside = (line <= lane) & (lax.div(line, per_owner) == lax.div(lane, per_owner))
+    running = jnp.sum(jnp.where(inside, counts_col, 0.0), axis=0, keepdims=True)
+    info = jnp.where(lane[:1] < n_fine, running, full)
+    index = lax.broadcasted_iota(jnp.int32, (1, rows), 1).astype(jnp.float32)
+    row_key = fine_id * rows + index
+    rank = jnp.zeros((1, rows), jnp.float32)
+    for start in range(0, rows, LANES):
+        other = column_of(row_key[:, start : start + LANES])
+        rank = rank + jnp.sum(jnp.where(other < row_key, 1.0, 0.0), axis=0, keepdims=True)
+    rank = (rank - before).astype(jnp.int32)
+    place = swapped(coarse.astype(jnp.int32), full.astype(jnp.int32), home)
+    table = place * capacity + rank
+    pos_ref[...] = jnp.concatenate(
+        [table[:, start : start + LANES] for start in range(0, rows, LANES)], axis=0
+    )
+    later = jnp.where(place == home, n_owner * main + rank - main, -1)
+    pos_row[...] = jnp.where(rank < main, place * main + rank, later)
+    copies[0].wait()
+    x = x_ref[...].astype(jnp.float32)
+    squares = jnp.sum(x * x, axis=1, keepdims=True)
+    unit[...] = (x * lax.rsqrt(squares + epsilon)).astype(jnp.bfloat16)
+
+    def chosen_rows(start, count):
+        slot = lax.broadcasted_iota(jnp.int32, (count, rows), 0) + start
+        chosen = jnp.where(slot == pos_row[...], 1.0, 0.0).astype(jnp.bfloat16)
+        return jnp.dot(chosen, unit[...], preferred_element_type=jnp.float32).astype(jnp.bfloat16)
+
+    extra_ref[:rest, :] = chosen_rows(n_owner * main, rest)
+    extra_ref[rest:, :] = jnp.zeros((extra_ref.shape[0] - rest, extra_ref.shape[1]), jnp.bfloat16)
+    extra_ref[rest:, :LANES] = jnp.broadcast_to(
+        info, (extra_ref.shape[0] - rest, LANES)
+    ).astype(jnp.bfloat16)
+    count = n_owner * main // 4
+    for start in range(0, n_owner * main, count):
+        main_ref[start : start + count, :] = chosen_rows(start, count)
+
+
+def fast_pack(embeddings, labels, owner_map, n_owner, capacity, main, home):
+    rows, width = embeddings.shape
+    n_fine = owner_map.shape[0]
+    vmem = pl.BlockSpec(memory_space=pltpu.VMEM)
+    anywhere = pl.BlockSpec(memory_space=pl.ANY)
+    lab_shape = (rows // LANES, LANES)
+    return pl.pallas_call(
+        functools.partial(fast_pack_kernel, n_owner, capacity, main, home),
+        out_shape=(
+            jax.ShapeDtypeStruct((n_owner * main, width), jnp.bfloat16),
+            jax.ShapeDtypeStruct((capacity - main + INFO, width), jnp.bfloat16),
+            jax.ShapeDtypeStruct(lab_shape, jnp.int32),
+        ),
+        in_specs=[anywhere] * 3,
+        out_specs=(vmem,) * 3,
+        scratch_shapes=[
+            pltpu.VMEM((rows, width), jnp.bfloat16),
+            pltpu.VMEM(lab_shape, jnp.int32),
+            pltpu.VMEM((1, n_fine), jnp.int32),
+            pltpu.VMEM((rows, width), jnp.bfloat16),
+            pltpu.VMEM((1, rows), jnp.int32),
+            pltpu.SemaphoreType.DMA((3,)),
+        ],
+        compiler_params=pltpu.CompilerParams(vmem_limit_bytes=FAST_LIMIT),
+    )(embeddings, labels.reshape(lab_shape), owner_map.reshape(1, n_fine))
+
+
+def pieces(start, count, parts):
+    return [(start + i * (count // parts), count // parts) for i in range(parts)]
+
+
+def fast_counts_kernel(
+    n_owner, n_fine, capacity, main, home, mine_ref, other_ref, gathered, *refs
+):
+    out_ref, unfit_ref, rows_ref, lab_lane, lab_sub, bias, result, sems = refs
+    per_owner = n_fine // n_owner
+    rest = capacity - main
+    n_main, n_rest = n_owner * main, n_owner * rest
+    total = n_main + n_rest
+    grp = lax.axis_index("grp")
+    me = lax.axis_index("cl")
+    is_home = me == home
+    copies = [
+        pltpu.make_async_copy(
+            gathered.at[pl.ds((2 * k + lax.rem(grp + member, 2)) * (rest + INFO), rest)],
+            rows_ref.at[pl.ds(member * n_rest + k * rest, rest)],
+            sems.at[member * n_owner + k],
+        )
+        for member in range(2)
+        for k in range(n_owner)
+    ]
+
+    @pl.when(is_home)
+    def _():
+        for copy in copies:
+            copy.start()
+
+    def info_of(line):
+        start = pl.multiple_of(line * (rest + INFO) + rest, INFO)
+        return gathered[pl.ds(start, INFO), :LANES][:1].astype(jnp.float32)
+
+    lane = lax.broadcasted_iota(jnp.int32, (1, LANES), 1)
+    hot = jnp.max(jnp.where(lane == n_fine, info_of(0), 0.0), axis=1, keepdims=True)
+    hot = hot.astype(jnp.int32)
+    lane_cluster = lax.div(lane, per_owner)
+    is_edge = lane_cluster == swapped(me, hot, home)
+    last = (lane < n_fine) & (lax.rem(lane, per_owner) == per_owner - 1) & (lane_cluster != hot)
+    unfit = jnp.zeros((1, LANES), jnp.float32)
+    for member in range(2):
+        for k in range(n_owner):
+            info = info_of(2 * k + lax.rem(grp + member, 2))
+            wrong = (last & (info > main)) | ((lane == n_fine) & (info != hot.astype(jnp.float32)))
+            unfit = unfit + jnp.where(wrong, 1.0, 0.0)
+            edges = jnp.where(is_edge, info, 2.0 * capacity)
+
+            def write(start, first, count, edges=edges):
+                slot = lax.broadcasted_iota(jnp.int32, (count, LANES), 0) + first
+                label = jnp.where(slot.astype(jnp.float32) >= edges, 1.0, 0.0)
+                label = jnp.broadcast_to(jnp.sum(label, axis=1, keepdims=True), (count, LANES))
+                lab_sub[start : start + count, :] = label
+                bias[start : start + count, :] = jnp.where(
+                    label < per_owner, NEIGHBOUR - SCALE, DEAD
+                )
+
+            write(member * n_main + k * main, 0, main)
+
+            @pl.when(is_home)
+            def _():
+                write(2 * n_main + member * n_rest + k * rest, main, rest)
+
+    unfit_ref[...] = jnp.broadcast_to(
+        jnp.max(unfit, axis=1, keepdims=True), unfit_ref.shape
+    ).astype(jnp.int32)
+
+    def turn(start, count, to):
+        for i in range(0, count, LANES):
+            block = jnp.transpose(lab_sub[start + i : start + i + LANES, :])[:1]
+            lab_lane[:, to + i : to + i + LANES] = jnp.where(block < per_owner, block, -1.0)
+
+    turn(0, n_main, 0)
+
+    @pl.when(is_home)
+    def _():
+        turn(2 * n_main, n_rest, n_main)
+
+    near = [(mine_ref, s, s, d) for s, d in pieces(0, n_main, 2)]
+    near += [(other_ref, s, s + n_main, d) for s, d in pieces(0, n_main, 2)]
+    far = [(rows_ref, s, s + 2 * n_main, d) for s, d in pieces(0, 2 * n_rest, 4)]
+
+    def sums(rows_i, label_i, tiles):
+        wide = rows_i.shape[0]
+
+        def scores_of(tile):
+            ref, start, _, deep = tile
+            return lax.dot_general(
+                ref[start : start + deep, :],
+                rows_i,
+                (((1,), (1,)), ((), ())),
+                preferred_element_type=jnp.float32,
+            )
+
+        acc = jnp.zeros((8, wide), jnp.float32)
+        ahead = scores_of(tiles[0])
+        for i, (_, _, place, deep) in enumerate(tiles):
+            scores = ahead
+            if i + 1 < len(tiles):
+                ahead = scores_of(tiles[i + 1])
+            label_j = jnp.concatenate([lab_sub[place : place + deep, :]] * (wide // LANES), axis=1)
+            bias_j = jnp.concatenate([bias[place : place + deep, :]] * (wide // LANES), axis=1)
+            shift = jnp.where(label_j == label_i, -SCALE, bias_j)
+            terms = jnp.exp2(scores * SCALE + shift)
+            acc = acc + jnp.sum(terms.reshape(deep // 8, 8, wide), axis=0)
+        return jnp.sum(acc, axis=0, keepdims=True)
+
+    def block(ref, start, wide, to):
+        label_i = lab_lane[:, pl.ds(to, wide)]
+        result[:, pl.ds(to, wide)] = sums(ref[pl.ds(start, wide), :], label_i, near)
+
+    def block_far(ref, start, wide, to):
+        label_i = lab_lane[:, pl.ds(to, wide)]
+        result[:, pl.ds(to, wide)] += sums(ref[pl.ds(start, wide), :], label_i, far)
+
+    def each_block(ref, count, to, run):
+        wide = 256
+        full = count // wide
+
+        @pl.loop(0, full)
+        def _(i):
+            start = pl.multiple_of(i * wide, wide)
+            run(ref, start, wide, pl.multiple_of(start + to, LANES))
+
+        if count % wide:
+            run(ref, full * wide, count % wide, full * wide + to)
+
+    each_block(mine_ref, n_main, 0, block)
+
+    @pl.when(is_home)
+    def _():
+        for copy in copies:
+            copy.wait()
+        each_block(mine_ref, n_main, 0, block_far)
+        each_block(rows_ref, n_rest, n_main, block)
+        each_block(rows_ref, n_rest, n_main, block_far)
+
+    values = jnp.log(jnp.where(lab_lane[...] >= 0, result[...], 1.0))
+    for k in range(n_owner):
+        out_ref[k, :, :main] = values[:, k * main : (k + 1) * main]
+        out_ref[k, :, main:] = values[:, n_main + k * rest : n_main + (k + 1) * rest]
+
+
+def fast_counts(mine, other, gathered, n_owner, n_fine, capacity, main, home):
+    width = mine.shape[1]
+    total = n_owner * capacity
+    n_rest = n_owner * (capacity - main)
+    vmem = pl.BlockSpec(memory_space=pltpu.VMEM)
+    return pl.pallas_call(
+        functools.partial(fast_counts_kernel, n_owner, n_fine, capacity, main, home),
+        out_shape=(
+            jax.ShapeDtypeStruct((n_owner, 1, capacity), jnp.float32),
+            jax.ShapeDtypeStruct((8, LANES), jnp.int32),
+        ),
+        in_specs=[vmem] * 3,
+        out_specs=(vmem, vmem),
+        scratch_shapes=[
+            pltpu.VMEM((2 * n_rest, width), jnp.bfloat16),
+            pltpu.VMEM((1, total), jnp.float32),
+            pltpu.VMEM((2 * total, LANES), jnp.float32),
+            pltpu.VMEM((2 * total, LANES), jnp.float32),
+            pltpu.VMEM((1, total), jnp.float32),
+            pltpu.SemaphoreType.DMA((2 * n_owner,)),
+        ],
+        compiler_params=pltpu.CompilerParams(vmem_limit_bytes=FAST_LIMIT),
+    )(mine, other, gathered)
+
+
+def fast_unpack_kernel(values_ref, pos_ref, out_ref):
+    pos = pos_ref[...]
+    lane = lax.rem(pos, LANES)
+    line = lax.div(pos, LANES)
+    out = jnp.zeros(pos.shape, jnp.float32)
+    per = values_ref.shape[2] // LANES
+    for r in range(values_ref.shape[0] * per):
+        start = r % per * LANES
+        table = jnp.broadcast_to(values_ref[r // per, :, start : start + LANES], pos.shape)
+        found = jnp.take_along_axis(table, lane, axis=1)
+        out = jnp.where(line == r, found, out)
+    out_ref[...] = out
+
+
+def fast_unpack(values, pos):
+    vmem = pl.BlockSpec(memory_space=pltpu.VMEM)
+    return pl.pallas_call(
+        fast_unpack_kernel,
+        out_shape=jax.ShapeDtypeStruct(pos.shape, jnp.float32),
+        in_specs=[vmem, vmem],
+        out_specs=vmem,
+    )(values, pos)
+
+
+def general(embeddings, labels, owner_map):
     n_owner = lax.axis_size("cl")
     capacity = SLOTS // n_owner
     rows, width = embeddings.shape
@@ -228,6 +523,31 @@
     return unpack(returned.reshape(SLOTS), pos).reshape(rows)
 
 
+def body(embeddings, labels, owner_map):
+    n_owner = lax.axis_size("cl")
+    capacity = SLOTS // n_owner
+    rows = embeddings.shape[0]
+    n_fine = owner_map.shape[0]
+    main = -(-(rows // n_owner * 9 // 8) // 16) * 16
+    if main >= capacity or n_fine >= LANES:
+        return general(embeddings, labels, owner_map)
+    home = n_owner // 4
+    width = embeddings.shape[1]
+    packed, extra, pos = fast_pack(embeddings, labels, owner_map, n_owner, capacity, main, home)
+    gathered = lax.all_gather(extra, ("cl", "grp"), tiled=True)
+    mine = lax.all_to_all(
+        packed.reshape(n_owner, main, width), "cl", split_axis=0, concat_axis=0, tiled=True
+    ).reshape(n_owner * main, width)
+    other = lax.ppermute(mine, "grp", [(0, 1), (1, 0)])
+    results, unfit = fast_counts(mine, other, gathered, n_owner, n_fine, capacity, main, home)
+    returned = lax.all_to_all(results, "cl", split_axis=0, concat_axis=0, tiled=True)
+    return lax.cond(
+        unfit[0, 0] == 0,
+        lambda: fast_unpack(returned, pos).reshape(rows),
+        lambda: general(embeddings, labels, owner_map),
+    )
+
+
 def solution(mesh):
     return jax.shard_map(
         body,

time: 144 us -> 128 us (0.89)
  blocking collectives: 107 us -> 67.4 us
  starting transfers between devices: 0.01 us -> 20.6 us
  Pallas kernels: 32.3 us -> 13.8 us
  between operations: 0.03 us -> 14.1 us
  waiting for transfers between devices: 0.01 us -> 9.06 us
  local copies, waits for them, and re-layouts: 4.97 us -> 3 us
    all_to_all x0 -> x1, starting transfers between devices: none -> 20.6 us  [body(): lax.all_to_all(results, 'cl', split_axis=0, concat_axis=0, tiled=True)]
    all_to_all x2 -> x1, blocking collectives: 87.3 us -> 67.4 us  [body(): lax.all_to_all(packed.reshape(n_owner, main, width), 'cl', split_axis=0,...]
    all_gather x1 -> x0, blocking collectives: 19.3 us -> none  [body(): counts = lax.all_gather(counts, ('cl', 'grp'), tiled=True)]
    pallas_call x3, Pallas kernels: 32.3 us -> 13.8 us  [the longest x1 8.54 us: fast_counts(): pl.pallas_call(functools.partial(fast_counts_kernel, n_owner, n_fine, cap...]
    all_to_all x0 -> x1, waiting for transfers between devices: none -> 5.35 us  [body(): lax.all_to_all(results, 'cl', split_axis=0, concat_axis=0, tiled=True)]
    ppermute x1, waiting for transfers between devices: 0.01 us -> 3.69 us  [body(): other = lax.ppermute(mine, 'grp', [(0, 1), (1, 0)])]
    unnamed x10 -> x8, local copies, waits for them, and re-layouts: 4.97 us -> 2.49 us
  transfers between devices with their start and end apart: 1 -> 3, of which waited for: 0 -> 2; matrix products, arithmetic and copies ran while one was open for 0% -> 0% of each run, Pallas kernels for 0% -> 0%
where the time goes in v3:
time: 128 us
  blocking collectives  67.4 us (53%)
  starting transfers between devices  20.6 us (16%)
  between operations  14.1 us (11%)
  Pallas kernels  13.8 us (11%)
  waiting for transfers between devices  9.06 us (7%)
  local copies, waits for them, and re-layouts  3 us (2%)
    all_to_all x1, blocking collectives, body(): lax.all_to_all(packed.reshape(n_owner, main, width), 'cl', split_axis=0,...  67.4 us
    all_to_all x1, starting transfers between devices, body(): lax.all_to_all(results, 'cl', split_axis=0, concat_axis=0, tiled=True)  20.6 us
    pallas_call x1, Pallas kernels, fast_counts(): pl.pallas_call(functools.partial(fast_counts_kernel, n_owner, n_fine, cap...  8.54 us
    all_to_all x1, waiting for transfers between devices, body(): lax.all_to_all(results, 'cl', split_axis=0, concat_axis=0, tiled=True)  5.35 us
    pallas_call x1, Pallas kernels, fast_pack(): pl.pallas_call(functools.partial(fast_pack_kernel, n_owner, capacity, mai...  5.15 us
    ppermute x1, waiting for transfers between devices, body(): other = lax.ppermute(mine, 'grp', [(0, 1), (1, 0)])  3.69 us
  transfers between devices with their start and end apart: 3, of which 2 were waited for; matrix products, arithmetic and copies ran while one was open for 0% of the time, Pallas kernels for 0%

profile of v3, /device:TPU:0, one launch (start us, length us, event | category | flops | bytes accessed | tf_op | source)
XLA Modules:
  0.0 127.9 jit_solution(10259636576165235020)
XLA Ops:
  6.5 0.0 all-gather.3.cloned.1.call-start
  6.5 5.2 %shard_map.39 = (bf16[1152,768]{1,0:T(8,128)(2,1)S(1)}, bf16[128,768]{1,0:T(8,128)(2,1)}, s32[8,128]{1,0:T(8,128)S(1)}) custom-call(bf16[1024,768]{1,0:T(8,128)(2,1)} %x_hbm.1, s32[8,128]{1,0:T(8,128)} %bitcast.25, s32[1,64]{1,0:T(1,128)} %bitcast.29), custom_call_target="tpu_custom_call" | custom-call | tf_op jit(solution)/shard_map/pallas_call | solution.py:296
  11.7 0.0 all-gather.3.cloned.1.call-update
  11.7 0.0 copy-start.3
  11.7 67.4 %all_to_all.23 = bf16[8,144,768]{2,1,0:T(8,128)(2,1)S(1)} all-to-all(bf16[8,144,768]{2,1,0:T(8,128)(2,1)S(1)} %bitcast.20), channel_id=1, replica_groups=mesh['parts'=2,'cl'=8,'grp'=2] {'cl'}, dimensions={0} | all-to-all | bytes 3538944 | tf_op jit(solution)/shard_map/all_to_all | solution.py:538
  79.1 0.0 copy-start.5
  79.1 0.0 collective-permute-start.1
  79.1 3.7 %collective-permute-done.1.other_ref = bf16[1152,768]{1,0:T(8,128)(2,1)S(1)} collective-permute-done((bf16[1152,768]{1,0:T(8,128)(2,1)S(1)}, bf16[1152,768]{1,0:T(8,128)(2,1)S(1)}, u32[]{:S(2)}, u32[]{:S(2)}) %collective-permute-start.1) | collective-permute-done | bytes 1769504 | tf_op jit(solution)/shard_map/ppermute | solution.py:541
  82.8 0.0 all-gather.3.cloned.1.call-done.gathered
  82.8 0.0 copy-start
  82.8 1.9 %copy-done = bf16[2048,768]{1,0:T(8,128)(2,1)S(1)} copy-done((bf16[2048,768]{1,0:T(8,128)(2,1)S(1)}, bf16[2048,768]{1,0:T(8,128)(2,1)}, u32[]{:S(2)}) %copy-start) | copy-done | bytes 3145752
  84.7 8.5 %shard_map.40 = (f32[8,1,256]{2,1,0:T(1,128)}, s32[8,128]{1,0:T(8,128)S(1)}) custom-call(bf16[1152,768]{1,0:T(8,128)(2,1)S(1)} %bitcast.18, bf16[1152,768]{1,0:T(8,128)(2,1)S(1)} %collective-permute-done.1.other_ref, bf16[2048,768]{1,0:T(8,128)(2,1)S(1)} %copy-done), custom_call_target="tpu_custom_call" | custom-call | tf_op jit(solution)/shard_map/pallas_call | solution.py:465
  93.2 20.6 %all-to-all-start.3 = ((f32[8,1,256]{2,1,0:T(1,128)}), f32[8,1,256]{2,1,0:T(1,128)S(1)}, u32[]{:S(2)}, u32[]{:S(2)}) async-start(f32[8,1,256]{2,1,0:T(1,128)} %get-tuple-element.34), calls=%async_computation.3 | async-start | bytes 16384 | tf_op jit(solution)/shard_map/all_to_all | solution.py:543
  113.8 0.5 slice.3
  115.0 5.4 %all-to-all-done.3 = f32[8,1,256]{2,1,0:T(1,128)S(1)} async-done(((f32[8,1,256]{2,1,0:T(1,128)}), f32[8,1,256]{2,1,0:T(1,128)S(1)}, u32[]{:S(2)}, u32[]{:S(2)}) %all-to-all-start.3) | async-done | bytes 8224 | tf_op jit(solution)/shard_map/all_to_all | solution.py:543
  120.3 0.0 copy-done.3
  120.3 0.0 copy-done.5
  120.3 0.1 conditional.1
  120.3 0.1 branch_1_fun.1
  120.4 0.0 copy-start.4
  120.4 0.6 copy-done.4
Async XLA Ops:
  6.5 76.3 %all-gather.3.cloned.1.call-start = ((), (), s32[]{:S(2)}) async-start(), calls=%async_computation.4 | async-start | bytes 3342336 | tf_op jit(solution)/shard_map/all_gather | solution.py:537
  11.7 108.6 %copy-start.3 = (s32[1024]{0:T(1024)S(1)}, s32[1024]{0:T(1024)}, u32[]{:S(2)}) copy-start(s32[1024]{0:T(1024)} %param.6) | copy-start | bytes 12292
  79.1 41.2 %copy-start.5 = (s32[64]{0:T(128)S(1)}, s32[64]{0:T(128)}, u32[]{:S(2)}) copy-start(s32[64]{0:T(128)} %param.7) | copy-start | bytes 772
  79.1 3.7 %collective-permute-start.1 = (bf16[1152,768]{1,0:T(8,128)(2,1)S(1)}, bf16[1152,768]{1,0:T(8,128)(2,1)S(1)}, u32[]{:S(2)}, u32[]{:S(2)}) collective-permute-start(bf16[1152,768]{1,0:T(8,128)(2,1)S(1)} %bitcast.17), channel_id=1, source_target_pairs={{0,1},{1,0},{2,3},{3,2},{4,5},{5,4},{6,7},{7,6},{8,9},{9,8},{10,11... | collective-permute-start | bytes 5308424 | tf_op jit(solution)/shard_map/ppermute | solution.py:541
  82.8 1.9 %copy-start = (bf16[2048,768]{1,0:T(8,128)(2,1)S(1)}, bf16[2048,768]{1,0:T(8,128)(2,1)}, u32[]{:S(2)}) copy-start(bf16[2048,768]{1,0:T(8,128)(2,1)} %all-gather.3.cloned.1.call-done.gathered) | copy-start | bytes 9437188
  93.2 27.1 %all-to-all-start.3 = ((f32[8,1,256]{2,1,0:T(1,128)}), f32[8,1,256]{2,1,0:T(1,128)S(1)}, u32[]{:S(2)}, u32[]{:S(2)}) async-start(f32[8,1,256]{2,1,0:T(1,128)} %get-tuple-element.34), calls=%async_computation.3 | async-start | bytes 16384 | tf_op jit(solution)/shard_map/all_to_all | solution.py:543
  120.4 0.6 copy-start.4
Sparse Core Ops, SparseCore 0:
  11.8 64.5 all-gather.2

commit v4 on v3

--- a/solution.py
+++ b/solution.py
@@ -266,7 +266,8 @@
         [table[:, start : start + LANES] for start in range(0, rows, LANES)], axis=0
     )
     later = jnp.where(place == home, n_owner * main + rank - main, -1)
-    pos_row[...] = jnp.where(rank < main, place * main + rank, later)
+    fits = rank < jnp.where(place == home, main, main - 1)
+    pos_row[...] = jnp.where(fits, place * main + rank, later)
     copies[0].wait()
     x = x_ref[...].astype(jnp.float32)
     squares = jnp.sum(x * x, axis=1, keepdims=True)
@@ -285,6 +286,12 @@
     count = n_owner * main // 4
     for start in range(0, n_owner * main, count):
         main_ref[start : start + count, :] = chosen_rows(start, count)
+    for owner in range(n_owner):
+        if owner != home:
+            tail = slice((owner + 1) * main - INFO, (owner + 1) * main)
+            old = main_ref[tail, :LANES].astype(jnp.float32)
+            down = lax.broadcasted_iota(jnp.int32, old.shape, 0)
+            main_ref[tail, :LANES] = jnp.where(down == INFO - 1, info, old).astype(jnp.bfloat16)
 
 
 def fast_pack(embeddings, labels, owner_map, n_owner, capacity, main, home):
@@ -318,38 +325,67 @@
     return [(start + i * (count // parts), count // parts) for i in range(parts)]
 
 
+def gather_kernel(n_owner, rest, home, *refs):
+    chunks, out, sems = refs[:n_owner], refs[n_owner], refs[n_owner + 1]
+    copies = []
+    for k, chunk in enumerate(chunks):
+        source = home ^ k
+        parts = (
+            (0, rest, source * rest),
+            (rest, INFO, n_owner * rest + source * INFO),
+        )
+        for start, count, to in parts:
+            copies.append(
+                pltpu.make_async_copy(
+                    chunk.at[pl.ds(start, count)],
+                    out.at[pl.ds(to, count)],
+                    sems.at[len(copies)],
+                )
+            )
+
+    @pl.when(lax.axis_index("cl") == home)
+    def _():
+        for copy in copies:
+            copy.start()
+        for copy in copies:
+            copy.wait()
+
+
+def gather_rest(chunks, n_owner, rest, home):
+    anywhere = pl.BlockSpec(memory_space=pl.ANY)
+    shape = (n_owner * (rest + INFO), chunks[0].shape[1])
+    return pl.pallas_call(
+        functools.partial(gather_kernel, n_owner, rest, home),
+        out_shape=jax.ShapeDtypeStruct(shape, jnp.bfloat16),
+        in_specs=[anywhere] * n_owner,
+        out_specs=anywhere,
+        scratch_shapes=[pltpu.SemaphoreType.DMA((2 * n_owner,))],
+        cost_estimate=pl.CostEstimate(
+            flops=0, bytes_accessed=4 * shape[0] * shape[1], transcendentals=0
+        ),
+    )(*chunks)
+
+
 def fast_counts_kernel(
-    n_owner, n_fine, capacity, main, home, mine_ref, other_ref, gathered, *refs
+    n_owner, n_fine, capacity, main, home, mine_ref, other_ref, rest_mine, rest_other, *refs
 ):
-    out_ref, unfit_ref, rows_ref, lab_lane, lab_sub, bias, result, sems = refs
+    out_ref, unfit_ref, lab_lane, lab_sub, bias, result, score_a, score_b = refs
     per_owner = n_fine // n_owner
     rest = capacity - main
     n_main, n_rest = n_owner * main, n_owner * rest
-    total = n_main + n_rest
-    grp = lax.axis_index("grp")
     me = lax.axis_index("cl")
     is_home = me == home
-    copies = [
-        pltpu.make_async_copy(
-            gathered.at[pl.ds((2 * k + lax.rem(grp + member, 2)) * (rest + INFO), rest)],
-            rows_ref.at[pl.ds(member * n_rest + k * rest, rest)],
-            sems.at[member * n_owner + k],
-        )
-        for member in range(2)
-        for k in range(n_owner)
-    ]
-
-    @pl.when(is_home)
-    def _():
-        for copy in copies:
-            copy.start()
-
-    def info_of(line):
-        start = pl.multiple_of(line * (rest + INFO) + rest, INFO)
-        return gathered[pl.ds(start, INFO), :LANES][:1].astype(jnp.float32)
+    mains, rests = (mine_ref, other_ref), (rest_mine, rest_other)
+
+    def info_of(member, k):
+        in_main = mains[member][(k + 1) * main - INFO : (k + 1) * main, :LANES]
+        start = n_rest + k * INFO
+        in_rest = rests[member][start : start + INFO, :LANES]
+        in_main = in_main.astype(jnp.float32)[INFO - 1 :]
+        return jnp.where(is_home, in_rest.astype(jnp.float32)[INFO - 1 :], in_main)
 
     lane = lax.broadcasted_iota(jnp.int32, (1, LANES), 1)
-    hot = jnp.max(jnp.where(lane == n_fine, info_of(0), 0.0), axis=1, keepdims=True)
+    hot = jnp.max(jnp.where(lane == n_fine, info_of(0, 0), 0.0), axis=1, keepdims=True)
     hot = hot.astype(jnp.int32)
     lane_cluster = lax.div(lane, per_owner)
     is_edge = lane_cluster == swapped(me, hot, home)
@@ -357,8 +393,8 @@
     unfit = jnp.zeros((1, LANES), jnp.float32)
     for member in range(2):
         for k in range(n_owner):
-            info = info_of(2 * k + lax.rem(grp + member, 2))
-            wrong = (last & (info > main)) | ((lane == n_fine) & (info != hot.astype(jnp.float32)))
+            info = info_of(member, k)
+            wrong = (last & (info >= main)) | ((lane == n_fine) & (info != hot.astype(jnp.float32)))
             unfit = unfit + jnp.where(wrong, 1.0, 0.0)
             edges = jnp.where(is_edge, info, 2.0 * capacity)
 
@@ -394,14 +430,17 @@
 
     near = [(mine_ref, s, s, d) for s, d in pieces(0, n_main, 2)]
     near += [(other_ref, s, s + n_main, d) for s, d in pieces(0, n_main, 2)]
-    far = [(rows_ref, s, s + 2 * n_main, d) for s, d in pieces(0, 2 * n_rest, 4)]
+    far = [(rest_mine, s, s + 2 * n_main, d) for s, d in pieces(0, n_rest, 2)]
+    far += [(rest_other, s, s + 2 * n_main + n_rest, d) for s, d in pieces(0, n_rest, 2)]
+    step = 32
 
     def sums(rows_i, label_i, tiles):
         wide = rows_i.shape[0]
-
-        def scores_of(tile):
+        repeat = wide // LANES
+
+        def scores_to(buffer, tile):
             ref, start, _, deep = tile
-            return lax.dot_general(
+            buffer[:deep, :wide] = lax.dot_general(
                 ref[start : start + deep, :],
                 rows_i,
                 (((1,), (1,)), ((), ())),
@@ -409,16 +448,19 @@
             )
 
         acc = jnp.zeros((8, wide), jnp.float32)
-        ahead = scores_of(tiles[0])
+        here, ahead = score_a, score_b
+        scores_to(here, tiles[0])
         for i, (_, _, place, deep) in enumerate(tiles):
-            scores = ahead
             if i + 1 < len(tiles):
-                ahead = scores_of(tiles[i + 1])
-            label_j = jnp.concatenate([lab_sub[place : place + deep, :]] * (wide // LANES), axis=1)
-            bias_j = jnp.concatenate([bias[place : place + deep, :]] * (wide // LANES), axis=1)
-            shift = jnp.where(label_j == label_i, -SCALE, bias_j)
-            terms = jnp.exp2(scores * SCALE + shift)
-            acc = acc + jnp.sum(terms.reshape(deep // 8, 8, wide), axis=0)
+                scores_to(ahead, tiles[i + 1])
+            for c in range(0, deep, step):
+                part = slice(place + c, place + c + step)
+                label_j = jnp.concatenate([lab_sub[part, :]] * repeat, axis=1)
+                bias_j = jnp.concatenate([bias[part, :]] * repeat, axis=1)
+                shift = jnp.where(label_j == label_i, -SCALE, bias_j)
+                terms = jnp.exp2(here[c : c + step, :wide] * SCALE + shift)
+                acc = acc + jnp.sum(terms.reshape(step // 8, 8, wide), axis=0)
+            here, ahead = ahead, here
         return jnp.sum(acc, axis=0, keepdims=True)
 
     def block(ref, start, wide, to):
@@ -445,11 +487,9 @@
 
     @pl.when(is_home)
     def _():
-        for copy in copies:
-            copy.wait()
         each_block(mine_ref, n_main, 0, block_far)
-        each_block(rows_ref, n_rest, n_main, block)
-        each_block(rows_ref, n_rest, n_main, block_far)
+        each_block(rest_mine, n_rest, n_main, block)
+        each_block(rest_mine, n_rest, n_main, block_far)
 
     values = jnp.log(jnp.where(lab_lane[...] >= 0, result[...], 1.0))
     for k in range(n_owner):
@@ -457,10 +497,9 @@
         out_ref[k, :, main:] = values[:, n_main + k * rest : n_main + (k + 1) * rest]
 
 
-def fast_counts(mine, other, gathered, n_owner, n_fine, capacity, main, home):
-    width = mine.shape[1]
+def fast_counts(arrays, n_owner, n_fine, capacity, main, home):
     total = n_owner * capacity
-    n_rest = n_owner * (capacity - main)
+    n_main = n_owner * main
     vmem = pl.BlockSpec(memory_space=pltpu.VMEM)
     return pl.pallas_call(
         functools.partial(fast_counts_kernel, n_owner, n_fine, capacity, main, home),
@@ -468,18 +507,18 @@
             jax.ShapeDtypeStruct((n_owner, 1, capacity), jnp.float32),
             jax.ShapeDtypeStruct((8, LANES), jnp.int32),
         ),
-        in_specs=[vmem] * 3,
+        in_specs=[vmem] * 4,
         out_specs=(vmem, vmem),
         scratch_shapes=[
-            pltpu.VMEM((2 * n_rest, width), jnp.bfloat16),
             pltpu.VMEM((1, total), jnp.float32),
             pltpu.VMEM((2 * total, LANES), jnp.float32),
             pltpu.VMEM((2 * total, LANES), jnp.float32),
             pltpu.VMEM((1, total), jnp.float32),
-            pltpu.SemaphoreType.DMA((2 * n_owner,)),
+            pltpu.VMEM((n_main // 2, 256), jnp.float32),
+            pltpu.VMEM((n_main // 2, 256), jnp.float32),
         ],
         compiler_params=pltpu.CompilerParams(vmem_limit_bytes=FAST_LIMIT),
-    )(mine, other, gathered)
+    )(*arrays)
 
 
 def fast_unpack_kernel(values_ref, pos_ref, out_ref):
@@ -534,12 +573,18 @@
     home = n_owner // 4
     width = embeddings.shape[1]
     packed, extra, pos = fast_pack(embeddings, labels, owner_map, n_owner, capacity, main, home)
-    gathered = lax.all_gather(extra, ("cl", "grp"), tiled=True)
+    rest = capacity - main
+    chunks = [extra]
+    chunks += [lax.ppermute(extra, "cl", [(home ^ k, home)]) for k in range(1, n_owner)]
+    rest_mine = gather_rest(chunks, n_owner, rest, home)
+    pairs = [(2 * home, 2 * home + 1), (2 * home + 1, 2 * home)]
+    rest_other = lax.ppermute(rest_mine, ("cl", "grp"), pairs)
     mine = lax.all_to_all(
         packed.reshape(n_owner, main, width), "cl", split_axis=0, concat_axis=0, tiled=True
     ).reshape(n_owner * main, width)
     other = lax.ppermute(mine, "grp", [(0, 1), (1, 0)])
-    results, unfit = fast_counts(mine, other, gathered, n_owner, n_fine, capacity, main, home)
+    arrays = (mine, other, rest_mine, rest_other)
+    results, unfit = fast_counts(arrays, n_owner, n_fine, capacity, main, home)
     returned = lax.all_to_all(results, "cl", split_axis=0, concat_axis=0, tiled=True)
     return lax.cond(
         unfit[0, 0] == 0,

time: 128 us -> 164 us (1.28)
  starting transfers between devices: 20.6 us -> 138 us
  blocking collectives: 67.4 us -> 0 us
  between operations: 14.1 us -> 0.76 us
    all_to_all x1 -> x0, blocking collectives: 67.4 us -> none  [body(): lax.all_to_all(packed.reshape(n_owner, main, width), 'cl', split_axis=0,...]
    ppermute x0 -> x8, starting transfers between devices: none -> 57.6 us  [the longest x7 56.9 us: body(): lax.ppermute(extra, 'cl', [(home ^ k, home)])]
    all_to_all x1, starting transfers between devices: 20.6 us -> 72.6 us  [body(): lax.all_to_all(results, 'cl', split_axis=0, concat_axis=0, tiled=True)]
    all_to_all x0 -> x1, starting transfers between devices: none -> 7.29 us  [body(): lax.all_to_all(packed.reshape(n_owner, main, width), 'cl', split_axis=0,...]
    ppermute x1, waiting for transfers between devices: 3.69 us -> 1.16 us  [body(): other = lax.ppermute(mine, 'grp', [(0, 1), (1, 0)])]
  transfers between devices with their start and end apart: 3 -> 11, of which waited for: 2 -> 3; matrix products, arithmetic and copies ran while one was open for 0% -> 0% of each run, Pallas kernels for 0% -> 0%
where the time goes in v4:
time: 164 us
  starting transfers between devices  138 us (84%)
  Pallas kernels  14.9 us (9%)
  waiting for transfers between devices  8.09 us (5%)
  local copies, waits for them, and re-layouts  2.52 us (2%)
    all_to_all x1, starting transfers between devices, body(): lax.all_to_all(results, 'cl', split_axis=0, concat_axis=0, tiled=True)  72.6 us
    ppermute x7, starting transfers between devices, body(): lax.ppermute(extra, 'cl', [(home ^ k, home)])  56.9 us
    pallas_call x1, Pallas kernels, fast_counts(): pl.pallas_call(functools.partial(fast_counts_kernel, n_owner, n_fine, cap...  8.67 us
    all_to_all x1, starting transfers between devices, body(): lax.all_to_all(packed.reshape(n_owner, main, width), 'cl', split_axis=0,...  7.29 us
    pallas_call x1, Pallas kernels, fast_pack(): pl.pallas_call(functools.partial(fast_pack_kernel, n_owner, capacity, mai...  5.96 us
    all_to_all x1, waiting for transfers between devices, body(): lax.all_to_all(results, 'cl', split_axis=0, concat_axis=0, tiled=True)  5.35 us
  transfers between devices with their start and end apart: 11, of which 3 were waited for; matrix products, arithmetic and copies ran while one was open for 0% of the time, Pallas kernels for 0%

profile of v4, /device:TPU:0, one launch (start us, length us, event | category | flops | bytes accessed | tf_op | source)
XLA Modules:
  0.0 163.8 jit_solution(9891398452092445700)
XLA Ops:
  0.0 6.0 %shard_map.39 = (bf16[1152,768]{1,0:T(8,128)(2,1)}, bf16[128,768]{1,0:T(8,128)(2,1)}, s32[8,128]{1,0:T(8,128)S(1)}) custom-call(bf16[1024,768]{1,0:T(8,128)(2,1)} %x_hbm.1, s32[8,128]{1,0:T(8,128)} %bitcast.24, s32[1,64]{1,0:T(1,128)} %bitcast.28), custom_call_target="tpu_custom_call" | custom-call | tf_op jit(solution)/shard_map/pallas_call | solution.py:303
  6.0 7.3 %all-to-all-start.2 = ((bf16[8,144,768]{2,1,0:T(8,128)(2,1)}), bf16[8,144,768]{2,1,0:T(8,128)(2,1)S(1)}, u32[]{:S(2)}, u32[]{:S(2)}) async-start(bf16[8,144,768]{2,1,0:T(8,128)(2,1)} %bitcast.12), calls=%async_computation.2 | async-start | bytes 3538944 | tf_op jit(solution)/shard_map/all_to_all | solution.py:582
  13.3 0.7 collective-permute-start.8
  13.9 0.7 collective-permute-start.7
  14.6 1.3 collective-permute-start.6
  16.0 1.3 collective-permute-start.5
  17.3 1.3 collective-permute-start.4
  18.6 0.0 collective-permute-done.8.refs_7_
  18.6 0.0 copy-start.3
  18.6 50.2 %collective-permute-start.3 = (bf16[128,768]{1,0:T(8,128)(2,1)}, bf16[128,768]{1,0:T(8,128)(2,1)}, u32[]{:S(2)}, u32[]{:S(2)}) collective-permute-start(bf16[128,768]{1,0:T(8,128)(2,1)} %get-tuple-element.32.refs_0_), channel_id=1, source_target_pairs={{0,4},{1,5},{16,20},{17,21}} | collective-permute-start | bytes 589832 | tf_op jit(solution)/shard_map/ppermute | solution.py:578
  68.8 0.0 collective-permute-done.7.refs_6_
  68.8 0.0 copy-start.4
  68.8 1.3 collective-permute-start.2
  70.1 0.0 copy-done.3
  70.1 0.0 copy-done.4
  70.1 0.0 collective-permute-done.6.refs_5_
  70.1 0.0 all-to-all-done.2
  70.2 0.1 collective-permute-start.1
  70.2 0.0 collective-permute-done.5.refs_4_
  70.2 0.0 collective-permute-done.4.refs_3_
  70.3 1.6 collective-permute-done.3.refs_2_
  71.8 0.0 collective-permute-done.2.refs_1_
  71.8 0.0 copy-start.5
  71.8 0.0 copy-start.7
  71.8 0.1 shard_map.40.rest_mine
  72.0 0.8 collective-permute-start.9
  72.7 0.0 collective-permute-done.9.rest_other
  72.7 1.2 collective-permute-done.1.other_ref
  73.9 0.0 copy-start
  73.9 1.4 copy-done
  75.3 8.7 %shard_map.41 = (f32[8,1,256]{2,1,0:T(1,128)}, s32[8,128]{1,0:T(8,128)S(1)}) custom-call(bf16[1152,768]{1,0:T(8,128)(2,1)S(1)} %bitcast.18, bf16[1152,768]{1,0:T(8,128)(2,1)S(1)} %collective-permute-done.1.other_ref, bf16[1024,768]{1,0:T(8,128)(2,1)S(1)} %copy-done, bf16[1024,768]{1,0:T(8,128)(2,1)S(1)} %collective-permute-done.9.rest_other), custom_call_target="tpu_custom_call" | custom-call | tf_op jit(solution)/shard_map/pallas_call | solution.py:504
  84.0 72.6 %all-to-all-start.3 = ((f32[8,1,256]{2,1,0:T(1,128)}), f32[8,1,256]{2,1,0:T(1,128)S(1)}, u32[]{:S(2)}, u32[]{:S(2)}) async-start(f32[8,1,256]{2,1,0:T(1,128)} %get-tuple-element.34), calls=%async_computation.3 | async-start | bytes 16384 | tf_op jit(solution)/shard_map/all_to_all | solution.py:588
  156.6 0.5 slice.3
  157.7 5.4 %all-to-all-done.3 = f32[8,1,256]{2,1,0:T(1,128)S(1)} async-done(((f32[8,1,256]{2,1,0:T(1,128)}), f32[8,1,256]{2,1,0:T(1,128)S(1)}, u32[]{:S(2)}, u32[]{:S(2)}) %all-to-all-start.3) | async-done | bytes 8224 | tf_op jit(solution)/shard_map/all_to_all | solution.py:588
  163.1 0.0 copy-done.5
  163.1 0.0 copy-done.7
  163.1 0.1 conditional.1
  163.1 0.1 branch_1_fun.1
  163.2 0.0 copy-start.6
  163.2 0.6 copy-done.6
Async XLA Ops:
  6.0 64.2 %all-to-all-start.2 = ((bf16[8,144,768]{2,1,0:T(8,128)(2,1)}), bf16[8,144,768]{2,1,0:T(8,128)(2,1)S(1)}, u32[]{:S(2)}, u32[]{:S(2)}) async-start(bf16[8,144,768]{2,1,0:T(8,128)(2,1)} %bitcast.12), calls=%async_computation.2 | async-start | bytes 3538944 | tf_op jit(solution)/shard_map/all_to_all | solution.py:582
  13.3 5.4 %collective-permute-start.8 = (bf16[128,768]{1,0:T(8,128)(2,1)}, bf16[128,768]{1,0:T(8,128)(2,1)S(1)}, u32[]{:S(2)}, u32[]{:S(2)}) collective-permute-start(bf16[128,768]{1,0:T(8,128)(2,1)} %get-tuple-element.32.refs_0_), channel_id=1, source_target_pairs={{10,4},{11,5},{26,20},{27,21}} | collective-permute-start | bytes 589832 | tf_op jit(solution)/shard_map/ppermute | solution.py:578
  13.9 54.9 %collective-permute-start.7 = (bf16[128,768]{1,0:T(8,128)(2,1)}, bf16[128,768]{1,0:T(8,128)(2,1)S(1)}, u32[]{:S(2)}, u32[]{:S(2)}) collective-permute-start(bf16[128,768]{1,0:T(8,128)(2,1)} %get-tuple-element.32.refs_0_), channel_id=1, source_target_pairs={{8,4},{9,5},{24,20},{25,21}} | collective-permute-start | bytes 589832 | tf_op jit(solution)/shard_map/ppermute | solution.py:578
  14.6 55.5 %collective-permute-start.6 = (bf16[128,768]{1,0:T(8,128)(2,1)}, bf16[128,768]{1,0:T(8,128)(2,1)}, u32[]{:S(2)}, u32[]{:S(2)}) collective-permute-start(bf16[128,768]{1,0:T(8,128)(2,1)} %get-tuple-element.32.refs_0_), channel_id=1, source_target_pairs={{14,4},{15,5},{30,20},{31,21}} | collective-permute-start | bytes 589832 | tf_op jit(solution)/shard_map/ppermute | solution.py:578
  16.0 54.3 %collective-permute-start.5 = (bf16[128,768]{1,0:T(8,128)(2,1)}, bf16[128,768]{1,0:T(8,128)(2,1)}, u32[]{:S(2)}, u32[]{:S(2)}) collective-permute-start(bf16[128,768]{1,0:T(8,128)(2,1)} %get-tuple-element.32.refs_0_), channel_id=1, source_target_pairs={{12,4},{13,5},{28,20},{29,21}} | collective-permute-start | bytes 589832 | tf_op jit(solution)/shard_map/ppermute | solution.py:578
  17.3 52.9 %collective-permute-start.4 = (bf16[128,768]{1,0:T(8,128)(2,1)}, bf16[128,768]{1,0:T(8,128)(2,1)}, u32[]{:S(2)}, u32[]{:S(2)}) collective-permute-start(bf16[128,768]{1,0:T(8,128)(2,1)} %get-tuple-element.32.refs_0_), channel_id=1, source_target_pairs={{2,4},{3,5},{18,20},{19,21}} | collective-permute-start | bytes 589832 | tf_op jit(solution)/shard_map/ppermute | solution.py:578
  18.6 51.5 %copy-start.3 = (bf16[128,768]{1,0:T(8,128)(2,1)}, bf16[128,768]{1,0:T(8,128)(2,1)S(1)}, u32[]{:S(2)}) copy-start(bf16[128,768]{1,0:T(8,128)(2,1)S(1)} %collective-permute-done.8.refs_7_) | copy-start | bytes 589828
  18.6 53.2 %collective-permute-start.3 = (bf16[128,768]{1,0:T(8,128)(2,1)}, bf16[128,768]{1,0:T(8,128)(2,1)}, u32[]{:S(2)}, u32[]{:S(2)}) collective-permute-start(bf16[128,768]{1,0:T(8,128)(2,1)} %get-tuple-element.32.refs_0_), channel_id=1, source_target_pairs={{0,4},{1,5},{16,20},{17,21}} | collective-permute-start | bytes 589832 | tf_op jit(solution)/shard_map/ppermute | solution.py:578
  68.8 1.3 copy-start.4
  68.8 3.0 %collective-permute-start.2 = (bf16[128,768]{1,0:T(8,128)(2,1)}, bf16[128,768]{1,0:T(8,128)(2,1)}, u32[]{:S(2)}, u32[]{:S(2)}) collective-permute-start(bf16[128,768]{1,0:T(8,128)(2,1)} %get-tuple-element.32.refs_0_), channel_id=1, source_target_pairs={{6,4},{7,5},{22,20},{23,21}} | collective-permute-start | bytes 589832 | tf_op jit(solution)/shard_map/ppermute | solution.py:578
  70.2 3.8 %collective-permute-start.1 = (bf16[1152,768]{1,0:T(8,128)(2,1)S(1)}, bf16[1152,768]{1,0:T(8,128)(2,1)S(1)}, u32[]{:S(2)}, u32[]{:S(2)}) collective-permute-start(bf16[1152,768]{1,0:T(8,128)(2,1)S(1)} %bitcast.17), channel_id=1, source_target_pairs={{0,1},{1,0},{2,3},{3,2},{4,5},{5,4},{6,7},{7,6},{8,9},{9,8},{10,11... | collective-permute-start | bytes 5308424 | tf_op jit(solution)/shard_map/ppermute | solution.py:585
  71.8 91.3 %copy-start.5 = (s32[1024]{0:T(1024)S(1)}, s32[1024]{0:T(1024)}, u32[]{:S(2)}) copy-start(s32[1024]{0:T(1024)} %param.6) | copy-start | bytes 12292
  71.8 91.3 %copy-start.7 = (s32[64]{0:T(128)S(1)}, s32[64]{0:T(128)}, u32[]{:S(2)}) copy-start(s32[64]{0:T(128)} %param.7) | copy-start | bytes 772
  72.0 0.8 collective-permute-start.9
  73.9 1.4 copy-start
  84.0 79.1 %all-to-all-start.3 = ((f32[8,1,256]{2,1,0:T(1,128)}), f32[8,1,256]{2,1,0:T(1,128)S(1)}, u32[]{:S(2)}, u32[]{:S(2)}) async-start(f32[8,1,256]{2,1,0:T(1,128)} %get-tuple-element.34), calls=%async_computation.3 | async-start | bytes 16384 | tf_op jit(solution)/shard_map/all_to_all | solution.py:588
  163.2 0.6 copy-start.6

commit v5 on v1

--- a/solution.py
+++ b/solution.py
@@ -19,6 +19,8 @@
 NEIGHBOUR = math.log2(neighbour_factor)
 DEAD = -1e30
 VMEM_LIMIT = 48 * 1024 * 1024
+FAST_LIMIT = 40 * 1024 * 1024
+INFO = 16
 
 
 def column_of(row):
@@ -211,7 +213,503 @@
     )(values.reshape(-1, LANES), pos)
 
 
-def body(embeddings, labels, owner_map):
+def pieces(start, count, parts):
+    return [(start + i * (count // parts), count // parts) for i in range(parts)]
+
+
+def swapped(x, first, second):
+    return jnp.where(x == first, second, jnp.where(x == second, first, x))
+
+
+def place_kernel(n_owner, capacity, main, home, x_hbm, lab_hbm, map_hbm, *refs):
+    unit, slot_ref, info_ref, extra_ref, pos_ref, x_ref, lab_ref, map_ref, sems = refs
+    copies = [
+        pltpu.make_async_copy(src, dst, sems.at[i])
+        for i, (src, dst) in enumerate(((x_hbm, x_ref), (lab_hbm, lab_ref), (map_hbm, map_ref)))
+    ]
+    for copy in copies:
+        copy.start()
+    rows = x_ref.shape[0]
+    n_fine = map_ref.shape[1]
+    per_owner = n_fine // n_owner
+    rest = capacity - main
+    copies[1].wait()
+    copies[2].wait()
+    owner_row = map_ref[...].astype(jnp.float32)
+    fine_row = lax.broadcasted_iota(jnp.int32, (1, n_fine), 1).astype(jnp.float32)
+    key_row = owner_row * n_fine + fine_row
+    key_col = column_of(key_row)
+    sorted_col = jnp.sum(jnp.where(key_row < key_col, 1.0, 0.0), axis=1, keepdims=True)
+    lab = lab_ref[...].astype(jnp.float32)
+    lab_row = jnp.concatenate([lab[b : b + 1, :] for b in range(lab.shape[0])], axis=1)
+    fine_col = lax.broadcasted_iota(jnp.int32, (n_fine, rows), 0).astype(jnp.float32)
+    fine_id = jnp.sum(jnp.where(fine_col == lab_row, sorted_col, 0.0), axis=0, keepdims=True)
+    counts_col = jnp.sum(jnp.where(fine_col == fine_id, 1.0, 0.0), axis=1, keepdims=True)
+    coarse = jnp.floor((fine_id + 0.5) * (1.0 / per_owner))
+    first = coarse * per_owner
+    before = jnp.sum(jnp.where(fine_col < first, counts_col, 0.0), axis=0, keepdims=True)
+    upto = jnp.sum(jnp.where(fine_col < first + per_owner, counts_col, 0.0), axis=0, keepdims=True)
+    full = jnp.min(
+        jnp.where(upto - before == capacity, coarse, float(n_owner)), axis=1, keepdims=True
+    )
+    line = lax.broadcasted_iota(jnp.int32, (n_fine, LANES), 0)
+    lane = lax.broadcasted_iota(jnp.int32, (n_fine, LANES), 1)
+    inside = (line <= lane) & (lax.div(line, per_owner) == lax.div(lane, per_owner))
+    running = jnp.sum(jnp.where(inside, counts_col, 0.0), axis=0, keepdims=True)
+    info = jnp.where(lane[:1] < n_fine, running, full)
+    info_ref[...] = info
+    index = lax.broadcasted_iota(jnp.int32, (1, rows), 1).astype(jnp.float32)
+    row_key = fine_id * rows + index
+    rank = jnp.zeros((1, rows), jnp.float32)
+    for start in range(0, rows, LANES):
+        other = column_of(row_key[:, start : start + LANES])
+        rank = rank + jnp.sum(jnp.where(other < row_key, 1.0, 0.0), axis=0, keepdims=True)
+    rank = (rank - before).astype(jnp.int32)
+    place = swapped(coarse.astype(jnp.int32), full.astype(jnp.int32), home)
+    table = place * capacity + rank
+    pos_ref[...] = jnp.concatenate(
+        [table[:, start : start + LANES] for start in range(0, rows, LANES)], axis=0
+    )
+    later = jnp.where(place == home, n_owner * main + rank - main, -1)
+    fits = rank < jnp.where(place == home, main, main - 1)
+    slot = jnp.where(fits, place * main + rank, later)
+    slot_ref[...] = slot
+    copies[0].wait()
+    x = x_ref[...].astype(jnp.float32)
+    squares = jnp.sum(x * x, axis=1, keepdims=True)
+    unit[...] = (x * lax.rsqrt(squares + epsilon)).astype(jnp.bfloat16)
+    extra_ref[:rest, :] = chosen_rows(unit, slot, n_owner * main, rest)
+    extra_ref[rest:, :] = jnp.zeros((INFO, extra_ref.shape[1]), jnp.bfloat16)
+    extra_ref[rest:, :LANES] = jnp.broadcast_to(info, (INFO, LANES)).astype(jnp.bfloat16)
+
+
+def chosen_rows(unit, slot, start, count):
+    here = lax.broadcasted_iota(jnp.int32, (count, unit.shape[0]), 0) + start
+    chosen = jnp.where(here == slot, 1.0, 0.0).astype(jnp.bfloat16)
+    return jnp.dot(chosen, unit[...], preferred_element_type=jnp.float32).astype(jnp.bfloat16)
+
+
+def main_kernel(n_owner, main, home, unit, slot_ref, info_ref, main_ref):
+    count = n_owner * main // 4
+    for start in range(0, n_owner * main, count):
+        main_ref[start : start + count, :] = chosen_rows(unit, slot_ref[...], start, count)
+    for owner in range(n_owner):
+        if owner != home:
+            tail = slice((owner + 1) * main - INFO, (owner + 1) * main)
+            old = main_ref[tail, :LANES].astype(jnp.float32)
+            down = lax.broadcasted_iota(jnp.int32, old.shape, 0)
+            new = jnp.where(down == INFO - 1, info_ref[...], old)
+            main_ref[tail, :LANES] = new.astype(jnp.bfloat16)
+
+
+def vmem_specs(count):
+    return (pl.BlockSpec(memory_space=pltpu.VMEM),) * count
+
+
+def place_rows(embeddings, labels, owner_map, n_owner, capacity, main, home):
+    rows, width = embeddings.shape
+    n_fine = owner_map.shape[0]
+    lab_shape = (rows // LANES, LANES)
+    return pl.pallas_call(
+        functools.partial(place_kernel, n_owner, capacity, main, home),
+        out_shape=(
+            jax.ShapeDtypeStruct((rows, width), jnp.bfloat16),
+            jax.ShapeDtypeStruct((1, rows), jnp.int32),
+            jax.ShapeDtypeStruct((1, LANES), jnp.float32),
+            jax.ShapeDtypeStruct((capacity - main + INFO, width), jnp.bfloat16),
+            jax.ShapeDtypeStruct(lab_shape, jnp.int32),
+        ),
+        in_specs=[pl.BlockSpec(memory_space=pl.ANY)] * 3,
+        out_specs=vmem_specs(5),
+        scratch_shapes=[
+            pltpu.VMEM((rows, width), jnp.bfloat16),
+            pltpu.VMEM(lab_shape, jnp.int32),
+            pltpu.VMEM((1, n_fine), jnp.int32),
+            pltpu.SemaphoreType.DMA((3,)),
+        ],
+        compiler_params=pltpu.CompilerParams(vmem_limit_bytes=FAST_LIMIT),
+    )(embeddings, labels.reshape(lab_shape), owner_map.reshape(1, n_fine))
+
+
+def pack_main(unit, slot, info, n_owner, main, home):
+    return pl.pallas_call(
+        functools.partial(main_kernel, n_owner, main, home),
+        out_shape=jax.ShapeDtypeStruct((n_owner * main, unit.shape[1]), jnp.bfloat16),
+        in_specs=list(vmem_specs(3)),
+        out_specs=vmem_specs(1)[0],
+        compiler_params=pltpu.CompilerParams(vmem_limit_bytes=FAST_LIMIT),
+        cost_estimate=pl.CostEstimate(
+            flops=2 * n_owner * main * unit.shape[0] * unit.shape[1],
+            bytes_accessed=4 * unit.shape[0] * unit.shape[1],
+            transcendentals=0,
+        ),
+    )(unit, slot, info)
+
+
+def gather_kernel(rest, plane, *refs):
+    chunks, out = refs[:-1], refs[-1]
+
+    @pl.when(lax.div(lax.axis_index("cl"), 2) == plane)
+    def _():
+        for z, chunk in enumerate(chunks):
+            out[z * rest : (z + 1) * rest, :] = chunk[:rest, :]
+            start = len(chunks) * rest + z * INFO
+            out[start : start + INFO, :] = chunk[rest:, :]
+
+
+def gather_rest(chunks, rest, plane):
+    shape = (len(chunks) * (rest + INFO), chunks[0].shape[1])
+    return pl.pallas_call(
+        functools.partial(gather_kernel, rest, plane),
+        out_shape=jax.ShapeDtypeStruct(shape, jnp.bfloat16),
+        in_specs=list(vmem_specs(len(chunks))),
+        out_specs=vmem_specs(1)[0],
+        cost_estimate=pl.CostEstimate(
+            flops=0, bytes_accessed=4 * shape[0] * shape[1], transcendentals=0
+        ),
+    )(*chunks)
+
+
+class Layout:
+    def __init__(self, n_owner, n_fine, capacity, main, home):
+        self.n_owner, self.n_fine, self.capacity = n_owner, n_fine, capacity
+        self.main, self.home = main, home
+        self.rest = capacity - main
+        self.per_owner = n_fine // n_owner
+        self.planes = n_owner // 2
+        self.n_main = n_owner * main
+        self.n_rest = self.planes * self.rest
+        self.rest_lines = self.planes * (self.rest + INFO)
+        self.total = self.n_main + 2 * self.rest_lines
+
+    def rest_at(self, y):
+        return self.n_main + y * self.rest_lines
+
+
+def info_line(lay, is_home, main_ref, rest_refs, source):
+    in_main = main_ref[(source + 1) * lay.main - INFO : (source + 1) * lay.main, :LANES]
+    z, y = source // 2, source % 2
+    start = lay.n_rest + z * INFO
+    in_rest = rest_refs[y][start : start + INFO, :LANES]
+    in_main = in_main.astype(jnp.float32)[INFO - 1 :]
+    return jnp.where(is_home, in_rest.astype(jnp.float32)[INFO - 1 :], in_main)
+
+
+def write_labels(lay, infos, cluster, is_home, lab_sub, bias):
+    lane = lax.broadcasted_iota(jnp.int32, (1, LANES), 1)
+    is_edge = lax.div(lane, lay.per_owner) == cluster
+    for source, info in enumerate(infos):
+        edges = jnp.where(is_edge, info, 2.0 * lay.capacity)
+
+        def write(start, first, count, edges=edges):
+            slot = lax.broadcasted_iota(jnp.int32, (count, LANES), 0) + first
+            label = jnp.where(slot.astype(jnp.float32) >= edges, 1.0, 0.0)
+            label = jnp.broadcast_to(jnp.sum(label, axis=1, keepdims=True), (count, LANES))
+            lab_sub[start : start + count, :] = label
+            bias[start : start + count, :] = jnp.where(
+                label < lay.per_owner, NEIGHBOUR - SCALE, DEAD
+            )
+
+        write(source * lay.main, 0, lay.main)
+
+        @pl.when(is_home)
+        def _(source=source, write=write):
+            start = lay.rest_at(source % 2) + source // 2 * lay.rest
+            write(start, lay.main, lay.rest)
+
+    @pl.when(is_home)
+    def _():
+        for y in range(2):
+            start = lay.rest_at(y) + lay.n_rest
+            lab_sub[start : start + lay.rest_lines - lay.n_rest, :] = jnp.full(
+                (lay.rest_lines - lay.n_rest, LANES), float(lay.per_owner), jnp.float32
+            )
+
+
+def hot_of(lay, info):
+    lane = lax.broadcasted_iota(jnp.int32, (1, LANES), 1)
+    hot = jnp.max(jnp.where(lane == lay.n_fine, info, 0.0), axis=1, keepdims=True)
+    return hot.astype(jnp.int32)
+
+
+def pair_sums(rows_i, label_i, tiles, buffers):
+    wide = rows_i.shape[0]
+    repeat = wide // LANES
+    dead_i = jnp.where(label_i >= 0, 0.0, DEAD)
+    step = 32
+
+    def scores_to(buffer, tile):
+        ref, start, deep = tile[:3]
+        buffer[:deep, :wide] = lax.dot_general(
+            ref[start : start + deep, :],
+            rows_i,
+            (((1,), (1,)), ((), ())),
+            preferred_element_type=jnp.float32,
+        )
+
+    acc = jnp.zeros((8, wide), jnp.float32)
+    here, ahead = buffers
+    scores_to(here, tiles[0])
+    for i, (_, _, deep, lab_sub, bias, place, back) in enumerate(tiles):
+        if i + 1 < len(tiles):
+            scores_to(ahead, tiles[i + 1])
+        for c in range(0, deep, step):
+            part = slice(place + c, place + c + step)
+            label_j = jnp.concatenate([lab_sub[part, :]] * repeat, axis=1)
+            bias_j = jnp.concatenate([bias[part, :]] * repeat, axis=1)
+            if back is not None:
+                bias_j = bias_j + dead_i
+            shift = jnp.where(label_j == label_i, -SCALE, bias_j)
+            terms = jnp.exp2(here[c : c + step, :wide] * SCALE + shift)
+            acc = acc + jnp.sum(terms.reshape(step // 8, 8, wide), axis=0)
+            if back is not None:
+                across = terms[:, :LANES]
+                for r in range(1, repeat):
+                    across = across + terms[:, r * LANES : (r + 1) * LANES]
+                back[part, :] += across
+        here, ahead = ahead, here
+    return jnp.sum(acc, axis=0, keepdims=True)
+
+
+def each_block(count, run):
+    wide = 256
+    full = count // wide
+
+    @pl.loop(0, full)
+    def _(i):
+        run(pl.multiple_of(i * wide, wide), wide)
+
+    if count % wide:
+        run(full * wide, count % wide)
+
+
+def row_sums(back, start, count):
+    ones = jnp.ones((8, LANES), jnp.float32)
+    sums = lax.dot_general(
+        ones,
+        back[start : start + count, :],
+        (((1,), (1,)), ((), ())),
+        precision=lax.Precision.HIGHEST,
+        preferred_element_type=jnp.float32,
+    )
+    return sums[:1]
+
+
+def inner_kernel(lay, mine, rest_a, rest_b, sums, lab_lane, lab_sub, bias, back, buf_a, buf_b):
+    me = lax.axis_index("cl")
+    is_home = me == lay.home
+    rests = (rest_a, rest_b)
+    infos = [info_line(lay, is_home, mine, rests, s) for s in range(lay.n_owner)]
+    cluster = swapped(me, hot_of(lay, infos[0]), lay.home)
+    write_labels(lay, infos, cluster, is_home, lab_sub, bias)
+
+    def turn(start, count):
+        for i in range(start, start + count, LANES):
+            block = jnp.transpose(lab_sub[i : i + LANES, :])[:1]
+            lab_lane[:, i : i + LANES] = jnp.where(block < lay.per_owner, block, -1.0)
+
+    turn(0, lay.n_main)
+    buffers = (buf_a, buf_b)
+    own = [
+        (mine, s, d, lab_sub, bias, s, None) for s, d in pieces(0, lay.n_main, 2)
+    ]
+
+    def main_block(start, wide):
+        place = pl.ds(start, wide)
+        sums[:, place] = pair_sums(mine[place, :], lab_lane[:, place], own, buffers)
+
+    each_block(lay.n_main, main_block)
+
+    @pl.when(is_home)
+    def _():
+        turn(lay.n_main, 2 * lay.rest_lines)
+        n_back = 2 * lay.rest_lines
+        back[lay.n_main : lay.n_main + n_back, :] = jnp.zeros((n_back, LANES), jnp.float32)
+        seconds = [(rests[y], 0, lay.n_rest, lab_sub, bias, lay.rest_at(y), back) for y in (0, 1)]
+
+        def more(start, wide):
+            place = pl.ds(start, wide)
+            sums[:, place] += pair_sums(mine[place, :], lab_lane[:, place], seconds, buffers)
+
+        each_block(lay.n_main, more)
+        among = [tile[:6] + (None,) for tile in seconds]
+        for y in range(2):
+
+            def rest_block(start, wide, y=y):
+                place = pl.ds(start + lay.rest_at(y), wide)
+                rows_i = rests[y][pl.ds(start, wide), :]
+                sums[:, place] = pair_sums(rows_i, lab_lane[:, place], among, buffers)
+
+            each_block(lay.rest_lines, rest_block)
+        place = slice(lay.n_main, lay.n_main + n_back)
+        sums[:, place] += row_sums(back, lay.n_main, n_back)
+
+
+def cross_kernel(lay, *refs):
+    mine, rest_a, rest_b, other, other_a, other_b, lab_lane, sums = refs[:8]
+    out, out_other, unfit_ref, lab_sub, bias, back, buf_a, buf_b = refs[8:]
+    me = lax.axis_index("cl")
+    grp = lax.axis_index("grp")
+    is_home = me == lay.home
+    rests, others = (rest_a, rest_b), (other_a, other_b)
+    infos = [info_line(lay, is_home, other, others, s) for s in range(lay.n_owner)]
+    own = [info_line(lay, is_home, mine, rests, s) for s in range(lay.n_owner)]
+    hot = hot_of(lay, own[0])
+    lane = lax.broadcasted_iota(jnp.int32, (1, LANES), 1)
+    last = (lane < lay.n_fine) & (lax.rem(lane, lay.per_owner) == lay.per_owner - 1)
+    last = last & (lax.div(lane, lay.per_owner) != hot)
+    unfit = jnp.zeros((1, LANES), jnp.float32)
+    for info in infos + own:
+        wrong = last & (info >= lay.main)
+        differs = (info != hot.astype(jnp.float32)) | (info >= lay.n_owner)
+        wrong = wrong | ((lane == lay.n_fine) & differs)
+        unfit = unfit + jnp.where(wrong, 1.0, 0.0)
+    unfit_ref[...] = jnp.broadcast_to(
+        jnp.max(unfit, axis=1, keepdims=True), unfit_ref.shape
+    ).astype(jnp.int32)
+    write_labels(lay, infos, swapped(me, hot, lay.home), is_home, lab_sub, bias)
+    back[: lay.n_main, :] = jnp.zeros((lay.n_main, LANES), jnp.float32)
+    buffers = (buf_a, buf_b)
+    out[...] = sums[...]
+    half = 512
+
+    def main_tiles(low):
+        start, count = (0, half) if low else (half, lay.n_main - half)
+        return [(other, s, d, lab_sub, bias, s, back) for s, d in pieces(start, count, 2)]
+
+    def main_blocks(first, count, low):
+        def run(start, wide):
+            place = pl.ds(first + start, wide)
+            out[:, place] += pair_sums(
+                mine[place, :], lab_lane[:, place], main_tiles(low), buffers
+            )
+
+        each_block(count, run)
+
+    @pl.when(grp == 0)
+    def _():
+        main_blocks(0, half, True)
+        main_blocks(half, lay.n_main - half, False)
+
+    @pl.when(grp == 1)
+    def _():
+        main_blocks(0, half, False)
+        main_blocks(half, lay.n_main - half, True)
+
+    @pl.when(is_home)
+    def _():
+        back[lay.n_main :, :] = jnp.zeros((2 * lay.rest_lines, LANES), jnp.float32)
+        seconds = [(others[y], 0, lay.n_rest, lab_sub, bias, lay.rest_at(y), back) for y in (0, 1)]
+
+        def more(start, wide):
+            place = pl.ds(start, wide)
+            out[:, place] += pair_sums(mine[place, :], lab_lane[:, place], seconds, buffers)
+
+        each_block(lay.n_main, more)
+        for y in range(2):
+            for g in range(2):
+
+                @pl.when(grp == g)
+                def _(y=y, g=g):
+                    ref, _, _, _, _, place_j, _ = seconds[y ^ g]
+                    tiles = [
+                        (ref, s, d, lab_sub, bias, place_j + s, back)
+                        for s, d in pieces(0, lay.n_rest, 2)
+                    ]
+
+                    def run(start, wide):
+                        place = pl.ds(start + lay.rest_at(y), wide)
+                        rows_i = rests[y][pl.ds(start, wide), :]
+                        out[:, place] += pair_sums(rows_i, lab_lane[:, place], tiles, buffers)
+
+                    each_block(lay.rest_lines, run)
+
+        out_other[:, lay.n_main :] = row_sums(back, lay.n_main, 2 * lay.rest_lines)
+
+    out_other[:, : lay.n_main] = row_sums(back, 0, lay.n_main)
+
+
+def join_kernel(lay, sums, more, out_ref):
+    values = jnp.log(sums[...] + more[...])
+    for source in range(lay.n_owner):
+        out_ref[source, :, : lay.main] = values[:, source * lay.main : (source + 1) * lay.main]
+        start = lay.rest_at(source % 2) + source // 2 * lay.rest
+        out_ref[source, :, lay.main :] = values[:, start : start + lay.rest]
+
+
+def inner_sums(lay, mine, rests):
+    row = jax.ShapeDtypeStruct((1, lay.total), jnp.float32)
+    side = pltpu.VMEM((lay.total, LANES), jnp.float32)
+    buffer = pltpu.VMEM((lay.n_main // 2, 256), jnp.float32)
+    return pl.pallas_call(
+        functools.partial(inner_kernel, lay),
+        out_shape=(row, row),
+        in_specs=list(vmem_specs(3)),
+        out_specs=vmem_specs(2),
+        scratch_shapes=[side, side, side, buffer, buffer],
+        compiler_params=pltpu.CompilerParams(vmem_limit_bytes=FAST_LIMIT),
+        cost_estimate=pair_cost(lay, mine),
+    )(mine, *rests)
+
+
+def cross_sums(lay, mine, rests, other, others, lab_lane, sums):
+    row = jax.ShapeDtypeStruct((1, lay.total), jnp.float32)
+    side = pltpu.VMEM((lay.total, LANES), jnp.float32)
+    buffer = pltpu.VMEM((lay.n_main // 2, 256), jnp.float32)
+    return pl.pallas_call(
+        functools.partial(cross_kernel, lay),
+        out_shape=(row, row, jax.ShapeDtypeStruct((8, LANES), jnp.int32)),
+        in_specs=list(vmem_specs(8)),
+        out_specs=vmem_specs(3),
+        scratch_shapes=[side, side, side, buffer, buffer],
+        compiler_params=pltpu.CompilerParams(vmem_limit_bytes=FAST_LIMIT),
+        cost_estimate=pair_cost(lay, mine),
+    )(mine, *rests, other, *others, lab_lane, sums)
+
+
+def pair_cost(lay, rows):
+    pairs = lay.n_main * lay.n_main
+    return pl.CostEstimate(
+        flops=2 * pairs * rows.shape[1],
+        bytes_accessed=4 * lay.n_main * rows.shape[1],
+        transcendentals=pairs,
+    )
+
+
+def join(lay, sums, more):
+    return pl.pallas_call(
+        functools.partial(join_kernel, lay),
+        out_shape=jax.ShapeDtypeStruct((lay.n_owner, 1, lay.capacity), jnp.float32),
+        in_specs=list(vmem_specs(2)),
+        out_specs=vmem_specs(1)[0],
+    )(sums, more)
+
+
+def fast_unpack_kernel(values_ref, pos_ref, out_ref):
+    pos = pos_ref[...]
+    lane = lax.rem(pos, LANES)
+    line = lax.div(pos, LANES)
+    out = jnp.zeros(pos.shape, jnp.float32)
+    per = values_ref.shape[2] // LANES
+    for r in range(values_ref.shape[0] * per):
+        start = r % per * LANES
+        table = jnp.broadcast_to(values_ref[r // per, :, start : start + LANES], pos.shape)
+        found = jnp.take_along_axis(table, lane, axis=1)
+        out = jnp.where(line == r, found, out)
+    out_ref[...] = out
+
+
+def fast_unpack(values, pos):
+    vmem = pl.BlockSpec(memory_space=pltpu.VMEM)
+    return pl.pallas_call(
+        fast_unpack_kernel,
+        out_shape=jax.ShapeDtypeStruct(pos.shape, jnp.float32),
+        in_specs=[vmem, vmem],
+        out_specs=vmem,
+    )(values, pos)
+
+
+def general(embeddings, labels, owner_map):
     n_owner = lax.axis_size("cl")
     capacity = SLOTS // n_owner
     rows, width = embeddings.shape
@@ -228,6 +726,48 @@
     return unpack(returned.reshape(SLOTS), pos).reshape(rows)
 
 
+def body(embeddings, labels, owner_map):
+    n_owner = lax.axis_size("cl")
+    capacity = SLOTS // n_owner
+    rows, width = embeddings.shape
+    n_fine = owner_map.shape[0]
+    main = -(-(rows // n_owner * 9 // 8) // 16) * 16
+    if main >= capacity or n_fine >= LANES:
+        return general(embeddings, labels, owner_map)
+    planes = n_owner // 2
+    plane = planes // 2 - 1
+    home = 2 * plane
+    lay = Layout(n_owner, n_fine, capacity, main, home)
+    unit, slot, info, extra, pos = place_rows(
+        embeddings, labels, owner_map, n_owner, capacity, main, home
+    )
+    chunks = [
+        extra
+        if z == plane
+        else lax.ppermute(extra, "cl", [(2 * z + y, 2 * plane + y) for y in range(2)])
+        for z in range(planes)
+    ]
+    rest_a = gather_rest(chunks, lay.rest, plane)
+    rest_b = lax.ppermute(rest_a, "cl", [(home + 1, home)])
+    rests = (rest_a, rest_b)
+    swap = [(2 * home, 2 * home + 1), (2 * home + 1, 2 * home)]
+    others = tuple(lax.ppermute(x, ("cl", "grp"), swap) for x in rests)
+    packed = pack_main(unit, slot, info, n_owner, main, home)
+    mine = lax.all_to_all(
+        packed.reshape(n_owner, main, width), "cl", split_axis=0, concat_axis=0, tiled=True
+    ).reshape(n_owner * main, width)
+    other = lax.ppermute(mine, "grp", [(0, 1), (1, 0)])
+    sums, lab_lane = inner_sums(lay, mine, rests)
+    sums, for_other, unfit = cross_sums(lay, mine, rests, other, others, lab_lane, sums)
+    results = join(lay, sums, lax.ppermute(for_other, "grp", [(0, 1), (1, 0)]))
+    returned = lax.all_to_all(results, "cl", split_axis=0, concat_axis=0, tiled=True)
+    return lax.cond(
+        unfit[0, 0] == 0,
+        lambda: fast_unpack(returned, pos).reshape(rows),
+        lambda: general(embeddings, labels, owner_map),
+    )
+
+
 def solution(mesh):
     return jax.shard_map(
         body,

time: 144 us -> 127 us (0.88)
  blocking collectives: 107 us -> 0 us
  starting transfers between devices: 0.01 us -> 54.4 us
  waiting for transfers between devices: 0.01 us -> 46.5 us
  Pallas kernels: 32.3 us -> 20.1 us
    all_to_all x2 -> x0, blocking collectives: 87.3 us -> none  [the longest x1 77.8 us: body(): lax.all_to_all(packed.reshape(n_owner, capacity, width), 'cl', split_axis...]
    all_to_all x0 -> x2, waiting for transfers between devices: none -> 45.7 us  [the longest x1 40.3 us: body(): lax.all_to_all(packed.reshape(n_owner, main, width), 'cl', split_axis=0,...]
    all_to_all x0 -> x2, starting transfers between devices: none -> 45.3 us  [the longest x1 38.1 us: body(): lax.all_to_all(results, 'cl', split_axis=0, concat_axis=0, tiled=True)]
    all_gather x1 -> x0, blocking collectives: 19.3 us -> none  [body(): counts = lax.all_gather(counts, ('cl', 'grp'), tiled=True)]
    pallas_call x3 -> x7, Pallas kernels: 32.3 us -> 20.1 us  [the longest x1 5.79 us: cross_sums(): pl.pallas_call(functools.partial(cross_kernel, lay), out_shape=(row, row,...]
    ppermute x0 -> x7, starting transfers between devices: none -> 9.09 us  [the longest x3 6.51 us: body(): lax.ppermute(extra, 'cl', [(2 * z + y, 2 * plane + y) for y in range(2)])]
    unnamed x10 -> x24, local copies, waits for them, and re-layouts: 4.97 us -> 4.36 us
  transfers between devices with their start and end apart: 1 -> 10, of which waited for: 0 -> 3; matrix products, arithmetic and copies ran while one was open for 0% -> 0% of each run, Pallas kernels for 0% -> 5%
where the time goes in v5:
time: 127 us
  starting transfers between devices  54.4 us (43%)
  waiting for transfers between devices  46.5 us (37%)
  Pallas kernels  20.1 us (16%)
  local copies, waits for them, and re-layouts  4.87 us (4%)
    all_to_all x1, waiting for transfers between devices, body(): lax.all_to_all(packed.reshape(n_owner, main, width), 'cl', split_axis=0,...  40.3 us
    all_to_all x1, starting transfers between devices, body(): lax.all_to_all(results, 'cl', split_axis=0, concat_axis=0, tiled=True)  38.1 us
    all_to_all x1, starting transfers between devices, body(): lax.all_to_all(packed.reshape(n_owner, main, width), 'cl', split_axis=0,...  7.28 us
    ppermute x3, starting transfers between devices, body(): lax.ppermute(extra, 'cl', [(2 * z + y, 2 * plane + y) for y in range(2)])  6.51 us
    pallas_call x1, Pallas kernels, cross_sums(): pl.pallas_call(functools.partial(cross_kernel, lay), out_shape=(row, row,...  5.79 us
    all_to_all x1, waiting for transfers between devices, body(): lax.all_to_all(results, 'cl', split_axis=0, concat_axis=0, tiled=True)  5.35 us
    pallas_call x1, Pallas kernels, inner_sums(): pl.pallas_call(functools.partial(inner_kernel, lay), out_shape=(row, row)...  4.63 us
    unnamed x24, local copies, waits for them, and re-layouts  4.36 us
  transfers between devices with their start and end apart: 10, of which 3 were waited for; matrix products, arithmetic and copies ran while one was open for 0% of the time, Pallas kernels for 5%

profile of v5, /device:TPU:0, one launch (start us, length us, event | category | flops | bytes accessed | tf_op | source)
XLA Modules:
  0.0 126.8 jit_solution(5613269326446685071)
XLA Ops:
  0.0 2.8 %shard_map.39 = (bf16[1024,768]{1,0:T(8,128)(2,1)S(1)}, s32[1,1024]{1,0:T(1,128)S(1)}, f32[1,128]{1,0:T(1,128)S(1)}, bf16[128,768]{1,0:T(8,128)(2,1)S(1)}, s32[8,128]{1,0:T(8,128)S(1)}) custom-call(bf16[1024,768]{1,0:T(8,128)(2,1)} %x_hbm.1, s32[8,128]{1,0:T(8,128)} %bitcast.25, s32[1,64]{1,0:T(1,128)} %bitcast.29), custom_call_target="tpu_custom_call" | custom-call | tf_op jit(solution)/shard_map/pallas_call | solution.py:313
  2.8 0.0 copy-start.2
  2.8 3.2 %shard_map.40 = bf16[1152,768]{1,0:T(8,128)(2,1)} custom-call(bf16[1024,768]{1,0:T(8,128)(2,1)S(1)} %get-tuple-element.36.unit, s32[1,1024]{1,0:T(1,128)S(1)} %get-tuple-element.37.slot_ref, f32[1,128]{1,0:T(1,128)S(1)} %get-tuple-element.38.info_ref), custom_call_target="tpu_custom_call" | custom-call | flops 1811939328 | bytes 3145728 | tf_op jit(solution)/shard_map/pallas_call | solution.py:335
  6.1 7.3 %all-to-all-start.2 = ((bf16[8,144,768]{2,1,0:T(8,128)(2,1)}), bf16[8,144,768]{2,1,0:T(8,128)(2,1)S(1)}, u32[]{:S(2)}, u32[]{:S(2)}) async-start(bf16[8,144,768]{2,1,0:T(8,128)(2,1)} %bitcast.12), calls=%async_computation.2 | async-start | bytes 3538944 | tf_op jit(solution)/shard_map/all_to_all | solution.py:756
  13.3 0.7 collective-permute-start.3
  14.0 0.7 collective-permute-start.2
  14.7 0.0 copy-done.2
  14.7 5.2 %collective-permute-start.1 = (bf16[128,768]{1,0:T(8,128)(2,1)S(1)}, bf16[128,768]{1,0:T(8,128)(2,1)S(1)}, u32[]{:S(2)}, u32[]{:S(2)}) collective-permute-start(bf16[128,768]{1,0:T(8,128)(2,1)S(1)} %get-tuple-element.39.refs_1_), channel_id=1, source_target_pairs={{0,4},{2,6},{1,5},{3,7},{16,20},{18,22},{17,21},{19,23}} | collective-permute-start | bytes 589832 | tf_op jit(solution)/shard_map/ppermute | solution.py:747
  19.9 40.3 %all-to-all-done.2 = bf16[8,144,768]{2,1,0:T(8,128)(2,1)S(1)} async-done(((bf16[8,144,768]{2,1,0:T(8,128)(2,1)}), bf16[8,144,768]{2,1,0:T(8,128)(2,1)S(1)}, u32[]{:S(2)}, u32[]{:S(2)}) %all-to-all-start.2) | async-done | bytes 1769504 | tf_op jit(solution)/shard_map/all_to_all | solution.py:756
  60.2 0.0 collective-permute-start.5
  60.2 0.0 collective-permute-done.3.refs_3_
  60.2 0.0 copy-start.7
  60.2 0.0 collective-permute-done.2.refs_2_
  60.2 0.0 copy-start.8
  60.2 0.0 collective-permute-done.1.refs_0_
  60.2 0.6 copy-done.7
  60.9 0.1 copy-done.8
  61.0 0.0 copy-start.9
  61.0 0.7 copy-done.9
  61.6 2.1 %shard_map.41.rest_a.refs_1_ = bf16[512,768]{1,0:T(8,128)(2,1)} custom-call(bf16[128,768]{1,0:T(8,128)(2,1)} %copy-done.9, bf16[128,768]{1,0:T(8,128)(2,1)} %copy-done.2, bf16[128,768]{1,0:T(8,128)(2,1)} %copy-done.8, bf16[128,768]{1,0:T(8,128)(2,1)} %copy-done.7), custom_call_target="tpu_custom_call" | custom-call | bytes 1572864 | tf_op jit(solution)/shard_map/pallas_call | solution.py:362
  63.8 0.7 collective-permute-start.4
  64.5 0.7 collective-permute-start.6
  65.2 0.0 collective-permute-done.4.rest_b.refs_2_
  65.2 0.7 collective-permute-start.7
  65.9 0.0 copy-start
  65.9 1.1 copy-done
  67.0 0.0 copy-start.1
  67.0 4.6 %shard_map.42 = (f32[1,2176]{1,0:T(1,128)S(1)}, f32[1,2176]{1,0:T(1,128)S(1)}) custom-call(bf16[1152,768]{1,0:T(8,128)(2,1)S(1)} %bitcast.19, bf16[512,768]{1,0:T(8,128)(2,1)S(1)} %copy-done, bf16[512,768]{1,0:T(8,128)(2,1)S(1)} %collective-permute-done.4.rest_b.refs_2_), custom_call_target="tpu_custom_call" | custom-call | flops 2038431744 | bytes 3538944 | tf_op jit(solution)/shard_map/pallas_call | solution.py:644
  71.7 0.0 collective-permute-done.6.refs_4_
  71.7 0.0 collective-permute-done.7.refs_5_
  71.7 0.0 collective-permute-done.5.refs_3_
  71.7 0.0 copy-done.1
  71.7 0.0 copy-start.5
  71.7 0.0 copy-start.10
  71.7 0.0 copy-start.13
  71.8 5.8 %shard_map.43 = (f32[1,2176]{1,0:T(1,128)S(1)}, f32[1,2176]{1,0:T(1,128)S(1)}, s32[8,128]{1,0:T(8,128)S(1)}) custom-call(bf16[1152,768]{1,0:T(8,128)(2,1)S(1)} %bitcast.20, bf16[512,768]{1,0:T(8,128)(2,1)S(1)} %copy-done.1, bf16[512,768]{1,0:T(8,128)(2,1)S(1)} %collective-permute-done.4.rest_b.refs_2_, bf16[1152,768]{1,0:T(8,128)(2,1)} %collective-permute-done.5.refs_3_, ...), custom_call_target="tpu_custom_call" | custom-call | flops 2038431744 | bytes 3538944 | tf_op jit(solution)/shard_map/pallas_call | solution.py:659
  77.5 0.0 copy-start.3
  77.5 0.6 copy-done.3
  78.2 0.5 collective-permute-start.8
  78.6 0.8 collective-permute-done.8.more
  79.5 0.0 copy-start.11
  79.5 0.6 copy-done.11
  80.0 1.5 %shard_map.44 = f32[8,1,256]{2,1,0:T(1,128)} custom-call(f32[1,2176]{1,0:T(1,128)} %copy-done.3, f32[1,2176]{1,0:T(1,128)} %copy-done.11), custom_call_target="tpu_custom_call" | custom-call | tf_op jit(solution)/shard_map/pallas_call | solution.py:680
  81.5 38.1 %all-to-all-start.3 = ((f32[8,1,256]{2,1,0:T(1,128)}), f32[8,1,256]{2,1,0:T(1,128)S(1)}, u32[]{:S(2)}, u32[]{:S(2)}) async-start(f32[8,1,256]{2,1,0:T(1,128)} %shard_map.44), calls=%async_computation.3 | async-start | bytes 16384 | tf_op jit(solution)/shard_map/all_to_all | solution.py:763
  119.6 0.5 slice.3
  120.7 5.4 %all-to-all-done.3 = f32[8,1,256]{2,1,0:T(1,128)S(1)} async-done(((f32[8,1,256]{2,1,0:T(1,128)}), f32[8,1,256]{2,1,0:T(1,128)S(1)}, u32[]{:S(2)}, u32[]{:S(2)}) %all-to-all-start.3) | async-done | bytes 8224 | tf_op jit(solution)/shard_map/all_to_all | solution.py:763
  126.1 0.0 copy-done.5
  126.1 0.0 copy-done.10
  126.1 0.0 copy-done.13
  126.1 0.1 conditional.1
  126.1 0.1 branch_1_fun.1
  126.2 0.0 copy-start.12
  126.2 0.6 copy-done.12
Async XLA Ops:
  2.8 11.9 %copy-start.2 = (bf16[128,768]{1,0:T(8,128)(2,1)}, bf16[128,768]{1,0:T(8,128)(2,1)S(1)}, u32[]{:S(2)}) copy-start(bf16[128,768]{1,0:T(8,128)(2,1)S(1)} %get-tuple-element.39.refs_1_) | copy-start | bytes 589828
  6.1 54.1 %all-to-all-start.2 = ((bf16[8,144,768]{2,1,0:T(8,128)(2,1)}), bf16[8,144,768]{2,1,0:T(8,128)(2,1)S(1)}, u32[]{:S(2)}, u32[]{:S(2)}) async-start(bf16[8,144,768]{2,1,0:T(8,128)(2,1)} %bitcast.12), calls=%async_computation.2 | async-start | bytes 3538944 | tf_op jit(solution)/shard_map/all_to_all | solution.py:756
  13.3 46.9 %collective-permute-start.3 = (bf16[128,768]{1,0:T(8,128)(2,1)S(1)}, bf16[128,768]{1,0:T(8,128)(2,1)S(1)}, u32[]{:S(2)}, u32[]{:S(2)}) collective-permute-start(bf16[128,768]{1,0:T(8,128)(2,1)S(1)} %get-tuple-element.39.refs_1_), channel_id=1, source_target_pairs={{12,4},{14,6},{13,5},{15,7},{28,20},{30,22},{29,21},{31,23}} | collective-permute-start | bytes 589832 | tf_op jit(solution)/shard_map/ppermute | solution.py:747
  14.0 46.2 %collective-permute-start.2 = (bf16[128,768]{1,0:T(8,128)(2,1)S(1)}, bf16[128,768]{1,0:T(8,128)(2,1)S(1)}, u32[]{:S(2)}, u32[]{:S(2)}) collective-permute-start(bf16[128,768]{1,0:T(8,128)(2,1)S(1)} %get-tuple-element.39.refs_1_), channel_id=1, source_target_pairs={{8,4},{10,6},{9,5},{11,7},{24,20},{26,22},{25,21},{27,23}} | collective-permute-start | bytes 589832 | tf_op jit(solution)/shard_map/ppermute | solution.py:747
  14.7 45.5 %collective-permute-start.1 = (bf16[128,768]{1,0:T(8,128)(2,1)S(1)}, bf16[128,768]{1,0:T(8,128)(2,1)S(1)}, u32[]{:S(2)}, u32[]{:S(2)}) collective-permute-start(bf16[128,768]{1,0:T(8,128)(2,1)S(1)} %get-tuple-element.39.refs_1_), channel_id=1, source_target_pairs={{0,4},{2,6},{1,5},{3,7},{16,20},{18,22},{17,21},{19,23}} | collective-permute-start | bytes 589832 | tf_op jit(solution)/shard_map/ppermute | solution.py:747
  60.2 11.5 %collective-permute-start.5 = (bf16[1152,768]{1,0:T(8,128)(2,1)S(1)}, bf16[1152,768]{1,0:T(8,128)(2,1)}, u32[]{:S(2)}, u32[]{:S(2)}) collective-permute-start(bf16[1152,768]{1,0:T(8,128)(2,1)S(1)} %bitcast.18), channel_id=1, source_target_pairs={{0,1},{1,0},{2,3},{3,2},{4,5},{5,4},{6,7},{7,6},{8,9},{9,8},{10,11... | collective-permute-start | bytes 5308424 | tf_op jit(solution)/shard_map/ppermute | solution.py:759
  60.2 0.7 copy-start.7
  60.2 0.7 copy-start.8
  61.0 0.7 copy-start.9
  63.8 1.4 %collective-permute-start.4 = (bf16[512,768]{1,0:T(8,128)(2,1)}, bf16[512,768]{1,0:T(8,128)(2,1)S(1)}, u32[]{:S(2)}, u32[]{:S(2)}) collective-permute-start(bf16[512,768]{1,0:T(8,128)(2,1)} %shard_map.41.rest_a.refs_1_), channel_id=1, source_target_pairs={{6,4},{7,5},{22,20},{23,21}} | collective-permute-start | bytes 2359304 | tf_op jit(solution)/shard_map/ppermute | solution.py:751
  64.5 7.2 %collective-permute-start.6 = (bf16[512,768]{1,0:T(8,128)(2,1)}, bf16[512,768]{1,0:T(8,128)(2,1)S(1)}, u32[]{:S(2)}, u32[]{:S(2)}) collective-permute-start(bf16[512,768]{1,0:T(8,128)(2,1)} %shard_map.41.rest_a.refs_1_), channel_id=1, source_target_pairs={{4,5},{5,4},{20,21},{21,20}} | collective-permute-start | bytes 2359304 | tf_op jit(solution)/shard_map/ppermute | solution.py:754
  65.2 6.5 %collective-permute-start.7 = (bf16[512,768]{1,0:T(8,128)(2,1)S(1)}, bf16[512,768]{1,0:T(8,128)(2,1)S(1)}, u32[]{:S(2)}, u32[]{:S(2)}) collective-permute-start(bf16[512,768]{1,0:T(8,128)(2,1)S(1)} %collective-permute-done.4.rest_b.refs_2_), channel_id=1, source_target_pairs={{4,5},{5,4},{20,21},{21,20}} | collective-permute-start | bytes 2359304 | tf_op jit(solution)/shard_map/ppermute | solution.py:754
  65.9 1.1 copy-start
  67.0 4.7 %copy-start.1 = (bf16[512,768]{1,0:T(8,128)(2,1)S(1)}, bf16[512,768]{1,0:T(8,128)(2,1)}, u32[]{:S(2)}) copy-start(bf16[512,768]{1,0:T(8,128)(2,1)} %shard_map.41.rest_a.refs_1_) | copy-start | bytes 2359300
  71.7 54.4 %copy-start.5 = (bf16[1024,768]{1,0:T(8,128)(2,1)S(1)}, bf16[1024,768]{1,0:T(8,128)(2,1)}, u32[]{:S(2)}) copy-start(bf16[1024,768]{1,0:T(8,128)(2,1)} %x_hbm.1) | copy-start | bytes 4718596
  71.7 54.4 %copy-start.10 = (s32[1024]{0:T(1024)S(1)}, s32[1024]{0:T(1024)}, u32[]{:S(2)}) copy-start(s32[1024]{0:T(1024)} %param.6) | copy-start | bytes 12292
  71.7 54.3 %copy-start.13 = (s32[64]{0:T(128)S(1)}, s32[64]{0:T(128)}, u32[]{:S(2)}) copy-start(s32[64]{0:T(128)} %param.7) | copy-start | bytes 772
  77.5 0.6 copy-start.3
  78.2 1.3 %collective-permute-start.8 = (f32[1,2176]{1,0:T(1,128)S(1)}, f32[1,2176]{1,0:T(1,128)S(1)}, u32[]{:S(2)}, u32[]{:S(2)}) collective-permute-start(f32[1,2176]{1,0:T(1,128)S(1)} %get-tuple-element.44), channel_id=1, source_target_pairs={{0,1},{1,0},{2,3},{3,2},{4,5},{5,4},{6,7},{7,6},{8,9},{9,8},{10,11... | collective-permute-start | bytes 26120 | tf_op jit(solution)/shard_map/ppermute | solution.py:762
  79.5 0.6 copy-start.11
  81.5 44.6 %all-to-all-start.3 = ((f32[8,1,256]{2,1,0:T(1,128)}), f32[8,1,256]{2,1,0:T(1,128)S(1)}, u32[]{:S(2)}, u32[]{:S(2)}) async-start(f32[8,1,256]{2,1,0:T(1,128)} %shard_map.44), calls=%async_computation.3 | async-start | bytes 16384 | tf_op jit(solution)/shard_map/all_to_all | solution.py:763
  126.2 0.6 copy-start.12

commit v6 on v5

--- a/solution.py
+++ b/solution.py
@@ -213,10 +213,6 @@
     )(values.reshape(-1, LANES), pos)
 
 
-def pieces(start, count, parts):
-    return [(start + i * (count // parts), count // parts) for i in range(parts)]
-
-
 def swapped(x, first, second):
     return jnp.where(x == first, second, jnp.where(x == second, first, x))
 
@@ -346,21 +342,36 @@
     )(unit, slot, info)
 
 
-def gather_kernel(rest, plane, *refs):
+def gate_kernel(*refs):
+    pass
+
+
+def after(rows, received):
+    anywhere = pl.BlockSpec(memory_space=pl.ANY)
+    return pl.pallas_call(
+        gate_kernel,
+        out_shape=jax.ShapeDtypeStruct(rows.shape, rows.dtype),
+        in_specs=[anywhere] * (1 + len(received)),
+        out_specs=anywhere,
+        input_output_aliases={0: 0},
+    )(rows, *received)
+
+
+def gather_kernel(rest, home, *refs):
     chunks, out = refs[:-1], refs[-1]
 
-    @pl.when(lax.div(lax.axis_index("cl"), 2) == plane)
+    @pl.when(lax.axis_index("cl") == home)
     def _():
-        for z, chunk in enumerate(chunks):
-            out[z * rest : (z + 1) * rest, :] = chunk[:rest, :]
-            start = len(chunks) * rest + z * INFO
+        for source, chunk in enumerate(chunks):
+            out[source * rest : (source + 1) * rest, :] = chunk[:rest, :]
+            start = len(chunks) * rest + source * INFO
             out[start : start + INFO, :] = chunk[rest:, :]
 
 
-def gather_rest(chunks, rest, plane):
+def gather_rest(chunks, rest, home):
     shape = (len(chunks) * (rest + INFO), chunks[0].shape[1])
     return pl.pallas_call(
-        functools.partial(gather_kernel, rest, plane),
+        functools.partial(gather_kernel, rest, home),
         out_shape=jax.ShapeDtypeStruct(shape, jnp.bfloat16),
         in_specs=list(vmem_specs(len(chunks))),
         out_specs=vmem_specs(1)[0],
@@ -376,21 +387,15 @@
         self.main, self.home = main, home
         self.rest = capacity - main
         self.per_owner = n_fine // n_owner
-        self.planes = n_owner // 2
         self.n_main = n_owner * main
-        self.n_rest = self.planes * self.rest
-        self.rest_lines = self.planes * (self.rest + INFO)
-        self.total = self.n_main + 2 * self.rest_lines
-
-    def rest_at(self, y):
-        return self.n_main + y * self.rest_lines
-
-
-def info_line(lay, is_home, main_ref, rest_refs, source):
+        self.n_rest = n_owner * self.rest
+        self.total = self.n_main + self.n_rest
+
+
+def info_line(lay, is_home, main_ref, rest_ref, source):
     in_main = main_ref[(source + 1) * lay.main - INFO : (source + 1) * lay.main, :LANES]
-    z, y = source // 2, source % 2
-    start = lay.n_rest + z * INFO
-    in_rest = rest_refs[y][start : start + INFO, :LANES]
+    start = lay.n_rest + source * INFO
+    in_rest = rest_ref[start : start + INFO, :LANES]
     in_main = in_main.astype(jnp.float32)[INFO - 1 :]
     return jnp.where(is_home, in_rest.astype(jnp.float32)[INFO - 1 :], in_main)
 
@@ -414,16 +419,7 @@
 
         @pl.when(is_home)
         def _(source=source, write=write):
-            start = lay.rest_at(source % 2) + source // 2 * lay.rest
-            write(start, lay.main, lay.rest)
-
-    @pl.when(is_home)
-    def _():
-        for y in range(2):
-            start = lay.rest_at(y) + lay.n_rest
-            lab_sub[start : start + lay.rest_lines - lay.n_rest, :] = jnp.full(
-                (lay.rest_lines - lay.n_rest, LANES), float(lay.per_owner), jnp.float32
-            )
+            write(lay.n_main + source * lay.rest, lay.main, lay.rest)
 
 
 def hot_of(lay, info):
@@ -432,74 +428,88 @@
     return hot.astype(jnp.int32)
 
 
-def pair_sums(rows_i, label_i, tiles, buffers):
-    wide = rows_i.shape[0]
+def scores_to(buffer, rows_j, rows_i):
+    buffer[: rows_j.shape[0], : rows_i.shape[0]] = lax.dot_general(
+        rows_j,
+        rows_i,
+        (((1,), (1,)), ((), ())),
+        preferred_element_type=jnp.float32,
+    )
+
+
+def add_terms(acc, buffer, deep, label_i, lab_sub, bias, place):
+    wide = label_i.shape[1]
     repeat = wide // LANES
-    dead_i = jnp.where(label_i >= 0, 0.0, DEAD)
     step = 32
-
-    def scores_to(buffer, tile):
-        ref, start, deep = tile[:3]
-        buffer[:deep, :wide] = lax.dot_general(
-            ref[start : start + deep, :],
-            rows_i,
-            (((1,), (1,)), ((), ())),
-            preferred_element_type=jnp.float32,
-        )
-
-    acc = jnp.zeros((8, wide), jnp.float32)
-    here, ahead = buffers
-    scores_to(here, tiles[0])
-    for i, (_, _, deep, lab_sub, bias, place, back) in enumerate(tiles):
-        if i + 1 < len(tiles):
-            scores_to(ahead, tiles[i + 1])
-        for c in range(0, deep, step):
-            part = slice(place + c, place + c + step)
-            label_j = jnp.concatenate([lab_sub[part, :]] * repeat, axis=1)
-            bias_j = jnp.concatenate([bias[part, :]] * repeat, axis=1)
-            if back is not None:
-                bias_j = bias_j + dead_i
-            shift = jnp.where(label_j == label_i, -SCALE, bias_j)
-            terms = jnp.exp2(here[c : c + step, :wide] * SCALE + shift)
-            acc = acc + jnp.sum(terms.reshape(step // 8, 8, wide), axis=0)
-            if back is not None:
-                across = terms[:, :LANES]
-                for r in range(1, repeat):
-                    across = across + terms[:, r * LANES : (r + 1) * LANES]
-                back[part, :] += across
-        here, ahead = ahead, here
-    return jnp.sum(acc, axis=0, keepdims=True)
-
-
-def each_block(count, run):
+    for c in range(0, deep, step):
+        part = slice(place + c, place + c + step)
+        label_j = jnp.concatenate([lab_sub[part, :]] * repeat, axis=1)
+        bias_j = jnp.concatenate([bias[part, :]] * repeat, axis=1)
+        shift = jnp.where(label_j == label_i, -SCALE, bias_j)
+        terms = jnp.exp2(buffer[c : c + step, :wide] * SCALE + shift)
+        acc = acc + jnp.sum(terms.reshape(step // 8, 8, wide), axis=0)
+    return acc
+
+
+def main_sums(lay, rows_i, rows_j, lab_lane, lab_sub, bias, buffers, put):
+    half = lay.n_main // 2
+    low, high = buffers
+
+    def run(start, wide):
+        place = pl.ds(start, wide)
+        here, label_i = rows_i[place, :], lab_lane[:, place]
+        scores_to(low, rows_j[:half, :], here)
+        scores_to(high, rows_j[half : lay.n_main, :], here)
+        acc = jnp.zeros((8, wide), jnp.float32)
+        acc = add_terms(acc, low, half, label_i, lab_sub, bias, 0)
+        acc = add_terms(acc, high, half, label_i, lab_sub, bias, half)
+        put(place, jnp.sum(acc, axis=0, keepdims=True))
+
     wide = 256
-    full = count // wide
+    full = lay.n_main // wide
 
     @pl.loop(0, full)
     def _(i):
         run(pl.multiple_of(i * wide, wide), wide)
 
-    if count % wide:
-        run(full * wide, count % wide)
-
-
-def row_sums(back, start, count):
-    ones = jnp.ones((8, LANES), jnp.float32)
-    sums = lax.dot_general(
-        ones,
-        back[start : start + count, :],
-        (((1,), (1,)), ((), ())),
-        precision=lax.Precision.HIGHEST,
-        preferred_element_type=jnp.float32,
-    )
-    return sums[:1]
-
-
-def inner_kernel(lay, mine, rest_a, rest_b, sums, lab_lane, lab_sub, bias, back, buf_a, buf_b):
+    if lay.n_main % wide:
+        run(full * wide, lay.n_main % wide)
+
+
+def all_sums(lay, rows_i, rows_j, rest_j, lab_lane, lab_sub, bias, buffers, put):
+    wide = 256
+    blocks = lay.total // wide
+    first, second = buffers
+
+    def place_of(block):
+        return pl.ds(pl.multiple_of(block * wide, wide), wide)
+
+    scores_to(first, rows_j[: lay.n_main, :], rows_i[:wide, :])
+
+    @pl.loop(0, blocks)
+    def _(block):
+        place = place_of(block)
+        label_i = lab_lane[:, place]
+        scores_to(second, rest_j[: lay.n_rest, :], rows_i[place, :])
+        acc = jnp.zeros((8, wide), jnp.float32)
+        acc = add_terms(acc, first, lay.n_main, label_i, lab_sub, bias, 0)
+        scores_to(first, rows_j[: lay.n_main, :], rows_i[place_of(jnp.minimum(block + 1, blocks - 1)), :])
+        acc = add_terms(acc, second, lay.n_rest, label_i, lab_sub, bias, lay.n_main)
+        put(place, jnp.sum(acc, axis=0, keepdims=True))
+
+
+def join_rows(lay, mine, rest, rows):
+    for start in range(0, lay.n_main, lay.main):
+        rows[start : start + lay.main, :] = mine[start : start + lay.main, :]
+    for start in range(0, lay.n_rest, lay.rest):
+        to = lay.n_main + start
+        rows[to : to + lay.rest, :] = rest[start : start + lay.rest, :]
+
+
+def inner_kernel(lay, mine, rest, sums, lab_lane, lab_sub, bias, rows, buf_a, buf_b):
     me = lax.axis_index("cl")
     is_home = me == lay.home
-    rests = (rest_a, rest_b)
-    infos = [info_line(lay, is_home, mine, rests, s) for s in range(lay.n_owner)]
+    infos = [info_line(lay, is_home, mine, rest, s) for s in range(lay.n_owner)]
     cluster = swapped(me, hot_of(lay, infos[0]), lay.home)
     write_labels(lay, infos, cluster, is_home, lab_sub, bias)
 
@@ -508,52 +518,30 @@
             block = jnp.transpose(lab_sub[i : i + LANES, :])[:1]
             lab_lane[:, i : i + LANES] = jnp.where(block < lay.per_owner, block, -1.0)
 
+    def put(place, values):
+        sums[:, place] = values
+
     turn(0, lay.n_main)
     buffers = (buf_a, buf_b)
-    own = [
-        (mine, s, d, lab_sub, bias, s, None) for s, d in pieces(0, lay.n_main, 2)
-    ]
-
-    def main_block(start, wide):
-        place = pl.ds(start, wide)
-        sums[:, place] = pair_sums(mine[place, :], lab_lane[:, place], own, buffers)
-
-    each_block(lay.n_main, main_block)
 
     @pl.when(is_home)
     def _():
-        turn(lay.n_main, 2 * lay.rest_lines)
-        n_back = 2 * lay.rest_lines
-        back[lay.n_main : lay.n_main + n_back, :] = jnp.zeros((n_back, LANES), jnp.float32)
-        seconds = [(rests[y], 0, lay.n_rest, lab_sub, bias, lay.rest_at(y), back) for y in (0, 1)]
-
-        def more(start, wide):
-            place = pl.ds(start, wide)
-            sums[:, place] += pair_sums(mine[place, :], lab_lane[:, place], seconds, buffers)
-
-        each_block(lay.n_main, more)
-        among = [tile[:6] + (None,) for tile in seconds]
-        for y in range(2):
-
-            def rest_block(start, wide, y=y):
-                place = pl.ds(start + lay.rest_at(y), wide)
-                rows_i = rests[y][pl.ds(start, wide), :]
-                sums[:, place] = pair_sums(rows_i, lab_lane[:, place], among, buffers)
-
-            each_block(lay.rest_lines, rest_block)
-        place = slice(lay.n_main, lay.n_main + n_back)
-        sums[:, place] += row_sums(back, lay.n_main, n_back)
+        turn(lay.n_main, lay.n_rest)
+        join_rows(lay, mine, rest, rows)
+        all_sums(lay, rows, mine, rest, lab_lane, lab_sub, bias, buffers, put)
+
+    @pl.when(jnp.logical_not(is_home))
+    def _():
+        main_sums(lay, mine, mine, lab_lane, lab_sub, bias, buffers, put)
 
 
 def cross_kernel(lay, *refs):
-    mine, rest_a, rest_b, other, other_a, other_b, lab_lane, sums = refs[:8]
-    out, out_other, unfit_ref, lab_sub, bias, back, buf_a, buf_b = refs[8:]
+    mine, rest, other, rest_other, lab_lane, sums = refs[:6]
+    out_ref, unfit_ref, lab_sub, bias, rows, total, buf_a, buf_b = refs[6:]
     me = lax.axis_index("cl")
-    grp = lax.axis_index("grp")
     is_home = me == lay.home
-    rests, others = (rest_a, rest_b), (other_a, other_b)
-    infos = [info_line(lay, is_home, other, others, s) for s in range(lay.n_owner)]
-    own = [info_line(lay, is_home, mine, rests, s) for s in range(lay.n_owner)]
+    infos = [info_line(lay, is_home, other, rest_other, s) for s in range(lay.n_owner)]
+    own = [info_line(lay, is_home, mine, rest, s) for s in range(lay.n_owner)]
     hot = hot_of(lay, own[0])
     lane = lax.broadcasted_iota(jnp.int32, (1, LANES), 1)
     last = (lane < lay.n_fine) & (lax.rem(lane, lay.per_owner) == lay.per_owner - 1)
@@ -568,103 +556,32 @@
         jnp.max(unfit, axis=1, keepdims=True), unfit_ref.shape
     ).astype(jnp.int32)
     write_labels(lay, infos, swapped(me, hot, lay.home), is_home, lab_sub, bias)
-    back[: lay.n_main, :] = jnp.zeros((lay.n_main, LANES), jnp.float32)
     buffers = (buf_a, buf_b)
-    out[...] = sums[...]
-    half = 512
-
-    def main_tiles(low):
-        start, count = (0, half) if low else (half, lay.n_main - half)
-        return [(other, s, d, lab_sub, bias, s, back) for s, d in pieces(start, count, 2)]
-
-    def main_blocks(first, count, low):
-        def run(start, wide):
-            place = pl.ds(first + start, wide)
-            out[:, place] += pair_sums(
-                mine[place, :], lab_lane[:, place], main_tiles(low), buffers
-            )
-
-        each_block(count, run)
-
-    @pl.when(grp == 0)
-    def _():
-        main_blocks(0, half, True)
-        main_blocks(half, lay.n_main - half, False)
-
-    @pl.when(grp == 1)
-    def _():
-        main_blocks(0, half, False)
-        main_blocks(half, lay.n_main - half, True)
+
+    def put(place, values):
+        values = values + sums[:, place]
+        total[:, place] = jnp.log(jnp.where(lab_lane[:, place] >= 0, values, 1.0))
 
     @pl.when(is_home)
     def _():
-        back[lay.n_main :, :] = jnp.zeros((2 * lay.rest_lines, LANES), jnp.float32)
-        seconds = [(others[y], 0, lay.n_rest, lab_sub, bias, lay.rest_at(y), back) for y in (0, 1)]
-
-        def more(start, wide):
-            place = pl.ds(start, wide)
-            out[:, place] += pair_sums(mine[place, :], lab_lane[:, place], seconds, buffers)
-
-        each_block(lay.n_main, more)
-        for y in range(2):
-            for g in range(2):
-
-                @pl.when(grp == g)
-                def _(y=y, g=g):
-                    ref, _, _, _, _, place_j, _ = seconds[y ^ g]
-                    tiles = [
-                        (ref, s, d, lab_sub, bias, place_j + s, back)
-                        for s, d in pieces(0, lay.n_rest, 2)
-                    ]
-
-                    def run(start, wide):
-                        place = pl.ds(start + lay.rest_at(y), wide)
-                        rows_i = rests[y][pl.ds(start, wide), :]
-                        out[:, place] += pair_sums(rows_i, lab_lane[:, place], tiles, buffers)
-
-                    each_block(lay.rest_lines, run)
-
-        out_other[:, lay.n_main :] = row_sums(back, lay.n_main, 2 * lay.rest_lines)
-
-    out_other[:, : lay.n_main] = row_sums(back, 0, lay.n_main)
-
-
-def join_kernel(lay, sums, more, out_ref):
-    values = jnp.log(sums[...] + more[...])
+        join_rows(lay, mine, rest, rows)
+        all_sums(lay, rows, other, rest_other, lab_lane, lab_sub, bias, buffers, put)
+
+    @pl.when(jnp.logical_not(is_home))
+    def _():
+        main_sums(lay, mine, other, lab_lane, lab_sub, bias, buffers, put)
+
     for source in range(lay.n_owner):
-        out_ref[source, :, : lay.main] = values[:, source * lay.main : (source + 1) * lay.main]
-        start = lay.rest_at(source % 2) + source // 2 * lay.rest
-        out_ref[source, :, lay.main :] = values[:, start : start + lay.rest]
-
-
-def inner_sums(lay, mine, rests):
-    row = jax.ShapeDtypeStruct((1, lay.total), jnp.float32)
+        out_ref[source, :, : lay.main] = total[:, source * lay.main : (source + 1) * lay.main]
+        start = lay.n_main + source * lay.rest
+        out_ref[source, :, lay.main :] = total[:, start : start + lay.rest]
+
+
+def pair_scratch(lay, width):
     side = pltpu.VMEM((lay.total, LANES), jnp.float32)
-    buffer = pltpu.VMEM((lay.n_main // 2, 256), jnp.float32)
-    return pl.pallas_call(
-        functools.partial(inner_kernel, lay),
-        out_shape=(row, row),
-        in_specs=list(vmem_specs(3)),
-        out_specs=vmem_specs(2),
-        scratch_shapes=[side, side, side, buffer, buffer],
-        compiler_params=pltpu.CompilerParams(vmem_limit_bytes=FAST_LIMIT),
-        cost_estimate=pair_cost(lay, mine),
-    )(mine, *rests)
-
-
-def cross_sums(lay, mine, rests, other, others, lab_lane, sums):
-    row = jax.ShapeDtypeStruct((1, lay.total), jnp.float32)
-    side = pltpu.VMEM((lay.total, LANES), jnp.float32)
-    buffer = pltpu.VMEM((lay.n_main // 2, 256), jnp.float32)
-    return pl.pallas_call(
-        functools.partial(cross_kernel, lay),
-        out_shape=(row, row, jax.ShapeDtypeStruct((8, LANES), jnp.int32)),
-        in_specs=list(vmem_specs(8)),
-        out_specs=vmem_specs(3),
-        scratch_shapes=[side, side, side, buffer, buffer],
-        compiler_params=pltpu.CompilerParams(vmem_limit_bytes=FAST_LIMIT),
-        cost_estimate=pair_cost(lay, mine),
-    )(mine, *rests, other, *others, lab_lane, sums)
+    buffer = pltpu.VMEM((lay.n_main, 256), jnp.float32)
+    rows = pltpu.VMEM((lay.total, width), jnp.bfloat16)
+    return [side, side, rows], [buffer, buffer]
 
 
 def pair_cost(lay, rows):
@@ -676,13 +593,35 @@
     )
 
 
-def join(lay, sums, more):
-    return pl.pallas_call(
-        functools.partial(join_kernel, lay),
-        out_shape=jax.ShapeDtypeStruct((lay.n_owner, 1, lay.capacity), jnp.float32),
+def inner_sums(lay, mine, rest):
+    row = jax.ShapeDtypeStruct((1, lay.total), jnp.float32)
+    sides, buffers = pair_scratch(lay, mine.shape[1])
+    return pl.pallas_call(
+        functools.partial(inner_kernel, lay),
+        out_shape=(row, row),
         in_specs=list(vmem_specs(2)),
-        out_specs=vmem_specs(1)[0],
-    )(sums, more)
+        out_specs=vmem_specs(2),
+        scratch_shapes=sides + buffers,
+        compiler_params=pltpu.CompilerParams(vmem_limit_bytes=FAST_LIMIT),
+        cost_estimate=pair_cost(lay, mine),
+    )(mine, rest)
+
+
+def cross_sums(lay, mine, rest, other, rest_other, lab_lane, sums):
+    row = pltpu.VMEM((1, lay.total), jnp.float32)
+    sides, buffers = pair_scratch(lay, mine.shape[1])
+    return pl.pallas_call(
+        functools.partial(cross_kernel, lay),
+        out_shape=(
+            jax.ShapeDtypeStruct((lay.n_owner, 1, lay.capacity), jnp.float32),
+            jax.ShapeDtypeStruct((8, LANES), jnp.int32),
+        ),
+        in_specs=list(vmem_specs(6)),
+        out_specs=vmem_specs(2),
+        scratch_shapes=sides + [row] + buffers,
+        compiler_params=pltpu.CompilerParams(vmem_limit_bytes=FAST_LIMIT),
+        cost_estimate=pair_cost(lay, mine),
+    )(mine, rest, other, rest_other, lab_lane, sums)
 
 
 def fast_unpack_kernel(values_ref, pos_ref, out_ref):
@@ -734,32 +673,27 @@
     main = -(-(rows // n_owner * 9 // 8) // 16) * 16
     if main >= capacity or n_fine >= LANES:
         return general(embeddings, labels, owner_map)
-    planes = n_owner // 2
-    plane = planes // 2 - 1
-    home = 2 * plane
+    home = n_owner // 4
     lay = Layout(n_owner, n_fine, capacity, main, home)
     unit, slot, info, extra, pos = place_rows(
         embeddings, labels, owner_map, n_owner, capacity, main, home
     )
     chunks = [
-        extra
-        if z == plane
-        else lax.ppermute(extra, "cl", [(2 * z + y, 2 * plane + y) for y in range(2)])
-        for z in range(planes)
+        extra if source == home else lax.ppermute(extra, "cl", [(source, home)])
+        for source in range(n_owner)
     ]
-    rest_a = gather_rest(chunks, lay.rest, plane)
-    rest_b = lax.ppermute(rest_a, "cl", [(home + 1, home)])
-    rests = (rest_a, rest_b)
-    swap = [(2 * home, 2 * home + 1), (2 * home + 1, 2 * home)]
-    others = tuple(lax.ppermute(x, ("cl", "grp"), swap) for x in rests)
     packed = pack_main(unit, slot, info, n_owner, main, home)
+    packed = after(packed, chunks[:home] + chunks[home + 1 :])
+    rest = gather_rest(chunks, lay.rest, home)
+    rest_other = lax.ppermute(
+        rest, ("cl", "grp"), [(2 * home, 2 * home + 1), (2 * home + 1, 2 * home)]
+    )
     mine = lax.all_to_all(
         packed.reshape(n_owner, main, width), "cl", split_axis=0, concat_axis=0, tiled=True
     ).reshape(n_owner * main, width)
     other = lax.ppermute(mine, "grp", [(0, 1), (1, 0)])
-    sums, lab_lane = inner_sums(lay, mine, rests)
-    sums, for_other, unfit = cross_sums(lay, mine, rests, other, others, lab_lane, sums)
-    results = join(lay, sums, lax.ppermute(for_other, "grp", [(0, 1), (1, 0)]))
+    sums, lab_lane = inner_sums(lay, mine, rest)
+    results, unfit = cross_sums(lay, mine, rest, other, rest_other, lab_lane, sums)
     returned = lax.all_to_all(results, "cl", split_axis=0, concat_axis=0, tiled=True)
     return lax.cond(
         unfit[0, 0] == 0,

time: 127 us -> 113 us (0.89)
  blocking collectives: 0 us -> 48.5 us
  waiting for transfers between devices: 46.5 us -> 5.37 us
  starting transfers between devices: 54.4 us -> 34.9 us
  Pallas kernels: 20.1 us -> 17.6 us
    all_to_all x0 -> x1, blocking collectives: none -> 48.5 us  [body(): lax.all_to_all(packed.reshape(n_owner, main, width), 'cl', split_axis=0,...]
    all_to_all x1 -> x0, waiting for transfers between devices: 40.3 us -> none  [body(): lax.all_to_all(packed.reshape(n_owner, main, width), 'cl', split_axis=0,...]
    all_to_all x1, starting transfers between devices: 38.1 us -> 17.4 us  [body(): lax.all_to_all(results, 'cl', split_axis=0, concat_axis=0, tiled=True)]
    ppermute x7 -> x8, starting transfers between devices: 9.09 us -> 17.4 us  [the longest x7 16.7 us: body(): lax.ppermute(extra, 'cl', [(source, home)])]
    all_to_all x1 -> x0, starting transfers between devices: 7.28 us -> none  [body(): lax.all_to_all(packed.reshape(n_owner, main, width), 'cl', split_axis=0,...]
    pallas_call x3, Pallas kernels: 9.36 us -> 7.84 us  [the longest x1 5.2 us: cross_sums(): pl.pallas_call(functools.partial(cross_kernel, lay), out_shape=(jax.Shape...]
    unnamed x24 -> x28, local copies, waits for them, and re-layouts: 4.36 us -> 4.76 us
  transfers between devices with their start and end apart: 10 -> 10, of which waited for: 3 -> 1; matrix products, arithmetic and copies ran while one was open for 0% -> 0% of each run, Pallas kernels for 5% -> 8%
where the time goes in v6:
time: 113 us
  blocking collectives  48.5 us (43%)
  starting transfers between devices  34.9 us (31%)
  Pallas kernels  17.6 us (16%)
  waiting for transfers between devices  5.37 us (5%)
  local copies, waits for them, and re-layouts  5.27 us (5%)
    all_to_all x1, blocking collectives, body(): lax.all_to_all(packed.reshape(n_owner, main, width), 'cl', split_axis=0,...  48.5 us
    all_to_all x1, starting transfers between devices, body(): lax.all_to_all(results, 'cl', split_axis=0, concat_axis=0, tiled=True)  17.4 us
    ppermute x7, starting transfers between devices, body(): lax.ppermute(extra, 'cl', [(source, home)])  16.7 us
    all_to_all x1, waiting for transfers between devices, body(): lax.all_to_all(results, 'cl', split_axis=0, concat_axis=0, tiled=True)  5.35 us
    pallas_call x1, Pallas kernels, cross_sums(): pl.pallas_call(functools.partial(cross_kernel, lay), out_shape=(jax.Shape...  5.2 us
    unnamed x28, local copies, waits for them, and re-layouts  4.76 us
    pallas_call x1, Pallas kernels, inner_sums(): pl.pallas_call(functools.partial(inner_kernel, lay), out_shape=(row, row)...  4.69 us
    pallas_call x1, Pallas kernels, place_rows(): pl.pallas_call(functools.partial(place_kernel, n_owner, capacity, main, h...  2.93 us
  transfers between devices with their start and end apart: 10, of which 1 were waited for; matrix products, arithmetic and copies ran while one was open for 0% of the time, Pallas kernels for 8%

profile of v6, /device:TPU:0, one launch (start us, length us, event | category | flops | bytes accessed | tf_op | source)
XLA Modules:
  0.0 112.5 jit_solution(16265283369925643096)
XLA Ops:
  0.0 2.9 %shard_map.39 = (bf16[1024,768]{1,0:T(8,128)(2,1)S(1)}, s32[1,1024]{1,0:T(1,128)S(1)}, f32[1,128]{1,0:T(1,128)S(1)}, bf16[128,768]{1,0:T(8,128)(2,1)S(1)}, s32[8,128]{1,0:T(8,128)S(1)}) custom-call(bf16[1024,768]{1,0:T(8,128)(2,1)} %x_hbm.1, s32[8,128]{1,0:T(8,128)} %bitcast.26, s32[1,64]{1,0:T(1,128)} %bitcast.30), custom_call_target="tpu_custom_call" | custom-call | tf_op jit(solution)/shard_map/pallas_call | solution.py:309
  2.9 0.0 copy-start.3
  3.0 0.7 collective-permute-start.7
  3.6 0.7 collective-permute-start.6
  4.3 0.7 collective-permute-start.5
  5.0 0.7 collective-permute-start.4
  5.7 0.7 collective-permute-start.3
  6.4 0.0 collective-permute-done.7.refs_7_
  6.4 0.0 copy-start.6
  6.4 0.7 collective-permute-start.2
  7.1 0.0 collective-permute-done.6.refs_6_
  7.1 0.0 copy-start.7
  7.1 12.7 %collective-permute-start.1 = (bf16[128,768]{1,0:T(8,128)(2,1)S(1)}, bf16[128,768]{1,0:T(8,128)(2,1)S(1)}, u32[]{:S(2)}, u32[]{:S(2)}) collective-permute-start(bf16[128,768]{1,0:T(8,128)(2,1)S(1)} %get-tuple-element.38.refs_2_), channel_id=1, source_target_pairs={{0,4},{1,5},{16,20},{17,21}} | collective-permute-start | bytes 589832 | tf_op jit(solution)/shard_map/ppermute | solution.py:682
  19.7 2.0 %shard_map.40.refs_0_ = bf16[1152,768]{1,0:T(8,128)(2,1)S(1)} custom-call(bf16[1024,768]{1,0:T(8,128)(2,1)S(1)} %get-tuple-element.35.unit, s32[1,1024]{1,0:T(1,128)S(1)} %get-tuple-element.36.slot_ref, f32[1,128]{1,0:T(1,128)S(1)} %get-tuple-element.37.info_ref), custom_call_target="tpu_custom_call" | custom-call | flops 1811939328 | bytes 3145728 | tf_op jit(solution)/shard_map/pallas_call | solution.py:331
  21.8 0.0 copy-done.3
  21.8 0.0 copy-done.6
  21.8 0.0 copy-done.7
  21.8 0.0 copy-start
  21.8 1.2 %copy-done = bf16[1152,768]{1,0:T(8,128)(2,1)} copy-done((bf16[1152,768]{1,0:T(8,128)(2,1)}, bf16[1152,768]{1,0:T(8,128)(2,1)S(1)}, u32[]{:S(2)}) %copy-start) | copy-done | bytes 1769496
  23.0 0.0 collective-permute-done.5.refs_5_
  23.0 0.0 copy-start.8
  23.0 0.0 collective-permute-done.4.refs_4_
  23.0 0.0 copy-start.9
  23.1 0.0 collective-permute-done.3.refs_3_
  23.1 0.0 copy-start.10
  23.1 0.0 collective-permute-done.2.refs_2_.refs_1_
  23.1 0.0 copy-start.11
  23.1 0.0 collective-permute-done.1.refs_1_.refs_0_
  23.1 0.6 copy-done.8
  23.7 0.1 copy-done.9
  23.8 0.1 copy-done.10
  23.9 0.1 copy-done.11
  23.9 0.0 copy-start.12
  23.9 0.7 copy-done.12
  24.6 48.5 %all_to_all.23 = bf16[8,144,768]{2,1,0:T(8,128)(2,1)S(1)} all-to-all(bf16[8,144,768]{2,1,0:T(8,128)(2,1)} %bitcast.17), channel_id=1, replica_groups=mesh['parts'=2,'cl'=8,'grp'=2] {'cl'}, dimensions={0} | all-to-all | bytes 3538944 | tf_op jit(solution)/shard_map/all_to_all | solution.py:691
  73.1 0.0 collective-permute-start.8
  73.1 2.6 %shard_map.42.rest.refs_1_ = bf16[1024,768]{1,0:T(8,128)(2,1)} custom-call(bf16[128,768]{1,0:T(8,128)(2,1)} %copy-done.12, bf16[128,768]{1,0:T(8,128)(2,1)} %copy-done.11, bf16[128,768]{1,0:T(8,128)(2,1)} %copy-done.3, bf16[128,768]{1,0:T(8,128)(2,1)} %copy-done.10, bf16[128,768]{1,0:T(8,128)(2,1)} %copy-done.9, bf16[128,768]{1,0:T(8,128)(2,1)} %copy-done.8, ...), custom_call_target="tpu_custom_call" | custom-call | bytes 3145728 | tf_op jit(solution)/shard_map/pallas_call | solution.py:373
  75.8 0.7 collective-permute-start.9
  76.5 0.0 copy-start.1
  76.5 1.4 %copy-done.1 = bf16[1024,768]{1,0:T(8,128)(2,1)S(1)} copy-done((bf16[1024,768]{1,0:T(8,128)(2,1)S(1)}, bf16[1024,768]{1,0:T(8,128)(2,1)}, u32[]{:S(2)}) %copy-start.1) | copy-done | bytes 1572888
  77.9 0.0 copy-start.2
  77.9 4.7 %shard_map.43 = (f32[1,2048]{1,0:T(1,128)S(1)}, f32[1,2048]{1,0:T(1,128)S(1)}) custom-call(bf16[1152,768]{1,0:T(8,128)(2,1)S(1)} %bitcast.20, bf16[1024,768]{1,0:T(8,128)(2,1)S(1)} %copy-done.1), custom_call_target="tpu_custom_call" | custom-call | flops 2038431744 | bytes 3538944 | tf_op jit(solution)/shard_map/pallas_call | solution.py:599
  82.6 0.0 collective-permute-done.9.refs_3_
  82.6 0.0 collective-permute-done.8.refs_2_
  82.6 0.0 copy-done.2
  82.7 0.0 copy-start.13
  82.7 0.0 copy-start.15
  82.7 5.2 %shard_map.44 = (f32[8,1,256]{2,1,0:T(1,128)}, s32[8,128]{1,0:T(8,128)S(1)}) custom-call(bf16[1152,768]{1,0:T(8,128)(2,1)S(1)} %bitcast.21, bf16[1024,768]{1,0:T(8,128)(2,1)S(1)} %copy-done.2, bf16[1152,768]{1,0:T(8,128)(2,1)S(1)} %collective-permute-done.8.refs_2_, bf16[1024,768]{1,0:T(8,128)(2,1)S(1)} %collective-permute-done.9.refs_3_, ...), custom_call_target="tpu_custom_call" | custom-call | flops 2038431744 | bytes 3538944 | tf_op jit(solution)/shard_map/pallas_call | solution.py:613
  87.9 17.4 %all-to-all-start.3 = ((f32[8,1,256]{2,1,0:T(1,128)}), f32[8,1,256]{2,1,0:T(1,128)S(1)}, u32[]{:S(2)}, u32[]{:S(2)}) async-start(f32[8,1,256]{2,1,0:T(1,128)} %get-tuple-element.42), calls=%async_computation.3 | async-start | bytes 16384 | tf_op jit(solution)/shard_map/all_to_all | solution.py:697
  105.3 0.5 slice.3
  106.5 5.4 %all-to-all-done.3 = f32[8,1,256]{2,1,0:T(1,128)S(1)} async-done(((f32[8,1,256]{2,1,0:T(1,128)}), f32[8,1,256]{2,1,0:T(1,128)S(1)}, u32[]{:S(2)}, u32[]{:S(2)}) %all-to-all-start.3) | async-done | bytes 8224 | tf_op jit(solution)/shard_map/all_to_all | solution.py:697
  111.8 0.0 copy-done.13
  111.8 0.0 copy-done.15
  111.8 0.1 conditional.1
  111.8 0.1 branch_1_fun.1
  111.9 0.0 copy-start.14
  111.9 0.6 copy-done.14
  (1 shorter events, 0.0 us)
Async XLA Ops:
  2.9 18.8 %copy-start.3 = (bf16[128,768]{1,0:T(8,128)(2,1)}, bf16[128,768]{1,0:T(8,128)(2,1)S(1)}, u32[]{:S(2)}) copy-start(bf16[128,768]{1,0:T(8,128)(2,1)S(1)} %get-tuple-element.38.refs_2_) | copy-start | bytes 589828
  3.0 3.4 %collective-permute-start.7 = (bf16[128,768]{1,0:T(8,128)(2,1)S(1)}, bf16[128,768]{1,0:T(8,128)(2,1)S(1)}, u32[]{:S(2)}, u32[]{:S(2)}) collective-permute-start(bf16[128,768]{1,0:T(8,128)(2,1)S(1)} %get-tuple-element.38.refs_2_), channel_id=1, source_target_pairs={{14,4},{15,5},{30,20},{31,21}} | collective-permute-start | bytes 589832 | tf_op jit(solution)/shard_map/ppermute | solution.py:682
  3.6 3.4 %collective-permute-start.6 = (bf16[128,768]{1,0:T(8,128)(2,1)S(1)}, bf16[128,768]{1,0:T(8,128)(2,1)S(1)}, u32[]{:S(2)}, u32[]{:S(2)}) collective-permute-start(bf16[128,768]{1,0:T(8,128)(2,1)S(1)} %get-tuple-element.38.refs_2_), channel_id=1, source_target_pairs={{12,4},{13,5},{28,20},{29,21}} | collective-permute-start | bytes 589832 | tf_op jit(solution)/shard_map/ppermute | solution.py:682
  4.3 18.7 %collective-permute-start.5 = (bf16[128,768]{1,0:T(8,128)(2,1)S(1)}, bf16[128,768]{1,0:T(8,128)(2,1)S(1)}, u32[]{:S(2)}, u32[]{:S(2)}) collective-permute-start(bf16[128,768]{1,0:T(8,128)(2,1)S(1)} %get-tuple-element.38.refs_2_), channel_id=1, source_target_pairs={{10,4},{11,5},{26,20},{27,21}} | collective-permute-start | bytes 589832 | tf_op jit(solution)/shard_map/ppermute | solution.py:682
  5.0 18.0 %collective-permute-start.4 = (bf16[128,768]{1,0:T(8,128)(2,1)S(1)}, bf16[128,768]{1,0:T(8,128)(2,1)S(1)}, u32[]{:S(2)}, u32[]{:S(2)}) collective-permute-start(bf16[128,768]{1,0:T(8,128)(2,1)S(1)} %get-tuple-element.38.refs_2_), channel_id=1, source_target_pairs={{8,4},{9,5},{24,20},{25,21}} | collective-permute-start | bytes 589832 | tf_op jit(solution)/shard_map/ppermute | solution.py:682
  5.7 17.4 %collective-permute-start.3 = (bf16[128,768]{1,0:T(8,128)(2,1)S(1)}, bf16[128,768]{1,0:T(8,128)(2,1)S(1)}, u32[]{:S(2)}, u32[]{:S(2)}) collective-permute-start(bf16[128,768]{1,0:T(8,128)(2,1)S(1)} %get-tuple-element.38.refs_2_), channel_id=1, source_target_pairs={{6,4},{7,5},{22,20},{23,21}} | collective-permute-start | bytes 589832 | tf_op jit(solution)/shard_map/ppermute | solution.py:682
  6.4 15.4 %copy-start.6 = (bf16[128,768]{1,0:T(8,128)(2,1)}, bf16[128,768]{1,0:T(8,128)(2,1)S(1)}, u32[]{:S(2)}) copy-start(bf16[128,768]{1,0:T(8,128)(2,1)S(1)} %collective-permute-done.7.refs_7_) | copy-start | bytes 589828
  6.4 16.7 %collective-permute-start.2 = (bf16[128,768]{1,0:T(8,128)(2,1)S(1)}, bf16[128,768]{1,0:T(8,128)(2,1)S(1)}, u32[]{:S(2)}, u32[]{:S(2)}) collective-permute-start(bf16[128,768]{1,0:T(8,128)(2,1)S(1)} %get-tuple-element.38.refs_2_), channel_id=1, source_target_pairs={{2,4},{3,5},{18,20},{19,21}} | collective-permute-start | bytes 589832 | tf_op jit(solution)/shard_map/ppermute | solution.py:682
  7.1 14.7 %copy-start.7 = (bf16[128,768]{1,0:T(8,128)(2,1)}, bf16[128,768]{1,0:T(8,128)(2,1)S(1)}, u32[]{:S(2)}) copy-start(bf16[128,768]{1,0:T(8,128)(2,1)S(1)} %collective-permute-done.6.refs_6_) | copy-start | bytes 589828
  7.1 16.0 %collective-permute-start.1 = (bf16[128,768]{1,0:T(8,128)(2,1)S(1)}, bf16[128,768]{1,0:T(8,128)(2,1)S(1)}, u32[]{:S(2)}, u32[]{:S(2)}) collective-permute-start(bf16[128,768]{1,0:T(8,128)(2,1)S(1)} %get-tuple-element.38.refs_2_), channel_id=1, source_target_pairs={{0,4},{1,5},{16,20},{17,21}} | collective-permute-start | bytes 589832 | tf_op jit(solution)/shard_map/ppermute | solution.py:682
  21.8 1.2 %copy-start = (bf16[1152,768]{1,0:T(8,128)(2,1)}, bf16[1152,768]{1,0:T(8,128)(2,1)S(1)}, u32[]{:S(2)}) copy-start(bf16[1152,768]{1,0:T(8,128)(2,1)S(1)} %shard_map.40.refs_0_) | copy-start | bytes 5308420
  23.0 0.7 copy-start.8
  23.0 0.8 copy-start.9
  23.1 0.8 copy-start.10
  23.1 0.8 copy-start.11
  23.9 0.7 copy-start.12
  73.1 9.5 %collective-permute-start.8 = (bf16[1152,768]{1,0:T(8,128)(2,1)S(1)}, bf16[1152,768]{1,0:T(8,128)(2,1)S(1)}, u32[]{:S(2)}, u32[]{:S(2)}) collective-permute-start(bf16[1152,768]{1,0:T(8,128)(2,1)S(1)} %bitcast.19), channel_id=1, source_target_pairs={{0,1},{1,0},{2,3},{3,2},{4,5},{5,4},{6,7},{7,6},{8,9},{9,8},{10,11... | collective-permute-start | bytes 5308424 | tf_op jit(solution)/shard_map/ppermute | solution.py:694
  75.8 6.9 %collective-permute-start.9 = (bf16[1024,768]{1,0:T(8,128)(2,1)}, bf16[1024,768]{1,0:T(8,128)(2,1)S(1)}, u32[]{:S(2)}, u32[]{:S(2)}) collective-permute-start(bf16[1024,768]{1,0:T(8,128)(2,1)} %shard_map.42.rest.refs_1_), channel_id=1, source_target_pairs={{4,5},{5,4},{20,21},{21,20}} | collective-permute-start | bytes 4718600 | tf_op jit(solution)/shard_map/ppermute | solution.py:688
  76.5 1.4 %copy-start.1 = (bf16[1024,768]{1,0:T(8,128)(2,1)S(1)}, bf16[1024,768]{1,0:T(8,128)(2,1)}, u32[]{:S(2)}) copy-start(bf16[1024,768]{1,0:T(8,128)(2,1)} %shard_map.42.rest.refs_1_) | copy-start | bytes 4718596
  77.9 4.7 %copy-start.2 = (bf16[1024,768]{1,0:T(8,128)(2,1)S(1)}, bf16[1024,768]{1,0:T(8,128)(2,1)}, u32[]{:S(2)}) copy-start(bf16[1024,768]{1,0:T(8,128)(2,1)} %shard_map.42.rest.refs_1_) | copy-start | bytes 4718596
  82.7 29.2 %copy-start.13 = (s32[1024]{0:T(1024)S(1)}, s32[1024]{0:T(1024)}, u32[]{:S(2)}) copy-start(s32[1024]{0:T(1024)} %param.6) | copy-start | bytes 12292
  82.7 29.2 %copy-start.15 = (s32[64]{0:T(128)S(1)}, s32[64]{0:T(128)}, u32[]{:S(2)}) copy-start(s32[64]{0:T(128)} %param.7) | copy-start | bytes 772
  87.9 23.9 %all-to-all-start.3 = ((f32[8,1,256]{2,1,0:T(1,128)}), f32[8,1,256]{2,1,0:T(1,128)S(1)}, u32[]{:S(2)}, u32[]{:S(2)}) async-start(f32[8,1,256]{2,1,0:T(1,128)} %get-tuple-element.42), calls=%async_computation.3 | async-start | bytes 16384 | tf_op jit(solution)/shard_map/all_to_all | solution.py:697
  111.9 0.6 copy-start.14

commit v7 on v1

--- a/solution.py
+++ b/solution.py
@@ -19,6 +19,8 @@
 NEIGHBOUR = math.log2(neighbour_factor)
 DEAD = -1e30
 VMEM_LIMIT = 48 * 1024 * 1024
+FAST_LIMIT = 40 * 1024 * 1024
+INFO = 16
 
 
 def column_of(row):
@@ -211,7 +213,425 @@
     )(values.reshape(-1, LANES), pos)
 
 
-def body(embeddings, labels, owner_map):
+def swapped(x, first, second):
+    return jnp.where(x == first, second, jnp.where(x == second, first, x))
+
+
+def place_kernel(lay, x_hbm, lab_hbm, map_hbm, *refs):
+    n_owner, capacity, main, home = lay.n_owner, lay.capacity, lay.main, lay.home
+    unit, slot_ref, info_ref, extra_ref, pos_ref, x_ref, lab_ref, map_ref, sems = refs
+    copies = [
+        pltpu.make_async_copy(src, dst, sems.at[i])
+        for i, (src, dst) in enumerate(((x_hbm, x_ref), (lab_hbm, lab_ref), (map_hbm, map_ref)))
+    ]
+    for copy in copies:
+        copy.start()
+    rows = x_ref.shape[0]
+    n_fine = map_ref.shape[1]
+    per_owner = n_fine // n_owner
+    copies[1].wait()
+    copies[2].wait()
+    owner_row = map_ref[...].astype(jnp.float32)
+    fine_row = lax.broadcasted_iota(jnp.int32, (1, n_fine), 1).astype(jnp.float32)
+    key_row = owner_row * n_fine + fine_row
+    key_col = column_of(key_row)
+    sorted_col = jnp.sum(jnp.where(key_row < key_col, 1.0, 0.0), axis=1, keepdims=True)
+    lab = lab_ref[...].astype(jnp.float32)
+    lab_row = jnp.concatenate([lab[b : b + 1, :] for b in range(lab.shape[0])], axis=1)
+    fine_col = lax.broadcasted_iota(jnp.int32, (n_fine, rows), 0).astype(jnp.float32)
+    fine_id = jnp.sum(jnp.where(fine_col == lab_row, sorted_col, 0.0), axis=0, keepdims=True)
+    counts_col = jnp.sum(jnp.where(fine_col == fine_id, 1.0, 0.0), axis=1, keepdims=True)
+    coarse = jnp.floor((fine_id + 0.5) * (1.0 / per_owner))
+    first = coarse * per_owner
+    before = jnp.sum(jnp.where(fine_col < first, counts_col, 0.0), axis=0, keepdims=True)
+    upto = jnp.sum(jnp.where(fine_col < first + per_owner, counts_col, 0.0), axis=0, keepdims=True)
+    full = jnp.min(
+        jnp.where(upto - before == capacity, coarse, float(n_owner)), axis=1, keepdims=True
+    )
+    line = lax.broadcasted_iota(jnp.int32, (n_fine, LANES), 0)
+    lane = lax.broadcasted_iota(jnp.int32, (n_fine, LANES), 1)
+    inside = (line <= lane) & (lax.div(line, per_owner) == lax.div(lane, per_owner))
+    running = jnp.sum(jnp.where(inside, counts_col, 0.0), axis=0, keepdims=True)
+    info = jnp.where(lane[:1] < n_fine, running, full)
+    info_ref[...] = info
+    index = lax.broadcasted_iota(jnp.int32, (1, rows), 1).astype(jnp.float32)
+    row_key = fine_id * rows + index
+    rank = jnp.zeros((1, rows), jnp.float32)
+    for start in range(0, rows, LANES):
+        other = column_of(row_key[:, start : start + LANES])
+        rank = rank + jnp.sum(jnp.where(other < row_key, 1.0, 0.0), axis=0, keepdims=True)
+    rank = (rank - before).astype(jnp.int32)
+    place = swapped(coarse.astype(jnp.int32), full.astype(jnp.int32), home)
+    table = place * capacity + rank
+    pos_ref[...] = jnp.concatenate(
+        [table[:, start : start + LANES] for start in range(0, rows, LANES)], axis=0
+    )
+    later = jnp.where(place == home, lay.n_main + rank - lay.head, -1)
+    fits = rank < jnp.where(place == home, lay.head, main - 1)
+    slot = jnp.where(fits, place * main + rank, later)
+    slot_ref[...] = slot
+    copies[0].wait()
+    x = x_ref[...].astype(jnp.float32)
+    squares = jnp.sum(x * x, axis=1, keepdims=True)
+    unit[...] = (x * lax.rsqrt(squares + epsilon)).astype(jnp.bfloat16)
+    extra_ref[...] = chosen_rows(unit, slot, lay.n_main, lay.rest)
+
+
+def chosen_rows(unit, slot, start, count):
+    here = lax.broadcasted_iota(jnp.int32, (count, unit.shape[0]), 0) + start
+    chosen = jnp.where(here == slot, 1.0, 0.0).astype(jnp.bfloat16)
+    return jnp.dot(chosen, unit[...], preferred_element_type=jnp.float32).astype(jnp.bfloat16)
+
+
+def main_kernel(lay, unit, slot_ref, info_ref, main_ref):
+    count = lay.n_main // 4
+    for start in range(0, lay.n_main, count):
+        main_ref[start : start + count, :] = chosen_rows(unit, slot_ref[...], start, count)
+    for owner in range(lay.n_owner):
+        tail = slice((owner + 1) * lay.main - INFO, (owner + 1) * lay.main)
+        old = main_ref[tail, :LANES].astype(jnp.float32)
+        down = lax.broadcasted_iota(jnp.int32, old.shape, 0)
+        new = jnp.where(down == INFO - 1, info_ref[...], old)
+        main_ref[tail, :LANES] = new.astype(jnp.bfloat16)
+
+
+def vmem_specs(count):
+    return (pl.BlockSpec(memory_space=pltpu.VMEM),) * count
+
+
+def place_rows(embeddings, labels, owner_map, lay):
+    rows, width = embeddings.shape
+    n_fine = owner_map.shape[0]
+    lab_shape = (rows // LANES, LANES)
+    return pl.pallas_call(
+        functools.partial(place_kernel, lay),
+        out_shape=(
+            jax.ShapeDtypeStruct((rows, width), jnp.bfloat16),
+            jax.ShapeDtypeStruct((1, rows), jnp.int32),
+            jax.ShapeDtypeStruct((1, LANES), jnp.float32),
+            jax.ShapeDtypeStruct((lay.rest, width), jnp.bfloat16),
+            jax.ShapeDtypeStruct(lab_shape, jnp.int32),
+        ),
+        in_specs=[pl.BlockSpec(memory_space=pl.ANY)] * 3,
+        out_specs=vmem_specs(5),
+        scratch_shapes=[
+            pltpu.VMEM((rows, width), jnp.bfloat16),
+            pltpu.VMEM(lab_shape, jnp.int32),
+            pltpu.VMEM((1, n_fine), jnp.int32),
+            pltpu.SemaphoreType.DMA((3,)),
+        ],
+        compiler_params=pltpu.CompilerParams(vmem_limit_bytes=FAST_LIMIT),
+    )(embeddings, labels.reshape(lab_shape), owner_map.reshape(1, n_fine))
+
+
+def pack_main(unit, slot, info, lay):
+    return pl.pallas_call(
+        functools.partial(main_kernel, lay),
+        out_shape=jax.ShapeDtypeStruct((lay.n_main, unit.shape[1]), jnp.bfloat16),
+        in_specs=list(vmem_specs(3)),
+        out_specs=vmem_specs(1)[0],
+        compiler_params=pltpu.CompilerParams(vmem_limit_bytes=FAST_LIMIT),
+        cost_estimate=pl.CostEstimate(
+            flops=2 * lay.n_main * unit.shape[0] * unit.shape[1],
+            bytes_accessed=4 * unit.shape[0] * unit.shape[1],
+            transcendentals=0,
+        ),
+    )(unit, slot, info)
+
+
+def gate_kernel(*refs):
+    pass
+
+
+def after(rows, received):
+    anywhere = pl.BlockSpec(memory_space=pl.ANY)
+    return pl.pallas_call(
+        gate_kernel,
+        out_shape=jax.ShapeDtypeStruct(rows.shape, rows.dtype),
+        in_specs=[anywhere] * 2,
+        out_specs=anywhere,
+        input_output_aliases={0: 0},
+    )(rows, received)
+
+
+class Layout:
+    def __init__(self, n_owner, n_fine, capacity, main, home):
+        self.n_owner, self.n_fine, self.capacity = n_owner, n_fine, capacity
+        self.main, self.home = main, home
+        self.head = main - INFO
+        self.rest = capacity - self.head
+        self.per_owner = n_fine // n_owner
+        self.n_main = n_owner * main
+        self.n_head = n_owner * self.head
+        self.n_rest = n_owner * self.rest
+
+
+def info_line(lay, main_ref, source):
+    end = (source + 1) * lay.main
+    return main_ref[end - INFO : end, :LANES].astype(jnp.float32)[INFO - 1 :]
+
+
+def lines_of(lay, main_ref):
+    return [info_line(lay, main_ref, source) for source in range(lay.n_owner)]
+
+
+def hot_of(lay, info):
+    lane = lax.broadcasted_iota(jnp.int32, (1, LANES), 1)
+    hot = jnp.max(jnp.where(lane == lay.n_fine, info, 0.0), axis=1, keepdims=True)
+    return hot.astype(jnp.int32)
+
+
+def write_labels(lay, infos, first, count, at, lab_sub, bias):
+    cluster = swapped(lax.axis_index("cl"), hot_of(lay, infos[0]), lay.home)
+    lane = lax.broadcasted_iota(jnp.int32, (1, LANES), 1)
+    is_edge = lax.div(lane, lay.per_owner) == cluster
+    for source, info in enumerate(infos):
+        edges = jnp.where(is_edge, info, 2.0 * lay.capacity)
+        slot = lax.broadcasted_iota(jnp.int32, (count, LANES), 0) + first
+        label = jnp.where(slot.astype(jnp.float32) >= edges, 1.0, 0.0)
+        label = jnp.broadcast_to(jnp.sum(label, axis=1, keepdims=True), (count, LANES))
+        start = at + source * count
+        lab_sub[start : start + count, :] = label
+        bias[start : start + count, :] = jnp.where(label < lay.per_owner, NEIGHBOUR - SCALE, DEAD)
+
+
+def turn_labels(lay, lab_sub, start, count, lab_lane, at):
+    for i in range(0, count, LANES):
+        block = jnp.transpose(lab_sub[start + i : start + i + LANES, :])[:1]
+        lab_lane[:, at + i : at + i + LANES] = jnp.where(block < lay.per_owner, block, -1.0)
+
+
+def copy_head(lay, main_ref, rows):
+    for source in range(lay.n_owner):
+        rows[source * lay.head : (source + 1) * lay.head, :] = main_ref[
+            source * lay.main : source * lay.main + lay.head, :
+        ]
+
+
+def pieces(start, count, parts):
+    return [(start + i * (count // parts), count // parts) for i in range(parts)]
+
+
+def stream(rows_i, first, count, tiles, lab_lane, at, lab_sub, bias, buffers, put):
+    step = 32
+    tiles = [(ref, s, d, place + s - start) for ref, start, n, place, parts in tiles for s, d in pieces(start, n, parts)]
+
+    def scores_to(buffer, tile, rows):
+        ref, start, deep, _ = tile
+        buffer[:deep, : rows.shape[0]] = lax.dot_general(
+            ref[start : start + deep, :],
+            rows,
+            (((1,), (1,)), ((), ())),
+            preferred_element_type=jnp.float32,
+        )
+
+    def run(start, blocks, wide):
+        repeat = wide // LANES
+
+        def rows_of(block):
+            return rows_i[pl.ds(pl.multiple_of(first + start + block * wide, LANES), wide), :]
+
+        scores_to(buffers[0], tiles[0], rows_of(0))
+
+        def body(block, carry):
+            here = rows_of(block)
+            place = pl.ds(pl.multiple_of(at + start + block * wide, LANES), wide)
+            label_i = lab_lane[:, place]
+            acc = jnp.zeros((8, wide), jnp.float32)
+            for i, (_, _, deep, line) in enumerate(tiles):
+                if i + 1 < len(tiles):
+                    scores_to(buffers[(i + 1) % 2], tiles[i + 1], here)
+                else:
+                    scores_to(buffers[0], tiles[0], rows_of(jnp.minimum(block + 1, blocks - 1)))
+                buffer = buffers[i % 2]
+                for c in range(0, deep, step):
+                    part = slice(line + c, line + c + step)
+                    label_j = jnp.concatenate([lab_sub[part, :]] * repeat, axis=1)
+                    bias_j = jnp.concatenate([bias[part, :]] * repeat, axis=1)
+                    shift = jnp.where(label_j == label_i, -SCALE, bias_j)
+                    terms = jnp.exp2(buffer[c : c + step, :wide] * SCALE + shift)
+                    acc = acc + jnp.sum(terms.reshape(step // 8, 8, wide), axis=0)
+            put(place, jnp.sum(acc, axis=0, keepdims=True))
+            return carry
+
+        lax.fori_loop(0, blocks, body, 0)
+
+    wide = 256
+    if count >= wide:
+        run(0, count // wide, wide)
+    if count % wide:
+        run(count - count % wide, 1, count % wide)
+
+
+def setter(ref):
+    def put(place, values):
+        ref[:, place] = values
+
+    return put
+
+
+def adder(ref):
+    def put(place, values):
+        ref[:, place] += values
+
+    return put
+
+
+def inner_kernel(lay, mine, sums, lab_lane, lab_sub, bias, rows, buf_a, buf_b):
+    is_home = lax.axis_index("cl") == lay.home
+    infos = lines_of(lay, mine)
+
+    def work(ref, count, per):
+        write_labels(lay, infos, 0, per, 0, lab_sub, bias)
+        turn_labels(lay, lab_sub, 0, count, lab_lane, 0)
+        tiles = [(ref, 0, count, 0, 4)]
+        stream(ref, 0, count, tiles, lab_lane, 0, lab_sub, bias, (buf_a, buf_b), setter(sums))
+
+    @pl.when(is_home)
+    def _():
+        copy_head(lay, mine, rows)
+        work(rows, lay.n_head, lay.head)
+
+    @pl.when(jnp.logical_not(is_home))
+    def _():
+        work(mine, lay.n_main, lay.main)
+
+
+def cross_kernel(lay, mine, other, sums, lab_lane, total, unfit_ref, lab_sub, bias, rows, rows_j, buf_a, buf_b):
+    is_home = lax.axis_index("cl") == lay.home
+    infos = lines_of(lay, other)
+    own = lines_of(lay, mine)
+    hot = hot_of(lay, own[0])
+    lane = lax.broadcasted_iota(jnp.int32, (1, LANES), 1)
+    last = (lane < lay.n_fine) & (lax.rem(lane, lay.per_owner) == lay.per_owner - 1)
+    last = last & (lax.div(lane, lay.per_owner) != hot)
+    unfit = jnp.zeros((1, LANES), jnp.float32)
+    for info in infos + own:
+        wrong = last & (info >= lay.main)
+        differs = (info != hot.astype(jnp.float32)) | (info >= lay.n_owner)
+        wrong = wrong | ((lane == lay.n_fine) & differs)
+        unfit = unfit + jnp.where(wrong, 1.0, 0.0)
+    unfit_ref[...] = jnp.broadcast_to(
+        jnp.max(unfit, axis=1, keepdims=True), unfit_ref.shape
+    ).astype(jnp.int32)
+    total[...] = sums[...]
+
+    def work(ref, ref_j, count, per):
+        write_labels(lay, infos, 0, per, 0, lab_sub, bias)
+        tiles = [(ref_j, 0, count, 0, 4)]
+        stream(ref, 0, count, tiles, lab_lane, 0, lab_sub, bias, (buf_a, buf_b), adder(total))
+
+    @pl.when(is_home)
+    def _():
+        copy_head(lay, mine, rows)
+        copy_head(lay, other, rows_j)
+        work(rows, rows_j, lay.n_head, lay.head)
+
+    @pl.when(jnp.logical_not(is_home))
+    def _():
+        work(mine, other, lay.n_main, lay.main)
+
+
+def rest_pairs(lay, rows, rest, rows_j, rest_j, lab_lane, lab_sub, bias, buffers, put):
+    seconds = (rest_j, 0, lay.n_rest, lay.n_head, 4)
+    mains = (rows_j, 0, lay.n_head, 0, 4)
+    stream(rows, 0, lay.n_head, [seconds], lab_lane, 0, lab_sub, bias, buffers, put)
+    stream(
+        rest, 0, lay.n_rest, [seconds, mains], lab_lane, lay.n_head, lab_sub, bias, buffers, put
+    )
+
+
+def inner_rest_kernel(lay, mine, rest, sums, lab_lane, lab_sub, bias, rows, buf_a, buf_b):
+    @pl.when(lax.axis_index("cl") == lay.home)
+    def _():
+        infos = lines_of(lay, mine)
+        write_labels(lay, infos, 0, lay.head, 0, lab_sub, bias)
+        write_labels(lay, infos, lay.head, lay.rest, lay.n_head, lab_sub, bias)
+        turn_labels(lay, lab_sub, 0, lay.n_head + lay.n_rest, lab_lane, 0)
+        copy_head(lay, mine, rows)
+        buffers = (buf_a, buf_b)
+        rest_pairs(lay, rows, rest, rows, rest, lab_lane, lab_sub, bias, buffers, setter(sums))
+
+
+def cross_rest_kernel(lay, *refs):
+    mine, rest, other, rest_other, main_sums, main_lane, sums, lab_lane = refs[:8]
+    out_ref, lab_sub, bias, rows, rows_j, total, buf_a, buf_b = refs[8:]
+    is_home = lax.axis_index("cl") == lay.home
+
+    @pl.when(is_home)
+    def _():
+        infos = lines_of(lay, other)
+        write_labels(lay, infos, 0, lay.head, 0, lab_sub, bias)
+        write_labels(lay, infos, lay.head, lay.rest, lay.n_head, lab_sub, bias)
+        copy_head(lay, mine, rows)
+        copy_head(lay, other, rows_j)
+        total[...] = sums[...]
+        total[:, : lay.n_head] += main_sums[:, : lay.n_head]
+        buffers = (buf_a, buf_b)
+        rest_pairs(
+            lay, rows, rest, rows_j, rest_other, lab_lane, lab_sub, bias, buffers, adder(total)
+        )
+        values = jnp.log(total[...])
+        for source in range(lay.n_owner):
+            start = source * lay.head
+            out_ref[source, :, : lay.head] = values[:, start : start + lay.head]
+            start = lay.n_head + source * lay.rest
+            out_ref[source, :, lay.head :] = values[:, start : start + lay.rest]
+
+    @pl.when(jnp.logical_not(is_home))
+    def _():
+        values = jnp.log(jnp.where(main_lane[...] >= 0, main_sums[...], 1.0))
+        for source in range(lay.n_owner):
+            start = source * lay.main
+            out_ref[source, :, : lay.main] = values[:, start : start + lay.main]
+
+
+def pair_call(kernel, lay, arrays, out_shape, lines, joins, more=()):
+    width = arrays[0].shape[1]
+    side = pltpu.VMEM((lines, LANES), jnp.float32)
+    rows = pltpu.VMEM((lay.n_head, width), jnp.bfloat16)
+    buffer = pltpu.VMEM((lay.n_main // 4, 256), jnp.float32)
+    out = pl.pallas_call(
+        functools.partial(kernel, lay),
+        out_shape=out_shape,
+        in_specs=list(vmem_specs(len(arrays))),
+        out_specs=vmem_specs(len(out_shape)),
+        scratch_shapes=[side, side] + [rows] * joins + list(more) + [buffer, buffer],
+        compiler_params=pltpu.CompilerParams(vmem_limit_bytes=FAST_LIMIT),
+        cost_estimate=pl.CostEstimate(
+            flops=2 * lay.n_main * lay.n_main * width,
+            bytes_accessed=4 * lay.n_main * width,
+            transcendentals=lay.n_main * lay.n_main,
+        ),
+    )(*arrays)
+    return out
+
+
+def fast_unpack_kernel(values_ref, pos_ref, out_ref):
+    pos = pos_ref[...]
+    lane = lax.rem(pos, LANES)
+    line = lax.div(pos, LANES)
+    out = jnp.zeros(pos.shape, jnp.float32)
+    per = values_ref.shape[2] // LANES
+    for r in range(values_ref.shape[0] * per):
+        start = r % per * LANES
+        table = jnp.broadcast_to(values_ref[r // per, :, start : start + LANES], pos.shape)
+        found = jnp.take_along_axis(table, lane, axis=1)
+        out = jnp.where(line == r, found, out)
+    out_ref[...] = out
+
+
+def fast_unpack(values, pos):
+    vmem = pl.BlockSpec(memory_space=pltpu.VMEM)
+    return pl.pallas_call(
+        fast_unpack_kernel,
+        out_shape=jax.ShapeDtypeStruct(pos.shape, jnp.float32),
+        in_specs=[vmem, vmem],
+        out_specs=vmem,
+    )(values, pos)
+
+
+def general(embeddings, labels, owner_map):
     n_owner = lax.axis_size("cl")
     capacity = SLOTS // n_owner
     rows, width = embeddings.shape
@@ -228,6 +648,65 @@
     return unpack(returned.reshape(SLOTS), pos).reshape(rows)
 
 
+def body(embeddings, labels, owner_map):
+    n_owner = lax.axis_size("cl")
+    capacity = SLOTS // n_owner
+    rows, width = embeddings.shape
+    n_fine = owner_map.shape[0]
+    main = -(-(rows // n_owner * 9 // 8) // 16) * 16
+    if main >= capacity or n_fine >= LANES:
+        return general(embeddings, labels, owner_map)
+    planes = n_owner // 2
+    plane = planes // 2 - 1
+    home = 2 * plane
+    lay = Layout(n_owner, n_fine, capacity, main, home)
+    unit, slot, info, extra, pos = place_rows(embeddings, labels, owner_map, lay)
+    moved = lax.ppermute(extra, "cl", [(2 * z + 1, 2 * z) for z in range(planes)])
+    both = jnp.concatenate([extra, moved], axis=0)
+    packed = after(pack_main(unit, slot, info, lay), both)
+    mine = lax.all_to_all(
+        packed.reshape(n_owner, main, width), "cl", split_axis=0, concat_axis=0, tiled=True
+    ).reshape(n_owner * main, width)
+    rest = jnp.concatenate(
+        [
+            both if z == plane else lax.ppermute(both, "cl", [(2 * z, home)])
+            for z in range(planes)
+        ],
+        axis=0,
+    )
+    other = lax.ppermute(mine, "grp", [(0, 1), (1, 0)])
+    rest_other = lax.ppermute(
+        rest, ("cl", "grp"), [(2 * home, 2 * home + 1), (2 * home + 1, 2 * home)]
+    )
+    row = jax.ShapeDtypeStruct((1, lay.n_main), jnp.float32)
+    long_row = jax.ShapeDtypeStruct((1, lay.n_head + lay.n_rest), jnp.float32)
+    flag = jax.ShapeDtypeStruct((8, LANES), jnp.int32)
+    table = jax.ShapeDtypeStruct((n_owner, 1, capacity), jnp.float32)
+    sums, main_lane = pair_call(inner_kernel, lay, (mine,), (row, row), lay.n_main, 1)
+    sums, unfit = pair_call(
+        cross_kernel, lay, (mine, other, sums, main_lane), (row, flag), lay.n_main, 2
+    )
+    lines = lay.n_head + lay.n_rest
+    rest_sums, lane = pair_call(
+        inner_rest_kernel, lay, (mine, rest), (long_row, long_row), lines, 1
+    )
+    (results,) = pair_call(
+        cross_rest_kernel,
+        lay,
+        (mine, rest, other, rest_other, sums, main_lane, rest_sums, lane),
+        (table,),
+        lines,
+        2,
+        (pltpu.VMEM(long_row.shape, jnp.float32),),
+    )
+    returned = lax.all_to_all(results, "cl", split_axis=0, concat_axis=0, tiled=True)
+    return lax.cond(
+        unfit[0, 0] == 0,
+        lambda: fast_unpack(returned, pos).reshape(rows),
+        lambda: general(embeddings, labels, owner_map),
+    )
+
+
 def solution(mesh):
     return jax.shard_map(
         body,

time: 144 us -> 113 us (0.78)
  blocking collectives: 107 us -> 0 us
  waiting for transfers between devices: 0.01 us -> 53.5 us
  starting transfers between devices: 0.01 us -> 37.1 us
  Pallas kernels: 32.3 us -> 13.9 us
  local copies, waits for them, and re-layouts: 4.97 us -> 7.43 us
    all_to_all x2 -> x0, blocking collectives: 87.3 us -> none  [the longest x1 77.8 us: body(): lax.all_to_all(packed.reshape(n_owner, capacity, width), 'cl', split_axis...]
    ppermute x0 -> x5, waiting for transfers between devices: none -> 33.5 us  [the longest x3 29.6 us: body(): lax.ppermute(both, 'cl', [(2 * z, home)])]
    all_to_all x0 -> x2, starting transfers between devices: none -> 28.2 us  [the longest x1 22.5 us: body(): lax.all_to_all(results, 'cl', split_axis=0, concat_axis=0, tiled=True)]
    all_to_all x0 -> x2, waiting for transfers between devices: none -> 20.1 us  [the longest x1 14.7 us: body(): lax.all_to_all(packed.reshape(n_owner, main, width), 'cl', split_axis=0,...]
    all_gather x1 -> x0, blocking collectives: 19.3 us -> none  [body(): counts = lax.all_gather(counts, ('cl', 'grp'), tiled=True)]
    pallas_call x3 -> x8, Pallas kernels: 32.3 us -> 13.9 us  [the longest x4 8.82 us: pair_call(): pl.pallas_call(functools.partial(kernel, lay), out_shape=out_shape, in_sp...]
    ppermute x0 -> x5, starting transfers between devices: none -> 8.82 us  [the longest x3 6.77 us: body(): lax.ppermute(both, 'cl', [(2 * z, home)])]
    concatenate x0 -> x2, local copies, waits for them, and re-layouts: none -> 1.71 us  [the longest x1 1.02 us: body(): jnp.concatenate([both if z == plane else lax.ppermute(both, 'cl', [(2 * z...]
  transfers between devices with their start and end apart: 1 -> 8, of which waited for: 0 -> 4; matrix products, arithmetic and copies ran while one was open for 0% -> 4% of each run, Pallas kernels for 0% -> 9%
where the time goes in v7:
time: 113 us
  waiting for transfers between devices  53.5 us (47%)
  starting transfers between devices  37.1 us (33%)
  Pallas kernels  13.9 us (12%)
  local copies, waits for them, and re-layouts  7.43 us (7%)
    ppermute x3, waiting for transfers between devices, body(): lax.ppermute(both, 'cl', [(2 * z, home)])  29.6 us
    all_to_all x1, starting transfers between devices, body(): lax.all_to_all(results, 'cl', split_axis=0, concat_axis=0, tiled=True)  22.5 us
    all_to_all x1, waiting for transfers between devices, body(): lax.all_to_all(packed.reshape(n_owner, main, width), 'cl', split_axis=0,...  14.7 us
    pallas_call x4, Pallas kernels, pair_call(): pl.pallas_call(functools.partial(kernel, lay), out_shape=out_shape, in_sp...  8.82 us
    ppermute x3, starting transfers between devices, body(): lax.ppermute(both, 'cl', [(2 * z, home)])  6.77 us
    all_to_all x1, starting transfers between devices, body(): lax.all_to_all(packed.reshape(n_owner, main, width), 'cl', split_axis=0,...  5.71 us
    all_to_all x1, waiting for transfers between devices, body(): lax.all_to_all(results, 'cl', split_axis=0, concat_axis=0, tiled=True)  5.35 us
    unnamed x15, local copies, waits for them, and re-layouts  5.2 us
  transfers between devices with their start and end apart: 8, of which 4 were waited for; matrix products, arithmetic and copies ran while one was open for 4% of the time, Pallas kernels for 9%

profile of v7, /device:TPU:0, one launch (start us, length us, event | category | flops | bytes accessed | tf_op | source)
XLA Modules:
  0.0 112.7 jit_solution(17332669263068942993)
XLA Ops:
  0.0 2.9 %shard_map.39 = (bf16[1024,768]{1,0:T(8,128)(2,1)S(1)}, s32[1,1024]{1,0:T(1,128)S(1)}, f32[1,128]{1,0:T(1,128)S(1)}, bf16[128,768]{1,0:T(8,128)(2,1)S(1)}, s32[8,128]{1,0:T(8,128)S(1)}) custom-call(bf16[1024,768]{1,0:T(8,128)(2,1)} %x_hbm.1, s32[8,128]{1,0:T(8,128)} %bitcast.28, s32[1,64]{1,0:T(1,128)} %bitcast.32), custom_call_target="tpu_custom_call" | custom-call | tf_op jit(solution)/shard_map/pallas_call | solution.py:306
  2.9 1.3 %collective-permute-start.1 = (bf16[128,768]{1,0:T(8,128)(2,1)S(1)}, bf16[128,768]{1,0:T(8,128)(2,1)S(1)}, u32[]{:S(2)}, u32[]{:S(2)}) collective-permute-start(bf16[128,768]{1,0:T(8,128)(2,1)S(1)} %get-tuple-element.40), channel_id=1, source_target_pairs={{2,0},{6,4},{10,8},{14,12},{3,1},{7,5},{11,9},{15,13},{18,16},{22,... | collective-permute-start | bytes 589832 | tf_op jit(solution)/shard_map/ppermute | solution.py:664
  4.2 0.7 constant_dynamic-update-slice_fusion.1
  4.9 2.0 %shard_map.40.refs_0_ = bf16[1152,768]{1,0:T(8,128)(2,1)S(1)} custom-call(bf16[1024,768]{1,0:T(8,128)(2,1)S(1)} %get-tuple-element.37.unit, s32[1,1024]{1,0:T(1,128)S(1)} %get-tuple-element.38.slot_ref, f32[1,128]{1,0:T(1,128)S(1)} %get-tuple-element.39.info_ref), custom_call_target="tpu_custom_call" | custom-call | flops 1811939328 | bytes 3145728 | tf_op jit(solution)/shard_map/pallas_call | solution.py:328
  6.9 0.0 copy-start
  7.0 1.2 %copy-done = bf16[1152,768]{1,0:T(8,128)(2,1)} copy-done((bf16[1152,768]{1,0:T(8,128)(2,1)}, bf16[1152,768]{1,0:T(8,128)(2,1)S(1)}, u32[]{:S(2)}) %copy-start) | copy-done | bytes 1769496
  8.2 3.9 %collective-permute-done.1 = bf16[128,768]{1,0:T(8,128)(2,1)S(1)} collective-permute-done((bf16[128,768]{1,0:T(8,128)(2,1)S(1)}, bf16[128,768]{1,0:T(8,128)(2,1)S(1)}, u32[]{:S(2)}, u32[]{:S(2)}) %collective-permute-start.1) | collective-permute-done | bytes 196640 | tf_op jit(solution)/shard_map/ppermute | solution.py:664
  12.1 0.0 copy-start.3
  12.1 0.7 copy-done.3
  12.8 0.7 constant_dynamic-update-slice_fusion.refs_1_
  13.5 5.7 %all-to-all-start.2 = ((bf16[8,144,768]{2,1,0:T(8,128)(2,1)}), bf16[8,144,768]{2,1,0:T(8,128)(2,1)S(1)}, u32[]{:S(2)}, u32[]{:S(2)}) async-start(bf16[8,144,768]{2,1,0:T(8,128)(2,1)} %bitcast.17), calls=%async_computation.2 | async-start | bytes 3538944 | tf_op jit(solution)/shard_map/all_to_all | solution.py:667
  19.2 3.9 %collective-permute-start.3 = (bf16[256,768]{1,0:T(8,128)(2,1)}, bf16[256,768]{1,0:T(8,128)(2,1)S(1)}, u32[]{:S(2)}, u32[]{:S(2)}) collective-permute-start(bf16[256,768]{1,0:T(8,128)(2,1)} %constant_dynamic-update-slice_fusion.refs_1_), channel_id=1, source_target_pairs={{0,4},{1,5},{16,20},{17,21}} | collective-permute-start | bytes 1179656 | tf_op jit(solution)/shard_map/ppermute | solution.py:672
  23.1 1.4 %collective-permute-start.4 = (bf16[256,768]{1,0:T(8,128)(2,1)}, bf16[256,768]{1,0:T(8,128)(2,1)}, u32[]{:S(2)}, u32[]{:S(2)}) collective-permute-start(bf16[256,768]{1,0:T(8,128)(2,1)} %constant_dynamic-update-slice_fusion.refs_1_), channel_id=1, source_target_pairs={{8,4},{9,5},{24,20},{25,21}} | collective-permute-start | bytes 1179656 | tf_op jit(solution)/shard_map/ppermute | solution.py:672
  24.6 1.4 %collective-permute-start.5 = (bf16[256,768]{1,0:T(8,128)(2,1)}, bf16[256,768]{1,0:T(8,128)(2,1)}, u32[]{:S(2)}, u32[]{:S(2)}) collective-permute-start(bf16[256,768]{1,0:T(8,128)(2,1)} %constant_dynamic-update-slice_fusion.refs_1_), channel_id=1, source_target_pairs={{12,4},{13,5},{28,20},{29,21}} | collective-permute-start | bytes 1179656 | tf_op jit(solution)/shard_map/ppermute | solution.py:672
  26.0 29.6 %collective-permute-done.3 = bf16[256,768]{1,0:T(8,128)(2,1)S(1)} collective-permute-done((bf16[256,768]{1,0:T(8,128)(2,1)}, bf16[256,768]{1,0:T(8,128)(2,1)S(1)}, u32[]{:S(2)}, u32[]{:S(2)}) %collective-permute-start.3) | collective-permute-done | bytes 393248 | tf_op jit(solution)/shard_map/ppermute | solution.py:672
  55.6 14.7 %all-to-all-done.2 = bf16[8,144,768]{2,1,0:T(8,128)(2,1)S(1)} async-done(((bf16[8,144,768]{2,1,0:T(8,128)(2,1)}), bf16[8,144,768]{2,1,0:T(8,128)(2,1)S(1)}, u32[]{:S(2)}, u32[]{:S(2)}) %all-to-all-start.2) | async-done | bytes 1769504 | tf_op jit(solution)/shard_map/all_to_all | solution.py:667
  70.3 0.0 collective-permute-start.2
  70.3 0.9 constant_dynamic-update-slice_fusion.4
  71.2 0.0 collective-permute-done.4
  71.2 1.0 constant_dynamic-update-slice_fusion.3
  72.3 0.0 collective-permute-done.5
  72.3 1.0 constant_dynamic-update-slice_fusion.2.rest.refs_1_
  73.3 0.8 collective-permute-start.6
  74.1 3.9 %shard_map.42 = (f32[1,1152]{1,0:T(1,128)S(1)}, f32[1,1152]{1,0:T(1,128)S(1)}) custom-call(bf16[1152,768]{1,0:T(8,128)(2,1)S(1)} %bitcast.20), custom_call_target="tpu_custom_call" | custom-call | flops 2038431744 | bytes 3538944 | tf_op jit(solution)/shard_map/pallas_call | solution.py:594
  78.0 0.0 collective-permute-done.2.other.refs_2_
  78.0 4.0 %shard_map.43 = (f32[1,1152]{1,0:T(1,128)S(1)}, s32[8,128]{1,0:T(8,128)S(1)}) custom-call(bf16[1152,768]{1,0:T(8,128)(2,1)S(1)} %bitcast.22, bf16[1152,768]{1,0:T(8,128)(2,1)S(1)} %collective-permute-done.2.other.refs_2_, f32[1,1152]{1,0:T(1,128)S(1)} %get-tuple-element.41.sums, f32[1,1152]{1,0:T(1,128)S(1)} %get-tuple-element.42.lab_lane.refs_5_), custom_call_target="tpu_custom_call" | custom-call | flops 2038431744 | bytes 3538944 | tf_op jit(solution)/shard_map/pallas_call | solution.py:594
  82.0 0.0 collective-permute-done.6.refs_3_
  82.0 0.0 copy-start.4
  82.1 0.0 copy-start.6
  82.1 0.9 shard_map.45
  83.0 22.5 %all-to-all-start.3 = ((f32[8,1,256]{2,1,0:T(1,128)}), f32[8,1,256]{2,1,0:T(1,128)S(1)}, u32[]{:S(2)}, u32[]{:S(2)}) async-start(f32[8,1,256]{2,1,0:T(1,128)} %shard_map.45), calls=%async_computation.3 | async-start | bytes 16384 | tf_op jit(solution)/shard_map/all_to_all | solution.py:702
  105.5 0.5 slice.3
  106.6 5.4 %all-to-all-done.3 = f32[8,1,256]{2,1,0:T(1,128)S(1)} async-done(((f32[8,1,256]{2,1,0:T(1,128)}), f32[8,1,256]{2,1,0:T(1,128)S(1)}, u32[]{:S(2)}, u32[]{:S(2)}) %all-to-all-start.3) | async-done | bytes 8224 | tf_op jit(solution)/shard_map/all_to_all | solution.py:702
  112.0 0.0 copy-done.4
  112.0 0.0 copy-done.6
  112.0 0.1 conditional.1
  112.0 0.1 branch_1_fun.1
  112.1 0.0 copy-start.5
  112.1 0.6 copy-done.5
  (4 shorter events, 0.1 us)
Async XLA Ops:
  2.9 9.2 %collective-permute-start.1 = (bf16[128,768]{1,0:T(8,128)(2,1)S(1)}, bf16[128,768]{1,0:T(8,128)(2,1)S(1)}, u32[]{:S(2)}, u32[]{:S(2)}) collective-permute-start(bf16[128,768]{1,0:T(8,128)(2,1)S(1)} %get-tuple-element.40), channel_id=1, source_target_pairs={{2,0},{6,4},{10,8},{14,12},{3,1},{7,5},{11,9},{15,13},{18,16},{22,... | collective-permute-start | bytes 589832 | tf_op jit(solution)/shard_map/ppermute | solution.py:664
  6.9 1.2 %copy-start = (bf16[1152,768]{1,0:T(8,128)(2,1)}, bf16[1152,768]{1,0:T(8,128)(2,1)S(1)}, u32[]{:S(2)}) copy-start(bf16[1152,768]{1,0:T(8,128)(2,1)S(1)} %shard_map.40.refs_0_) | copy-start | bytes 5308420
  12.1 0.7 copy-start.3
  13.5 56.8 %all-to-all-start.2 = ((bf16[8,144,768]{2,1,0:T(8,128)(2,1)}), bf16[8,144,768]{2,1,0:T(8,128)(2,1)S(1)}, u32[]{:S(2)}, u32[]{:S(2)}) async-start(bf16[8,144,768]{2,1,0:T(8,128)(2,1)} %bitcast.17), calls=%async_computation.2 | async-start | bytes 3538944 | tf_op jit(solution)/shard_map/all_to_all | solution.py:667
  19.2 36.3 %collective-permute-start.3 = (bf16[256,768]{1,0:T(8,128)(2,1)}, bf16[256,768]{1,0:T(8,128)(2,1)S(1)}, u32[]{:S(2)}, u32[]{:S(2)}) collective-permute-start(bf16[256,768]{1,0:T(8,128)(2,1)} %constant_dynamic-update-slice_fusion.refs_1_), channel_id=1, source_target_pairs={{0,4},{1,5},{16,20},{17,21}} | collective-permute-start | bytes 1179656 | tf_op jit(solution)/shard_map/ppermute | solution.py:672
  23.1 48.1 %collective-permute-start.4 = (bf16[256,768]{1,0:T(8,128)(2,1)}, bf16[256,768]{1,0:T(8,128)(2,1)}, u32[]{:S(2)}, u32[]{:S(2)}) collective-permute-start(bf16[256,768]{1,0:T(8,128)(2,1)} %constant_dynamic-update-slice_fusion.refs_1_), channel_id=1, source_target_pairs={{8,4},{9,5},{24,20},{25,21}} | collective-permute-start | bytes 1179656 | tf_op jit(solution)/shard_map/ppermute | solution.py:672
  24.6 47.7 %collective-permute-start.5 = (bf16[256,768]{1,0:T(8,128)(2,1)}, bf16[256,768]{1,0:T(8,128)(2,1)}, u32[]{:S(2)}, u32[]{:S(2)}) collective-permute-start(bf16[256,768]{1,0:T(8,128)(2,1)} %constant_dynamic-update-slice_fusion.refs_1_), channel_id=1, source_target_pairs={{12,4},{13,5},{28,20},{29,21}} | collective-permute-start | bytes 1179656 | tf_op jit(solution)/shard_map/ppermute | solution.py:672
  70.3 7.8 %collective-permute-start.2 = (bf16[1152,768]{1,0:T(8,128)(2,1)S(1)}, bf16[1152,768]{1,0:T(8,128)(2,1)S(1)}, u32[]{:S(2)}, u32[]{:S(2)}) collective-permute-start(bf16[1152,768]{1,0:T(8,128)(2,1)S(1)} %bitcast.19), channel_id=1, source_target_pairs={{0,1},{1,0},{2,3},{3,2},{4,5},{5,4},{6,7},{7,6},{8,9},{9,8},{10,11... | collective-permute-start | bytes 5308424 | tf_op jit(solution)/shard_map/ppermute | solution.py:677
  73.3 8.7 %collective-permute-start.6 = (bf16[1024,768]{1,0:T(8,128)(2,1)S(1)}, bf16[1024,768]{1,0:T(8,128)(2,1)S(1)}, u32[]{:S(2)}, u32[]{:S(2)}) collective-permute-start(bf16[1024,768]{1,0:T(8,128)(2,1)S(1)} %constant_dynamic-update-slice_fusion.2.rest.refs_1_), channel_id=1, source_target_pairs={{4,5},{5,4},{20,21},{21,20}} | collective-permute-start | bytes 4718600 | tf_op jit(solution)/shard_map/ppermute | solution.py:678
  82.0 30.0 %copy-start.4 = (s32[1024]{0:T(1024)S(1)}, s32[1024]{0:T(1024)}, u32[]{:S(2)}) copy-start(s32[1024]{0:T(1024)} %param.6) | copy-start | bytes 12292
  82.1 29.9 %copy-start.6 = (s32[64]{0:T(128)S(1)}, s32[64]{0:T(128)}, u32[]{:S(2)}) copy-start(s32[64]{0:T(128)} %param.7) | copy-start | bytes 772
  83.0 29.0 %all-to-all-start.3 = ((f32[8,1,256]{2,1,0:T(1,128)}), f32[8,1,256]{2,1,0:T(1,128)S(1)}, u32[]{:S(2)}, u32[]{:S(2)}) async-start(f32[8,1,256]{2,1,0:T(1,128)} %shard_map.45), calls=%async_computation.3 | async-start | bytes 16384 | tf_op jit(solution)/shard_map/all_to_all | solution.py:702
  112.1 0.6 copy-start.5

commit v8 on v7

--- a/solution.py
+++ b/solution.py
@@ -20,6 +20,7 @@
 DEAD = -1e30
 VMEM_LIMIT = 48 * 1024 * 1024
 FAST_LIMIT = 40 * 1024 * 1024
+WIDE = 512
 INFO = 16
 
 
@@ -339,19 +340,39 @@
     )(unit, slot, info)
 
 
+def pair_up_kernel(packed_in, extra, moved, packed, both):
+    rows = extra.shape[0]
+    both[:rows, :] = extra[...]
+    both[rows:, :] = moved[...]
+
+
+def pair_up(packed, extra, moved):
+    return pl.pallas_call(
+        pair_up_kernel,
+        out_shape=(
+            jax.ShapeDtypeStruct(packed.shape, packed.dtype),
+            jax.ShapeDtypeStruct((2 * extra.shape[0], extra.shape[1]), extra.dtype),
+        ),
+        in_specs=list(vmem_specs(3)),
+        out_specs=vmem_specs(2),
+        input_output_aliases={0: 0},
+        compiler_params=pltpu.CompilerParams(vmem_limit_bytes=FAST_LIMIT),
+    )(packed, extra, moved)
+
+
 def gate_kernel(*refs):
     pass
 
 
-def after(rows, received):
+def after(arrays, sums):
     anywhere = pl.BlockSpec(memory_space=pl.ANY)
     return pl.pallas_call(
         gate_kernel,
-        out_shape=jax.ShapeDtypeStruct(rows.shape, rows.dtype),
-        in_specs=[anywhere] * 2,
-        out_specs=anywhere,
-        input_output_aliases={0: 0},
-    )(rows, received)
+        out_shape=tuple(jax.ShapeDtypeStruct(x.shape, x.dtype) for x in arrays),
+        in_specs=[anywhere] * (len(arrays) + 1),
+        out_specs=(anywhere,) * len(arrays),
+        input_output_aliases={i: i for i in range(len(arrays))},
+    )(*arrays, sums)
 
 
 class Layout:
@@ -361,6 +382,7 @@
         self.head = main - INFO
         self.rest = capacity - self.head
         self.per_owner = n_fine // n_owner
+        self.planes = n_owner // 2
         self.n_main = n_owner * main
         self.n_head = n_owner * self.head
         self.n_rest = n_owner * self.rest
@@ -392,7 +414,10 @@
         label = jnp.broadcast_to(jnp.sum(label, axis=1, keepdims=True), (count, LANES))
         start = at + source * count
         lab_sub[start : start + count, :] = label
-        bias[start : start + count, :] = jnp.where(label < lay.per_owner, NEIGHBOUR - SCALE, DEAD)
+        if bias is not None:
+            bias[start : start + count, :] = jnp.where(
+                label < lay.per_owner, NEIGHBOUR - SCALE, DEAD
+            )
 
 
 def turn_labels(lay, lab_sub, start, count, lab_lane, at):
@@ -414,7 +439,11 @@
 
 def stream(rows_i, first, count, tiles, lab_lane, at, lab_sub, bias, buffers, put):
     step = 32
-    tiles = [(ref, s, d, place + s - start) for ref, start, n, place, parts in tiles for s, d in pieces(start, n, parts)]
+    tiles = [
+        (ref, s, d, place + s - start)
+        for ref, start, n, place, parts in tiles
+        for s, d in pieces(start, n, parts)
+    ]
 
     def scores_to(buffer, tile, rows):
         ref, start, deep, _ = tile
@@ -447,7 +476,10 @@
                 for c in range(0, deep, step):
                     part = slice(line + c, line + c + step)
                     label_j = jnp.concatenate([lab_sub[part, :]] * repeat, axis=1)
-                    bias_j = jnp.concatenate([bias[part, :]] * repeat, axis=1)
+                    if bias is None:
+                        bias_j = NEIGHBOUR - SCALE
+                    else:
+                        bias_j = jnp.concatenate([bias[part, :]] * repeat, axis=1)
                     shift = jnp.where(label_j == label_i, -SCALE, bias_j)
                     terms = jnp.exp2(buffer[c : c + step, :wide] * SCALE + shift)
                     acc = acc + jnp.sum(terms.reshape(step // 8, 8, wide), axis=0)
@@ -456,7 +488,7 @@
 
         lax.fori_loop(0, blocks, body, 0)
 
-    wide = 256
+    wide = WIDE
     if count >= wide:
         run(0, count // wide, wide)
     if count % wide:
@@ -481,7 +513,7 @@
     is_home = lax.axis_index("cl") == lay.home
     infos = lines_of(lay, mine)
 
-    def work(ref, count, per):
+    def work(ref, count, per, bias):
         write_labels(lay, infos, 0, per, 0, lab_sub, bias)
         turn_labels(lay, lab_sub, 0, count, lab_lane, 0)
         tiles = [(ref, 0, count, 0, 4)]
@@ -490,11 +522,11 @@
     @pl.when(is_home)
     def _():
         copy_head(lay, mine, rows)
-        work(rows, lay.n_head, lay.head)
+        work(rows, lay.n_head, lay.head, None)
 
     @pl.when(jnp.logical_not(is_home))
     def _():
-        work(mine, lay.n_main, lay.main)
+        work(mine, lay.n_main, lay.main, bias)
 
 
 def cross_kernel(lay, mine, other, sums, lab_lane, total, unfit_ref, lab_sub, bias, rows, rows_j, buf_a, buf_b):
@@ -516,7 +548,7 @@
     ).astype(jnp.int32)
     total[...] = sums[...]
 
-    def work(ref, ref_j, count, per):
+    def work(ref, ref_j, count, per, bias):
         write_labels(lay, infos, 0, per, 0, lab_sub, bias)
         tiles = [(ref_j, 0, count, 0, 4)]
         stream(ref, 0, count, tiles, lab_lane, 0, lab_sub, bias, (buf_a, buf_b), adder(total))
@@ -525,52 +557,59 @@
     def _():
         copy_head(lay, mine, rows)
         copy_head(lay, other, rows_j)
-        work(rows, rows_j, lay.n_head, lay.head)
+        work(rows, rows_j, lay.n_head, lay.head, None)
 
     @pl.when(jnp.logical_not(is_home))
     def _():
-        work(mine, other, lay.n_main, lay.main)
-
-
-def rest_pairs(lay, rows, rest, rows_j, rest_j, lab_lane, lab_sub, bias, buffers, put):
-    seconds = (rest_j, 0, lay.n_rest, lay.n_head, 4)
-    mains = (rows_j, 0, lay.n_head, 0, 4)
-    stream(rows, 0, lay.n_head, [seconds], lab_lane, 0, lab_sub, bias, buffers, put)
-    stream(
-        rest, 0, lay.n_rest, [seconds, mains], lab_lane, lay.n_head, lab_sub, bias, buffers, put
-    )
-
-
-def inner_rest_kernel(lay, mine, rest, sums, lab_lane, lab_sub, bias, rows, buf_a, buf_b):
+        work(mine, other, lay.n_main, lay.main, bias)
+
+
+def copy_all(lay, main_ref, rests, rows):
+    copy_head(lay, main_ref, rows)
+    for i, ref in enumerate(rests):
+        start = lay.n_head + i * ref.shape[0]
+        rows[start : start + ref.shape[0], :] = ref[...]
+
+
+def rest_labels(lay, infos, lab_sub):
+    write_labels(lay, infos, 0, lay.head, 0, lab_sub, None)
+    write_labels(lay, infos, lay.head, lay.rest, lay.n_head, lab_sub, None)
+
+
+def rest_pairs(lay, rows, rows_j, lab_lane, lab_sub, buffers, put):
+    n_head, n_rest = lay.n_head, lay.n_rest
+    seconds = (rows_j, n_head, n_rest, n_head, 4)
+    mains = (rows_j, 0, n_head, 0, 4)
+    stream(rows, 0, n_head, [seconds], lab_lane, 0, lab_sub, None, buffers, put)
+    stream(rows, n_head, n_rest, [seconds, mains], lab_lane, n_head, lab_sub, None, buffers, put)
+
+
+def inner_rest_kernel(lay, mine, *refs):
+    rests = refs[: lay.planes]
+    sums, lab_lane, lab_sub, rows, buf_a, buf_b = refs[lay.planes :]
+
     @pl.when(lax.axis_index("cl") == lay.home)
     def _():
-        infos = lines_of(lay, mine)
-        write_labels(lay, infos, 0, lay.head, 0, lab_sub, bias)
-        write_labels(lay, infos, lay.head, lay.rest, lay.n_head, lab_sub, bias)
+        rest_labels(lay, lines_of(lay, mine), lab_sub)
         turn_labels(lay, lab_sub, 0, lay.n_head + lay.n_rest, lab_lane, 0)
-        copy_head(lay, mine, rows)
-        buffers = (buf_a, buf_b)
-        rest_pairs(lay, rows, rest, rows, rest, lab_lane, lab_sub, bias, buffers, setter(sums))
-
-
-def cross_rest_kernel(lay, *refs):
-    mine, rest, other, rest_other, main_sums, main_lane, sums, lab_lane = refs[:8]
-    out_ref, lab_sub, bias, rows, rows_j, total, buf_a, buf_b = refs[8:]
+        copy_all(lay, mine, rests, rows)
+        rest_pairs(lay, rows, rows, lab_lane, lab_sub, (buf_a, buf_b), setter(sums))
+
+
+def cross_rest_kernel(lay, mine, other, *refs):
+    rests, refs = refs[: lay.planes], refs[lay.planes :]
+    others, refs = refs[: lay.planes], refs[lay.planes :]
+    main_sums, main_lane, sums, lab_lane, out_ref, lab_sub, rows, rows_j, total, buf_a, buf_b = refs
     is_home = lax.axis_index("cl") == lay.home
 
     @pl.when(is_home)
     def _():
-        infos = lines_of(lay, other)
-        write_labels(lay, infos, 0, lay.head, 0, lab_sub, bias)
-        write_labels(lay, infos, lay.head, lay.rest, lay.n_head, lab_sub, bias)
-        copy_head(lay, mine, rows)
-        copy_head(lay, other, rows_j)
+        rest_labels(lay, lines_of(lay, other), lab_sub)
+        copy_all(lay, mine, rests, rows)
+        copy_all(lay, other, others, rows_j)
         total[...] = sums[...]
         total[:, : lay.n_head] += main_sums[:, : lay.n_head]
-        buffers = (buf_a, buf_b)
-        rest_pairs(
-            lay, rows, rest, rows_j, rest_other, lab_lane, lab_sub, bias, buffers, adder(total)
-        )
+        rest_pairs(lay, rows, rows_j, lab_lane, lab_sub, (buf_a, buf_b), adder(total))
         values = jnp.log(total[...])
         for source in range(lay.n_owner):
             start = source * lay.head
@@ -586,17 +625,17 @@
             out_ref[source, :, : lay.main] = values[:, start : start + lay.main]
 
 
-def pair_call(kernel, lay, arrays, out_shape, lines, joins, more=()):
+def pair_call(kernel, lay, arrays, out_shape, sides, joins, more=()):
     width = arrays[0].shape[1]
-    side = pltpu.VMEM((lines, LANES), jnp.float32)
-    rows = pltpu.VMEM((lay.n_head, width), jnp.bfloat16)
-    buffer = pltpu.VMEM((lay.n_main // 4, 256), jnp.float32)
+    side = pltpu.VMEM((sides[0], LANES), jnp.float32)
+    rows = pltpu.VMEM((joins[0], width), jnp.bfloat16)
+    buffer = pltpu.VMEM((lay.n_main // 4, WIDE), jnp.float32)
     out = pl.pallas_call(
         functools.partial(kernel, lay),
         out_shape=out_shape,
         in_specs=list(vmem_specs(len(arrays))),
         out_specs=vmem_specs(len(out_shape)),
-        scratch_shapes=[side, side] + [rows] * joins + list(more) + [buffer, buffer],
+        scratch_shapes=[side] * sides[1] + [rows] * joins[1] + list(more) + [buffer, buffer],
         compiler_params=pltpu.CompilerParams(vmem_limit_bytes=FAST_LIMIT),
         cost_estimate=pl.CostEstimate(
             flops=2 * lay.n_main * lay.n_main * width,
@@ -662,42 +701,34 @@
     lay = Layout(n_owner, n_fine, capacity, main, home)
     unit, slot, info, extra, pos = place_rows(embeddings, labels, owner_map, lay)
     moved = lax.ppermute(extra, "cl", [(2 * z + 1, 2 * z) for z in range(planes)])
-    both = jnp.concatenate([extra, moved], axis=0)
-    packed = after(pack_main(unit, slot, info, lay), both)
+    packed, both = pair_up(pack_main(unit, slot, info, lay), extra, moved)
     mine = lax.all_to_all(
         packed.reshape(n_owner, main, width), "cl", split_axis=0, concat_axis=0, tiled=True
     ).reshape(n_owner * main, width)
-    rest = jnp.concatenate(
-        [
-            both if z == plane else lax.ppermute(both, "cl", [(2 * z, home)])
-            for z in range(planes)
-        ],
-        axis=0,
-    )
+    far = [lax.ppermute(both, "cl", [(2 * z, home)]) for z in range(planes) if z != plane]
     other = lax.ppermute(mine, "grp", [(0, 1), (1, 0)])
-    rest_other = lax.ppermute(
-        rest, ("cl", "grp"), [(2 * home, 2 * home + 1), (2 * home + 1, 2 * home)]
-    )
     row = jax.ShapeDtypeStruct((1, lay.n_main), jnp.float32)
-    long_row = jax.ShapeDtypeStruct((1, lay.n_head + lay.n_rest), jnp.float32)
+    lines = lay.n_head + lay.n_rest
+    long_row = jax.ShapeDtypeStruct((1, lines), jnp.float32)
     flag = jax.ShapeDtypeStruct((8, LANES), jnp.int32)
     table = jax.ShapeDtypeStruct((n_owner, 1, capacity), jnp.float32)
-    sums, main_lane = pair_call(inner_kernel, lay, (mine,), (row, row), lay.n_main, 1)
+    sides, joins = (lay.n_main, 2), (lay.n_head, 1)
+    sums, main_lane = pair_call(inner_kernel, lay, (mine,), (row, row), sides, joins)
+    joins = (lay.n_head, 2)
     sums, unfit = pair_call(
-        cross_kernel, lay, (mine, other, sums, main_lane), (row, flag), lay.n_main, 2
-    )
-    lines = lay.n_head + lay.n_rest
+        cross_kernel, lay, (mine, other, sums, main_lane), (row, flag), sides, joins
+    )
+    far = list(after(far, sums))
+    rests = far[:plane] + [both] + far[plane:]
+    swap = [(2 * home, 2 * home + 1), (2 * home + 1, 2 * home)]
+    rests_other = [lax.ppermute(x, ("cl", "grp"), swap) for x in rests]
     rest_sums, lane = pair_call(
-        inner_rest_kernel, lay, (mine, rest), (long_row, long_row), lines, 1
-    )
+        inner_rest_kernel, lay, (mine, *rests), (long_row, long_row), (lines, 1), (lines, 1)
+    )
+    arrays = (mine, other, *rests, *rests_other, sums, main_lane, rest_sums, lane)
+    total = pltpu.VMEM(long_row.shape, jnp.float32)
     (results,) = pair_call(
-        cross_rest_kernel,
-        lay,
-        (mine, rest, other, rest_other, sums, main_lane, rest_sums, lane),
-        (table,),
-        lines,
-        2,
-        (pltpu.VMEM(long_row.shape, jnp.float32),),
+        cross_rest_kernel, lay, arrays, (table,), (lines, 1), (lines, 2), (total,)
     )
     returned = lax.all_to_all(results, "cl", split_axis=0, concat_axis=0, tiled=True)
     return lax.cond(

time: 113 us -> 117 us (1.035)
  blocking collectives: 0 us -> 46 us
  waiting for transfers between devices: 53.5 us -> 11.2 us
    all_to_all x0 -> x1, blocking collectives: none -> 46 us  [body(): lax.all_to_all(packed.reshape(n_owner, main, width), 'cl', split_axis=0,...]
    ppermute x3, waiting for transfers between devices: 29.6 us -> 0.01 us  [body(): lax.ppermute(both, 'cl', [(2 * z, home)])]
    all_to_all x1 -> x0, waiting for transfers between devices: 14.7 us -> none  [body(): lax.all_to_all(packed.reshape(n_owner, main, width), 'cl', split_axis=0,...]
    all_to_all x1 -> x0, starting transfers between devices: 5.71 us -> none  [body(): lax.all_to_all(packed.reshape(n_owner, main, width), 'cl', split_axis=0,...]
    all_to_all x1, starting transfers between devices: 22.5 us -> 26.7 us  [body(): lax.all_to_all(results, 'cl', split_axis=0, concat_axis=0, tiled=True)]
    ppermute x1 -> x4, starting transfers between devices: 0.76 us -> 3.46 us  [body(): rests_other = [lax.ppermute(x, ('cl', 'grp'), swap) for x in rests]]
    ppermute x1, waiting for transfers between devices: 3.92 us -> 5.84 us  [body(): lax.ppermute(extra, 'cl', [(2 * z + 1, 2 * z) for z in range(planes)])]
    concatenate x2 -> x0, local copies, waits for them, and re-layouts: 1.71 us -> none  [the longest x1 1.02 us: body(): jnp.concatenate([both if z == plane else lax.ppermute(both, 'cl', [(2 * z...]
  transfers between devices with their start and end apart: 8 -> 10, of which waited for: 4 -> 2; matrix products, arithmetic and copies ran while one was open for 4% -> 0% of each run, Pallas kernels for 9% -> 8%
where the time goes in v8:
time: 117 us; the launch traced here: 116 us
  blocking collectives  46 us (39%)
  starting transfers between devices  37.1 us (32%)
  Pallas kernels  14 us (12%)
  waiting for transfers between devices  11.2 us (10%)
  local copies, waits for them, and re-layouts  7.3 us (6%)
    all_to_all x1, blocking collectives, body(): lax.all_to_all(packed.reshape(n_owner, main, width), 'cl', split_axis=0,...  46 us
    all_to_all x1, starting transfers between devices, body(): lax.all_to_all(results, 'cl', split_axis=0, concat_axis=0, tiled=True)  26.7 us
    pallas_call x4, Pallas kernels, pair_call(): pl.pallas_call(functools.partial(kernel, lay), out_shape=out_shape, in_sp...  9.05 us
    unnamed x32, local copies, waits for them, and re-layouts  6.79 us
    ppermute x1, waiting for transfers between devices, body(): lax.ppermute(extra, 'cl', [(2 * z + 1, 2 * z) for z in range(planes)])  5.84 us
    ppermute x3, starting transfers between devices, body(): lax.ppermute(both, 'cl', [(2 * z, home)])  5.59 us
    all_to_all x1, waiting for transfers between devices, body(): lax.all_to_all(results, 'cl', split_axis=0, concat_axis=0, tiled=True)  5.35 us
    ppermute x4, starting transfers between devices, body(): rests_other = [lax.ppermute(x, ('cl', 'grp'), swap) for x in rests]  3.46 us
  transfers between devices with their start and end apart: 10, of which 2 were waited for; matrix products, arithmetic and copies ran while one was open for 0% of the time, Pallas kernels for 8%

profile of v8, /device:TPU:0, one launch (start us, length us, event | category | flops | bytes accessed | tf_op | source)
XLA Modules:
  0.0 116.4 jit_solution(3510900216463971053)
XLA Ops:
  0.0 2.8 %shard_map.39 = (bf16[1024,768]{1,0:T(8,128)(2,1)S(1)}, s32[1,1024]{1,0:T(1,128)S(1)}, f32[1,128]{1,0:T(1,128)S(1)}, bf16[128,768]{1,0:T(8,128)(2,1)S(1)}, s32[8,128]{1,0:T(8,128)S(1)}) custom-call(bf16[1024,768]{1,0:T(8,128)(2,1)} %x_hbm.1, s32[8,128]{1,0:T(8,128)} %bitcast.28, s32[1,64]{1,0:T(1,128)} %bitcast.32), custom_call_target="tpu_custom_call" | custom-call | tf_op jit(solution)/shard_map/pallas_call | solution.py:307
  2.8 1.3 %collective-permute-start.1 = (bf16[128,768]{1,0:T(8,128)(2,1)S(1)}, bf16[128,768]{1,0:T(8,128)(2,1)S(1)}, u32[]{:S(2)}, u32[]{:S(2)}) collective-permute-start(bf16[128,768]{1,0:T(8,128)(2,1)S(1)} %get-tuple-element.45.extra), channel_id=1, source_target_pairs={{2,0},{6,4},{10,8},{14,12},{3,1},{7,5},{11,9},{15,13},{18,16},{22,... | collective-permute-start | bytes 589832 | tf_op jit(solution)/shard_map/ppermute | solution.py:703
  4.1 2.0 %shard_map.40.packed_in = bf16[1152,768]{1,0:T(8,128)(2,1)S(1)} custom-call(bf16[1024,768]{1,0:T(8,128)(2,1)S(1)} %get-tuple-element.42.unit, s32[1,1024]{1,0:T(1,128)S(1)} %get-tuple-element.43.slot_ref, f32[1,128]{1,0:T(1,128)S(1)} %get-tuple-element.44.info_ref), custom_call_target="tpu_custom_call" | custom-call | flops 1811939328 | bytes 3145728 | tf_op jit(solution)/shard_map/pallas_call | solution.py:329
  6.1 5.8 %collective-permute-done.1.moved = bf16[128,768]{1,0:T(8,128)(2,1)S(1)} collective-permute-done((bf16[128,768]{1,0:T(8,128)(2,1)S(1)}, bf16[128,768]{1,0:T(8,128)(2,1)S(1)}, u32[]{:S(2)}, u32[]{:S(2)}) %collective-permute-start.1) | collective-permute-done | bytes 196640 | tf_op jit(solution)/shard_map/ppermute | solution.py:703
  12.0 46.0 %all_to_all.23 = bf16[8,144,768]{2,1,0:T(8,128)(2,1)S(1)} all-to-all(bf16[8,144,768]{2,1,0:T(8,128)(2,1)S(1)} %bitcast.17), channel_id=1, replica_groups=mesh['parts'=2,'cl'=8,'grp'=2] {'cl'}, dimensions={0} | all-to-all | bytes 3538944 | tf_op jit(solution)/shard_map/all_to_all | solution.py:705
  58.0 0.0 collective-permute-start.2
  58.0 0.7 collective-permute-start.5
  58.6 0.7 collective-permute-start.4
  59.3 4.2 %collective-permute-start.3 = (bf16[256,768]{1,0:T(8,128)(2,1)S(1)}, bf16[256,768]{1,0:T(8,128)(2,1)S(1)}, u32[]{:S(2)}, u32[]{:S(2)}) collective-permute-start(bf16[256,768]{1,0:T(8,128)(2,1)S(1)} %get-tuple-element.50.refs_1_), channel_id=1, source_target_pairs={{0,4},{1,5},{16,20},{17,21}} | collective-permute-start | bytes 1179656 | tf_op jit(solution)/shard_map/ppermute | solution.py:708
  63.6 1.4 %collective-permute-start.7 = (bf16[256,768]{1,0:T(8,128)(2,1)S(1)}, bf16[256,768]{1,0:T(8,128)(2,1)}, u32[]{:S(2)}, u32[]{:S(2)}) collective-permute-start(bf16[256,768]{1,0:T(8,128)(2,1)S(1)} %get-tuple-element.50.refs_1_), channel_id=1, source_target_pairs={{4,5},{5,4},{20,21},{21,20}} | collective-permute-start | bytes 1179656 | tf_op jit(solution)/shard_map/ppermute | solution.py:724
  65.0 3.5 %shard_map.42 = (f32[1,1152]{1,0:T(1,128)S(1)}, f32[1,1152]{1,0:T(1,128)S(1)}) custom-call(bf16[1152,768]{1,0:T(8,128)(2,1)S(1)} %bitcast.20), custom_call_target="tpu_custom_call" | custom-call | flops 2038431744 | bytes 3538944 | tf_op jit(solution)/shard_map/pallas_call | solution.py:633
  68.5 0.0 collective-permute-done.2.other
  68.5 0.0 copy-start.12
  68.5 3.7 %shard_map.43 = (f32[1,1152]{1,0:T(1,128)S(1)}, s32[8,128]{1,0:T(8,128)S(1)}) custom-call(bf16[1152,768]{1,0:T(8,128)(2,1)S(1)} %bitcast.21, bf16[1152,768]{1,0:T(8,128)(2,1)S(1)} %collective-permute-done.2.other, f32[1,1152]{1,0:T(1,128)S(1)} %get-tuple-element.47.sums, f32[1,1152]{1,0:T(1,128)S(1)} %get-tuple-element.48.lab_lane.refs_9_), custom_call_target="tpu_custom_call" | custom-call | flops 2038431744 | bytes 3538944 | tf_op jit(solution)/shard_map/pallas_call | solution.py:633
  72.2 0.0 copy-done.12
  72.2 0.0 copy-start.9
  72.2 0.6 copy-done.9
  72.8 0.0 collective-permute-done.5.refs_2_
  72.8 0.0 copy-start
  72.8 0.0 collective-permute-done.4.refs_1_
  72.8 0.0 copy-start.3
  72.8 0.0 collective-permute-done.3.refs_0_
  72.8 0.0 copy-start.6
  72.8 0.7 copy-done
  73.6 0.1 copy-done.3
  73.7 0.2 copy-done.6
  73.9 0.7 collective-permute-start.6
  74.5 0.7 collective-permute-start.8
  75.2 0.7 collective-permute-start.9
  75.9 0.0 copy-start.1
  75.9 1.0 copy-done.1
  76.9 0.0 copy-start.4
  76.9 1.0 copy-done.4
  77.9 0.0 copy-start.7
  77.9 1.0 copy-done.7
  78.9 0.0 copy-start.2
  78.9 0.0 copy-start.5
  78.9 0.0 copy-start.8
  78.9 0.0 copy-start.10
  78.9 0.0 copy-start.13
  78.9 0.2 shard_map.45
  79.1 0.0 collective-permute-done.7.refs_5_
  79.2 0.0 collective-permute-done.6.refs_4_
  79.2 0.0 collective-permute-done.8.refs_6_
  79.2 0.0 collective-permute-done.9.refs_7_
  79.2 0.7 copy-done.2
  79.9 0.1 copy-done.5
  80.0 0.1 copy-done.8
  80.2 0.0 copy-done.10
  80.2 0.6 copy-done.13
  80.8 0.0 copy-start.15
  80.8 0.0 copy-start.17
  80.8 1.7 %shard_map.46 = f32[8,1,256]{2,1,0:T(1,128)} custom-call(bf16[1152,768]{1,0:T(8,128)(2,1)S(1)} %bitcast.23, bf16[1152,768]{1,0:T(8,128)(2,1)S(1)} %copy-done.13, bf16[256,768]{1,0:T(8,128)(2,1)S(1)} %copy-done.8, bf16[256,768]{1,0:T(8,128)(2,1)S(1)} %get-tuple-element.50.refs_1_, bf16[256,768]{1,0:T(8,128)(2,1)S(1)} %copy-done.5, ...), custom_call_target="tpu_custom_call" | custom-call | flops 2038431744 | bytes 3538944 | tf_op jit(solution)/shard_map/pallas_call | solution.py:633
  82.5 26.7 %all-to-all-start.3 = ((f32[8,1,256]{2,1,0:T(1,128)}), f32[8,1,256]{2,1,0:T(1,128)S(1)}, u32[]{:S(2)}, u32[]{:S(2)}) async-start(f32[8,1,256]{2,1,0:T(1,128)} %shard_map.46), calls=%async_computation.3 | async-start | bytes 16384 | tf_op jit(solution)/shard_map/all_to_all | solution.py:733
  109.2 0.5 slice.3
  110.4 5.4 %all-to-all-done.3 = f32[8,1,256]{2,1,0:T(1,128)S(1)} async-done(((f32[8,1,256]{2,1,0:T(1,128)}), f32[8,1,256]{2,1,0:T(1,128)S(1)}, u32[]{:S(2)}, u32[]{:S(2)}) %all-to-all-start.3) | async-done | bytes 8224 | tf_op jit(solution)/shard_map/all_to_all | solution.py:733
  115.7 0.0 copy-done.15
  115.7 0.0 copy-done.17
  115.7 0.1 conditional.1
  115.7 0.1 branch_1_fun.1
  115.8 0.0 copy-start.16
  115.8 0.6 copy-done.16
  (2 shorter events, 0.0 us)
Async XLA Ops:
  2.8 9.2 %collective-permute-start.1 = (bf16[128,768]{1,0:T(8,128)(2,1)S(1)}, bf16[128,768]{1,0:T(8,128)(2,1)S(1)}, u32[]{:S(2)}, u32[]{:S(2)}) collective-permute-start(bf16[128,768]{1,0:T(8,128)(2,1)S(1)} %get-tuple-element.45.extra), channel_id=1, source_target_pairs={{2,0},{6,4},{10,8},{14,12},{3,1},{7,5},{11,9},{15,13},{18,16},{22,... | collective-permute-start | bytes 589832 | tf_op jit(solution)/shard_map/ppermute | solution.py:703
  58.0 10.6 %collective-permute-start.2 = (bf16[1152,768]{1,0:T(8,128)(2,1)S(1)}, bf16[1152,768]{1,0:T(8,128)(2,1)S(1)}, u32[]{:S(2)}, u32[]{:S(2)}) collective-permute-start(bf16[1152,768]{1,0:T(8,128)(2,1)S(1)} %bitcast.19), channel_id=1, source_target_pairs={{0,1},{1,0},{2,3},{3,2},{4,5},{5,4},{6,7},{7,6},{8,9},{9,8},{10,11... | collective-permute-start | bytes 5308424 | tf_op jit(solution)/shard_map/ppermute | solution.py:709
  58.0 14.8 %collective-permute-start.5 = (bf16[256,768]{1,0:T(8,128)(2,1)S(1)}, bf16[256,768]{1,0:T(8,128)(2,1)S(1)}, u32[]{:S(2)}, u32[]{:S(2)}) collective-permute-start(bf16[256,768]{1,0:T(8,128)(2,1)S(1)} %get-tuple-element.50.refs_1_), channel_id=1, source_target_pairs={{12,4},{13,5},{28,20},{29,21}} | collective-permute-start | bytes 1179656 | tf_op jit(solution)/shard_map/ppermute | solution.py:708
  58.6 14.2 %collective-permute-start.4 = (bf16[256,768]{1,0:T(8,128)(2,1)S(1)}, bf16[256,768]{1,0:T(8,128)(2,1)S(1)}, u32[]{:S(2)}, u32[]{:S(2)}) collective-permute-start(bf16[256,768]{1,0:T(8,128)(2,1)S(1)} %get-tuple-element.50.refs_1_), channel_id=1, source_target_pairs={{8,4},{9,5},{24,20},{25,21}} | collective-permute-start | bytes 1179656 | tf_op jit(solution)/shard_map/ppermute | solution.py:708
  59.3 13.5 %collective-permute-start.3 = (bf16[256,768]{1,0:T(8,128)(2,1)S(1)}, bf16[256,768]{1,0:T(8,128)(2,1)S(1)}, u32[]{:S(2)}, u32[]{:S(2)}) collective-permute-start(bf16[256,768]{1,0:T(8,128)(2,1)S(1)} %get-tuple-element.50.refs_1_), channel_id=1, source_target_pairs={{0,4},{1,5},{16,20},{17,21}} | collective-permute-start | bytes 1179656 | tf_op jit(solution)/shard_map/ppermute | solution.py:708
  63.6 15.6 %collective-permute-start.7 = (bf16[256,768]{1,0:T(8,128)(2,1)S(1)}, bf16[256,768]{1,0:T(8,128)(2,1)}, u32[]{:S(2)}, u32[]{:S(2)}) collective-permute-start(bf16[256,768]{1,0:T(8,128)(2,1)S(1)} %get-tuple-element.50.refs_1_), channel_id=1, source_target_pairs={{4,5},{5,4},{20,21},{21,20}} | collective-permute-start | bytes 1179656 | tf_op jit(solution)/shard_map/ppermute | solution.py:724
  68.5 3.7 %copy-start.12 = (bf16[1152,768]{1,0:T(8,128)(2,1)}, bf16[1152,768]{1,0:T(8,128)(2,1)S(1)}, u32[]{:S(2)}) copy-start(bf16[1152,768]{1,0:T(8,128)(2,1)S(1)} %collective-permute-done.2.other) | copy-start | bytes 5308420
  72.2 0.6 copy-start.9
  72.8 0.7 copy-start
  72.8 0.9 copy-start.3
  72.8 1.0 copy-start.6
  73.9 5.3 %collective-permute-start.6 = (bf16[256,768]{1,0:T(8,128)(2,1)}, bf16[256,768]{1,0:T(8,128)(2,1)S(1)}, u32[]{:S(2)}, u32[]{:S(2)}) collective-permute-start(bf16[256,768]{1,0:T(8,128)(2,1)} %get-tuple-element.52.refs_0_), channel_id=1, source_target_pairs={{4,5},{5,4},{20,21},{21,20}} | collective-permute-start | bytes 1179656 | tf_op jit(solution)/shard_map/ppermute | solution.py:724
  74.5 4.6 %collective-permute-start.8 = (bf16[256,768]{1,0:T(8,128)(2,1)}, bf16[256,768]{1,0:T(8,128)(2,1)S(1)}, u32[]{:S(2)}, u32[]{:S(2)}) collective-permute-start(bf16[256,768]{1,0:T(8,128)(2,1)} %get-tuple-element.53.refs_2_), channel_id=1, source_target_pairs={{4,5},{5,4},{20,21},{21,20}} | collective-permute-start | bytes 1179656 | tf_op jit(solution)/shard_map/ppermute | solution.py:724
  75.2 3.9 %collective-permute-start.9 = (bf16[256,768]{1,0:T(8,128)(2,1)}, bf16[256,768]{1,0:T(8,128)(2,1)S(1)}, u32[]{:S(2)}, u32[]{:S(2)}) collective-permute-start(bf16[256,768]{1,0:T(8,128)(2,1)} %get-tuple-element.54.refs_3_), channel_id=1, source_target_pairs={{4,5},{5,4},{20,21},{21,20}} | collective-permute-start | bytes 1179656 | tf_op jit(solution)/shard_map/ppermute | solution.py:724
  75.9 1.0 copy-start.1
  76.9 1.0 copy-start.4
  77.9 1.0 copy-start.7
  78.9 1.0 copy-start.2
  78.9 1.1 copy-start.5
  78.9 1.2 %copy-start.8 = (bf16[256,768]{1,0:T(8,128)(2,1)S(1)}, bf16[256,768]{1,0:T(8,128)(2,1)}, u32[]{:S(2)}) copy-start(bf16[256,768]{1,0:T(8,128)(2,1)} %get-tuple-element.52.refs_0_) | copy-start | bytes 1179652
  78.9 1.2 %copy-start.10 = (f32[1,1152]{1,0:T(1,128)S(1)}, f32[1,1152]{1,0:T(1,128)}, u32[]{:S(2)}) copy-start(f32[1,1152]{1,0:T(1,128)} %copy-done.9) | copy-start | bytes 13828
  78.9 1.9 %copy-start.13 = (bf16[1152,768]{1,0:T(8,128)(2,1)S(1)}, bf16[1152,768]{1,0:T(8,128)(2,1)}, u32[]{:S(2)}) copy-start(bf16[1152,768]{1,0:T(8,128)(2,1)} %copy-done.12) | copy-start | bytes 5308420
  80.8 34.9 %copy-start.15 = (s32[1024]{0:T(1024)S(1)}, s32[1024]{0:T(1024)}, u32[]{:S(2)}) copy-start(s32[1024]{0:T(1024)} %param.6) | copy-start | bytes 12292
  80.8 34.9 %copy-start.17 = (s32[64]{0:T(128)S(1)}, s32[64]{0:T(128)}, u32[]{:S(2)}) copy-start(s32[64]{0:T(128)} %param.7) | copy-start | bytes 772
  82.5 33.2 %all-to-all-start.3 = ((f32[8,1,256]{2,1,0:T(1,128)}), f32[8,1,256]{2,1,0:T(1,128)S(1)}, u32[]{:S(2)}, u32[]{:S(2)}) async-start(f32[8,1,256]{2,1,0:T(1,128)} %shard_map.46), calls=%async_computation.3 | async-start | bytes 16384 | tf_op jit(solution)/shard_map/all_to_all | solution.py:733
  115.8 0.6 copy-start.16

commit v9 on v8

--- a/solution.py
+++ b/solution.py
@@ -19,7 +19,7 @@
 NEIGHBOUR = math.log2(neighbour_factor)
 DEAD = -1e30
 VMEM_LIMIT = 48 * 1024 * 1024
-FAST_LIMIT = 40 * 1024 * 1024
+FAST_LIMIT = 20 * 1024 * 1024
 WIDE = 512
 INFO = 16
 
@@ -340,39 +340,25 @@
     )(unit, slot, info)
 
 
-def pair_up_kernel(packed_in, extra, moved, packed, both):
-    rows = extra.shape[0]
-    both[:rows, :] = extra[...]
-    both[rows:, :] = moved[...]
-
-
-def pair_up(packed, extra, moved):
+def gather_kernel(home, *refs):
+    chunks, out = refs[:-2], refs[-1]
+
+    @pl.when(lax.axis_index("cl") == home)
+    def _():
+        for source, chunk in enumerate(chunks):
+            rows = chunk.shape[0]
+            out[source * rows : (source + 1) * rows, :] = chunk[...]
+
+
+def gather_rest(chunks, home, sums):
+    rows, width = chunks[0].shape
     return pl.pallas_call(
-        pair_up_kernel,
-        out_shape=(
-            jax.ShapeDtypeStruct(packed.shape, packed.dtype),
-            jax.ShapeDtypeStruct((2 * extra.shape[0], extra.shape[1]), extra.dtype),
-        ),
-        in_specs=list(vmem_specs(3)),
-        out_specs=vmem_specs(2),
-        input_output_aliases={0: 0},
+        functools.partial(gather_kernel, home),
+        out_shape=jax.ShapeDtypeStruct((len(chunks) * rows, width), jnp.bfloat16),
+        in_specs=list(vmem_specs(len(chunks) + 1)),
+        out_specs=vmem_specs(1)[0],
         compiler_params=pltpu.CompilerParams(vmem_limit_bytes=FAST_LIMIT),
-    )(packed, extra, moved)
-
-
-def gate_kernel(*refs):
-    pass
-
-
-def after(arrays, sums):
-    anywhere = pl.BlockSpec(memory_space=pl.ANY)
-    return pl.pallas_call(
-        gate_kernel,
-        out_shape=tuple(jax.ShapeDtypeStruct(x.shape, x.dtype) for x in arrays),
-        in_specs=[anywhere] * (len(arrays) + 1),
-        out_specs=(anywhere,) * len(arrays),
-        input_output_aliases={i: i for i in range(len(arrays))},
-    )(*arrays, sums)
+    )(*chunks, sums)
 
 
 class Layout:
@@ -382,7 +368,6 @@
         self.head = main - INFO
         self.rest = capacity - self.head
         self.per_owner = n_fine // n_owner
-        self.planes = n_owner // 2
         self.n_main = n_owner * main
         self.n_head = n_owner * self.head
         self.n_rest = n_owner * self.rest
@@ -437,7 +422,9 @@
     return [(start + i * (count // parts), count // parts) for i in range(parts)]
 
 
-def stream(rows_i, first, count, tiles, lab_lane, at, lab_sub, bias, buffers, put):
+def stream(
+    rows_i, first, count, tiles, lab_lane, at, lab_sub, bias, buffers, put, natural=False
+):
     step = 32
     tiles = [
         (ref, s, d, place + s - start)
@@ -480,8 +467,14 @@
                         bias_j = NEIGHBOUR - SCALE
                     else:
                         bias_j = jnp.concatenate([bias[part, :]] * repeat, axis=1)
-                    shift = jnp.where(label_j == label_i, -SCALE, bias_j)
-                    terms = jnp.exp2(buffer[c : c + step, :wide] * SCALE + shift)
+                    scores = buffer[c : c + step, :wide]
+                    if natural:
+                        low = math.log(neighbour_factor) - 1.0 / temper
+                        shift = jnp.where(label_j == label_i, -1.0 / temper, low)
+                        terms = jnp.exp(scores * (1.0 / temper) + shift)
+                    else:
+                        shift = jnp.where(label_j == label_i, -SCALE, bias_j)
+                        terms = jnp.exp2(scores * SCALE + shift)
                     acc = acc + jnp.sum(terms.reshape(step // 8, 8, wide), axis=0)
             put(place, jnp.sum(acc, axis=0, keepdims=True))
             return carry
@@ -543,9 +536,7 @@
         differs = (info != hot.astype(jnp.float32)) | (info >= lay.n_owner)
         wrong = wrong | ((lane == lay.n_fine) & differs)
         unfit = unfit + jnp.where(wrong, 1.0, 0.0)
-    unfit_ref[...] = jnp.broadcast_to(
-        jnp.max(unfit, axis=1, keepdims=True), unfit_ref.shape
-    ).astype(jnp.int32)
+    unfit_ref[0, 0] = jnp.max(unfit).astype(jnp.int32)
     total[...] = sums[...]
 
     def work(ref, ref_j, count, per, bias):
@@ -564,11 +555,9 @@
         work(mine, other, lay.n_main, lay.main, bias)
 
 
-def copy_all(lay, main_ref, rests, rows):
+def copy_all(lay, main_ref, rest, rows):
     copy_head(lay, main_ref, rows)
-    for i, ref in enumerate(rests):
-        start = lay.n_head + i * ref.shape[0]
-        rows[start : start + ref.shape[0], :] = ref[...]
+    rows[lay.n_head :, :] = rest[...]
 
 
 def rest_labels(lay, infos, lab_sub):
@@ -580,33 +569,30 @@
     n_head, n_rest = lay.n_head, lay.n_rest
     seconds = (rows_j, n_head, n_rest, n_head, 4)
     mains = (rows_j, 0, n_head, 0, 4)
-    stream(rows, 0, n_head, [seconds], lab_lane, 0, lab_sub, None, buffers, put)
-    stream(rows, n_head, n_rest, [seconds, mains], lab_lane, n_head, lab_sub, None, buffers, put)
-
-
-def inner_rest_kernel(lay, mine, *refs):
-    rests = refs[: lay.planes]
-    sums, lab_lane, lab_sub, rows, buf_a, buf_b = refs[lay.planes :]
+    stream(rows, 0, n_head, [seconds], lab_lane, 0, lab_sub, None, buffers, put, True)
+    second_tiles = [seconds, mains]
+    stream(rows, n_head, n_rest, second_tiles, lab_lane, n_head, lab_sub, None, buffers, put, True)
+
+
+def inner_rest_kernel(lay, mine, rest, sums, lab_lane, lab_sub, rows, buf_a, buf_b):
 
     @pl.when(lax.axis_index("cl") == lay.home)
     def _():
         rest_labels(lay, lines_of(lay, mine), lab_sub)
         turn_labels(lay, lab_sub, 0, lay.n_head + lay.n_rest, lab_lane, 0)
-        copy_all(lay, mine, rests, rows)
+        copy_all(lay, mine, rest, rows)
         rest_pairs(lay, rows, rows, lab_lane, lab_sub, (buf_a, buf_b), setter(sums))
 
 
-def cross_rest_kernel(lay, mine, other, *refs):
-    rests, refs = refs[: lay.planes], refs[lay.planes :]
-    others, refs = refs[: lay.planes], refs[lay.planes :]
+def cross_rest_kernel(lay, mine, other, rest, rest_other, *refs):
     main_sums, main_lane, sums, lab_lane, out_ref, lab_sub, rows, rows_j, total, buf_a, buf_b = refs
     is_home = lax.axis_index("cl") == lay.home
 
     @pl.when(is_home)
     def _():
         rest_labels(lay, lines_of(lay, other), lab_sub)
-        copy_all(lay, mine, rests, rows)
-        copy_all(lay, other, others, rows_j)
+        copy_all(lay, mine, rest, rows)
+        copy_all(lay, other, rest_other, rows_j)
         total[...] = sums[...]
         total[:, : lay.n_head] += main_sums[:, : lay.n_head]
         rest_pairs(lay, rows, rows_j, lab_lane, lab_sub, (buf_a, buf_b), adder(total))
@@ -625,7 +611,7 @@
             out_ref[source, :, : lay.main] = values[:, start : start + lay.main]
 
 
-def pair_call(kernel, lay, arrays, out_shape, sides, joins, more=()):
+def pair_call(kernel, lay, arrays, out_shape, sides, joins, more=(), out_specs=None):
     width = arrays[0].shape[1]
     side = pltpu.VMEM((sides[0], LANES), jnp.float32)
     rows = pltpu.VMEM((joins[0], width), jnp.bfloat16)
@@ -634,14 +620,9 @@
         functools.partial(kernel, lay),
         out_shape=out_shape,
         in_specs=list(vmem_specs(len(arrays))),
-        out_specs=vmem_specs(len(out_shape)),
+        out_specs=out_specs or vmem_specs(len(out_shape)),
         scratch_shapes=[side] * sides[1] + [rows] * joins[1] + list(more) + [buffer, buffer],
         compiler_params=pltpu.CompilerParams(vmem_limit_bytes=FAST_LIMIT),
-        cost_estimate=pl.CostEstimate(
-            flops=2 * lay.n_main * lay.n_main * width,
-            bytes_accessed=4 * lay.n_main * width,
-            transcendentals=lay.n_main * lay.n_main,
-        ),
     )(*arrays)
     return out
 
@@ -695,37 +676,36 @@
     main = -(-(rows // n_owner * 9 // 8) // 16) * 16
     if main >= capacity or n_fine >= LANES:
         return general(embeddings, labels, owner_map)
-    planes = n_owner // 2
-    plane = planes // 2 - 1
-    home = 2 * plane
+    home = n_owner // 4
     lay = Layout(n_owner, n_fine, capacity, main, home)
     unit, slot, info, extra, pos = place_rows(embeddings, labels, owner_map, lay)
-    moved = lax.ppermute(extra, "cl", [(2 * z + 1, 2 * z) for z in range(planes)])
-    packed, both = pair_up(pack_main(unit, slot, info, lay), extra, moved)
+    packed = pack_main(unit, slot, info, lay)
+    chunks = [
+        extra if source == home else lax.ppermute(extra, "cl", [(source, home)])
+        for source in range(n_owner)
+    ]
     mine = lax.all_to_all(
         packed.reshape(n_owner, main, width), "cl", split_axis=0, concat_axis=0, tiled=True
     ).reshape(n_owner * main, width)
-    far = [lax.ppermute(both, "cl", [(2 * z, home)]) for z in range(planes) if z != plane]
     other = lax.ppermute(mine, "grp", [(0, 1), (1, 0)])
     row = jax.ShapeDtypeStruct((1, lay.n_main), jnp.float32)
     lines = lay.n_head + lay.n_rest
     long_row = jax.ShapeDtypeStruct((1, lines), jnp.float32)
-    flag = jax.ShapeDtypeStruct((8, LANES), jnp.int32)
+    flag = jax.ShapeDtypeStruct((1, 1), jnp.int32)
     table = jax.ShapeDtypeStruct((n_owner, 1, capacity), jnp.float32)
     sides, joins = (lay.n_main, 2), (lay.n_head, 1)
     sums, main_lane = pair_call(inner_kernel, lay, (mine,), (row, row), sides, joins)
     joins = (lay.n_head, 2)
-    sums, unfit = pair_call(
-        cross_kernel, lay, (mine, other, sums, main_lane), (row, flag), sides, joins
-    )
-    far = list(after(far, sums))
-    rests = far[:plane] + [both] + far[plane:]
+    arrays = (mine, other, sums, main_lane)
+    specs = (pl.BlockSpec(memory_space=pltpu.VMEM), pl.BlockSpec(memory_space=pltpu.SMEM))
+    sums, unfit = pair_call(cross_kernel, lay, arrays, (row, flag), sides, joins, out_specs=specs)
+    rest = gather_rest(chunks, home, sums)
     swap = [(2 * home, 2 * home + 1), (2 * home + 1, 2 * home)]
-    rests_other = [lax.ppermute(x, ("cl", "grp"), swap) for x in rests]
+    rest_other = lax.ppermute(rest, ("cl", "grp"), swap)
     rest_sums, lane = pair_call(
-        inner_rest_kernel, lay, (mine, *rests), (long_row, long_row), (lines, 1), (lines, 1)
-    )
-    arrays = (mine, other, *rests, *rests_other, sums, main_lane, rest_sums, lane)
+        inner_rest_kernel, lay, (mine, rest), (long_row, long_row), (lines, 1), (lines, 1)
+    )
+    arrays = (mine, other, rest, rest_other, sums, main_lane, rest_sums, lane)
     total = pltpu.VMEM(long_row.shape, jnp.float32)
     (results,) = pair_call(
         cross_rest_kernel, lay, arrays, (table,), (lines, 1), (lines, 2), (total,)

time: 117 us -> 104 us (0.89)
  local copies, waits for them, and re-layouts: 7.3 us -> 0.61 us
  waiting for transfers between devices: 11.2 us -> 5.89 us
  starting transfers between devices: 37.1 us -> 33.4 us
  blocking collectives: 46 us -> 48.4 us
    all_to_all x1, starting transfers between devices: 26.7 us -> 16 us  [body(): lax.all_to_all(results, 'cl', split_axis=0, concat_axis=0, tiled=True)]
    ppermute x8, starting transfers between devices: 10.3 us -> 17.4 us  [the longest x7 16.6 us: body(): lax.ppermute(extra, 'cl', [(source, home)])]
    unnamed x32 -> x8, local copies, waits for them, and re-layouts: 6.79 us -> 0.61 us
    ppermute x8, waiting for transfers between devices: 5.85 us -> 0.02 us  [the longest x7 0.02 us: body(): lax.ppermute(extra, 'cl', [(source, home)])]
    all_to_all x1, blocking collectives: 46 us -> 48.4 us  [body(): lax.all_to_all(packed.reshape(n_owner, main, width), 'cl', split_axis=0,...]
  transfers between devices with their start and end apart: 10 -> 10, of which waited for: 2 -> 1; matrix products, arithmetic and copies ran while one was open for 0% -> 0% of each run, Pallas kernels for 8% -> 8%
where the time goes in v9:
time: 104 us; the launch traced here: 103 us
  blocking collectives  48.4 us (47%)
  starting transfers between devices  33.4 us (32%)
  Pallas kernels  14 us (13%)
  waiting for transfers between devices  5.89 us (6%)
    all_to_all x1, blocking collectives, body(): lax.all_to_all(packed.reshape(n_owner, main, width), 'cl', split_axis=0,...  48.4 us
    ppermute x7, starting transfers between devices, body(): lax.ppermute(extra, 'cl', [(source, home)])  16.6 us
    all_to_all x1, starting transfers between devices, body(): lax.all_to_all(results, 'cl', split_axis=0, concat_axis=0, tiled=True)  16 us
    pallas_call x4, Pallas kernels, pair_call(): pl.pallas_call(functools.partial(kernel, lay), out_shape=out_shape, in_sp...  9.12 us
    all_to_all x1, waiting for transfers between devices, body(): lax.all_to_all(results, 'cl', split_axis=0, concat_axis=0, tiled=True)  5.86 us
    pallas_call x1, Pallas kernels, place_rows(): pl.pallas_call(functools.partial(place_kernel, lay), out_shape=(jax.Shape...  2.81 us
  transfers between devices with their start and end apart: 10, of which 1 were waited for; matrix products, arithmetic and copies ran while one was open for 0% of the time, Pallas kernels for 8%

profile of v9, /device:TPU:0, one launch (start us, length us, event | category | flops | bytes accessed | tf_op | source)
XLA Modules:
  0.0 103.3 jit_solution(11044937416716964132)
XLA Ops:
  0.0 2.8 %shard_map.39 = (bf16[1024,768]{1,0:T(8,128)(2,1)S(1)}, s32[1,1024]{1,0:T(1,128)S(1)}, f32[1,128]{1,0:T(1,128)S(1)}, bf16[128,768]{1,0:T(8,128)(2,1)S(1)}, s32[8,128]{1,0:T(8,128)S(1)}) custom-call(bf16[1024,768]{1,0:T(8,128)(2,1)} %x_hbm.1, s32[8,128]{1,0:T(8,128)} %bitcast.28, s32[1,64]{1,0:T(1,128)} %bitcast.32), custom_call_target="tpu_custom_call" | custom-call | tf_op jit(solution)/shard_map/pallas_call | solution.py:307
  2.8 2.0 %shard_map.40 = bf16[1152,768]{1,0:T(8,128)(2,1)S(1)} custom-call(bf16[1024,768]{1,0:T(8,128)(2,1)S(1)} %get-tuple-element.37.unit, s32[1,1024]{1,0:T(1,128)S(1)} %get-tuple-element.38.slot_ref, f32[1,128]{1,0:T(1,128)S(1)} %get-tuple-element.39.info_ref), custom_call_target="tpu_custom_call" | custom-call | flops 1811939328 | bytes 3145728 | tf_op jit(solution)/shard_map/pallas_call | solution.py:329
  4.8 48.4 %all_to_all.23 = bf16[8,144,768]{2,1,0:T(8,128)(2,1)S(1)} all-to-all(bf16[8,144,768]{2,1,0:T(8,128)(2,1)S(1)} %bitcast.23), channel_id=1, replica_groups=mesh['parts'=2,'cl'=8,'grp'=2] {'cl'}, dimensions={0} | all-to-all | bytes 3538944 | tf_op jit(solution)/shard_map/all_to_all | solution.py:687
  53.2 0.0 collective-permute-start.1
  53.2 0.7 collective-permute-start.8
  53.9 0.7 collective-permute-start.7
  54.6 0.7 collective-permute-start.6
  55.3 0.7 collective-permute-start.5
  56.0 0.0 collective-permute-done.8.refs_7_
  56.0 0.7 collective-permute-start.4
  56.6 0.0 collective-permute-done.7.refs_6_
  56.7 0.7 collective-permute-start.3
  57.3 0.0 collective-permute-done.1.other
  57.3 12.6 %collective-permute-start.2 = (bf16[128,768]{1,0:T(8,128)(2,1)S(1)}, bf16[128,768]{1,0:T(8,128)(2,1)S(1)}, u32[]{:S(2)}, u32[]{:S(2)}) collective-permute-start(bf16[128,768]{1,0:T(8,128)(2,1)S(1)} %get-tuple-element.43.refs_2_), channel_id=1, source_target_pairs={{0,4},{1,5},{16,20},{17,21}} | collective-permute-start | bytes 589832 | tf_op jit(solution)/shard_map/ppermute | solution.py:684
  70.0 3.8 %shard_map.41 = (f32[1,1152]{1,0:T(1,128)S(1)}, f32[1,1152]{1,0:T(1,128)S(1)}) custom-call(bf16[1152,768]{1,0:T(8,128)(2,1)S(1)} %bitcast.16), custom_call_target="tpu_custom_call" | custom-call | tf_op jit(solution)/shard_map/pallas_call | solution.py:619
  73.7 4.5 %shard_map.42 = (f32[1,1152]{1,0:T(1,128)S(1)}, s32[1,1]{1,0:T(1,128)}) custom-call(bf16[1152,768]{1,0:T(8,128)(2,1)S(1)} %bitcast.17, bf16[1152,768]{1,0:T(8,128)(2,1)S(1)} %collective-permute-done.1.other, f32[1,1152]{1,0:T(1,128)S(1)} %get-tuple-element.40.sums, f32[1,1152]{1,0:T(1,128)S(1)} %get-tuple-element.41.lab_lane.refs_1_), custom_call_target="tpu_custom_call" | custom-call | tf_op jit(solution)/shard_map/pallas_call | solution.py:619
  78.2 0.0 collective-permute-done.6.refs_5_
  78.2 0.0 collective-permute-done.5.refs_4_
  78.2 0.0 collective-permute-done.4.refs_3_
  78.2 0.0 collective-permute-done.3.refs_1_
  78.2 0.0 collective-permute-done.2.refs_0_
  78.3 0.8 collective-permute-start.9
  79.0 0.2 shard_map.44
  79.2 0.0 collective-permute-done.9.rest_other
  79.2 0.0 copy-start.1
  79.3 0.0 copy-start.3
  79.3 0.0 copy-start.5
  79.3 0.7 shard_map.45
  80.0 16.0 %all-to-all-start.3 = ((f32[8,1,256]{2,1,0:T(1,128)}), f32[8,1,256]{2,1,0:T(1,128)S(1)}, u32[]{:S(2)}, u32[]{:S(2)}) async-start(f32[8,1,256]{2,1,0:T(1,128)} %shard_map.45), calls=%async_computation.3 | async-start | bytes 16384 | tf_op jit(solution)/shard_map/all_to_all | solution.py:713
  96.7 5.9 %all-to-all-done.3 = f32[8,1,256]{2,1,0:T(1,128)S(1)} async-done(((f32[8,1,256]{2,1,0:T(1,128)}), f32[8,1,256]{2,1,0:T(1,128)S(1)}, u32[]{:S(2)}, u32[]{:S(2)}) %all-to-all-start.3) | async-done | bytes 8224 | tf_op jit(solution)/shard_map/all_to_all | solution.py:713
  102.6 0.0 copy-done.1
  102.6 0.0 copy-done.3
  102.6 0.0 copy-done.5
  102.6 0.1 conditional.1
  102.6 0.1 branch_1_fun.1
  102.7 0.0 copy-start.4
  102.7 0.6 copy-done.4
  (1 shorter events, 0.0 us)
Async XLA Ops:
  53.2 4.1 %collective-permute-start.1 = (bf16[1152,768]{1,0:T(8,128)(2,1)S(1)}, bf16[1152,768]{1,0:T(8,128)(2,1)S(1)}, u32[]{:S(2)}, u32[]{:S(2)}) collective-permute-start(bf16[1152,768]{1,0:T(8,128)(2,1)S(1)} %bitcast.15), channel_id=1, source_target_pairs={{0,1},{1,0},{2,3},{3,2},{4,5},{5,4},{6,7},{7,6},{8,9},{9,8},{10,11... | collective-permute-start | bytes 5308424 | tf_op jit(solution)/shard_map/ppermute | solution.py:690
  53.2 2.7 %collective-permute-start.8 = (bf16[128,768]{1,0:T(8,128)(2,1)S(1)}, bf16[128,768]{1,0:T(8,128)(2,1)S(1)}, u32[]{:S(2)}, u32[]{:S(2)}) collective-permute-start(bf16[128,768]{1,0:T(8,128)(2,1)S(1)} %get-tuple-element.43.refs_2_), channel_id=1, source_target_pairs={{14,4},{15,5},{30,20},{31,21}} | collective-permute-start | bytes 589832 | tf_op jit(solution)/shard_map/ppermute | solution.py:684
  53.9 2.7 %collective-permute-start.7 = (bf16[128,768]{1,0:T(8,128)(2,1)S(1)}, bf16[128,768]{1,0:T(8,128)(2,1)S(1)}, u32[]{:S(2)}, u32[]{:S(2)}) collective-permute-start(bf16[128,768]{1,0:T(8,128)(2,1)S(1)} %get-tuple-element.43.refs_2_), channel_id=1, source_target_pairs={{12,4},{13,5},{28,20},{29,21}} | collective-permute-start | bytes 589832 | tf_op jit(solution)/shard_map/ppermute | solution.py:684
  54.6 23.6 %collective-permute-start.6 = (bf16[128,768]{1,0:T(8,128)(2,1)S(1)}, bf16[128,768]{1,0:T(8,128)(2,1)S(1)}, u32[]{:S(2)}, u32[]{:S(2)}) collective-permute-start(bf16[128,768]{1,0:T(8,128)(2,1)S(1)} %get-tuple-element.43.refs_2_), channel_id=1, source_target_pairs={{10,4},{11,5},{26,20},{27,21}} | collective-permute-start | bytes 589832 | tf_op jit(solution)/shard_map/ppermute | solution.py:684
  55.3 22.9 %collective-permute-start.5 = (bf16[128,768]{1,0:T(8,128)(2,1)S(1)}, bf16[128,768]{1,0:T(8,128)(2,1)S(1)}, u32[]{:S(2)}, u32[]{:S(2)}) collective-permute-start(bf16[128,768]{1,0:T(8,128)(2,1)S(1)} %get-tuple-element.43.refs_2_), channel_id=1, source_target_pairs={{8,4},{9,5},{24,20},{25,21}} | collective-permute-start | bytes 589832 | tf_op jit(solution)/shard_map/ppermute | solution.py:684
  56.0 22.2 %collective-permute-start.4 = (bf16[128,768]{1,0:T(8,128)(2,1)S(1)}, bf16[128,768]{1,0:T(8,128)(2,1)S(1)}, u32[]{:S(2)}, u32[]{:S(2)}) collective-permute-start(bf16[128,768]{1,0:T(8,128)(2,1)S(1)} %get-tuple-element.43.refs_2_), channel_id=1, source_target_pairs={{6,4},{7,5},{22,20},{23,21}} | collective-permute-start | bytes 589832 | tf_op jit(solution)/shard_map/ppermute | solution.py:684
  56.7 21.6 %collective-permute-start.3 = (bf16[128,768]{1,0:T(8,128)(2,1)S(1)}, bf16[128,768]{1,0:T(8,128)(2,1)S(1)}, u32[]{:S(2)}, u32[]{:S(2)}) collective-permute-start(bf16[128,768]{1,0:T(8,128)(2,1)S(1)} %get-tuple-element.43.refs_2_), channel_id=1, source_target_pairs={{2,4},{3,5},{18,20},{19,21}} | collective-permute-start | bytes 589832 | tf_op jit(solution)/shard_map/ppermute | solution.py:684
  57.3 20.9 %collective-permute-start.2 = (bf16[128,768]{1,0:T(8,128)(2,1)S(1)}, bf16[128,768]{1,0:T(8,128)(2,1)S(1)}, u32[]{:S(2)}, u32[]{:S(2)}) collective-permute-start(bf16[128,768]{1,0:T(8,128)(2,1)S(1)} %get-tuple-element.43.refs_2_), channel_id=1, source_target_pairs={{0,4},{1,5},{16,20},{17,21}} | collective-permute-start | bytes 589832 | tf_op jit(solution)/shard_map/ppermute | solution.py:684
  78.3 1.0 collective-permute-start.9
  79.2 23.3 %copy-start.1 = (bf16[1024,768]{1,0:T(8,128)(2,1)S(1)}, bf16[1024,768]{1,0:T(8,128)(2,1)}, u32[]{:S(2)}) copy-start(bf16[1024,768]{1,0:T(8,128)(2,1)} %x_hbm.1) | copy-start | bytes 4718596
  79.3 23.3 %copy-start.3 = (s32[1024]{0:T(1024)S(1)}, s32[1024]{0:T(1024)}, u32[]{:S(2)}) copy-start(s32[1024]{0:T(1024)} %param.6) | copy-start | bytes 12292
  79.3 23.3 %copy-start.5 = (s32[64]{0:T(128)S(1)}, s32[64]{0:T(128)}, u32[]{:S(2)}) copy-start(s32[64]{0:T(128)} %param.7) | copy-start | bytes 772
  80.0 22.6 %all-to-all-start.3 = ((f32[8,1,256]{2,1,0:T(1,128)}), f32[8,1,256]{2,1,0:T(1,128)S(1)}, u32[]{:S(2)}, u32[]{:S(2)}) async-start(f32[8,1,256]{2,1,0:T(1,128)} %shard_map.45), calls=%async_computation.3 | async-start | bytes 16384 | tf_op jit(solution)/shard_map/all_to_all | solution.py:713
  102.7 0.6 copy-start.4

commit v10 on v9

--- a/solution.py
+++ b/solution.py
@@ -19,7 +19,7 @@
 NEIGHBOUR = math.log2(neighbour_factor)
 DEAD = -1e30
 VMEM_LIMIT = 48 * 1024 * 1024
-FAST_LIMIT = 20 * 1024 * 1024
+FAST_LIMIT = 24 * 1024 * 1024
 WIDE = 512
 INFO = 16
 
@@ -340,21 +340,54 @@
     )(unit, slot, info)
 
 
+def gate_kernel(*refs):
+    pass
+
+
+def after(rows, there):
+    anywhere = pl.BlockSpec(memory_space=pl.ANY)
+    return pl.pallas_call(
+        gate_kernel,
+        out_shape=jax.ShapeDtypeStruct(rows.shape, rows.dtype),
+        in_specs=[anywhere] * 2,
+        out_specs=anywhere,
+        input_output_aliases={0: 0},
+    )(rows, there)
+
+
+def pair_up_kernel(first, second, out):
+    rows = first.shape[0]
+    out[:rows, :] = first[...]
+    out[rows:, :] = second[...]
+
+
+def pair_up(first, second):
+    rows, width = first.shape
+    return pl.pallas_call(
+        pair_up_kernel,
+        out_shape=jax.ShapeDtypeStruct((2 * rows, width), jnp.bfloat16),
+        in_specs=list(vmem_specs(2)),
+        out_specs=vmem_specs(1)[0],
+        compiler_params=pltpu.CompilerParams(vmem_limit_bytes=FAST_LIMIT),
+    )(first, second)
+
+
 def gather_kernel(home, *refs):
     chunks, out = refs[:-2], refs[-1]
 
     @pl.when(lax.axis_index("cl") == home)
     def _():
-        for source, chunk in enumerate(chunks):
-            rows = chunk.shape[0]
-            out[source * rows : (source + 1) * rows, :] = chunk[...]
+        start = 0
+        for chunk in chunks:
+            out[start : start + chunk.shape[0], :] = chunk[...]
+            start += chunk.shape[0]
 
 
 def gather_rest(chunks, home, sums):
-    rows, width = chunks[0].shape
+    rows, width = sum(x.shape[0] for x in chunks), chunks[0].shape[1]
     return pl.pallas_call(
         functools.partial(gather_kernel, home),
-        out_shape=jax.ShapeDtypeStruct((len(chunks) * rows, width), jnp.bfloat16),
+        out_shape=jax.ShapeDtypeStruct((rows, width), jnp.bfloat16),
         in_specs=list(vmem_specs(len(chunks) + 1)),
         out_specs=vmem_specs(1)[0],
         compiler_params=pltpu.CompilerParams(vmem_limit_bytes=FAST_LIMIT),
@@ -423,7 +456,7 @@
 
 
 def stream(
-    rows_i, first, count, tiles, lab_lane, at, lab_sub, bias, buffers, put, natural=False
+    rows_i, first, count, tiles, lab_lane, at, lab_sub, bias, buffers, put, wide=WIDE
 ):
     step = 32
     tiles = [
@@ -468,20 +501,14 @@
                     else:
                         bias_j = jnp.concatenate([bias[part, :]] * repeat, axis=1)
                     scores = buffer[c : c + step, :wide]
-                    if natural:
-                        low = math.log(neighbour_factor) - 1.0 / temper
-                        shift = jnp.where(label_j == label_i, -1.0 / temper, low)
-                        terms = jnp.exp(scores * (1.0 / temper) + shift)
-                    else:
-                        shift = jnp.where(label_j == label_i, -SCALE, bias_j)
-                        terms = jnp.exp2(scores * SCALE + shift)
+                    shift = jnp.where(label_j == label_i, -SCALE, bias_j)
+                    terms = jnp.exp2(scores * SCALE + shift)
                     acc = acc + jnp.sum(terms.reshape(step // 8, 8, wide), axis=0)
             put(place, jnp.sum(acc, axis=0, keepdims=True))
             return carry
 
         lax.fori_loop(0, blocks, body, 0)
 
-    wide = WIDE
     if count >= wide:
         run(0, count // wide, wide)
     if count % wide:
@@ -509,7 +536,7 @@
     def work(ref, count, per, bias):
         write_labels(lay, infos, 0, per, 0, lab_sub, bias)
         turn_labels(lay, lab_sub, 0, count, lab_lane, 0)
-        tiles = [(ref, 0, count, 0, 4)]
+        tiles = [(ref, 0, count, 0, 2)]
         stream(ref, 0, count, tiles, lab_lane, 0, lab_sub, bias, (buf_a, buf_b), setter(sums))
 
     @pl.when(is_home)
@@ -541,7 +568,7 @@
 
     def work(ref, ref_j, count, per, bias):
         write_labels(lay, infos, 0, per, 0, lab_sub, bias)
-        tiles = [(ref_j, 0, count, 0, 4)]
+        tiles = [(ref_j, 0, count, 0, 2)]
         stream(ref, 0, count, tiles, lab_lane, 0, lab_sub, bias, (buf_a, buf_b), adder(total))
 
     @pl.when(is_home)
@@ -565,13 +592,13 @@
     write_labels(lay, infos, lay.head, lay.rest, lay.n_head, lab_sub, None)
 
 
-def rest_pairs(lay, rows, rows_j, lab_lane, lab_sub, buffers, put):
+def rest_pairs(lay, rows, rows_j, lab_lane, lab_sub, buffers, put, wide):
     n_head, n_rest = lay.n_head, lay.n_rest
-    seconds = (rows_j, n_head, n_rest, n_head, 4)
-    mains = (rows_j, 0, n_head, 0, 4)
-    stream(rows, 0, n_head, [seconds], lab_lane, 0, lab_sub, None, buffers, put, True)
+    seconds = (rows_j, n_head, n_rest, n_head, 2)
+    mains = (rows_j, 0, n_head, 0, 2)
+    stream(rows, 0, n_head, [seconds], lab_lane, 0, lab_sub, None, buffers, put, wide)
     second_tiles = [seconds, mains]
-    stream(rows, n_head, n_rest, second_tiles, lab_lane, n_head, lab_sub, None, buffers, put, True)
+    stream(rows, n_head, n_rest, second_tiles, lab_lane, n_head, lab_sub, None, buffers, put, wide)
 
 
 def inner_rest_kernel(lay, mine, rest, sums, lab_lane, lab_sub, rows, buf_a, buf_b):
@@ -581,7 +608,7 @@
         rest_labels(lay, lines_of(lay, mine), lab_sub)
         turn_labels(lay, lab_sub, 0, lay.n_head + lay.n_rest, lab_lane, 0)
         copy_all(lay, mine, rest, rows)
-        rest_pairs(lay, rows, rows, lab_lane, lab_sub, (buf_a, buf_b), setter(sums))
+        rest_pairs(lay, rows, rows, lab_lane, lab_sub, (buf_a, buf_b), setter(sums), WIDE)
 
 
 def cross_rest_kernel(lay, mine, other, rest, rest_other, *refs):
@@ -595,7 +622,7 @@
         copy_all(lay, other, rest_other, rows_j)
         total[...] = sums[...]
         total[:, : lay.n_head] += main_sums[:, : lay.n_head]
-        rest_pairs(lay, rows, rows_j, lab_lane, lab_sub, (buf_a, buf_b), adder(total))
+        rest_pairs(lay, rows, rows_j, lab_lane, lab_sub, (buf_a, buf_b), adder(total), 2 * WIDE)
         values = jnp.log(total[...])
         for source in range(lay.n_owner):
             start = source * lay.head
@@ -611,11 +638,11 @@
             out_ref[source, :, : lay.main] = values[:, start : start + lay.main]
 
 
-def pair_call(kernel, lay, arrays, out_shape, sides, joins, more=(), out_specs=None):
+def pair_call(kernel, lay, arrays, out_shape, sides, joins, more=(), out_specs=None, pairs=0):
     width = arrays[0].shape[1]
     side = pltpu.VMEM((sides[0], LANES), jnp.float32)
     rows = pltpu.VMEM((joins[0], width), jnp.bfloat16)
-    buffer = pltpu.VMEM((lay.n_main // 4, WIDE), jnp.float32)
+    buffer = pltpu.VMEM((lay.n_main // 2, 2 * WIDE), jnp.float32)
     out = pl.pallas_call(
         functools.partial(kernel, lay),
         out_shape=out_shape,
@@ -623,6 +650,9 @@
         out_specs=out_specs or vmem_specs(len(out_shape)),
         scratch_shapes=[side] * sides[1] + [rows] * joins[1] + list(more) + [buffer, buffer],
         compiler_params=pltpu.CompilerParams(vmem_limit_bytes=FAST_LIMIT),
+        cost_estimate=pl.CostEstimate(
+            flops=2 * pairs * width, bytes_accessed=1, transcendentals=pairs
+        ),
     )(*arrays)
     return out
 
@@ -680,13 +710,23 @@
     lay = Layout(n_owner, n_fine, capacity, main, home)
     unit, slot, info, extra, pos = place_rows(embeddings, labels, owner_map, lay)
     packed = pack_main(unit, slot, info, lay)
-    chunks = [
-        extra if source == home else lax.ppermute(extra, "cl", [(source, home)])
-        for source in range(n_owner)
-    ]
+    planes, plane = n_owner // 2, home // 2
+    turning = [z for z in range(planes) if z not in (plane, plane + 1)]
+    moved = lax.ppermute(extra, "cl", [(2 * z + 1, 2 * z) for z in turning])
+    both = pair_up(extra, moved)
+    chunks = []
+    for z in range(planes):
+        if z in turning:
+            chunks.append(lax.ppermute(both, "cl", [(2 * z, home)]))
+        else:
+            for source in (2 * z, 2 * z + 1):
+                chunks.append(
+                    extra if source == home else lax.ppermute(extra, "cl", [(source, home)])
+                )
     mine = lax.all_to_all(
         packed.reshape(n_owner, main, width), "cl", split_axis=0, concat_axis=0, tiled=True
     ).reshape(n_owner * main, width)
+    mine = after(mine, both)
     other = lax.ppermute(mine, "grp", [(0, 1), (1, 0)])
     row = jax.ShapeDtypeStruct((1, lay.n_main), jnp.float32)
     lines = lay.n_head + lay.n_rest
@@ -703,7 +743,13 @@
     swap = [(2 * home, 2 * home + 1), (2 * home + 1, 2 * home)]
     rest_other = lax.ppermute(rest, ("cl", "grp"), swap)
     rest_sums, lane = pair_call(
-        inner_rest_kernel, lay, (mine, rest), (long_row, long_row), (lines, 1), (lines, 1)
+        inner_rest_kernel,
+        lay,
+        (mine, rest),
+        (long_row, long_row),
+        (lines, 1),
+        (lines, 1),
+        pairs=3 * lay.n_head * lay.n_rest,
     )
     arrays = (mine, other, rest, rest_other, sums, main_lane, rest_sums, lane)
     total = pltpu.VMEM(long_row.shape, jnp.float32)

time: 104 us -> 100 us (0.962)
  blocking collectives: 48.4 us -> 0 us
  waiting for transfers between devices: 5.89 us -> 45 us
  local copies, waits for them, and re-layouts: 0.61 us -> 5.05 us
  Pallas kernels: 14 us -> 15.7 us
    all_to_all x1 -> x0, blocking collectives: 48.4 us -> none  [body(): lax.all_to_all(packed.reshape(n_owner, main, width), 'cl', split_axis=0,...]
    all_to_all x0 -> x1, waiting for transfers between devices: none -> 22.4 us  [body(): lax.all_to_all(packed.reshape(n_owner, main, width), 'cl', split_axis=0,...]
    ppermute x0 -> x3, waiting for transfers between devices: none -> 16.7 us  [the longest x1 16.7 us: body(): moved = lax.ppermute(extra, 'cl', [(2 * z + 1, 2 * z) for z in turning])]
    ppermute x7 -> x3, starting transfers between devices: 16.6 us -> 2.02 us  [body(): lax.ppermute(extra, 'cl', [(source, home)])]
    all_to_all x0 -> x1, starting transfers between devices: none -> 7.28 us  [body(): lax.all_to_all(packed.reshape(n_owner, main, width), 'cl', split_axis=0,...]
    unnamed x8 -> x18, local copies, waits for them, and re-layouts: 0.61 us -> 5.05 us
    ppermute x0 -> x3, starting transfers between devices: none -> 4.05 us  [the longest x2 2.77 us: body(): chunks.append(lax.ppermute(both, 'cl', [(2 * z, home)]))]
    all_to_all x1, starting transfers between devices: 16 us -> 19.3 us  [body(): lax.all_to_all(results, 'cl', split_axis=0, concat_axis=0, tiled=True)]
  transfers between devices with their start and end apart: 10 -> 10, of which waited for: 1 -> 3; matrix products, arithmetic and copies ran while one was open for 0% -> 0% of each run, Pallas kernels for 8% -> 9%
where the time goes in v10:
time: 100 us
  waiting for transfers between devices  45 us (45%)
  starting transfers between devices  33.4 us (33%)
  Pallas kernels  15.7 us (16%)
  local copies, waits for them, and re-layouts  5.05 us (5%)
    all_to_all x1, waiting for transfers between devices, body(): lax.all_to_all(packed.reshape(n_owner, main, width), 'cl', split_axis=0,...  22.4 us
    all_to_all x1, starting transfers between devices, body(): lax.all_to_all(results, 'cl', split_axis=0, concat_axis=0, tiled=True)  19.3 us
    ppermute x1, waiting for transfers between devices, body(): moved = lax.ppermute(extra, 'cl', [(2 * z + 1, 2 * z) for z in turning])  16.7 us
    pallas_call x4, Pallas kernels, pair_call(): pl.pallas_call(functools.partial(kernel, lay), out_shape=out_shape, in_sp...  9.42 us
    all_to_all x1, starting transfers between devices, body(): lax.all_to_all(packed.reshape(n_owner, main, width), 'cl', split_axis=0,...  7.28 us
    all_to_all x1, waiting for transfers between devices, body(): lax.all_to_all(results, 'cl', split_axis=0, concat_axis=0, tiled=True)  5.86 us
    unnamed x18, local copies, waits for them, and re-layouts  5.05 us
    pallas_call x1, Pallas kernels, pack_main(): pl.pallas_call(functools.partial(main_kernel, lay), out_shape=jax.ShapeDt...  3.3 us
  transfers between devices with their start and end apart: 10, of which 3 were waited for; matrix products, arithmetic and copies ran while one was open for 0% of the time, Pallas kernels for 9%

profile of v10, /device:TPU:0, one launch (start us, length us, event | category | flops | bytes accessed | tf_op | source)
XLA Modules:
  0.0 100.0 jit_solution(1530798666372406011)
XLA Ops:
  0.0 2.8 %shard_map.39 = (bf16[1024,768]{1,0:T(8,128)(2,1)S(1)}, s32[1,1024]{1,0:T(1,128)S(1)}, f32[1,128]{1,0:T(1,128)S(1)}, bf16[128,768]{1,0:T(8,128)(2,1)S(1)}, s32[8,128]{1,0:T(8,128)S(1)}) custom-call(bf16[1024,768]{1,0:T(8,128)(2,1)} %x_hbm.1, s32[8,128]{1,0:T(8,128)} %bitcast.23, s32[1,64]{1,0:T(1,128)} %bitcast.27), custom_call_target="tpu_custom_call" | custom-call | tf_op jit(solution)/shard_map/pallas_call | solution.py:307
  2.8 3.3 %shard_map.40 = bf16[1152,768]{1,0:T(8,128)(2,1)} custom-call(bf16[1024,768]{1,0:T(8,128)(2,1)S(1)} %get-tuple-element.37.unit, s32[1,1024]{1,0:T(1,128)S(1)} %get-tuple-element.38.slot_ref, f32[1,128]{1,0:T(1,128)S(1)} %get-tuple-element.39.info_ref), custom_call_target="tpu_custom_call" | custom-call | flops 1811939328 | bytes 3145728 | tf_op jit(solution)/shard_map/pallas_call | solution.py:329
  6.1 7.3 %all-to-all-start.2 = ((bf16[8,144,768]{2,1,0:T(8,128)(2,1)}), bf16[8,144,768]{2,1,0:T(8,128)(2,1)S(1)}, u32[]{:S(2)}, u32[]{:S(2)}) async-start(bf16[8,144,768]{2,1,0:T(8,128)(2,1)} %bitcast.12), calls=%async_computation.2 | async-start | bytes 3538944 | tf_op jit(solution)/shard_map/all_to_all | solution.py:726
  13.4 1.3 %collective-permute-start.1 = (bf16[128,768]{1,0:T(8,128)(2,1)S(1)}, bf16[128,768]{1,0:T(8,128)(2,1)S(1)}, u32[]{:S(2)}, u32[]{:S(2)}) collective-permute-start(bf16[128,768]{1,0:T(8,128)(2,1)S(1)} %get-tuple-element.40.first.refs_1_), channel_id=1, source_target_pairs={{2,0},{14,12},{3,1},{15,13},{18,16},{30,28},{19,17},{31,29}} | collective-permute-start | bytes 589832 | tf_op jit(solution)/shard_map/ppermute | solution.py:715
  14.7 16.7 %collective-permute-done.1.second = bf16[128,768]{1,0:T(8,128)(2,1)S(1)} collective-permute-done((bf16[128,768]{1,0:T(8,128)(2,1)S(1)}, bf16[128,768]{1,0:T(8,128)(2,1)S(1)}, u32[]{:S(2)}, u32[]{:S(2)}) %collective-permute-start.1) | collective-permute-done | bytes 196640 | tf_op jit(solution)/shard_map/ppermute | solution.py:715
  31.4 0.0 copy-start.3
  31.4 0.7 copy-done.3
  32.2 22.4 %all-to-all-done.2 = bf16[8,144,768]{2,1,0:T(8,128)(2,1)S(1)} async-done(((bf16[8,144,768]{2,1,0:T(8,128)(2,1)}), bf16[8,144,768]{2,1,0:T(8,128)(2,1)S(1)}, u32[]{:S(2)}, u32[]{:S(2)}) %all-to-all-start.2) | async-done | bytes 1769504 | tf_op jit(solution)/shard_map/all_to_all | solution.py:726
  54.6 0.0 copy-start
  54.6 1.2 %copy-done = bf16[8,144,768]{2,1,0:T(8,128)(2,1)} copy-done((bf16[8,144,768]{2,1,0:T(8,128)(2,1)}, bf16[8,144,768]{2,1,0:T(8,128)(2,1)S(1)}, u32[]{:S(2)}) %copy-start) | copy-done | bytes 1769496
  55.8 0.0 copy-start.4
  55.8 0.0 collective-permute-start.2
  55.9 1.0 copy-done.4
  56.8 0.7 collective-permute-start.7
  57.5 2.1 %collective-permute-start.3 = (bf16[256,768]{1,0:T(8,128)(2,1)S(1)}, bf16[256,768]{1,0:T(8,128)(2,1)S(1)}, u32[]{:S(2)}, u32[]{:S(2)}) collective-permute-start(bf16[256,768]{1,0:T(8,128)(2,1)S(1)} %copy-done.4), channel_id=1, source_target_pairs={{0,4},{1,5},{16,20},{17,21}} | collective-permute-start | bytes 1179656 | tf_op jit(solution)/shard_map/ppermute | solution.py:720
  59.6 0.7 collective-permute-start.6
  60.3 0.7 collective-permute-start.5
  61.0 0.0 collective-permute-done.2.other
  61.0 0.7 collective-permute-start.4
  61.7 0.0 copy-start.1
  61.7 1.5 %copy-done.1 = bf16[1152,768]{1,0:T(8,128)(2,1)S(1)} copy-done((bf16[1152,768]{1,0:T(8,128)(2,1)S(1)}, bf16[1152,768]{1,0:T(8,128)(2,1)}, u32[]{:S(2)}) %copy-start.1) | copy-done | bytes 1769496
  63.2 0.0 copy-start.2
  63.2 3.8 %shard_map.43 = (f32[1,1152]{1,0:T(1,128)S(1)}, f32[1,1152]{1,0:T(1,128)S(1)}) custom-call(bf16[1152,768]{1,0:T(8,128)(2,1)S(1)} %copy-done.1), custom_call_target="tpu_custom_call" | custom-call | bytes 1 | tf_op jit(solution)/shard_map/pallas_call | solution.py:646
  67.0 0.0 copy-done.2
  67.0 4.7 %shard_map.44 = (f32[1,1152]{1,0:T(1,128)S(1)}, s32[1,1]{1,0:T(1,128)}) custom-call(bf16[1152,768]{1,0:T(8,128)(2,1)S(1)} %copy-done.2, bf16[1152,768]{1,0:T(8,128)(2,1)S(1)} %collective-permute-done.2.other, f32[1,1152]{1,0:T(1,128)S(1)} %get-tuple-element.41.sums, f32[1,1152]{1,0:T(1,128)S(1)} %get-tuple-element.42.lab_lane.refs_1_), custom_call_target="tpu_custom_call" | custom-call | bytes 1 | tf_op jit(solution)/shard_map/pallas_call | solution.py:646
  71.7 0.0 collective-permute-done.6.refs_4_
  71.7 0.0 collective-permute-done.5.refs_3_
  71.7 0.0 collective-permute-done.4.refs_2_
  71.7 0.0 collective-permute-done.7.refs_5_
  71.8 0.0 collective-permute-done.3.refs_0_
  71.8 0.8 collective-permute-start.8
  72.6 0.2 shard_map.46
  72.8 0.0 collective-permute-done.8.rest_other
  72.8 0.0 copy-start.6
  72.8 0.0 copy-start.8
  72.8 0.0 copy-start.10
  72.8 0.7 shard_map.47
  73.5 19.3 %all-to-all-start.3 = ((f32[8,1,256]{2,1,0:T(1,128)}), f32[8,1,256]{2,1,0:T(1,128)S(1)}, u32[]{:S(2)}, u32[]{:S(2)}) async-start(f32[8,1,256]{2,1,0:T(1,128)} %shard_map.47), calls=%async_computation.3 | async-start | bytes 16384 | tf_op jit(solution)/shard_map/all_to_all | solution.py:759
  93.4 5.9 %all-to-all-done.3 = f32[8,1,256]{2,1,0:T(1,128)S(1)} async-done(((f32[8,1,256]{2,1,0:T(1,128)}), f32[8,1,256]{2,1,0:T(1,128)S(1)}, u32[]{:S(2)}, u32[]{:S(2)}) %all-to-all-start.3) | async-done | bytes 8224 | tf_op jit(solution)/shard_map/all_to_all | solution.py:759
  99.3 0.0 copy-done.6
  99.3 0.0 copy-done.8
  99.3 0.0 copy-done.10
  99.3 0.1 conditional.1
  99.3 0.1 branch_1_fun.1
  99.4 0.0 copy-start.9
  99.4 0.6 copy-done.9
  (3 shorter events, 0.0 us)
Async XLA Ops:
  6.1 48.5 %all-to-all-start.2 = ((bf16[8,144,768]{2,1,0:T(8,128)(2,1)}), bf16[8,144,768]{2,1,0:T(8,128)(2,1)S(1)}, u32[]{:S(2)}, u32[]{:S(2)}) async-start(bf16[8,144,768]{2,1,0:T(8,128)(2,1)} %bitcast.12), calls=%async_computation.2 | async-start | bytes 3538944 | tf_op jit(solution)/shard_map/all_to_all | solution.py:726
  13.4 18.0 %collective-permute-start.1 = (bf16[128,768]{1,0:T(8,128)(2,1)S(1)}, bf16[128,768]{1,0:T(8,128)(2,1)S(1)}, u32[]{:S(2)}, u32[]{:S(2)}) collective-permute-start(bf16[128,768]{1,0:T(8,128)(2,1)S(1)} %get-tuple-element.40.first.refs_1_), channel_id=1, source_target_pairs={{2,0},{14,12},{3,1},{15,13},{18,16},{30,28},{19,17},{31,29}} | collective-permute-start | bytes 589832 | tf_op jit(solution)/shard_map/ppermute | solution.py:715
  31.4 0.8 copy-start.3
  54.6 1.2 %copy-start = (bf16[8,144,768]{2,1,0:T(8,128)(2,1)}, bf16[8,144,768]{2,1,0:T(8,128)(2,1)S(1)}, u32[]{:S(2)}) copy-start(bf16[8,144,768]{2,1,0:T(8,128)(2,1)S(1)} %all-to-all-done.2) | copy-start | bytes 5308420
  55.8 1.0 copy-start.4
  55.8 5.1 %collective-permute-start.2 = (bf16[1152,768]{1,0:T(8,128)(2,1)}, bf16[1152,768]{1,0:T(8,128)(2,1)S(1)}, u32[]{:S(2)}, u32[]{:S(2)}) collective-permute-start(bf16[1152,768]{1,0:T(8,128)(2,1)} %shard_map.42.mine), channel_id=1, source_target_pairs={{0,1},{1,0},{2,3},{3,2},{4,5},{5,4},{6,7},{7,6},{8,9},{9,8},{10,11... | collective-permute-start | bytes 5308424 | tf_op jit(solution)/shard_map/ppermute | solution.py:730
  56.8 14.9 %collective-permute-start.7 = (bf16[256,768]{1,0:T(8,128)(2,1)S(1)}, bf16[256,768]{1,0:T(8,128)(2,1)S(1)}, u32[]{:S(2)}, u32[]{:S(2)}) collective-permute-start(bf16[256,768]{1,0:T(8,128)(2,1)S(1)} %copy-done.4), channel_id=1, source_target_pairs={{12,4},{13,5},{28,20},{29,21}} | collective-permute-start | bytes 1179656 | tf_op jit(solution)/shard_map/ppermute | solution.py:720
  57.5 14.2 %collective-permute-start.3 = (bf16[256,768]{1,0:T(8,128)(2,1)S(1)}, bf16[256,768]{1,0:T(8,128)(2,1)S(1)}, u32[]{:S(2)}, u32[]{:S(2)}) collective-permute-start(bf16[256,768]{1,0:T(8,128)(2,1)S(1)} %copy-done.4), channel_id=1, source_target_pairs={{0,4},{1,5},{16,20},{17,21}} | collective-permute-start | bytes 1179656 | tf_op jit(solution)/shard_map/ppermute | solution.py:720
  59.6 12.1 %collective-permute-start.6 = (bf16[128,768]{1,0:T(8,128)(2,1)S(1)}, bf16[128,768]{1,0:T(8,128)(2,1)S(1)}, u32[]{:S(2)}, u32[]{:S(2)}) collective-permute-start(bf16[128,768]{1,0:T(8,128)(2,1)S(1)} %get-tuple-element.40.first.refs_1_), channel_id=1, source_target_pairs={{10,4},{11,5},{26,20},{27,21}} | collective-permute-start | bytes 589832 | tf_op jit(solution)/shard_map/ppermute | solution.py:724
  60.3 11.4 %collective-permute-start.5 = (bf16[128,768]{1,0:T(8,128)(2,1)S(1)}, bf16[128,768]{1,0:T(8,128)(2,1)S(1)}, u32[]{:S(2)}, u32[]{:S(2)}) collective-permute-start(bf16[128,768]{1,0:T(8,128)(2,1)S(1)} %get-tuple-element.40.first.refs_1_), channel_id=1, source_target_pairs={{8,4},{9,5},{24,20},{25,21}} | collective-permute-start | bytes 589832 | tf_op jit(solution)/shard_map/ppermute | solution.py:724
  61.0 10.7 %collective-permute-start.4 = (bf16[128,768]{1,0:T(8,128)(2,1)S(1)}, bf16[128,768]{1,0:T(8,128)(2,1)S(1)}, u32[]{:S(2)}, u32[]{:S(2)}) collective-permute-start(bf16[128,768]{1,0:T(8,128)(2,1)S(1)} %get-tuple-element.40.first.refs_1_), channel_id=1, source_target_pairs={{6,4},{7,5},{22,20},{23,21}} | collective-permute-start | bytes 589832 | tf_op jit(solution)/shard_map/ppermute | solution.py:724
  61.7 1.5 %copy-start.1 = (bf16[1152,768]{1,0:T(8,128)(2,1)S(1)}, bf16[1152,768]{1,0:T(8,128)(2,1)}, u32[]{:S(2)}) copy-start(bf16[1152,768]{1,0:T(8,128)(2,1)} %shard_map.42.mine) | copy-start | bytes 5308420
  63.2 3.8 %copy-start.2 = (bf16[1152,768]{1,0:T(8,128)(2,1)S(1)}, bf16[1152,768]{1,0:T(8,128)(2,1)}, u32[]{:S(2)}) copy-start(bf16[1152,768]{1,0:T(8,128)(2,1)} %shard_map.42.mine) | copy-start | bytes 5308420
  71.8 1.0 collective-permute-start.8
  72.8 26.5 %copy-start.6 = (bf16[1024,768]{1,0:T(8,128)(2,1)S(1)}, bf16[1024,768]{1,0:T(8,128)(2,1)}, u32[]{:S(2)}) copy-start(bf16[1024,768]{1,0:T(8,128)(2,1)} %x_hbm.1) | copy-start | bytes 4718596
  72.8 26.5 %copy-start.8 = (s32[1024]{0:T(1024)S(1)}, s32[1024]{0:T(1024)}, u32[]{:S(2)}) copy-start(s32[1024]{0:T(1024)} %param.6) | copy-start | bytes 12292
  72.8 26.5 %copy-start.10 = (s32[64]{0:T(128)S(1)}, s32[64]{0:T(128)}, u32[]{:S(2)}) copy-start(s32[64]{0:T(128)} %param.7) | copy-start | bytes 772
  73.5 25.8 %all-to-all-start.3 = ((f32[8,1,256]{2,1,0:T(1,128)}), f32[8,1,256]{2,1,0:T(1,128)S(1)}, u32[]{:S(2)}, u32[]{:S(2)}) async-start(f32[8,1,256]{2,1,0:T(1,128)} %shard_map.47), calls=%async_computation.3 | async-start | bytes 16384 | tf_op jit(solution)/shard_map/all_to_all | solution.py:759
  99.4 0.6 copy-start.9

commit v11 on v10

--- a/solution.py
+++ b/solution.py
@@ -345,56 +345,45 @@
 
 
 def after(rows, there):
-    anywhere = pl.BlockSpec(memory_space=pl.ANY)
     return pl.pallas_call(
         gate_kernel,
         out_shape=jax.ShapeDtypeStruct(rows.shape, rows.dtype),
-        in_specs=[anywhere] * 2,
-        out_specs=anywhere,
-        input_output_aliases={0: 0},
-    )(rows, there)
-
-
-def pair_up_kernel(first, second, out):
-    rows = first.shape[0]
-    out[:rows, :] = first[...]
-    out[rows:, :] = second[...]
-
-
-def pair_up(first, second):
-    rows, width = first.shape
-    return pl.pallas_call(
-        pair_up_kernel,
-        out_shape=jax.ShapeDtypeStruct((2 * rows, width), jnp.bfloat16),
         in_specs=list(vmem_specs(2)),
         out_specs=vmem_specs(1)[0],
+        input_output_aliases={0: 0},
         compiler_params=pltpu.CompilerParams(vmem_limit_bytes=FAST_LIMIT),
-    )(first, second)
-
-
-def gather_kernel(home, *refs):
-    chunks, out = refs[:-2], refs[-1]
-
-    @pl.when(lax.axis_index("cl") == home)
-    def _():
+    )(rows, there)
+
+
+def lay_out_kernel(n_arrays, home, *refs):
+    chunks, out = refs[:n_arrays], refs[-1]
+
+    def copy():
         start = 0
         for chunk in chunks:
             out[start : start + chunk.shape[0], :] = chunk[...]
             start += chunk.shape[0]
 
-
-def gather_rest(chunks, home, sums):
+    if home is None:
+        copy()
+    else:
+        pl.when(lax.axis_index("cl") == home)(copy)
+
+
+def lay_out(chunks, home=None, waits=()):
     rows, width = sum(x.shape[0] for x in chunks), chunks[0].shape[1]
     return pl.pallas_call(
-        functools.partial(gather_kernel, home),
+        functools.partial(lay_out_kernel, len(chunks), home),
         out_shape=jax.ShapeDtypeStruct((rows, width), jnp.bfloat16),
-        in_specs=list(vmem_specs(len(chunks) + 1)),
+        in_specs=list(vmem_specs(len(chunks) + len(waits))),
         out_specs=vmem_specs(1)[0],
         compiler_params=pltpu.CompilerParams(vmem_limit_bytes=FAST_LIMIT),
-    )(*chunks, sums)
+    )(*chunks, *waits)
 
 
 class Layout:
+    early, late = (0, 1, 2, 3), (4, 6, 5, 7)
+
     def __init__(self, n_owner, n_fine, capacity, main, home):
         self.n_owner, self.n_fine, self.capacity = n_owner, n_fine, capacity
         self.main, self.home = main, home
@@ -403,7 +392,10 @@
         self.per_owner = n_fine // n_owner
         self.n_main = n_owner * main
         self.n_head = n_owner * self.head
-        self.n_rest = n_owner * self.rest
+        self.n_early = len(self.early) * self.rest
+        self.n_late = len(self.late) * self.rest
+        self.n_first = self.n_head + self.n_early
+        self.n_all = self.n_first + self.n_late
 
 
 def info_line(lay, main_ref, source):
@@ -421,16 +413,16 @@
     return hot.astype(jnp.int32)
 
 
-def write_labels(lay, infos, first, count, at, lab_sub, bias):
+def write_labels(lay, infos, sources, first, count, at, lab_sub, bias):
     cluster = swapped(lax.axis_index("cl"), hot_of(lay, infos[0]), lay.home)
     lane = lax.broadcasted_iota(jnp.int32, (1, LANES), 1)
     is_edge = lax.div(lane, lay.per_owner) == cluster
-    for source, info in enumerate(infos):
-        edges = jnp.where(is_edge, info, 2.0 * lay.capacity)
+    for i, source in enumerate(sources):
+        edges = jnp.where(is_edge, infos[source], 2.0 * lay.capacity)
         slot = lax.broadcasted_iota(jnp.int32, (count, LANES), 0) + first
         label = jnp.where(slot.astype(jnp.float32) >= edges, 1.0, 0.0)
         label = jnp.broadcast_to(jnp.sum(label, axis=1, keepdims=True), (count, LANES))
-        start = at + source * count
+        start = at + i * count
         lab_sub[start : start + count, :] = label
         if bias is not None:
             bias[start : start + count, :] = jnp.where(
@@ -438,9 +430,18 @@
             )
 
 
-def turn_labels(lay, lab_sub, start, count, lab_lane, at):
+def first_labels(lay, infos, lab_sub):
+    write_labels(lay, infos, range(lay.n_owner), 0, lay.head, 0, lab_sub, None)
+    write_labels(lay, infos, lay.early, lay.head, lay.rest, lay.n_head, lab_sub, None)
+
+
+def late_labels(lay, infos, lab_sub):
+    write_labels(lay, infos, lay.late, lay.head, lay.rest, 0, lab_sub, None)
+
+
+def turn_labels(lay, lab_sub, count, lab_lane, at):
     for i in range(0, count, LANES):
-        block = jnp.transpose(lab_sub[start + i : start + i + LANES, :])[:1]
+        block = jnp.transpose(lab_sub[i : i + LANES, :])[:1]
         lab_lane[:, at + i : at + i + LANES] = jnp.where(block < lay.per_owner, block, -1.0)
 
 
@@ -451,22 +452,21 @@
         ]
 
 
-def pieces(start, count, parts):
-    return [(start + i * (count // parts), count // parts) for i in range(parts)]
-
-
-def stream(
-    rows_i, first, count, tiles, lab_lane, at, lab_sub, bias, buffers, put, wide=WIDE
-):
+def pieces(count, parts):
+    return [(i * (count // parts), count // parts) for i in range(parts)]
+
+
+def stream(lanes, tiles, lab_lane, buffers, put):
+    rows_i, count, at = lanes
     step = 32
     tiles = [
-        (ref, s, d, place + s - start)
-        for ref, start, n, place, parts in tiles
-        for s, d in pieces(start, n, parts)
+        (ref, s, d, lab_sub, bias, line + s)
+        for ref, n, lab_sub, bias, line, parts in tiles
+        for s, d in pieces(n, parts)
     ]
 
     def scores_to(buffer, tile, rows):
-        ref, start, deep, _ = tile
+        ref, start, deep = tile[:3]
         buffer[:deep, : rows.shape[0]] = lax.dot_general(
             ref[start : start + deep, :],
             rows,
@@ -478,7 +478,7 @@
         repeat = wide // LANES
 
         def rows_of(block):
-            return rows_i[pl.ds(pl.multiple_of(first + start + block * wide, LANES), wide), :]
+            return rows_i[pl.ds(pl.multiple_of(start + block * wide, LANES), wide), :]
 
         scores_to(buffers[0], tiles[0], rows_of(0))
 
@@ -487,7 +487,7 @@
             place = pl.ds(pl.multiple_of(at + start + block * wide, LANES), wide)
             label_i = lab_lane[:, place]
             acc = jnp.zeros((8, wide), jnp.float32)
-            for i, (_, _, deep, line) in enumerate(tiles):
+            for i, (_, _, deep, lab_sub, bias, line) in enumerate(tiles):
                 if i + 1 < len(tiles):
                     scores_to(buffers[(i + 1) % 2], tiles[i + 1], here)
                 else:
@@ -500,19 +500,18 @@
                         bias_j = NEIGHBOUR - SCALE
                     else:
                         bias_j = jnp.concatenate([bias[part, :]] * repeat, axis=1)
-                    scores = buffer[c : c + step, :wide]
                     shift = jnp.where(label_j == label_i, -SCALE, bias_j)
-                    terms = jnp.exp2(scores * SCALE + shift)
+                    terms = jnp.exp2(buffer[c : c + step, :wide] * SCALE + shift)
                     acc = acc + jnp.sum(terms.reshape(step // 8, 8, wide), axis=0)
             put(place, jnp.sum(acc, axis=0, keepdims=True))
             return carry
 
         lax.fori_loop(0, blocks, body, 0)
 
-    if count >= wide:
-        run(0, count // wide, wide)
-    if count % wide:
-        run(count - count % wide, 1, count % wide)
+    if count >= WIDE:
+        run(0, count // WIDE, WIDE)
+    if count % WIDE:
+        run(count - count % WIDE, 1, count % WIDE)
 
 
 def setter(ref):
@@ -529,27 +528,31 @@
     return put
 
 
-def inner_kernel(lay, mine, sums, lab_lane, lab_sub, bias, rows, buf_a, buf_b):
+def inner_kernel(lay, mine, early, sums, lab_lane, lab_sub, rows, bias, buf_a, buf_b):
     is_home = lax.axis_index("cl") == lay.home
     infos = lines_of(lay, mine)
-
-    def work(ref, count, per, bias):
-        write_labels(lay, infos, 0, per, 0, lab_sub, bias)
-        turn_labels(lay, lab_sub, 0, count, lab_lane, 0)
-        tiles = [(ref, 0, count, 0, 2)]
-        stream(ref, 0, count, tiles, lab_lane, 0, lab_sub, bias, (buf_a, buf_b), setter(sums))
+    buffers = (buf_a, buf_b)
 
     @pl.when(is_home)
     def _():
         copy_head(lay, mine, rows)
-        work(rows, lay.n_head, lay.head, None)
+        first_labels(lay, infos, lab_sub)
+        turn_labels(lay, lab_sub, lay.n_first, lab_lane, 0)
+        tiles = [(rows, lay.n_head, lab_sub, None, 0, 2)]
+        tiles += [(early, lay.n_early, lab_sub, None, lay.n_head, 2)]
+        stream((rows, lay.n_head, 0), tiles, lab_lane, buffers, setter(sums))
+        stream((early, lay.n_early, lay.n_head), tiles, lab_lane, buffers, setter(sums))
 
     @pl.when(jnp.logical_not(is_home))
     def _():
-        work(mine, lay.n_main, lay.main, bias)
-
-
-def cross_kernel(lay, mine, other, sums, lab_lane, total, unfit_ref, lab_sub, bias, rows, rows_j, buf_a, buf_b):
+        write_labels(lay, infos, range(lay.n_owner), 0, lay.main, 0, lab_sub, bias)
+        turn_labels(lay, lab_sub, lay.n_main, lab_lane, 0)
+        tiles = [(mine, lay.n_main, lab_sub, bias, 0, 2)]
+        stream((mine, lay.n_main, 0), tiles, lab_lane, buffers, setter(sums))
+
+
+def cross_kernel(lay, mine, other, early, early_j, rows, sums, lab_lane, *refs):
+    total, unfit_ref, lab_sub, rows_j, bias, buf_a, buf_b = refs
     is_home = lax.axis_index("cl") == lay.home
     infos = lines_of(lay, other)
     own = lines_of(lay, mine)
@@ -565,96 +568,91 @@
         unfit = unfit + jnp.where(wrong, 1.0, 0.0)
     unfit_ref[0, 0] = jnp.max(unfit).astype(jnp.int32)
     total[...] = sums[...]
-
-    def work(ref, ref_j, count, per, bias):
-        write_labels(lay, infos, 0, per, 0, lab_sub, bias)
-        tiles = [(ref_j, 0, count, 0, 2)]
-        stream(ref, 0, count, tiles, lab_lane, 0, lab_sub, bias, (buf_a, buf_b), adder(total))
+    buffers = (buf_a, buf_b)
 
     @pl.when(is_home)
     def _():
-        copy_head(lay, mine, rows)
         copy_head(lay, other, rows_j)
-        work(rows, rows_j, lay.n_head, lay.head, None)
+        first_labels(lay, infos, lab_sub)
+        tiles = [(rows_j, lay.n_head, lab_sub, None, 0, 2)]
+        tiles += [(early_j, lay.n_early, lab_sub, None, lay.n_head, 2)]
+        stream((rows, lay.n_head, 0), tiles, lab_lane, buffers, adder(total))
+        stream((early, lay.n_early, lay.n_head), tiles, lab_lane, buffers, adder(total))
 
     @pl.when(jnp.logical_not(is_home))
     def _():
-        work(mine, other, lay.n_main, lay.main, bias)
-
-
-def copy_all(lay, main_ref, rest, rows):
-    copy_head(lay, main_ref, rows)
-    rows[lay.n_head :, :] = rest[...]
-
-
-def rest_labels(lay, infos, lab_sub):
-    write_labels(lay, infos, 0, lay.head, 0, lab_sub, None)
-    write_labels(lay, infos, lay.head, lay.rest, lay.n_head, lab_sub, None)
-
-
-def rest_pairs(lay, rows, rows_j, lab_lane, lab_sub, buffers, put, wide):
-    n_head, n_rest = lay.n_head, lay.n_rest
-    seconds = (rows_j, n_head, n_rest, n_head, 2)
-    mains = (rows_j, 0, n_head, 0, 2)
-    stream(rows, 0, n_head, [seconds], lab_lane, 0, lab_sub, None, buffers, put, wide)
-    second_tiles = [seconds, mains]
-    stream(rows, n_head, n_rest, second_tiles, lab_lane, n_head, lab_sub, None, buffers, put, wide)
-
-
-def inner_rest_kernel(lay, mine, rest, sums, lab_lane, lab_sub, rows, buf_a, buf_b):
+        write_labels(lay, infos, range(lay.n_owner), 0, lay.main, 0, lab_sub, bias)
+        tiles = [(other, lay.n_main, lab_sub, bias, 0, 2)]
+        stream((mine, lay.n_main, 0), tiles, lab_lane, buffers, adder(total))
+
+
+def late_pairs(lay, i_refs, j_refs, lab_sub, late_sub, lab_lane, buffers, put):
+    rows, early, late = i_refs
+    rows_j, early_j, late_j = j_refs
+    lates = [(late_j, lay.n_late, late_sub, None, 0, 2)]
+    every = lates + [(rows_j, lay.n_head, lab_sub, None, 0, 2)]
+    every += [(early_j, lay.n_early, lab_sub, None, lay.n_head, 2)]
+    stream((rows, lay.n_head, 0), lates, lab_lane, buffers, put)
+    stream((early, lay.n_early, lay.n_head), lates, lab_lane, buffers, put)
+    stream((late, lay.n_late, lay.n_first), every, lab_lane, buffers, put)
+
+
+def inner_late_kernel(lay, mine, early, late, rows, lab_sub, first_lane, *refs):
+    sums, lab_lane, late_sub, buf_a, buf_b = refs
 
     @pl.when(lax.axis_index("cl") == lay.home)
     def _():
-        rest_labels(lay, lines_of(lay, mine), lab_sub)
-        turn_labels(lay, lab_sub, 0, lay.n_head + lay.n_rest, lab_lane, 0)
-        copy_all(lay, mine, rest, rows)
-        rest_pairs(lay, rows, rows, lab_lane, lab_sub, (buf_a, buf_b), setter(sums), WIDE)
-
-
-def cross_rest_kernel(lay, mine, other, rest, rest_other, *refs):
-    main_sums, main_lane, sums, lab_lane, out_ref, lab_sub, rows, rows_j, total, buf_a, buf_b = refs
+        late_labels(lay, lines_of(lay, mine), late_sub)
+        lab_lane[:, : lay.n_first] = first_lane[...]
+        turn_labels(lay, late_sub, lay.n_late, lab_lane, lay.n_first)
+        refs = (rows, early, late)
+        buffers = (buf_a, buf_b)
+        late_pairs(lay, refs, refs, lab_sub, late_sub, lab_lane, buffers, setter(sums))
+
+
+def cross_late_kernel(lay, other, early, late, early_j, late_j, rows, rows_j, *refs):
+    lab_sub, first_lane, first_sums, lab_lane, sums = refs[:5]
+    out_ref, total, late_sub, buf_a, buf_b = refs[5:]
     is_home = lax.axis_index("cl") == lay.home
 
     @pl.when(is_home)
     def _():
-        rest_labels(lay, lines_of(lay, other), lab_sub)
-        copy_all(lay, mine, rest, rows)
-        copy_all(lay, other, rest_other, rows_j)
+        late_labels(lay, lines_of(lay, other), late_sub)
         total[...] = sums[...]
-        total[:, : lay.n_head] += main_sums[:, : lay.n_head]
-        rest_pairs(lay, rows, rows_j, lab_lane, lab_sub, (buf_a, buf_b), adder(total), 2 * WIDE)
+        total[:, : lay.n_first] += first_sums[...]
+        i_refs, j_refs = (rows, early, late), (rows_j, early_j, late_j)
+        buffers = (buf_a, buf_b)
+        late_pairs(lay, i_refs, j_refs, lab_sub, late_sub, lab_lane, buffers, adder(total))
         values = jnp.log(total[...])
         for source in range(lay.n_owner):
             start = source * lay.head
             out_ref[source, :, : lay.head] = values[:, start : start + lay.head]
-            start = lay.n_head + source * lay.rest
+        for i, source in enumerate(lay.early + lay.late):
+            start = lay.n_head + i * lay.rest
             out_ref[source, :, lay.head :] = values[:, start : start + lay.rest]
 
     @pl.when(jnp.logical_not(is_home))
     def _():
-        values = jnp.log(jnp.where(main_lane[...] >= 0, main_sums[...], 1.0))
+        values = jnp.log(jnp.where(first_lane[...] >= 0, first_sums[...], 1.0))
         for source in range(lay.n_owner):
             start = source * lay.main
             out_ref[source, :, : lay.main] = values[:, start : start + lay.main]
 
 
-def pair_call(kernel, lay, arrays, out_shape, sides, joins, more=(), out_specs=None, pairs=0):
+def pair_call(kernel, lay, arrays, out_shape, scratch, out_specs=None, pairs=0):
     width = arrays[0].shape[1]
-    side = pltpu.VMEM((sides[0], LANES), jnp.float32)
-    rows = pltpu.VMEM((joins[0], width), jnp.bfloat16)
-    buffer = pltpu.VMEM((lay.n_main // 2, 2 * WIDE), jnp.float32)
-    out = pl.pallas_call(
+    buffer = pltpu.VMEM((lay.n_main // 2, WIDE), jnp.float32)
+    return pl.pallas_call(
         functools.partial(kernel, lay),
         out_shape=out_shape,
         in_specs=list(vmem_specs(len(arrays))),
         out_specs=out_specs or vmem_specs(len(out_shape)),
-        scratch_shapes=[side] * sides[1] + [rows] * joins[1] + list(more) + [buffer, buffer],
+        scratch_shapes=list(scratch) + [buffer, buffer],
         compiler_params=pltpu.CompilerParams(vmem_limit_bytes=FAST_LIMIT),
         cost_estimate=pl.CostEstimate(
             flops=2 * pairs * width, bytes_accessed=1, transcendentals=pairs
         ),
     )(*arrays)
-    return out
 
 
 def fast_unpack_kernel(values_ref, pos_ref, out_ref):
@@ -704,57 +702,71 @@
     rows, width = embeddings.shape
     n_fine = owner_map.shape[0]
     main = -(-(rows // n_owner * 9 // 8) // 16) * 16
-    if main >= capacity or n_fine >= LANES:
+    if n_owner != 8 or main >= capacity or n_fine >= LANES:
         return general(embeddings, labels, owner_map)
-    home = n_owner // 4
+    home = 2
     lay = Layout(n_owner, n_fine, capacity, main, home)
     unit, slot, info, extra, pos = place_rows(embeddings, labels, owner_map, lay)
     packed = pack_main(unit, slot, info, lay)
-    planes, plane = n_owner // 2, home // 2
-    turning = [z for z in range(planes) if z not in (plane, plane + 1)]
-    moved = lax.ppermute(extra, "cl", [(2 * z + 1, 2 * z) for z in turning])
-    both = pair_up(extra, moved)
-    chunks = []
-    for z in range(planes):
-        if z in turning:
-            chunks.append(lax.ppermute(both, "cl", [(2 * z, home)]))
-        else:
-            for source in (2 * z, 2 * z + 1):
-                chunks.append(
-                    extra if source == home else lax.ppermute(extra, "cl", [(source, home)])
-                )
+
+    def hop(x, pairs):
+        return lax.ppermute(x, "cl", pairs)
+
+    def swap(x):
+        pairs = [(2 * home, 2 * home + 1), (2 * home + 1, 2 * home)]
+        return lax.ppermute(x, ("cl", "grp"), pairs)
+
+    both = lay_out([extra, hop(extra, [(1, 0), (6, 4), (7, 5)])])
+    early = lay_out([hop(both, [(0, home)]), extra, hop(extra, [(3, home)])], home)
+    early_j = swap(early)
     mine = lax.all_to_all(
         packed.reshape(n_owner, main, width), "cl", split_axis=0, concat_axis=0, tiled=True
     ).reshape(n_owner * main, width)
-    mine = after(mine, both)
+    mine = after(mine, early_j)
     other = lax.ppermute(mine, "grp", [(0, 1), (1, 0)])
-    row = jax.ShapeDtypeStruct((1, lay.n_main), jnp.float32)
-    lines = lay.n_head + lay.n_rest
-    long_row = jax.ShapeDtypeStruct((1, lines), jnp.float32)
-    flag = jax.ShapeDtypeStruct((1, 1), jnp.int32)
-    table = jax.ShapeDtypeStruct((n_owner, 1, capacity), jnp.float32)
-    sides, joins = (lay.n_main, 2), (lay.n_head, 1)
-    sums, main_lane = pair_call(inner_kernel, lay, (mine,), (row, row), sides, joins)
-    joins = (lay.n_head, 2)
-    arrays = (mine, other, sums, main_lane)
-    specs = (pl.BlockSpec(memory_space=pltpu.VMEM), pl.BlockSpec(memory_space=pltpu.SMEM))
-    sums, unfit = pair_call(cross_kernel, lay, arrays, (row, flag), sides, joins, out_specs=specs)
-    rest = gather_rest(chunks, home, sums)
-    swap = [(2 * home, 2 * home + 1), (2 * home + 1, 2 * home)]
-    rest_other = lax.ppermute(rest, ("cl", "grp"), swap)
-    rest_sums, lane = pair_call(
-        inner_rest_kernel,
+    late = [hop(both, [(4, home)]), hop(both, [(5, home)])]
+
+    def array(shape, dtype=jnp.float32):
+        return jax.ShapeDtypeStruct(shape, dtype)
+
+    def scratch(shape):
+        return pltpu.VMEM(shape, jnp.float32)
+
+    row, long_row = array((1, lay.n_first)), array((1, lay.n_all))
+    side, bias = array((lay.n_first, LANES)), scratch((lay.n_main, LANES))
+    heads = array((lay.n_head, width), jnp.bfloat16)
+    late_side = scratch((lay.n_late, LANES))
+    sums, first_lane, lab_sub, heads_i = pair_call(
+        inner_kernel, lay, (mine, early), (row, row, side, heads), (bias,)
+    )
+    specs = vmem_specs(1) + (pl.BlockSpec(memory_space=pltpu.SMEM),) + vmem_specs(2)
+    sums, unfit, lab_sub_j, heads_j = pair_call(
+        cross_kernel,
         lay,
-        (mine, rest),
+        (mine, other, early, early_j, heads_i, sums, first_lane),
+        (row, array((1, 1), jnp.int32), side, heads),
+        (bias,),
+        specs,
+    )
+    late = lay_out(late, home, (sums,))
+    late_j = swap(late)
+    late_sums, lane = pair_call(
+        inner_late_kernel,
+        lay,
+        (mine, early, late, heads_i, lab_sub, first_lane),
         (long_row, long_row),
-        (lines, 1),
-        (lines, 1),
-        pairs=3 * lay.n_head * lay.n_rest,
-    )
-    arrays = (mine, other, rest, rest_other, sums, main_lane, rest_sums, lane)
-    total = pltpu.VMEM(long_row.shape, jnp.float32)
+        (late_side,),
+        pairs=lay.n_late * (lay.n_all + lay.n_first),
+    )
     (results,) = pair_call(
-        cross_rest_kernel, lay, arrays, (table,), (lines, 1), (lines, 2), (total,)
+        cross_late_kernel,
+        lay,
+        (
+            *(other, early, late, early_j, late_j, heads_i, heads_j),
+            *(lab_sub_j, first_lane, sums, lane, late_sums),
+        ),
+        (array((n_owner, 1, capacity)),),
+        (scratch(long_row.shape), late_side),
     )
     returned = lax.all_to_all(results, "cl", split_axis=0, concat_axis=0, tiled=True)
     return lax.cond(

time: 100 us -> 95.1 us (0.951)
  local copies, waits for them, and re-layouts: 5.05 us -> 1.6 us
  waiting for transfers between devices: 45 us -> 43 us
    all_to_all x1, waiting for transfers between devices: 22.4 us -> 2.52 us  [body(): lax.all_to_all(packed.reshape(n_owner, main, width), 'cl', split_axis=0,...]
    ppermute x7, waiting for transfers between devices: 16.7 us -> 34.6 us  [the longest x5 34.6 us: hop(): return lax.ppermute(x, 'cl', pairs)]
    unnamed x18 -> x12, local copies, waits for them, and re-layouts: 5.05 us -> 1.6 us
  transfers between devices with their start and end apart: 10 -> 10, of which waited for: 3 -> 4; matrix products, arithmetic and copies ran while one was open for 0% -> 0% of each run, Pallas kernels for 9% -> 9%
where the time goes in v11:
time: 95.1 us; the launch traced here: 94.7 us
  waiting for transfers between devices  43 us (45%)
  starting transfers between devices  33.5 us (35%)
  Pallas kernels  15.6 us (16%)
  local copies, waits for them, and re-layouts  1.6 us (2%)
    ppermute x5, waiting for transfers between devices, hop(): return lax.ppermute(x, 'cl', pairs)  34.6 us
    all_to_all x1, starting transfers between devices, body(): lax.all_to_all(results, 'cl', split_axis=0, concat_axis=0, tiled=True)  20.2 us
    pallas_call x4, Pallas kernels, pair_call(): pl.pallas_call(functools.partial(kernel, lay), out_shape=out_shape, in_sp...  9.4 us
    all_to_all x1, starting transfers between devices, body(): lax.all_to_all(packed.reshape(n_owner, main, width), 'cl', split_axis=0,...  7.28 us
    all_to_all x1, waiting for transfers between devices, body(): lax.all_to_all(results, 'cl', split_axis=0, concat_axis=0, tiled=True)  5.86 us
    ppermute x5, starting transfers between devices, hop(): return lax.ppermute(x, 'cl', pairs)  4.63 us
    pallas_call x1, Pallas kernels, pack_main(): pl.pallas_call(functools.partial(main_kernel, lay), out_shape=jax.ShapeDt...  3.26 us
    pallas_call x1, Pallas kernels, place_rows(): pl.pallas_call(functools.partial(place_kernel, lay), out_shape=(jax.Shape...  2.81 us
  transfers between devices with their start and end apart: 10, of which 4 were waited for; matrix products, arithmetic and copies ran while one was open for 0% of the time, Pallas kernels for 9%

profile of v11, /device:TPU:0, one launch (start us, length us, event | category | flops | bytes accessed | tf_op | source)
XLA Modules:
  0.0 94.7 jit_solution(14834456086595446251)
XLA Ops:
  0.0 2.8 %shard_map.39 = (bf16[1024,768]{1,0:T(8,128)(2,1)S(1)}, s32[1,1024]{1,0:T(1,128)S(1)}, f32[1,128]{1,0:T(1,128)S(1)}, bf16[128,768]{1,0:T(8,128)(2,1)S(1)}, s32[8,128]{1,0:T(8,128)S(1)}) custom-call(bf16[1024,768]{1,0:T(8,128)(2,1)} %x_hbm.1, s32[8,128]{1,0:T(8,128)} %bitcast.23, s32[1,64]{1,0:T(1,128)} %bitcast.27), custom_call_target="tpu_custom_call" | custom-call | tf_op jit(solution)/shard_map/pallas_call | solution.py:307
  2.8 3.3 %shard_map.40 = bf16[1152,768]{1,0:T(8,128)(2,1)} custom-call(bf16[1024,768]{1,0:T(8,128)(2,1)S(1)} %get-tuple-element.41.unit, s32[1,1024]{1,0:T(1,128)S(1)} %get-tuple-element.42.slot_ref, f32[1,128]{1,0:T(1,128)S(1)} %get-tuple-element.43.info_ref), custom_call_target="tpu_custom_call" | custom-call | flops 1811939328 | bytes 3145728 | tf_op jit(solution)/shard_map/pallas_call | solution.py:329
  6.1 7.3 %all-to-all-start.2 = ((bf16[8,144,768]{2,1,0:T(8,128)(2,1)}), bf16[8,144,768]{2,1,0:T(8,128)(2,1)S(1)}, u32[]{:S(2)}, u32[]{:S(2)}) async-start(bf16[8,144,768]{2,1,0:T(8,128)(2,1)} %bitcast.12), calls=%async_computation.2 | async-start | bytes 3538944 | tf_op jit(solution)/shard_map/all_to_all | solution.py:722
  13.4 1.3 %collective-permute-start.1 = (bf16[128,768]{1,0:T(8,128)(2,1)S(1)}, bf16[128,768]{1,0:T(8,128)(2,1)S(1)}, u32[]{:S(2)}, u32[]{:S(2)}) collective-permute-start(bf16[128,768]{1,0:T(8,128)(2,1)S(1)} %get-tuple-element.44.refs_0_.refs_1_), channel_id=1, source_target_pairs={{2,0},{12,8},{14,10},{3,1},{13,9},{15,11},{18,16},{28,24},{30,26},... | collective-permute-start | bytes 589832 | tf_op jit(solution)/shard_map/ppermute | solution.py:713
  14.7 16.7 %collective-permute-done.1.refs_1_ = bf16[128,768]{1,0:T(8,128)(2,1)S(1)} collective-permute-done((bf16[128,768]{1,0:T(8,128)(2,1)S(1)}, bf16[128,768]{1,0:T(8,128)(2,1)S(1)}, u32[]{:S(2)}, u32[]{:S(2)}) %collective-permute-start.1) | collective-permute-done | bytes 196640 | tf_op jit(solution)/shard_map/ppermute | solution.py:713
  31.4 0.0 copy-start
  31.4 1.3 %collective-permute-start.2 = (bf16[256,768]{1,0:T(8,128)(2,1)S(1)}, bf16[256,768]{1,0:T(8,128)(2,1)S(1)}, u32[]{:S(2)}, u32[]{:S(2)}) collective-permute-start(bf16[256,768]{1,0:T(8,128)(2,1)S(1)} %shard_map.41), channel_id=1, source_target_pairs={{0,4},{1,5},{16,20},{17,21}} | collective-permute-start | bytes 1179656 | tf_op jit(solution)/shard_map/ppermute | solution.py:713
  32.7 0.7 collective-permute-start.3
  33.4 0.0 collective-permute-done.3.refs_2_
  33.4 0.0 copy-done
  33.4 17.9 %collective-permute-done.2.refs_0_ = bf16[256,768]{1,0:T(8,128)(2,1)S(1)} collective-permute-done((bf16[256,768]{1,0:T(8,128)(2,1)S(1)}, bf16[256,768]{1,0:T(8,128)(2,1)S(1)}, u32[]{:S(2)}, u32[]{:S(2)}) %collective-permute-start.2) | collective-permute-done | bytes 393248 | tf_op jit(solution)/shard_map/ppermute | solution.py:713
  51.3 0.7 collective-permute-start.4
  52.0 0.0 collective-permute-done.4.refs_1_.early_j
  52.1 2.5 %all-to-all-done.2 = bf16[8,144,768]{2,1,0:T(8,128)(2,1)S(1)} async-done(((bf16[8,144,768]{2,1,0:T(8,128)(2,1)}), bf16[8,144,768]{2,1,0:T(8,128)(2,1)S(1)}, u32[]{:S(2)}, u32[]{:S(2)}) %all-to-all-start.2) | async-done | bytes 1769504 | tf_op jit(solution)/shard_map/all_to_all | solution.py:722
  54.6 0.0 copy-start.1
  54.6 0.0 collective-permute-start.5
  54.6 1.0 %copy-done.1 = bf16[256,768]{1,0:T(8,128)(2,1)S(1)} copy-done((bf16[256,768]{1,0:T(8,128)(2,1)S(1)}, bf16[256,768]{1,0:T(8,128)(2,1)}, u32[]{:S(2)}) %copy-start.1) | copy-done | bytes 393240
  55.6 0.7 collective-permute-start.7
  56.3 0.7 collective-permute-start.6
  56.9 3.9 %shard_map.44 = (f32[1,1536]{1,0:T(1,128)S(1)}, f32[1,1536]{1,0:T(1,128)S(1)}, f32[1536,128]{1,0:T(8,128)S(1)}, bf16[1024,768]{1,0:T(8,128)(2,1)S(1)}) custom-call(bf16[1152,768]{1,0:T(8,128)(2,1)S(1)} %shard_map.43.mine, bf16[512,768]{1,0:T(8,128)(2,1)S(1)} %shard_map.42.early), custom_call_target="tpu_custom_call" | custom-call | bytes 1 | tf_op jit(solution)/shard_map/pallas_call | solution.py:645
  60.9 0.0 collective-permute-done.5.other
  60.9 4.8 %shard_map.45 = (f32[1,1536]{1,0:T(1,128)S(1)}, s32[1,1]{1,0:T(1,128)}, f32[1536,128]{1,0:T(8,128)S(1)}, bf16[1024,768]{1,0:T(8,128)(2,1)S(1)}) custom-call(bf16[1152,768]{1,0:T(8,128)(2,1)S(1)} %shard_map.43.mine, bf16[1152,768]{1,0:T(8,128)(2,1)S(1)} %collective-permute-done.5.other, bf16[512,768]{1,0:T(8,128)(2,1)S(1)} %shard_map.42.early, ...), custom_call_target="tpu_custom_call" | custom-call | bytes 1 | tf_op jit(solution)/shard_map/pallas_call | solution.py:645
  65.7 0.0 collective-permute-done.7.refs_1_
  65.7 0.0 collective-permute-done.6.refs_0_
  65.7 0.7 collective-permute-start.8
  66.5 0.0 collective-permute-done.8.late_j
  66.5 0.0 copy-start.3
  66.5 0.0 copy-start.5
  66.5 0.0 copy-start.7
  66.5 0.7 shard_map.48
  67.2 20.2 %all-to-all-start.3 = ((f32[8,1,256]{2,1,0:T(1,128)}), f32[8,1,256]{2,1,0:T(1,128)S(1)}, u32[]{:S(2)}, u32[]{:S(2)}) async-start(f32[8,1,256]{2,1,0:T(1,128)} %shard_map.48), calls=%async_computation.3 | async-start | bytes 16384 | tf_op jit(solution)/shard_map/all_to_all | solution.py:771
  88.1 5.9 %all-to-all-done.3 = f32[8,1,256]{2,1,0:T(1,128)S(1)} async-done(((f32[8,1,256]{2,1,0:T(1,128)}), f32[8,1,256]{2,1,0:T(1,128)S(1)}, u32[]{:S(2)}, u32[]{:S(2)}) %all-to-all-start.3) | async-done | bytes 8224 | tf_op jit(solution)/shard_map/all_to_all | solution.py:771
  93.9 0.0 copy-done.3
  93.9 0.0 copy-done.5
  93.9 0.0 copy-done.7
  93.9 0.1 conditional.1
  94.0 0.1 branch_1_fun.1
  94.1 0.0 copy-start.6
  94.1 0.6 copy-done.6
  (5 shorter events, 0.1 us)
Async XLA Ops:
  6.1 48.5 %all-to-all-start.2 = ((bf16[8,144,768]{2,1,0:T(8,128)(2,1)}), bf16[8,144,768]{2,1,0:T(8,128)(2,1)S(1)}, u32[]{:S(2)}, u32[]{:S(2)}) async-start(bf16[8,144,768]{2,1,0:T(8,128)(2,1)} %bitcast.12), calls=%async_computation.2 | async-start | bytes 3538944 | tf_op jit(solution)/shard_map/all_to_all | solution.py:722
  13.4 18.0 %collective-permute-start.1 = (bf16[128,768]{1,0:T(8,128)(2,1)S(1)}, bf16[128,768]{1,0:T(8,128)(2,1)S(1)}, u32[]{:S(2)}, u32[]{:S(2)}) collective-permute-start(bf16[128,768]{1,0:T(8,128)(2,1)S(1)} %get-tuple-element.44.refs_0_.refs_1_), channel_id=1, source_target_pairs={{2,0},{12,8},{14,10},{3,1},{13,9},{15,11},{18,16},{28,24},{30,26},... | collective-permute-start | bytes 589832 | tf_op jit(solution)/shard_map/ppermute | solution.py:713
  31.4 2.0 %copy-start = (bf16[256,768]{1,0:T(8,128)(2,1)}, bf16[256,768]{1,0:T(8,128)(2,1)S(1)}, u32[]{:S(2)}) copy-start(bf16[256,768]{1,0:T(8,128)(2,1)S(1)} %shard_map.41) | copy-start | bytes 1179652
  31.4 19.9 %collective-permute-start.2 = (bf16[256,768]{1,0:T(8,128)(2,1)S(1)}, bf16[256,768]{1,0:T(8,128)(2,1)S(1)}, u32[]{:S(2)}, u32[]{:S(2)}) collective-permute-start(bf16[256,768]{1,0:T(8,128)(2,1)S(1)} %shard_map.41), channel_id=1, source_target_pairs={{0,4},{1,5},{16,20},{17,21}} | collective-permute-start | bytes 1179656 | tf_op jit(solution)/shard_map/ppermute | solution.py:713
  32.7 0.7 collective-permute-start.3
  51.3 0.7 collective-permute-start.4
  54.6 1.0 %copy-start.1 = (bf16[256,768]{1,0:T(8,128)(2,1)S(1)}, bf16[256,768]{1,0:T(8,128)(2,1)}, u32[]{:S(2)}) copy-start(bf16[256,768]{1,0:T(8,128)(2,1)} %copy-done) | copy-start | bytes 1179652
  54.6 6.3 %collective-permute-start.5 = (bf16[1152,768]{1,0:T(8,128)(2,1)S(1)}, bf16[1152,768]{1,0:T(8,128)(2,1)S(1)}, u32[]{:S(2)}, u32[]{:S(2)}) collective-permute-start(bf16[1152,768]{1,0:T(8,128)(2,1)S(1)} %shard_map.43.mine), channel_id=1, source_target_pairs={{0,1},{1,0},{2,3},{3,2},{4,5},{5,4},{6,7},{7,6},{8,9},{9,8},{10,11... | collective-permute-start | bytes 5308424 | tf_op jit(solution)/shard_map/ppermute | solution.py:726
  55.6 10.1 %collective-permute-start.7 = (bf16[256,768]{1,0:T(8,128)(2,1)S(1)}, bf16[256,768]{1,0:T(8,128)(2,1)S(1)}, u32[]{:S(2)}, u32[]{:S(2)}) collective-permute-start(bf16[256,768]{1,0:T(8,128)(2,1)S(1)} %copy-done.1), channel_id=1, source_target_pairs={{10,4},{11,5},{26,20},{27,21}} | collective-permute-start | bytes 1179656 | tf_op jit(solution)/shard_map/ppermute | solution.py:713
  56.3 9.4 %collective-permute-start.6 = (bf16[256,768]{1,0:T(8,128)(2,1)S(1)}, bf16[256,768]{1,0:T(8,128)(2,1)S(1)}, u32[]{:S(2)}, u32[]{:S(2)}) collective-permute-start(bf16[256,768]{1,0:T(8,128)(2,1)S(1)} %copy-done.1), channel_id=1, source_target_pairs={{8,4},{9,5},{24,20},{25,21}} | collective-permute-start | bytes 1179656 | tf_op jit(solution)/shard_map/ppermute | solution.py:713
  65.7 0.7 collective-permute-start.8
  66.5 27.5 %copy-start.3 = (bf16[1024,768]{1,0:T(8,128)(2,1)S(1)}, bf16[1024,768]{1,0:T(8,128)(2,1)}, u32[]{:S(2)}) copy-start(bf16[1024,768]{1,0:T(8,128)(2,1)} %x_hbm.1) | copy-start | bytes 4718596
  66.5 27.5 %copy-start.5 = (s32[1024]{0:T(1024)S(1)}, s32[1024]{0:T(1024)}, u32[]{:S(2)}) copy-start(s32[1024]{0:T(1024)} %param.6) | copy-start | bytes 12292
  66.5 27.5 %copy-start.7 = (s32[64]{0:T(128)S(1)}, s32[64]{0:T(128)}, u32[]{:S(2)}) copy-start(s32[64]{0:T(128)} %param.7) | copy-start | bytes 772
  67.2 26.7 %all-to-all-start.3 = ((f32[8,1,256]{2,1,0:T(1,128)}), f32[8,1,256]{2,1,0:T(1,128)S(1)}, u32[]{:S(2)}, u32[]{:S(2)}) async-start(f32[8,1,256]{2,1,0:T(1,128)} %shard_map.48), calls=%async_computation.3 | async-start | bytes 16384 | tf_op jit(solution)/shard_map/all_to_all | solution.py:771
  94.1 0.6 copy-start.6

commit v12 on v11

--- a/solution.py
+++ b/solution.py
@@ -19,7 +19,7 @@
 NEIGHBOUR = math.log2(neighbour_factor)
 DEAD = -1e30
 VMEM_LIMIT = 48 * 1024 * 1024
-FAST_LIMIT = 24 * 1024 * 1024
+FAST_LIMIT = 16 * 1024 * 1024
 WIDE = 512
 INFO = 16
 
@@ -219,15 +219,15 @@
 
 
 def place_kernel(lay, x_hbm, lab_hbm, map_hbm, *refs):
+    main_hbm, hot_ref, tail_ref, pos_ref, x_ref, lab_ref, map_ref, unit, main_ref, sems = refs
     n_owner, capacity, main, home = lay.n_owner, lay.capacity, lay.main, lay.home
-    unit, slot_ref, info_ref, extra_ref, pos_ref, x_ref, lab_ref, map_ref, sems = refs
     copies = [
         pltpu.make_async_copy(src, dst, sems.at[i])
         for i, (src, dst) in enumerate(((x_hbm, x_ref), (lab_hbm, lab_ref), (map_hbm, map_ref)))
     ]
     for copy in copies:
         copy.start()
-    rows = x_ref.shape[0]
+    rows, width = x_ref.shape
     n_fine = map_ref.shape[1]
     per_owner = n_fine // n_owner
     copies[1].wait()
@@ -254,7 +254,6 @@
     inside = (line <= lane) & (lax.div(line, per_owner) == lax.div(lane, per_owner))
     running = jnp.sum(jnp.where(inside, counts_col, 0.0), axis=0, keepdims=True)
     info = jnp.where(lane[:1] < n_fine, running, full)
-    info_ref[...] = info
     index = lax.broadcasted_iota(jnp.int32, (1, rows), 1).astype(jnp.float32)
     row_key = fine_id * rows + index
     rank = jnp.zeros((1, rows), jnp.float32)
@@ -267,33 +266,41 @@
     pos_ref[...] = jnp.concatenate(
         [table[:, start : start + LANES] for start in range(0, rows, LANES)], axis=0
     )
-    later = jnp.where(place == home, lay.n_main + rank - lay.head, -1)
     fits = rank < jnp.where(place == home, lay.head, main - 1)
-    slot = jnp.where(fits, place * main + rank, later)
-    slot_ref[...] = slot
+    slot = jnp.where(fits, place * main + rank, -1)
+    hot_slot = jnp.where(place == home, rank, -1)
     copies[0].wait()
     x = x_ref[...].astype(jnp.float32)
     squares = jnp.sum(x * x, axis=1, keepdims=True)
     unit[...] = (x * lax.rsqrt(squares + epsilon)).astype(jnp.bfloat16)
-    extra_ref[...] = chosen_rows(unit, slot, lay.n_main, lay.rest)
-
-
-def chosen_rows(unit, slot, start, count):
-    here = lax.broadcasted_iota(jnp.int32, (count, unit.shape[0]), 0) + start
-    chosen = jnp.where(here == slot, 1.0, 0.0).astype(jnp.bfloat16)
-    return jnp.dot(chosen, unit[...], preferred_element_type=jnp.float32).astype(jnp.bfloat16)
-
-
-def main_kernel(lay, unit, slot_ref, info_ref, main_ref):
-    count = lay.n_main // 4
-    for start in range(0, lay.n_main, count):
-        main_ref[start : start + count, :] = chosen_rows(unit, slot_ref[...], start, count)
-    for owner in range(lay.n_owner):
-        tail = slice((owner + 1) * lay.main - INFO, (owner + 1) * lay.main)
-        old = main_ref[tail, :LANES].astype(jnp.float32)
-        down = lax.broadcasted_iota(jnp.int32, old.shape, 0)
-        new = jnp.where(down == INFO - 1, info_ref[...], old)
-        main_ref[tail, :LANES] = new.astype(jnp.bfloat16)
+
+    def chosen_rows(slot, start, count):
+        here = lax.broadcasted_iota(jnp.int32, (count, rows), 0) + start
+        chosen = jnp.where(here == slot, 1.0, 0.0).astype(jnp.bfloat16)
+        return jnp.dot(chosen, unit[...], preferred_element_type=jnp.float32)
+
+    count = 2 * main
+    down = lax.broadcasted_iota(jnp.int32, (count, LANES), 0)
+    is_info = lax.rem(down, main) == main - 1
+    writes = []
+    for i, start in enumerate(range(0, lay.n_main, count)):
+        packed = chosen_rows(slot, start, count)
+        place = slice(start, start + count)
+        main_ref[place, LANES:] = packed[:, LANES:].astype(jnp.bfloat16)
+        main_ref[place, :LANES] = jnp.where(is_info, info, packed[:, :LANES]).astype(jnp.bfloat16)
+        writes.append(
+            pltpu.make_async_copy(
+                main_ref.at[pl.ds(start, count)], main_hbm.at[pl.ds(start, count)], sems.at[3 + i]
+            )
+        )
+        writes[-1].start()
+    hot = chosen_rows(hot_slot, 0, capacity).astype(jnp.bfloat16)
+    hot_ref[:capacity, :] = hot
+    hot_ref[capacity:, :] = jnp.zeros((INFO, width), jnp.bfloat16)
+    hot_ref[capacity:, :LANES] = jnp.broadcast_to(info, (INFO, LANES)).astype(jnp.bfloat16)
+    tail_ref[...] = hot[lay.head :, :]
+    for write in writes:
+        write.wait()
 
 
 def vmem_specs(count):
@@ -304,55 +311,64 @@
     rows, width = embeddings.shape
     n_fine = owner_map.shape[0]
     lab_shape = (rows // LANES, LANES)
+    anywhere = pl.BlockSpec(memory_space=pl.ANY)
     return pl.pallas_call(
         functools.partial(place_kernel, lay),
         out_shape=(
-            jax.ShapeDtypeStruct((rows, width), jnp.bfloat16),
-            jax.ShapeDtypeStruct((1, rows), jnp.int32),
-            jax.ShapeDtypeStruct((1, LANES), jnp.float32),
+            jax.ShapeDtypeStruct((lay.n_main, width), jnp.bfloat16),
+            jax.ShapeDtypeStruct((lay.capacity + INFO, width), jnp.bfloat16),
             jax.ShapeDtypeStruct((lay.rest, width), jnp.bfloat16),
             jax.ShapeDtypeStruct(lab_shape, jnp.int32),
         ),
-        in_specs=[pl.BlockSpec(memory_space=pl.ANY)] * 3,
-        out_specs=vmem_specs(5),
+        in_specs=[anywhere] * 3,
+        out_specs=(anywhere,) + vmem_specs(3),
         scratch_shapes=[
             pltpu.VMEM((rows, width), jnp.bfloat16),
             pltpu.VMEM(lab_shape, jnp.int32),
             pltpu.VMEM((1, n_fine), jnp.int32),
-            pltpu.SemaphoreType.DMA((3,)),
+            pltpu.VMEM((rows, width), jnp.bfloat16),
+            pltpu.VMEM((lay.n_main, width), jnp.bfloat16),
+            pltpu.SemaphoreType.DMA((3 + lay.n_owner // 2,)),
         ],
         compiler_params=pltpu.CompilerParams(vmem_limit_bytes=FAST_LIMIT),
     )(embeddings, labels.reshape(lab_shape), owner_map.reshape(1, n_fine))
 
 
-def pack_main(unit, slot, info, lay):
-    return pl.pallas_call(
-        functools.partial(main_kernel, lay),
-        out_shape=jax.ShapeDtypeStruct((lay.n_main, unit.shape[1]), jnp.bfloat16),
-        in_specs=list(vmem_specs(3)),
-        out_specs=vmem_specs(1)[0],
-        compiler_params=pltpu.CompilerParams(vmem_limit_bytes=FAST_LIMIT),
-        cost_estimate=pl.CostEstimate(
-            flops=2 * lay.n_main * unit.shape[0] * unit.shape[1],
-            bytes_accessed=4 * unit.shape[0] * unit.shape[1],
-            transcendentals=0,
-        ),
-    )(unit, slot, info)
-
-
 def gate_kernel(*refs):
     pass
 
 
-def after(rows, there):
+def after(rows, *there):
     return pl.pallas_call(
         gate_kernel,
         out_shape=jax.ShapeDtypeStruct(rows.shape, rows.dtype),
-        in_specs=list(vmem_specs(2)),
+        in_specs=list(vmem_specs(1 + len(there))),
         out_specs=vmem_specs(1)[0],
         input_output_aliases={0: 0},
         compiler_params=pltpu.CompilerParams(vmem_limit_bytes=FAST_LIMIT),
-    )(rows, there)
+    )(rows, *there)
+
+
+def lay_early_kernel(lay, *refs):
+    chunks, out = refs[:-1], refs[-1]
+
+    @pl.when(lax.axis_index("cl") == lay.home)
+    def _():
+        for i, chunk in enumerate(chunks):
+            out[i * lay.capacity : (i + 1) * lay.capacity, :] = chunk[: lay.capacity, :]
+            start = lay.n_early + i * INFO
+            out[start : start + INFO, :] = chunk[lay.capacity :, :]
+
+
+def lay_early(chunks, lay):
+    rows, width = sum(x.shape[0] for x in chunks), chunks[0].shape[1]
+    return pl.pallas_call(
+        functools.partial(lay_early_kernel, lay),
+        out_shape=jax.ShapeDtypeStruct((rows, width), jnp.bfloat16),
+        in_specs=list(vmem_specs(len(chunks))),
+        out_specs=vmem_specs(1)[0],
+        compiler_params=pltpu.CompilerParams(vmem_limit_bytes=FAST_LIMIT),
+    )(*chunks)
 
 
 def lay_out_kernel(n_arrays, home, *refs):
@@ -382,7 +398,7 @@
 
 
 class Layout:
-    early, late = (0, 1, 2, 3), (4, 6, 5, 7)
+    early, heads, late = (0, 1, 2, 3), (4, 5, 6, 7), (4, 6, 5, 7)
 
     def __init__(self, n_owner, n_fine, capacity, main, home):
         self.n_owner, self.n_fine, self.capacity = n_owner, n_fine, capacity
@@ -391,10 +407,10 @@
         self.rest = capacity - self.head
         self.per_owner = n_fine // n_owner
         self.n_main = n_owner * main
-        self.n_head = n_owner * self.head
-        self.n_early = len(self.early) * self.rest
+        self.n_early = len(self.early) * capacity
+        self.n_head = len(self.heads) * self.head
         self.n_late = len(self.late) * self.rest
-        self.n_first = self.n_head + self.n_early
+        self.n_first = self.n_early + self.n_head
         self.n_all = self.n_first + self.n_late
 
 
@@ -430,13 +446,12 @@
             )
 
 
-def first_labels(lay, infos, lab_sub):
-    write_labels(lay, infos, range(lay.n_owner), 0, lay.head, 0, lab_sub, None)
-    write_labels(lay, infos, lay.early, lay.head, lay.rest, lay.n_head, lab_sub, None)
-
-
-def late_labels(lay, infos, lab_sub):
-    write_labels(lay, infos, lay.late, lay.head, lay.rest, 0, lab_sub, None)
+def early_lines(lay, early):
+    starts = [lay.n_early + i * INFO for i in range(len(lay.early))]
+    return {
+        source: early[start : start + INFO, :LANES].astype(jnp.float32)[INFO - 1 :]
+        for source, start in zip(lay.early, starts)
+    }
 
 
 def turn_labels(lay, lab_sub, count, lab_lane, at):
@@ -446,8 +461,8 @@
 
 
 def copy_head(lay, main_ref, rows):
-    for source in range(lay.n_owner):
-        rows[source * lay.head : (source + 1) * lay.head, :] = main_ref[
+    for i, source in enumerate(lay.heads):
+        rows[i * lay.head : (i + 1) * lay.head, :] = main_ref[
             source * lay.main : source * lay.main + lay.head, :
         ]
 
@@ -528,7 +543,34 @@
     return put
 
 
-def inner_kernel(lay, mine, early, sums, lab_lane, lab_sub, rows, bias, buf_a, buf_b):
+def inner_early_kernel(lay, early, sums, lab_lane, lab_sub, buf_a, buf_b):
+    @pl.when(lax.axis_index("cl") == lay.home)
+    def _():
+        infos = early_lines(lay, early)
+        write_labels(lay, infos, lay.early, 0, lay.capacity, 0, lab_sub, None)
+        turn_labels(lay, lab_sub, lay.n_early, lab_lane, 0)
+        tiles = [(early, lay.n_early, lab_sub, None, 0, 2)]
+        stream((early, lay.n_early, 0), tiles, lab_lane, (buf_a, buf_b), setter(sums))
+
+
+def cross_early_kernel(lay, early, early_j, sums, lab_lane, total, lab_sub, buf_a, buf_b):
+    @pl.when(lax.axis_index("cl") == lay.home)
+    def _():
+        infos = early_lines(lay, early_j)
+        write_labels(lay, infos, lay.early, 0, lay.capacity, 0, lab_sub, None)
+        total[...] = sums[...]
+        tiles = [(early_j, lay.n_early, lab_sub, None, 0, 2)]
+        stream((early, lay.n_early, 0), tiles, lab_lane, (buf_a, buf_b), adder(total))
+
+
+def grown_pairs(old_i, new_i, old_j, new_j, lab_lane, buffers, put):
+    for lanes in old_i:
+        stream(lanes, [new_j], lab_lane, buffers, put)
+    stream(new_i, [new_j] + old_j, lab_lane, buffers, put)
+
+
+def inner_kernel(lay, mine, early, early_sums, early_lane, early_sub, *refs):
+    sums, lab_lane, lab_sub, rows, bias, buf_a, buf_b = refs
     is_home = lax.axis_index("cl") == lay.home
     infos = lines_of(lay, mine)
     buffers = (buf_a, buf_b)
@@ -536,12 +578,20 @@
     @pl.when(is_home)
     def _():
         copy_head(lay, mine, rows)
-        first_labels(lay, infos, lab_sub)
-        turn_labels(lay, lab_sub, lay.n_first, lab_lane, 0)
-        tiles = [(rows, lay.n_head, lab_sub, None, 0, 2)]
-        tiles += [(early, lay.n_early, lab_sub, None, lay.n_head, 2)]
-        stream((rows, lay.n_head, 0), tiles, lab_lane, buffers, setter(sums))
-        stream((early, lay.n_early, lay.n_head), tiles, lab_lane, buffers, setter(sums))
+        write_labels(lay, infos, lay.heads, 0, lay.head, 0, lab_sub, None)
+        lab_lane[:, : lay.n_early] = early_lane[...]
+        turn_labels(lay, lab_sub, lay.n_head, lab_lane, lay.n_early)
+        sums[:, : lay.n_early] = early_sums[...]
+        sums[:, lay.n_early :] = jnp.zeros((1, lay.n_head), jnp.float32)
+        grown_pairs(
+            [(early, lay.n_early, 0)],
+            (rows, lay.n_head, lay.n_early),
+            [(early, lay.n_early, early_sub, None, 0, 2)],
+            (rows, lay.n_head, lab_sub, None, 0, 2),
+            lab_lane,
+            buffers,
+            adder(sums),
+        )
 
     @pl.when(jnp.logical_not(is_home))
     def _():
@@ -551,7 +601,7 @@
         stream((mine, lay.n_main, 0), tiles, lab_lane, buffers, setter(sums))
 
 
-def cross_kernel(lay, mine, other, early, early_j, rows, sums, lab_lane, *refs):
+def cross_kernel(lay, mine, other, early, early_j, early_sub_j, rows, sums, lab_lane, *refs):
     total, unfit_ref, lab_sub, rows_j, bias, buf_a, buf_b = refs
     is_home = lax.axis_index("cl") == lay.home
     infos = lines_of(lay, other)
@@ -573,11 +623,16 @@
     @pl.when(is_home)
     def _():
         copy_head(lay, other, rows_j)
-        first_labels(lay, infos, lab_sub)
-        tiles = [(rows_j, lay.n_head, lab_sub, None, 0, 2)]
-        tiles += [(early_j, lay.n_early, lab_sub, None, lay.n_head, 2)]
-        stream((rows, lay.n_head, 0), tiles, lab_lane, buffers, adder(total))
-        stream((early, lay.n_early, lay.n_head), tiles, lab_lane, buffers, adder(total))
+        write_labels(lay, infos, lay.heads, 0, lay.head, 0, lab_sub, None)
+        grown_pairs(
+            [(early, lay.n_early, 0)],
+            (rows, lay.n_head, lay.n_early),
+            [(early_j, lay.n_early, early_sub_j, None, 0, 2)],
+            (rows_j, lay.n_head, lab_sub, None, 0, 2),
+            lab_lane,
+            buffers,
+            adder(total),
+        )
 
     @pl.when(jnp.logical_not(is_home))
     def _():
@@ -586,49 +641,60 @@
         stream((mine, lay.n_main, 0), tiles, lab_lane, buffers, adder(total))
 
 
-def late_pairs(lay, i_refs, j_refs, lab_sub, late_sub, lab_lane, buffers, put):
-    rows, early, late = i_refs
-    rows_j, early_j, late_j = j_refs
-    lates = [(late_j, lay.n_late, late_sub, None, 0, 2)]
-    every = lates + [(rows_j, lay.n_head, lab_sub, None, 0, 2)]
-    every += [(early_j, lay.n_early, lab_sub, None, lay.n_head, 2)]
-    stream((rows, lay.n_head, 0), lates, lab_lane, buffers, put)
-    stream((early, lay.n_early, lay.n_head), lates, lab_lane, buffers, put)
-    stream((late, lay.n_late, lay.n_first), every, lab_lane, buffers, put)
-
-
-def inner_late_kernel(lay, mine, early, late, rows, lab_sub, first_lane, *refs):
+def late_pairs(lay, i_refs, j_refs, subs, lab_lane, buffers, put):
+    early, rows, late = i_refs
+    early_j, rows_j, late_j = j_refs
+    early_sub, lab_sub, late_sub = subs
+    grown_pairs(
+        [(early, lay.n_early, 0), (rows, lay.n_head, lay.n_early)],
+        (late, lay.n_late, lay.n_first),
+        [
+            (early_j, lay.n_early, early_sub, None, 0, 2),
+            (rows_j, lay.n_head, lab_sub, None, 0, 2),
+        ],
+        (late_j, lay.n_late, late_sub, None, 0, 2),
+        lab_lane,
+        buffers,
+        put,
+    )
+
+
+def inner_late_kernel(lay, mine, early, late, rows, early_sub, lab_sub, first_lane, *refs):
     sums, lab_lane, late_sub, buf_a, buf_b = refs
 
     @pl.when(lax.axis_index("cl") == lay.home)
     def _():
-        late_labels(lay, lines_of(lay, mine), late_sub)
+        infos = lines_of(lay, mine)
+        write_labels(lay, infos, lay.late, lay.head, lay.rest, 0, late_sub, None)
         lab_lane[:, : lay.n_first] = first_lane[...]
         turn_labels(lay, late_sub, lay.n_late, lab_lane, lay.n_first)
-        refs = (rows, early, late)
-        buffers = (buf_a, buf_b)
-        late_pairs(lay, refs, refs, lab_sub, late_sub, lab_lane, buffers, setter(sums))
+        refs, subs = (early, rows, late), (early_sub, lab_sub, late_sub)
+        late_pairs(lay, refs, refs, subs, lab_lane, (buf_a, buf_b), setter(sums))
 
 
 def cross_late_kernel(lay, other, early, late, early_j, late_j, rows, rows_j, *refs):
-    lab_sub, first_lane, first_sums, lab_lane, sums = refs[:5]
-    out_ref, total, late_sub, buf_a, buf_b = refs[5:]
+    early_sub, lab_sub, first_lane, first_sums, lab_lane, sums = refs[:6]
+    out_ref, total, late_sub, buf_a, buf_b = refs[6:]
     is_home = lax.axis_index("cl") == lay.home
 
     @pl.when(is_home)
     def _():
-        late_labels(lay, lines_of(lay, other), late_sub)
+        infos = lines_of(lay, other)
+        write_labels(lay, infos, lay.late, lay.head, lay.rest, 0, late_sub, None)
         total[...] = sums[...]
         total[:, : lay.n_first] += first_sums[...]
-        i_refs, j_refs = (rows, early, late), (rows_j, early_j, late_j)
-        buffers = (buf_a, buf_b)
-        late_pairs(lay, i_refs, j_refs, lab_sub, late_sub, lab_lane, buffers, adder(total))
+        i_refs, j_refs = (early, rows, late), (early_j, rows_j, late_j)
+        subs = (early_sub, lab_sub, late_sub)
+        late_pairs(lay, i_refs, j_refs, subs, lab_lane, (buf_a, buf_b), adder(total))
         values = jnp.log(total[...])
-        for source in range(lay.n_owner):
-            start = source * lay.head
+        for i, source in enumerate(lay.early):
+            start = i * lay.capacity
+            out_ref[source, :, :] = values[:, start : start + lay.capacity]
+        for i, source in enumerate(lay.heads):
+            start = lay.n_early + i * lay.head
             out_ref[source, :, : lay.head] = values[:, start : start + lay.head]
-        for i, source in enumerate(lay.early + lay.late):
-            start = lay.n_head + i * lay.rest
+        for i, source in enumerate(lay.late):
+            start = lay.n_first + i * lay.rest
             out_ref[source, :, lay.head :] = values[:, start : start + lay.rest]
 
     @pl.when(jnp.logical_not(is_home))
@@ -706,8 +772,7 @@
         return general(embeddings, labels, owner_map)
     home = 2
     lay = Layout(n_owner, n_fine, capacity, main, home)
-    unit, slot, info, extra, pos = place_rows(embeddings, labels, owner_map, lay)
-    packed = pack_main(unit, slot, info, lay)
+    packed, hot, tail, pos = place_rows(embeddings, labels, owner_map, lay)
 
     def hop(x, pairs):
         return lax.ppermute(x, "cl", pairs)
@@ -716,34 +781,51 @@
         pairs = [(2 * home, 2 * home + 1), (2 * home + 1, 2 * home)]
         return lax.ppermute(x, ("cl", "grp"), pairs)
 
-    both = lay_out([extra, hop(extra, [(1, 0), (6, 4), (7, 5)])])
-    early = lay_out([hop(both, [(0, home)]), extra, hop(extra, [(3, home)])], home)
+    def array(shape, dtype=jnp.float32):
+        return jax.ShapeDtypeStruct(shape, dtype)
+
+    def scratch(shape):
+        return pltpu.VMEM(shape, jnp.float32)
+
+    both = lay_out([tail, hop(tail, [(6, 4), (7, 5)])])
+    early = [hot if s == home else hop(hot, [(s, home)]) for s in lay.early]
+    early = lay_early(early, lay)
     early_j = swap(early)
+    early_row, early_side = array((1, lay.n_early)), array((lay.n_early, LANES))
+    pairs = lay.n_early * lay.n_early
+    early_sums, early_lane, early_sub = pair_call(
+        inner_early_kernel, lay, (early,), (early_row, early_row, early_side), (), pairs=pairs
+    )
+    early_sums, early_sub_j = pair_call(
+        cross_early_kernel,
+        lay,
+        (early, early_j, early_sums, early_lane),
+        (early_row, early_side),
+        (),
+        pairs=pairs,
+    )
     mine = lax.all_to_all(
         packed.reshape(n_owner, main, width), "cl", split_axis=0, concat_axis=0, tiled=True
     ).reshape(n_owner * main, width)
-    mine = after(mine, early_j)
+    mine = after(mine, early_sums, both)
     other = lax.ppermute(mine, "grp", [(0, 1), (1, 0)])
     late = [hop(both, [(4, home)]), hop(both, [(5, home)])]
-
-    def array(shape, dtype=jnp.float32):
-        return jax.ShapeDtypeStruct(shape, dtype)
-
-    def scratch(shape):
-        return pltpu.VMEM(shape, jnp.float32)
-
     row, long_row = array((1, lay.n_first)), array((1, lay.n_all))
-    side, bias = array((lay.n_first, LANES)), scratch((lay.n_main, LANES))
+    side, bias = array((lay.n_main, LANES)), scratch((lay.n_main, LANES))
     heads = array((lay.n_head, width), jnp.bfloat16)
     late_side = scratch((lay.n_late, LANES))
     sums, first_lane, lab_sub, heads_i = pair_call(
-        inner_kernel, lay, (mine, early), (row, row, side, heads), (bias,)
+        inner_kernel,
+        lay,
+        (mine, early, early_sums, early_lane, early_sub),
+        (row, row, side, heads),
+        (bias,),
     )
     specs = vmem_specs(1) + (pl.BlockSpec(memory_space=pltpu.SMEM),) + vmem_specs(2)
     sums, unfit, lab_sub_j, heads_j = pair_call(
         cross_kernel,
         lay,
-        (mine, other, early, early_j, heads_i, sums, first_lane),
+        (mine, other, early, early_j, early_sub_j, heads_i, sums, first_lane),
         (row, array((1, 1), jnp.int32), side, heads),
         (bias,),
         specs,
@@ -753,7 +835,7 @@
     late_sums, lane = pair_call(
         inner_late_kernel,
         lay,
-        (mine, early, late, heads_i, lab_sub, first_lane),
+        (mine, early, late, heads_i, early_sub, lab_sub, first_lane),
         (long_row, long_row),
         (late_side,),
         pairs=lay.n_late * (lay.n_all + lay.n_first),
@@ -763,7 +845,7 @@
         lay,
         (
             *(other, early, late, early_j, late_j, heads_i, heads_j),
-            *(lab_sub_j, first_lane, sums, lane, late_sums),
+            *(early_sub_j, lab_sub_j, first_lane, sums, lane, late_sums),
         ),
         (array((n_owner, 1, capacity)),),
         (scratch(long_row.shape), late_side),

time: 95.1 us -> 107 us (1.13)
  starting transfers between devices: 33.5 us -> 45.5 us
  local copies, waits for them, and re-layouts: 1.6 us -> 7.69 us
  waiting for transfers between devices: 43 us -> 37.8 us
    all_to_all x1, starting transfers between devices: 20.2 us -> 28.1 us  [body(): lax.all_to_all(results, 'cl', split_axis=0, concat_axis=0, tiled=True)]
    unnamed x12 -> x32, local copies, waits for them, and re-layouts: 1.6 us -> 7.69 us
    ppermute x5 -> x6, starting transfers between devices: 4.63 us -> 8.69 us  [hop(): return lax.ppermute(x, 'cl', pairs)]
    pallas_call x1, Pallas kernels: 3.26 us -> 0.01 us  [lay_early(): pl.pallas_call(functools.partial(lay_early_kernel, lay), out_shape=jax.Sh...]
    ppermute x5 -> x6, waiting for transfers between devices: 34.6 us -> 31.9 us  [hop(): return lax.ppermute(x, 'cl', pairs)]
    all_to_all x1, waiting for transfers between devices: 2.52 us -> 0.01 us  [body(): lax.all_to_all(packed.reshape(n_owner, main, width), 'cl', split_axis=0,...]
    pallas_call x1, Pallas kernels: 2.81 us -> 5.27 us  [place_rows(): pl.pallas_call(functools.partial(place_kernel, lay), out_shape=(jax.Shape...]
    pallas_call x4 -> x6, Pallas kernels: 9.4 us -> 9.17 us  [pair_call(): pl.pallas_call(functools.partial(kernel, lay), out_shape=out_shape, in_sp...]
  transfers between devices with their start and end apart: 10 -> 11, of which waited for: 4 -> 2; matrix products, arithmetic and copies ran while one was open for 0% -> 0% of each run, Pallas kernels for 9% -> 8%
where the time goes in v12:
time: 107 us
  starting transfers between devices  45.5 us (43%)
  waiting for transfers between devices  37.8 us (35%)
  Pallas kernels  14.6 us (14%)
  local copies, waits for them, and re-layouts  7.69 us (7%)
    ppermute x6, waiting for transfers between devices, hop(): return lax.ppermute(x, 'cl', pairs)  31.9 us
    all_to_all x1, starting transfers between devices, body(): lax.all_to_all(results, 'cl', split_axis=0, concat_axis=0, tiled=True)  28.1 us
    pallas_call x6, Pallas kernels, pair_call(): pl.pallas_call(functools.partial(kernel, lay), out_shape=out_shape, in_sp...  9.17 us
    ppermute x6, starting transfers between devices, hop(): return lax.ppermute(x, 'cl', pairs)  8.69 us
    unnamed x32, local copies, waits for them, and re-layouts  7.69 us
    all_to_all x1, starting transfers between devices, body(): lax.all_to_all(packed.reshape(n_owner, main, width), 'cl', split_axis=0,...  7.28 us
    all_to_all x1, waiting for transfers between devices, body(): lax.all_to_all(results, 'cl', split_axis=0, concat_axis=0, tiled=True)  5.86 us
    pallas_call x1, Pallas kernels, place_rows(): pl.pallas_call(functools.partial(place_kernel, lay), out_shape=(jax.Shape...  5.27 us
  transfers between devices with their start and end apart: 11, of which 2 were waited for; matrix products, arithmetic and copies ran while one was open for 0% of the time, Pallas kernels for 8%

profile of v12, /device:TPU:0, one launch (start us, length us, event | category | flops | bytes accessed | tf_op | source)
XLA Modules:
  0.0 106.6 jit_solution(5950732281418958140)
XLA Ops:
  0.0 5.3 %shard_map.39 = (bf16[1152,768]{1,0:T(8,128)(2,1)}, bf16[272,768]{1,0:T(8,128)(2,1)S(1)}, bf16[128,768]{1,0:T(8,128)(2,1)S(1)}, s32[8,128]{1,0:T(8,128)S(1)}) custom-call(bf16[1024,768]{1,0:T(8,128)(2,1)} %x_hbm.1, s32[8,128]{1,0:T(8,128)} %bitcast.23, s32[1,64]{1,0:T(1,128)} %bitcast.27), custom_call_target="tpu_custom_call" | custom-call | tf_op jit(solution)/shard_map/pallas_call | solution.py:315
  5.3 0.0 copy-start.10
  5.3 0.7 copy-done.10
  6.0 0.0 copy-start.8
  6.0 7.3 %all-to-all-start.2 = ((bf16[8,144,768]{2,1,0:T(8,128)(2,1)}), bf16[8,144,768]{2,1,0:T(8,128)(2,1)S(1)}, u32[]{:S(2)}, u32[]{:S(2)}) async-start(bf16[8,144,768]{2,1,0:T(8,128)(2,1)} %bitcast.12), calls=%async_computation.2 | async-start | bytes 3538944 | tf_op jit(solution)/shard_map/all_to_all | solution.py:807
  13.2 0.7 collective-permute-start.3
  13.9 0.7 collective-permute-start.2
  14.6 0.0 copy-done.8
  14.6 5.2 %collective-permute-start.1 = (bf16[272,768]{1,0:T(8,128)(2,1)S(1)}, bf16[272,768]{1,0:T(8,128)(2,1)S(1)}, u32[]{:S(2)}, u32[]{:S(2)}) collective-permute-start(bf16[272,768]{1,0:T(8,128)(2,1)S(1)} %get-tuple-element.46.refs_2_), channel_id=1, source_target_pairs={{0,4},{1,5},{16,20},{17,21}} | collective-permute-start | bytes 1253384 | tf_op jit(solution)/shard_map/ppermute | solution.py:778
  19.8 0.0 collective-permute-done.3.refs_3_
  19.8 0.0 collective-permute-done.2.refs_1_
  19.8 31.9 %collective-permute-done.1.refs_0_ = bf16[272,768]{1,0:T(8,128)(2,1)S(1)} collective-permute-done((bf16[272,768]{1,0:T(8,128)(2,1)S(1)}, bf16[272,768]{1,0:T(8,128)(2,1)S(1)}, u32[]{:S(2)}, u32[]{:S(2)}) %collective-permute-start.1) | collective-permute-done | bytes 417824 | tf_op jit(solution)/shard_map/ppermute | solution.py:778
  51.8 0.0 copy-start.9
  51.8 1.0 copy-done.9
  52.8 0.8 collective-permute-start.4
  53.5 0.7 collective-permute-start.5
  54.2 0.0 collective-permute-done.5.refs_1_
  54.2 0.0 copy-start.11
  54.2 0.9 copy-done.11
  55.2 0.0 copy-start.4
  55.2 0.7 copy-done.4
  55.9 0.0 copy-start.6
  55.9 0.8 copy-done.6
  56.7 0.0 collective-permute-done.4.early_j
  56.7 0.0 copy-start
  56.7 1.2 %copy-done = bf16[1088,768]{1,0:T(8,128)(2,1)} copy-done((bf16[1088,768]{1,0:T(8,128)(2,1)}, bf16[1088,768]{1,0:T(8,128)(2,1)S(1)}, u32[]{:S(2)}) %copy-start) | copy-done | bytes 1671192
  57.9 0.0 copy-start.2
  57.9 0.8 copy-done.2
  58.7 0.0 all-to-all-done.2
  58.7 0.0 copy-start.5
  58.7 1.0 copy-done.5
  59.7 0.0 copy-start.7
  59.7 0.0 collective-permute-start.6
  59.7 0.8 collective-permute-start.8
  60.5 0.7 collective-permute-start.7
  61.2 0.0 copy-done.7
  61.2 0.0 copy-start.1
  61.2 0.0 copy-start.3
  61.2 3.8 %shard_map.45 = (f32[1,1536]{1,0:T(1,128)S(1)}, f32[1,1536]{1,0:T(1,128)S(1)}, f32[1152,128]{1,0:T(8,128)S(1)}, bf16[512,768]{1,0:T(8,128)(2,1)S(1)}) custom-call(bf16[1152,768]{1,0:T(8,128)(2,1)S(1)} %shard_map.44.mine, bf16[1088,768]{1,0:T(8,128)(2,1)S(1)} %shard_map.40.early, f32[1,1024]{1,0:T(1,128)S(1)} %get-tuple-element.49.refs_1_.early_sums, ...), custom_call_target="tpu_custom_call" | custom-call | bytes 1 | tf_op jit(solution)/shard_map/pallas_call | solution.py:711
  65.0 0.0 collective-permute-done.6.other
  65.1 0.0 copy-done.1
  65.1 0.0 copy-done.3
  65.1 4.6 %shard_map.46 = (f32[1,1536]{1,0:T(1,128)S(1)}, s32[1,1]{1,0:T(1,128)}, f32[1152,128]{1,0:T(8,128)S(1)}, bf16[512,768]{1,0:T(8,128)(2,1)S(1)}) custom-call(bf16[1152,768]{1,0:T(8,128)(2,1)S(1)} %shard_map.44.mine, bf16[1152,768]{1,0:T(8,128)(2,1)S(1)} %collective-permute-done.6.other, bf16[1088,768]{1,0:T(8,128)(2,1)S(1)} %shard_map.40.early, ...), custom_call_target="tpu_custom_call" | custom-call | bytes 1 | tf_op jit(solution)/shard_map/pallas_call | solution.py:711
  69.7 0.0 collective-permute-done.8.refs_1_
  69.7 0.0 collective-permute-done.7.refs_0_
  69.8 0.7 collective-permute-start.9
  70.5 0.0 collective-permute-done.9.late_j
  70.5 0.0 copy-start.13
  70.5 0.0 copy-start.15
  70.5 0.0 copy-start.17
  70.5 0.7 shard_map.49
  71.2 28.1 %all-to-all-start.3 = ((f32[8,1,256]{2,1,0:T(1,128)}), f32[8,1,256]{2,1,0:T(1,128)S(1)}, u32[]{:S(2)}, u32[]{:S(2)}) async-start(f32[8,1,256]{2,1,0:T(1,128)} %shard_map.49), calls=%async_computation.3 | async-start | bytes 16384 | tf_op jit(solution)/shard_map/all_to_all | solution.py:853
  100.0 5.9 %all-to-all-done.3 = f32[8,1,256]{2,1,0:T(1,128)S(1)} async-done(((f32[8,1,256]{2,1,0:T(1,128)}), f32[8,1,256]{2,1,0:T(1,128)S(1)}, u32[]{:S(2)}, u32[]{:S(2)}) %all-to-all-start.3) | async-done | bytes 8224 | tf_op jit(solution)/shard_map/all_to_all | solution.py:853
  105.8 0.0 copy-done.13
  105.8 0.0 copy-done.15
  105.8 0.0 copy-done.17
  105.8 0.1 conditional.1
  105.9 0.1 branch_1_fun.1
  106.0 0.0 copy-start.16
  106.0 0.6 copy-done.16
  (7 shorter events, 0.1 us)
Async XLA Ops:
  5.3 0.7 copy-start.10
  6.0 8.7 %copy-start.8 = (bf16[272,768]{1,0:T(8,128)(2,1)}, bf16[272,768]{1,0:T(8,128)(2,1)S(1)}, u32[]{:S(2)}) copy-start(bf16[272,768]{1,0:T(8,128)(2,1)S(1)} %get-tuple-element.46.refs_2_) | copy-start | bytes 1253380
  6.0 52.7 %all-to-all-start.2 = ((bf16[8,144,768]{2,1,0:T(8,128)(2,1)}), bf16[8,144,768]{2,1,0:T(8,128)(2,1)S(1)}, u32[]{:S(2)}, u32[]{:S(2)}) async-start(bf16[8,144,768]{2,1,0:T(8,128)(2,1)} %bitcast.12), calls=%async_computation.2 | async-start | bytes 3538944 | tf_op jit(solution)/shard_map/all_to_all | solution.py:807
  13.2 6.6 %collective-permute-start.3 = (bf16[272,768]{1,0:T(8,128)(2,1)S(1)}, bf16[272,768]{1,0:T(8,128)(2,1)S(1)}, u32[]{:S(2)}, u32[]{:S(2)}) collective-permute-start(bf16[272,768]{1,0:T(8,128)(2,1)S(1)} %get-tuple-element.46.refs_2_), channel_id=1, source_target_pairs={{6,4},{7,5},{22,20},{23,21}} | collective-permute-start | bytes 1253384 | tf_op jit(solution)/shard_map/ppermute | solution.py:778
  13.9 5.9 %collective-permute-start.2 = (bf16[272,768]{1,0:T(8,128)(2,1)S(1)}, bf16[272,768]{1,0:T(8,128)(2,1)S(1)}, u32[]{:S(2)}, u32[]{:S(2)}) collective-permute-start(bf16[272,768]{1,0:T(8,128)(2,1)S(1)} %get-tuple-element.46.refs_2_), channel_id=1, source_target_pairs={{2,4},{3,5},{18,20},{19,21}} | collective-permute-start | bytes 1253384 | tf_op jit(solution)/shard_map/ppermute | solution.py:778
  14.6 37.1 %collective-permute-start.1 = (bf16[272,768]{1,0:T(8,128)(2,1)S(1)}, bf16[272,768]{1,0:T(8,128)(2,1)S(1)}, u32[]{:S(2)}, u32[]{:S(2)}) collective-permute-start(bf16[272,768]{1,0:T(8,128)(2,1)S(1)} %get-tuple-element.46.refs_2_), channel_id=1, source_target_pairs={{0,4},{1,5},{16,20},{17,21}} | collective-permute-start | bytes 1253384 | tf_op jit(solution)/shard_map/ppermute | solution.py:778
  51.8 1.0 copy-start.9
  52.8 4.0 %collective-permute-start.4 = (bf16[1088,768]{1,0:T(8,128)(2,1)S(1)}, bf16[1088,768]{1,0:T(8,128)(2,1)S(1)}, u32[]{:S(2)}, u32[]{:S(2)}) collective-permute-start(bf16[1088,768]{1,0:T(8,128)(2,1)S(1)} %shard_map.40.early), channel_id=1, source_target_pairs={{4,5},{5,4},{20,21},{21,20}} | collective-permute-start | bytes 5013512 | tf_op jit(solution)/shard_map/ppermute | solution.py:782
  53.5 0.7 collective-permute-start.5
  54.2 0.9 copy-start.11
  55.2 0.8 copy-start.4
  55.9 0.8 copy-start.6
  56.7 1.2 %copy-start = (bf16[1088,768]{1,0:T(8,128)(2,1)}, bf16[1088,768]{1,0:T(8,128)(2,1)S(1)}, u32[]{:S(2)}) copy-start(bf16[1088,768]{1,0:T(8,128)(2,1)S(1)} %collective-permute-done.4.early_j) | copy-start | bytes 5013508
  57.9 0.8 copy-start.2
  58.7 1.0 copy-start.5
  59.7 1.5 %copy-start.7 = (f32[1024,128]{1,0:T(8,128)S(1)}, f32[1024,128]{1,0:T(8,128)}, u32[]{:S(2)}) copy-start(f32[1024,128]{1,0:T(8,128)} %copy-done.6) | copy-start | bytes 1572868
  59.7 5.4 %collective-permute-start.6 = (bf16[1152,768]{1,0:T(8,128)(2,1)S(1)}, bf16[1152,768]{1,0:T(8,128)(2,1)S(1)}, u32[]{:S(2)}, u32[]{:S(2)}) collective-permute-start(bf16[1152,768]{1,0:T(8,128)(2,1)S(1)} %shard_map.44.mine), channel_id=1, source_target_pairs={{0,1},{1,0},{2,3},{3,2},{4,5},{5,4},{6,7},{7,6},{8,9},{9,8},{10,11... | collective-permute-start | bytes 5308424 | tf_op jit(solution)/shard_map/ppermute | solution.py:811
  59.7 10.0 %collective-permute-start.8 = (bf16[256,768]{1,0:T(8,128)(2,1)S(1)}, bf16[256,768]{1,0:T(8,128)(2,1)S(1)}, u32[]{:S(2)}, u32[]{:S(2)}) collective-permute-start(bf16[256,768]{1,0:T(8,128)(2,1)S(1)} %copy-done.5), channel_id=1, source_target_pairs={{10,4},{11,5},{26,20},{27,21}} | collective-permute-start | bytes 1179656 | tf_op jit(solution)/shard_map/ppermute | solution.py:778
  60.5 9.2 %collective-permute-start.7 = (bf16[256,768]{1,0:T(8,128)(2,1)S(1)}, bf16[256,768]{1,0:T(8,128)(2,1)S(1)}, u32[]{:S(2)}, u32[]{:S(2)}) collective-permute-start(bf16[256,768]{1,0:T(8,128)(2,1)S(1)} %copy-done.5), channel_id=1, source_target_pairs={{8,4},{9,5},{24,20},{25,21}} | collective-permute-start | bytes 1179656 | tf_op jit(solution)/shard_map/ppermute | solution.py:778
  61.2 3.9 %copy-start.1 = (bf16[1088,768]{1,0:T(8,128)(2,1)S(1)}, bf16[1088,768]{1,0:T(8,128)(2,1)}, u32[]{:S(2)}) copy-start(bf16[1088,768]{1,0:T(8,128)(2,1)} %copy-done) | copy-start | bytes 5013508
  61.2 3.9 %copy-start.3 = (f32[1024,128]{1,0:T(8,128)S(1)}, f32[1024,128]{1,0:T(8,128)}, u32[]{:S(2)}) copy-start(f32[1024,128]{1,0:T(8,128)} %copy-done.2) | copy-start | bytes 1572868
  69.8 0.7 collective-permute-start.9
  70.5 35.3 %copy-start.13 = (bf16[1024,768]{1,0:T(8,128)(2,1)S(1)}, bf16[1024,768]{1,0:T(8,128)(2,1)}, u32[]{:S(2)}) copy-start(bf16[1024,768]{1,0:T(8,128)(2,1)} %x_hbm.1) | copy-start | bytes 4718596
  70.5 35.3 %copy-start.15 = (s32[1024]{0:T(1024)S(1)}, s32[1024]{0:T(1024)}, u32[]{:S(2)}) copy-start(s32[1024]{0:T(1024)} %param.6) | copy-start | bytes 12292
  70.5 35.3 %copy-start.17 = (s32[64]{0:T(128)S(1)}, s32[64]{0:T(128)}, u32[]{:S(2)}) copy-start(s32[64]{0:T(128)} %param.7) | copy-start | bytes 772
  71.2 34.6 %all-to-all-start.3 = ((f32[8,1,256]{2,1,0:T(1,128)}), f32[8,1,256]{2,1,0:T(1,128)S(1)}, u32[]{:S(2)}, u32[]{:S(2)}) async-start(f32[8,1,256]{2,1,0:T(1,128)} %shard_map.49), calls=%async_computation.3 | async-start | bytes 16384 | tf_op jit(solution)/shard_map/all_to_all | solution.py:853
  106.0 0.6 copy-start.16

commit v13 on v11

--- a/solution.py
+++ b/solution.py
@@ -19,7 +19,7 @@
 NEIGHBOUR = math.log2(neighbour_factor)
 DEAD = -1e30
 VMEM_LIMIT = 48 * 1024 * 1024
-FAST_LIMIT = 24 * 1024 * 1024
+FAST_LIMIT = 16 * 1024 * 1024
 WIDE = 512
 INFO = 16
 
@@ -219,15 +219,15 @@
 
 
 def place_kernel(lay, x_hbm, lab_hbm, map_hbm, *refs):
+    main_hbm, tail_ref, pos_ref, x_ref, lab_ref, map_ref, unit, main_ref, sems = refs
     n_owner, capacity, main, home = lay.n_owner, lay.capacity, lay.main, lay.home
-    unit, slot_ref, info_ref, extra_ref, pos_ref, x_ref, lab_ref, map_ref, sems = refs
     copies = [
         pltpu.make_async_copy(src, dst, sems.at[i])
         for i, (src, dst) in enumerate(((x_hbm, x_ref), (lab_hbm, lab_ref), (map_hbm, map_ref)))
     ]
     for copy in copies:
         copy.start()
-    rows = x_ref.shape[0]
+    rows, width = x_ref.shape
     n_fine = map_ref.shape[1]
     per_owner = n_fine // n_owner
     copies[1].wait()
@@ -254,7 +254,6 @@
     inside = (line <= lane) & (lax.div(line, per_owner) == lax.div(lane, per_owner))
     running = jnp.sum(jnp.where(inside, counts_col, 0.0), axis=0, keepdims=True)
     info = jnp.where(lane[:1] < n_fine, running, full)
-    info_ref[...] = info
     index = lax.broadcasted_iota(jnp.int32, (1, rows), 1).astype(jnp.float32)
     row_key = fine_id * rows + index
     rank = jnp.zeros((1, rows), jnp.float32)
@@ -267,33 +266,37 @@
     pos_ref[...] = jnp.concatenate(
         [table[:, start : start + LANES] for start in range(0, rows, LANES)], axis=0
     )
-    later = jnp.where(place == home, lay.n_main + rank - lay.head, -1)
     fits = rank < jnp.where(place == home, lay.head, main - 1)
-    slot = jnp.where(fits, place * main + rank, later)
-    slot_ref[...] = slot
+    slot = jnp.where(fits, place * main + rank, -1)
+    tail_slot = jnp.where(place == home, rank - lay.head, -1)
     copies[0].wait()
     x = x_ref[...].astype(jnp.float32)
     squares = jnp.sum(x * x, axis=1, keepdims=True)
     unit[...] = (x * lax.rsqrt(squares + epsilon)).astype(jnp.bfloat16)
-    extra_ref[...] = chosen_rows(unit, slot, lay.n_main, lay.rest)
-
-
-def chosen_rows(unit, slot, start, count):
-    here = lax.broadcasted_iota(jnp.int32, (count, unit.shape[0]), 0) + start
-    chosen = jnp.where(here == slot, 1.0, 0.0).astype(jnp.bfloat16)
-    return jnp.dot(chosen, unit[...], preferred_element_type=jnp.float32).astype(jnp.bfloat16)
-
-
-def main_kernel(lay, unit, slot_ref, info_ref, main_ref):
-    count = lay.n_main // 4
-    for start in range(0, lay.n_main, count):
-        main_ref[start : start + count, :] = chosen_rows(unit, slot_ref[...], start, count)
-    for owner in range(lay.n_owner):
-        tail = slice((owner + 1) * lay.main - INFO, (owner + 1) * lay.main)
-        old = main_ref[tail, :LANES].astype(jnp.float32)
-        down = lax.broadcasted_iota(jnp.int32, old.shape, 0)
-        new = jnp.where(down == INFO - 1, info_ref[...], old)
-        main_ref[tail, :LANES] = new.astype(jnp.bfloat16)
+
+    def chosen_rows(slot, start, count):
+        here = lax.broadcasted_iota(jnp.int32, (count, rows), 0) + start
+        chosen = jnp.where(here == slot, 1.0, 0.0).astype(jnp.bfloat16)
+        return jnp.dot(chosen, unit[...], preferred_element_type=jnp.float32)
+
+    count = 2 * main
+    down = lax.broadcasted_iota(jnp.int32, (count, LANES), 0)
+    is_info = lax.rem(down, main) == main - 1
+    writes = []
+    for i, start in enumerate(range(0, lay.n_main, count)):
+        packed = chosen_rows(slot, start, count)
+        place = slice(start, start + count)
+        main_ref[place, LANES:] = packed[:, LANES:].astype(jnp.bfloat16)
+        main_ref[place, :LANES] = jnp.where(is_info, info, packed[:, :LANES]).astype(jnp.bfloat16)
+        writes.append(
+            pltpu.make_async_copy(
+                main_ref.at[pl.ds(start, count)], main_hbm.at[pl.ds(start, count)], sems.at[3 + i]
+            )
+        )
+        writes[-1].start()
+    tail_ref[...] = chosen_rows(tail_slot, 0, lay.rest).astype(jnp.bfloat16)
+    for write in writes:
+        write.wait()
 
 
 def vmem_specs(count):
@@ -304,55 +307,41 @@
     rows, width = embeddings.shape
     n_fine = owner_map.shape[0]
     lab_shape = (rows // LANES, LANES)
+    anywhere = pl.BlockSpec(memory_space=pl.ANY)
     return pl.pallas_call(
         functools.partial(place_kernel, lay),
         out_shape=(
-            jax.ShapeDtypeStruct((rows, width), jnp.bfloat16),
-            jax.ShapeDtypeStruct((1, rows), jnp.int32),
-            jax.ShapeDtypeStruct((1, LANES), jnp.float32),
+            jax.ShapeDtypeStruct((lay.n_main, width), jnp.bfloat16),
             jax.ShapeDtypeStruct((lay.rest, width), jnp.bfloat16),
             jax.ShapeDtypeStruct(lab_shape, jnp.int32),
         ),
-        in_specs=[pl.BlockSpec(memory_space=pl.ANY)] * 3,
-        out_specs=vmem_specs(5),
+        in_specs=[anywhere] * 3,
+        out_specs=(anywhere,) + vmem_specs(2),
         scratch_shapes=[
             pltpu.VMEM((rows, width), jnp.bfloat16),
             pltpu.VMEM(lab_shape, jnp.int32),
             pltpu.VMEM((1, n_fine), jnp.int32),
-            pltpu.SemaphoreType.DMA((3,)),
+            pltpu.VMEM((rows, width), jnp.bfloat16),
+            pltpu.VMEM((lay.n_main, width), jnp.bfloat16),
+            pltpu.SemaphoreType.DMA((3 + lay.n_owner // 2,)),
         ],
         compiler_params=pltpu.CompilerParams(vmem_limit_bytes=FAST_LIMIT),
     )(embeddings, labels.reshape(lab_shape), owner_map.reshape(1, n_fine))
 
 
-def pack_main(unit, slot, info, lay):
-    return pl.pallas_call(
-        functools.partial(main_kernel, lay),
-        out_shape=jax.ShapeDtypeStruct((lay.n_main, unit.shape[1]), jnp.bfloat16),
-        in_specs=list(vmem_specs(3)),
-        out_specs=vmem_specs(1)[0],
-        compiler_params=pltpu.CompilerParams(vmem_limit_bytes=FAST_LIMIT),
-        cost_estimate=pl.CostEstimate(
-            flops=2 * lay.n_main * unit.shape[0] * unit.shape[1],
-            bytes_accessed=4 * unit.shape[0] * unit.shape[1],
-            transcendentals=0,
-        ),
-    )(unit, slot, info)
-
-
 def gate_kernel(*refs):
     pass
 
 
-def after(rows, there):
+def after(rows, *there):
     return pl.pallas_call(
         gate_kernel,
         out_shape=jax.ShapeDtypeStruct(rows.shape, rows.dtype),
-        in_specs=list(vmem_specs(2)),
+        in_specs=list(vmem_specs(1 + len(there))),
         out_specs=vmem_specs(1)[0],
         input_output_aliases={0: 0},
         compiler_params=pltpu.CompilerParams(vmem_limit_bytes=FAST_LIMIT),
-    )(rows, there)
+    )(rows, *there)
 
 
 def lay_out_kernel(n_arrays, home, *refs):
@@ -460,8 +449,8 @@
     rows_i, count, at = lanes
     step = 32
     tiles = [
-        (ref, s, d, lab_sub, bias, line + s)
-        for ref, n, lab_sub, bias, line, parts in tiles
+        (ref, s, d, lab_sub, bias, line + s, back)
+        for ref, n, lab_sub, bias, line, parts, back in tiles
         for s, d in pieces(n, parts)
     ]
 
@@ -487,7 +476,7 @@
             place = pl.ds(pl.multiple_of(at + start + block * wide, LANES), wide)
             label_i = lab_lane[:, place]
             acc = jnp.zeros((8, wide), jnp.float32)
-            for i, (_, _, deep, lab_sub, bias, line) in enumerate(tiles):
+            for i, (_, _, deep, lab_sub, bias, line, back) in enumerate(tiles):
                 if i + 1 < len(tiles):
                     scores_to(buffers[(i + 1) % 2], tiles[i + 1], here)
                 else:
@@ -503,6 +492,11 @@
                     shift = jnp.where(label_j == label_i, -SCALE, bias_j)
                     terms = jnp.exp2(buffer[c : c + step, :wide] * SCALE + shift)
                     acc = acc + jnp.sum(terms.reshape(step // 8, 8, wide), axis=0)
+                    if back is not None:
+                        across = terms[:, :LANES]
+                        for r in range(1, repeat):
+                            across = across + terms[:, r * LANES : (r + 1) * LANES]
+                        back[slice(line + c, line + c + step), :] += across
             put(place, jnp.sum(acc, axis=0, keepdims=True))
             return carry
 
@@ -514,6 +508,12 @@
         run(count - count % WIDE, 1, count % WIDE)
 
 
+def turn_sums(back, count, sums, at):
+    for i in range(0, count, LANES):
+        block = jnp.transpose(back[i : i + LANES, :])
+        sums[:, at + i : at + i + LANES] += jnp.sum(block, axis=0, keepdims=True)
+
+
 def setter(ref):
     def put(place, values):
         ref[:, place] = values
@@ -528,7 +528,7 @@
     return put
 
 
-def inner_kernel(lay, mine, early, sums, lab_lane, lab_sub, rows, bias, buf_a, buf_b):
+def inner_kernel(lay, mine, early, sums, lab_lane, lab_sub, rows, bias, back, buf_a, buf_b):
     is_home = lax.axis_index("cl") == lay.home
     infos = lines_of(lay, mine)
     buffers = (buf_a, buf_b)
@@ -538,16 +538,20 @@
         copy_head(lay, mine, rows)
         first_labels(lay, infos, lab_sub)
         turn_labels(lay, lab_sub, lay.n_first, lab_lane, 0)
-        tiles = [(rows, lay.n_head, lab_sub, None, 0, 2)]
-        tiles += [(early, lay.n_early, lab_sub, None, lay.n_head, 2)]
+        early_sub = lab_sub.at[pl.ds(lay.n_head, lay.n_early)]
+        back[...] = jnp.zeros(back.shape, jnp.float32)
+        tiles = [(rows, lay.n_head, lab_sub, None, 0, 2, None)]
+        tiles += [(early, lay.n_early, early_sub, None, 0, 2, back)]
         stream((rows, lay.n_head, 0), tiles, lab_lane, buffers, setter(sums))
+        tiles = [(early, lay.n_early, early_sub, None, 0, 2, None)]
         stream((early, lay.n_early, lay.n_head), tiles, lab_lane, buffers, setter(sums))
+        turn_sums(back, lay.n_early, sums, lay.n_head)
 
     @pl.when(jnp.logical_not(is_home))
     def _():
         write_labels(lay, infos, range(lay.n_owner), 0, lay.main, 0, lab_sub, bias)
         turn_labels(lay, lab_sub, lay.n_main, lab_lane, 0)
-        tiles = [(mine, lay.n_main, lab_sub, bias, 0, 2)]
+        tiles = [(mine, lay.n_main, lab_sub, bias, 0, 2, None)]
         stream((mine, lay.n_main, 0), tiles, lab_lane, buffers, setter(sums))
 
 
@@ -574,31 +578,33 @@
     def _():
         copy_head(lay, other, rows_j)
         first_labels(lay, infos, lab_sub)
-        tiles = [(rows_j, lay.n_head, lab_sub, None, 0, 2)]
-        tiles += [(early_j, lay.n_early, lab_sub, None, lay.n_head, 2)]
+        tiles = [(rows_j, lay.n_head, lab_sub, None, 0, 2, None)]
+        tiles += [(early_j, lay.n_early, lab_sub, None, lay.n_head, 2, None)]
         stream((rows, lay.n_head, 0), tiles, lab_lane, buffers, adder(total))
         stream((early, lay.n_early, lay.n_head), tiles, lab_lane, buffers, adder(total))
 
     @pl.when(jnp.logical_not(is_home))
     def _():
         write_labels(lay, infos, range(lay.n_owner), 0, lay.main, 0, lab_sub, bias)
-        tiles = [(other, lay.n_main, lab_sub, bias, 0, 2)]
+        tiles = [(other, lay.n_main, lab_sub, bias, 0, 2, None)]
         stream((mine, lay.n_main, 0), tiles, lab_lane, buffers, adder(total))
 
 
-def late_pairs(lay, i_refs, j_refs, lab_sub, late_sub, lab_lane, buffers, put):
+def late_pairs(lay, i_refs, j_refs, lab_sub, late_sub, lab_lane, buffers, put, back=None):
     rows, early, late = i_refs
     rows_j, early_j, late_j = j_refs
-    lates = [(late_j, lay.n_late, late_sub, None, 0, 2)]
-    every = lates + [(rows_j, lay.n_head, lab_sub, None, 0, 2)]
-    every += [(early_j, lay.n_early, lab_sub, None, lay.n_head, 2)]
+    lates = [(late_j, lay.n_late, late_sub, None, 0, 2, back)]
     stream((rows, lay.n_head, 0), lates, lab_lane, buffers, put)
     stream((early, lay.n_early, lay.n_head), lates, lab_lane, buffers, put)
+    every = [(late_j, lay.n_late, late_sub, None, 0, 2, None)]
+    if back is None:
+        every += [(rows_j, lay.n_head, lab_sub, None, 0, 2, None)]
+        every += [(early_j, lay.n_early, lab_sub, None, lay.n_head, 2, None)]
     stream((late, lay.n_late, lay.n_first), every, lab_lane, buffers, put)
 
 
 def inner_late_kernel(lay, mine, early, late, rows, lab_sub, first_lane, *refs):
-    sums, lab_lane, late_sub, buf_a, buf_b = refs
+    sums, lab_lane, late_sub, back, buf_a, buf_b = refs
 
     @pl.when(lax.axis_index("cl") == lay.home)
     def _():
@@ -607,7 +613,10 @@
         turn_labels(lay, late_sub, lay.n_late, lab_lane, lay.n_first)
         refs = (rows, early, late)
         buffers = (buf_a, buf_b)
-        late_pairs(lay, refs, refs, lab_sub, late_sub, lab_lane, buffers, setter(sums))
+        back[...] = jnp.zeros(back.shape, jnp.float32)
+        put = setter(sums)
+        late_pairs(lay, refs, refs, lab_sub, late_sub, lab_lane, buffers, put, back)
+        turn_sums(back, lay.n_late, sums, lay.n_first)
 
 
 def cross_late_kernel(lay, other, early, late, early_j, late_j, rows, rows_j, *refs):
@@ -706,8 +715,7 @@
         return general(embeddings, labels, owner_map)
     home = 2
     lay = Layout(n_owner, n_fine, capacity, main, home)
-    unit, slot, info, extra, pos = place_rows(embeddings, labels, owner_map, lay)
-    packed = pack_main(unit, slot, info, lay)
+    packed, extra, pos = place_rows(embeddings, labels, owner_map, lay)
 
     def hop(x, pairs):
         return lax.ppermute(x, "cl", pairs)
@@ -716,14 +724,15 @@
         pairs = [(2 * home, 2 * home + 1), (2 * home + 1, 2 * home)]
         return lax.ppermute(x, ("cl", "grp"), pairs)
 
-    both = lay_out([extra, hop(extra, [(1, 0), (6, 4), (7, 5)])])
-    early = lay_out([hop(both, [(0, home)]), extra, hop(extra, [(3, home)])], home)
-    early_j = swap(early)
+    both = lay_out([extra, hop(extra, [(6, 4), (7, 5)])])
+    early = [extra if s == home else hop(extra, [(s, home)]) for s in lay.early]
+    early = lay_out(early, home)
     mine = lax.all_to_all(
         packed.reshape(n_owner, main, width), "cl", split_axis=0, concat_axis=0, tiled=True
     ).reshape(n_owner * main, width)
-    mine = after(mine, early_j)
+    mine = after(mine, early, both)
     other = lax.ppermute(mine, "grp", [(0, 1), (1, 0)])
+    early_j = swap(early)
     late = [hop(both, [(4, home)]), hop(both, [(5, home)])]
 
     def array(shape, dtype=jnp.float32):
@@ -735,9 +744,9 @@
     row, long_row = array((1, lay.n_first)), array((1, lay.n_all))
     side, bias = array((lay.n_first, LANES)), scratch((lay.n_main, LANES))
     heads = array((lay.n_head, width), jnp.bfloat16)
-    late_side = scratch((lay.n_late, LANES))
+    late_side, early_side = scratch((lay.n_late, LANES)), scratch((lay.n_early, LANES))
     sums, first_lane, lab_sub, heads_i = pair_call(
-        inner_kernel, lay, (mine, early), (row, row, side, heads), (bias,)
+        inner_kernel, lay, (mine, early), (row, row, side, heads), (bias, early_side)
     )
     specs = vmem_specs(1) + (pl.BlockSpec(memory_space=pltpu.SMEM),) + vmem_specs(2)
     sums, unfit, lab_sub_j, heads_j = pair_call(
@@ -755,7 +764,7 @@
         lay,
         (mine, early, late, heads_i, lab_sub, first_lane),
         (long_row, long_row),
-        (late_side,),
+        (late_side, late_side),
         pairs=lay.n_late * (lay.n_all + lay.n_first),
     )
     (results,) = pair_call(

time: 95.1 us -> 89.3 us (0.939)
  waiting for transfers between devices: 43 us -> 39.8 us
  local copies, waits for them, and re-layouts: 1.6 us -> 0.61 us
    ppermute x5 -> x6, waiting for transfers between devices: 34.6 us -> 26.5 us  [hop(): return lax.ppermute(x, 'cl', pairs)]
    all_to_all x1, waiting for transfers between devices: 2.52 us -> 7.45 us  [body(): lax.all_to_all(packed.reshape(n_owner, main, width), 'cl', split_axis=0,...]
    all_to_all x1, starting transfers between devices: 20.2 us -> 15.6 us  [body(): lax.all_to_all(results, 'cl', split_axis=0, concat_axis=0, tiled=True)]
    ppermute x5 -> x6, starting transfers between devices: 4.63 us -> 8.55 us  [hop(): return lax.ppermute(x, 'cl', pairs)]
    pallas_call x1 -> x0, Pallas kernels: 3.26 us -> none  [pack_main(): pl.pallas_call(functools.partial(main_kernel, lay), out_shape=jax.ShapeDt...]
    pallas_call x1, Pallas kernels: 2.81 us -> 5.23 us  [place_rows(): pl.pallas_call(functools.partial(place_kernel, lay), out_shape=(jax.Shape...]
    unnamed x12 -> x8, local copies, waits for them, and re-layouts: 1.6 us -> 0.61 us
  transfers between devices with their start and end apart: 10 -> 11, of which waited for: 4 -> 3; matrix products, arithmetic and copies ran while one was open for 0% -> 0% of each run, Pallas kernels for 9% -> 10%
where the time goes in v13:
time: 89.3 us; the launch traced here: 89 us
  waiting for transfers between devices  39.8 us (45%)
  starting transfers between devices  32.9 us (37%)
  Pallas kernels  14.8 us (17%)
    ppermute x6, waiting for transfers between devices, hop(): return lax.ppermute(x, 'cl', pairs)  26.5 us
    all_to_all x1, starting transfers between devices, body(): lax.all_to_all(results, 'cl', split_axis=0, concat_axis=0, tiled=True)  15.6 us
    pallas_call x4, Pallas kernels, pair_call(): pl.pallas_call(functools.partial(kernel, lay), out_shape=out_shape, in_sp...  9.4 us
    ppermute x6, starting transfers between devices, hop(): return lax.ppermute(x, 'cl', pairs)  8.55 us
    all_to_all x1, waiting for transfers between devices, body(): lax.all_to_all(packed.reshape(n_owner, main, width), 'cl', split_axis=0,...  7.45 us
    all_to_all x1, starting transfers between devices, body(): lax.all_to_all(packed.reshape(n_owner, main, width), 'cl', split_axis=0,...  7.29 us
    all_to_all x1, waiting for transfers between devices, body(): lax.all_to_all(results, 'cl', split_axis=0, concat_axis=0, tiled=True)  5.86 us
    pallas_call x1, Pallas kernels, place_rows(): pl.pallas_call(functools.partial(place_kernel, lay), out_shape=(jax.Shape...  5.23 us
  transfers between devices with their start and end apart: 11, of which 3 were waited for; matrix products, arithmetic and copies ran while one was open for 0% of the time, Pallas kernels for 10%

profile of v13, /device:TPU:0, one launch (start us, length us, event | category | flops | bytes accessed | tf_op | source)
XLA Modules:
  0.0 89.0 jit_solution(7907136992686253637)
XLA Ops:
  0.0 5.2 %shard_map.39 = (bf16[1152,768]{1,0:T(8,128)(2,1)}, bf16[128,768]{1,0:T(8,128)(2,1)S(1)}, s32[8,128]{1,0:T(8,128)S(1)}) custom-call(bf16[1024,768]{1,0:T(8,128)(2,1)} %x_hbm.1, s32[8,128]{1,0:T(8,128)} %bitcast.23, s32[1,64]{1,0:T(1,128)} %bitcast.27), custom_call_target="tpu_custom_call" | custom-call | tf_op jit(solution)/shard_map/pallas_call | solution.py:311
  5.2 7.3 %all-to-all-start.2 = ((bf16[8,144,768]{2,1,0:T(8,128)(2,1)}), bf16[8,144,768]{2,1,0:T(8,128)(2,1)S(1)}, u32[]{:S(2)}, u32[]{:S(2)}) async-start(bf16[8,144,768]{2,1,0:T(8,128)(2,1)} %bitcast.12), calls=%async_computation.2 | async-start | bytes 3538944 | tf_op jit(solution)/shard_map/all_to_all | solution.py:730
  12.5 0.7 collective-permute-start.4
  13.2 0.7 collective-permute-start.3
  13.9 0.7 collective-permute-start.2
  14.6 5.2 %collective-permute-start.1 = (bf16[128,768]{1,0:T(8,128)(2,1)S(1)}, bf16[128,768]{1,0:T(8,128)(2,1)S(1)}, u32[]{:S(2)}, u32[]{:S(2)}) collective-permute-start(bf16[128,768]{1,0:T(8,128)(2,1)S(1)} %get-tuple-element.40.refs_2_.refs_0_), channel_id=1, source_target_pairs={{0,4},{1,5},{16,20},{17,21}} | collective-permute-start | bytes 589832 | tf_op jit(solution)/shard_map/ppermute | solution.py:721
  19.7 0.0 collective-permute-done.4.refs_1_
  19.8 0.0 collective-permute-done.3.refs_3_
  19.8 0.0 collective-permute-done.2.refs_1_
  19.8 26.5 %collective-permute-done.1.refs_0_ = bf16[128,768]{1,0:T(8,128)(2,1)S(1)} collective-permute-done((bf16[128,768]{1,0:T(8,128)(2,1)S(1)}, bf16[128,768]{1,0:T(8,128)(2,1)S(1)}, u32[]{:S(2)}, u32[]{:S(2)}) %collective-permute-start.1) | collective-permute-done | bytes 196640 | tf_op jit(solution)/shard_map/ppermute | solution.py:721
  46.3 7.4 %all-to-all-done.2 = bf16[8,144,768]{2,1,0:T(8,128)(2,1)S(1)} async-done(((bf16[8,144,768]{2,1,0:T(8,128)(2,1)}), bf16[8,144,768]{2,1,0:T(8,128)(2,1)S(1)}, u32[]{:S(2)}, u32[]{:S(2)}) %all-to-all-start.2) | async-done | bytes 1769504 | tf_op jit(solution)/shard_map/all_to_all | solution.py:730
  53.7 0.0 collective-permute-start.5
  53.8 0.7 collective-permute-start.6
  54.5 0.7 collective-permute-start.8
  55.2 0.7 collective-permute-start.7
  55.8 3.9 %shard_map.43 = (f32[1,1536]{1,0:T(1,128)S(1)}, f32[1,1536]{1,0:T(1,128)S(1)}, f32[1536,128]{1,0:T(8,128)S(1)}, bf16[1024,768]{1,0:T(8,128)(2,1)S(1)}) custom-call(bf16[1152,768]{1,0:T(8,128)(2,1)S(1)} %shard_map.42.mine, bf16[512,768]{1,0:T(8,128)(2,1)S(1)} %shard_map.40.refs_1_.early), custom_call_target="tpu_custom_call" | custom-call | bytes 1 | tf_op jit(solution)/shard_map/pallas_call | solution.py:654
  59.8 0.0 collective-permute-done.6.early_j
  59.8 0.0 collective-permute-done.5.other
  59.8 4.8 %shard_map.44 = (f32[1,1536]{1,0:T(1,128)S(1)}, s32[1,1]{1,0:T(1,128)}, f32[1536,128]{1,0:T(8,128)S(1)}, bf16[1024,768]{1,0:T(8,128)(2,1)S(1)}) custom-call(bf16[1152,768]{1,0:T(8,128)(2,1)S(1)} %shard_map.42.mine, bf16[1152,768]{1,0:T(8,128)(2,1)S(1)} %collective-permute-done.5.other, bf16[512,768]{1,0:T(8,128)(2,1)S(1)} %shard_map.40.refs_1_.early, ...), custom_call_target="tpu_custom_call" | custom-call | bytes 1 | tf_op jit(solution)/shard_map/pallas_call | solution.py:654
  64.6 0.0 collective-permute-done.8.refs_1_
  64.6 0.0 collective-permute-done.7.refs_0_
  64.6 0.7 collective-permute-start.9
  65.4 0.0 collective-permute-done.9.late_j
  65.4 0.0 copy-start.1
  65.4 0.0 copy-start.3
  65.4 0.0 copy-start.5
  65.4 0.7 shard_map.47
  66.1 15.6 %all-to-all-start.3 = ((f32[8,1,256]{2,1,0:T(1,128)}), f32[8,1,256]{2,1,0:T(1,128)S(1)}, u32[]{:S(2)}, u32[]{:S(2)}) async-start(f32[8,1,256]{2,1,0:T(1,128)} %shard_map.47), calls=%async_computation.3 | async-start | bytes 16384 | tf_op jit(solution)/shard_map/all_to_all | solution.py:780
  82.4 5.9 %all-to-all-done.3 = f32[8,1,256]{2,1,0:T(1,128)S(1)} async-done(((f32[8,1,256]{2,1,0:T(1,128)}), f32[8,1,256]{2,1,0:T(1,128)S(1)}, u32[]{:S(2)}, u32[]{:S(2)}) %all-to-all-start.3) | async-done | bytes 8224 | tf_op jit(solution)/shard_map/all_to_all | solution.py:780
  88.3 0.0 copy-done.1
  88.3 0.0 copy-done.3
  88.3 0.0 copy-done.5
  88.3 0.1 conditional.1
  88.3 0.1 branch_1_fun.1
  88.4 0.0 copy-start.4
  88.4 0.6 copy-done.4
  (5 shorter events, 0.1 us)
Async XLA Ops:
  5.2 48.5 %all-to-all-start.2 = ((bf16[8,144,768]{2,1,0:T(8,128)(2,1)}), bf16[8,144,768]{2,1,0:T(8,128)(2,1)S(1)}, u32[]{:S(2)}, u32[]{:S(2)}) async-start(bf16[8,144,768]{2,1,0:T(8,128)(2,1)} %bitcast.12), calls=%async_computation.2 | async-start | bytes 3538944 | tf_op jit(solution)/shard_map/all_to_all | solution.py:730
  12.5 7.2 %collective-permute-start.4 = (bf16[128,768]{1,0:T(8,128)(2,1)S(1)}, bf16[128,768]{1,0:T(8,128)(2,1)S(1)}, u32[]{:S(2)}, u32[]{:S(2)}) collective-permute-start(bf16[128,768]{1,0:T(8,128)(2,1)S(1)} %get-tuple-element.40.refs_2_.refs_0_), channel_id=1, source_target_pairs={{12,8},{14,10},{13,9},{15,11},{28,24},{30,26},{29,25},{31,27}} | collective-permute-start | bytes 589832 | tf_op jit(solution)/shard_map/ppermute | solution.py:721
  13.2 6.6 %collective-permute-start.3 = (bf16[128,768]{1,0:T(8,128)(2,1)S(1)}, bf16[128,768]{1,0:T(8,128)(2,1)S(1)}, u32[]{:S(2)}, u32[]{:S(2)}) collective-permute-start(bf16[128,768]{1,0:T(8,128)(2,1)S(1)} %get-tuple-element.40.refs_2_.refs_0_), channel_id=1, source_target_pairs={{6,4},{7,5},{22,20},{23,21}} | collective-permute-start | bytes 589832 | tf_op jit(solution)/shard_map/ppermute | solution.py:721
  13.9 5.9 %collective-permute-start.2 = (bf16[128,768]{1,0:T(8,128)(2,1)S(1)}, bf16[128,768]{1,0:T(8,128)(2,1)S(1)}, u32[]{:S(2)}, u32[]{:S(2)}) collective-permute-start(bf16[128,768]{1,0:T(8,128)(2,1)S(1)} %get-tuple-element.40.refs_2_.refs_0_), channel_id=1, source_target_pairs={{2,4},{3,5},{18,20},{19,21}} | collective-permute-start | bytes 589832 | tf_op jit(solution)/shard_map/ppermute | solution.py:721
  14.6 31.7 %collective-permute-start.1 = (bf16[128,768]{1,0:T(8,128)(2,1)S(1)}, bf16[128,768]{1,0:T(8,128)(2,1)S(1)}, u32[]{:S(2)}, u32[]{:S(2)}) collective-permute-start(bf16[128,768]{1,0:T(8,128)(2,1)S(1)} %get-tuple-element.40.refs_2_.refs_0_), channel_id=1, source_target_pairs={{0,4},{1,5},{16,20},{17,21}} | collective-permute-start | bytes 589832 | tf_op jit(solution)/shard_map/ppermute | solution.py:721
  53.7 6.0 %collective-permute-start.5 = (bf16[1152,768]{1,0:T(8,128)(2,1)S(1)}, bf16[1152,768]{1,0:T(8,128)(2,1)S(1)}, u32[]{:S(2)}, u32[]{:S(2)}) collective-permute-start(bf16[1152,768]{1,0:T(8,128)(2,1)S(1)} %shard_map.42.mine), channel_id=1, source_target_pairs={{0,1},{1,0},{2,3},{3,2},{4,5},{5,4},{6,7},{7,6},{8,9},{9,8},{10,11... | collective-permute-start | bytes 5308424 | tf_op jit(solution)/shard_map/ppermute | solution.py:734
  53.8 6.0 %collective-permute-start.6 = (bf16[512,768]{1,0:T(8,128)(2,1)S(1)}, bf16[512,768]{1,0:T(8,128)(2,1)S(1)}, u32[]{:S(2)}, u32[]{:S(2)}) collective-permute-start(bf16[512,768]{1,0:T(8,128)(2,1)S(1)} %shard_map.40.refs_1_.early), channel_id=1, source_target_pairs={{4,5},{5,4},{20,21},{21,20}} | collective-permute-start | bytes 2359304 | tf_op jit(solution)/shard_map/ppermute | solution.py:725
  54.5 10.1 %collective-permute-start.8 = (bf16[256,768]{1,0:T(8,128)(2,1)S(1)}, bf16[256,768]{1,0:T(8,128)(2,1)S(1)}, u32[]{:S(2)}, u32[]{:S(2)}) collective-permute-start(bf16[256,768]{1,0:T(8,128)(2,1)S(1)} %shard_map.41.refs_2_), channel_id=1, source_target_pairs={{10,4},{11,5},{26,20},{27,21}} | collective-permute-start | bytes 1179656 | tf_op jit(solution)/shard_map/ppermute | solution.py:721
  55.2 9.4 %collective-permute-start.7 = (bf16[256,768]{1,0:T(8,128)(2,1)S(1)}, bf16[256,768]{1,0:T(8,128)(2,1)S(1)}, u32[]{:S(2)}, u32[]{:S(2)}) collective-permute-start(bf16[256,768]{1,0:T(8,128)(2,1)S(1)} %shard_map.41.refs_2_), channel_id=1, source_target_pairs={{8,4},{9,5},{24,20},{25,21}} | collective-permute-start | bytes 1179656 | tf_op jit(solution)/shard_map/ppermute | solution.py:721
  64.6 0.7 collective-permute-start.9
  65.4 22.9 %copy-start.1 = (bf16[1024,768]{1,0:T(8,128)(2,1)S(1)}, bf16[1024,768]{1,0:T(8,128)(2,1)}, u32[]{:S(2)}) copy-start(bf16[1024,768]{1,0:T(8,128)(2,1)} %x_hbm.1) | copy-start | bytes 4718596
  65.4 22.9 %copy-start.3 = (s32[1024]{0:T(1024)S(1)}, s32[1024]{0:T(1024)}, u32[]{:S(2)}) copy-start(s32[1024]{0:T(1024)} %param.6) | copy-start | bytes 12292
  65.4 22.9 %copy-start.5 = (s32[64]{0:T(128)S(1)}, s32[64]{0:T(128)}, u32[]{:S(2)}) copy-start(s32[64]{0:T(128)} %param.7) | copy-start | bytes 772
  66.1 22.2 %all-to-all-start.3 = ((f32[8,1,256]{2,1,0:T(1,128)}), f32[8,1,256]{2,1,0:T(1,128)S(1)}, u32[]{:S(2)}, u32[]{:S(2)}) async-start(f32[8,1,256]{2,1,0:T(1,128)} %shard_map.47), calls=%async_computation.3 | async-start | bytes 16384 | tf_op jit(solution)/shard_map/all_to_all | solution.py:780
  88.4 0.6 copy-start.4

commit v14 on v13

--- a/solution.py
+++ b/solution.py
@@ -471,7 +471,7 @@
 
         scores_to(buffers[0], tiles[0], rows_of(0))
 
-        def body(block, carry):
+        def one_block(block):
             here = rows_of(block)
             place = pl.ds(pl.multiple_of(at + start + block * wide, LANES), wide)
             label_i = lab_lane[:, place]
@@ -479,8 +479,12 @@
             for i, (_, _, deep, lab_sub, bias, line, back) in enumerate(tiles):
                 if i + 1 < len(tiles):
                     scores_to(buffers[(i + 1) % 2], tiles[i + 1], here)
-                else:
-                    scores_to(buffers[0], tiles[0], rows_of(jnp.minimum(block + 1, blocks - 1)))
+                elif blocks > 1:
+
+                    @pl.when(block + 1 < blocks)
+                    def _():
+                        scores_to(buffers[0], tiles[0], rows_of(block + 1))
+
                 buffer = buffers[i % 2]
                 for c in range(0, deep, step):
                     part = slice(line + c, line + c + step)
@@ -496,11 +500,13 @@
                         across = terms[:, :LANES]
                         for r in range(1, repeat):
                             across = across + terms[:, r * LANES : (r + 1) * LANES]
-                        back[slice(line + c, line + c + step), :] += across
+                        back[part, :] += across
             put(place, jnp.sum(acc, axis=0, keepdims=True))
-            return carry
-
-        lax.fori_loop(0, blocks, body, 0)
+
+        if blocks == 1:
+            one_block(0)
+        else:
+            pl.loop(0, blocks)(one_block)
 
     if count >= WIDE:
         run(0, count // WIDE, WIDE)
@@ -538,14 +544,17 @@
         copy_head(lay, mine, rows)
         first_labels(lay, infos, lab_sub)
         turn_labels(lay, lab_sub, lay.n_first, lab_lane, 0)
-        early_sub = lab_sub.at[pl.ds(lay.n_head, lay.n_early)]
         back[...] = jnp.zeros(back.shape, jnp.float32)
-        tiles = [(rows, lay.n_head, lab_sub, None, 0, 2, None)]
-        tiles += [(early, lay.n_early, early_sub, None, 0, 2, back)]
-        stream((rows, lay.n_head, 0), tiles, lab_lane, buffers, setter(sums))
-        tiles = [(early, lay.n_early, early_sub, None, 0, 2, None)]
-        stream((early, lay.n_early, lay.n_head), tiles, lab_lane, buffers, setter(sums))
-        turn_sums(back, lay.n_early, sums, lay.n_head)
+        size = lay.n_early
+        blocks = [(rows.at[pl.ds(start, size)], start) for start in range(0, lay.n_head, size)]
+        blocks.append((early, lay.n_head))
+        for i, (ref, at) in enumerate(blocks):
+            tiles = [
+                (ref_j, size, lab_sub, None, at_j, 2, None if at_j == at else back)
+                for ref_j, at_j in blocks[i:]
+            ]
+            stream((ref, size, at), tiles, lab_lane, buffers, setter(sums))
+        turn_sums(back, lay.n_first, sums, 0)
 
     @pl.when(jnp.logical_not(is_home))
     def _():
@@ -744,9 +753,9 @@
     row, long_row = array((1, lay.n_first)), array((1, lay.n_all))
     side, bias = array((lay.n_first, LANES)), scratch((lay.n_main, LANES))
     heads = array((lay.n_head, width), jnp.bfloat16)
-    late_side, early_side = scratch((lay.n_late, LANES)), scratch((lay.n_early, LANES))
+    late_side, first_side = scratch((lay.n_late, LANES)), scratch((lay.n_first, LANES))
     sums, first_lane, lab_sub, heads_i = pair_call(
-        inner_kernel, lay, (mine, early), (row, row, side, heads), (bias, early_side)
+        inner_kernel, lay, (mine, early), (row, row, side, heads), (bias, first_side)
     )
     specs = vmem_specs(1) + (pl.BlockSpec(memory_space=pltpu.SMEM),) + vmem_specs(2)
     sums, unfit, lab_sub_j, heads_j = pair_call(

time: 89.3 us -> 89 us (level)
  no operation moved by 1% of the time
where the time goes in v14:
time: 89 us; the launch traced here: 88.6 us
  waiting for transfers between devices  39.8 us (45%)
  starting transfers between devices  32.3 us (36%)
  Pallas kernels  15 us (17%)
    ppermute x6, waiting for transfers between devices, hop(): return lax.ppermute(x, 'cl', pairs)  26.5 us
    all_to_all x1, starting transfers between devices, body(): lax.all_to_all(results, 'cl', split_axis=0, concat_axis=0, tiled=True)  15.1 us
    pallas_call x4, Pallas kernels, pair_call(): pl.pallas_call(functools.partial(kernel, lay), out_shape=out_shape, in_sp...  9.61 us
    ppermute x6, starting transfers between devices, hop(): return lax.ppermute(x, 'cl', pairs)  8.55 us
    all_to_all x1, waiting for transfers between devices, body(): lax.all_to_all(packed.reshape(n_owner, main, width), 'cl', split_axis=0,...  7.45 us
    all_to_all x1, starting transfers between devices, body(): lax.all_to_all(packed.reshape(n_owner, main, width), 'cl', split_axis=0,...  7.29 us
    all_to_all x1, waiting for transfers between devices, body(): lax.all_to_all(results, 'cl', split_axis=0, concat_axis=0, tiled=True)  5.86 us
    pallas_call x1, Pallas kernels, place_rows(): pl.pallas_call(functools.partial(place_kernel, lay), out_shape=(jax.Shape...  5.23 us
  transfers between devices with their start and end apart: 11, of which 3 were waited for; matrix products, arithmetic and copies ran while one was open for 0% of the time, Pallas kernels for 10%

profile of v14, /device:TPU:0, one launch (start us, length us, event | category | flops | bytes accessed | tf_op | source)
XLA Modules:
  0.0 88.6 jit_solution(9706555531934207938)
XLA Ops:
  0.0 5.2 %shard_map.39 = (bf16[1152,768]{1,0:T(8,128)(2,1)}, bf16[128,768]{1,0:T(8,128)(2,1)S(1)}, s32[8,128]{1,0:T(8,128)S(1)}) custom-call(bf16[1024,768]{1,0:T(8,128)(2,1)} %x_hbm.1, s32[8,128]{1,0:T(8,128)} %bitcast.23, s32[1,64]{1,0:T(1,128)} %bitcast.27), custom_call_target="tpu_custom_call" | custom-call | tf_op jit(solution)/shard_map/pallas_call | solution.py:311
  5.2 7.3 %all-to-all-start.2 = ((bf16[8,144,768]{2,1,0:T(8,128)(2,1)}), bf16[8,144,768]{2,1,0:T(8,128)(2,1)S(1)}, u32[]{:S(2)}, u32[]{:S(2)}) async-start(bf16[8,144,768]{2,1,0:T(8,128)(2,1)} %bitcast.12), calls=%async_computation.2 | async-start | bytes 3538944 | tf_op jit(solution)/shard_map/all_to_all | solution.py:739
  12.5 0.7 collective-permute-start.4
  13.2 0.7 collective-permute-start.3
  13.9 0.7 collective-permute-start.2
  14.6 5.2 %collective-permute-start.1 = (bf16[128,768]{1,0:T(8,128)(2,1)S(1)}, bf16[128,768]{1,0:T(8,128)(2,1)S(1)}, u32[]{:S(2)}, u32[]{:S(2)}) collective-permute-start(bf16[128,768]{1,0:T(8,128)(2,1)S(1)} %get-tuple-element.40.refs_2_.refs_0_), channel_id=1, source_target_pairs={{0,4},{1,5},{16,20},{17,21}} | collective-permute-start | bytes 589832 | tf_op jit(solution)/shard_map/ppermute | solution.py:730
  19.7 0.0 collective-permute-done.4.refs_1_
  19.8 0.0 collective-permute-done.3.refs_3_
  19.8 0.0 collective-permute-done.2.refs_1_
  19.8 26.5 %collective-permute-done.1.refs_0_ = bf16[128,768]{1,0:T(8,128)(2,1)S(1)} collective-permute-done((bf16[128,768]{1,0:T(8,128)(2,1)S(1)}, bf16[128,768]{1,0:T(8,128)(2,1)S(1)}, u32[]{:S(2)}, u32[]{:S(2)}) %collective-permute-start.1) | collective-permute-done | bytes 196640 | tf_op jit(solution)/shard_map/ppermute | solution.py:730
  46.3 7.4 %all-to-all-done.2 = bf16[8,144,768]{2,1,0:T(8,128)(2,1)S(1)} async-done(((bf16[8,144,768]{2,1,0:T(8,128)(2,1)}), bf16[8,144,768]{2,1,0:T(8,128)(2,1)S(1)}, u32[]{:S(2)}, u32[]{:S(2)}) %all-to-all-start.2) | async-done | bytes 1769504 | tf_op jit(solution)/shard_map/all_to_all | solution.py:739
  53.7 0.0 collective-permute-start.5
  53.8 0.7 collective-permute-start.6
  54.5 0.7 collective-permute-start.8
  55.2 0.7 collective-permute-start.7
  55.8 4.1 %shard_map.43 = (f32[1,1536]{1,0:T(1,128)S(1)}, f32[1,1536]{1,0:T(1,128)S(1)}, f32[1536,128]{1,0:T(8,128)S(1)}, bf16[1024,768]{1,0:T(8,128)(2,1)S(1)}) custom-call(bf16[1152,768]{1,0:T(8,128)(2,1)S(1)} %shard_map.42.mine, bf16[512,768]{1,0:T(8,128)(2,1)S(1)} %shard_map.40.refs_1_.early), custom_call_target="tpu_custom_call" | custom-call | bytes 1 | tf_op jit(solution)/shard_map/pallas_call | solution.py:663
  59.9 0.0 collective-permute-done.6.early_j
  59.9 0.0 collective-permute-done.5.other
  59.9 4.8 %shard_map.44 = (f32[1,1536]{1,0:T(1,128)S(1)}, s32[1,1]{1,0:T(1,128)}, f32[1536,128]{1,0:T(8,128)S(1)}, bf16[1024,768]{1,0:T(8,128)(2,1)S(1)}) custom-call(bf16[1152,768]{1,0:T(8,128)(2,1)S(1)} %shard_map.42.mine, bf16[1152,768]{1,0:T(8,128)(2,1)S(1)} %collective-permute-done.5.other, bf16[512,768]{1,0:T(8,128)(2,1)S(1)} %shard_map.40.refs_1_.early, ...), custom_call_target="tpu_custom_call" | custom-call | bytes 1 | tf_op jit(solution)/shard_map/pallas_call | solution.py:663
  64.8 0.0 collective-permute-done.8.refs_1_
  64.8 0.0 collective-permute-done.7.refs_0_
  64.8 0.7 collective-permute-start.9
  65.6 0.0 collective-permute-done.9.late_j
  65.6 0.0 copy-start.1
  65.6 0.0 copy-start.3
  65.6 0.0 copy-start.5
  65.6 0.7 shard_map.47
  66.3 15.1 %all-to-all-start.3 = ((f32[8,1,256]{2,1,0:T(1,128)}), f32[8,1,256]{2,1,0:T(1,128)S(1)}, u32[]{:S(2)}, u32[]{:S(2)}) async-start(f32[8,1,256]{2,1,0:T(1,128)} %shard_map.47), calls=%async_computation.3 | async-start | bytes 16384 | tf_op jit(solution)/shard_map/all_to_all | solution.py:789
  82.0 5.9 %all-to-all-done.3 = f32[8,1,256]{2,1,0:T(1,128)S(1)} async-done(((f32[8,1,256]{2,1,0:T(1,128)}), f32[8,1,256]{2,1,0:T(1,128)S(1)}, u32[]{:S(2)}, u32[]{:S(2)}) %all-to-all-start.3) | async-done | bytes 8224 | tf_op jit(solution)/shard_map/all_to_all | solution.py:789
  87.9 0.0 copy-done.1
  87.9 0.0 copy-done.3
  87.9 0.0 copy-done.5
  87.9 0.1 conditional.1
  87.9 0.1 branch_1_fun.1
  88.0 0.0 copy-start.4
  88.0 0.6 copy-done.4
  (5 shorter events, 0.1 us)
Async XLA Ops:
  5.2 48.5 %all-to-all-start.2 = ((bf16[8,144,768]{2,1,0:T(8,128)(2,1)}), bf16[8,144,768]{2,1,0:T(8,128)(2,1)S(1)}, u32[]{:S(2)}, u32[]{:S(2)}) async-start(bf16[8,144,768]{2,1,0:T(8,128)(2,1)} %bitcast.12), calls=%async_computation.2 | async-start | bytes 3538944 | tf_op jit(solution)/shard_map/all_to_all | solution.py:739
  12.5 7.2 %collective-permute-start.4 = (bf16[128,768]{1,0:T(8,128)(2,1)S(1)}, bf16[128,768]{1,0:T(8,128)(2,1)S(1)}, u32[]{:S(2)}, u32[]{:S(2)}) collective-permute-start(bf16[128,768]{1,0:T(8,128)(2,1)S(1)} %get-tuple-element.40.refs_2_.refs_0_), channel_id=1, source_target_pairs={{12,8},{14,10},{13,9},{15,11},{28,24},{30,26},{29,25},{31,27}} | collective-permute-start | bytes 589832 | tf_op jit(solution)/shard_map/ppermute | solution.py:730
  13.2 6.6 %collective-permute-start.3 = (bf16[128,768]{1,0:T(8,128)(2,1)S(1)}, bf16[128,768]{1,0:T(8,128)(2,1)S(1)}, u32[]{:S(2)}, u32[]{:S(2)}) collective-permute-start(bf16[128,768]{1,0:T(8,128)(2,1)S(1)} %get-tuple-element.40.refs_2_.refs_0_), channel_id=1, source_target_pairs={{6,4},{7,5},{22,20},{23,21}} | collective-permute-start | bytes 589832 | tf_op jit(solution)/shard_map/ppermute | solution.py:730
  13.9 5.9 %collective-permute-start.2 = (bf16[128,768]{1,0:T(8,128)(2,1)S(1)}, bf16[128,768]{1,0:T(8,128)(2,1)S(1)}, u32[]{:S(2)}, u32[]{:S(2)}) collective-permute-start(bf16[128,768]{1,0:T(8,128)(2,1)S(1)} %get-tuple-element.40.refs_2_.refs_0_), channel_id=1, source_target_pairs={{2,4},{3,5},{18,20},{19,21}} | collective-permute-start | bytes 589832 | tf_op jit(solution)/shard_map/ppermute | solution.py:730
  14.6 31.7 %collective-permute-start.1 = (bf16[128,768]{1,0:T(8,128)(2,1)S(1)}, bf16[128,768]{1,0:T(8,128)(2,1)S(1)}, u32[]{:S(2)}, u32[]{:S(2)}) collective-permute-start(bf16[128,768]{1,0:T(8,128)(2,1)S(1)} %get-tuple-element.40.refs_2_.refs_0_), channel_id=1, source_target_pairs={{0,4},{1,5},{16,20},{17,21}} | collective-permute-start | bytes 589832 | tf_op jit(solution)/shard_map/ppermute | solution.py:730
  53.7 6.2 %collective-permute-start.5 = (bf16[1152,768]{1,0:T(8,128)(2,1)S(1)}, bf16[1152,768]{1,0:T(8,128)(2,1)S(1)}, u32[]{:S(2)}, u32[]{:S(2)}) collective-permute-start(bf16[1152,768]{1,0:T(8,128)(2,1)S(1)} %shard_map.42.mine), channel_id=1, source_target_pairs={{0,1},{1,0},{2,3},{3,2},{4,5},{5,4},{6,7},{7,6},{8,9},{9,8},{10,11... | collective-permute-start | bytes 5308424 | tf_op jit(solution)/shard_map/ppermute | solution.py:743
  53.8 6.2 %collective-permute-start.6 = (bf16[512,768]{1,0:T(8,128)(2,1)S(1)}, bf16[512,768]{1,0:T(8,128)(2,1)S(1)}, u32[]{:S(2)}, u32[]{:S(2)}) collective-permute-start(bf16[512,768]{1,0:T(8,128)(2,1)S(1)} %shard_map.40.refs_1_.early), channel_id=1, source_target_pairs={{4,5},{5,4},{20,21},{21,20}} | collective-permute-start | bytes 2359304 | tf_op jit(solution)/shard_map/ppermute | solution.py:734
  54.5 10.3 %collective-permute-start.8 = (bf16[256,768]{1,0:T(8,128)(2,1)S(1)}, bf16[256,768]{1,0:T(8,128)(2,1)S(1)}, u32[]{:S(2)}, u32[]{:S(2)}) collective-permute-start(bf16[256,768]{1,0:T(8,128)(2,1)S(1)} %shard_map.41.refs_2_), channel_id=1, source_target_pairs={{10,4},{11,5},{26,20},{27,21}} | collective-permute-start | bytes 1179656 | tf_op jit(solution)/shard_map/ppermute | solution.py:730
  55.2 9.6 %collective-permute-start.7 = (bf16[256,768]{1,0:T(8,128)(2,1)S(1)}, bf16[256,768]{1,0:T(8,128)(2,1)S(1)}, u32[]{:S(2)}, u32[]{:S(2)}) collective-permute-start(bf16[256,768]{1,0:T(8,128)(2,1)S(1)} %shard_map.41.refs_2_), channel_id=1, source_target_pairs={{8,4},{9,5},{24,20},{25,21}} | collective-permute-start | bytes 1179656 | tf_op jit(solution)/shard_map/ppermute | solution.py:730
  64.8 0.7 collective-permute-start.9
  65.6 22.3 %copy-start.1 = (bf16[1024,768]{1,0:T(8,128)(2,1)S(1)}, bf16[1024,768]{1,0:T(8,128)(2,1)}, u32[]{:S(2)}) copy-start(bf16[1024,768]{1,0:T(8,128)(2,1)} %x_hbm.1) | copy-start | bytes 4718596
  65.6 22.3 %copy-start.3 = (s32[1024]{0:T(1024)S(1)}, s32[1024]{0:T(1024)}, u32[]{:S(2)}) copy-start(s32[1024]{0:T(1024)} %param.6) | copy-start | bytes 12292
  65.6 22.3 %copy-start.5 = (s32[64]{0:T(128)S(1)}, s32[64]{0:T(128)}, u32[]{:S(2)}) copy-start(s32[64]{0:T(128)} %param.7) | copy-start | bytes 772
  66.3 21.6 %all-to-all-start.3 = ((f32[8,1,256]{2,1,0:T(1,128)}), f32[8,1,256]{2,1,0:T(1,128)S(1)}, u32[]{:S(2)}, u32[]{:S(2)}) async-start(f32[8,1,256]{2,1,0:T(1,128)} %shard_map.47), calls=%async_computation.3 | async-start | bytes 16384 | tf_op jit(solution)/shard_map/all_to_all | solution.py:789
  88.0 0.6 copy-start.4

commit v15 on v14

--- a/solution.py
+++ b/solution.py
@@ -730,8 +730,7 @@
         return lax.ppermute(x, "cl", pairs)
 
     def swap(x):
-        pairs = [(2 * home, 2 * home + 1), (2 * home + 1, 2 * home)]
-        return lax.ppermute(x, ("cl", "grp"), pairs)
+        return lax.ppermute(x, "grp", [(0, 1), (1, 0)])
 
     both = lay_out([extra, hop(extra, [(6, 4), (7, 5)])])
     early = [extra if s == home else hop(extra, [(s, home)]) for s in lay.early]
@@ -740,8 +739,7 @@
         packed.reshape(n_owner, main, width), "cl", split_axis=0, concat_axis=0, tiled=True
     ).reshape(n_owner * main, width)
     mine = after(mine, early, both)
-    other = lax.ppermute(mine, "grp", [(0, 1), (1, 0)])
-    early_j = swap(early)
+    other, early_j = swap(mine), swap(early)
     late = [hop(both, [(4, home)]), hop(both, [(5, home)])]
 
     def array(shape, dtype=jnp.float32):

time: 89 us -> 85.2 us (0.957)
  starting transfers between devices: 32.3 us -> 26.4 us
  waiting for transfers between devices: 39.8 us -> 42.1 us
    all_to_all x1, starting transfers between devices: 15.1 us -> 9.97 us  [body(): lax.all_to_all(results, 'cl', split_axis=0, concat_axis=0, tiled=True)]
    ppermute x3, waiting for transfers between devices: 0.01 us -> 2.25 us  [swap(): return lax.ppermute(x, 'grp', [(0, 1), (1, 0)])]
  transfers between devices with their start and end apart: 11 -> 11, of which waited for: 3 -> 4; matrix products, arithmetic and copies ran while one was open for 0% -> 0% of each run, Pallas kernels for 10% -> 11%
where the time goes in v15:
time: 85.2 us; the launch traced here: 84.8 us
  waiting for transfers between devices  42.1 us (49%)
  starting transfers between devices  26.4 us (31%)
  Pallas kernels  14.9 us (17%)
    ppermute x6, waiting for transfers between devices, hop(): return lax.ppermute(x, 'cl', pairs)  26.5 us
    all_to_all x1, starting transfers between devices, body(): lax.all_to_all(results, 'cl', split_axis=0, concat_axis=0, tiled=True)  9.97 us
    pallas_call x4, Pallas kernels, pair_call(): pl.pallas_call(functools.partial(kernel, lay), out_shape=out_shape, in_sp...  9.58 us
    ppermute x6, starting transfers between devices, hop(): return lax.ppermute(x, 'cl', pairs)  8.54 us
    all_to_all x1, waiting for transfers between devices, body(): lax.all_to_all(packed.reshape(n_owner, main, width), 'cl', split_axis=0,...  7.45 us
    all_to_all x1, starting transfers between devices, body(): lax.all_to_all(packed.reshape(n_owner, main, width), 'cl', split_axis=0,...  7.29 us
    all_to_all x1, waiting for transfers between devices, body(): lax.all_to_all(results, 'cl', split_axis=0, concat_axis=0, tiled=True)  5.86 us
    pallas_call x1, Pallas kernels, place_rows(): pl.pallas_call(functools.partial(place_kernel, lay), out_shape=(jax.Shape...  5.23 us
  transfers between devices with their start and end apart: 11, of which 4 were waited for; matrix products, arithmetic and copies ran while one was open for 0% of the time, Pallas kernels for 11%

profile of v15, /device:TPU:0, one launch (start us, length us, event | category | flops | bytes accessed | tf_op | source)
XLA Modules:
  0.0 84.8 jit_solution(15916791801588902542)
XLA Ops:
  0.0 5.2 %shard_map.39 = (bf16[1152,768]{1,0:T(8,128)(2,1)}, bf16[128,768]{1,0:T(8,128)(2,1)S(1)}, s32[8,128]{1,0:T(8,128)S(1)}) custom-call(bf16[1024,768]{1,0:T(8,128)(2,1)} %x_hbm.1, s32[8,128]{1,0:T(8,128)} %bitcast.23, s32[1,64]{1,0:T(1,128)} %bitcast.27), custom_call_target="tpu_custom_call" | custom-call | tf_op jit(solution)/shard_map/pallas_call | solution.py:311
  5.2 7.3 %all-to-all-start.2 = ((bf16[8,144,768]{2,1,0:T(8,128)(2,1)}), bf16[8,144,768]{2,1,0:T(8,128)(2,1)S(1)}, u32[]{:S(2)}, u32[]{:S(2)}) async-start(bf16[8,144,768]{2,1,0:T(8,128)(2,1)} %bitcast.12), calls=%async_computation.2 | async-start | bytes 3538944 | tf_op jit(solution)/shard_map/all_to_all | solution.py:738
  12.5 0.7 collective-permute-start.4
  13.2 0.7 collective-permute-start.3
  13.9 0.7 collective-permute-start.2
  14.6 5.2 %collective-permute-start.1 = (bf16[128,768]{1,0:T(8,128)(2,1)S(1)}, bf16[128,768]{1,0:T(8,128)(2,1)S(1)}, u32[]{:S(2)}, u32[]{:S(2)}) collective-permute-start(bf16[128,768]{1,0:T(8,128)(2,1)S(1)} %get-tuple-element.40.refs_2_.refs_0_), channel_id=1, source_target_pairs={{0,4},{1,5},{16,20},{17,21}} | collective-permute-start | bytes 589832 | tf_op jit(solution)/shard_map/ppermute | solution.py:730
  19.7 0.0 collective-permute-done.4.refs_1_
  19.8 0.0 collective-permute-done.3.refs_3_
  19.8 0.0 collective-permute-done.2.refs_1_
  19.8 26.5 %collective-permute-done.1.refs_0_ = bf16[128,768]{1,0:T(8,128)(2,1)S(1)} collective-permute-done((bf16[128,768]{1,0:T(8,128)(2,1)S(1)}, bf16[128,768]{1,0:T(8,128)(2,1)S(1)}, u32[]{:S(2)}, u32[]{:S(2)}) %collective-permute-start.1) | collective-permute-done | bytes 196640 | tf_op jit(solution)/shard_map/ppermute | solution.py:730
  46.3 7.4 %all-to-all-done.2 = bf16[8,144,768]{2,1,0:T(8,128)(2,1)S(1)} async-done(((bf16[8,144,768]{2,1,0:T(8,128)(2,1)}), bf16[8,144,768]{2,1,0:T(8,128)(2,1)S(1)}, u32[]{:S(2)}, u32[]{:S(2)}) %all-to-all-start.2) | async-done | bytes 1769504 | tf_op jit(solution)/shard_map/all_to_all | solution.py:738
  53.7 0.0 collective-permute-start.5
  53.8 0.5 collective-permute-start.6
  54.3 0.7 collective-permute-start.8
  54.9 0.7 collective-permute-start.7
  55.6 4.0 %shard_map.43 = (f32[1,1536]{1,0:T(1,128)S(1)}, f32[1,1536]{1,0:T(1,128)S(1)}, f32[1536,128]{1,0:T(8,128)S(1)}, bf16[1024,768]{1,0:T(8,128)(2,1)S(1)}) custom-call(bf16[1152,768]{1,0:T(8,128)(2,1)S(1)} %shard_map.42.mine, bf16[512,768]{1,0:T(8,128)(2,1)S(1)} %shard_map.40.refs_1_.early), custom_call_target="tpu_custom_call" | custom-call | bytes 1 | tf_op jit(solution)/shard_map/pallas_call | solution.py:663
  59.7 0.0 collective-permute-done.6.early_j
  59.7 0.0 collective-permute-done.5.other
  59.7 4.8 %shard_map.44 = (f32[1,1536]{1,0:T(1,128)S(1)}, s32[1,1]{1,0:T(1,128)}, f32[1536,128]{1,0:T(8,128)S(1)}, bf16[1024,768]{1,0:T(8,128)(2,1)S(1)}) custom-call(bf16[1152,768]{1,0:T(8,128)(2,1)S(1)} %shard_map.42.mine, bf16[1152,768]{1,0:T(8,128)(2,1)S(1)} %collective-permute-done.5.other, bf16[512,768]{1,0:T(8,128)(2,1)S(1)} %shard_map.40.refs_1_.early, ...), custom_call_target="tpu_custom_call" | custom-call | bytes 1 | tf_op jit(solution)/shard_map/pallas_call | solution.py:663
  64.6 0.0 collective-permute-done.8.refs_1_
  64.6 0.0 collective-permute-done.7.refs_0_
  64.6 0.1 collective-permute-start.9
  64.7 2.2 %collective-permute-done.9.late_j = bf16[512,768]{1,0:T(8,128)(2,1)S(1)} collective-permute-done((bf16[512,768]{1,0:T(8,128)(2,1)S(1)}, bf16[512,768]{1,0:T(8,128)(2,1)S(1)}, u32[]{:S(2)}, u32[]{:S(2)}) %collective-permute-start.9) | collective-permute-done | bytes 786464 | tf_op jit(solution)/shard_map/ppermute | solution.py:733
  67.0 0.0 copy-start.1
  67.0 0.0 copy-start.3
  67.0 0.0 copy-start.5
  67.0 0.7 shard_map.47
  67.6 10.0 %all-to-all-start.3 = ((f32[8,1,256]{2,1,0:T(1,128)}), f32[8,1,256]{2,1,0:T(1,128)S(1)}, u32[]{:S(2)}, u32[]{:S(2)}) async-start(f32[8,1,256]{2,1,0:T(1,128)} %shard_map.47), calls=%async_computation.3 | async-start | bytes 16384 | tf_op jit(solution)/shard_map/all_to_all | solution.py:787
  78.3 5.9 %all-to-all-done.3 = f32[8,1,256]{2,1,0:T(1,128)S(1)} async-done(((f32[8,1,256]{2,1,0:T(1,128)}), f32[8,1,256]{2,1,0:T(1,128)S(1)}, u32[]{:S(2)}, u32[]{:S(2)}) %all-to-all-start.3) | async-done | bytes 8224 | tf_op jit(solution)/shard_map/all_to_all | solution.py:787
  84.1 0.0 copy-done.1
  84.1 0.0 copy-done.3
  84.1 0.0 copy-done.5
  84.1 0.1 conditional.1
  84.1 0.1 branch_1_fun.1
  84.2 0.0 copy-start.4
  84.3 0.6 copy-done.4
  (5 shorter events, 0.1 us)
Async XLA Ops:
  5.2 48.5 %all-to-all-start.2 = ((bf16[8,144,768]{2,1,0:T(8,128)(2,1)}), bf16[8,144,768]{2,1,0:T(8,128)(2,1)S(1)}, u32[]{:S(2)}, u32[]{:S(2)}) async-start(bf16[8,144,768]{2,1,0:T(8,128)(2,1)} %bitcast.12), calls=%async_computation.2 | async-start | bytes 3538944 | tf_op jit(solution)/shard_map/all_to_all | solution.py:738
  12.5 7.2 %collective-permute-start.4 = (bf16[128,768]{1,0:T(8,128)(2,1)S(1)}, bf16[128,768]{1,0:T(8,128)(2,1)S(1)}, u32[]{:S(2)}, u32[]{:S(2)}) collective-permute-start(bf16[128,768]{1,0:T(8,128)(2,1)S(1)} %get-tuple-element.40.refs_2_.refs_0_), channel_id=1, source_target_pairs={{12,8},{14,10},{13,9},{15,11},{28,24},{30,26},{29,25},{31,27}} | collective-permute-start | bytes 589832 | tf_op jit(solution)/shard_map/ppermute | solution.py:730
  13.2 6.6 %collective-permute-start.3 = (bf16[128,768]{1,0:T(8,128)(2,1)S(1)}, bf16[128,768]{1,0:T(8,128)(2,1)S(1)}, u32[]{:S(2)}, u32[]{:S(2)}) collective-permute-start(bf16[128,768]{1,0:T(8,128)(2,1)S(1)} %get-tuple-element.40.refs_2_.refs_0_), channel_id=1, source_target_pairs={{6,4},{7,5},{22,20},{23,21}} | collective-permute-start | bytes 589832 | tf_op jit(solution)/shard_map/ppermute | solution.py:730
  13.9 5.9 %collective-permute-start.2 = (bf16[128,768]{1,0:T(8,128)(2,1)S(1)}, bf16[128,768]{1,0:T(8,128)(2,1)S(1)}, u32[]{:S(2)}, u32[]{:S(2)}) collective-permute-start(bf16[128,768]{1,0:T(8,128)(2,1)S(1)} %get-tuple-element.40.refs_2_.refs_0_), channel_id=1, source_target_pairs={{2,4},{3,5},{18,20},{19,21}} | collective-permute-start | bytes 589832 | tf_op jit(solution)/shard_map/ppermute | solution.py:730
  14.6 31.7 %collective-permute-start.1 = (bf16[128,768]{1,0:T(8,128)(2,1)S(1)}, bf16[128,768]{1,0:T(8,128)(2,1)S(1)}, u32[]{:S(2)}, u32[]{:S(2)}) collective-permute-start(bf16[128,768]{1,0:T(8,128)(2,1)S(1)} %get-tuple-element.40.refs_2_.refs_0_), channel_id=1, source_target_pairs={{0,4},{1,5},{16,20},{17,21}} | collective-permute-start | bytes 589832 | tf_op jit(solution)/shard_map/ppermute | solution.py:730
  53.7 5.9 %collective-permute-start.5 = (bf16[1152,768]{1,0:T(8,128)(2,1)S(1)}, bf16[1152,768]{1,0:T(8,128)(2,1)S(1)}, u32[]{:S(2)}, u32[]{:S(2)}) collective-permute-start(bf16[1152,768]{1,0:T(8,128)(2,1)S(1)} %shard_map.42.mine), channel_id=1, source_target_pairs={{0,1},{1,0},{2,3},{3,2},{4,5},{5,4},{6,7},{7,6},{8,9},{9,8},{10,11... | collective-permute-start | bytes 5308424 | tf_op jit(solution)/shard_map/ppermute | solution.py:733
  53.8 5.9 %collective-permute-start.6 = (bf16[512,768]{1,0:T(8,128)(2,1)S(1)}, bf16[512,768]{1,0:T(8,128)(2,1)S(1)}, u32[]{:S(2)}, u32[]{:S(2)}) collective-permute-start(bf16[512,768]{1,0:T(8,128)(2,1)S(1)} %shard_map.40.refs_1_.early), channel_id=1, source_target_pairs={{0,1},{1,0},{2,3},{3,2},{4,5},{5,4},{6,7},{7,6},{8,9},{9,8},{10,11... | collective-permute-start | bytes 2359304 | tf_op jit(solution)/shard_map/ppermute | solution.py:733
  54.3 10.3 %collective-permute-start.8 = (bf16[256,768]{1,0:T(8,128)(2,1)S(1)}, bf16[256,768]{1,0:T(8,128)(2,1)S(1)}, u32[]{:S(2)}, u32[]{:S(2)}) collective-permute-start(bf16[256,768]{1,0:T(8,128)(2,1)S(1)} %shard_map.41.refs_2_), channel_id=1, source_target_pairs={{10,4},{11,5},{26,20},{27,21}} | collective-permute-start | bytes 1179656 | tf_op jit(solution)/shard_map/ppermute | solution.py:730
  54.9 9.6 %collective-permute-start.7 = (bf16[256,768]{1,0:T(8,128)(2,1)S(1)}, bf16[256,768]{1,0:T(8,128)(2,1)S(1)}, u32[]{:S(2)}, u32[]{:S(2)}) collective-permute-start(bf16[256,768]{1,0:T(8,128)(2,1)S(1)} %shard_map.41.refs_2_), channel_id=1, source_target_pairs={{8,4},{9,5},{24,20},{25,21}} | collective-permute-start | bytes 1179656 | tf_op jit(solution)/shard_map/ppermute | solution.py:730
  64.6 2.4 %collective-permute-start.9 = (bf16[512,768]{1,0:T(8,128)(2,1)S(1)}, bf16[512,768]{1,0:T(8,128)(2,1)S(1)}, u32[]{:S(2)}, u32[]{:S(2)}) collective-permute-start(bf16[512,768]{1,0:T(8,128)(2,1)S(1)} %shard_map.45.late), channel_id=1, source_target_pairs={{0,1},{1,0},{2,3},{3,2},{4,5},{5,4},{6,7},{7,6},{8,9},{9,8},{10,11... | collective-permute-start | bytes 2359304 | tf_op jit(solution)/shard_map/ppermute | solution.py:733
  67.0 17.2 %copy-start.1 = (bf16[1024,768]{1,0:T(8,128)(2,1)S(1)}, bf16[1024,768]{1,0:T(8,128)(2,1)}, u32[]{:S(2)}) copy-start(bf16[1024,768]{1,0:T(8,128)(2,1)} %x_hbm.1) | copy-start | bytes 4718596
  67.0 17.2 %copy-start.3 = (s32[1024]{0:T(1024)S(1)}, s32[1024]{0:T(1024)}, u32[]{:S(2)}) copy-start(s32[1024]{0:T(1024)} %param.6) | copy-start | bytes 12292
  67.0 17.2 %copy-start.5 = (s32[64]{0:T(128)S(1)}, s32[64]{0:T(128)}, u32[]{:S(2)}) copy-start(s32[64]{0:T(128)} %param.7) | copy-start | bytes 772
  67.6 16.5 %all-to-all-start.3 = ((f32[8,1,256]{2,1,0:T(1,128)}), f32[8,1,256]{2,1,0:T(1,128)S(1)}, u32[]{:S(2)}, u32[]{:S(2)}) async-start(f32[8,1,256]{2,1,0:T(1,128)} %shard_map.47), calls=%async_computation.3 | async-start | bytes 16384 | tf_op jit(solution)/shard_map/all_to_all | solution.py:787
  84.2 0.6 copy-start.4

commit v16 on v15

--- a/solution.py
+++ b/solution.py
@@ -727,7 +727,8 @@
     packed, extra, pos = place_rows(embeddings, labels, owner_map, lay)
 
     def hop(x, pairs):
-        return lax.ppermute(x, "cl", pairs)
+        partner = dict(pairs) | {target: source for source, target in pairs}
+        return lax.ppermute(x, "cl", [(i, partner.get(i, i)) for i in range(n_owner)])
 
     def swap(x):
         return lax.ppermute(x, "grp", [(0, 1), (1, 0)])

time: 85.2 us -> 92.3 us (1.083)
  starting transfers between devices: 26.4 us -> 36.2 us
  waiting for transfers between devices: 42.1 us -> 39.4 us
    all_to_all x1, starting transfers between devices: 9.97 us -> 17 us  [body(): lax.all_to_all(results, 'cl', split_axis=0, concat_axis=0, tiled=True)]
    ppermute x6, starting transfers between devices: 8.54 us -> 11.2 us  [hop(): lax.ppermute(x, 'cl', [(i, partner.get(i, i)) for i in range(n_owner)])]
    ppermute x6, waiting for transfers between devices: 26.5 us -> 23.8 us  [hop(): lax.ppermute(x, 'cl', [(i, partner.get(i, i)) for i in range(n_owner)])]
  transfers between devices with their start and end apart: 11 -> 11, of which waited for: 4 -> 4; matrix products, arithmetic and copies ran while one was open for 0% -> 0% of each run, Pallas kernels for 11% -> 10%
where the time goes in v16:
time: 92.3 us; the launch traced here: 91.9 us
  waiting for transfers between devices  39.4 us (43%)
  starting transfers between devices  36.2 us (39%)
  Pallas kernels  14.9 us (16%)
    ppermute x6, waiting for transfers between devices, hop(): lax.ppermute(x, 'cl', [(i, partner.get(i, i)) for i in range(n_owner)])  23.8 us
    all_to_all x1, starting transfers between devices, body(): lax.all_to_all(results, 'cl', split_axis=0, concat_axis=0, tiled=True)  17 us
    ppermute x6, starting transfers between devices, hop(): lax.ppermute(x, 'cl', [(i, partner.get(i, i)) for i in range(n_owner)])  11.2 us
    pallas_call x4, Pallas kernels, pair_call(): pl.pallas_call(functools.partial(kernel, lay), out_shape=out_shape, in_sp...  9.58 us
    all_to_all x1, waiting for transfers between devices, body(): lax.all_to_all(packed.reshape(n_owner, main, width), 'cl', split_axis=0,...  7.45 us
    all_to_all x1, starting transfers between devices, body(): lax.all_to_all(packed.reshape(n_owner, main, width), 'cl', split_axis=0,...  7.29 us
    all_to_all x1, waiting for transfers between devices, body(): lax.all_to_all(results, 'cl', split_axis=0, concat_axis=0, tiled=True)  5.86 us
    pallas_call x1, Pallas kernels, place_rows(): pl.pallas_call(functools.partial(place_kernel, lay), out_shape=(jax.Shape...  5.23 us
  transfers between devices with their start and end apart: 11, of which 4 were waited for; matrix products, arithmetic and copies ran while one was open for 0% of the time, Pallas kernels for 10%

profile of v16, /device:TPU:0, one launch (start us, length us, event | category | flops | bytes accessed | tf_op | source)
XLA Modules:
  0.0 91.9 jit_solution(736623782763566306)
XLA Ops:
  0.0 5.2 %shard_map.39 = (bf16[1152,768]{1,0:T(8,128)(2,1)}, bf16[128,768]{1,0:T(8,128)(2,1)S(1)}, s32[8,128]{1,0:T(8,128)S(1)}) custom-call(bf16[1024,768]{1,0:T(8,128)(2,1)} %x_hbm.1, s32[8,128]{1,0:T(8,128)} %bitcast.23, s32[1,64]{1,0:T(1,128)} %bitcast.27), custom_call_target="tpu_custom_call" | custom-call | tf_op jit(solution)/shard_map/pallas_call | solution.py:311
  5.2 7.3 %all-to-all-start.2 = ((bf16[8,144,768]{2,1,0:T(8,128)(2,1)}), bf16[8,144,768]{2,1,0:T(8,128)(2,1)S(1)}, u32[]{:S(2)}, u32[]{:S(2)}) async-start(bf16[8,144,768]{2,1,0:T(8,128)(2,1)} %bitcast.12), calls=%async_computation.2 | async-start | bytes 3538944 | tf_op jit(solution)/shard_map/all_to_all | solution.py:739
  12.5 0.7 collective-permute-start.4
  13.2 0.7 collective-permute-start.3
  13.9 0.7 collective-permute-start.2
  14.6 7.9 %collective-permute-start.1 = (bf16[128,768]{1,0:T(8,128)(2,1)S(1)}, bf16[128,768]{1,0:T(8,128)(2,1)S(1)}, u32[]{:S(2)}, u32[]{:S(2)}) collective-permute-start(bf16[128,768]{1,0:T(8,128)(2,1)S(1)} %get-tuple-element.40.refs_2_.refs_0_), channel_id=1, source_target_pairs={{0,4},{2,2},{4,0},{6,6},{8,8},{10,10},{12,12},{14,14},{1,5},{3,3},... | collective-permute-start | bytes 589832 | tf_op jit(solution)/shard_map/ppermute | solution.py:731
  22.4 0.0 collective-permute-done.4.refs_1_
  22.5 0.0 collective-permute-done.3.refs_3_
  22.5 0.0 collective-permute-done.2.refs_1_
  22.5 23.8 %collective-permute-done.1.refs_0_ = bf16[128,768]{1,0:T(8,128)(2,1)S(1)} collective-permute-done((bf16[128,768]{1,0:T(8,128)(2,1)S(1)}, bf16[128,768]{1,0:T(8,128)(2,1)S(1)}, u32[]{:S(2)}, u32[]{:S(2)}) %collective-permute-start.1) | collective-permute-done | bytes 196640 | tf_op jit(solution)/shard_map/ppermute | solution.py:731
  46.3 7.4 %all-to-all-done.2 = bf16[8,144,768]{2,1,0:T(8,128)(2,1)S(1)} async-done(((bf16[8,144,768]{2,1,0:T(8,128)(2,1)}), bf16[8,144,768]{2,1,0:T(8,128)(2,1)S(1)}, u32[]{:S(2)}, u32[]{:S(2)}) %all-to-all-start.2) | async-done | bytes 1769504 | tf_op jit(solution)/shard_map/all_to_all | solution.py:739
  53.7 0.0 collective-permute-start.5
  53.8 0.5 collective-permute-start.6
  54.3 0.7 collective-permute-start.8
  54.9 0.7 collective-permute-start.7
  55.6 4.0 %shard_map.43 = (f32[1,1536]{1,0:T(1,128)S(1)}, f32[1,1536]{1,0:T(1,128)S(1)}, f32[1536,128]{1,0:T(8,128)S(1)}, bf16[1024,768]{1,0:T(8,128)(2,1)S(1)}) custom-call(bf16[1152,768]{1,0:T(8,128)(2,1)S(1)} %shard_map.42.mine, bf16[512,768]{1,0:T(8,128)(2,1)S(1)} %shard_map.40.refs_1_.early), custom_call_target="tpu_custom_call" | custom-call | bytes 1 | tf_op jit(solution)/shard_map/pallas_call | solution.py:663
  59.7 0.0 collective-permute-done.6.early_j
  59.7 0.0 collective-permute-done.5.other
  59.7 4.8 %shard_map.44 = (f32[1,1536]{1,0:T(1,128)S(1)}, s32[1,1]{1,0:T(1,128)}, f32[1536,128]{1,0:T(8,128)S(1)}, bf16[1024,768]{1,0:T(8,128)(2,1)S(1)}) custom-call(bf16[1152,768]{1,0:T(8,128)(2,1)S(1)} %shard_map.42.mine, bf16[1152,768]{1,0:T(8,128)(2,1)S(1)} %collective-permute-done.5.other, bf16[512,768]{1,0:T(8,128)(2,1)S(1)} %shard_map.40.refs_1_.early, ...), custom_call_target="tpu_custom_call" | custom-call | bytes 1 | tf_op jit(solution)/shard_map/pallas_call | solution.py:663
  64.6 0.0 collective-permute-done.8.refs_1_
  64.6 0.0 collective-permute-done.7.refs_0_
  64.6 0.1 collective-permute-start.9
  64.7 2.2 %collective-permute-done.9.late_j = bf16[512,768]{1,0:T(8,128)(2,1)S(1)} collective-permute-done((bf16[512,768]{1,0:T(8,128)(2,1)S(1)}, bf16[512,768]{1,0:T(8,128)(2,1)S(1)}, u32[]{:S(2)}, u32[]{:S(2)}) %collective-permute-start.9) | collective-permute-done | bytes 786464 | tf_op jit(solution)/shard_map/ppermute | solution.py:734
  67.0 0.0 copy-start.1
  67.0 0.0 copy-start.3
  67.0 0.0 copy-start.5
  67.0 0.7 shard_map.47
  67.6 17.0 %all-to-all-start.3 = ((f32[8,1,256]{2,1,0:T(1,128)}), f32[8,1,256]{2,1,0:T(1,128)S(1)}, u32[]{:S(2)}, u32[]{:S(2)}) async-start(f32[8,1,256]{2,1,0:T(1,128)} %shard_map.47), calls=%async_computation.3 | async-start | bytes 16384 | tf_op jit(solution)/shard_map/all_to_all | solution.py:788
  85.3 5.9 %all-to-all-done.3 = f32[8,1,256]{2,1,0:T(1,128)S(1)} async-done(((f32[8,1,256]{2,1,0:T(1,128)}), f32[8,1,256]{2,1,0:T(1,128)S(1)}, u32[]{:S(2)}, u32[]{:S(2)}) %all-to-all-start.3) | async-done | bytes 8224 | tf_op jit(solution)/shard_map/all_to_all | solution.py:788
  91.2 0.0 copy-done.1
  91.2 0.0 copy-done.3
  91.2 0.0 copy-done.5
  91.2 0.1 conditional.1
  91.2 0.1 branch_1_fun.1
  91.3 0.0 copy-start.4
  91.3 0.6 copy-done.4
  (5 shorter events, 0.1 us)
Async XLA Ops:
  5.2 48.5 %all-to-all-start.2 = ((bf16[8,144,768]{2,1,0:T(8,128)(2,1)}), bf16[8,144,768]{2,1,0:T(8,128)(2,1)S(1)}, u32[]{:S(2)}, u32[]{:S(2)}) async-start(bf16[8,144,768]{2,1,0:T(8,128)(2,1)} %bitcast.12), calls=%async_computation.2 | async-start | bytes 3538944 | tf_op jit(solution)/shard_map/all_to_all | solution.py:739
  12.5 9.9 %collective-permute-start.4 = (bf16[128,768]{1,0:T(8,128)(2,1)S(1)}, bf16[128,768]{1,0:T(8,128)(2,1)S(1)}, u32[]{:S(2)}, u32[]{:S(2)}) collective-permute-start(bf16[128,768]{1,0:T(8,128)(2,1)S(1)} %get-tuple-element.40.refs_2_.refs_0_), channel_id=1, source_target_pairs={{0,0},{2,2},{4,4},{6,6},{8,12},{10,14},{12,8},{14,10},{1,1},{3,3},... | collective-permute-start | bytes 589832 | tf_op jit(solution)/shard_map/ppermute | solution.py:731
  13.2 9.3 %collective-permute-start.3 = (bf16[128,768]{1,0:T(8,128)(2,1)S(1)}, bf16[128,768]{1,0:T(8,128)(2,1)S(1)}, u32[]{:S(2)}, u32[]{:S(2)}) collective-permute-start(bf16[128,768]{1,0:T(8,128)(2,1)S(1)} %get-tuple-element.40.refs_2_.refs_0_), channel_id=1, source_target_pairs={{0,0},{2,2},{4,6},{6,4},{8,8},{10,10},{12,12},{14,14},{1,1},{3,3},... | collective-permute-start | bytes 589832 | tf_op jit(solution)/shard_map/ppermute | solution.py:731
  13.9 8.6 %collective-permute-start.2 = (bf16[128,768]{1,0:T(8,128)(2,1)S(1)}, bf16[128,768]{1,0:T(8,128)(2,1)S(1)}, u32[]{:S(2)}, u32[]{:S(2)}) collective-permute-start(bf16[128,768]{1,0:T(8,128)(2,1)S(1)} %get-tuple-element.40.refs_2_.refs_0_), channel_id=1, source_target_pairs={{0,0},{2,4},{4,2},{6,6},{8,8},{10,10},{12,12},{14,14},{1,1},{3,5},... | collective-permute-start | bytes 589832 | tf_op jit(solution)/shard_map/ppermute | solution.py:731
  14.6 31.7 %collective-permute-start.1 = (bf16[128,768]{1,0:T(8,128)(2,1)S(1)}, bf16[128,768]{1,0:T(8,128)(2,1)S(1)}, u32[]{:S(2)}, u32[]{:S(2)}) collective-permute-start(bf16[128,768]{1,0:T(8,128)(2,1)S(1)} %get-tuple-element.40.refs_2_.refs_0_), channel_id=1, source_target_pairs={{0,4},{2,2},{4,0},{6,6},{8,8},{10,10},{12,12},{14,14},{1,5},{3,3},... | collective-permute-start | bytes 589832 | tf_op jit(solution)/shard_map/ppermute | solution.py:731
  53.7 5.9 %collective-permute-start.5 = (bf16[1152,768]{1,0:T(8,128)(2,1)S(1)}, bf16[1152,768]{1,0:T(8,128)(2,1)S(1)}, u32[]{:S(2)}, u32[]{:S(2)}) collective-permute-start(bf16[1152,768]{1,0:T(8,128)(2,1)S(1)} %shard_map.42.mine), channel_id=1, source_target_pairs={{0,1},{1,0},{2,3},{3,2},{4,5},{5,4},{6,7},{7,6},{8,9},{9,8},{10,11... | collective-permute-start | bytes 5308424 | tf_op jit(solution)/shard_map/ppermute | solution.py:734
  53.8 5.9 %collective-permute-start.6 = (bf16[512,768]{1,0:T(8,128)(2,1)S(1)}, bf16[512,768]{1,0:T(8,128)(2,1)S(1)}, u32[]{:S(2)}, u32[]{:S(2)}) collective-permute-start(bf16[512,768]{1,0:T(8,128)(2,1)S(1)} %shard_map.40.refs_1_.early), channel_id=1, source_target_pairs={{0,1},{1,0},{2,3},{3,2},{4,5},{5,4},{6,7},{7,6},{8,9},{9,8},{10,11... | collective-permute-start | bytes 2359304 | tf_op jit(solution)/shard_map/ppermute | solution.py:734
  54.3 10.3 %collective-permute-start.8 = (bf16[256,768]{1,0:T(8,128)(2,1)S(1)}, bf16[256,768]{1,0:T(8,128)(2,1)S(1)}, u32[]{:S(2)}, u32[]{:S(2)}) collective-permute-start(bf16[256,768]{1,0:T(8,128)(2,1)S(1)} %shard_map.41.refs_2_), channel_id=1, source_target_pairs={{0,0},{2,2},{4,10},{6,6},{8,8},{10,4},{12,12},{14,14},{1,1},{3,3},... | collective-permute-start | bytes 1179656 | tf_op jit(solution)/shard_map/ppermute | solution.py:731
  54.9 9.6 %collective-permute-start.7 = (bf16[256,768]{1,0:T(8,128)(2,1)S(1)}, bf16[256,768]{1,0:T(8,128)(2,1)S(1)}, u32[]{:S(2)}, u32[]{:S(2)}) collective-permute-start(bf16[256,768]{1,0:T(8,128)(2,1)S(1)} %shard_map.41.refs_2_), channel_id=1, source_target_pairs={{0,0},{2,2},{4,8},{6,6},{8,4},{10,10},{12,12},{14,14},{1,1},{3,3},... | collective-permute-start | bytes 1179656 | tf_op jit(solution)/shard_map/ppermute | solution.py:731
  64.6 2.4 %collective-permute-start.9 = (bf16[512,768]{1,0:T(8,128)(2,1)S(1)}, bf16[512,768]{1,0:T(8,128)(2,1)S(1)}, u32[]{:S(2)}, u32[]{:S(2)}) collective-permute-start(bf16[512,768]{1,0:T(8,128)(2,1)S(1)} %shard_map.45.late), channel_id=1, source_target_pairs={{0,1},{1,0},{2,3},{3,2},{4,5},{5,4},{6,7},{7,6},{8,9},{9,8},{10,11... | collective-permute-start | bytes 2359304 | tf_op jit(solution)/shard_map/ppermute | solution.py:734
  67.0 24.2 %copy-start.1 = (bf16[1024,768]{1,0:T(8,128)(2,1)S(1)}, bf16[1024,768]{1,0:T(8,128)(2,1)}, u32[]{:S(2)}) copy-start(bf16[1024,768]{1,0:T(8,128)(2,1)} %x_hbm.1) | copy-start | bytes 4718596
  67.0 24.2 %copy-start.3 = (s32[1024]{0:T(1024)S(1)}, s32[1024]{0:T(1024)}, u32[]{:S(2)}) copy-start(s32[1024]{0:T(1024)} %param.6) | copy-start | bytes 12292
  67.0 24.2 %copy-start.5 = (s32[64]{0:T(128)S(1)}, s32[64]{0:T(128)}, u32[]{:S(2)}) copy-start(s32[64]{0:T(128)} %param.7) | copy-start | bytes 772
  67.6 23.5 %all-to-all-start.3 = ((f32[8,1,256]{2,1,0:T(1,128)}), f32[8,1,256]{2,1,0:T(1,128)S(1)}, u32[]{:S(2)}, u32[]{:S(2)}) async-start(f32[8,1,256]{2,1,0:T(1,128)} %shard_map.47), calls=%async_computation.3 | async-start | bytes 16384 | tf_op jit(solution)/shard_map/all_to_all | solution.py:788
  91.3 0.6 copy-start.4

commit v17 on v15

--- a/solution.py
+++ b/solution.py
@@ -732,15 +732,15 @@
     def swap(x):
         return lax.ppermute(x, "grp", [(0, 1), (1, 0)])
 
-    both = lay_out([extra, hop(extra, [(6, 4), (7, 5)])])
+    moved = hop(extra, [(6, 4), (7, 5)])
     early = [extra if s == home else hop(extra, [(s, home)]) for s in lay.early]
     early = lay_out(early, home)
     mine = lax.all_to_all(
         packed.reshape(n_owner, main, width), "cl", split_axis=0, concat_axis=0, tiled=True
     ).reshape(n_owner * main, width)
-    mine = after(mine, early, both)
+    mine = after(mine, early, moved)
     other, early_j = swap(mine), swap(early)
-    late = [hop(both, [(4, home)]), hop(both, [(5, home)])]
+    late = [hop(x, [(s, home)]) for s in (4, 5) for x in (extra, moved)]
 
     def array(shape, dtype=jnp.float32):
         return jax.ShapeDtypeStruct(shape, dtype)

time: 85.2 us -> 86.1 us (1.011)
  waiting for transfers between devices: 42.1 us -> 44.3 us
  starting transfers between devices: 26.4 us -> 25.1 us
    all_to_all x1, starting transfers between devices: 9.97 us -> 7.26 us  [body(): lax.all_to_all(results, 'cl', split_axis=0, concat_axis=0, tiled=True)]
    ppermute x3, waiting for transfers between devices: 2.25 us -> 4.42 us  [swap(): return lax.ppermute(x, 'grp', [(0, 1), (1, 0)])]
    ppermute x6 -> x8, starting transfers between devices: 8.54 us -> 9.85 us  [hop(): return lax.ppermute(x, 'cl', pairs)]
    ppermute x6 -> x8, waiting for transfers between devices: 26.5 us -> 26.6 us  [hop(): return lax.ppermute(x, 'cl', pairs)]
  transfers between devices with their start and end apart: 11 -> 13, of which waited for: 4 -> 5; matrix products, arithmetic and copies ran while one was open for 0% -> 0% of each run, Pallas kernels for 11% -> 10%
where the time goes in v17:
time: 86.1 us; the launch traced here: 85.8 us
  waiting for transfers between devices  44.3 us (51%)
  starting transfers between devices  25.1 us (29%)
  Pallas kernels  14.9 us (17%)
    ppermute x8, waiting for transfers between devices, hop(): return lax.ppermute(x, 'cl', pairs)  26.6 us
    ppermute x8, starting transfers between devices, hop(): return lax.ppermute(x, 'cl', pairs)  9.85 us
    pallas_call x4, Pallas kernels, pair_call(): pl.pallas_call(functools.partial(kernel, lay), out_shape=out_shape, in_sp...  9.58 us
    all_to_all x1, waiting for transfers between devices, body(): lax.all_to_all(packed.reshape(n_owner, main, width), 'cl', split_axis=0,...  7.44 us
    all_to_all x1, starting transfers between devices, body(): lax.all_to_all(packed.reshape(n_owner, main, width), 'cl', split_axis=0,...  7.29 us
    all_to_all x1, starting transfers between devices, body(): lax.all_to_all(results, 'cl', split_axis=0, concat_axis=0, tiled=True)  7.26 us
    all_to_all x1, waiting for transfers between devices, body(): lax.all_to_all(results, 'cl', split_axis=0, concat_axis=0, tiled=True)  5.86 us
    pallas_call x1, Pallas kernels, place_rows(): pl.pallas_call(functools.partial(place_kernel, lay), out_shape=(jax.Shape...  5.22 us
  transfers between devices with their start and end apart: 13, of which 5 were waited for; matrix products, arithmetic and copies ran while one was open for 0% of the time, Pallas kernels for 10%

profile of v17, /device:TPU:0, one launch (start us, length us, event | category | flops | bytes accessed | tf_op | source)
XLA Modules:
  0.0 85.8 jit_solution(15934337607960599750)
XLA Ops:
  0.0 5.2 %shard_map.39 = (bf16[1152,768]{1,0:T(8,128)(2,1)}, bf16[128,768]{1,0:T(8,128)(2,1)S(1)}, s32[8,128]{1,0:T(8,128)S(1)}) custom-call(bf16[1024,768]{1,0:T(8,128)(2,1)} %x_hbm.1, s32[8,128]{1,0:T(8,128)} %bitcast.23, s32[1,64]{1,0:T(1,128)} %bitcast.27), custom_call_target="tpu_custom_call" | custom-call | tf_op jit(solution)/shard_map/pallas_call | solution.py:311
  5.2 7.3 %all-to-all-start.2 = ((bf16[8,144,768]{2,1,0:T(8,128)(2,1)}), bf16[8,144,768]{2,1,0:T(8,128)(2,1)S(1)}, u32[]{:S(2)}, u32[]{:S(2)}) async-start(bf16[8,144,768]{2,1,0:T(8,128)(2,1)} %bitcast.12), calls=%async_computation.2 | async-start | bytes 3538944 | tf_op jit(solution)/shard_map/all_to_all | solution.py:738
  12.5 0.7 collective-permute-start.3
  13.2 0.7 collective-permute-start.2
  13.9 5.2 %collective-permute-start.1 = (bf16[128,768]{1,0:T(8,128)(2,1)S(1)}, bf16[128,768]{1,0:T(8,128)(2,1)S(1)}, u32[]{:S(2)}, u32[]{:S(2)}) collective-permute-start(bf16[128,768]{1,0:T(8,128)(2,1)S(1)} %get-tuple-element.40.refs_2_), channel_id=1, source_target_pairs={{0,4},{1,5},{16,20},{17,21}} | collective-permute-start | bytes 589832 | tf_op jit(solution)/shard_map/ppermute | solution.py:730
  19.1 0.7 collective-permute-start.4
  19.7 0.0 collective-permute-done.3.refs_3_
  19.7 0.0 collective-permute-done.2.refs_1_
  19.8 26.5 %collective-permute-done.1.refs_0_ = bf16[128,768]{1,0:T(8,128)(2,1)S(1)} collective-permute-done((bf16[128,768]{1,0:T(8,128)(2,1)S(1)}, bf16[128,768]{1,0:T(8,128)(2,1)S(1)}, u32[]{:S(2)}, u32[]{:S(2)}) %collective-permute-start.1) | collective-permute-done | bytes 196640 | tf_op jit(solution)/shard_map/ppermute | solution.py:730
  46.3 0.0 collective-permute-done.4.refs_2_
  46.3 7.4 %all-to-all-done.2 = bf16[8,144,768]{2,1,0:T(8,128)(2,1)S(1)} async-done(((bf16[8,144,768]{2,1,0:T(8,128)(2,1)}), bf16[8,144,768]{2,1,0:T(8,128)(2,1)S(1)}, u32[]{:S(2)}, u32[]{:S(2)}) %all-to-all-start.2) | async-done | bytes 1769504 | tf_op jit(solution)/shard_map/all_to_all | solution.py:738
  53.7 0.0 collective-permute-start.5
  53.7 0.5 collective-permute-start.6
  54.3 0.7 collective-permute-start.9
  54.9 0.7 collective-permute-start.7
  55.6 0.7 collective-permute-start.10
  56.3 2.3 %collective-permute-done.6.early_j = bf16[512,768]{1,0:T(8,128)(2,1)S(1)} collective-permute-done((bf16[512,768]{1,0:T(8,128)(2,1)S(1)}, bf16[512,768]{1,0:T(8,128)(2,1)S(1)}, u32[]{:S(2)}, u32[]{:S(2)}) %collective-permute-start.6) | collective-permute-done | bytes 786464 | tf_op jit(solution)/shard_map/ppermute | solution.py:733
  58.6 0.7 collective-permute-start.8
  59.2 4.1 %shard_map.42 = (f32[1,1536]{1,0:T(1,128)S(1)}, f32[1,1536]{1,0:T(1,128)S(1)}, f32[1536,128]{1,0:T(8,128)S(1)}, bf16[1024,768]{1,0:T(8,128)(2,1)S(1)}) custom-call(bf16[1152,768]{1,0:T(8,128)(2,1)S(1)} %shard_map.41.mine, bf16[512,768]{1,0:T(8,128)(2,1)S(1)} %shard_map.40.refs_1_.early), custom_call_target="tpu_custom_call" | custom-call | bytes 1 | tf_op jit(solution)/shard_map/pallas_call | solution.py:663
  63.3 0.0 collective-permute-done.5.other
  63.3 4.8 %shard_map.43 = (f32[1,1536]{1,0:T(1,128)S(1)}, s32[1,1]{1,0:T(1,128)}, f32[1536,128]{1,0:T(8,128)S(1)}, bf16[1024,768]{1,0:T(8,128)(2,1)S(1)}) custom-call(bf16[1152,768]{1,0:T(8,128)(2,1)S(1)} %shard_map.41.mine, bf16[1152,768]{1,0:T(8,128)(2,1)S(1)} %collective-permute-done.5.other, bf16[512,768]{1,0:T(8,128)(2,1)S(1)} %shard_map.40.refs_1_.early, ...), custom_call_target="tpu_custom_call" | custom-call | bytes 1 | tf_op jit(solution)/shard_map/pallas_call | solution.py:663
  68.2 0.0 collective-permute-done.9.refs_2_
  68.2 0.0 collective-permute-done.7.refs_0_
  68.2 0.0 collective-permute-done.10.refs_3_
  68.2 0.0 collective-permute-done.8.refs_1_
  68.2 0.2 collective-permute-start.11
  68.4 2.1 %collective-permute-done.11.late_j = bf16[512,768]{1,0:T(8,128)(2,1)S(1)} collective-permute-done((bf16[512,768]{1,0:T(8,128)(2,1)S(1)}, bf16[512,768]{1,0:T(8,128)(2,1)S(1)}, u32[]{:S(2)}, u32[]{:S(2)}) %collective-permute-start.11) | collective-permute-done | bytes 786464 | tf_op jit(solution)/shard_map/ppermute | solution.py:733
  70.6 0.0 copy-start.1
  70.6 0.0 copy-start.3
  70.6 0.0 copy-start.5
  70.6 0.7 shard_map.46
  71.3 7.3 %all-to-all-start.3 = ((f32[8,1,256]{2,1,0:T(1,128)}), f32[8,1,256]{2,1,0:T(1,128)S(1)}, u32[]{:S(2)}, u32[]{:S(2)}) async-start(f32[8,1,256]{2,1,0:T(1,128)} %shard_map.46), calls=%async_computation.3 | async-start | bytes 16384 | tf_op jit(solution)/shard_map/all_to_all | solution.py:787
  79.2 5.9 %all-to-all-done.3 = f32[8,1,256]{2,1,0:T(1,128)S(1)} async-done(((f32[8,1,256]{2,1,0:T(1,128)}), f32[8,1,256]{2,1,0:T(1,128)S(1)}, u32[]{:S(2)}, u32[]{:S(2)}) %all-to-all-start.3) | async-done | bytes 8224 | tf_op jit(solution)/shard_map/all_to_all | solution.py:787
  85.0 0.0 copy-done.1
  85.0 0.0 copy-done.3
  85.0 0.0 copy-done.5
  85.0 0.1 conditional.1
  85.1 0.1 branch_1_fun.1
  85.2 0.0 copy-start.4
  85.2 0.6 copy-done.4
  (4 shorter events, 0.0 us)
Async XLA Ops:
  5.2 48.5 %all-to-all-start.2 = ((bf16[8,144,768]{2,1,0:T(8,128)(2,1)}), bf16[8,144,768]{2,1,0:T(8,128)(2,1)S(1)}, u32[]{:S(2)}, u32[]{:S(2)}) async-start(bf16[8,144,768]{2,1,0:T(8,128)(2,1)} %bitcast.12), calls=%async_computation.2 | async-start | bytes 3538944 | tf_op jit(solution)/shard_map/all_to_all | solution.py:738
  12.5 7.2 %collective-permute-start.3 = (bf16[128,768]{1,0:T(8,128)(2,1)S(1)}, bf16[128,768]{1,0:T(8,128)(2,1)S(1)}, u32[]{:S(2)}, u32[]{:S(2)}) collective-permute-start(bf16[128,768]{1,0:T(8,128)(2,1)S(1)} %get-tuple-element.40.refs_2_), channel_id=1, source_target_pairs={{6,4},{7,5},{22,20},{23,21}} | collective-permute-start | bytes 589832 | tf_op jit(solution)/shard_map/ppermute | solution.py:730
  13.2 6.6 %collective-permute-start.2 = (bf16[128,768]{1,0:T(8,128)(2,1)S(1)}, bf16[128,768]{1,0:T(8,128)(2,1)S(1)}, u32[]{:S(2)}, u32[]{:S(2)}) collective-permute-start(bf16[128,768]{1,0:T(8,128)(2,1)S(1)} %get-tuple-element.40.refs_2_), channel_id=1, source_target_pairs={{2,4},{3,5},{18,20},{19,21}} | collective-permute-start | bytes 589832 | tf_op jit(solution)/shard_map/ppermute | solution.py:730
  13.9 32.4 %collective-permute-start.1 = (bf16[128,768]{1,0:T(8,128)(2,1)S(1)}, bf16[128,768]{1,0:T(8,128)(2,1)S(1)}, u32[]{:S(2)}, u32[]{:S(2)}) collective-permute-start(bf16[128,768]{1,0:T(8,128)(2,1)S(1)} %get-tuple-element.40.refs_2_), channel_id=1, source_target_pairs={{0,4},{1,5},{16,20},{17,21}} | collective-permute-start | bytes 589832 | tf_op jit(solution)/shard_map/ppermute | solution.py:730
  19.1 27.2 %collective-permute-start.4 = (bf16[128,768]{1,0:T(8,128)(2,1)S(1)}, bf16[128,768]{1,0:T(8,128)(2,1)S(1)}, u32[]{:S(2)}, u32[]{:S(2)}) collective-permute-start(bf16[128,768]{1,0:T(8,128)(2,1)S(1)} %get-tuple-element.40.refs_2_), channel_id=1, source_target_pairs={{12,8},{14,10},{13,9},{15,11},{28,24},{30,26},{29,25},{31,27}} | collective-permute-start | bytes 589832 | tf_op jit(solution)/shard_map/ppermute | solution.py:730
  53.7 9.5 %collective-permute-start.5 = (bf16[1152,768]{1,0:T(8,128)(2,1)S(1)}, bf16[1152,768]{1,0:T(8,128)(2,1)S(1)}, u32[]{:S(2)}, u32[]{:S(2)}) collective-permute-start(bf16[1152,768]{1,0:T(8,128)(2,1)S(1)} %shard_map.41.mine), channel_id=1, source_target_pairs={{0,1},{1,0},{2,3},{3,2},{4,5},{5,4},{6,7},{7,6},{8,9},{9,8},{10,11... | collective-permute-start | bytes 5308424 | tf_op jit(solution)/shard_map/ppermute | solution.py:733
  53.7 4.8 %collective-permute-start.6 = (bf16[512,768]{1,0:T(8,128)(2,1)S(1)}, bf16[512,768]{1,0:T(8,128)(2,1)S(1)}, u32[]{:S(2)}, u32[]{:S(2)}) collective-permute-start(bf16[512,768]{1,0:T(8,128)(2,1)S(1)} %shard_map.40.refs_1_.early), channel_id=1, source_target_pairs={{0,1},{1,0},{2,3},{3,2},{4,5},{5,4},{6,7},{7,6},{8,9},{9,8},{10,11... | collective-permute-start | bytes 2359304 | tf_op jit(solution)/shard_map/ppermute | solution.py:733
  54.3 13.9 %collective-permute-start.9 = (bf16[128,768]{1,0:T(8,128)(2,1)S(1)}, bf16[128,768]{1,0:T(8,128)(2,1)S(1)}, u32[]{:S(2)}, u32[]{:S(2)}) collective-permute-start(bf16[128,768]{1,0:T(8,128)(2,1)S(1)} %get-tuple-element.40.refs_2_), channel_id=1, source_target_pairs={{10,4},{11,5},{26,20},{27,21}} | collective-permute-start | bytes 589832 | tf_op jit(solution)/shard_map/ppermute | solution.py:730
  54.9 13.2 %collective-permute-start.7 = (bf16[128,768]{1,0:T(8,128)(2,1)S(1)}, bf16[128,768]{1,0:T(8,128)(2,1)S(1)}, u32[]{:S(2)}, u32[]{:S(2)}) collective-permute-start(bf16[128,768]{1,0:T(8,128)(2,1)S(1)} %get-tuple-element.40.refs_2_), channel_id=1, source_target_pairs={{8,4},{9,5},{24,20},{25,21}} | collective-permute-start | bytes 589832 | tf_op jit(solution)/shard_map/ppermute | solution.py:730
  55.6 12.6 %collective-permute-start.10 = (bf16[128,768]{1,0:T(8,128)(2,1)S(1)}, bf16[128,768]{1,0:T(8,128)(2,1)S(1)}, u32[]{:S(2)}, u32[]{:S(2)}) collective-permute-start(bf16[128,768]{1,0:T(8,128)(2,1)S(1)} %collective-permute-done.4.refs_2_), channel_id=1, source_target_pairs={{10,4},{11,5},{26,20},{27,21}} | collective-permute-start | bytes 589832 | tf_op jit(solution)/shard_map/ppermute | solution.py:730
  58.6 9.6 %collective-permute-start.8 = (bf16[128,768]{1,0:T(8,128)(2,1)S(1)}, bf16[128,768]{1,0:T(8,128)(2,1)S(1)}, u32[]{:S(2)}, u32[]{:S(2)}) collective-permute-start(bf16[128,768]{1,0:T(8,128)(2,1)S(1)} %collective-permute-done.4.refs_2_), channel_id=1, source_target_pairs={{8,4},{9,5},{24,20},{25,21}} | collective-permute-start | bytes 589832 | tf_op jit(solution)/shard_map/ppermute | solution.py:730
  68.2 2.4 %collective-permute-start.11 = (bf16[512,768]{1,0:T(8,128)(2,1)S(1)}, bf16[512,768]{1,0:T(8,128)(2,1)S(1)}, u32[]{:S(2)}, u32[]{:S(2)}) collective-permute-start(bf16[512,768]{1,0:T(8,128)(2,1)S(1)} %shard_map.44.late), channel_id=1, source_target_pairs={{0,1},{1,0},{2,3},{3,2},{4,5},{5,4},{6,7},{7,6},{8,9},{9,8},{10,11... | collective-permute-start | bytes 2359304 | tf_op jit(solution)/shard_map/ppermute | solution.py:733
  70.6 14.5 %copy-start.1 = (bf16[1024,768]{1,0:T(8,128)(2,1)S(1)}, bf16[1024,768]{1,0:T(8,128)(2,1)}, u32[]{:S(2)}) copy-start(bf16[1024,768]{1,0:T(8,128)(2,1)} %x_hbm.1) | copy-start | bytes 4718596
  70.6 14.5 %copy-start.3 = (s32[1024]{0:T(1024)S(1)}, s32[1024]{0:T(1024)}, u32[]{:S(2)}) copy-start(s32[1024]{0:T(1024)} %param.6) | copy-start | bytes 12292
  70.6 14.5 %copy-start.5 = (s32[64]{0:T(128)S(1)}, s32[64]{0:T(128)}, u32[]{:S(2)}) copy-start(s32[64]{0:T(128)} %param.7) | copy-start | bytes 772
  71.3 13.8 %all-to-all-start.3 = ((f32[8,1,256]{2,1,0:T(1,128)}), f32[8,1,256]{2,1,0:T(1,128)S(1)}, u32[]{:S(2)}, u32[]{:S(2)}) async-start(f32[8,1,256]{2,1,0:T(1,128)} %shard_map.46), calls=%async_computation.3 | async-start | bytes 16384 | tf_op jit(solution)/shard_map/all_to_all | solution.py:787
  85.2 0.6 copy-start.4

commit v18 on v17

--- a/solution.py
+++ b/solution.py
@@ -564,8 +564,20 @@
         stream((mine, lay.n_main, 0), tiles, lab_lane, buffers, setter(sums))
 
 
+def half_blocks(ref_i, ref_j, lab_sub, line, back, at, lab_lane, buffers, put):
+    half = ref_j.shape[0] // 2
+    grp = lax.axis_index("grp")
+    for h in range(2):
+        start = pl.multiple_of((h ^ grp) * half, half)
+        rows_j = ref_j.at[pl.ds(start, half)]
+        sub = lab_sub.at[pl.ds(line + start, half)]
+        backs = back.at[pl.ds(line + start, half)]
+        lanes = (ref_i.at[pl.ds(h * half, half)], half, at + h * half)
+        stream(lanes, [(rows_j, half, sub, None, 0, 1, backs)], lab_lane, buffers, put)
+
+
 def cross_kernel(lay, mine, other, early, early_j, rows, sums, lab_lane, *refs):
-    total, unfit_ref, lab_sub, rows_j, bias, buf_a, buf_b = refs
+    total, for_other, unfit_ref, lab_sub, rows_j, bias, back, buf_a, buf_b = refs
     is_home = lax.axis_index("cl") == lay.home
     infos = lines_of(lay, other)
     own = lines_of(lay, mine)
@@ -587,10 +599,23 @@
     def _():
         copy_head(lay, other, rows_j)
         first_labels(lay, infos, lab_sub)
-        tiles = [(rows_j, lay.n_head, lab_sub, None, 0, 2, None)]
-        tiles += [(early_j, lay.n_early, lab_sub, None, lay.n_head, 2, None)]
-        stream((rows, lay.n_head, 0), tiles, lab_lane, buffers, adder(total))
-        stream((early, lay.n_early, lay.n_head), tiles, lab_lane, buffers, adder(total))
+        back[...] = jnp.zeros(back.shape, jnp.float32)
+        size = lay.n_early
+        blocks_i = [rows.at[pl.ds(start, size)] for start in range(0, lay.n_head, size)] + [early]
+        blocks_j = [rows_j.at[pl.ds(start, size)] for start in range(0, lay.n_head, size)]
+        blocks_j.append(early_j)
+        put, n = adder(total), len(blocks_i)
+        for i, ref in enumerate(blocks_i):
+            tiles = [
+                (blocks_j[j], size, lab_sub, None, j * size, 2, back)
+                for j in ((i + step) % n for step in range(1, (n + 1) // 2))
+            ]
+            stream((ref, size, i * size), tiles, lab_lane, buffers, put)
+            half_blocks(
+                ref, blocks_j[i], lab_sub, i * size, back, i * size, lab_lane, buffers, put
+            )
+        for_other[...] = jnp.zeros(for_other.shape, jnp.float32)
+        turn_sums(back, lay.n_first, for_other, 0)
 
     @pl.when(jnp.logical_not(is_home))
     def _():
@@ -599,20 +624,14 @@
         stream((mine, lay.n_main, 0), tiles, lab_lane, buffers, adder(total))
 
 
-def late_pairs(lay, i_refs, j_refs, lab_sub, late_sub, lab_lane, buffers, put, back=None):
-    rows, early, late = i_refs
-    rows_j, early_j, late_j = j_refs
+def late_pairs(lay, i_refs, late_j, late_sub, back, lab_lane, buffers, put):
+    rows, early = i_refs
     lates = [(late_j, lay.n_late, late_sub, None, 0, 2, back)]
     stream((rows, lay.n_head, 0), lates, lab_lane, buffers, put)
     stream((early, lay.n_early, lay.n_head), lates, lab_lane, buffers, put)
-    every = [(late_j, lay.n_late, late_sub, None, 0, 2, None)]
-    if back is None:
-        every += [(rows_j, lay.n_head, lab_sub, None, 0, 2, None)]
-        every += [(early_j, lay.n_early, lab_sub, None, lay.n_head, 2, None)]
-    stream((late, lay.n_late, lay.n_first), every, lab_lane, buffers, put)
-
-
-def inner_late_kernel(lay, mine, early, late, rows, lab_sub, first_lane, *refs):
+
+
+def inner_late_kernel(lay, mine, early, late, rows, first_lane, *refs):
     sums, lab_lane, late_sub, back, buf_a, buf_b = refs
 
     @pl.when(lax.axis_index("cl") == lay.home)
@@ -620,41 +639,52 @@
         late_labels(lay, lines_of(lay, mine), late_sub)
         lab_lane[:, : lay.n_first] = first_lane[...]
         turn_labels(lay, late_sub, lay.n_late, lab_lane, lay.n_first)
-        refs = (rows, early, late)
         buffers = (buf_a, buf_b)
         back[...] = jnp.zeros(back.shape, jnp.float32)
         put = setter(sums)
-        late_pairs(lay, refs, refs, lab_sub, late_sub, lab_lane, buffers, put, back)
+        late_pairs(lay, (rows, early), late, late_sub, back, lab_lane, buffers, put)
+        tiles = [(late, lay.n_late, late_sub, None, 0, 2, None)]
+        stream((late, lay.n_late, lay.n_first), tiles, lab_lane, buffers, put)
         turn_sums(back, lay.n_late, sums, lay.n_first)
 
 
-def cross_late_kernel(lay, other, early, late, early_j, late_j, rows, rows_j, *refs):
-    lab_sub, first_lane, first_sums, lab_lane, sums = refs[:5]
-    out_ref, total, late_sub, buf_a, buf_b = refs[5:]
+def cross_late_kernel(lay, other, early, late, late_j, rows, first_lane, *refs):
+    first_sums, first_other, lab_lane, sums, out_ref, total, late_sub, back, buf_a, buf_b = refs
     is_home = lax.axis_index("cl") == lay.home
+    grp = lax.axis_index("grp")
 
     @pl.when(is_home)
     def _():
-        late_labels(lay, lines_of(lay, other), late_sub)
+        infos = lines_of(lay, other)
+        write_labels(lay, infos, lay.late, lay.head, lay.rest, 0, late_sub, None)
         total[...] = sums[...]
         total[:, : lay.n_first] += first_sums[...]
-        i_refs, j_refs = (rows, early, late), (rows_j, early_j, late_j)
-        buffers = (buf_a, buf_b)
-        late_pairs(lay, i_refs, j_refs, lab_sub, late_sub, lab_lane, buffers, adder(total))
-        values = jnp.log(total[...])
-        for source in range(lay.n_owner):
-            start = source * lay.head
-            out_ref[source, :, : lay.head] = values[:, start : start + lay.head]
-        for i, source in enumerate(lay.early + lay.late):
-            start = lay.n_head + i * lay.rest
-            out_ref[source, :, lay.head :] = values[:, start : start + lay.rest]
+        back[...] = jnp.zeros(back.shape, jnp.float32)
+        buffers, put = (buf_a, buf_b), adder(total)
+        late_pairs(lay, (rows, early), late_j, late_sub, back, lab_lane, buffers, put)
+        half_blocks(late, late_j, late_sub, 0, back, lay.n_first, lab_lane, buffers, put)
+
+        def write(line, values):
+            for source in range(lay.n_owner):
+                start = source * lay.head
+                out_ref[2 * source + line, :, : lay.head] = values[:, start : start + lay.head]
+            for i, source in enumerate(lay.early + lay.late):
+                start = lay.n_head + i * lay.rest
+                out_ref[2 * source + line, :, lay.head :] = values[:, start : start + lay.rest]
+
+        write(grp, total[...])
+        total[:, : lay.n_first] = first_other[...]
+        total[:, lay.n_first :] = jnp.zeros((1, lay.n_late), jnp.float32)
+        turn_sums(back, lay.n_late, total, lay.n_first)
+        write(1 - grp, total[...])
 
     @pl.when(jnp.logical_not(is_home))
     def _():
-        values = jnp.log(jnp.where(first_lane[...] >= 0, first_sums[...], 1.0))
+        out_ref[...] = jnp.zeros(out_ref.shape, jnp.float32)
+        values = jnp.where(first_lane[...] >= 0, first_sums[...], 1.0)
         for source in range(lay.n_owner):
             start = source * lay.main
-            out_ref[source, :, : lay.main] = values[:, start : start + lay.main]
+            out_ref[2 * source + grp, :, : lay.main] = values[:, start : start + lay.main]
 
 
 def pair_call(kernel, lay, arrays, out_shape, scratch, out_specs=None, pairs=0):
@@ -677,14 +707,14 @@
     pos = pos_ref[...]
     lane = lax.rem(pos, LANES)
     line = lax.div(pos, LANES)
-    out = jnp.zeros(pos.shape, jnp.float32)
+    out = jnp.ones(pos.shape, jnp.float32)
     per = values_ref.shape[2] // LANES
-    for r in range(values_ref.shape[0] * per):
-        start = r % per * LANES
-        table = jnp.broadcast_to(values_ref[r // per, :, start : start + LANES], pos.shape)
-        found = jnp.take_along_axis(table, lane, axis=1)
+    for r in range(values_ref.shape[0] // 2 * per):
+        owner, part = r // per, slice(r % per * LANES, (r % per + 1) * LANES)
+        table = values_ref[2 * owner, :, part] + values_ref[2 * owner + 1, :, part]
+        found = jnp.take_along_axis(jnp.broadcast_to(table, pos.shape), lane, axis=1)
         out = jnp.where(line == r, found, out)
-    out_ref[...] = out
+    out_ref[...] = jnp.log(out)
 
 
 def fast_unpack(values, pos):
@@ -755,13 +785,13 @@
     sums, first_lane, lab_sub, heads_i = pair_call(
         inner_kernel, lay, (mine, early), (row, row, side, heads), (bias, first_side)
     )
-    specs = vmem_specs(1) + (pl.BlockSpec(memory_space=pltpu.SMEM),) + vmem_specs(2)
-    sums, unfit, lab_sub_j, heads_j = pair_call(
+    specs = vmem_specs(2) + (pl.BlockSpec(memory_space=pltpu.SMEM),) + vmem_specs(2)
+    sums, first_other, unfit, _, _ = pair_call(
         cross_kernel,
         lay,
         (mine, other, early, early_j, heads_i, sums, first_lane),
-        (row, array((1, 1), jnp.int32), side, heads),
-        (bias,),
+        (row, row, array((1, 1), jnp.int32), side, heads),
+        (bias, first_side),
         specs,
     )
     late = lay_out(late, home, (sums,))
@@ -769,7 +799,7 @@
     late_sums, lane = pair_call(
         inner_late_kernel,
         lay,
-        (mine, early, late, heads_i, lab_sub, first_lane),
+        (mine, early, late, heads_i, first_lane),
         (long_row, long_row),
         (late_side, late_side),
         pairs=lay.n_late * (lay.n_all + lay.n_first),
@@ -777,14 +807,13 @@
     (results,) = pair_call(
         cross_late_kernel,
         lay,
-        (
-            *(other, early, late, early_j, late_j, heads_i, heads_j),
-            *(lab_sub_j, first_lane, sums, lane, late_sums),
-        ),
-        (array((n_owner, 1, capacity)),),
-        (scratch(long_row.shape), late_side),
-    )
-    returned = lax.all_to_all(results, "cl", split_axis=0, concat_axis=0, tiled=True)
+        (other, early, late, late_j, heads_i, first_lane, sums, first_other, lane, late_sums),
+        (array((2 * n_owner, 1, capacity)),),
+        (scratch(long_row.shape), late_side, late_side),
+    )
+    returned = lax.all_to_all(
+        results, ("cl", "grp"), split_axis=0, concat_axis=0, tiled=True
+    )
     return lax.cond(
         unfit[0, 0] == 0,
         lambda: fast_unpack(returned, pos).reshape(rows),

time: 86.1 us -> 84.9 us (0.986)
  starting transfers between devices: 25.1 us -> 20.9 us
  Pallas kernels: 14.9 us -> 16.7 us
  waiting for transfers between devices: 44.3 us -> 45.5 us
    all_to_all x1, starting transfers between devices: 7.26 us -> 4.27 us  [body(): lax.all_to_all(results, ('cl', 'grp'), split_axis=0, concat_axis=0, tiled...]
    pallas_call x4, Pallas kernels: 9.58 us -> 11.4 us  [pair_call(): pl.pallas_call(functools.partial(kernel, lay), out_shape=out_shape, in_sp...]
    ppermute x8, waiting for transfers between devices: 26.6 us -> 27.8 us  [hop(): return lax.ppermute(x, 'cl', pairs)]
    ppermute x8, starting transfers between devices: 9.85 us -> 8.61 us  [hop(): return lax.ppermute(x, 'cl', pairs)]
  transfers between devices with their start and end apart: 13 -> 13, of which waited for: 5 -> 5; matrix products, arithmetic and copies ran while one was open for 0% -> 0% of each run, Pallas kernels for 10% -> 13%
where the time goes in v18:
time: 84.9 us; the launch traced here: 84.5 us
  waiting for transfers between devices  45.5 us (54%)
  starting transfers between devices  20.9 us (25%)
  Pallas kernels  16.7 us (20%)
    ppermute x8, waiting for transfers between devices, hop(): return lax.ppermute(x, 'cl', pairs)  27.8 us
    pallas_call x4, Pallas kernels, pair_call(): pl.pallas_call(functools.partial(kernel, lay), out_shape=out_shape, in_sp...  11.4 us
    ppermute x8, starting transfers between devices, hop(): return lax.ppermute(x, 'cl', pairs)  8.61 us
    all_to_all x1, waiting for transfers between devices, body(): lax.all_to_all(packed.reshape(n_owner, main, width), 'cl', split_axis=0,...  7.43 us
    all_to_all x1, starting transfers between devices, body(): lax.all_to_all(packed.reshape(n_owner, main, width), 'cl', split_axis=0,...  7.29 us
    all_to_all x1, waiting for transfers between devices, body(): lax.all_to_all(results, ('cl', 'grp'), split_axis=0, concat_axis=0, tiled...  5.85 us
    pallas_call x1, Pallas kernels, place_rows(): pl.pallas_call(functools.partial(place_kernel, lay), out_shape=(jax.Shape...  5.22 us
    ppermute x3, waiting for transfers between devices, swap(): return lax.ppermute(x, 'grp', [(0, 1), (1, 0)])  4.44 us
  transfers between devices with their start and end apart: 13, of which 5 were waited for; matrix products, arithmetic and copies ran while one was open for 0% of the time, Pallas kernels for 13%

profile of v18, /device:TPU:0, one launch (start us, length us, event | category | flops | bytes accessed | tf_op | source)
XLA Modules:
  0.0 84.5 jit_solution(15206792889331543674)
XLA Ops:
  0.0 5.2 %shard_map.39 = (bf16[1152,768]{1,0:T(8,128)(2,1)}, bf16[128,768]{1,0:T(8,128)(2,1)S(1)}, s32[8,128]{1,0:T(8,128)S(1)}) custom-call(bf16[1024,768]{1,0:T(8,128)(2,1)} %x_hbm.1, s32[8,128]{1,0:T(8,128)} %bitcast.23, s32[1,64]{1,0:T(1,128)} %bitcast.27), custom_call_target="tpu_custom_call" | custom-call | tf_op jit(solution)/shard_map/pallas_call | solution.py:311
  5.2 7.3 %all-to-all-start.2 = ((bf16[8,144,768]{2,1,0:T(8,128)(2,1)}), bf16[8,144,768]{2,1,0:T(8,128)(2,1)S(1)}, u32[]{:S(2)}, u32[]{:S(2)}) async-start(bf16[8,144,768]{2,1,0:T(8,128)(2,1)} %bitcast.12), calls=%async_computation.2 | async-start | bytes 3538944 | tf_op jit(solution)/shard_map/all_to_all | solution.py:768
  12.5 3.9 %collective-permute-start.1 = (bf16[128,768]{1,0:T(8,128)(2,1)S(1)}, bf16[128,768]{1,0:T(8,128)(2,1)S(1)}, u32[]{:S(2)}, u32[]{:S(2)}) collective-permute-start(bf16[128,768]{1,0:T(8,128)(2,1)S(1)} %get-tuple-element.38.refs_2_), channel_id=1, source_target_pairs={{0,4},{1,5},{16,20},{17,21}} | collective-permute-start | bytes 589832 | tf_op jit(solution)/shard_map/ppermute | solution.py:760
  16.5 0.7 collective-permute-start.2
  17.1 0.7 collective-permute-start.3
  17.8 0.7 collective-permute-start.4
  18.5 27.8 %collective-permute-done.1.refs_0_ = bf16[128,768]{1,0:T(8,128)(2,1)S(1)} collective-permute-done((bf16[128,768]{1,0:T(8,128)(2,1)S(1)}, bf16[128,768]{1,0:T(8,128)(2,1)S(1)}, u32[]{:S(2)}, u32[]{:S(2)}) %collective-permute-start.1) | collective-permute-done | bytes 196640 | tf_op jit(solution)/shard_map/ppermute | solution.py:760
  46.3 0.0 collective-permute-done.2.refs_1_
  46.3 0.0 collective-permute-done.3.refs_3_
  46.3 0.0 collective-permute-done.4.refs_2_
  46.3 7.4 %all-to-all-done.2 = bf16[8,144,768]{2,1,0:T(8,128)(2,1)S(1)} async-done(((bf16[8,144,768]{2,1,0:T(8,128)(2,1)}), bf16[8,144,768]{2,1,0:T(8,128)(2,1)S(1)}, u32[]{:S(2)}, u32[]{:S(2)}) %all-to-all-start.2) | async-done | bytes 1769504 | tf_op jit(solution)/shard_map/all_to_all | solution.py:768
  53.7 0.0 collective-permute-start.5
  53.7 0.5 collective-permute-start.6
  54.3 0.7 collective-permute-start.7
  54.9 0.7 collective-permute-start.9
  55.6 0.7 collective-permute-start.10
  56.3 2.3 %collective-permute-done.6.early_j = bf16[512,768]{1,0:T(8,128)(2,1)S(1)} collective-permute-done((bf16[512,768]{1,0:T(8,128)(2,1)S(1)}, bf16[512,768]{1,0:T(8,128)(2,1)S(1)}, u32[]{:S(2)}, u32[]{:S(2)}) %collective-permute-start.6) | collective-permute-done | bytes 786464 | tf_op jit(solution)/shard_map/ppermute | solution.py:763
  58.6 0.7 collective-permute-start.8
  59.2 4.9 %shard_map.42 = (f32[1,1536]{1,0:T(1,128)S(1)}, f32[1,1536]{1,0:T(1,128)S(1)}, f32[1536,128]{1,0:T(8,128)}, bf16[1024,768]{1,0:T(8,128)(2,1)S(1)}) custom-call(bf16[1152,768]{1,0:T(8,128)(2,1)S(1)} %shard_map.41.mine, bf16[512,768]{1,0:T(8,128)(2,1)S(1)} %shard_map.40.refs_1_.early), custom_call_target="tpu_custom_call" | custom-call | bytes 1 | tf_op jit(solution)/shard_map/pallas_call | solution.py:693
  64.1 0.0 collective-permute-done.5.other
  64.1 5.8 %shard_map.43 = (f32[1,1536]{1,0:T(1,128)S(1)}, f32[1,1536]{1,0:T(1,128)S(1)}, s32[1,1]{1,0:T(1,128)}, f32[1536,128]{1,0:T(8,128)}, bf16[1024,768]{1,0:T(8,128)(2,1)}) custom-call(bf16[1152,768]{1,0:T(8,128)(2,1)S(1)} %shard_map.41.mine, bf16[1152,768]{1,0:T(8,128)(2,1)S(1)} %collective-permute-done.5.other, bf16[512,768]{1,0:T(8,128)(2,1)S(1)} %shard_map.40.refs_1_.early, ...), custom_call_target="tpu_custom_call" | custom-call | bytes 1 | tf_op jit(solution)/shard_map/pallas_call | solution.py:693
  69.9 0.0 collective-permute-done.7.refs_0_
  70.0 0.0 collective-permute-done.9.refs_2_
  70.0 0.0 collective-permute-done.10.refs_3_
  70.0 0.0 collective-permute-done.8.refs_1_
  70.0 0.2 collective-permute-start.11
  70.2 2.2 %collective-permute-done.11.late_j = bf16[512,768]{1,0:T(8,128)(2,1)S(1)} collective-permute-done((bf16[512,768]{1,0:T(8,128)(2,1)S(1)}, bf16[512,768]{1,0:T(8,128)(2,1)S(1)}, u32[]{:S(2)}, u32[]{:S(2)}) %collective-permute-start.11) | collective-permute-done | bytes 786464 | tf_op jit(solution)/shard_map/ppermute | solution.py:763
  72.4 0.0 copy-start.1
  72.4 0.0 copy-start.3
  72.4 0.0 copy-start.5
  72.4 0.7 shard_map.46
  73.0 4.3 %all-to-all-start.3 = ((f32[16,1,256]{2,1,0:T(1,128)}), f32[16,1,256]{2,1,0:T(1,128)S(1)}, u32[]{:S(2)}, u32[]{:S(2)}) async-start(f32[16,1,256]{2,1,0:T(1,128)} %shard_map.46), calls=%async_computation.3 | async-start | bytes 32768 | tf_op jit(solution)/shard_map/all_to_all | solution.py:814
  78.0 5.8 %all-to-all-done.3 = f32[16,1,256]{2,1,0:T(1,128)S(1)} async-done(((f32[16,1,256]{2,1,0:T(1,128)}), f32[16,1,256]{2,1,0:T(1,128)S(1)}, u32[]{:S(2)}, u32[]{:S(2)}) %all-to-all-start.3) | async-done | bytes 16416 | tf_op jit(solution)/shard_map/all_to_all | solution.py:814
  83.8 0.0 copy-done.1
  83.8 0.0 copy-done.3
  83.8 0.0 copy-done.5
  83.8 0.1 conditional.1
  83.8 0.1 branch_1_fun.1
  83.9 0.0 copy-start.4
  83.9 0.6 copy-done.4
  (4 shorter events, 0.0 us)
Async XLA Ops:
  5.2 48.5 %all-to-all-start.2 = ((bf16[8,144,768]{2,1,0:T(8,128)(2,1)}), bf16[8,144,768]{2,1,0:T(8,128)(2,1)S(1)}, u32[]{:S(2)}, u32[]{:S(2)}) async-start(bf16[8,144,768]{2,1,0:T(8,128)(2,1)} %bitcast.12), calls=%async_computation.2 | async-start | bytes 3538944 | tf_op jit(solution)/shard_map/all_to_all | solution.py:768
  12.5 33.8 %collective-permute-start.1 = (bf16[128,768]{1,0:T(8,128)(2,1)S(1)}, bf16[128,768]{1,0:T(8,128)(2,1)S(1)}, u32[]{:S(2)}, u32[]{:S(2)}) collective-permute-start(bf16[128,768]{1,0:T(8,128)(2,1)S(1)} %get-tuple-element.38.refs_2_), channel_id=1, source_target_pairs={{0,4},{1,5},{16,20},{17,21}} | collective-permute-start | bytes 589832 | tf_op jit(solution)/shard_map/ppermute | solution.py:760
  16.5 29.8 %collective-permute-start.2 = (bf16[128,768]{1,0:T(8,128)(2,1)S(1)}, bf16[128,768]{1,0:T(8,128)(2,1)S(1)}, u32[]{:S(2)}, u32[]{:S(2)}) collective-permute-start(bf16[128,768]{1,0:T(8,128)(2,1)S(1)} %get-tuple-element.38.refs_2_), channel_id=1, source_target_pairs={{2,4},{3,5},{18,20},{19,21}} | collective-permute-start | bytes 589832 | tf_op jit(solution)/shard_map/ppermute | solution.py:760
  17.1 29.2 %collective-permute-start.3 = (bf16[128,768]{1,0:T(8,128)(2,1)S(1)}, bf16[128,768]{1,0:T(8,128)(2,1)S(1)}, u32[]{:S(2)}, u32[]{:S(2)}) collective-permute-start(bf16[128,768]{1,0:T(8,128)(2,1)S(1)} %get-tuple-element.38.refs_2_), channel_id=1, source_target_pairs={{6,4},{7,5},{22,20},{23,21}} | collective-permute-start | bytes 589832 | tf_op jit(solution)/shard_map/ppermute | solution.py:760
  17.8 28.5 %collective-permute-start.4 = (bf16[128,768]{1,0:T(8,128)(2,1)S(1)}, bf16[128,768]{1,0:T(8,128)(2,1)S(1)}, u32[]{:S(2)}, u32[]{:S(2)}) collective-permute-start(bf16[128,768]{1,0:T(8,128)(2,1)S(1)} %get-tuple-element.38.refs_2_), channel_id=1, source_target_pairs={{12,8},{14,10},{13,9},{15,11},{28,24},{30,26},{29,25},{31,27}} | collective-permute-start | bytes 589832 | tf_op jit(solution)/shard_map/ppermute | solution.py:760
  53.7 10.4 %collective-permute-start.5 = (bf16[1152,768]{1,0:T(8,128)(2,1)S(1)}, bf16[1152,768]{1,0:T(8,128)(2,1)S(1)}, u32[]{:S(2)}, u32[]{:S(2)}) collective-permute-start(bf16[1152,768]{1,0:T(8,128)(2,1)S(1)} %shard_map.41.mine), channel_id=1, source_target_pairs={{0,1},{1,0},{2,3},{3,2},{4,5},{5,4},{6,7},{7,6},{8,9},{9,8},{10,11... | collective-permute-start | bytes 5308424 | tf_op jit(solution)/shard_map/ppermute | solution.py:763
  53.7 4.8 %collective-permute-start.6 = (bf16[512,768]{1,0:T(8,128)(2,1)S(1)}, bf16[512,768]{1,0:T(8,128)(2,1)S(1)}, u32[]{:S(2)}, u32[]{:S(2)}) collective-permute-start(bf16[512,768]{1,0:T(8,128)(2,1)S(1)} %shard_map.40.refs_1_.early), channel_id=1, source_target_pairs={{0,1},{1,0},{2,3},{3,2},{4,5},{5,4},{6,7},{7,6},{8,9},{9,8},{10,11... | collective-permute-start | bytes 2359304 | tf_op jit(solution)/shard_map/ppermute | solution.py:763
  54.3 15.7 %collective-permute-start.7 = (bf16[128,768]{1,0:T(8,128)(2,1)S(1)}, bf16[128,768]{1,0:T(8,128)(2,1)S(1)}, u32[]{:S(2)}, u32[]{:S(2)}) collective-permute-start(bf16[128,768]{1,0:T(8,128)(2,1)S(1)} %get-tuple-element.38.refs_2_), channel_id=1, source_target_pairs={{8,4},{9,5},{24,20},{25,21}} | collective-permute-start | bytes 589832 | tf_op jit(solution)/shard_map/ppermute | solution.py:760
  54.9 15.0 %collective-permute-start.9 = (bf16[128,768]{1,0:T(8,128)(2,1)S(1)}, bf16[128,768]{1,0:T(8,128)(2,1)S(1)}, u32[]{:S(2)}, u32[]{:S(2)}) collective-permute-start(bf16[128,768]{1,0:T(8,128)(2,1)S(1)} %get-tuple-element.38.refs_2_), channel_id=1, source_target_pairs={{10,4},{11,5},{26,20},{27,21}} | collective-permute-start | bytes 589832 | tf_op jit(solution)/shard_map/ppermute | solution.py:760
  55.6 14.4 %collective-permute-start.10 = (bf16[128,768]{1,0:T(8,128)(2,1)S(1)}, bf16[128,768]{1,0:T(8,128)(2,1)S(1)}, u32[]{:S(2)}, u32[]{:S(2)}) collective-permute-start(bf16[128,768]{1,0:T(8,128)(2,1)S(1)} %collective-permute-done.4.refs_2_), channel_id=1, source_target_pairs={{10,4},{11,5},{26,20},{27,21}} | collective-permute-start | bytes 589832 | tf_op jit(solution)/shard_map/ppermute | solution.py:760
  58.6 11.4 %collective-permute-start.8 = (bf16[128,768]{1,0:T(8,128)(2,1)S(1)}, bf16[128,768]{1,0:T(8,128)(2,1)S(1)}, u32[]{:S(2)}, u32[]{:S(2)}) collective-permute-start(bf16[128,768]{1,0:T(8,128)(2,1)S(1)} %collective-permute-done.4.refs_2_), channel_id=1, source_target_pairs={{8,4},{9,5},{24,20},{25,21}} | collective-permute-start | bytes 589832 | tf_op jit(solution)/shard_map/ppermute | solution.py:760
  70.0 2.4 %collective-permute-start.11 = (bf16[512,768]{1,0:T(8,128)(2,1)S(1)}, bf16[512,768]{1,0:T(8,128)(2,1)S(1)}, u32[]{:S(2)}, u32[]{:S(2)}) collective-permute-start(bf16[512,768]{1,0:T(8,128)(2,1)S(1)} %shard_map.44.late), channel_id=1, source_target_pairs={{0,1},{1,0},{2,3},{3,2},{4,5},{5,4},{6,7},{7,6},{8,9},{9,8},{10,11... | collective-permute-start | bytes 2359304 | tf_op jit(solution)/shard_map/ppermute | solution.py:763
  72.4 11.5 %copy-start.1 = (bf16[1024,768]{1,0:T(8,128)(2,1)S(1)}, bf16[1024,768]{1,0:T(8,128)(2,1)}, u32[]{:S(2)}) copy-start(bf16[1024,768]{1,0:T(8,128)(2,1)} %x_hbm.1) | copy-start | bytes 4718596
  72.4 11.5 %copy-start.3 = (s32[1024]{0:T(1024)S(1)}, s32[1024]{0:T(1024)}, u32[]{:S(2)}) copy-start(s32[1024]{0:T(1024)} %param.6) | copy-start | bytes 12292
  72.4 11.5 %copy-start.5 = (s32[64]{0:T(128)S(1)}, s32[64]{0:T(128)}, u32[]{:S(2)}) copy-start(s32[64]{0:T(128)} %param.7) | copy-start | bytes 772
  73.0 10.8 %all-to-all-start.3 = ((f32[16,1,256]{2,1,0:T(1,128)}), f32[16,1,256]{2,1,0:T(1,128)S(1)}, u32[]{:S(2)}, u32[]{:S(2)}) async-start(f32[16,1,256]{2,1,0:T(1,128)} %shard_map.46), calls=%async_computation.3 | async-start | bytes 32768 | tf_op jit(solution)/shard_map/all_to_all | solution.py:814
  83.9 0.6 copy-start.4

commit v19 on v18

--- a/solution.py
+++ b/solution.py
@@ -371,7 +371,7 @@
 
 
 class Layout:
-    early, late = (0, 1, 2, 3), (4, 6, 5, 7)
+    early, late = (0, 1, 2, 3, 4, 5), (6, 7)
 
     def __init__(self, n_owner, n_fine, capacity, main, home):
         self.n_owner, self.n_fine, self.capacity = n_owner, n_fine, capacity
@@ -534,6 +534,15 @@
     return put
 
 
+def blocks_of(lay, rows, early):
+    blocks = []
+    for ref, count, at in ((rows, lay.n_head, 0), (early, lay.n_early, lay.n_head)):
+        for start in range(0, count, WIDE):
+            size = min(WIDE, count - start)
+            blocks.append((ref.at[pl.ds(start, size)], size, at + start))
+    return blocks
+
+
 def inner_kernel(lay, mine, early, sums, lab_lane, lab_sub, rows, bias, back, buf_a, buf_b):
     is_home = lax.axis_index("cl") == lay.home
     infos = lines_of(lay, mine)
@@ -545,13 +554,11 @@
         first_labels(lay, infos, lab_sub)
         turn_labels(lay, lab_sub, lay.n_first, lab_lane, 0)
         back[...] = jnp.zeros(back.shape, jnp.float32)
-        size = lay.n_early
-        blocks = [(rows.at[pl.ds(start, size)], start) for start in range(0, lay.n_head, size)]
-        blocks.append((early, lay.n_head))
-        for i, (ref, at) in enumerate(blocks):
+        blocks = blocks_of(lay, rows, early)
+        for i, (ref, size, at) in enumerate(blocks):
             tiles = [
-                (ref_j, size, lab_sub, None, at_j, 2, None if at_j == at else back)
-                for ref_j, at_j in blocks[i:]
+                (ref_j, size_j, lab_sub, None, at_j, 2, None if at_j == at else back)
+                for ref_j, size_j, at_j in blocks[i:]
             ]
             stream((ref, size, at), tiles, lab_lane, buffers, setter(sums))
         turn_sums(back, lay.n_first, sums, 0)
@@ -600,20 +607,24 @@
         copy_head(lay, other, rows_j)
         first_labels(lay, infos, lab_sub)
         back[...] = jnp.zeros(back.shape, jnp.float32)
-        size = lay.n_early
-        blocks_i = [rows.at[pl.ds(start, size)] for start in range(0, lay.n_head, size)] + [early]
-        blocks_j = [rows_j.at[pl.ds(start, size)] for start in range(0, lay.n_head, size)]
-        blocks_j.append(early_j)
+        blocks_i = blocks_of(lay, rows, early)
+        blocks_j = blocks_of(lay, rows_j, early_j)
         put, n = adder(total), len(blocks_i)
-        for i, ref in enumerate(blocks_i):
+
+        def is_taken(i, j):
+            step = (j - i) % n
+            return 0 < 2 * step < n or (2 * step == n and i < j)
+
+        for i, (ref, size, at) in enumerate(blocks_i):
             tiles = [
-                (blocks_j[j], size, lab_sub, None, j * size, 2, back)
-                for j in ((i + step) % n for step in range(1, (n + 1) // 2))
+                (ref_j, size_j, lab_sub, None, at_j, 2, back)
+                for j, (ref_j, size_j, at_j) in enumerate(blocks_j)
+                if is_taken(i, j)
             ]
-            stream((ref, size, i * size), tiles, lab_lane, buffers, put)
-            half_blocks(
-                ref, blocks_j[i], lab_sub, i * size, back, i * size, lab_lane, buffers, put
-            )
+            if tiles:
+                stream((ref, size, at), tiles, lab_lane, buffers, put)
+            ref_j = blocks_j[i][0]
+            half_blocks(ref, ref_j, lab_sub, at, back, at, lab_lane, buffers, put)
         for_other[...] = jnp.zeros(for_other.shape, jnp.float32)
         turn_sums(back, lay.n_first, for_other, 0)
 
@@ -770,7 +781,7 @@
     ).reshape(n_owner * main, width)
     mine = after(mine, early, moved)
     other, early_j = swap(mine), swap(early)
-    late = [hop(x, [(s, home)]) for s in (4, 5) for x in (extra, moved)]
+    late = [hop(moved, [(s, home)]) for s in (4, 5)]
 
     def array(shape, dtype=jnp.float32):
         return jax.ShapeDtypeStruct(shape, dtype)

time: 84.9 us -> 90.7 us (1.068)
  starting transfers between devices: 20.9 us -> 29.4 us
  waiting for transfers between devices: 45.5 us -> 42.8 us
    all_to_all x1, starting transfers between devices: 4.27 us -> 12.9 us  [body(): lax.all_to_all(results, ('cl', 'grp'), split_axis=0, concat_axis=0, tiled...]
    ppermute x3, waiting for transfers between devices: 4.44 us -> 1.69 us  [swap(): return lax.ppermute(x, 'grp', [(0, 1), (1, 0)])]
  transfers between devices with their start and end apart: 13 -> 13, of which waited for: 5 -> 4; matrix products, arithmetic and copies ran while one was open for 0% -> 0% of each run, Pallas kernels for 13% -> 12%
where the time goes in v19:
time: 90.7 us; the launch traced here: 90.3 us
  waiting for transfers between devices  42.8 us (47%)
  starting transfers between devices  29.4 us (32%)
  Pallas kernels  16.7 us (18%)
    ppermute x8, waiting for transfers between devices, hop(): return lax.ppermute(x, 'cl', pairs)  27.1 us
    all_to_all x1, starting transfers between devices, body(): lax.all_to_all(results, ('cl', 'grp'), split_axis=0, concat_axis=0, tiled...  12.9 us
    pallas_call x4, Pallas kernels, pair_call(): pl.pallas_call(functools.partial(kernel, lay), out_shape=out_shape, in_sp...  11.3 us
    ppermute x8, starting transfers between devices, hop(): return lax.ppermute(x, 'cl', pairs)  8.61 us
    all_to_all x1, waiting for transfers between devices, body(): lax.all_to_all(packed.reshape(n_owner, main, width), 'cl', split_axis=0,...  8.12 us
    all_to_all x1, starting transfers between devices, body(): lax.all_to_all(packed.reshape(n_owner, main, width), 'cl', split_axis=0,...  7.29 us
    all_to_all x1, waiting for transfers between devices, body(): lax.all_to_all(results, ('cl', 'grp'), split_axis=0, concat_axis=0, tiled...  5.85 us
    pallas_call x1, Pallas kernels, place_rows(): pl.pallas_call(functools.partial(place_kernel, lay), out_shape=(jax.Shape...  5.22 us
  transfers between devices with their start and end apart: 13, of which 4 were waited for; matrix products, arithmetic and copies ran while one was open for 0% of the time, Pallas kernels for 12%

profile of v19, /device:TPU:0, one launch (start us, length us, event | category | flops | bytes accessed | tf_op | source)
XLA Modules:
  0.0 90.3 jit_solution(15958534858801193221)
XLA Ops:
  0.0 5.2 %shard_map.39 = (bf16[1152,768]{1,0:T(8,128)(2,1)}, bf16[128,768]{1,0:T(8,128)(2,1)S(1)}, s32[8,128]{1,0:T(8,128)S(1)}) custom-call(bf16[1024,768]{1,0:T(8,128)(2,1)} %x_hbm.1, s32[8,128]{1,0:T(8,128)} %bitcast.23, s32[1,64]{1,0:T(1,128)} %bitcast.27), custom_call_target="tpu_custom_call" | custom-call | tf_op jit(solution)/shard_map/pallas_call | solution.py:311
  5.2 7.3 %all-to-all-start.2 = ((bf16[8,144,768]{2,1,0:T(8,128)(2,1)}), bf16[8,144,768]{2,1,0:T(8,128)(2,1)S(1)}, u32[]{:S(2)}, u32[]{:S(2)}) async-start(bf16[8,144,768]{2,1,0:T(8,128)(2,1)} %bitcast.12), calls=%async_computation.2 | async-start | bytes 3538944 | tf_op jit(solution)/shard_map/all_to_all | solution.py:779
  12.5 3.9 %collective-permute-start.1 = (bf16[128,768]{1,0:T(8,128)(2,1)S(1)}, bf16[128,768]{1,0:T(8,128)(2,1)S(1)}, u32[]{:S(2)}, u32[]{:S(2)}) collective-permute-start(bf16[128,768]{1,0:T(8,128)(2,1)S(1)} %get-tuple-element.38.refs_2_), channel_id=1, source_target_pairs={{0,4},{1,5},{16,20},{17,21}} | collective-permute-start | bytes 589832 | tf_op jit(solution)/shard_map/ppermute | solution.py:771
  16.5 0.7 collective-permute-start.2
  17.1 0.7 collective-permute-start.3
  17.8 0.7 collective-permute-start.4
  18.5 0.7 collective-permute-start.5
  19.2 27.1 %collective-permute-done.1.refs_0_ = bf16[128,768]{1,0:T(8,128)(2,1)S(1)} collective-permute-done((bf16[128,768]{1,0:T(8,128)(2,1)S(1)}, bf16[128,768]{1,0:T(8,128)(2,1)S(1)}, u32[]{:S(2)}, u32[]{:S(2)}) %collective-permute-start.1) | collective-permute-done | bytes 196640 | tf_op jit(solution)/shard_map/ppermute | solution.py:771
  46.3 0.7 collective-permute-start.6
  47.0 0.0 collective-permute-done.2.refs_1_
  47.0 0.0 collective-permute-done.3.refs_3_
  47.0 0.0 collective-permute-done.4.refs_4_
  47.0 0.0 collective-permute-done.5.refs_5_
  47.0 0.0 collective-permute-done.6.refs_2_
  47.0 8.1 %all-to-all-done.2 = bf16[8,144,768]{2,1,0:T(8,128)(2,1)S(1)} async-done(((bf16[8,144,768]{2,1,0:T(8,128)(2,1)}), bf16[8,144,768]{2,1,0:T(8,128)(2,1)S(1)}, u32[]{:S(2)}, u32[]{:S(2)}) %all-to-all-start.2) | async-done | bytes 1769504 | tf_op jit(solution)/shard_map/all_to_all | solution.py:779
  55.2 0.0 collective-permute-start.7
  55.2 0.5 collective-permute-start.8
  55.7 0.7 collective-permute-start.10
  56.3 0.7 collective-permute-start.9
  57.0 4.9 %shard_map.42 = (f32[1,1792]{1,0:T(1,128)S(1)}, f32[1,1792]{1,0:T(1,128)S(1)}, f32[1792,128]{1,0:T(8,128)}, bf16[1024,768]{1,0:T(8,128)(2,1)S(1)}) custom-call(bf16[1152,768]{1,0:T(8,128)(2,1)S(1)} %shard_map.41.mine, bf16[768,768]{1,0:T(8,128)(2,1)S(1)} %shard_map.40.refs_1_.early), custom_call_target="tpu_custom_call" | custom-call | bytes 1 | tf_op jit(solution)/shard_map/pallas_call | solution.py:704
  61.9 0.0 collective-permute-done.8.early_j
  61.9 0.0 collective-permute-done.7.other
  61.9 5.8 %shard_map.43 = (f32[1,1792]{1,0:T(1,128)S(1)}, f32[1,1792]{1,0:T(1,128)S(1)}, s32[1,1]{1,0:T(1,128)}, f32[1792,128]{1,0:T(8,128)}, bf16[1024,768]{1,0:T(8,128)(2,1)}) custom-call(bf16[1152,768]{1,0:T(8,128)(2,1)S(1)} %shard_map.41.mine, bf16[1152,768]{1,0:T(8,128)(2,1)S(1)} %collective-permute-done.7.other, bf16[768,768]{1,0:T(8,128)(2,1)S(1)} %shard_map.40.refs_1_.early, ...), custom_call_target="tpu_custom_call" | custom-call | bytes 1 | tf_op jit(solution)/shard_map/pallas_call | solution.py:704
  67.7 0.0 collective-permute-done.10.refs_1_
  67.7 0.0 collective-permute-done.9.refs_0_
  67.8 0.1 collective-permute-start.11
  67.9 1.7 %collective-permute-done.11.late_j = bf16[256,768]{1,0:T(8,128)(2,1)S(1)} collective-permute-done((bf16[256,768]{1,0:T(8,128)(2,1)S(1)}, bf16[256,768]{1,0:T(8,128)(2,1)S(1)}, u32[]{:S(2)}, u32[]{:S(2)}) %collective-permute-start.11) | collective-permute-done | bytes 393248 | tf_op jit(solution)/shard_map/ppermute | solution.py:774
  69.5 0.0 copy-start.1
  69.5 0.0 copy-start.3
  69.5 0.0 copy-start.5
  69.5 0.7 shard_map.46
  70.2 12.9 %all-to-all-start.3 = ((f32[16,1,256]{2,1,0:T(1,128)}), f32[16,1,256]{2,1,0:T(1,128)S(1)}, u32[]{:S(2)}, u32[]{:S(2)}) async-start(f32[16,1,256]{2,1,0:T(1,128)} %shard_map.46), calls=%async_computation.3 | async-start | bytes 32768 | tf_op jit(solution)/shard_map/all_to_all | solution.py:825
  83.8 5.8 %all-to-all-done.3 = f32[16,1,256]{2,1,0:T(1,128)S(1)} async-done(((f32[16,1,256]{2,1,0:T(1,128)}), f32[16,1,256]{2,1,0:T(1,128)S(1)}, u32[]{:S(2)}, u32[]{:S(2)}) %all-to-all-start.3) | async-done | bytes 16416 | tf_op jit(solution)/shard_map/all_to_all | solution.py:825
  89.6 0.0 copy-done.1
  89.6 0.0 copy-done.3
  89.6 0.0 copy-done.5
  89.6 0.1 conditional.1
  89.6 0.1 branch_1_fun.1
  89.7 0.0 copy-start.4
  89.8 0.6 copy-done.4
  (4 shorter events, 0.0 us)
Async XLA Ops:
  5.2 49.9 %all-to-all-start.2 = ((bf16[8,144,768]{2,1,0:T(8,128)(2,1)}), bf16[8,144,768]{2,1,0:T(8,128)(2,1)S(1)}, u32[]{:S(2)}, u32[]{:S(2)}) async-start(bf16[8,144,768]{2,1,0:T(8,128)(2,1)} %bitcast.12), calls=%async_computation.2 | async-start | bytes 3538944 | tf_op jit(solution)/shard_map/all_to_all | solution.py:779
  12.5 33.8 %collective-permute-start.1 = (bf16[128,768]{1,0:T(8,128)(2,1)S(1)}, bf16[128,768]{1,0:T(8,128)(2,1)S(1)}, u32[]{:S(2)}, u32[]{:S(2)}) collective-permute-start(bf16[128,768]{1,0:T(8,128)(2,1)S(1)} %get-tuple-element.38.refs_2_), channel_id=1, source_target_pairs={{0,4},{1,5},{16,20},{17,21}} | collective-permute-start | bytes 589832 | tf_op jit(solution)/shard_map/ppermute | solution.py:771
  16.5 30.5 %collective-permute-start.2 = (bf16[128,768]{1,0:T(8,128)(2,1)S(1)}, bf16[128,768]{1,0:T(8,128)(2,1)S(1)}, u32[]{:S(2)}, u32[]{:S(2)}) collective-permute-start(bf16[128,768]{1,0:T(8,128)(2,1)S(1)} %get-tuple-element.38.refs_2_), channel_id=1, source_target_pairs={{2,4},{3,5},{18,20},{19,21}} | collective-permute-start | bytes 589832 | tf_op jit(solution)/shard_map/ppermute | solution.py:771
  17.1 29.8 %collective-permute-start.3 = (bf16[128,768]{1,0:T(8,128)(2,1)S(1)}, bf16[128,768]{1,0:T(8,128)(2,1)S(1)}, u32[]{:S(2)}, u32[]{:S(2)}) collective-permute-start(bf16[128,768]{1,0:T(8,128)(2,1)S(1)} %get-tuple-element.38.refs_2_), channel_id=1, source_target_pairs={{6,4},{7,5},{22,20},{23,21}} | collective-permute-start | bytes 589832 | tf_op jit(solution)/shard_map/ppermute | solution.py:771
  17.8 29.2 %collective-permute-start.4 = (bf16[128,768]{1,0:T(8,128)(2,1)S(1)}, bf16[128,768]{1,0:T(8,128)(2,1)S(1)}, u32[]{:S(2)}, u32[]{:S(2)}) collective-permute-start(bf16[128,768]{1,0:T(8,128)(2,1)S(1)} %get-tuple-element.38.refs_2_), channel_id=1, source_target_pairs={{8,4},{9,5},{24,20},{25,21}} | collective-permute-start | bytes 589832 | tf_op jit(solution)/shard_map/ppermute | solution.py:771
  18.5 28.5 %collective-permute-start.5 = (bf16[128,768]{1,0:T(8,128)(2,1)S(1)}, bf16[128,768]{1,0:T(8,128)(2,1)S(1)}, u32[]{:S(2)}, u32[]{:S(2)}) collective-permute-start(bf16[128,768]{1,0:T(8,128)(2,1)S(1)} %get-tuple-element.38.refs_2_), channel_id=1, source_target_pairs={{10,4},{11,5},{26,20},{27,21}} | collective-permute-start | bytes 589832 | tf_op jit(solution)/shard_map/ppermute | solution.py:771
  46.3 0.7 collective-permute-start.6
  55.2 6.8 %collective-permute-start.7 = (bf16[1152,768]{1,0:T(8,128)(2,1)S(1)}, bf16[1152,768]{1,0:T(8,128)(2,1)S(1)}, u32[]{:S(2)}, u32[]{:S(2)}) collective-permute-start(bf16[1152,768]{1,0:T(8,128)(2,1)S(1)} %shard_map.41.mine), channel_id=1, source_target_pairs={{0,1},{1,0},{2,3},{3,2},{4,5},{5,4},{6,7},{7,6},{8,9},{9,8},{10,11... | collective-permute-start | bytes 5308424 | tf_op jit(solution)/shard_map/ppermute | solution.py:774
  55.2 6.8 %collective-permute-start.8 = (bf16[768,768]{1,0:T(8,128)(2,1)S(1)}, bf16[768,768]{1,0:T(8,128)(2,1)S(1)}, u32[]{:S(2)}, u32[]{:S(2)}) collective-permute-start(bf16[768,768]{1,0:T(8,128)(2,1)S(1)} %shard_map.40.refs_1_.early), channel_id=1, source_target_pairs={{0,1},{1,0},{2,3},{3,2},{4,5},{5,4},{6,7},{7,6},{8,9},{9,8},{10,11... | collective-permute-start | bytes 3538952 | tf_op jit(solution)/shard_map/ppermute | solution.py:774
  55.7 12.0 %collective-permute-start.10 = (bf16[128,768]{1,0:T(8,128)(2,1)S(1)}, bf16[128,768]{1,0:T(8,128)(2,1)S(1)}, u32[]{:S(2)}, u32[]{:S(2)}) collective-permute-start(bf16[128,768]{1,0:T(8,128)(2,1)S(1)} %collective-permute-done.6.refs_2_), channel_id=1, source_target_pairs={{10,4},{11,5},{26,20},{27,21}} | collective-permute-start | bytes 589832 | tf_op jit(solution)/shard_map/ppermute | solution.py:771
  56.3 11.4 %collective-permute-start.9 = (bf16[128,768]{1,0:T(8,128)(2,1)S(1)}, bf16[128,768]{1,0:T(8,128)(2,1)S(1)}, u32[]{:S(2)}, u32[]{:S(2)}) collective-permute-start(bf16[128,768]{1,0:T(8,128)(2,1)S(1)} %collective-permute-done.6.refs_2_), channel_id=1, source_target_pairs={{8,4},{9,5},{24,20},{25,21}} | collective-permute-start | bytes 589832 | tf_op jit(solution)/shard_map/ppermute | solution.py:771
  67.8 1.8 %collective-permute-start.11 = (bf16[256,768]{1,0:T(8,128)(2,1)S(1)}, bf16[256,768]{1,0:T(8,128)(2,1)S(1)}, u32[]{:S(2)}, u32[]{:S(2)}) collective-permute-start(bf16[256,768]{1,0:T(8,128)(2,1)S(1)} %shard_map.44.late), channel_id=1, source_target_pairs={{0,1},{1,0},{2,3},{3,2},{4,5},{5,4},{6,7},{7,6},{8,9},{9,8},{10,11... | collective-permute-start | bytes 1179656 | tf_op jit(solution)/shard_map/ppermute | solution.py:774
  69.5 20.1 %copy-start.1 = (bf16[1024,768]{1,0:T(8,128)(2,1)S(1)}, bf16[1024,768]{1,0:T(8,128)(2,1)}, u32[]{:S(2)}) copy-start(bf16[1024,768]{1,0:T(8,128)(2,1)} %x_hbm.1) | copy-start | bytes 4718596
  69.5 20.1 %copy-start.3 = (s32[1024]{0:T(1024)S(1)}, s32[1024]{0:T(1024)}, u32[]{:S(2)}) copy-start(s32[1024]{0:T(1024)} %param.6) | copy-start | bytes 12292
  69.5 20.1 %copy-start.5 = (s32[64]{0:T(128)S(1)}, s32[64]{0:T(128)}, u32[]{:S(2)}) copy-start(s32[64]{0:T(128)} %param.7) | copy-start | bytes 772
  70.2 19.4 %all-to-all-start.3 = ((f32[16,1,256]{2,1,0:T(1,128)}), f32[16,1,256]{2,1,0:T(1,128)S(1)}, u32[]{:S(2)}, u32[]{:S(2)}) async-start(f32[16,1,256]{2,1,0:T(1,128)} %shard_map.46), calls=%async_computation.3 | async-start | bytes 32768 | tf_op jit(solution)/shard_map/all_to_all | solution.py:825
  89.7 0.6 copy-start.4

commit v20 on v18

--- a/solution.py
+++ b/solution.py
@@ -534,7 +534,7 @@
     return put
 
 
-def inner_kernel(lay, mine, early, sums, lab_lane, lab_sub, rows, bias, back, buf_a, buf_b):
+def inner_kernel(lay, mine, early, sums, lab_lane, rows, lab_sub, bias, back, buf_a, buf_b):
     is_home = lax.axis_index("cl") == lay.home
     infos = lines_of(lay, mine)
     buffers = (buf_a, buf_b)
@@ -577,7 +577,7 @@
 
 
 def cross_kernel(lay, mine, other, early, early_j, rows, sums, lab_lane, *refs):
-    total, for_other, unfit_ref, lab_sub, rows_j, bias, back, buf_a, buf_b = refs
+    total, for_other, unfit_ref, lab_sub, bias, back, rows_j, buf_a, buf_b = refs
     is_home = lax.axis_index("cl") == lay.home
     infos = lines_of(lay, other)
     own = lines_of(lay, mine)
@@ -762,15 +762,15 @@
     def swap(x):
         return lax.ppermute(x, "grp", [(0, 1), (1, 0)])
 
-    moved = hop(extra, [(6, 4), (7, 5)])
+    both = lay_out([extra, hop(extra, [(6, 4), (7, 5)])])
     early = [extra if s == home else hop(extra, [(s, home)]) for s in lay.early]
     early = lay_out(early, home)
     mine = lax.all_to_all(
         packed.reshape(n_owner, main, width), "cl", split_axis=0, concat_axis=0, tiled=True
     ).reshape(n_owner * main, width)
-    mine = after(mine, early, moved)
+    mine = after(mine, early, both)
     other, early_j = swap(mine), swap(early)
-    late = [hop(x, [(s, home)]) for s in (4, 5) for x in (extra, moved)]
+    late = [hop(both, [(s, home)]) for s in (4, 5)]
 
     def array(shape, dtype=jnp.float32):
         return jax.ShapeDtypeStruct(shape, dtype)
@@ -779,19 +779,19 @@
         return pltpu.VMEM(shape, jnp.float32)
 
     row, long_row = array((1, lay.n_first)), array((1, lay.n_all))
-    side, bias = array((lay.n_first, LANES)), scratch((lay.n_main, LANES))
+    bias = scratch((lay.n_main, LANES))
     heads = array((lay.n_head, width), jnp.bfloat16)
     late_side, first_side = scratch((lay.n_late, LANES)), scratch((lay.n_first, LANES))
-    sums, first_lane, lab_sub, heads_i = pair_call(
-        inner_kernel, lay, (mine, early), (row, row, side, heads), (bias, first_side)
-    )
-    specs = vmem_specs(2) + (pl.BlockSpec(memory_space=pltpu.SMEM),) + vmem_specs(2)
-    sums, first_other, unfit, _, _ = pair_call(
+    sums, first_lane, heads_i = pair_call(
+        inner_kernel, lay, (mine, early), (row, row, heads), (first_side, bias, first_side)
+    )
+    specs = vmem_specs(2) + (pl.BlockSpec(memory_space=pltpu.SMEM),)
+    sums, first_other, unfit = pair_call(
         cross_kernel,
         lay,
         (mine, other, early, early_j, heads_i, sums, first_lane),
-        (row, row, array((1, 1), jnp.int32), side, heads),
-        (bias, first_side),
+        (row, row, array((1, 1), jnp.int32)),
+        (first_side, bias, first_side, pltpu.VMEM(heads.shape, heads.dtype)),
         specs,
     )
     late = lay_out(late, home, (sums,))

time: 84.9 us -> 84.9 us (level)
  starting transfers between devices: 20.9 us -> 24.9 us
  waiting for transfers between devices: 45.5 us -> 43.3 us
  Pallas kernels: 16.7 us -> 14.9 us
    all_to_all x1, starting transfers between devices: 4.27 us -> 9.69 us  [body(): lax.all_to_all(results, ('cl', 'grp'), split_axis=0, concat_axis=0, tiled...]
    ppermute x3, waiting for transfers between devices: 4.44 us -> 2.25 us  [swap(): return lax.ppermute(x, 'grp', [(0, 1), (1, 0)])]
    pallas_call x4, Pallas kernels: 11.4 us -> 9.57 us  [pair_call(): pl.pallas_call(functools.partial(kernel, lay), out_shape=out_shape, in_sp...]
    ppermute x8 -> x6, starting transfers between devices: 8.61 us -> 7.3 us  [hop(): return lax.ppermute(x, 'cl', pairs)]
    ppermute x8 -> x6, waiting for transfers between devices: 27.8 us -> 27.8 us  [hop(): return lax.ppermute(x, 'cl', pairs)]
  transfers between devices with their start and end apart: 13 -> 11, of which waited for: 5 -> 4; matrix products, arithmetic and copies ran while one was open for 0% -> 0% of each run, Pallas kernels for 13% -> 11%
where the time goes in v20:
time: 84.9 us; the launch traced here: 84.5 us
  waiting for transfers between devices  43.3 us (51%)
  starting transfers between devices  24.9 us (29%)
  Pallas kernels  14.9 us (18%)
    ppermute x6, waiting for transfers between devices, hop(): return lax.ppermute(x, 'cl', pairs)  27.8 us
    all_to_all x1, starting transfers between devices, body(): lax.all_to_all(results, ('cl', 'grp'), split_axis=0, concat_axis=0, tiled...  9.69 us
    pallas_call x4, Pallas kernels, pair_call(): pl.pallas_call(functools.partial(kernel, lay), out_shape=out_shape, in_sp...  9.57 us
    all_to_all x1, waiting for transfers between devices, body(): lax.all_to_all(packed.reshape(n_owner, main, width), 'cl', split_axis=0,...  7.44 us
    ppermute x6, starting transfers between devices, hop(): return lax.ppermute(x, 'cl', pairs)  7.3 us
    all_to_all x1, starting transfers between devices, body(): lax.all_to_all(packed.reshape(n_owner, main, width), 'cl', split_axis=0,...  7.29 us
    all_to_all x1, waiting for transfers between devices, body(): lax.all_to_all(results, ('cl', 'grp'), split_axis=0, concat_axis=0, tiled...  5.85 us
    pallas_call x1, Pallas kernels, place_rows(): pl.pallas_call(functools.partial(place_kernel, lay), out_shape=(jax.Shape...  5.23 us
  transfers between devices with their start and end apart: 11, of which 4 were waited for; matrix products, arithmetic and copies ran while one was open for 0% of the time, Pallas kernels for 11%

profile of v20, /device:TPU:0, one launch (start us, length us, event | category | flops | bytes accessed | tf_op | source)
XLA Modules:
  0.0 84.5 jit_solution(9585464366917000362)
XLA Ops:
  0.0 5.2 %shard_map.39 = (bf16[1152,768]{1,0:T(8,128)(2,1)}, bf16[128,768]{1,0:T(8,128)(2,1)S(1)}, s32[8,128]{1,0:T(8,128)S(1)}) custom-call(bf16[1024,768]{1,0:T(8,128)(2,1)} %x_hbm.1, s32[8,128]{1,0:T(8,128)} %bitcast.23, s32[1,64]{1,0:T(1,128)} %bitcast.27), custom_call_target="tpu_custom_call" | custom-call | tf_op jit(solution)/shard_map/pallas_call | solution.py:311
  5.2 7.3 %all-to-all-start.2 = ((bf16[8,144,768]{2,1,0:T(8,128)(2,1)}), bf16[8,144,768]{2,1,0:T(8,128)(2,1)S(1)}, u32[]{:S(2)}, u32[]{:S(2)}) async-start(bf16[8,144,768]{2,1,0:T(8,128)(2,1)} %bitcast.12), calls=%async_computation.2 | async-start | bytes 3538944 | tf_op jit(solution)/shard_map/all_to_all | solution.py:768
  12.5 0.7 collective-permute-start.4
  13.2 3.9 %collective-permute-start.1 = (bf16[128,768]{1,0:T(8,128)(2,1)S(1)}, bf16[128,768]{1,0:T(8,128)(2,1)S(1)}, u32[]{:S(2)}, u32[]{:S(2)}) collective-permute-start(bf16[128,768]{1,0:T(8,128)(2,1)S(1)} %get-tuple-element.38.refs_2_.refs_0_), channel_id=1, source_target_pairs={{0,4},{1,5},{16,20},{17,21}} | collective-permute-start | bytes 589832 | tf_op jit(solution)/shard_map/ppermute | solution.py:760
  17.1 0.7 collective-permute-start.2
  17.8 0.7 collective-permute-start.3
  18.5 0.0 collective-permute-done.4.refs_1_
  18.6 27.7 %collective-permute-done.1.refs_0_ = bf16[128,768]{1,0:T(8,128)(2,1)S(1)} collective-permute-done((bf16[128,768]{1,0:T(8,128)(2,1)S(1)}, bf16[128,768]{1,0:T(8,128)(2,1)S(1)}, u32[]{:S(2)}, u32[]{:S(2)}) %collective-permute-start.1) | collective-permute-done | bytes 196640 | tf_op jit(solution)/shard_map/ppermute | solution.py:760
  46.3 0.0 collective-permute-done.2.refs_1_
  46.3 0.0 collective-permute-done.3.refs_3_
  46.3 7.4 %all-to-all-done.2 = bf16[8,144,768]{2,1,0:T(8,128)(2,1)S(1)} async-done(((bf16[8,144,768]{2,1,0:T(8,128)(2,1)}), bf16[8,144,768]{2,1,0:T(8,128)(2,1)S(1)}, u32[]{:S(2)}, u32[]{:S(2)}) %all-to-all-start.2) | async-done | bytes 1769504 | tf_op jit(solution)/shard_map/all_to_all | solution.py:768
  53.7 0.0 collective-permute-start.5
  53.8 0.5 collective-permute-start.6
  54.3 0.7 collective-permute-start.7
  54.9 0.7 collective-permute-start.8
  55.6 4.0 %shard_map.43 = (f32[1,1536]{1,0:T(1,128)S(1)}, f32[1,1536]{1,0:T(1,128)S(1)}, bf16[1024,768]{1,0:T(8,128)(2,1)S(1)}) custom-call(bf16[1152,768]{1,0:T(8,128)(2,1)S(1)} %shard_map.42.mine, bf16[512,768]{1,0:T(8,128)(2,1)S(1)} %shard_map.40.refs_1_.early), custom_call_target="tpu_custom_call" | custom-call | bytes 1 | tf_op jit(solution)/shard_map/pallas_call | solution.py:693
  59.6 0.0 collective-permute-done.6.early_j
  59.6 0.0 collective-permute-done.5.other
  59.6 4.9 %shard_map.44 = (f32[1,1536]{1,0:T(1,128)S(1)}, f32[1,1536]{1,0:T(1,128)S(1)}, s32[1,1]{1,0:T(1,128)}) custom-call(bf16[1152,768]{1,0:T(8,128)(2,1)S(1)} %shard_map.42.mine, bf16[1152,768]{1,0:T(8,128)(2,1)S(1)} %collective-permute-done.5.other, bf16[512,768]{1,0:T(8,128)(2,1)S(1)} %shard_map.40.refs_1_.early, ...), custom_call_target="tpu_custom_call" | custom-call | bytes 1 | tf_op jit(solution)/shard_map/pallas_call | solution.py:693
  64.5 0.0 collective-permute-done.7.refs_0_
  64.5 0.0 collective-permute-done.8.refs_1_
  64.6 0.1 collective-permute-start.9
  64.7 2.2 %collective-permute-done.9.late_j = bf16[512,768]{1,0:T(8,128)(2,1)S(1)} collective-permute-done((bf16[512,768]{1,0:T(8,128)(2,1)S(1)}, bf16[512,768]{1,0:T(8,128)(2,1)S(1)}, u32[]{:S(2)}, u32[]{:S(2)}) %collective-permute-start.9) | collective-permute-done | bytes 786464 | tf_op jit(solution)/shard_map/ppermute | solution.py:763
  66.9 0.0 copy-start.1
  66.9 0.0 copy-start.3
  66.9 0.0 copy-start.5
  66.9 0.7 shard_map.47
  67.6 9.7 %all-to-all-start.3 = ((f32[16,1,256]{2,1,0:T(1,128)}), f32[16,1,256]{2,1,0:T(1,128)S(1)}, u32[]{:S(2)}, u32[]{:S(2)}) async-start(f32[16,1,256]{2,1,0:T(1,128)} %shard_map.47), calls=%async_computation.3 | async-start | bytes 32768 | tf_op jit(solution)/shard_map/all_to_all | solution.py:814
  78.0 5.8 %all-to-all-done.3 = f32[16,1,256]{2,1,0:T(1,128)S(1)} async-done(((f32[16,1,256]{2,1,0:T(1,128)}), f32[16,1,256]{2,1,0:T(1,128)S(1)}, u32[]{:S(2)}, u32[]{:S(2)}) %all-to-all-start.3) | async-done | bytes 16416 | tf_op jit(solution)/shard_map/all_to_all | solution.py:814
  83.8 0.0 copy-done.1
  83.8 0.0 copy-done.3
  83.8 0.0 copy-done.5
  83.8 0.1 conditional.1
  83.8 0.1 branch_1_fun.1
  83.9 0.0 copy-start.4
  84.0 0.6 copy-done.4
  (5 shorter events, 0.1 us)
Async XLA Ops:
  5.2 48.5 %all-to-all-start.2 = ((bf16[8,144,768]{2,1,0:T(8,128)(2,1)}), bf16[8,144,768]{2,1,0:T(8,128)(2,1)S(1)}, u32[]{:S(2)}, u32[]{:S(2)}) async-start(bf16[8,144,768]{2,1,0:T(8,128)(2,1)} %bitcast.12), calls=%async_computation.2 | async-start | bytes 3538944 | tf_op jit(solution)/shard_map/all_to_all | solution.py:768
  12.5 6.0 %collective-permute-start.4 = (bf16[128,768]{1,0:T(8,128)(2,1)S(1)}, bf16[128,768]{1,0:T(8,128)(2,1)S(1)}, u32[]{:S(2)}, u32[]{:S(2)}) collective-permute-start(bf16[128,768]{1,0:T(8,128)(2,1)S(1)} %get-tuple-element.38.refs_2_.refs_0_), channel_id=1, source_target_pairs={{12,8},{14,10},{13,9},{15,11},{28,24},{30,26},{29,25},{31,27}} | collective-permute-start | bytes 589832 | tf_op jit(solution)/shard_map/ppermute | solution.py:760
  13.2 33.1 %collective-permute-start.1 = (bf16[128,768]{1,0:T(8,128)(2,1)S(1)}, bf16[128,768]{1,0:T(8,128)(2,1)S(1)}, u32[]{:S(2)}, u32[]{:S(2)}) collective-permute-start(bf16[128,768]{1,0:T(8,128)(2,1)S(1)} %get-tuple-element.38.refs_2_.refs_0_), channel_id=1, source_target_pairs={{0,4},{1,5},{16,20},{17,21}} | collective-permute-start | bytes 589832 | tf_op jit(solution)/shard_map/ppermute | solution.py:760
  17.1 29.2 %collective-permute-start.2 = (bf16[128,768]{1,0:T(8,128)(2,1)S(1)}, bf16[128,768]{1,0:T(8,128)(2,1)S(1)}, u32[]{:S(2)}, u32[]{:S(2)}) collective-permute-start(bf16[128,768]{1,0:T(8,128)(2,1)S(1)} %get-tuple-element.38.refs_2_.refs_0_), channel_id=1, source_target_pairs={{2,4},{3,5},{18,20},{19,21}} | collective-permute-start | bytes 589832 | tf_op jit(solution)/shard_map/ppermute | solution.py:760
  17.8 28.5 %collective-permute-start.3 = (bf16[128,768]{1,0:T(8,128)(2,1)S(1)}, bf16[128,768]{1,0:T(8,128)(2,1)S(1)}, u32[]{:S(2)}, u32[]{:S(2)}) collective-permute-start(bf16[128,768]{1,0:T(8,128)(2,1)S(1)} %get-tuple-element.38.refs_2_.refs_0_), channel_id=1, source_target_pairs={{6,4},{7,5},{22,20},{23,21}} | collective-permute-start | bytes 589832 | tf_op jit(solution)/shard_map/ppermute | solution.py:760
  53.7 5.9 %collective-permute-start.5 = (bf16[1152,768]{1,0:T(8,128)(2,1)S(1)}, bf16[1152,768]{1,0:T(8,128)(2,1)S(1)}, u32[]{:S(2)}, u32[]{:S(2)}) collective-permute-start(bf16[1152,768]{1,0:T(8,128)(2,1)S(1)} %shard_map.42.mine), channel_id=1, source_target_pairs={{0,1},{1,0},{2,3},{3,2},{4,5},{5,4},{6,7},{7,6},{8,9},{9,8},{10,11... | collective-permute-start | bytes 5308424 | tf_op jit(solution)/shard_map/ppermute | solution.py:763
  53.8 5.9 %collective-permute-start.6 = (bf16[512,768]{1,0:T(8,128)(2,1)S(1)}, bf16[512,768]{1,0:T(8,128)(2,1)S(1)}, u32[]{:S(2)}, u32[]{:S(2)}) collective-permute-start(bf16[512,768]{1,0:T(8,128)(2,1)S(1)} %shard_map.40.refs_1_.early), channel_id=1, source_target_pairs={{0,1},{1,0},{2,3},{3,2},{4,5},{5,4},{6,7},{7,6},{8,9},{9,8},{10,11... | collective-permute-start | bytes 2359304 | tf_op jit(solution)/shard_map/ppermute | solution.py:763
  54.3 10.3 %collective-permute-start.7 = (bf16[256,768]{1,0:T(8,128)(2,1)S(1)}, bf16[256,768]{1,0:T(8,128)(2,1)S(1)}, u32[]{:S(2)}, u32[]{:S(2)}) collective-permute-start(bf16[256,768]{1,0:T(8,128)(2,1)S(1)} %shard_map.41.refs_2_), channel_id=1, source_target_pairs={{8,4},{9,5},{24,20},{25,21}} | collective-permute-start | bytes 1179656 | tf_op jit(solution)/shard_map/ppermute | solution.py:760
  54.9 9.6 %collective-permute-start.8 = (bf16[256,768]{1,0:T(8,128)(2,1)S(1)}, bf16[256,768]{1,0:T(8,128)(2,1)S(1)}, u32[]{:S(2)}, u32[]{:S(2)}) collective-permute-start(bf16[256,768]{1,0:T(8,128)(2,1)S(1)} %shard_map.41.refs_2_), channel_id=1, source_target_pairs={{10,4},{11,5},{26,20},{27,21}} | collective-permute-start | bytes 1179656 | tf_op jit(solution)/shard_map/ppermute | solution.py:760
  64.6 2.4 %collective-permute-start.9 = (bf16[512,768]{1,0:T(8,128)(2,1)S(1)}, bf16[512,768]{1,0:T(8,128)(2,1)S(1)}, u32[]{:S(2)}, u32[]{:S(2)}) collective-permute-start(bf16[512,768]{1,0:T(8,128)(2,1)S(1)} %shard_map.45.late), channel_id=1, source_target_pairs={{0,1},{1,0},{2,3},{3,2},{4,5},{5,4},{6,7},{7,6},{8,9},{9,8},{10,11... | collective-permute-start | bytes 2359304 | tf_op jit(solution)/shard_map/ppermute | solution.py:763
  66.9 16.9 %copy-start.1 = (bf16[1024,768]{1,0:T(8,128)(2,1)S(1)}, bf16[1024,768]{1,0:T(8,128)(2,1)}, u32[]{:S(2)}) copy-start(bf16[1024,768]{1,0:T(8,128)(2,1)} %x_hbm.1) | copy-start | bytes 4718596
  66.9 16.9 %copy-start.3 = (s32[1024]{0:T(1024)S(1)}, s32[1024]{0:T(1024)}, u32[]{:S(2)}) copy-start(s32[1024]{0:T(1024)} %param.6) | copy-start | bytes 12292
  66.9 16.9 %copy-start.5 = (s32[64]{0:T(128)S(1)}, s32[64]{0:T(128)}, u32[]{:S(2)}) copy-start(s32[64]{0:T(128)} %param.7) | copy-start | bytes 772
  67.6 16.2 %all-to-all-start.3 = ((f32[16,1,256]{2,1,0:T(1,128)}), f32[16,1,256]{2,1,0:T(1,128)S(1)}, u32[]{:S(2)}, u32[]{:S(2)}) async-start(f32[16,1,256]{2,1,0:T(1,128)} %shard_map.47), calls=%async_computation.3 | async-start | bytes 32768 | tf_op jit(solution)/shard_map/all_to_all | solution.py:814
  83.9 0.6 copy-start.4

commit v21 on v20

--- a/solution.py
+++ b/solution.py
@@ -577,7 +577,8 @@
 
 
 def cross_kernel(lay, mine, other, early, early_j, rows, sums, lab_lane, *refs):
-    total, for_other, unfit_ref, lab_sub, bias, back, rows_j, buf_a, buf_b = refs
+    total, for_other, unfit_ref, late_sub, late_sub_j, long_lane = refs[:6]
+    lab_sub, bias, back, rows_j, buf_a, buf_b = refs[6:]
     is_home = lax.axis_index("cl") == lay.home
     infos = lines_of(lay, other)
     own = lines_of(lay, mine)
@@ -614,6 +615,10 @@
             half_blocks(
                 ref, blocks_j[i], lab_sub, i * size, back, i * size, lab_lane, buffers, put
             )
+        write_labels(lay, own, lay.late, lay.head, lay.rest, 0, late_sub, None)
+        write_labels(lay, infos, lay.late, lay.head, lay.rest, 0, late_sub_j, None)
+        long_lane[:, : lay.n_first] = lab_lane[...]
+        turn_labels(lay, late_sub, lay.n_late, long_lane, lay.n_first)
         for_other[...] = jnp.zeros(for_other.shape, jnp.float32)
         turn_sums(back, lay.n_first, for_other, 0)
 
@@ -631,14 +636,9 @@
     stream((early, lay.n_early, lay.n_head), lates, lab_lane, buffers, put)
 
 
-def inner_late_kernel(lay, mine, early, late, rows, first_lane, *refs):
-    sums, lab_lane, late_sub, back, buf_a, buf_b = refs
-
+def inner_late_kernel(lay, early, late, rows, late_sub, lab_lane, sums, back, buf_a, buf_b):
     @pl.when(lax.axis_index("cl") == lay.home)
     def _():
-        late_labels(lay, lines_of(lay, mine), late_sub)
-        lab_lane[:, : lay.n_first] = first_lane[...]
-        turn_labels(lay, late_sub, lay.n_late, lab_lane, lay.n_first)
         buffers = (buf_a, buf_b)
         back[...] = jnp.zeros(back.shape, jnp.float32)
         put = setter(sums)
@@ -648,15 +648,13 @@
         turn_sums(back, lay.n_late, sums, lay.n_first)
 
 
-def cross_late_kernel(lay, other, early, late, late_j, rows, first_lane, *refs):
-    first_sums, first_other, lab_lane, sums, out_ref, total, late_sub, back, buf_a, buf_b = refs
+def cross_late_kernel(lay, early, late, late_j, rows, late_sub, lab_lane, first_lane, *refs):
+    first_sums, first_other, sums, out_ref, total, back, buf_a, buf_b = refs
     is_home = lax.axis_index("cl") == lay.home
     grp = lax.axis_index("grp")
 
     @pl.when(is_home)
     def _():
-        infos = lines_of(lay, other)
-        write_labels(lay, infos, lay.late, lay.head, lay.rest, 0, late_sub, None)
         total[...] = sums[...]
         total[:, : lay.n_first] += first_sums[...]
         back[...] = jnp.zeros(back.shape, jnp.float32)
@@ -781,35 +779,36 @@
     row, long_row = array((1, lay.n_first)), array((1, lay.n_all))
     bias = scratch((lay.n_main, LANES))
     heads = array((lay.n_head, width), jnp.bfloat16)
+    late_lines = array((lay.n_late, LANES))
     late_side, first_side = scratch((lay.n_late, LANES)), scratch((lay.n_first, LANES))
     sums, first_lane, heads_i = pair_call(
         inner_kernel, lay, (mine, early), (row, row, heads), (first_side, bias, first_side)
     )
-    specs = vmem_specs(2) + (pl.BlockSpec(memory_space=pltpu.SMEM),)
-    sums, first_other, unfit = pair_call(
+    specs = vmem_specs(2) + (pl.BlockSpec(memory_space=pltpu.SMEM),) + vmem_specs(3)
+    sums, first_other, unfit, late_sub, late_sub_j, lane = pair_call(
         cross_kernel,
         lay,
         (mine, other, early, early_j, heads_i, sums, first_lane),
-        (row, row, array((1, 1), jnp.int32)),
+        (row, row, array((1, 1), jnp.int32), late_lines, late_lines, long_row),
         (first_side, bias, first_side, pltpu.VMEM(heads.shape, heads.dtype)),
         specs,
     )
     late = lay_out(late, home, (sums,))
     late_j = swap(late)
-    late_sums, lane = pair_call(
+    (late_sums,) = pair_call(
         inner_late_kernel,
         lay,
-        (mine, early, late, heads_i, first_lane),
-        (long_row, long_row),
-        (late_side, late_side),
-        pairs=lay.n_late * (lay.n_all + lay.n_first),
+        (early, late, heads_i, late_sub, lane),
+        (long_row,),
+        (late_side,),
+        pairs=lay.n_late * lay.n_all,
     )
     (results,) = pair_call(
         cross_late_kernel,
         lay,
-        (other, early, late, late_j, heads_i, first_lane, sums, first_other, lane, late_sums),
+        (early, late, late_j, heads_i, late_sub_j, lane, first_lane, sums, first_other, late_sums),
         (array((2 * n_owner, 1, capacity)),),
-        (scratch(long_row.shape), late_side, late_side),
+        (scratch(long_row.shape), late_side),
     )
     returned = lax.all_to_all(
         results, ("cl", "grp"), split_axis=0, concat_axis=0, tiled=True

time: 84.9 us -> 84.9 us (level)
  no operation moved by 1% of the time
where the time goes in v21:
time: 84.9 us; the launch traced here: 84.6 us
  waiting for transfers between devices  43.3 us (51%)
  starting transfers between devices  24.9 us (29%)
  Pallas kernels  14.9 us (18%)
    ppermute x6, waiting for transfers between devices, hop(): return lax.ppermute(x, 'cl', pairs)  27.8 us
    all_to_all x1, starting transfers between devices, body(): lax.all_to_all(results, ('cl', 'grp'), split_axis=0, concat_axis=0, tiled...  9.75 us
    pallas_call x4, Pallas kernels, pair_call(): pl.pallas_call(functools.partial(kernel, lay), out_shape=out_shape, in_sp...  9.54 us
    all_to_all x1, waiting for transfers between devices, body(): lax.all_to_all(packed.reshape(n_owner, main, width), 'cl', split_axis=0,...  7.44 us
    ppermute x6, starting transfers between devices, hop(): return lax.ppermute(x, 'cl', pairs)  7.3 us
    all_to_all x1, starting transfers between devices, body(): lax.all_to_all(packed.reshape(n_owner, main, width), 'cl', split_axis=0,...  7.29 us
    all_to_all x1, waiting for transfers between devices, body(): lax.all_to_all(results, ('cl', 'grp'), split_axis=0, concat_axis=0, tiled...  5.85 us
    pallas_call x1, Pallas kernels, place_rows(): pl.pallas_call(functools.partial(place_kernel, lay), out_shape=(jax.Shape...  5.23 us
  transfers between devices with their start and end apart: 11, of which 4 were waited for; matrix products, arithmetic and copies ran while one was open for 0% of the time, Pallas kernels for 11%

profile of v21, /device:TPU:0, one launch (start us, length us, event | category | flops | bytes accessed | tf_op | source)
XLA Modules:
  0.0 84.6 jit_solution(265882455010617734)
XLA Ops:
  0.0 5.2 %shard_map.39 = (bf16[1152,768]{1,0:T(8,128)(2,1)}, bf16[128,768]{1,0:T(8,128)(2,1)S(1)}, s32[8,128]{1,0:T(8,128)S(1)}) custom-call(bf16[1024,768]{1,0:T(8,128)(2,1)} %x_hbm.1, s32[8,128]{1,0:T(8,128)} %bitcast.23, s32[1,64]{1,0:T(1,128)} %bitcast.27), custom_call_target="tpu_custom_call" | custom-call | tf_op jit(solution)/shard_map/pallas_call | solution.py:311
  5.2 7.3 %all-to-all-start.2 = ((bf16[8,144,768]{2,1,0:T(8,128)(2,1)}), bf16[8,144,768]{2,1,0:T(8,128)(2,1)S(1)}, u32[]{:S(2)}, u32[]{:S(2)}) async-start(bf16[8,144,768]{2,1,0:T(8,128)(2,1)} %bitcast.12), calls=%async_computation.2 | async-start | bytes 3538944 | tf_op jit(solution)/shard_map/all_to_all | solution.py:766
  12.5 0.7 collective-permute-start.4
  13.2 3.9 %collective-permute-start.1 = (bf16[128,768]{1,0:T(8,128)(2,1)S(1)}, bf16[128,768]{1,0:T(8,128)(2,1)S(1)}, u32[]{:S(2)}, u32[]{:S(2)}) collective-permute-start(bf16[128,768]{1,0:T(8,128)(2,1)S(1)} %get-tuple-element.39.refs_2_.refs_0_), channel_id=1, source_target_pairs={{0,4},{1,5},{16,20},{17,21}} | collective-permute-start | bytes 589832 | tf_op jit(solution)/shard_map/ppermute | solution.py:758
  17.1 0.7 collective-permute-start.2
  17.8 0.7 collective-permute-start.3
  18.5 0.0 collective-permute-done.4.refs_1_
  18.6 27.7 %collective-permute-done.1.refs_0_ = bf16[128,768]{1,0:T(8,128)(2,1)S(1)} collective-permute-done((bf16[128,768]{1,0:T(8,128)(2,1)S(1)}, bf16[128,768]{1,0:T(8,128)(2,1)S(1)}, u32[]{:S(2)}, u32[]{:S(2)}) %collective-permute-start.1) | collective-permute-done | bytes 196640 | tf_op jit(solution)/shard_map/ppermute | solution.py:758
  46.3 0.0 collective-permute-done.2.refs_1_
  46.3 0.0 collective-permute-done.3.refs_3_
  46.3 7.4 %all-to-all-done.2 = bf16[8,144,768]{2,1,0:T(8,128)(2,1)S(1)} async-done(((bf16[8,144,768]{2,1,0:T(8,128)(2,1)}), bf16[8,144,768]{2,1,0:T(8,128)(2,1)S(1)}, u32[]{:S(2)}, u32[]{:S(2)}) %all-to-all-start.2) | async-done | bytes 1769504 | tf_op jit(solution)/shard_map/all_to_all | solution.py:766
  53.8 0.0 collective-permute-start.5
  53.8 0.5 collective-permute-start.6
  54.3 0.7 collective-permute-start.7
  54.9 0.7 collective-permute-start.8
  55.6 4.0 %shard_map.43 = (f32[1,1536]{1,0:T(1,128)S(1)}, f32[1,1536]{1,0:T(1,128)S(1)}, bf16[1024,768]{1,0:T(8,128)(2,1)S(1)}) custom-call(bf16[1152,768]{1,0:T(8,128)(2,1)S(1)} %shard_map.42.mine, bf16[512,768]{1,0:T(8,128)(2,1)S(1)} %shard_map.40.refs_1_.early), custom_call_target="tpu_custom_call" | custom-call | bytes 1 | tf_op jit(solution)/shard_map/pallas_call | solution.py:691
  59.6 0.0 collective-permute-done.6.early_j
  59.6 0.0 collective-permute-done.5.other
  59.6 4.9 %shard_map.44 = (f32[1,1536]{1,0:T(1,128)S(1)}, f32[1,1536]{1,0:T(1,128)S(1)}, s32[1,1]{1,0:T(1,128)}, f32[512,128]{1,0:T(8,128)S(1)}, f32[512,128]{1,0:T(8,128)S(1)}, /*index=5*/f32[1,2048]{1,0:T(1,128)S(1)}) custom-call(bf16[1152,768]{1,0:T(8,128)(2,1)S(1)} %shard_map.42.mine, bf16[1152,768]{1,0:T(8,128)(2,1)S(1)} %collective-permute-done.5.other, ...), custom_call_target="tpu_custom_call" | custom-call | bytes 1 | tf_op jit(solution)/shard_map/pallas_call | solution.py:691
  64.5 0.0 collective-permute-done.7.refs_0_
  64.5 0.0 collective-permute-done.8.refs_1_
  64.6 0.1 collective-permute-start.9
  64.7 2.2 %collective-permute-done.9.late_j = bf16[512,768]{1,0:T(8,128)(2,1)S(1)} collective-permute-done((bf16[512,768]{1,0:T(8,128)(2,1)S(1)}, bf16[512,768]{1,0:T(8,128)(2,1)S(1)}, u32[]{:S(2)}, u32[]{:S(2)}) %collective-permute-start.9) | collective-permute-done | bytes 786464 | tf_op jit(solution)/shard_map/ppermute | solution.py:761
  66.9 0.0 copy-start.1
  66.9 0.0 copy-start.3
  66.9 0.0 copy-start.5
  66.9 0.7 shard_map.47
  67.6 9.8 %all-to-all-start.3 = ((f32[16,1,256]{2,1,0:T(1,128)}), f32[16,1,256]{2,1,0:T(1,128)S(1)}, u32[]{:S(2)}, u32[]{:S(2)}) async-start(f32[16,1,256]{2,1,0:T(1,128)} %shard_map.47), calls=%async_computation.3 | async-start | bytes 32768 | tf_op jit(solution)/shard_map/all_to_all | solution.py:813
  78.0 5.8 %all-to-all-done.3 = f32[16,1,256]{2,1,0:T(1,128)S(1)} async-done(((f32[16,1,256]{2,1,0:T(1,128)}), f32[16,1,256]{2,1,0:T(1,128)S(1)}, u32[]{:S(2)}, u32[]{:S(2)}) %all-to-all-start.3) | async-done | bytes 16416 | tf_op jit(solution)/shard_map/all_to_all | solution.py:813
  83.9 0.0 copy-done.1
  83.9 0.0 copy-done.3
  83.9 0.0 copy-done.5
  83.9 0.1 conditional.1
  83.9 0.1 branch_1_fun.1
  84.0 0.0 copy-start.4
  84.0 0.6 copy-done.4
  (5 shorter events, 0.1 us)
Async XLA Ops:
  5.2 48.5 %all-to-all-start.2 = ((bf16[8,144,768]{2,1,0:T(8,128)(2,1)}), bf16[8,144,768]{2,1,0:T(8,128)(2,1)S(1)}, u32[]{:S(2)}, u32[]{:S(2)}) async-start(bf16[8,144,768]{2,1,0:T(8,128)(2,1)} %bitcast.12), calls=%async_computation.2 | async-start | bytes 3538944 | tf_op jit(solution)/shard_map/all_to_all | solution.py:766
  12.5 6.0 %collective-permute-start.4 = (bf16[128,768]{1,0:T(8,128)(2,1)S(1)}, bf16[128,768]{1,0:T(8,128)(2,1)S(1)}, u32[]{:S(2)}, u32[]{:S(2)}) collective-permute-start(bf16[128,768]{1,0:T(8,128)(2,1)S(1)} %get-tuple-element.39.refs_2_.refs_0_), channel_id=1, source_target_pairs={{12,8},{14,10},{13,9},{15,11},{28,24},{30,26},{29,25},{31,27}} | collective-permute-start | bytes 589832 | tf_op jit(solution)/shard_map/ppermute | solution.py:758
  13.2 33.1 %collective-permute-start.1 = (bf16[128,768]{1,0:T(8,128)(2,1)S(1)}, bf16[128,768]{1,0:T(8,128)(2,1)S(1)}, u32[]{:S(2)}, u32[]{:S(2)}) collective-permute-start(bf16[128,768]{1,0:T(8,128)(2,1)S(1)} %get-tuple-element.39.refs_2_.refs_0_), channel_id=1, source_target_pairs={{0,4},{1,5},{16,20},{17,21}} | collective-permute-start | bytes 589832 | tf_op jit(solution)/shard_map/ppermute | solution.py:758
  17.1 29.2 %collective-permute-start.2 = (bf16[128,768]{1,0:T(8,128)(2,1)S(1)}, bf16[128,768]{1,0:T(8,128)(2,1)S(1)}, u32[]{:S(2)}, u32[]{:S(2)}) collective-permute-start(bf16[128,768]{1,0:T(8,128)(2,1)S(1)} %get-tuple-element.39.refs_2_.refs_0_), channel_id=1, source_target_pairs={{2,4},{3,5},{18,20},{19,21}} | collective-permute-start | bytes 589832 | tf_op jit(solution)/shard_map/ppermute | solution.py:758
  17.8 28.5 %collective-permute-start.3 = (bf16[128,768]{1,0:T(8,128)(2,1)S(1)}, bf16[128,768]{1,0:T(8,128)(2,1)S(1)}, u32[]{:S(2)}, u32[]{:S(2)}) collective-permute-start(bf16[128,768]{1,0:T(8,128)(2,1)S(1)} %get-tuple-element.39.refs_2_.refs_0_), channel_id=1, source_target_pairs={{6,4},{7,5},{22,20},{23,21}} | collective-permute-start | bytes 589832 | tf_op jit(solution)/shard_map/ppermute | solution.py:758
  53.8 5.9 %collective-permute-start.5 = (bf16[1152,768]{1,0:T(8,128)(2,1)S(1)}, bf16[1152,768]{1,0:T(8,128)(2,1)S(1)}, u32[]{:S(2)}, u32[]{:S(2)}) collective-permute-start(bf16[1152,768]{1,0:T(8,128)(2,1)S(1)} %shard_map.42.mine), channel_id=1, source_target_pairs={{0,1},{1,0},{2,3},{3,2},{4,5},{5,4},{6,7},{7,6},{8,9},{9,8},{10,11... | collective-permute-start | bytes 5308424 | tf_op jit(solution)/shard_map/ppermute | solution.py:761
  53.8 5.9 %collective-permute-start.6 = (bf16[512,768]{1,0:T(8,128)(2,1)S(1)}, bf16[512,768]{1,0:T(8,128)(2,1)S(1)}, u32[]{:S(2)}, u32[]{:S(2)}) collective-permute-start(bf16[512,768]{1,0:T(8,128)(2,1)S(1)} %shard_map.40.refs_1_.early), channel_id=1, source_target_pairs={{0,1},{1,0},{2,3},{3,2},{4,5},{5,4},{6,7},{7,6},{8,9},{9,8},{10,11... | collective-permute-start | bytes 2359304 | tf_op jit(solution)/shard_map/ppermute | solution.py:761
  54.3 10.3 %collective-permute-start.7 = (bf16[256,768]{1,0:T(8,128)(2,1)S(1)}, bf16[256,768]{1,0:T(8,128)(2,1)S(1)}, u32[]{:S(2)}, u32[]{:S(2)}) collective-permute-start(bf16[256,768]{1,0:T(8,128)(2,1)S(1)} %shard_map.41.refs_2_), channel_id=1, source_target_pairs={{8,4},{9,5},{24,20},{25,21}} | collective-permute-start | bytes 1179656 | tf_op jit(solution)/shard_map/ppermute | solution.py:758
  54.9 9.6 %collective-permute-start.8 = (bf16[256,768]{1,0:T(8,128)(2,1)S(1)}, bf16[256,768]{1,0:T(8,128)(2,1)S(1)}, u32[]{:S(2)}, u32[]{:S(2)}) collective-permute-start(bf16[256,768]{1,0:T(8,128)(2,1)S(1)} %shard_map.41.refs_2_), channel_id=1, source_target_pairs={{10,4},{11,5},{26,20},{27,21}} | collective-permute-start | bytes 1179656 | tf_op jit(solution)/shard_map/ppermute | solution.py:758
  64.6 2.4 %collective-permute-start.9 = (bf16[512,768]{1,0:T(8,128)(2,1)S(1)}, bf16[512,768]{1,0:T(8,128)(2,1)S(1)}, u32[]{:S(2)}, u32[]{:S(2)}) collective-permute-start(bf16[512,768]{1,0:T(8,128)(2,1)S(1)} %shard_map.45.late), channel_id=1, source_target_pairs={{0,1},{1,0},{2,3},{3,2},{4,5},{5,4},{6,7},{7,6},{8,9},{9,8},{10,11... | collective-permute-start | bytes 2359304 | tf_op jit(solution)/shard_map/ppermute | solution.py:761
  66.9 16.9 %copy-start.1 = (bf16[1024,768]{1,0:T(8,128)(2,1)S(1)}, bf16[1024,768]{1,0:T(8,128)(2,1)}, u32[]{:S(2)}) copy-start(bf16[1024,768]{1,0:T(8,128)(2,1)} %x_hbm.1) | copy-start | bytes 4718596
  66.9 16.9 %copy-start.3 = (s32[1024]{0:T(1024)S(1)}, s32[1024]{0:T(1024)}, u32[]{:S(2)}) copy-start(s32[1024]{0:T(1024)} %param.6) | copy-start | bytes 12292
  66.9 16.9 %copy-start.5 = (s32[64]{0:T(128)S(1)}, s32[64]{0:T(128)}, u32[]{:S(2)}) copy-start(s32[64]{0:T(128)} %param.7) | copy-start | bytes 772
  67.6 16.3 %all-to-all-start.3 = ((f32[16,1,256]{2,1,0:T(1,128)}), f32[16,1,256]{2,1,0:T(1,128)S(1)}, u32[]{:S(2)}, u32[]{:S(2)}) async-start(f32[16,1,256]{2,1,0:T(1,128)} %shard_map.47), calls=%async_computation.3 | async-start | bytes 32768 | tf_op jit(solution)/shard_map/all_to_all | solution.py:813
  84.0 0.6 copy-start.4

commit v22 on v21

--- a/solution.py
+++ b/solution.py
@@ -267,8 +267,11 @@
         [table[:, start : start + LANES] for start in range(0, rows, LANES)], axis=0
     )
     fits = rank < jnp.where(place == home, lay.head, main - 1)
-    slot = jnp.where(fits, place * main + rank, -1)
-    tail_slot = jnp.where(place == home, rank - lay.head, -1)
+    slot = jnp.where(
+        fits,
+        place * main + rank,
+        jnp.where(place == home, lay.n_main + rank - lay.head, -1),
+    )
     copies[0].wait()
     x = x_ref[...].astype(jnp.float32)
     squares = jnp.sum(x * x, axis=1, keepdims=True)
@@ -279,22 +282,23 @@
         chosen = jnp.where(here == slot, 1.0, 0.0).astype(jnp.bfloat16)
         return jnp.dot(chosen, unit[...], preferred_element_type=jnp.float32)
 
-    count = 2 * main
+    count = lay.n_main // 2
     down = lax.broadcasted_iota(jnp.int32, (count, LANES), 0)
     is_info = lax.rem(down, main) == main - 1
     writes = []
-    for i, start in enumerate(range(0, lay.n_main, count)):
-        packed = chosen_rows(slot, start, count)
+    for i, start in enumerate((0, count)):
+        packed = chosen_rows(slot, start, count + i * lay.rest)
         place = slice(start, start + count)
-        main_ref[place, LANES:] = packed[:, LANES:].astype(jnp.bfloat16)
-        main_ref[place, :LANES] = jnp.where(is_info, info, packed[:, :LANES]).astype(jnp.bfloat16)
+        main_ref[place, LANES:] = packed[:count, LANES:].astype(jnp.bfloat16)
+        first_lanes = jnp.where(is_info, info, packed[:count, :LANES])
+        main_ref[place, :LANES] = first_lanes.astype(jnp.bfloat16)
         writes.append(
             pltpu.make_async_copy(
                 main_ref.at[pl.ds(start, count)], main_hbm.at[pl.ds(start, count)], sems.at[3 + i]
             )
         )
         writes[-1].start()
-    tail_ref[...] = chosen_rows(tail_slot, 0, lay.rest).astype(jnp.bfloat16)
+    tail_ref[...] = packed[count:, :].astype(jnp.bfloat16)
     for write in writes:
         write.wait()
 
@@ -323,7 +327,7 @@
             pltpu.VMEM((1, n_fine), jnp.int32),
             pltpu.VMEM((rows, width), jnp.bfloat16),
             pltpu.VMEM((lay.n_main, width), jnp.bfloat16),
-            pltpu.SemaphoreType.DMA((3 + lay.n_owner // 2,)),
+            pltpu.SemaphoreType.DMA((5,)),
         ],
         compiler_params=pltpu.CompilerParams(vmem_limit_bytes=FAST_LIMIT),
     )(embeddings, labels.reshape(lab_shape), owner_map.reshape(1, n_fine))
@@ -371,7 +375,7 @@
 
 
 class Layout:
-    early, late = (0, 1, 2, 3), (4, 6, 5, 7)
+    early, late = (0, 1, 2, 3), (5, 7, 4, 6)
 
     def __init__(self, n_owner, n_fine, capacity, main, home):
         self.n_owner, self.n_fine, self.capacity = n_owner, n_fine, capacity
@@ -768,7 +772,7 @@
     ).reshape(n_owner * main, width)
     mine = after(mine, early, both)
     other, early_j = swap(mine), swap(early)
-    late = [hop(both, [(s, home)]) for s in (4, 5)]
+    late = [hop(both, [(s, home)]) for s in (5, 4)]
 
     def array(shape, dtype=jnp.float32):
         return jax.ShapeDtypeStruct(shape, dtype)

time: 84.9 us -> 84.2 us (level)
  starting transfers between devices: 24.9 us -> 24 us
    all_to_all x1, starting transfers between devices: 9.75 us -> 8.85 us  [body(): lax.all_to_all(results, ('cl', 'grp'), split_axis=0, concat_axis=0, tiled...]
where the time goes in v22:
time: 84.2 us; the launch traced here: 83.9 us
  waiting for transfers between devices  43.3 us (51%)
  starting transfers between devices  24 us (29%)
  Pallas kernels  15.2 us (18%)
    ppermute x6, waiting for transfers between devices, hop(): return lax.ppermute(x, 'cl', pairs)  27.8 us
    pallas_call x4, Pallas kernels, pair_call(): pl.pallas_call(functools.partial(kernel, lay), out_shape=out_shape, in_sp...  9.54 us
    all_to_all x1, starting transfers between devices, body(): lax.all_to_all(results, ('cl', 'grp'), split_axis=0, concat_axis=0, tiled...  8.85 us
    all_to_all x1, waiting for transfers between devices, body(): lax.all_to_all(packed.reshape(n_owner, main, width), 'cl', split_axis=0,...  7.45 us
    ppermute x6, starting transfers between devices, hop(): return lax.ppermute(x, 'cl', pairs)  7.3 us
    all_to_all x1, starting transfers between devices, body(): lax.all_to_all(packed.reshape(n_owner, main, width), 'cl', split_axis=0,...  7.29 us
    all_to_all x1, waiting for transfers between devices, body(): lax.all_to_all(results, ('cl', 'grp'), split_axis=0, concat_axis=0, tiled...  5.85 us
    pallas_call x1, Pallas kernels, place_rows(): pl.pallas_call(functools.partial(place_kernel, lay), out_shape=(jax.Shape...  5.48 us
  transfers between devices with their start and end apart: 11, of which 4 were waited for; matrix products, arithmetic and copies ran while one was open for 0% of the time, Pallas kernels for 11%

profile of v22, /device:TPU:0, one launch (start us, length us, event | category | flops | bytes accessed | tf_op | source)
XLA Modules:
  0.0 83.9 jit_solution(18052297699949641638)
XLA Ops:
  0.0 5.5 %shard_map.39 = (bf16[1152,768]{1,0:T(8,128)(2,1)}, bf16[128,768]{1,0:T(8,128)(2,1)S(1)}, s32[8,128]{1,0:T(8,128)S(1)}) custom-call(bf16[1024,768]{1,0:T(8,128)(2,1)} %x_hbm.1, s32[8,128]{1,0:T(8,128)} %bitcast.23, s32[1,64]{1,0:T(1,128)} %bitcast.27), custom_call_target="tpu_custom_call" | custom-call | tf_op jit(solution)/shard_map/pallas_call | solution.py:315
  5.5 7.3 %all-to-all-start.2 = ((bf16[8,144,768]{2,1,0:T(8,128)(2,1)}), bf16[8,144,768]{2,1,0:T(8,128)(2,1)S(1)}, u32[]{:S(2)}, u32[]{:S(2)}) async-start(bf16[8,144,768]{2,1,0:T(8,128)(2,1)} %bitcast.12), calls=%async_computation.2 | async-start | bytes 3538944 | tf_op jit(solution)/shard_map/all_to_all | solution.py:770
  12.8 0.7 collective-permute-start.4
  13.4 3.9 %collective-permute-start.1 = (bf16[128,768]{1,0:T(8,128)(2,1)S(1)}, bf16[128,768]{1,0:T(8,128)(2,1)S(1)}, u32[]{:S(2)}, u32[]{:S(2)}) collective-permute-start(bf16[128,768]{1,0:T(8,128)(2,1)S(1)} %get-tuple-element.39.refs_2_.refs_0_), channel_id=1, source_target_pairs={{0,4},{1,5},{16,20},{17,21}} | collective-permute-start | bytes 589832 | tf_op jit(solution)/shard_map/ppermute | solution.py:762
  17.4 0.7 collective-permute-start.2
  18.1 0.7 collective-permute-start.3
  18.8 0.0 collective-permute-done.4.refs_1_
  18.8 27.7 %collective-permute-done.1.refs_0_ = bf16[128,768]{1,0:T(8,128)(2,1)S(1)} collective-permute-done((bf16[128,768]{1,0:T(8,128)(2,1)S(1)}, bf16[128,768]{1,0:T(8,128)(2,1)S(1)}, u32[]{:S(2)}, u32[]{:S(2)}) %collective-permute-start.1) | collective-permute-done | bytes 196640 | tf_op jit(solution)/shard_map/ppermute | solution.py:762
  46.5 0.0 collective-permute-done.2.refs_1_
  46.5 0.0 collective-permute-done.3.refs_3_
  46.6 7.4 %all-to-all-done.2 = bf16[8,144,768]{2,1,0:T(8,128)(2,1)S(1)} async-done(((bf16[8,144,768]{2,1,0:T(8,128)(2,1)}), bf16[8,144,768]{2,1,0:T(8,128)(2,1)S(1)}, u32[]{:S(2)}, u32[]{:S(2)}) %all-to-all-start.2) | async-done | bytes 1769504 | tf_op jit(solution)/shard_map/all_to_all | solution.py:770
  54.0 0.0 collective-permute-start.5
  54.0 0.5 collective-permute-start.6
  54.5 0.7 collective-permute-start.7
  55.2 0.7 collective-permute-start.8
  55.9 4.0 %shard_map.43 = (f32[1,1536]{1,0:T(1,128)S(1)}, f32[1,1536]{1,0:T(1,128)S(1)}, bf16[1024,768]{1,0:T(8,128)(2,1)S(1)}) custom-call(bf16[1152,768]{1,0:T(8,128)(2,1)S(1)} %shard_map.42.mine, bf16[512,768]{1,0:T(8,128)(2,1)S(1)} %shard_map.40.refs_1_.early), custom_call_target="tpu_custom_call" | custom-call | bytes 1 | tf_op jit(solution)/shard_map/pallas_call | solution.py:695
  59.8 0.0 collective-permute-done.6.early_j
  59.9 0.0 collective-permute-done.5.other
  59.9 4.9 %shard_map.44 = (f32[1,1536]{1,0:T(1,128)S(1)}, f32[1,1536]{1,0:T(1,128)S(1)}, s32[1,1]{1,0:T(1,128)}, f32[512,128]{1,0:T(8,128)S(1)}, f32[512,128]{1,0:T(8,128)S(1)}, /*index=5*/f32[1,2048]{1,0:T(1,128)S(1)}) custom-call(bf16[1152,768]{1,0:T(8,128)(2,1)S(1)} %shard_map.42.mine, bf16[1152,768]{1,0:T(8,128)(2,1)S(1)} %collective-permute-done.5.other, ...), custom_call_target="tpu_custom_call" | custom-call | bytes 1 | tf_op jit(solution)/shard_map/pallas_call | solution.py:695
  64.8 0.0 collective-permute-done.7.refs_0_
  64.8 0.0 collective-permute-done.8.refs_1_
  64.8 0.1 collective-permute-start.9
  64.9 2.2 %collective-permute-done.9.late_j = bf16[512,768]{1,0:T(8,128)(2,1)S(1)} collective-permute-done((bf16[512,768]{1,0:T(8,128)(2,1)S(1)}, bf16[512,768]{1,0:T(8,128)(2,1)S(1)}, u32[]{:S(2)}, u32[]{:S(2)}) %collective-permute-start.9) | collective-permute-done | bytes 786464 | tf_op jit(solution)/shard_map/ppermute | solution.py:765
  67.2 0.0 copy-start.1
  67.2 0.0 copy-start.3
  67.2 0.0 copy-start.5
  67.2 0.7 shard_map.47
  67.8 8.8 %all-to-all-start.3 = ((f32[16,1,256]{2,1,0:T(1,128)}), f32[16,1,256]{2,1,0:T(1,128)S(1)}, u32[]{:S(2)}, u32[]{:S(2)}) async-start(f32[16,1,256]{2,1,0:T(1,128)} %shard_map.47), calls=%async_computation.3 | async-start | bytes 32768 | tf_op jit(solution)/shard_map/all_to_all | solution.py:817
  77.3 5.8 %all-to-all-done.3 = f32[16,1,256]{2,1,0:T(1,128)S(1)} async-done(((f32[16,1,256]{2,1,0:T(1,128)}), f32[16,1,256]{2,1,0:T(1,128)S(1)}, u32[]{:S(2)}, u32[]{:S(2)}) %all-to-all-start.3) | async-done | bytes 16416 | tf_op jit(solution)/shard_map/all_to_all | solution.py:817
  83.2 0.0 copy-done.1
  83.2 0.0 copy-done.3
  83.2 0.0 copy-done.5
  83.2 0.1 conditional.1
  83.2 0.1 branch_1_fun.1
  83.3 0.0 copy-start.4
  83.3 0.6 copy-done.4
  (5 shorter events, 0.1 us)
Async XLA Ops:
  5.5 48.5 %all-to-all-start.2 = ((bf16[8,144,768]{2,1,0:T(8,128)(2,1)}), bf16[8,144,768]{2,1,0:T(8,128)(2,1)S(1)}, u32[]{:S(2)}, u32[]{:S(2)}) async-start(bf16[8,144,768]{2,1,0:T(8,128)(2,1)} %bitcast.12), calls=%async_computation.2 | async-start | bytes 3538944 | tf_op jit(solution)/shard_map/all_to_all | solution.py:770
  12.8 6.0 %collective-permute-start.4 = (bf16[128,768]{1,0:T(8,128)(2,1)S(1)}, bf16[128,768]{1,0:T(8,128)(2,1)S(1)}, u32[]{:S(2)}, u32[]{:S(2)}) collective-permute-start(bf16[128,768]{1,0:T(8,128)(2,1)S(1)} %get-tuple-element.39.refs_2_.refs_0_), channel_id=1, source_target_pairs={{12,8},{14,10},{13,9},{15,11},{28,24},{30,26},{29,25},{31,27}} | collective-permute-start | bytes 589832 | tf_op jit(solution)/shard_map/ppermute | solution.py:762
  13.4 33.1 %collective-permute-start.1 = (bf16[128,768]{1,0:T(8,128)(2,1)S(1)}, bf16[128,768]{1,0:T(8,128)(2,1)S(1)}, u32[]{:S(2)}, u32[]{:S(2)}) collective-permute-start(bf16[128,768]{1,0:T(8,128)(2,1)S(1)} %get-tuple-element.39.refs_2_.refs_0_), channel_id=1, source_target_pairs={{0,4},{1,5},{16,20},{17,21}} | collective-permute-start | bytes 589832 | tf_op jit(solution)/shard_map/ppermute | solution.py:762
  17.4 29.2 %collective-permute-start.2 = (bf16[128,768]{1,0:T(8,128)(2,1)S(1)}, bf16[128,768]{1,0:T(8,128)(2,1)S(1)}, u32[]{:S(2)}, u32[]{:S(2)}) collective-permute-start(bf16[128,768]{1,0:T(8,128)(2,1)S(1)} %get-tuple-element.39.refs_2_.refs_0_), channel_id=1, source_target_pairs={{2,4},{3,5},{18,20},{19,21}} | collective-permute-start | bytes 589832 | tf_op jit(solution)/shard_map/ppermute | solution.py:762
  18.1 28.5 %collective-permute-start.3 = (bf16[128,768]{1,0:T(8,128)(2,1)S(1)}, bf16[128,768]{1,0:T(8,128)(2,1)S(1)}, u32[]{:S(2)}, u32[]{:S(2)}) collective-permute-start(bf16[128,768]{1,0:T(8,128)(2,1)S(1)} %get-tuple-element.39.refs_2_.refs_0_), channel_id=1, source_target_pairs={{6,4},{7,5},{22,20},{23,21}} | collective-permute-start | bytes 589832 | tf_op jit(solution)/shard_map/ppermute | solution.py:762
  54.0 5.9 %collective-permute-start.5 = (bf16[1152,768]{1,0:T(8,128)(2,1)S(1)}, bf16[1152,768]{1,0:T(8,128)(2,1)S(1)}, u32[]{:S(2)}, u32[]{:S(2)}) collective-permute-start(bf16[1152,768]{1,0:T(8,128)(2,1)S(1)} %shard_map.42.mine), channel_id=1, source_target_pairs={{0,1},{1,0},{2,3},{3,2},{4,5},{5,4},{6,7},{7,6},{8,9},{9,8},{10,11... | collective-permute-start | bytes 5308424 | tf_op jit(solution)/shard_map/ppermute | solution.py:765
  54.0 5.8 %collective-permute-start.6 = (bf16[512,768]{1,0:T(8,128)(2,1)S(1)}, bf16[512,768]{1,0:T(8,128)(2,1)S(1)}, u32[]{:S(2)}, u32[]{:S(2)}) collective-permute-start(bf16[512,768]{1,0:T(8,128)(2,1)S(1)} %shard_map.40.refs_1_.early), channel_id=1, source_target_pairs={{0,1},{1,0},{2,3},{3,2},{4,5},{5,4},{6,7},{7,6},{8,9},{9,8},{10,11... | collective-permute-start | bytes 2359304 | tf_op jit(solution)/shard_map/ppermute | solution.py:765
  54.5 10.3 %collective-permute-start.7 = (bf16[256,768]{1,0:T(8,128)(2,1)S(1)}, bf16[256,768]{1,0:T(8,128)(2,1)S(1)}, u32[]{:S(2)}, u32[]{:S(2)}) collective-permute-start(bf16[256,768]{1,0:T(8,128)(2,1)S(1)} %shard_map.41.refs_2_), channel_id=1, source_target_pairs={{10,4},{11,5},{26,20},{27,21}} | collective-permute-start | bytes 1179656 | tf_op jit(solution)/shard_map/ppermute | solution.py:762
  55.2 9.6 %collective-permute-start.8 = (bf16[256,768]{1,0:T(8,128)(2,1)S(1)}, bf16[256,768]{1,0:T(8,128)(2,1)S(1)}, u32[]{:S(2)}, u32[]{:S(2)}) collective-permute-start(bf16[256,768]{1,0:T(8,128)(2,1)S(1)} %shard_map.41.refs_2_), channel_id=1, source_target_pairs={{8,4},{9,5},{24,20},{25,21}} | collective-permute-start | bytes 1179656 | tf_op jit(solution)/shard_map/ppermute | solution.py:762
  64.8 2.4 %collective-permute-start.9 = (bf16[512,768]{1,0:T(8,128)(2,1)S(1)}, bf16[512,768]{1,0:T(8,128)(2,1)S(1)}, u32[]{:S(2)}, u32[]{:S(2)}) collective-permute-start(bf16[512,768]{1,0:T(8,128)(2,1)S(1)} %shard_map.45.late), channel_id=1, source_target_pairs={{0,1},{1,0},{2,3},{3,2},{4,5},{5,4},{6,7},{7,6},{8,9},{9,8},{10,11... | collective-permute-start | bytes 2359304 | tf_op jit(solution)/shard_map/ppermute | solution.py:765
  67.2 16.0 %copy-start.1 = (bf16[1024,768]{1,0:T(8,128)(2,1)S(1)}, bf16[1024,768]{1,0:T(8,128)(2,1)}, u32[]{:S(2)}) copy-start(bf16[1024,768]{1,0:T(8,128)(2,1)} %x_hbm.1) | copy-start | bytes 4718596
  67.2 16.0 %copy-start.3 = (s32[1024]{0:T(1024)S(1)}, s32[1024]{0:T(1024)}, u32[]{:S(2)}) copy-start(s32[1024]{0:T(1024)} %param.6) | copy-start | bytes 12292
  67.2 16.0 %copy-start.5 = (s32[64]{0:T(128)S(1)}, s32[64]{0:T(128)}, u32[]{:S(2)}) copy-start(s32[64]{0:T(128)} %param.7) | copy-start | bytes 772
  67.8 15.4 %all-to-all-start.3 = ((f32[16,1,256]{2,1,0:T(1,128)}), f32[16,1,256]{2,1,0:T(1,128)S(1)}, u32[]{:S(2)}, u32[]{:S(2)}) async-start(f32[16,1,256]{2,1,0:T(1,128)} %shard_map.47), calls=%async_computation.3 | async-start | bytes 32768 | tf_op jit(solution)/shard_map/all_to_all | solution.py:817
  83.3 0.6 copy-start.4

commit v23 on v21

--- a/solution.py
+++ b/solution.py
@@ -230,8 +230,11 @@
     rows, width = x_ref.shape
     n_fine = map_ref.shape[1]
     per_owner = n_fine // n_owner
-    copies[1].wait()
-    copies[2].wait()
+    for copy in copies:
+        copy.wait()
+    x = x_ref[...].astype(jnp.float32)
+    squares = jnp.sum(x * x, axis=1, keepdims=True)
+    unit[...] = (x * lax.rsqrt(squares + epsilon)).astype(jnp.bfloat16)
     owner_row = map_ref[...].astype(jnp.float32)
     fine_row = lax.broadcasted_iota(jnp.int32, (1, n_fine), 1).astype(jnp.float32)
     key_row = owner_row * n_fine + fine_row
@@ -269,10 +272,6 @@
     fits = rank < jnp.where(place == home, lay.head, main - 1)
     slot = jnp.where(fits, place * main + rank, -1)
     tail_slot = jnp.where(place == home, rank - lay.head, -1)
-    copies[0].wait()
-    x = x_ref[...].astype(jnp.float32)
-    squares = jnp.sum(x * x, axis=1, keepdims=True)
-    unit[...] = (x * lax.rsqrt(squares + epsilon)).astype(jnp.bfloat16)
 
     def chosen_rows(slot, start, count):
         here = lax.broadcasted_iota(jnp.int32, (count, rows), 0) + start
@@ -371,7 +370,7 @@
 
 
 class Layout:
-    early, late = (0, 1, 2, 3), (4, 6, 5, 7)
+    early, late = (0, 1, 2, 3), (5, 7, 4, 6)
 
     def __init__(self, n_owner, n_fine, capacity, main, home):
         self.n_owner, self.n_fine, self.capacity = n_owner, n_fine, capacity
@@ -768,7 +767,7 @@
     ).reshape(n_owner * main, width)
     mine = after(mine, early, both)
     other, early_j = swap(mine), swap(early)
-    late = [hop(both, [(s, home)]) for s in (4, 5)]
+    late = [hop(both, [(s, home)]) for s in (5, 4)]
 
     def array(shape, dtype=jnp.float32):
         return jax.ShapeDtypeStruct(shape, dtype)

time: 84.9 us -> 84.2 us (level)
  starting transfers between devices: 24.9 us -> 24 us
    all_to_all x1, starting transfers between devices: 9.75 us -> 8.85 us  [body(): lax.all_to_all(results, ('cl', 'grp'), split_axis=0, concat_axis=0, tiled...]
where the time goes in v23:
time: 84.2 us; the launch traced here: 83.9 us
  waiting for transfers between devices  43.3 us (51%)
  starting transfers between devices  24 us (29%)
  Pallas kernels  15.1 us (18%)
    ppermute x6, waiting for transfers between devices, hop(): return lax.ppermute(x, 'cl', pairs)  27.8 us
    pallas_call x4, Pallas kernels, pair_call(): pl.pallas_call(functools.partial(kernel, lay), out_shape=out_shape, in_sp...  9.54 us
    all_to_all x1, starting transfers between devices, body(): lax.all_to_all(results, ('cl', 'grp'), split_axis=0, concat_axis=0, tiled...  8.85 us
    all_to_all x1, waiting for transfers between devices, body(): lax.all_to_all(packed.reshape(n_owner, main, width), 'cl', split_axis=0,...  7.44 us
    ppermute x6, starting transfers between devices, hop(): return lax.ppermute(x, 'cl', pairs)  7.3 us
    all_to_all x1, starting transfers between devices, body(): lax.all_to_all(packed.reshape(n_owner, main, width), 'cl', split_axis=0,...  7.29 us
    all_to_all x1, waiting for transfers between devices, body(): lax.all_to_all(results, ('cl', 'grp'), split_axis=0, concat_axis=0, tiled...  5.85 us
    pallas_call x1, Pallas kernels, place_rows(): pl.pallas_call(functools.partial(place_kernel, lay), out_shape=(jax.Shape...  5.44 us
  transfers between devices with their start and end apart: 11, of which 4 were waited for; matrix products, arithmetic and copies ran while one was open for 0% of the time, Pallas kernels for 11%

profile of v23, /device:TPU:0, one launch (start us, length us, event | category | flops | bytes accessed | tf_op | source)
XLA Modules:
  0.0 83.9 jit_solution(5081239592087792758)
XLA Ops:
  0.0 5.4 %shard_map.39 = (bf16[1152,768]{1,0:T(8,128)(2,1)}, bf16[128,768]{1,0:T(8,128)(2,1)S(1)}, s32[8,128]{1,0:T(8,128)S(1)}) custom-call(bf16[1024,768]{1,0:T(8,128)(2,1)} %x_hbm.1, s32[8,128]{1,0:T(8,128)} %bitcast.23, s32[1,64]{1,0:T(1,128)} %bitcast.27), custom_call_target="tpu_custom_call" | custom-call | tf_op jit(solution)/shard_map/pallas_call | solution.py:310
  5.5 7.3 %all-to-all-start.2 = ((bf16[8,144,768]{2,1,0:T(8,128)(2,1)}), bf16[8,144,768]{2,1,0:T(8,128)(2,1)S(1)}, u32[]{:S(2)}, u32[]{:S(2)}) async-start(bf16[8,144,768]{2,1,0:T(8,128)(2,1)} %bitcast.12), calls=%async_computation.2 | async-start | bytes 3538944 | tf_op jit(solution)/shard_map/all_to_all | solution.py:765
  12.7 0.7 collective-permute-start.4
  13.4 3.9 %collective-permute-start.1 = (bf16[128,768]{1,0:T(8,128)(2,1)S(1)}, bf16[128,768]{1,0:T(8,128)(2,1)S(1)}, u32[]{:S(2)}, u32[]{:S(2)}) collective-permute-start(bf16[128,768]{1,0:T(8,128)(2,1)S(1)} %get-tuple-element.39.refs_2_.refs_0_), channel_id=1, source_target_pairs={{0,4},{1,5},{16,20},{17,21}} | collective-permute-start | bytes 589832 | tf_op jit(solution)/shard_map/ppermute | solution.py:757
  17.4 0.7 collective-permute-start.2
  18.0 0.7 collective-permute-start.3
  18.7 0.0 collective-permute-done.4.refs_1_
  18.8 27.7 %collective-permute-done.1.refs_0_ = bf16[128,768]{1,0:T(8,128)(2,1)S(1)} collective-permute-done((bf16[128,768]{1,0:T(8,128)(2,1)S(1)}, bf16[128,768]{1,0:T(8,128)(2,1)S(1)}, u32[]{:S(2)}, u32[]{:S(2)}) %collective-permute-start.1) | collective-permute-done | bytes 196640 | tf_op jit(solution)/shard_map/ppermute | solution.py:757
  46.5 0.0 collective-permute-done.2.refs_1_
  46.5 0.0 collective-permute-done.3.refs_3_
  46.5 7.4 %all-to-all-done.2 = bf16[8,144,768]{2,1,0:T(8,128)(2,1)S(1)} async-done(((bf16[8,144,768]{2,1,0:T(8,128)(2,1)}), bf16[8,144,768]{2,1,0:T(8,128)(2,1)S(1)}, u32[]{:S(2)}, u32[]{:S(2)}) %all-to-all-start.2) | async-done | bytes 1769504 | tf_op jit(solution)/shard_map/all_to_all | solution.py:765
  54.0 0.0 collective-permute-start.5
  54.0 0.5 collective-permute-start.6
  54.5 0.7 collective-permute-start.7
  55.2 0.7 collective-permute-start.8
  55.9 4.0 %shard_map.43 = (f32[1,1536]{1,0:T(1,128)S(1)}, f32[1,1536]{1,0:T(1,128)S(1)}, bf16[1024,768]{1,0:T(8,128)(2,1)S(1)}) custom-call(bf16[1152,768]{1,0:T(8,128)(2,1)S(1)} %shard_map.42.mine, bf16[512,768]{1,0:T(8,128)(2,1)S(1)} %shard_map.40.refs_1_.early), custom_call_target="tpu_custom_call" | custom-call | bytes 1 | tf_op jit(solution)/shard_map/pallas_call | solution.py:690
  59.8 0.0 collective-permute-done.6.early_j
  59.8 0.0 collective-permute-done.5.other
  59.8 4.9 %shard_map.44 = (f32[1,1536]{1,0:T(1,128)S(1)}, f32[1,1536]{1,0:T(1,128)S(1)}, s32[1,1]{1,0:T(1,128)}, f32[512,128]{1,0:T(8,128)S(1)}, f32[512,128]{1,0:T(8,128)S(1)}, /*index=5*/f32[1,2048]{1,0:T(1,128)S(1)}) custom-call(bf16[1152,768]{1,0:T(8,128)(2,1)S(1)} %shard_map.42.mine, bf16[1152,768]{1,0:T(8,128)(2,1)S(1)} %collective-permute-done.5.other, ...), custom_call_target="tpu_custom_call" | custom-call | bytes 1 | tf_op jit(solution)/shard_map/pallas_call | solution.py:690
  64.7 0.0 collective-permute-done.7.refs_0_
  64.7 0.0 collective-permute-done.8.refs_1_
  64.8 0.1 collective-permute-start.9
  64.9 2.2 %collective-permute-done.9.late_j = bf16[512,768]{1,0:T(8,128)(2,1)S(1)} collective-permute-done((bf16[512,768]{1,0:T(8,128)(2,1)S(1)}, bf16[512,768]{1,0:T(8,128)(2,1)S(1)}, u32[]{:S(2)}, u32[]{:S(2)}) %collective-permute-start.9) | collective-permute-done | bytes 786464 | tf_op jit(solution)/shard_map/ppermute | solution.py:760
  67.1 0.0 copy-start.1
  67.1 0.0 copy-start.3
  67.1 0.0 copy-start.5
  67.1 0.7 shard_map.47
  67.8 8.9 %all-to-all-start.3 = ((f32[16,1,256]{2,1,0:T(1,128)}), f32[16,1,256]{2,1,0:T(1,128)S(1)}, u32[]{:S(2)}, u32[]{:S(2)}) async-start(f32[16,1,256]{2,1,0:T(1,128)} %shard_map.47), calls=%async_computation.3 | async-start | bytes 32768 | tf_op jit(solution)/shard_map/all_to_all | solution.py:812
  77.3 5.8 %all-to-all-done.3 = f32[16,1,256]{2,1,0:T(1,128)S(1)} async-done(((f32[16,1,256]{2,1,0:T(1,128)}), f32[16,1,256]{2,1,0:T(1,128)S(1)}, u32[]{:S(2)}, u32[]{:S(2)}) %all-to-all-start.3) | async-done | bytes 16416 | tf_op jit(solution)/shard_map/all_to_all | solution.py:812
  83.2 0.0 copy-done.1
  83.2 0.0 copy-done.3
  83.2 0.0 copy-done.5
  83.2 0.1 conditional.1
  83.2 0.1 branch_1_fun.1
  83.3 0.0 copy-start.4
  83.3 0.6 copy-done.4
  (5 shorter events, 0.1 us)
Async XLA Ops:
  5.5 48.5 %all-to-all-start.2 = ((bf16[8,144,768]{2,1,0:T(8,128)(2,1)}), bf16[8,144,768]{2,1,0:T(8,128)(2,1)S(1)}, u32[]{:S(2)}, u32[]{:S(2)}) async-start(bf16[8,144,768]{2,1,0:T(8,128)(2,1)} %bitcast.12), calls=%async_computation.2 | async-start | bytes 3538944 | tf_op jit(solution)/shard_map/all_to_all | solution.py:765
  12.7 6.0 %collective-permute-start.4 = (bf16[128,768]{1,0:T(8,128)(2,1)S(1)}, bf16[128,768]{1,0:T(8,128)(2,1)S(1)}, u32[]{:S(2)}, u32[]{:S(2)}) collective-permute-start(bf16[128,768]{1,0:T(8,128)(2,1)S(1)} %get-tuple-element.39.refs_2_.refs_0_), channel_id=1, source_target_pairs={{12,8},{14,10},{13,9},{15,11},{28,24},{30,26},{29,25},{31,27}} | collective-permute-start | bytes 589832 | tf_op jit(solution)/shard_map/ppermute | solution.py:757
  13.4 33.1 %collective-permute-start.1 = (bf16[128,768]{1,0:T(8,128)(2,1)S(1)}, bf16[128,768]{1,0:T(8,128)(2,1)S(1)}, u32[]{:S(2)}, u32[]{:S(2)}) collective-permute-start(bf16[128,768]{1,0:T(8,128)(2,1)S(1)} %get-tuple-element.39.refs_2_.refs_0_), channel_id=1, source_target_pairs={{0,4},{1,5},{16,20},{17,21}} | collective-permute-start | bytes 589832 | tf_op jit(solution)/shard_map/ppermute | solution.py:757
  17.4 29.2 %collective-permute-start.2 = (bf16[128,768]{1,0:T(8,128)(2,1)S(1)}, bf16[128,768]{1,0:T(8,128)(2,1)S(1)}, u32[]{:S(2)}, u32[]{:S(2)}) collective-permute-start(bf16[128,768]{1,0:T(8,128)(2,1)S(1)} %get-tuple-element.39.refs_2_.refs_0_), channel_id=1, source_target_pairs={{2,4},{3,5},{18,20},{19,21}} | collective-permute-start | bytes 589832 | tf_op jit(solution)/shard_map/ppermute | solution.py:757
  18.0 28.5 %collective-permute-start.3 = (bf16[128,768]{1,0:T(8,128)(2,1)S(1)}, bf16[128,768]{1,0:T(8,128)(2,1)S(1)}, u32[]{:S(2)}, u32[]{:S(2)}) collective-permute-start(bf16[128,768]{1,0:T(8,128)(2,1)S(1)} %get-tuple-element.39.refs_2_.refs_0_), channel_id=1, source_target_pairs={{6,4},{7,5},{22,20},{23,21}} | collective-permute-start | bytes 589832 | tf_op jit(solution)/shard_map/ppermute | solution.py:757
  54.0 5.9 %collective-permute-start.5 = (bf16[1152,768]{1,0:T(8,128)(2,1)S(1)}, bf16[1152,768]{1,0:T(8,128)(2,1)S(1)}, u32[]{:S(2)}, u32[]{:S(2)}) collective-permute-start(bf16[1152,768]{1,0:T(8,128)(2,1)S(1)} %shard_map.42.mine), channel_id=1, source_target_pairs={{0,1},{1,0},{2,3},{3,2},{4,5},{5,4},{6,7},{7,6},{8,9},{9,8},{10,11... | collective-permute-start | bytes 5308424 | tf_op jit(solution)/shard_map/ppermute | solution.py:760
  54.0 5.9 %collective-permute-start.6 = (bf16[512,768]{1,0:T(8,128)(2,1)S(1)}, bf16[512,768]{1,0:T(8,128)(2,1)S(1)}, u32[]{:S(2)}, u32[]{:S(2)}) collective-permute-start(bf16[512,768]{1,0:T(8,128)(2,1)S(1)} %shard_map.40.refs_1_.early), channel_id=1, source_target_pairs={{0,1},{1,0},{2,3},{3,2},{4,5},{5,4},{6,7},{7,6},{8,9},{9,8},{10,11... | collective-permute-start | bytes 2359304 | tf_op jit(solution)/shard_map/ppermute | solution.py:760
  54.5 10.3 %collective-permute-start.7 = (bf16[256,768]{1,0:T(8,128)(2,1)S(1)}, bf16[256,768]{1,0:T(8,128)(2,1)S(1)}, u32[]{:S(2)}, u32[]{:S(2)}) collective-permute-start(bf16[256,768]{1,0:T(8,128)(2,1)S(1)} %shard_map.41.refs_2_), channel_id=1, source_target_pairs={{10,4},{11,5},{26,20},{27,21}} | collective-permute-start | bytes 1179656 | tf_op jit(solution)/shard_map/ppermute | solution.py:757
  55.2 9.6 %collective-permute-start.8 = (bf16[256,768]{1,0:T(8,128)(2,1)S(1)}, bf16[256,768]{1,0:T(8,128)(2,1)S(1)}, u32[]{:S(2)}, u32[]{:S(2)}) collective-permute-start(bf16[256,768]{1,0:T(8,128)(2,1)S(1)} %shard_map.41.refs_2_), channel_id=1, source_target_pairs={{8,4},{9,5},{24,20},{25,21}} | collective-permute-start | bytes 1179656 | tf_op jit(solution)/shard_map/ppermute | solution.py:757
  64.8 2.4 %collective-permute-start.9 = (bf16[512,768]{1,0:T(8,128)(2,1)S(1)}, bf16[512,768]{1,0:T(8,128)(2,1)S(1)}, u32[]{:S(2)}, u32[]{:S(2)}) collective-permute-start(bf16[512,768]{1,0:T(8,128)(2,1)S(1)} %shard_map.45.late), channel_id=1, source_target_pairs={{0,1},{1,0},{2,3},{3,2},{4,5},{5,4},{6,7},{7,6},{8,9},{9,8},{10,11... | collective-permute-start | bytes 2359304 | tf_op jit(solution)/shard_map/ppermute | solution.py:760
  67.1 16.0 %copy-start.1 = (bf16[1024,768]{1,0:T(8,128)(2,1)S(1)}, bf16[1024,768]{1,0:T(8,128)(2,1)}, u32[]{:S(2)}) copy-start(bf16[1024,768]{1,0:T(8,128)(2,1)} %x_hbm.1) | copy-start | bytes 4718596
  67.1 16.0 %copy-start.3 = (s32[1024]{0:T(1024)S(1)}, s32[1024]{0:T(1024)}, u32[]{:S(2)}) copy-start(s32[1024]{0:T(1024)} %param.6) | copy-start | bytes 12292
  67.1 16.0 %copy-start.5 = (s32[64]{0:T(128)S(1)}, s32[64]{0:T(128)}, u32[]{:S(2)}) copy-start(s32[64]{0:T(128)} %param.7) | copy-start | bytes 772
  67.8 15.4 %all-to-all-start.3 = ((f32[16,1,256]{2,1,0:T(1,128)}), f32[16,1,256]{2,1,0:T(1,128)S(1)}, u32[]{:S(2)}, u32[]{:S(2)}) async-start(f32[16,1,256]{2,1,0:T(1,128)} %shard_map.47), calls=%async_computation.3 | async-start | bytes 32768 | tf_op jit(solution)/shard_map/all_to_all | solution.py:812
  83.3 0.6 copy-start.4

commit v24 on v21

--- a/solution.py
+++ b/solution.py
@@ -371,7 +371,7 @@
 
 
 class Layout:
-    early, late = (0, 1, 2, 3), (4, 6, 5, 7)
+    early, late = (0, 1, 2, 3), (5, 4, 7, 6)
 
     def __init__(self, n_owner, n_fine, capacity, main, home):
         self.n_owner, self.n_fine, self.capacity = n_owner, n_fine, capacity
@@ -760,15 +760,15 @@
     def swap(x):
         return lax.ppermute(x, "grp", [(0, 1), (1, 0)])
 
-    both = lay_out([extra, hop(extra, [(6, 4), (7, 5)])])
-    early = [extra if s == home else hop(extra, [(s, home)]) for s in lay.early]
-    early = lay_out(early, home)
+    arrived = {s: extra if s == home else hop(extra, [(s, home)]) for s in (0, 1, 2, 3, 5, 4)}
+    early = lay_out([arrived[s] for s in lay.early], home)
     mine = lax.all_to_all(
         packed.reshape(n_owner, main, width), "cl", split_axis=0, concat_axis=0, tiled=True
     ).reshape(n_owner * main, width)
-    mine = after(mine, early, both)
-    other, early_j = swap(mine), swap(early)
-    late = [hop(both, [(s, home)]) for s in (4, 5)]
+    mine = after(mine, early)
+    other = swap(mine)
+    early_j = swap(lay_out([early], home, (arrived[5], arrived[4])))
+    late = [arrived[5], arrived[4]] + [hop(extra, [(s, home)]) for s in (7, 6)]
 
     def array(shape, dtype=jnp.float32):
         return jax.ShapeDtypeStruct(shape, dtype)

time: 84.9 us -> 91.3 us (1.075)
  starting transfers between devices: 24.9 us -> 30.6 us
    all_to_all x1, starting transfers between devices: 9.75 us -> 14.7 us  [body(): lax.all_to_all(results, ('cl', 'grp'), split_axis=0, concat_axis=0, tiled...]
    ppermute x6 -> x7, waiting for transfers between devices: 27.8 us -> 28.5 us  [hop(): return lax.ppermute(x, 'cl', pairs)]
    ppermute x6 -> x7, starting transfers between devices: 7.3 us -> 7.94 us  [hop(): return lax.ppermute(x, 'cl', pairs)]
  transfers between devices with their start and end apart: 11 -> 12, of which waited for: 4 -> 4; matrix products, arithmetic and copies ran while one was open for 0% -> 0% of each run, Pallas kernels for 11% -> 10%
where the time goes in v24:
time: 91.3 us; the launch traced here: 91 us
  waiting for transfers between devices  44 us (48%)
  starting transfers between devices  30.6 us (34%)
  Pallas kernels  14.9 us (16%)
    ppermute x7, waiting for transfers between devices, hop(): return lax.ppermute(x, 'cl', pairs)  28.5 us
    all_to_all x1, starting transfers between devices, body(): lax.all_to_all(results, ('cl', 'grp'), split_axis=0, concat_axis=0, tiled...  14.7 us
    pallas_call x4, Pallas kernels, pair_call(): pl.pallas_call(functools.partial(kernel, lay), out_shape=out_shape, in_sp...  9.54 us
    ppermute x7, starting transfers between devices, hop(): return lax.ppermute(x, 'cl', pairs)  7.94 us
    all_to_all x1, waiting for transfers between devices, body(): lax.all_to_all(packed.reshape(n_owner, main, width), 'cl', split_axis=0,...  7.44 us
    all_to_all x1, starting transfers between devices, body(): lax.all_to_all(packed.reshape(n_owner, main, width), 'cl', split_axis=0,...  7.29 us
    all_to_all x1, waiting for transfers between devices, body(): lax.all_to_all(results, ('cl', 'grp'), split_axis=0, concat_axis=0, tiled...  5.85 us
    pallas_call x1, Pallas kernels, place_rows(): pl.pallas_call(functools.partial(place_kernel, lay), out_shape=(jax.Shape...  5.23 us
  transfers between devices with their start and end apart: 12, of which 4 were waited for; matrix products, arithmetic and copies ran while one was open for 0% of the time, Pallas kernels for 10%

profile of v24, /device:TPU:0, one launch (start us, length us, event | category | flops | bytes accessed | tf_op | source)
XLA Modules:
  0.0 91.0 jit_solution(5116526243593172923)
XLA Ops:
  0.0 5.2 %shard_map.39 = (bf16[1152,768]{1,0:T(8,128)(2,1)}, bf16[128,768]{1,0:T(8,128)(2,1)S(1)}, s32[8,128]{1,0:T(8,128)S(1)}) custom-call(bf16[1024,768]{1,0:T(8,128)(2,1)} %x_hbm.1, s32[8,128]{1,0:T(8,128)} %bitcast.23, s32[1,64]{1,0:T(1,128)} %bitcast.27), custom_call_target="tpu_custom_call" | custom-call | tf_op jit(solution)/shard_map/pallas_call | solution.py:311
  5.2 7.3 %all-to-all-start.2 = ((bf16[8,144,768]{2,1,0:T(8,128)(2,1)}), bf16[8,144,768]{2,1,0:T(8,128)(2,1)S(1)}, u32[]{:S(2)}, u32[]{:S(2)}) async-start(bf16[8,144,768]{2,1,0:T(8,128)(2,1)} %bitcast.12), calls=%async_computation.2 | async-start | bytes 3538944 | tf_op jit(solution)/shard_map/all_to_all | solution.py:765
  12.5 3.9 %collective-permute-start.1 = (bf16[128,768]{1,0:T(8,128)(2,1)S(1)}, bf16[128,768]{1,0:T(8,128)(2,1)S(1)}, u32[]{:S(2)}, u32[]{:S(2)}) collective-permute-start(bf16[128,768]{1,0:T(8,128)(2,1)S(1)} %get-tuple-element.39.refs_2_), channel_id=1, source_target_pairs={{0,4},{1,5},{16,20},{17,21}} | collective-permute-start | bytes 589832 | tf_op jit(solution)/shard_map/ppermute | solution.py:758
  16.5 0.7 collective-permute-start.2
  17.1 0.7 collective-permute-start.3
  17.8 28.5 %collective-permute-done.1.refs_0_ = bf16[128,768]{1,0:T(8,128)(2,1)S(1)} collective-permute-done((bf16[128,768]{1,0:T(8,128)(2,1)S(1)}, bf16[128,768]{1,0:T(8,128)(2,1)S(1)}, u32[]{:S(2)}, u32[]{:S(2)}) %collective-permute-start.1) | collective-permute-done | bytes 196640 | tf_op jit(solution)/shard_map/ppermute | solution.py:758
  46.3 0.0 collective-permute-done.2.refs_1_
  46.3 0.0 collective-permute-done.3.refs_3_
  46.3 7.4 %all-to-all-done.2 = bf16[8,144,768]{2,1,0:T(8,128)(2,1)S(1)} async-done(((bf16[8,144,768]{2,1,0:T(8,128)(2,1)}), bf16[8,144,768]{2,1,0:T(8,128)(2,1)S(1)}, u32[]{:S(2)}, u32[]{:S(2)}) %all-to-all-start.2) | async-done | bytes 1769504 | tf_op jit(solution)/shard_map/all_to_all | solution.py:765
  53.7 0.0 collective-permute-start.4
  53.8 0.7 collective-permute-start.5
  54.4 0.7 collective-permute-start.6
  55.1 0.0 collective-permute-done.5.refs_1_.refs_0_
  55.1 0.0 collective-permute-done.6.refs_2_.refs_1_
  55.1 0.6 collective-permute-start.7
  55.7 0.7 collective-permute-start.8
  56.4 0.7 collective-permute-start.9
  57.1 4.0 %shard_map.43 = (f32[1,1536]{1,0:T(1,128)S(1)}, f32[1,1536]{1,0:T(1,128)S(1)}, bf16[1024,768]{1,0:T(8,128)(2,1)S(1)}) custom-call(bf16[1152,768]{1,0:T(8,128)(2,1)S(1)} %shard_map.41.mine, bf16[512,768]{1,0:T(8,128)(2,1)S(1)} %shard_map.40.refs_1_.refs_0_.early), custom_call_target="tpu_custom_call" | custom-call | bytes 1 | tf_op jit(solution)/shard_map/pallas_call | solution.py:691
  61.0 0.0 collective-permute-done.7.early_j
  61.0 0.0 collective-permute-done.4.other
  61.1 4.9 %shard_map.44 = (f32[1,1536]{1,0:T(1,128)S(1)}, f32[1,1536]{1,0:T(1,128)S(1)}, s32[1,1]{1,0:T(1,128)}, f32[512,128]{1,0:T(8,128)S(1)}, f32[512,128]{1,0:T(8,128)S(1)}, /*index=5*/f32[1,2048]{1,0:T(1,128)S(1)}) custom-call(bf16[1152,768]{1,0:T(8,128)(2,1)S(1)} %shard_map.41.mine, bf16[1152,768]{1,0:T(8,128)(2,1)S(1)} %collective-permute-done.4.other, ...), custom_call_target="tpu_custom_call" | custom-call | bytes 1 | tf_op jit(solution)/shard_map/pallas_call | solution.py:691
  66.0 0.0 collective-permute-done.8.refs_2_
  66.0 0.0 collective-permute-done.9.refs_3_
  66.0 0.1 collective-permute-start.10
  66.1 2.2 %collective-permute-done.10.late_j = bf16[512,768]{1,0:T(8,128)(2,1)S(1)} collective-permute-done((bf16[512,768]{1,0:T(8,128)(2,1)S(1)}, bf16[512,768]{1,0:T(8,128)(2,1)S(1)}, u32[]{:S(2)}, u32[]{:S(2)}) %collective-permute-start.10) | collective-permute-done | bytes 786464 | tf_op jit(solution)/shard_map/ppermute | solution.py:761
  68.4 0.0 copy-start.1
  68.4 0.0 copy-start.3
  68.4 0.0 copy-start.5
  68.4 0.7 shard_map.47
  69.0 14.7 %all-to-all-start.3 = ((f32[16,1,256]{2,1,0:T(1,128)}), f32[16,1,256]{2,1,0:T(1,128)S(1)}, u32[]{:S(2)}, u32[]{:S(2)}) async-start(f32[16,1,256]{2,1,0:T(1,128)} %shard_map.47), calls=%async_computation.3 | async-start | bytes 32768 | tf_op jit(solution)/shard_map/all_to_all | solution.py:813
  84.4 5.8 %all-to-all-done.3 = f32[16,1,256]{2,1,0:T(1,128)S(1)} async-done(((f32[16,1,256]{2,1,0:T(1,128)}), f32[16,1,256]{2,1,0:T(1,128)S(1)}, u32[]{:S(2)}, u32[]{:S(2)}) %all-to-all-start.3) | async-done | bytes 16416 | tf_op jit(solution)/shard_map/all_to_all | solution.py:813
  90.2 0.0 copy-done.1
  90.2 0.0 copy-done.3
  90.2 0.0 copy-done.5
  90.2 0.1 conditional.1
  90.3 0.1 branch_1_fun.1
  90.4 0.0 copy-start.4
  90.4 0.6 copy-done.4
  (5 shorter events, 0.0 us)
Async XLA Ops:
  5.2 48.5 %all-to-all-start.2 = ((bf16[8,144,768]{2,1,0:T(8,128)(2,1)}), bf16[8,144,768]{2,1,0:T(8,128)(2,1)S(1)}, u32[]{:S(2)}, u32[]{:S(2)}) async-start(bf16[8,144,768]{2,1,0:T(8,128)(2,1)} %bitcast.12), calls=%async_computation.2 | async-start | bytes 3538944 | tf_op jit(solution)/shard_map/all_to_all | solution.py:765
  12.5 33.8 %collective-permute-start.1 = (bf16[128,768]{1,0:T(8,128)(2,1)S(1)}, bf16[128,768]{1,0:T(8,128)(2,1)S(1)}, u32[]{:S(2)}, u32[]{:S(2)}) collective-permute-start(bf16[128,768]{1,0:T(8,128)(2,1)S(1)} %get-tuple-element.39.refs_2_), channel_id=1, source_target_pairs={{0,4},{1,5},{16,20},{17,21}} | collective-permute-start | bytes 589832 | tf_op jit(solution)/shard_map/ppermute | solution.py:758
  16.5 29.8 %collective-permute-start.2 = (bf16[128,768]{1,0:T(8,128)(2,1)S(1)}, bf16[128,768]{1,0:T(8,128)(2,1)S(1)}, u32[]{:S(2)}, u32[]{:S(2)}) collective-permute-start(bf16[128,768]{1,0:T(8,128)(2,1)S(1)} %get-tuple-element.39.refs_2_), channel_id=1, source_target_pairs={{2,4},{3,5},{18,20},{19,21}} | collective-permute-start | bytes 589832 | tf_op jit(solution)/shard_map/ppermute | solution.py:758
  17.1 29.2 %collective-permute-start.3 = (bf16[128,768]{1,0:T(8,128)(2,1)S(1)}, bf16[128,768]{1,0:T(8,128)(2,1)S(1)}, u32[]{:S(2)}, u32[]{:S(2)}) collective-permute-start(bf16[128,768]{1,0:T(8,128)(2,1)S(1)} %get-tuple-element.39.refs_2_), channel_id=1, source_target_pairs={{6,4},{7,5},{22,20},{23,21}} | collective-permute-start | bytes 589832 | tf_op jit(solution)/shard_map/ppermute | solution.py:758
  53.7 7.3 %collective-permute-start.4 = (bf16[1152,768]{1,0:T(8,128)(2,1)S(1)}, bf16[1152,768]{1,0:T(8,128)(2,1)S(1)}, u32[]{:S(2)}, u32[]{:S(2)}) collective-permute-start(bf16[1152,768]{1,0:T(8,128)(2,1)S(1)} %shard_map.41.mine), channel_id=1, source_target_pairs={{0,1},{1,0},{2,3},{3,2},{4,5},{5,4},{6,7},{7,6},{8,9},{9,8},{10,11... | collective-permute-start | bytes 5308424 | tf_op jit(solution)/shard_map/ppermute | solution.py:761
  53.8 1.4 %collective-permute-start.5 = (bf16[128,768]{1,0:T(8,128)(2,1)S(1)}, bf16[128,768]{1,0:T(8,128)(2,1)S(1)}, u32[]{:S(2)}, u32[]{:S(2)}) collective-permute-start(bf16[128,768]{1,0:T(8,128)(2,1)S(1)} %get-tuple-element.39.refs_2_), channel_id=1, source_target_pairs={{10,4},{11,5},{26,20},{27,21}} | collective-permute-start | bytes 589832 | tf_op jit(solution)/shard_map/ppermute | solution.py:758
  54.4 0.7 collective-permute-start.6
  55.1 5.9 %collective-permute-start.7 = (bf16[512,768]{1,0:T(8,128)(2,1)S(1)}, bf16[512,768]{1,0:T(8,128)(2,1)S(1)}, u32[]{:S(2)}, u32[]{:S(2)}) collective-permute-start(bf16[512,768]{1,0:T(8,128)(2,1)S(1)} %shard_map.42), channel_id=1, source_target_pairs={{0,1},{1,0},{2,3},{3,2},{4,5},{5,4},{6,7},{7,6},{8,9},{9,8},{10,11... | collective-permute-start | bytes 2359304 | tf_op jit(solution)/shard_map/ppermute | solution.py:761
  55.7 10.2 %collective-permute-start.8 = (bf16[128,768]{1,0:T(8,128)(2,1)S(1)}, bf16[128,768]{1,0:T(8,128)(2,1)S(1)}, u32[]{:S(2)}, u32[]{:S(2)}) collective-permute-start(bf16[128,768]{1,0:T(8,128)(2,1)S(1)} %get-tuple-element.39.refs_2_), channel_id=1, source_target_pairs={{14,4},{15,5},{30,20},{31,21}} | collective-permute-start | bytes 589832 | tf_op jit(solution)/shard_map/ppermute | solution.py:758
  56.4 9.6 %collective-permute-start.9 = (bf16[128,768]{1,0:T(8,128)(2,1)S(1)}, bf16[128,768]{1,0:T(8,128)(2,1)S(1)}, u32[]{:S(2)}, u32[]{:S(2)}) collective-permute-start(bf16[128,768]{1,0:T(8,128)(2,1)S(1)} %get-tuple-element.39.refs_2_), channel_id=1, source_target_pairs={{12,4},{13,5},{28,20},{29,21}} | collective-permute-start | bytes 589832 | tf_op jit(solution)/shard_map/ppermute | solution.py:758
  66.0 2.4 %collective-permute-start.10 = (bf16[512,768]{1,0:T(8,128)(2,1)S(1)}, bf16[512,768]{1,0:T(8,128)(2,1)S(1)}, u32[]{:S(2)}, u32[]{:S(2)}) collective-permute-start(bf16[512,768]{1,0:T(8,128)(2,1)S(1)} %shard_map.45.late), channel_id=1, source_target_pairs={{0,1},{1,0},{2,3},{3,2},{4,5},{5,4},{6,7},{7,6},{8,9},{9,8},{10,11... | collective-permute-start | bytes 2359304 | tf_op jit(solution)/shard_map/ppermute | solution.py:761
  68.4 21.9 %copy-start.1 = (bf16[1024,768]{1,0:T(8,128)(2,1)S(1)}, bf16[1024,768]{1,0:T(8,128)(2,1)}, u32[]{:S(2)}) copy-start(bf16[1024,768]{1,0:T(8,128)(2,1)} %x_hbm.1) | copy-start | bytes 4718596
  68.4 21.9 %copy-start.3 = (s32[1024]{0:T(1024)S(1)}, s32[1024]{0:T(1024)}, u32[]{:S(2)}) copy-start(s32[1024]{0:T(1024)} %param.6) | copy-start | bytes 12292
  68.4 21.9 %copy-start.5 = (s32[64]{0:T(128)S(1)}, s32[64]{0:T(128)}, u32[]{:S(2)}) copy-start(s32[64]{0:T(128)} %param.7) | copy-start | bytes 772
  69.0 21.2 %all-to-all-start.3 = ((f32[16,1,256]{2,1,0:T(1,128)}), f32[16,1,256]{2,1,0:T(1,128)S(1)}, u32[]{:S(2)}, u32[]{:S(2)}) async-start(f32[16,1,256]{2,1,0:T(1,128)} %shard_map.47), calls=%async_computation.3 | async-start | bytes 32768 | tf_op jit(solution)/shard_map/all_to_all | solution.py:813
  90.4 0.6 copy-start.4

commit v25 on v21

--- a/solution.py
+++ b/solution.py
@@ -371,7 +371,7 @@
 
 
 class Layout:
-    early, late = (0, 1, 2, 3), (4, 6, 5, 7)
+    early, late = (0, 1, 2, 3), (5, 7, 4, 6)
 
     def __init__(self, n_owner, n_fine, capacity, main, home):
         self.n_owner, self.n_fine, self.capacity = n_owner, n_fine, capacity
@@ -534,7 +534,7 @@
     return put
 
 
-def inner_kernel(lay, mine, early, sums, lab_lane, rows, lab_sub, bias, back, buf_a, buf_b):
+def inner_kernel(lay, mine, early, sums, lab_lane, lab_sub, rows, bias, back, buf_a, buf_b):
     is_home = lax.axis_index("cl") == lay.home
     infos = lines_of(lay, mine)
     buffers = (buf_a, buf_b)
@@ -577,8 +577,8 @@
 
 
 def cross_kernel(lay, mine, other, early, early_j, rows, sums, lab_lane, *refs):
-    total, for_other, unfit_ref, late_sub, late_sub_j, long_lane = refs[:6]
-    lab_sub, bias, back, rows_j, buf_a, buf_b = refs[6:]
+    total, for_other, unfit_ref, late_sub, late_sub_j, long_lane, late_lane_j = refs[:7]
+    lab_sub, bias, back, rows_j, buf_a, buf_b = refs[7:]
     is_home = lax.axis_index("cl") == lay.home
     infos = lines_of(lay, other)
     own = lines_of(lay, mine)
@@ -619,6 +619,7 @@
         write_labels(lay, infos, lay.late, lay.head, lay.rest, 0, late_sub_j, None)
         long_lane[:, : lay.n_first] = lab_lane[...]
         turn_labels(lay, late_sub, lay.n_late, long_lane, lay.n_first)
+        turn_labels(lay, late_sub_j, lay.n_late, late_lane_j, 0)
         for_other[...] = jnp.zeros(for_other.shape, jnp.float32)
         turn_sums(back, lay.n_first, for_other, 0)
 
@@ -629,27 +630,30 @@
         stream((mine, lay.n_main, 0), tiles, lab_lane, buffers, adder(total))
 
 
-def late_pairs(lay, i_refs, late_j, late_sub, back, lab_lane, buffers, put):
-    rows, early = i_refs
-    lates = [(late_j, lay.n_late, late_sub, None, 0, 2, back)]
-    stream((rows, lay.n_head, 0), lates, lab_lane, buffers, put)
-    stream((early, lay.n_early, lay.n_head), lates, lab_lane, buffers, put)
-
-
-def inner_late_kernel(lay, early, late, rows, late_sub, lab_lane, sums, back, buf_a, buf_b):
+def first_tiles(lay, rows, early, lab_sub, back):
+    return [
+        (rows, lay.n_head, lab_sub, None, 0, 4, back),
+        (early, lay.n_early, lab_sub, None, lay.n_head, 2, back),
+    ]
+
+
+def inner_late_kernel(lay, early, late, rows, lab_sub, late_sub, lab_lane, sums, *refs):
+    back, buf_a, buf_b = refs
+
     @pl.when(lax.axis_index("cl") == lay.home)
     def _():
-        buffers = (buf_a, buf_b)
         back[...] = jnp.zeros(back.shape, jnp.float32)
-        put = setter(sums)
-        late_pairs(lay, (rows, early), late, late_sub, back, lab_lane, buffers, put)
-        tiles = [(late, lay.n_late, late_sub, None, 0, 2, None)]
-        stream((late, lay.n_late, lay.n_first), tiles, lab_lane, buffers, put)
-        turn_sums(back, lay.n_late, sums, lay.n_first)
-
-
-def cross_late_kernel(lay, early, late, late_j, rows, late_sub, lab_lane, first_lane, *refs):
-    first_sums, first_other, sums, out_ref, total, back, buf_a, buf_b = refs
+        sums[:, : lay.n_first] = jnp.zeros((1, lay.n_first), jnp.float32)
+        tiles = first_tiles(lay, rows, early, lab_sub, back)
+        tiles.append((late, lay.n_late, late_sub, None, 0, 2, None))
+        lanes = (late, lay.n_late, lay.n_first)
+        stream(lanes, tiles, lab_lane, (buf_a, buf_b), setter(sums))
+        turn_sums(back, lay.n_first, sums, 0)
+
+
+def cross_late_kernel(lay, early, late, late_j, rows, lab_sub, late_sub, lab_lane, *refs):
+    late_lane, first_lane, first_sums, first_other, sums, out_ref = refs[:6]
+    total, late_other, back, late_back, buf_a, buf_b = refs[6:]
     is_home = lax.axis_index("cl") == lay.home
     grp = lax.axis_index("grp")
 
@@ -658,9 +662,14 @@
         total[...] = sums[...]
         total[:, : lay.n_first] += first_sums[...]
         back[...] = jnp.zeros(back.shape, jnp.float32)
-        buffers, put = (buf_a, buf_b), adder(total)
-        late_pairs(lay, (rows, early), late_j, late_sub, back, lab_lane, buffers, put)
-        half_blocks(late, late_j, late_sub, 0, back, lay.n_first, lab_lane, buffers, put)
+        late_back[...] = jnp.zeros(late_back.shape, jnp.float32)
+        buffers = (buf_a, buf_b)
+        tiles = first_tiles(lay, rows, early, lab_sub, back)
+        stream((late_j, lay.n_late, 0), tiles, late_lane, buffers, setter(late_other))
+        turn_sums(back, lay.n_first, total, 0)
+        put = adder(total)
+        half_blocks(late, late_j, late_sub, 0, late_back, lay.n_first, lab_lane, buffers, put)
+        turn_sums(late_back, lay.n_late, late_other, 0)
 
         def write(line, values):
             for source in range(lay.n_owner):
@@ -672,8 +681,7 @@
 
         write(grp, total[...])
         total[:, : lay.n_first] = first_other[...]
-        total[:, lay.n_first :] = jnp.zeros((1, lay.n_late), jnp.float32)
-        turn_sums(back, lay.n_late, total, lay.n_first)
+        total[:, lay.n_first :] = late_other[...]
         write(1 - grp, total[...])
 
     @pl.when(jnp.logical_not(is_home))
@@ -768,7 +776,7 @@
     ).reshape(n_owner * main, width)
     mine = after(mine, early, both)
     other, early_j = swap(mine), swap(early)
-    late = [hop(both, [(s, home)]) for s in (4, 5)]
+    late = [hop(both, [(s, home)]) for s in (5, 4)]
 
     def array(shape, dtype=jnp.float32):
         return jax.ShapeDtypeStruct(shape, dtype)
@@ -779,17 +787,18 @@
     row, long_row = array((1, lay.n_first)), array((1, lay.n_all))
     bias = scratch((lay.n_main, LANES))
     heads = array((lay.n_head, width), jnp.bfloat16)
-    late_lines = array((lay.n_late, LANES))
+    late_lines, first_lines = array((lay.n_late, LANES)), array((lay.n_first, LANES))
+    late_row = array((1, lay.n_late))
     late_side, first_side = scratch((lay.n_late, LANES)), scratch((lay.n_first, LANES))
-    sums, first_lane, heads_i = pair_call(
-        inner_kernel, lay, (mine, early), (row, row, heads), (first_side, bias, first_side)
-    )
-    specs = vmem_specs(2) + (pl.BlockSpec(memory_space=pltpu.SMEM),) + vmem_specs(3)
-    sums, first_other, unfit, late_sub, late_sub_j, lane = pair_call(
+    sums, first_lane, lab_sub, heads_i = pair_call(
+        inner_kernel, lay, (mine, early), (row, row, first_lines, heads), (bias, first_side)
+    )
+    specs = vmem_specs(2) + (pl.BlockSpec(memory_space=pltpu.SMEM),) + vmem_specs(4)
+    sums, first_other, unfit, late_sub, late_sub_j, lane, lane_j = pair_call(
         cross_kernel,
         lay,
         (mine, other, early, early_j, heads_i, sums, first_lane),
-        (row, row, array((1, 1), jnp.int32), late_lines, late_lines, long_row),
+        (row, row, array((1, 1), jnp.int32), late_lines, late_lines, long_row, late_row),
         (first_side, bias, first_side, pltpu.VMEM(heads.shape, heads.dtype)),
         specs,
     )
@@ -798,17 +807,20 @@
     (late_sums,) = pair_call(
         inner_late_kernel,
         lay,
-        (early, late, heads_i, late_sub, lane),
+        (early, late, heads_i, lab_sub, late_sub, lane),
         (long_row,),
-        (late_side,),
+        (first_side,),
         pairs=lay.n_late * lay.n_all,
     )
     (results,) = pair_call(
         cross_late_kernel,
         lay,
-        (early, late, late_j, heads_i, late_sub_j, lane, first_lane, sums, first_other, late_sums),
+        (
+            *(early, late, late_j, heads_i, lab_sub, late_sub_j, lane, lane_j),
+            *(first_lane, sums, first_other, late_sums),
+        ),
         (array((2 * n_owner, 1, capacity)),),
-        (scratch(long_row.shape), late_side),
+        (scratch(long_row.shape), scratch(late_row.shape), first_side, late_side),
     )
     returned = lax.all_to_all(
         results, ("cl", "grp"), split_axis=0, concat_axis=0, tiled=True

time: 84.9 us -> 81.9 us (0.965)
  starting transfers between devices: 24.9 us -> 21.8 us
    all_to_all x1, starting transfers between devices: 9.75 us -> 6.65 us  [body(): lax.all_to_all(results, ('cl', 'grp'), split_axis=0, concat_axis=0, tiled...]
where the time goes in v25:
time: 81.9 us; the launch traced here: 81.6 us
  waiting for transfers between devices  43.3 us (53%)
  starting transfers between devices  21.8 us (27%)
  Pallas kernels  15 us (18%)
  between operations  0.82 us (1%)
    ppermute x6, waiting for transfers between devices, hop(): return lax.ppermute(x, 'cl', pairs)  27.8 us
    pallas_call x4, Pallas kernels, pair_call(): pl.pallas_call(functools.partial(kernel, lay), out_shape=out_shape, in_sp...  9.62 us
    all_to_all x1, waiting for transfers between devices, body(): lax.all_to_all(packed.reshape(n_owner, main, width), 'cl', split_axis=0,...  7.44 us
    ppermute x6, starting transfers between devices, hop(): return lax.ppermute(x, 'cl', pairs)  7.3 us
    all_to_all x1, starting transfers between devices, body(): lax.all_to_all(packed.reshape(n_owner, main, width), 'cl', split_axis=0,...  7.29 us
    all_to_all x1, starting transfers between devices, body(): lax.all_to_all(results, ('cl', 'grp'), split_axis=0, concat_axis=0, tiled...  6.65 us
    all_to_all x1, waiting for transfers between devices, body(): lax.all_to_all(results, ('cl', 'grp'), split_axis=0, concat_axis=0, tiled...  5.85 us
    pallas_call x1, Pallas kernels, place_rows(): pl.pallas_call(functools.partial(place_kernel, lay), out_shape=(jax.Shape...  5.23 us
  transfers between devices with their start and end apart: 11, of which 4 were waited for; matrix products, arithmetic and copies ran while one was open for 0% of the time, Pallas kernels for 11%

profile of v25, /device:TPU:0, one launch (start us, length us, event | category | flops | bytes accessed | tf_op | source)
XLA Modules:
  0.0 81.6 jit_solution(11217938422503287988)
XLA Ops:
  0.0 5.2 %shard_map.39 = (bf16[1152,768]{1,0:T(8,128)(2,1)}, bf16[128,768]{1,0:T(8,128)(2,1)S(1)}, s32[8,128]{1,0:T(8,128)S(1)}) custom-call(bf16[1024,768]{1,0:T(8,128)(2,1)} %x_hbm.1, s32[8,128]{1,0:T(8,128)} %bitcast.23, s32[1,64]{1,0:T(1,128)} %bitcast.27), custom_call_target="tpu_custom_call" | custom-call | tf_op jit(solution)/shard_map/pallas_call | solution.py:311
  5.2 7.3 %all-to-all-start.2 = ((bf16[8,144,768]{2,1,0:T(8,128)(2,1)}), bf16[8,144,768]{2,1,0:T(8,128)(2,1)S(1)}, u32[]{:S(2)}, u32[]{:S(2)}) async-start(bf16[8,144,768]{2,1,0:T(8,128)(2,1)} %bitcast.12), calls=%async_computation.2 | async-start | bytes 3538944 | tf_op jit(solution)/shard_map/all_to_all | solution.py:774
  12.5 0.7 collective-permute-start.4
  13.2 3.9 %collective-permute-start.1 = (bf16[128,768]{1,0:T(8,128)(2,1)S(1)}, bf16[128,768]{1,0:T(8,128)(2,1)S(1)}, u32[]{:S(2)}, u32[]{:S(2)}) collective-permute-start(bf16[128,768]{1,0:T(8,128)(2,1)S(1)} %get-tuple-element.41.refs_2_.refs_0_), channel_id=1, source_target_pairs={{0,4},{1,5},{16,20},{17,21}} | collective-permute-start | bytes 589832 | tf_op jit(solution)/shard_map/ppermute | solution.py:766
  17.1 0.7 collective-permute-start.2
  17.8 0.7 collective-permute-start.3
  18.5 0.0 collective-permute-done.4.refs_1_
  18.6 27.7 %collective-permute-done.1.refs_0_ = bf16[128,768]{1,0:T(8,128)(2,1)S(1)} collective-permute-done((bf16[128,768]{1,0:T(8,128)(2,1)S(1)}, bf16[128,768]{1,0:T(8,128)(2,1)S(1)}, u32[]{:S(2)}, u32[]{:S(2)}) %collective-permute-start.1) | collective-permute-done | bytes 196640 | tf_op jit(solution)/shard_map/ppermute | solution.py:766
  46.3 0.0 collective-permute-done.2.refs_1_
  46.3 0.0 collective-permute-done.3.refs_3_
  46.3 7.4 %all-to-all-done.2 = bf16[8,144,768]{2,1,0:T(8,128)(2,1)S(1)} async-done(((bf16[8,144,768]{2,1,0:T(8,128)(2,1)}), bf16[8,144,768]{2,1,0:T(8,128)(2,1)S(1)}, u32[]{:S(2)}, u32[]{:S(2)}) %all-to-all-start.2) | async-done | bytes 1769504 | tf_op jit(solution)/shard_map/all_to_all | solution.py:774
  53.8 0.0 collective-permute-start.5
  53.8 0.5 collective-permute-start.6
  54.3 0.7 collective-permute-start.7
  54.9 0.7 collective-permute-start.8
  55.6 4.0 %shard_map.43 = (f32[1,1536]{1,0:T(1,128)S(1)}, f32[1,1536]{1,0:T(1,128)S(1)}, f32[1536,128]{1,0:T(8,128)S(1)}, bf16[1024,768]{1,0:T(8,128)(2,1)S(1)}) custom-call(bf16[1152,768]{1,0:T(8,128)(2,1)S(1)} %shard_map.42.mine, bf16[512,768]{1,0:T(8,128)(2,1)S(1)} %shard_map.40.refs_1_.early), custom_call_target="tpu_custom_call" | custom-call | bytes 1 | tf_op jit(solution)/shard_map/pallas_call | solution.py:699
  59.7 0.0 collective-permute-done.6.early_j
  59.7 0.0 collective-permute-done.5.other
  59.7 4.9 %shard_map.44 = (f32[1,1536]{1,0:T(1,128)S(1)}, f32[1,1536]{1,0:T(1,128)S(1)}, s32[1,1]{1,0:T(1,128)}, f32[512,128]{1,0:T(8,128)S(1)}, f32[512,128]{1,0:T(8,128)...) custom-call(bf16[1152,768]{1,0:T(8,128)(2,1)S(1)} %shard_map.42.mine, ...), custom_call_target="tpu_custom_call" | custom-call | bytes 1 | tf_op jit(solution)/shard_map/pallas_call | solution.py:699
  64.6 0.0 collective-permute-done.7.refs_0_
  64.6 0.0 collective-permute-done.8.refs_1_
  64.6 0.1 collective-permute-start.9
  64.7 2.2 %collective-permute-done.9.late_j = bf16[512,768]{1,0:T(8,128)(2,1)S(1)} collective-permute-done((bf16[512,768]{1,0:T(8,128)(2,1)S(1)}, bf16[512,768]{1,0:T(8,128)(2,1)S(1)}, u32[]{:S(2)}, u32[]{:S(2)}) %collective-permute-start.9) | collective-permute-done | bytes 786464 | tf_op jit(solution)/shard_map/ppermute | solution.py:769
  67.0 0.0 copy-start.1
  67.0 0.0 copy-start.3
  67.0 0.0 copy-start.5
  67.0 0.7 shard_map.47
  67.7 6.6 %all-to-all-start.3 = ((f32[16,1,256]{2,1,0:T(1,128)}), f32[16,1,256]{2,1,0:T(1,128)S(1)}, u32[]{:S(2)}, u32[]{:S(2)}) async-start(f32[16,1,256]{2,1,0:T(1,128)} %shard_map.47), calls=%async_computation.3 | async-start | bytes 32768 | tf_op jit(solution)/shard_map/all_to_all | solution.py:825
  75.0 5.8 %all-to-all-done.3 = f32[16,1,256]{2,1,0:T(1,128)S(1)} async-done(((f32[16,1,256]{2,1,0:T(1,128)}), f32[16,1,256]{2,1,0:T(1,128)S(1)}, u32[]{:S(2)}, u32[]{:S(2)}) %all-to-all-start.3) | async-done | bytes 16416 | tf_op jit(solution)/shard_map/all_to_all | solution.py:825
  80.8 0.0 copy-done.1
  80.8 0.0 copy-done.3
  80.8 0.0 copy-done.5
  80.8 0.1 conditional.1
  80.9 0.1 branch_1_fun.1
  81.0 0.0 copy-start.4
  81.0 0.6 copy-done.4
  (5 shorter events, 0.1 us)
Async XLA Ops:
  5.2 48.5 %all-to-all-start.2 = ((bf16[8,144,768]{2,1,0:T(8,128)(2,1)}), bf16[8,144,768]{2,1,0:T(8,128)(2,1)S(1)}, u32[]{:S(2)}, u32[]{:S(2)}) async-start(bf16[8,144,768]{2,1,0:T(8,128)(2,1)} %bitcast.12), calls=%async_computation.2 | async-start | bytes 3538944 | tf_op jit(solution)/shard_map/all_to_all | solution.py:774
  12.5 6.0 %collective-permute-start.4 = (bf16[128,768]{1,0:T(8,128)(2,1)S(1)}, bf16[128,768]{1,0:T(8,128)(2,1)S(1)}, u32[]{:S(2)}, u32[]{:S(2)}) collective-permute-start(bf16[128,768]{1,0:T(8,128)(2,1)S(1)} %get-tuple-element.41.refs_2_.refs_0_), channel_id=1, source_target_pairs={{12,8},{14,10},{13,9},{15,11},{28,24},{30,26},{29,25},{31,27}} | collective-permute-start | bytes 589832 | tf_op jit(solution)/shard_map/ppermute | solution.py:766
  13.2 33.1 %collective-permute-start.1 = (bf16[128,768]{1,0:T(8,128)(2,1)S(1)}, bf16[128,768]{1,0:T(8,128)(2,1)S(1)}, u32[]{:S(2)}, u32[]{:S(2)}) collective-permute-start(bf16[128,768]{1,0:T(8,128)(2,1)S(1)} %get-tuple-element.41.refs_2_.refs_0_), channel_id=1, source_target_pairs={{0,4},{1,5},{16,20},{17,21}} | collective-permute-start | bytes 589832 | tf_op jit(solution)/shard_map/ppermute | solution.py:766
  17.1 29.2 %collective-permute-start.2 = (bf16[128,768]{1,0:T(8,128)(2,1)S(1)}, bf16[128,768]{1,0:T(8,128)(2,1)S(1)}, u32[]{:S(2)}, u32[]{:S(2)}) collective-permute-start(bf16[128,768]{1,0:T(8,128)(2,1)S(1)} %get-tuple-element.41.refs_2_.refs_0_), channel_id=1, source_target_pairs={{2,4},{3,5},{18,20},{19,21}} | collective-permute-start | bytes 589832 | tf_op jit(solution)/shard_map/ppermute | solution.py:766
  17.8 28.5 %collective-permute-start.3 = (bf16[128,768]{1,0:T(8,128)(2,1)S(1)}, bf16[128,768]{1,0:T(8,128)(2,1)S(1)}, u32[]{:S(2)}, u32[]{:S(2)}) collective-permute-start(bf16[128,768]{1,0:T(8,128)(2,1)S(1)} %get-tuple-element.41.refs_2_.refs_0_), channel_id=1, source_target_pairs={{6,4},{7,5},{22,20},{23,21}} | collective-permute-start | bytes 589832 | tf_op jit(solution)/shard_map/ppermute | solution.py:766
  53.8 5.9 %collective-permute-start.5 = (bf16[1152,768]{1,0:T(8,128)(2,1)S(1)}, bf16[1152,768]{1,0:T(8,128)(2,1)S(1)}, u32[]{:S(2)}, u32[]{:S(2)}) collective-permute-start(bf16[1152,768]{1,0:T(8,128)(2,1)S(1)} %shard_map.42.mine), channel_id=1, source_target_pairs={{0,1},{1,0},{2,3},{3,2},{4,5},{5,4},{6,7},{7,6},{8,9},{9,8},{10,11... | collective-permute-start | bytes 5308424 | tf_op jit(solution)/shard_map/ppermute | solution.py:769
  53.8 5.9 %collective-permute-start.6 = (bf16[512,768]{1,0:T(8,128)(2,1)S(1)}, bf16[512,768]{1,0:T(8,128)(2,1)S(1)}, u32[]{:S(2)}, u32[]{:S(2)}) collective-permute-start(bf16[512,768]{1,0:T(8,128)(2,1)S(1)} %shard_map.40.refs_1_.early), channel_id=1, source_target_pairs={{0,1},{1,0},{2,3},{3,2},{4,5},{5,4},{6,7},{7,6},{8,9},{9,8},{10,11... | collective-permute-start | bytes 2359304 | tf_op jit(solution)/shard_map/ppermute | solution.py:769
  54.3 10.3 %collective-permute-start.7 = (bf16[256,768]{1,0:T(8,128)(2,1)S(1)}, bf16[256,768]{1,0:T(8,128)(2,1)S(1)}, u32[]{:S(2)}, u32[]{:S(2)}) collective-permute-start(bf16[256,768]{1,0:T(8,128)(2,1)S(1)} %shard_map.41.refs_2_), channel_id=1, source_target_pairs={{10,4},{11,5},{26,20},{27,21}} | collective-permute-start | bytes 1179656 | tf_op jit(solution)/shard_map/ppermute | solution.py:766
  54.9 9.7 %collective-permute-start.8 = (bf16[256,768]{1,0:T(8,128)(2,1)S(1)}, bf16[256,768]{1,0:T(8,128)(2,1)S(1)}, u32[]{:S(2)}, u32[]{:S(2)}) collective-permute-start(bf16[256,768]{1,0:T(8,128)(2,1)S(1)} %shard_map.41.refs_2_), channel_id=1, source_target_pairs={{8,4},{9,5},{24,20},{25,21}} | collective-permute-start | bytes 1179656 | tf_op jit(solution)/shard_map/ppermute | solution.py:766
  64.6 2.4 %collective-permute-start.9 = (bf16[512,768]{1,0:T(8,128)(2,1)S(1)}, bf16[512,768]{1,0:T(8,128)(2,1)S(1)}, u32[]{:S(2)}, u32[]{:S(2)}) collective-permute-start(bf16[512,768]{1,0:T(8,128)(2,1)S(1)} %shard_map.45.late), channel_id=1, source_target_pairs={{0,1},{1,0},{2,3},{3,2},{4,5},{5,4},{6,7},{7,6},{8,9},{9,8},{10,11... | collective-permute-start | bytes 2359304 | tf_op jit(solution)/shard_map/ppermute | solution.py:769
  67.0 13.8 %copy-start.1 = (bf16[1024,768]{1,0:T(8,128)(2,1)S(1)}, bf16[1024,768]{1,0:T(8,128)(2,1)}, u32[]{:S(2)}) copy-start(bf16[1024,768]{1,0:T(8,128)(2,1)} %x_hbm.1) | copy-start | bytes 4718596
  67.0 13.8 %copy-start.3 = (s32[1024]{0:T(1024)S(1)}, s32[1024]{0:T(1024)}, u32[]{:S(2)}) copy-start(s32[1024]{0:T(1024)} %param.6) | copy-start | bytes 12292
  67.0 13.8 %copy-start.5 = (s32[64]{0:T(128)S(1)}, s32[64]{0:T(128)}, u32[]{:S(2)}) copy-start(s32[64]{0:T(128)} %param.7) | copy-start | bytes 772
  67.7 13.2 %all-to-all-start.3 = ((f32[16,1,256]{2,1,0:T(1,128)}), f32[16,1,256]{2,1,0:T(1,128)S(1)}, u32[]{:S(2)}, u32[]{:S(2)}) async-start(f32[16,1,256]{2,1,0:T(1,128)} %shard_map.47), calls=%async_computation.3 | async-start | bytes 32768 | tf_op jit(solution)/shard_map/all_to_all | solution.py:825
  81.0 0.6 copy-start.4

commit v26 on v25

--- a/solution.py
+++ b/solution.py
@@ -775,7 +775,7 @@
         packed.reshape(n_owner, main, width), "cl", split_axis=0, concat_axis=0, tiled=True
     ).reshape(n_owner * main, width)
     mine = after(mine, early, both)
-    other, early_j = swap(mine), swap(early)
+    other = swap(mine)
     late = [hop(both, [(s, home)]) for s in (5, 4)]
 
     def array(shape, dtype=jnp.float32):
@@ -793,6 +793,7 @@
     sums, first_lane, lab_sub, heads_i = pair_call(
         inner_kernel, lay, (mine, early), (row, row, first_lines, heads), (bias, first_side)
     )
+    early_j = swap(lay_out([early], home, (sums,)))
     specs = vmem_specs(2) + (pl.BlockSpec(memory_space=pltpu.SMEM),) + vmem_specs(4)
     sums, first_other, unfit, late_sub, late_sub_j, lane, lane_j = pair_call(
         cross_kernel,

time: 81.9 us -> 85 us (1.038)
  starting transfers between devices: 21.8 us -> 24.8 us
    all_to_all x1, starting transfers between devices: 6.65 us -> 9.16 us  [body(): lax.all_to_all(results, ('cl', 'grp'), split_axis=0, concat_axis=0, tiled...]
  transfers between devices with their start and end apart: 11 -> 11, of which waited for: 4 -> 5; matrix products, arithmetic and copies ran while one was open for 0% -> 0% of each run, Pallas kernels for 11% -> 11%
where the time goes in v26:
time: 85 us; the launch traced here: 84.7 us
  waiting for transfers between devices  43.5 us (51%)
  starting transfers between devices  24.8 us (29%)
  Pallas kernels  15 us (18%)
    ppermute x6, waiting for transfers between devices, hop(): return lax.ppermute(x, 'cl', pairs)  27.8 us
    pallas_call x4, Pallas kernels, pair_call(): pl.pallas_call(functools.partial(kernel, lay), out_shape=out_shape, in_sp...  9.59 us
    all_to_all x1, starting transfers between devices, body(): lax.all_to_all(results, ('cl', 'grp'), split_axis=0, concat_axis=0, tiled...  9.16 us
    all_to_all x1, waiting for transfers between devices, body(): lax.all_to_all(packed.reshape(n_owner, main, width), 'cl', split_axis=0,...  7.44 us
    ppermute x6, starting transfers between devices, hop(): return lax.ppermute(x, 'cl', pairs)  7.3 us
    all_to_all x1, starting transfers between devices, body(): lax.all_to_all(packed.reshape(n_owner, main, width), 'cl', split_axis=0,...  7.29 us
    all_to_all x1, waiting for transfers between devices, body(): lax.all_to_all(results, ('cl', 'grp'), split_axis=0, concat_axis=0, tiled...  5.85 us
    pallas_call x1, Pallas kernels, place_rows(): pl.pallas_call(functools.partial(place_kernel, lay), out_shape=(jax.Shape...  5.23 us
  transfers between devices with their start and end apart: 11, of which 5 were waited for; matrix products, arithmetic and copies ran while one was open for 0% of the time, Pallas kernels for 11%

profile of v26, /device:TPU:0, one launch (start us, length us, event | category | flops | bytes accessed | tf_op | source)
XLA Modules:
  0.0 84.7 jit_solution(16824424238364976982)
XLA Ops:
  0.0 5.2 %shard_map.39 = (bf16[1152,768]{1,0:T(8,128)(2,1)}, bf16[128,768]{1,0:T(8,128)(2,1)S(1)}, s32[8,128]{1,0:T(8,128)S(1)}) custom-call(bf16[1024,768]{1,0:T(8,128)(2,1)} %x_hbm.1, s32[8,128]{1,0:T(8,128)} %bitcast.23, s32[1,64]{1,0:T(1,128)} %bitcast.27), custom_call_target="tpu_custom_call" | custom-call | tf_op jit(solution)/shard_map/pallas_call | solution.py:311
  5.2 7.3 %all-to-all-start.2 = ((bf16[8,144,768]{2,1,0:T(8,128)(2,1)}), bf16[8,144,768]{2,1,0:T(8,128)(2,1)S(1)}, u32[]{:S(2)}, u32[]{:S(2)}) async-start(bf16[8,144,768]{2,1,0:T(8,128)(2,1)} %bitcast.12), calls=%async_computation.2 | async-start | bytes 3538944 | tf_op jit(solution)/shard_map/all_to_all | solution.py:774
  12.5 0.7 collective-permute-start.4
  13.2 3.9 %collective-permute-start.1 = (bf16[128,768]{1,0:T(8,128)(2,1)S(1)}, bf16[128,768]{1,0:T(8,128)(2,1)S(1)}, u32[]{:S(2)}, u32[]{:S(2)}) collective-permute-start(bf16[128,768]{1,0:T(8,128)(2,1)S(1)} %get-tuple-element.41.refs_2_.refs_0_), channel_id=1, source_target_pairs={{0,4},{1,5},{16,20},{17,21}} | collective-permute-start | bytes 589832 | tf_op jit(solution)/shard_map/ppermute | solution.py:766
  17.1 0.7 collective-permute-start.2
  17.8 0.7 collective-permute-start.3
  18.5 0.0 collective-permute-done.4.refs_1_
  18.6 27.7 %collective-permute-done.1.refs_0_ = bf16[128,768]{1,0:T(8,128)(2,1)S(1)} collective-permute-done((bf16[128,768]{1,0:T(8,128)(2,1)S(1)}, bf16[128,768]{1,0:T(8,128)(2,1)S(1)}, u32[]{:S(2)}, u32[]{:S(2)}) %collective-permute-start.1) | collective-permute-done | bytes 196640 | tf_op jit(solution)/shard_map/ppermute | solution.py:766
  46.3 0.0 collective-permute-done.2.refs_1_
  46.3 0.0 collective-permute-done.3.refs_3_
  46.3 7.4 %all-to-all-done.2 = bf16[8,144,768]{2,1,0:T(8,128)(2,1)S(1)} async-done(((bf16[8,144,768]{2,1,0:T(8,128)(2,1)}), bf16[8,144,768]{2,1,0:T(8,128)(2,1)S(1)}, u32[]{:S(2)}, u32[]{:S(2)}) %all-to-all-start.2) | async-done | bytes 1769504 | tf_op jit(solution)/shard_map/all_to_all | solution.py:774
  53.8 0.0 collective-permute-start.5
  53.8 4.0 %shard_map.43 = (f32[1,1536]{1,0:T(1,128)S(1)}, f32[1,1536]{1,0:T(1,128)S(1)}, f32[1536,128]{1,0:T(8,128)S(1)}, bf16[1024,768]{1,0:T(8,128)(2,1)S(1)}) custom-call(bf16[1152,768]{1,0:T(8,128)(2,1)S(1)} %shard_map.42.mine, bf16[512,768]{1,0:T(8,128)(2,1)S(1)} %shard_map.40.refs_1_.early.refs_0_), custom_call_target="tpu_custom_call" | custom-call | bytes 1 | tf_op jit(solution)/shard_map/pallas_call | solution.py:699
  57.8 0.6 collective-permute-start.6
  58.4 0.7 collective-permute-start.7
  59.1 0.7 collective-permute-start.8
  59.8 0.5 collective-permute-done.6.early_j
  60.3 0.0 collective-permute-done.5.other
  60.3 4.9 %shard_map.45 = (f32[1,1536]{1,0:T(1,128)S(1)}, f32[1,1536]{1,0:T(1,128)S(1)}, s32[1,1]{1,0:T(1,128)}, f32[512,128]{1,0:T(8,128)S(1)}, f32[512,128]{1,0:T(8,128)...) custom-call(bf16[1152,768]{1,0:T(8,128)(2,1)S(1)} %shard_map.42.mine, ...), custom_call_target="tpu_custom_call" | custom-call | bytes 1 | tf_op jit(solution)/shard_map/pallas_call | solution.py:699
  65.2 0.0 collective-permute-done.7.refs_0_
  65.2 0.0 collective-permute-done.8.refs_1_
  65.2 0.4 collective-permute-start.9
  65.7 1.9 %collective-permute-done.9.late_j = bf16[512,768]{1,0:T(8,128)(2,1)S(1)} collective-permute-done((bf16[512,768]{1,0:T(8,128)(2,1)S(1)}, bf16[512,768]{1,0:T(8,128)(2,1)S(1)}, u32[]{:S(2)}, u32[]{:S(2)}) %collective-permute-start.9) | collective-permute-done | bytes 786464 | tf_op jit(solution)/shard_map/ppermute | solution.py:769
  67.6 0.0 copy-start.1
  67.6 0.0 copy-start.3
  67.6 0.0 copy-start.5
  67.6 0.7 shard_map.48
  68.3 9.2 %all-to-all-start.3 = ((f32[16,1,256]{2,1,0:T(1,128)}), f32[16,1,256]{2,1,0:T(1,128)S(1)}, u32[]{:S(2)}, u32[]{:S(2)}) async-start(f32[16,1,256]{2,1,0:T(1,128)} %shard_map.48), calls=%async_computation.3 | async-start | bytes 32768 | tf_op jit(solution)/shard_map/all_to_all | solution.py:826
  78.1 5.8 %all-to-all-done.3 = f32[16,1,256]{2,1,0:T(1,128)S(1)} async-done(((f32[16,1,256]{2,1,0:T(1,128)}), f32[16,1,256]{2,1,0:T(1,128)S(1)}, u32[]{:S(2)}, u32[]{:S(2)}) %all-to-all-start.3) | async-done | bytes 16416 | tf_op jit(solution)/shard_map/all_to_all | solution.py:826
  83.9 0.0 copy-done.1
  83.9 0.0 copy-done.3
  83.9 0.0 copy-done.5
  83.9 0.1 conditional.1
  84.0 0.1 branch_1_fun.1
  84.1 0.0 copy-start.4
  84.1 0.6 copy-done.4
  (6 shorter events, 0.1 us)
Async XLA Ops:
  5.2 48.5 %all-to-all-start.2 = ((bf16[8,144,768]{2,1,0:T(8,128)(2,1)}), bf16[8,144,768]{2,1,0:T(8,128)(2,1)S(1)}, u32[]{:S(2)}, u32[]{:S(2)}) async-start(bf16[8,144,768]{2,1,0:T(8,128)(2,1)} %bitcast.12), calls=%async_computation.2 | async-start | bytes 3538944 | tf_op jit(solution)/shard_map/all_to_all | solution.py:774
  12.5 6.0 %collective-permute-start.4 = (bf16[128,768]{1,0:T(8,128)(2,1)S(1)}, bf16[128,768]{1,0:T(8,128)(2,1)S(1)}, u32[]{:S(2)}, u32[]{:S(2)}) collective-permute-start(bf16[128,768]{1,0:T(8,128)(2,1)S(1)} %get-tuple-element.41.refs_2_.refs_0_), channel_id=1, source_target_pairs={{12,8},{14,10},{13,9},{15,11},{28,24},{30,26},{29,25},{31,27}} | collective-permute-start | bytes 589832 | tf_op jit(solution)/shard_map/ppermute | solution.py:766
  13.2 33.1 %collective-permute-start.1 = (bf16[128,768]{1,0:T(8,128)(2,1)S(1)}, bf16[128,768]{1,0:T(8,128)(2,1)S(1)}, u32[]{:S(2)}, u32[]{:S(2)}) collective-permute-start(bf16[128,768]{1,0:T(8,128)(2,1)S(1)} %get-tuple-element.41.refs_2_.refs_0_), channel_id=1, source_target_pairs={{0,4},{1,5},{16,20},{17,21}} | collective-permute-start | bytes 589832 | tf_op jit(solution)/shard_map/ppermute | solution.py:766
  17.1 29.2 %collective-permute-start.2 = (bf16[128,768]{1,0:T(8,128)(2,1)S(1)}, bf16[128,768]{1,0:T(8,128)(2,1)S(1)}, u32[]{:S(2)}, u32[]{:S(2)}) collective-permute-start(bf16[128,768]{1,0:T(8,128)(2,1)S(1)} %get-tuple-element.41.refs_2_.refs_0_), channel_id=1, source_target_pairs={{2,4},{3,5},{18,20},{19,21}} | collective-permute-start | bytes 589832 | tf_op jit(solution)/shard_map/ppermute | solution.py:766
  17.8 28.5 %collective-permute-start.3 = (bf16[128,768]{1,0:T(8,128)(2,1)S(1)}, bf16[128,768]{1,0:T(8,128)(2,1)S(1)}, u32[]{:S(2)}, u32[]{:S(2)}) collective-permute-start(bf16[128,768]{1,0:T(8,128)(2,1)S(1)} %get-tuple-element.41.refs_2_.refs_0_), channel_id=1, source_target_pairs={{6,4},{7,5},{22,20},{23,21}} | collective-permute-start | bytes 589832 | tf_op jit(solution)/shard_map/ppermute | solution.py:766
  53.8 6.5 %collective-permute-start.5 = (bf16[1152,768]{1,0:T(8,128)(2,1)S(1)}, bf16[1152,768]{1,0:T(8,128)(2,1)S(1)}, u32[]{:S(2)}, u32[]{:S(2)}) collective-permute-start(bf16[1152,768]{1,0:T(8,128)(2,1)S(1)} %shard_map.42.mine), channel_id=1, source_target_pairs={{0,1},{1,0},{2,3},{3,2},{4,5},{5,4},{6,7},{7,6},{8,9},{9,8},{10,11... | collective-permute-start | bytes 5308424 | tf_op jit(solution)/shard_map/ppermute | solution.py:769
  57.8 2.5 %collective-permute-start.6 = (bf16[512,768]{1,0:T(8,128)(2,1)S(1)}, bf16[512,768]{1,0:T(8,128)(2,1)S(1)}, u32[]{:S(2)}, u32[]{:S(2)}) collective-permute-start(bf16[512,768]{1,0:T(8,128)(2,1)S(1)} %shard_map.44), channel_id=1, source_target_pairs={{0,1},{1,0},{2,3},{3,2},{4,5},{5,4},{6,7},{7,6},{8,9},{9,8},{10,11... | collective-permute-start | bytes 2359304 | tf_op jit(solution)/shard_map/ppermute | solution.py:769
  58.4 6.8 %collective-permute-start.7 = (bf16[256,768]{1,0:T(8,128)(2,1)S(1)}, bf16[256,768]{1,0:T(8,128)(2,1)S(1)}, u32[]{:S(2)}, u32[]{:S(2)}) collective-permute-start(bf16[256,768]{1,0:T(8,128)(2,1)S(1)} %shard_map.41.refs_2_), channel_id=1, source_target_pairs={{10,4},{11,5},{26,20},{27,21}} | collective-permute-start | bytes 1179656 | tf_op jit(solution)/shard_map/ppermute | solution.py:766
  59.1 6.1 %collective-permute-start.8 = (bf16[256,768]{1,0:T(8,128)(2,1)S(1)}, bf16[256,768]{1,0:T(8,128)(2,1)S(1)}, u32[]{:S(2)}, u32[]{:S(2)}) collective-permute-start(bf16[256,768]{1,0:T(8,128)(2,1)S(1)} %shard_map.41.refs_2_), channel_id=1, source_target_pairs={{8,4},{9,5},{24,20},{25,21}} | collective-permute-start | bytes 1179656 | tf_op jit(solution)/shard_map/ppermute | solution.py:766
  65.2 2.4 %collective-permute-start.9 = (bf16[512,768]{1,0:T(8,128)(2,1)S(1)}, bf16[512,768]{1,0:T(8,128)(2,1)S(1)}, u32[]{:S(2)}, u32[]{:S(2)}) collective-permute-start(bf16[512,768]{1,0:T(8,128)(2,1)S(1)} %shard_map.46.late), channel_id=1, source_target_pairs={{0,1},{1,0},{2,3},{3,2},{4,5},{5,4},{6,7},{7,6},{8,9},{9,8},{10,11... | collective-permute-start | bytes 2359304 | tf_op jit(solution)/shard_map/ppermute | solution.py:769
  67.6 16.3 %copy-start.1 = (bf16[1024,768]{1,0:T(8,128)(2,1)S(1)}, bf16[1024,768]{1,0:T(8,128)(2,1)}, u32[]{:S(2)}) copy-start(bf16[1024,768]{1,0:T(8,128)(2,1)} %x_hbm.1) | copy-start | bytes 4718596
  67.6 16.3 %copy-start.3 = (s32[1024]{0:T(1024)S(1)}, s32[1024]{0:T(1024)}, u32[]{:S(2)}) copy-start(s32[1024]{0:T(1024)} %param.6) | copy-start | bytes 12292
  67.6 16.4 %copy-start.5 = (s32[64]{0:T(128)S(1)}, s32[64]{0:T(128)}, u32[]{:S(2)}) copy-start(s32[64]{0:T(128)} %param.7) | copy-start | bytes 772
  68.3 15.7 %all-to-all-start.3 = ((f32[16,1,256]{2,1,0:T(1,128)}), f32[16,1,256]{2,1,0:T(1,128)S(1)}, u32[]{:S(2)}, u32[]{:S(2)}) async-start(f32[16,1,256]{2,1,0:T(1,128)} %shard_map.48), calls=%async_computation.3 | async-start | bytes 32768 | tf_op jit(solution)/shard_map/all_to_all | solution.py:826
  84.1 0.6 copy-start.4

commit v27 on v25

--- a/solution.py
+++ b/solution.py
@@ -219,7 +219,7 @@
 
 
 def place_kernel(lay, x_hbm, lab_hbm, map_hbm, *refs):
-    main_hbm, tail_ref, pos_ref, x_ref, lab_ref, map_ref, unit, main_ref, sems = refs
+    main_hbm, unit, tail_slot_ref, pos_ref, x_ref, lab_ref, map_ref, main_ref, sems = refs
     n_owner, capacity, main, home = lay.n_owner, lay.capacity, lay.main, lay.home
     copies = [
         pltpu.make_async_copy(src, dst, sems.at[i])
@@ -268,23 +268,18 @@
     )
     fits = rank < jnp.where(place == home, lay.head, main - 1)
     slot = jnp.where(fits, place * main + rank, -1)
-    tail_slot = jnp.where(place == home, rank - lay.head, -1)
+    tail_slot_ref[...] = jnp.where(place == home, rank - lay.head, -1)
     copies[0].wait()
     x = x_ref[...].astype(jnp.float32)
     squares = jnp.sum(x * x, axis=1, keepdims=True)
     unit[...] = (x * lax.rsqrt(squares + epsilon)).astype(jnp.bfloat16)
-
-    def chosen_rows(slot, start, count):
-        here = lax.broadcasted_iota(jnp.int32, (count, rows), 0) + start
-        chosen = jnp.where(here == slot, 1.0, 0.0).astype(jnp.bfloat16)
-        return jnp.dot(chosen, unit[...], preferred_element_type=jnp.float32)
 
     count = 2 * main
     down = lax.broadcasted_iota(jnp.int32, (count, LANES), 0)
     is_info = lax.rem(down, main) == main - 1
     writes = []
     for i, start in enumerate(range(0, lay.n_main, count)):
-        packed = chosen_rows(slot, start, count)
+        packed = chosen_rows(unit, slot, start, count)
         place = slice(start, start + count)
         main_ref[place, LANES:] = packed[:, LANES:].astype(jnp.bfloat16)
         main_ref[place, :LANES] = jnp.where(is_info, info, packed[:, :LANES]).astype(jnp.bfloat16)
@@ -294,9 +289,28 @@
             )
         )
         writes[-1].start()
-    tail_ref[...] = chosen_rows(tail_slot, 0, lay.rest).astype(jnp.bfloat16)
     for write in writes:
         write.wait()
+
+
+def chosen_rows(unit, slot, start, count):
+    here = lax.broadcasted_iota(jnp.int32, (count, unit.shape[0]), 0) + start
+    chosen = jnp.where(here == slot, 1.0, 0.0).astype(jnp.bfloat16)
+    return jnp.dot(chosen, unit[...], preferred_element_type=jnp.float32)
+
+
+def tail_kernel(unit, slot_ref, out_ref):
+    out_ref[...] = chosen_rows(unit, slot_ref[...], 0, out_ref.shape[0]).astype(jnp.bfloat16)
+
+
+def tail_rows(unit, slot, lay):
+    return pl.pallas_call(
+        tail_kernel,
+        out_shape=jax.ShapeDtypeStruct((lay.rest, unit.shape[1]), jnp.bfloat16),
+        in_specs=list(vmem_specs(2)),
+        out_specs=vmem_specs(1)[0],
+        compiler_params=pltpu.CompilerParams(vmem_limit_bytes=FAST_LIMIT),
+    )(unit, slot)
 
 
 def vmem_specs(count):
@@ -312,16 +326,16 @@
         functools.partial(place_kernel, lay),
         out_shape=(
             jax.ShapeDtypeStruct((lay.n_main, width), jnp.bfloat16),
-            jax.ShapeDtypeStruct((lay.rest, width), jnp.bfloat16),
+            jax.ShapeDtypeStruct((rows, width), jnp.bfloat16),
+            jax.ShapeDtypeStruct((1, rows), jnp.int32),
             jax.ShapeDtypeStruct(lab_shape, jnp.int32),
         ),
         in_specs=[anywhere] * 3,
-        out_specs=(anywhere,) + vmem_specs(2),
+        out_specs=(anywhere,) + vmem_specs(3),
         scratch_shapes=[
             pltpu.VMEM((rows, width), jnp.bfloat16),
             pltpu.VMEM(lab_shape, jnp.int32),
             pltpu.VMEM((1, n_fine), jnp.int32),
-            pltpu.VMEM((rows, width), jnp.bfloat16),
             pltpu.VMEM((lay.n_main, width), jnp.bfloat16),
             pltpu.SemaphoreType.DMA((3 + lay.n_owner // 2,)),
         ],
@@ -445,7 +459,7 @@
     return [(i * (count // parts), count // parts) for i in range(parts)]
 
 
-def stream(lanes, tiles, lab_lane, buffers, put):
+def stream(lanes, tiles, lab_lane, buffers, put, one_way=None):
     rows_i, count, at = lanes
     step = 32
     tiles = [
@@ -495,7 +509,8 @@
                         bias_j = jnp.concatenate([bias[part, :]] * repeat, axis=1)
                     shift = jnp.where(label_j == label_i, -SCALE, bias_j)
                     terms = jnp.exp2(buffer[c : c + step, :wide] * SCALE + shift)
-                    acc = acc + jnp.sum(terms.reshape(step // 8, 8, wide), axis=0)
+                    if one_way is None or back is not one_way:
+                        acc = acc + jnp.sum(terms.reshape(step // 8, 8, wide), axis=0)
                     if back is not None:
                         across = terms[:, :LANES]
                         for r in range(1, repeat):
@@ -577,8 +592,8 @@
 
 
 def cross_kernel(lay, mine, other, early, early_j, rows, sums, lab_lane, *refs):
-    total, for_other, unfit_ref, late_sub, late_sub_j, long_lane, late_lane_j = refs[:7]
-    lab_sub, bias, back, rows_j, buf_a, buf_b = refs[7:]
+    total, for_other, unfit_ref, late_sub, long_lane, late_lane_j = refs[:6]
+    lab_sub, bias, back, rows_j, late_sub_j, buf_a, buf_b = refs[6:]
     is_home = lax.axis_index("cl") == lay.home
     infos = lines_of(lay, other)
     own = lines_of(lay, mine)
@@ -651,9 +666,9 @@
         turn_sums(back, lay.n_first, sums, 0)
 
 
-def cross_late_kernel(lay, early, late, late_j, rows, lab_sub, late_sub, lab_lane, *refs):
-    late_lane, first_lane, first_sums, first_other, sums, out_ref = refs[:6]
-    total, late_other, back, late_back, buf_a, buf_b = refs[6:]
+def cross_late_kernel(lay, early, late, late_j, rows, lab_sub, late_sub, late_lane, *refs):
+    first_lane, first_sums, first_other, sums, out_ref = refs[:5]
+    total, late_other, back, late_back, buf_a, buf_b = refs[5:]
     is_home = lax.axis_index("cl") == lay.home
     grp = lax.axis_index("grp")
 
@@ -665,11 +680,11 @@
         late_back[...] = jnp.zeros(late_back.shape, jnp.float32)
         buffers = (buf_a, buf_b)
         tiles = first_tiles(lay, rows, early, lab_sub, back)
-        stream((late_j, lay.n_late, 0), tiles, late_lane, buffers, setter(late_other))
+        tiles.append((late, lay.n_late, late_sub, None, 0, 2, late_back))
+        lanes, put = (late_j, lay.n_late, 0), setter(late_other)
+        stream(lanes, tiles, late_lane, buffers, put, one_way=late_back)
         turn_sums(back, lay.n_first, total, 0)
-        put = adder(total)
-        half_blocks(late, late_j, late_sub, 0, late_back, lay.n_first, lab_lane, buffers, put)
-        turn_sums(late_back, lay.n_late, late_other, 0)
+        turn_sums(late_back, lay.n_late, total, lay.n_first)
 
         def write(line, values):
             for source in range(lay.n_owner):
@@ -760,7 +775,8 @@
         return general(embeddings, labels, owner_map)
     home = 2
     lay = Layout(n_owner, n_fine, capacity, main, home)
-    packed, extra, pos = place_rows(embeddings, labels, owner_map, lay)
+    packed, unit, tail_slot, pos = place_rows(embeddings, labels, owner_map, lay)
+    extra = tail_rows(unit, tail_slot, lay)
 
     def hop(x, pairs):
         return lax.ppermute(x, "cl", pairs)
@@ -793,13 +809,13 @@
     sums, first_lane, lab_sub, heads_i = pair_call(
         inner_kernel, lay, (mine, early), (row, row, first_lines, heads), (bias, first_side)
     )
-    specs = vmem_specs(2) + (pl.BlockSpec(memory_space=pltpu.SMEM),) + vmem_specs(4)
-    sums, first_other, unfit, late_sub, late_sub_j, lane, lane_j = pair_call(
+    specs = vmem_specs(2) + (pl.BlockSpec(memory_space=pltpu.SMEM),) + vmem_specs(3)
+    sums, first_other, unfit, late_sub, lane, lane_j = pair_call(
         cross_kernel,
         lay,
         (mine, other, early, early_j, heads_i, sums, first_lane),
-        (row, row, array((1, 1), jnp.int32), late_lines, late_lines, long_row, late_row),
-        (first_side, bias, first_side, pltpu.VMEM(heads.shape, heads.dtype)),
+        (row, row, array((1, 1), jnp.int32), late_lines, long_row, late_row),
+        (first_side, bias, first_side, pltpu.VMEM(heads.shape, heads.dtype), late_side),
         specs,
     )
     late = lay_out(late, home, (sums,))
@@ -816,7 +832,7 @@
         cross_late_kernel,
         lay,
         (
-            *(early, late, late_j, heads_i, lab_sub, late_sub_j, lane, lane_j),
+            *(early, late, late_j, heads_i, lab_sub, late_sub, lane_j),
             *(first_lane, sums, first_other, late_sums),
         ),
         (array((2 * n_owner, 1, capacity)),),

time: 81.9 us -> 81.9 us (level)
  transfers between devices with their start and end apart: 11 -> 11, of which waited for: 4 -> 4; matrix products, arithmetic and copies ran while one was open for 0% -> 0% of each run, Pallas kernels for 11% -> 12%
where the time goes in v27:
time: 81.9 us; the launch traced here: 81.6 us
  waiting for transfers between devices  42.9 us (52%)
  starting transfers between devices  21.9 us (27%)
  Pallas kernels  15.4 us (19%)
  between operations  0.83 us (1%)
    ppermute x6, waiting for transfers between devices, hop(): return lax.ppermute(x, 'cl', pairs)  27.3 us
    pallas_call x4, Pallas kernels, pair_call(): pl.pallas_call(functools.partial(kernel, lay), out_shape=out_shape, in_sp...  9.63 us
    all_to_all x1, waiting for transfers between devices, body(): lax.all_to_all(packed.reshape(n_owner, main, width), 'cl', split_axis=0,...  7.45 us
    ppermute x6, starting transfers between devices, hop(): return lax.ppermute(x, 'cl', pairs)  7.31 us
    all_to_all x1, starting transfers between devices, body(): lax.all_to_all(packed.reshape(n_owner, main, width), 'cl', split_axis=0,...  7.3 us
    all_to_all x1, starting transfers between devices, body(): lax.all_to_all(results, ('cl', 'grp'), split_axis=0, concat_axis=0, tiled...  6.74 us
    all_to_all x1, waiting for transfers between devices, body(): lax.all_to_all(results, ('cl', 'grp'), split_axis=0, concat_axis=0, tiled...  5.85 us
    pallas_call x1, Pallas kernels, place_rows(): pl.pallas_call(functools.partial(place_kernel, lay), out_shape=(jax.Shape...  5.2 us
  transfers between devices with their start and end apart: 11, of which 4 were waited for; matrix products, arithmetic and copies ran while one was open for 0% of the time, Pallas kernels for 12%

profile of v27, /device:TPU:0, one launch (start us, length us, event | category | flops | bytes accessed | tf_op | source)
XLA Modules:
  0.0 81.6 jit_solution(7661404634728922821)
XLA Ops:
  0.0 5.2 %shard_map.39 = (bf16[1152,768]{1,0:T(8,128)(2,1)}, bf16[1024,768]{1,0:T(8,128)(2,1)S(1)}, s32[1,1024]{1,0:T(1,128)S(1)}, s32[8,128]{1,0:T(8,128)S(1)}) custom-call(bf16[1024,768]{1,0:T(8,128)(2,1)} %x_hbm.1, s32[8,128]{1,0:T(8,128)} %bitcast.23, s32[1,64]{1,0:T(1,128)} %bitcast.27), custom_call_target="tpu_custom_call" | custom-call | tf_op jit(solution)/shard_map/pallas_call | solution.py:325
  5.2 7.3 %all-to-all-start.2 = ((bf16[8,144,768]{2,1,0:T(8,128)(2,1)}), bf16[8,144,768]{2,1,0:T(8,128)(2,1)S(1)}, u32[]{:S(2)}, u32[]{:S(2)}) async-start(bf16[8,144,768]{2,1,0:T(8,128)(2,1)} %bitcast.12), calls=%async_computation.2 | async-start | bytes 3538944 | tf_op jit(solution)/shard_map/all_to_all | solution.py:790
  12.5 0.4 shard_map.40.refs_2_.refs_0_
  12.9 0.7 collective-permute-start.4
  13.6 3.9 %collective-permute-start.1 = (bf16[128,768]{1,0:T(8,128)(2,1)S(1)}, bf16[128,768]{1,0:T(8,128)(2,1)S(1)}, u32[]{:S(2)}, u32[]{:S(2)}) collective-permute-start(bf16[128,768]{1,0:T(8,128)(2,1)S(1)} %shard_map.40.refs_2_.refs_0_), channel_id=1, source_target_pairs={{0,4},{1,5},{16,20},{17,21}} | collective-permute-start | bytes 589832 | tf_op jit(solution)/shard_map/ppermute | solution.py:782
  17.5 0.7 collective-permute-start.2
  18.2 0.7 collective-permute-start.3
  18.9 0.0 collective-permute-done.4.refs_1_
  19.0 27.3 %collective-permute-done.1.refs_0_ = bf16[128,768]{1,0:T(8,128)(2,1)S(1)} collective-permute-done((bf16[128,768]{1,0:T(8,128)(2,1)S(1)}, bf16[128,768]{1,0:T(8,128)(2,1)S(1)}, u32[]{:S(2)}, u32[]{:S(2)}) %collective-permute-start.1) | collective-permute-done | bytes 196640 | tf_op jit(solution)/shard_map/ppermute | solution.py:782
  46.3 0.0 collective-permute-done.2.refs_1_
  46.3 0.0 collective-permute-done.3.refs_3_
  46.3 7.4 %all-to-all-done.2 = bf16[8,144,768]{2,1,0:T(8,128)(2,1)S(1)} async-done(((bf16[8,144,768]{2,1,0:T(8,128)(2,1)}), bf16[8,144,768]{2,1,0:T(8,128)(2,1)S(1)}, u32[]{:S(2)}, u32[]{:S(2)}) %all-to-all-start.2) | async-done | bytes 1769504 | tf_op jit(solution)/shard_map/all_to_all | solution.py:790
  53.7 0.0 collective-permute-start.5
  53.7 0.5 collective-permute-start.6
  54.2 0.7 collective-permute-start.7
  54.9 0.7 collective-permute-start.8
  55.6 4.1 %shard_map.44 = (f32[1,1536]{1,0:T(1,128)S(1)}, f32[1,1536]{1,0:T(1,128)S(1)}, f32[1536,128]{1,0:T(8,128)S(1)}, bf16[1024,768]{1,0:T(8,128)(2,1)S(1)}) custom-call(bf16[1152,768]{1,0:T(8,128)(2,1)S(1)} %shard_map.43.mine, bf16[512,768]{1,0:T(8,128)(2,1)S(1)} %shard_map.41.refs_1_.early), custom_call_target="tpu_custom_call" | custom-call | bytes 1 | tf_op jit(solution)/shard_map/pallas_call | solution.py:714
  59.7 0.0 collective-permute-done.6.early_j
  59.7 0.0 collective-permute-done.5.other
  59.7 4.9 %shard_map.45 = (f32[1,1536]{1,0:T(1,128)S(1)}, f32[1,1536]{1,0:T(1,128)S(1)}, s32[1,1]{1,0:T(1,128)}, f32[512,128]{1,0:T(8,128)S(1)}, f32[1,2048]{1,0:T(1,128)S(1)}, /*index=5*/f32[1,512]{1,0:T(1,128)S(1)}) custom-call(bf16[1152,768]{1,0:T(8,128)(2,1)S(1)} %shard_map.43.mine, bf16[1152,768]{1,0:T(8,128)(2,1)S(1)} %collective-permute-done.5.other, ...), custom_call_target="tpu_custom_call" | custom-call | bytes 1 | tf_op jit(solution)/shard_map/pallas_call | solution.py:714
  64.6 0.0 collective-permute-done.7.refs_0_
  64.6 0.0 collective-permute-done.8.refs_1_
  64.6 0.1 collective-permute-start.9
  64.7 2.2 %collective-permute-done.9.late_j = bf16[512,768]{1,0:T(8,128)(2,1)S(1)} collective-permute-done((bf16[512,768]{1,0:T(8,128)(2,1)S(1)}, bf16[512,768]{1,0:T(8,128)(2,1)S(1)}, u32[]{:S(2)}, u32[]{:S(2)}) %collective-permute-start.9) | collective-permute-done | bytes 786464 | tf_op jit(solution)/shard_map/ppermute | solution.py:785
  67.0 0.0 copy-start.1
  67.0 0.0 copy-start.3
  67.0 0.0 copy-start.5
  67.0 0.7 shard_map.48
  67.7 6.7 %all-to-all-start.3 = ((f32[16,1,256]{2,1,0:T(1,128)}), f32[16,1,256]{2,1,0:T(1,128)S(1)}, u32[]{:S(2)}, u32[]{:S(2)}) async-start(f32[16,1,256]{2,1,0:T(1,128)} %shard_map.48), calls=%async_computation.3 | async-start | bytes 32768 | tf_op jit(solution)/shard_map/all_to_all | solution.py:841
  75.1 5.8 %all-to-all-done.3 = f32[16,1,256]{2,1,0:T(1,128)S(1)} async-done(((f32[16,1,256]{2,1,0:T(1,128)}), f32[16,1,256]{2,1,0:T(1,128)S(1)}, u32[]{:S(2)}, u32[]{:S(2)}) %all-to-all-start.3) | async-done | bytes 16416 | tf_op jit(solution)/shard_map/all_to_all | solution.py:841
  80.9 0.0 copy-done.1
  80.9 0.0 copy-done.3
  80.9 0.0 copy-done.5
  80.9 0.1 conditional.1
  80.9 0.1 branch_1_fun.1
  81.0 0.0 copy-start.4
  81.0 0.6 copy-done.4
  (5 shorter events, 0.1 us)
Async XLA Ops:
  5.2 48.5 %all-to-all-start.2 = ((bf16[8,144,768]{2,1,0:T(8,128)(2,1)}), bf16[8,144,768]{2,1,0:T(8,128)(2,1)S(1)}, u32[]{:S(2)}, u32[]{:S(2)}) async-start(bf16[8,144,768]{2,1,0:T(8,128)(2,1)} %bitcast.12), calls=%async_computation.2 | async-start | bytes 3538944 | tf_op jit(solution)/shard_map/all_to_all | solution.py:790
  12.9 6.0 %collective-permute-start.4 = (bf16[128,768]{1,0:T(8,128)(2,1)S(1)}, bf16[128,768]{1,0:T(8,128)(2,1)S(1)}, u32[]{:S(2)}, u32[]{:S(2)}) collective-permute-start(bf16[128,768]{1,0:T(8,128)(2,1)S(1)} %shard_map.40.refs_2_.refs_0_), channel_id=1, source_target_pairs={{12,8},{14,10},{13,9},{15,11},{28,24},{30,26},{29,25},{31,27}} | collective-permute-start | bytes 589832 | tf_op jit(solution)/shard_map/ppermute | solution.py:782
  13.6 32.7 %collective-permute-start.1 = (bf16[128,768]{1,0:T(8,128)(2,1)S(1)}, bf16[128,768]{1,0:T(8,128)(2,1)S(1)}, u32[]{:S(2)}, u32[]{:S(2)}) collective-permute-start(bf16[128,768]{1,0:T(8,128)(2,1)S(1)} %shard_map.40.refs_2_.refs_0_), channel_id=1, source_target_pairs={{0,4},{1,5},{16,20},{17,21}} | collective-permute-start | bytes 589832 | tf_op jit(solution)/shard_map/ppermute | solution.py:782
  17.5 28.7 %collective-permute-start.2 = (bf16[128,768]{1,0:T(8,128)(2,1)S(1)}, bf16[128,768]{1,0:T(8,128)(2,1)S(1)}, u32[]{:S(2)}, u32[]{:S(2)}) collective-permute-start(bf16[128,768]{1,0:T(8,128)(2,1)S(1)} %shard_map.40.refs_2_.refs_0_), channel_id=1, source_target_pairs={{2,4},{3,5},{18,20},{19,21}} | collective-permute-start | bytes 589832 | tf_op jit(solution)/shard_map/ppermute | solution.py:782
  18.2 28.0 %collective-permute-start.3 = (bf16[128,768]{1,0:T(8,128)(2,1)S(1)}, bf16[128,768]{1,0:T(8,128)(2,1)S(1)}, u32[]{:S(2)}, u32[]{:S(2)}) collective-permute-start(bf16[128,768]{1,0:T(8,128)(2,1)S(1)} %shard_map.40.refs_2_.refs_0_), channel_id=1, source_target_pairs={{6,4},{7,5},{22,20},{23,21}} | collective-permute-start | bytes 589832 | tf_op jit(solution)/shard_map/ppermute | solution.py:782
  53.7 6.0 %collective-permute-start.5 = (bf16[1152,768]{1,0:T(8,128)(2,1)S(1)}, bf16[1152,768]{1,0:T(8,128)(2,1)S(1)}, u32[]{:S(2)}, u32[]{:S(2)}) collective-permute-start(bf16[1152,768]{1,0:T(8,128)(2,1)S(1)} %shard_map.43.mine), channel_id=1, source_target_pairs={{0,1},{1,0},{2,3},{3,2},{4,5},{5,4},{6,7},{7,6},{8,9},{9,8},{10,11... | collective-permute-start | bytes 5308424 | tf_op jit(solution)/shard_map/ppermute | solution.py:785
  53.7 5.9 %collective-permute-start.6 = (bf16[512,768]{1,0:T(8,128)(2,1)S(1)}, bf16[512,768]{1,0:T(8,128)(2,1)S(1)}, u32[]{:S(2)}, u32[]{:S(2)}) collective-permute-start(bf16[512,768]{1,0:T(8,128)(2,1)S(1)} %shard_map.41.refs_1_.early), channel_id=1, source_target_pairs={{0,1},{1,0},{2,3},{3,2},{4,5},{5,4},{6,7},{7,6},{8,9},{9,8},{10,11... | collective-permute-start | bytes 2359304 | tf_op jit(solution)/shard_map/ppermute | solution.py:785
  54.2 10.3 %collective-permute-start.7 = (bf16[256,768]{1,0:T(8,128)(2,1)S(1)}, bf16[256,768]{1,0:T(8,128)(2,1)S(1)}, u32[]{:S(2)}, u32[]{:S(2)}) collective-permute-start(bf16[256,768]{1,0:T(8,128)(2,1)S(1)} %shard_map.42.refs_2_), channel_id=1, source_target_pairs={{10,4},{11,5},{26,20},{27,21}} | collective-permute-start | bytes 1179656 | tf_op jit(solution)/shard_map/ppermute | solution.py:782
  54.9 9.7 %collective-permute-start.8 = (bf16[256,768]{1,0:T(8,128)(2,1)S(1)}, bf16[256,768]{1,0:T(8,128)(2,1)S(1)}, u32[]{:S(2)}, u32[]{:S(2)}) collective-permute-start(bf16[256,768]{1,0:T(8,128)(2,1)S(1)} %shard_map.42.refs_2_), channel_id=1, source_target_pairs={{8,4},{9,5},{24,20},{25,21}} | collective-permute-start | bytes 1179656 | tf_op jit(solution)/shard_map/ppermute | solution.py:782
  64.6 2.4 %collective-permute-start.9 = (bf16[512,768]{1,0:T(8,128)(2,1)S(1)}, bf16[512,768]{1,0:T(8,128)(2,1)S(1)}, u32[]{:S(2)}, u32[]{:S(2)}) collective-permute-start(bf16[512,768]{1,0:T(8,128)(2,1)S(1)} %shard_map.46.late), channel_id=1, source_target_pairs={{0,1},{1,0},{2,3},{3,2},{4,5},{5,4},{6,7},{7,6},{8,9},{9,8},{10,11... | collective-permute-start | bytes 2359304 | tf_op jit(solution)/shard_map/ppermute | solution.py:785
  67.0 13.9 %copy-start.1 = (bf16[1024,768]{1,0:T(8,128)(2,1)S(1)}, bf16[1024,768]{1,0:T(8,128)(2,1)}, u32[]{:S(2)}) copy-start(bf16[1024,768]{1,0:T(8,128)(2,1)} %x_hbm.1) | copy-start | bytes 4718596
  67.0 13.9 %copy-start.3 = (s32[1024]{0:T(1024)S(1)}, s32[1024]{0:T(1024)}, u32[]{:S(2)}) copy-start(s32[1024]{0:T(1024)} %param.6) | copy-start | bytes 12292
  67.0 13.9 %copy-start.5 = (s32[64]{0:T(128)S(1)}, s32[64]{0:T(128)}, u32[]{:S(2)}) copy-start(s32[64]{0:T(128)} %param.7) | copy-start | bytes 772
  67.7 13.2 %all-to-all-start.3 = ((f32[16,1,256]{2,1,0:T(1,128)}), f32[16,1,256]{2,1,0:T(1,128)S(1)}, u32[]{:S(2)}, u32[]{:S(2)}) async-start(f32[16,1,256]{2,1,0:T(1,128)} %shard_map.48), calls=%async_computation.3 | async-start | bytes 32768 | tf_op jit(solution)/shard_map/all_to_all | solution.py:841
  81.0 0.6 copy-start.4

commit v28 on v25

--- a/solution.py
+++ b/solution.py
@@ -447,7 +447,7 @@
 
 def stream(lanes, tiles, lab_lane, buffers, put):
     rows_i, count, at = lanes
-    step = 32
+    step = 16
     tiles = [
         (ref, s, d, lab_sub, bias, line + s, back)
         for ref, n, lab_sub, bias, line, parts, back in tiles

time: 81.9 us -> 81.9 us (level)
  no operation moved by 1% of the time
where the time goes in v28:
time: 81.9 us; the launch traced here: 81.5 us
  waiting for transfers between devices  43.3 us (53%)
  starting transfers between devices  21.9 us (27%)
  Pallas kernels  14.9 us (18%)
  between operations  0.82 us (1%)
    ppermute x6, waiting for transfers between devices, hop(): return lax.ppermute(x, 'cl', pairs)  27.8 us
    pallas_call x4, Pallas kernels, pair_call(): pl.pallas_call(functools.partial(kernel, lay), out_shape=out_shape, in_sp...  9.5 us
    all_to_all x1, waiting for transfers between devices, body(): lax.all_to_all(packed.reshape(n_owner, main, width), 'cl', split_axis=0,...  7.44 us
    ppermute x6, starting transfers between devices, hop(): return lax.ppermute(x, 'cl', pairs)  7.3 us
    all_to_all x1, starting transfers between devices, body(): lax.all_to_all(packed.reshape(n_owner, main, width), 'cl', split_axis=0,...  7.29 us
    all_to_all x1, starting transfers between devices, body(): lax.all_to_all(results, ('cl', 'grp'), split_axis=0, concat_axis=0, tiled...  6.76 us
    all_to_all x1, waiting for transfers between devices, body(): lax.all_to_all(results, ('cl', 'grp'), split_axis=0, concat_axis=0, tiled...  5.85 us
    pallas_call x1, Pallas kernels, place_rows(): pl.pallas_call(functools.partial(place_kernel, lay), out_shape=(jax.Shape...  5.23 us
  transfers between devices with their start and end apart: 11, of which 4 were waited for; matrix products, arithmetic and copies ran while one was open for 0% of the time, Pallas kernels for 11%

profile of v28, /device:TPU:0, one launch (start us, length us, event | category | flops | bytes accessed | tf_op | source)
XLA Modules:
  0.0 81.5 jit_solution(12176724735713908931)
XLA Ops:
  0.0 5.2 %shard_map.39 = (bf16[1152,768]{1,0:T(8,128)(2,1)}, bf16[128,768]{1,0:T(8,128)(2,1)S(1)}, s32[8,128]{1,0:T(8,128)S(1)}) custom-call(bf16[1024,768]{1,0:T(8,128)(2,1)} %x_hbm.1, s32[8,128]{1,0:T(8,128)} %bitcast.23, s32[1,64]{1,0:T(1,128)} %bitcast.27), custom_call_target="tpu_custom_call" | custom-call | tf_op jit(solution)/shard_map/pallas_call | solution.py:311
  5.2 7.3 %all-to-all-start.2 = ((bf16[8,144,768]{2,1,0:T(8,128)(2,1)}), bf16[8,144,768]{2,1,0:T(8,128)(2,1)S(1)}, u32[]{:S(2)}, u32[]{:S(2)}) async-start(bf16[8,144,768]{2,1,0:T(8,128)(2,1)} %bitcast.12), calls=%async_computation.2 | async-start | bytes 3538944 | tf_op jit(solution)/shard_map/all_to_all | solution.py:774
  12.5 0.7 collective-permute-start.4
  13.2 3.9 %collective-permute-start.1 = (bf16[128,768]{1,0:T(8,128)(2,1)S(1)}, bf16[128,768]{1,0:T(8,128)(2,1)S(1)}, u32[]{:S(2)}, u32[]{:S(2)}) collective-permute-start(bf16[128,768]{1,0:T(8,128)(2,1)S(1)} %get-tuple-element.41.refs_2_.refs_0_), channel_id=1, source_target_pairs={{0,4},{1,5},{16,20},{17,21}} | collective-permute-start | bytes 589832 | tf_op jit(solution)/shard_map/ppermute | solution.py:766
  17.1 0.7 collective-permute-start.2
  17.8 0.7 collective-permute-start.3
  18.5 0.0 collective-permute-done.4.refs_1_
  18.6 27.7 %collective-permute-done.1.refs_0_ = bf16[128,768]{1,0:T(8,128)(2,1)S(1)} collective-permute-done((bf16[128,768]{1,0:T(8,128)(2,1)S(1)}, bf16[128,768]{1,0:T(8,128)(2,1)S(1)}, u32[]{:S(2)}, u32[]{:S(2)}) %collective-permute-start.1) | collective-permute-done | bytes 196640 | tf_op jit(solution)/shard_map/ppermute | solution.py:766
  46.3 0.0 collective-permute-done.2.refs_1_
  46.3 0.0 collective-permute-done.3.refs_3_
  46.3 7.4 %all-to-all-done.2 = bf16[8,144,768]{2,1,0:T(8,128)(2,1)S(1)} async-done(((bf16[8,144,768]{2,1,0:T(8,128)(2,1)}), bf16[8,144,768]{2,1,0:T(8,128)(2,1)S(1)}, u32[]{:S(2)}, u32[]{:S(2)}) %all-to-all-start.2) | async-done | bytes 1769504 | tf_op jit(solution)/shard_map/all_to_all | solution.py:774
  53.8 0.0 collective-permute-start.5
  53.8 0.5 collective-permute-start.6
  54.3 0.7 collective-permute-start.7
  54.9 0.7 collective-permute-start.8
  55.6 4.0 %shard_map.43 = (f32[1,1536]{1,0:T(1,128)S(1)}, f32[1,1536]{1,0:T(1,128)S(1)}, f32[1536,128]{1,0:T(8,128)S(1)}, bf16[1024,768]{1,0:T(8,128)(2,1)S(1)}) custom-call(bf16[1152,768]{1,0:T(8,128)(2,1)S(1)} %shard_map.42.mine, bf16[512,768]{1,0:T(8,128)(2,1)S(1)} %shard_map.40.refs_1_.early), custom_call_target="tpu_custom_call" | custom-call | bytes 1 | tf_op jit(solution)/shard_map/pallas_call | solution.py:699
  59.6 0.0 collective-permute-done.6.early_j
  59.6 0.0 collective-permute-done.5.other
  59.6 4.8 %shard_map.44 = (f32[1,1536]{1,0:T(1,128)S(1)}, f32[1,1536]{1,0:T(1,128)S(1)}, s32[1,1]{1,0:T(1,128)}, f32[512,128]{1,0:T(8,128)S(1)}, f32[512,128]{1,0:T(8,128)...) custom-call(bf16[1152,768]{1,0:T(8,128)(2,1)S(1)} %shard_map.42.mine, ...), custom_call_target="tpu_custom_call" | custom-call | bytes 1 | tf_op jit(solution)/shard_map/pallas_call | solution.py:699
  64.5 0.0 collective-permute-done.7.refs_0_
  64.5 0.0 collective-permute-done.8.refs_1_
  64.5 0.1 collective-permute-start.9
  64.6 2.2 %collective-permute-done.9.late_j = bf16[512,768]{1,0:T(8,128)(2,1)S(1)} collective-permute-done((bf16[512,768]{1,0:T(8,128)(2,1)S(1)}, bf16[512,768]{1,0:T(8,128)(2,1)S(1)}, u32[]{:S(2)}, u32[]{:S(2)}) %collective-permute-start.9) | collective-permute-done | bytes 786464 | tf_op jit(solution)/shard_map/ppermute | solution.py:769
  66.9 0.0 copy-start.1
  66.9 0.0 copy-start.3
  66.9 0.0 copy-start.5
  66.9 0.7 shard_map.47
  67.6 6.8 %all-to-all-start.3 = ((f32[16,1,256]{2,1,0:T(1,128)}), f32[16,1,256]{2,1,0:T(1,128)S(1)}, u32[]{:S(2)}, u32[]{:S(2)}) async-start(f32[16,1,256]{2,1,0:T(1,128)} %shard_map.47), calls=%async_computation.3 | async-start | bytes 32768 | tf_op jit(solution)/shard_map/all_to_all | solution.py:825
  75.0 5.8 %all-to-all-done.3 = f32[16,1,256]{2,1,0:T(1,128)S(1)} async-done(((f32[16,1,256]{2,1,0:T(1,128)}), f32[16,1,256]{2,1,0:T(1,128)S(1)}, u32[]{:S(2)}, u32[]{:S(2)}) %all-to-all-start.3) | async-done | bytes 16416 | tf_op jit(solution)/shard_map/all_to_all | solution.py:825
  80.8 0.0 copy-done.1
  80.8 0.0 copy-done.3
  80.8 0.0 copy-done.5
  80.8 0.1 conditional.1
  80.9 0.1 branch_1_fun.1
  81.0 0.0 copy-start.4
  81.0 0.6 copy-done.4
  (5 shorter events, 0.1 us)
Async XLA Ops:
  5.2 48.5 %all-to-all-start.2 = ((bf16[8,144,768]{2,1,0:T(8,128)(2,1)}), bf16[8,144,768]{2,1,0:T(8,128)(2,1)S(1)}, u32[]{:S(2)}, u32[]{:S(2)}) async-start(bf16[8,144,768]{2,1,0:T(8,128)(2,1)} %bitcast.12), calls=%async_computation.2 | async-start | bytes 3538944 | tf_op jit(solution)/shard_map/all_to_all | solution.py:774
  12.5 6.0 %collective-permute-start.4 = (bf16[128,768]{1,0:T(8,128)(2,1)S(1)}, bf16[128,768]{1,0:T(8,128)(2,1)S(1)}, u32[]{:S(2)}, u32[]{:S(2)}) collective-permute-start(bf16[128,768]{1,0:T(8,128)(2,1)S(1)} %get-tuple-element.41.refs_2_.refs_0_), channel_id=1, source_target_pairs={{12,8},{14,10},{13,9},{15,11},{28,24},{30,26},{29,25},{31,27}} | collective-permute-start | bytes 589832 | tf_op jit(solution)/shard_map/ppermute | solution.py:766
  13.2 33.1 %collective-permute-start.1 = (bf16[128,768]{1,0:T(8,128)(2,1)S(1)}, bf16[128,768]{1,0:T(8,128)(2,1)S(1)}, u32[]{:S(2)}, u32[]{:S(2)}) collective-permute-start(bf16[128,768]{1,0:T(8,128)(2,1)S(1)} %get-tuple-element.41.refs_2_.refs_0_), channel_id=1, source_target_pairs={{0,4},{1,5},{16,20},{17,21}} | collective-permute-start | bytes 589832 | tf_op jit(solution)/shard_map/ppermute | solution.py:766
  17.1 29.2 %collective-permute-start.2 = (bf16[128,768]{1,0:T(8,128)(2,1)S(1)}, bf16[128,768]{1,0:T(8,128)(2,1)S(1)}, u32[]{:S(2)}, u32[]{:S(2)}) collective-permute-start(bf16[128,768]{1,0:T(8,128)(2,1)S(1)} %get-tuple-element.41.refs_2_.refs_0_), channel_id=1, source_target_pairs={{2,4},{3,5},{18,20},{19,21}} | collective-permute-start | bytes 589832 | tf_op jit(solution)/shard_map/ppermute | solution.py:766
  17.8 28.5 %collective-permute-start.3 = (bf16[128,768]{1,0:T(8,128)(2,1)S(1)}, bf16[128,768]{1,0:T(8,128)(2,1)S(1)}, u32[]{:S(2)}, u32[]{:S(2)}) collective-permute-start(bf16[128,768]{1,0:T(8,128)(2,1)S(1)} %get-tuple-element.41.refs_2_.refs_0_), channel_id=1, source_target_pairs={{6,4},{7,5},{22,20},{23,21}} | collective-permute-start | bytes 589832 | tf_op jit(solution)/shard_map/ppermute | solution.py:766
  53.8 5.9 %collective-permute-start.5 = (bf16[1152,768]{1,0:T(8,128)(2,1)S(1)}, bf16[1152,768]{1,0:T(8,128)(2,1)S(1)}, u32[]{:S(2)}, u32[]{:S(2)}) collective-permute-start(bf16[1152,768]{1,0:T(8,128)(2,1)S(1)} %shard_map.42.mine), channel_id=1, source_target_pairs={{0,1},{1,0},{2,3},{3,2},{4,5},{5,4},{6,7},{7,6},{8,9},{9,8},{10,11... | collective-permute-start | bytes 5308424 | tf_op jit(solution)/shard_map/ppermute | solution.py:769
  53.8 5.9 %collective-permute-start.6 = (bf16[512,768]{1,0:T(8,128)(2,1)S(1)}, bf16[512,768]{1,0:T(8,128)(2,1)S(1)}, u32[]{:S(2)}, u32[]{:S(2)}) collective-permute-start(bf16[512,768]{1,0:T(8,128)(2,1)S(1)} %shard_map.40.refs_1_.early), channel_id=1, source_target_pairs={{0,1},{1,0},{2,3},{3,2},{4,5},{5,4},{6,7},{7,6},{8,9},{9,8},{10,11... | collective-permute-start | bytes 2359304 | tf_op jit(solution)/shard_map/ppermute | solution.py:769
  54.3 10.2 %collective-permute-start.7 = (bf16[256,768]{1,0:T(8,128)(2,1)S(1)}, bf16[256,768]{1,0:T(8,128)(2,1)S(1)}, u32[]{:S(2)}, u32[]{:S(2)}) collective-permute-start(bf16[256,768]{1,0:T(8,128)(2,1)S(1)} %shard_map.41.refs_2_), channel_id=1, source_target_pairs={{10,4},{11,5},{26,20},{27,21}} | collective-permute-start | bytes 1179656 | tf_op jit(solution)/shard_map/ppermute | solution.py:766
  54.9 9.5 %collective-permute-start.8 = (bf16[256,768]{1,0:T(8,128)(2,1)S(1)}, bf16[256,768]{1,0:T(8,128)(2,1)S(1)}, u32[]{:S(2)}, u32[]{:S(2)}) collective-permute-start(bf16[256,768]{1,0:T(8,128)(2,1)S(1)} %shard_map.41.refs_2_), channel_id=1, source_target_pairs={{8,4},{9,5},{24,20},{25,21}} | collective-permute-start | bytes 1179656 | tf_op jit(solution)/shard_map/ppermute | solution.py:766
  64.5 2.4 %collective-permute-start.9 = (bf16[512,768]{1,0:T(8,128)(2,1)S(1)}, bf16[512,768]{1,0:T(8,128)(2,1)S(1)}, u32[]{:S(2)}, u32[]{:S(2)}) collective-permute-start(bf16[512,768]{1,0:T(8,128)(2,1)S(1)} %shard_map.45.late), channel_id=1, source_target_pairs={{0,1},{1,0},{2,3},{3,2},{4,5},{5,4},{6,7},{7,6},{8,9},{9,8},{10,11... | collective-permute-start | bytes 2359304 | tf_op jit(solution)/shard_map/ppermute | solution.py:769
  66.9 14.0 %copy-start.1 = (bf16[1024,768]{1,0:T(8,128)(2,1)S(1)}, bf16[1024,768]{1,0:T(8,128)(2,1)}, u32[]{:S(2)}) copy-start(bf16[1024,768]{1,0:T(8,128)(2,1)} %x_hbm.1) | copy-start | bytes 4718596
  66.9 14.0 %copy-start.3 = (s32[1024]{0:T(1024)S(1)}, s32[1024]{0:T(1024)}, u32[]{:S(2)}) copy-start(s32[1024]{0:T(1024)} %param.6) | copy-start | bytes 12292
  66.9 14.0 %copy-start.5 = (s32[64]{0:T(128)S(1)}, s32[64]{0:T(128)}, u32[]{:S(2)}) copy-start(s32[64]{0:T(128)} %param.7) | copy-start | bytes 772
  67.6 13.3 %all-to-all-start.3 = ((f32[16,1,256]{2,1,0:T(1,128)}), f32[16,1,256]{2,1,0:T(1,128)S(1)}, u32[]{:S(2)}, u32[]{:S(2)}) async-start(f32[16,1,256]{2,1,0:T(1,128)} %shard_map.47), calls=%async_computation.3 | async-start | bytes 32768 | tf_op jit(solution)/shard_map/all_to_all | solution.py:825
  81.0 0.6 copy-start.4

commit v29 on v28

--- a/solution.py
+++ b/solution.py
@@ -630,10 +630,10 @@
         stream((mine, lay.n_main, 0), tiles, lab_lane, buffers, adder(total))
 
 
-def first_tiles(lay, rows, early, lab_sub, back):
+def first_tiles(lay, rows, early, lab_sub, back, size):
     return [
-        (rows, lay.n_head, lab_sub, None, 0, 4, back),
-        (early, lay.n_early, lab_sub, None, lay.n_head, 2, back),
+        (rows, lay.n_head, lab_sub, None, 0, lay.n_head // size, back),
+        (early, lay.n_early, lab_sub, None, lay.n_head, lay.n_early // size, back),
     ]
 
 
@@ -644,8 +644,8 @@
     def _():
         back[...] = jnp.zeros(back.shape, jnp.float32)
         sums[:, : lay.n_first] = jnp.zeros((1, lay.n_first), jnp.float32)
-        tiles = first_tiles(lay, rows, early, lab_sub, back)
-        tiles.append((late, lay.n_late, late_sub, None, 0, 2, None))
+        tiles = first_tiles(lay, rows, early, lab_sub, back, 512)
+        tiles.append((late, lay.n_late, late_sub, None, 0, 1, None))
         lanes = (late, lay.n_late, lay.n_first)
         stream(lanes, tiles, lab_lane, (buf_a, buf_b), setter(sums))
         turn_sums(back, lay.n_first, sums, 0)
@@ -664,7 +664,7 @@
         back[...] = jnp.zeros(back.shape, jnp.float32)
         late_back[...] = jnp.zeros(late_back.shape, jnp.float32)
         buffers = (buf_a, buf_b)
-        tiles = first_tiles(lay, rows, early, lab_sub, back)
+        tiles = first_tiles(lay, rows, early, lab_sub, back, 128)
         stream((late_j, lay.n_late, 0), tiles, late_lane, buffers, setter(late_other))
         turn_sums(back, lay.n_first, total, 0)
         put = adder(total)

time: 81.9 us -> 83.6 us (1.021)
  starting transfers between devices: 21.9 us -> 23.7 us
    all_to_all x1, starting transfers between devices: 6.76 us -> 8.54 us  [body(): lax.all_to_all(results, ('cl', 'grp'), split_axis=0, concat_axis=0, tiled...]
where the time goes in v29:
time: 83.6 us; the launch traced here: 83.3 us
  waiting for transfers between devices  43.3 us (52%)
  starting transfers between devices  23.7 us (28%)
  Pallas kernels  14.9 us (18%)
    ppermute x6, waiting for transfers between devices, hop(): return lax.ppermute(x, 'cl', pairs)  27.8 us
    pallas_call x4, Pallas kernels, pair_call(): pl.pallas_call(functools.partial(kernel, lay), out_shape=out_shape, in_sp...  9.5 us
    all_to_all x1, starting transfers between devices, body(): lax.all_to_all(results, ('cl', 'grp'), split_axis=0, concat_axis=0, tiled...  8.54 us
    all_to_all x1, waiting for transfers between devices, body(): lax.all_to_all(packed.reshape(n_owner, main, width), 'cl', split_axis=0,...  7.44 us
    ppermute x6, starting transfers between devices, hop(): return lax.ppermute(x, 'cl', pairs)  7.3 us
    all_to_all x1, starting transfers between devices, body(): lax.all_to_all(packed.reshape(n_owner, main, width), 'cl', split_axis=0,...  7.29 us
    all_to_all x1, waiting for transfers between devices, body(): lax.all_to_all(results, ('cl', 'grp'), split_axis=0, concat_axis=0, tiled...  5.85 us
    pallas_call x1, Pallas kernels, place_rows(): pl.pallas_call(functools.partial(place_kernel, lay), out_shape=(jax.Shape...  5.23 us
  transfers between devices with their start and end apart: 11, of which 4 were waited for; matrix products, arithmetic and copies ran while one was open for 0% of the time, Pallas kernels for 11%

profile of v29, /device:TPU:0, one launch (start us, length us, event | category | flops | bytes accessed | tf_op | source)
XLA Modules:
  0.0 83.3 jit_solution(2439983616368182817)
XLA Ops:
  0.0 5.2 %shard_map.39 = (bf16[1152,768]{1,0:T(8,128)(2,1)}, bf16[128,768]{1,0:T(8,128)(2,1)S(1)}, s32[8,128]{1,0:T(8,128)S(1)}) custom-call(bf16[1024,768]{1,0:T(8,128)(2,1)} %x_hbm.1, s32[8,128]{1,0:T(8,128)} %bitcast.23, s32[1,64]{1,0:T(1,128)} %bitcast.27), custom_call_target="tpu_custom_call" | custom-call | tf_op jit(solution)/shard_map/pallas_call | solution.py:311
  5.2 7.3 %all-to-all-start.2 = ((bf16[8,144,768]{2,1,0:T(8,128)(2,1)}), bf16[8,144,768]{2,1,0:T(8,128)(2,1)S(1)}, u32[]{:S(2)}, u32[]{:S(2)}) async-start(bf16[8,144,768]{2,1,0:T(8,128)(2,1)} %bitcast.12), calls=%async_computation.2 | async-start | bytes 3538944 | tf_op jit(solution)/shard_map/all_to_all | solution.py:774
  12.5 0.7 collective-permute-start.4
  13.2 3.9 %collective-permute-start.1 = (bf16[128,768]{1,0:T(8,128)(2,1)S(1)}, bf16[128,768]{1,0:T(8,128)(2,1)S(1)}, u32[]{:S(2)}, u32[]{:S(2)}) collective-permute-start(bf16[128,768]{1,0:T(8,128)(2,1)S(1)} %get-tuple-element.41.refs_2_.refs_0_), channel_id=1, source_target_pairs={{0,4},{1,5},{16,20},{17,21}} | collective-permute-start | bytes 589832 | tf_op jit(solution)/shard_map/ppermute | solution.py:766
  17.1 0.7 collective-permute-start.2
  17.8 0.7 collective-permute-start.3
  18.5 0.0 collective-permute-done.4.refs_1_
  18.6 27.7 %collective-permute-done.1.refs_0_ = bf16[128,768]{1,0:T(8,128)(2,1)S(1)} collective-permute-done((bf16[128,768]{1,0:T(8,128)(2,1)S(1)}, bf16[128,768]{1,0:T(8,128)(2,1)S(1)}, u32[]{:S(2)}, u32[]{:S(2)}) %collective-permute-start.1) | collective-permute-done | bytes 196640 | tf_op jit(solution)/shard_map/ppermute | solution.py:766
  46.3 0.0 collective-permute-done.2.refs_1_
  46.3 0.0 collective-permute-done.3.refs_3_
  46.3 7.4 %all-to-all-done.2 = bf16[8,144,768]{2,1,0:T(8,128)(2,1)S(1)} async-done(((bf16[8,144,768]{2,1,0:T(8,128)(2,1)}), bf16[8,144,768]{2,1,0:T(8,128)(2,1)S(1)}, u32[]{:S(2)}, u32[]{:S(2)}) %all-to-all-start.2) | async-done | bytes 1769504 | tf_op jit(solution)/shard_map/all_to_all | solution.py:774
  53.8 0.0 collective-permute-start.5
  53.8 0.5 collective-permute-start.6
  54.3 0.7 collective-permute-start.7
  54.9 0.7 collective-permute-start.8
  55.6 4.0 %shard_map.43 = (f32[1,1536]{1,0:T(1,128)S(1)}, f32[1,1536]{1,0:T(1,128)S(1)}, f32[1536,128]{1,0:T(8,128)S(1)}, bf16[1024,768]{1,0:T(8,128)(2,1)S(1)}) custom-call(bf16[1152,768]{1,0:T(8,128)(2,1)S(1)} %shard_map.42.mine, bf16[512,768]{1,0:T(8,128)(2,1)S(1)} %shard_map.40.refs_1_.early), custom_call_target="tpu_custom_call" | custom-call | bytes 1 | tf_op jit(solution)/shard_map/pallas_call | solution.py:699
  59.6 0.0 collective-permute-done.6.early_j
  59.6 0.0 collective-permute-done.5.other
  59.6 4.8 %shard_map.44 = (f32[1,1536]{1,0:T(1,128)S(1)}, f32[1,1536]{1,0:T(1,128)S(1)}, s32[1,1]{1,0:T(1,128)}, f32[512,128]{1,0:T(8,128)S(1)}, f32[512,128]{1,0:T(8,128)...) custom-call(bf16[1152,768]{1,0:T(8,128)(2,1)S(1)} %shard_map.42.mine, ...), custom_call_target="tpu_custom_call" | custom-call | bytes 1 | tf_op jit(solution)/shard_map/pallas_call | solution.py:699
  64.5 0.0 collective-permute-done.7.refs_0_
  64.5 0.0 collective-permute-done.8.refs_1_
  64.5 0.1 collective-permute-start.9
  64.6 2.2 %collective-permute-done.9.late_j = bf16[512,768]{1,0:T(8,128)(2,1)S(1)} collective-permute-done((bf16[512,768]{1,0:T(8,128)(2,1)S(1)}, bf16[512,768]{1,0:T(8,128)(2,1)S(1)}, u32[]{:S(2)}, u32[]{:S(2)}) %collective-permute-start.9) | collective-permute-done | bytes 786464 | tf_op jit(solution)/shard_map/ppermute | solution.py:769
  66.9 0.0 copy-start.1
  66.9 0.0 copy-start.3
  66.9 0.0 copy-start.5
  66.9 0.7 shard_map.47
  67.6 8.5 %all-to-all-start.3 = ((f32[16,1,256]{2,1,0:T(1,128)}), f32[16,1,256]{2,1,0:T(1,128)S(1)}, u32[]{:S(2)}, u32[]{:S(2)}) async-start(f32[16,1,256]{2,1,0:T(1,128)} %shard_map.47), calls=%async_computation.3 | async-start | bytes 32768 | tf_op jit(solution)/shard_map/all_to_all | solution.py:825
  76.8 5.8 %all-to-all-done.3 = f32[16,1,256]{2,1,0:T(1,128)S(1)} async-done(((f32[16,1,256]{2,1,0:T(1,128)}), f32[16,1,256]{2,1,0:T(1,128)S(1)}, u32[]{:S(2)}, u32[]{:S(2)}) %all-to-all-start.3) | async-done | bytes 16416 | tf_op jit(solution)/shard_map/all_to_all | solution.py:825
  82.6 0.0 copy-done.1
  82.6 0.0 copy-done.3
  82.6 0.0 copy-done.5
  82.6 0.1 conditional.1
  82.6 0.1 branch_1_fun.1
  82.7 0.0 copy-start.4
  82.7 0.6 copy-done.4
  (5 shorter events, 0.1 us)
Async XLA Ops:
  5.2 48.5 %all-to-all-start.2 = ((bf16[8,144,768]{2,1,0:T(8,128)(2,1)}), bf16[8,144,768]{2,1,0:T(8,128)(2,1)S(1)}, u32[]{:S(2)}, u32[]{:S(2)}) async-start(bf16[8,144,768]{2,1,0:T(8,128)(2,1)} %bitcast.12), calls=%async_computation.2 | async-start | bytes 3538944 | tf_op jit(solution)/shard_map/all_to_all | solution.py:774
  12.5 6.0 %collective-permute-start.4 = (bf16[128,768]{1,0:T(8,128)(2,1)S(1)}, bf16[128,768]{1,0:T(8,128)(2,1)S(1)}, u32[]{:S(2)}, u32[]{:S(2)}) collective-permute-start(bf16[128,768]{1,0:T(8,128)(2,1)S(1)} %get-tuple-element.41.refs_2_.refs_0_), channel_id=1, source_target_pairs={{12,8},{14,10},{13,9},{15,11},{28,24},{30,26},{29,25},{31,27}} | collective-permute-start | bytes 589832 | tf_op jit(solution)/shard_map/ppermute | solution.py:766
  13.2 33.1 %collective-permute-start.1 = (bf16[128,768]{1,0:T(8,128)(2,1)S(1)}, bf16[128,768]{1,0:T(8,128)(2,1)S(1)}, u32[]{:S(2)}, u32[]{:S(2)}) collective-permute-start(bf16[128,768]{1,0:T(8,128)(2,1)S(1)} %get-tuple-element.41.refs_2_.refs_0_), channel_id=1, source_target_pairs={{0,4},{1,5},{16,20},{17,21}} | collective-permute-start | bytes 589832 | tf_op jit(solution)/shard_map/ppermute | solution.py:766
  17.1 29.2 %collective-permute-start.2 = (bf16[128,768]{1,0:T(8,128)(2,1)S(1)}, bf16[128,768]{1,0:T(8,128)(2,1)S(1)}, u32[]{:S(2)}, u32[]{:S(2)}) collective-permute-start(bf16[128,768]{1,0:T(8,128)(2,1)S(1)} %get-tuple-element.41.refs_2_.refs_0_), channel_id=1, source_target_pairs={{2,4},{3,5},{18,20},{19,21}} | collective-permute-start | bytes 589832 | tf_op jit(solution)/shard_map/ppermute | solution.py:766
  17.8 28.5 %collective-permute-start.3 = (bf16[128,768]{1,0:T(8,128)(2,1)S(1)}, bf16[128,768]{1,0:T(8,128)(2,1)S(1)}, u32[]{:S(2)}, u32[]{:S(2)}) collective-permute-start(bf16[128,768]{1,0:T(8,128)(2,1)S(1)} %get-tuple-element.41.refs_2_.refs_0_), channel_id=1, source_target_pairs={{6,4},{7,5},{22,20},{23,21}} | collective-permute-start | bytes 589832 | tf_op jit(solution)/shard_map/ppermute | solution.py:766
  53.8 5.9 %collective-permute-start.5 = (bf16[1152,768]{1,0:T(8,128)(2,1)S(1)}, bf16[1152,768]{1,0:T(8,128)(2,1)S(1)}, u32[]{:S(2)}, u32[]{:S(2)}) collective-permute-start(bf16[1152,768]{1,0:T(8,128)(2,1)S(1)} %shard_map.42.mine), channel_id=1, source_target_pairs={{0,1},{1,0},{2,3},{3,2},{4,5},{5,4},{6,7},{7,6},{8,9},{9,8},{10,11... | collective-permute-start | bytes 5308424 | tf_op jit(solution)/shard_map/ppermute | solution.py:769
  53.8 5.9 %collective-permute-start.6 = (bf16[512,768]{1,0:T(8,128)(2,1)S(1)}, bf16[512,768]{1,0:T(8,128)(2,1)S(1)}, u32[]{:S(2)}, u32[]{:S(2)}) collective-permute-start(bf16[512,768]{1,0:T(8,128)(2,1)S(1)} %shard_map.40.refs_1_.early), channel_id=1, source_target_pairs={{0,1},{1,0},{2,3},{3,2},{4,5},{5,4},{6,7},{7,6},{8,9},{9,8},{10,11... | collective-permute-start | bytes 2359304 | tf_op jit(solution)/shard_map/ppermute | solution.py:769
  54.3 10.2 %collective-permute-start.7 = (bf16[256,768]{1,0:T(8,128)(2,1)S(1)}, bf16[256,768]{1,0:T(8,128)(2,1)S(1)}, u32[]{:S(2)}, u32[]{:S(2)}) collective-permute-start(bf16[256,768]{1,0:T(8,128)(2,1)S(1)} %shard_map.41.refs_2_), channel_id=1, source_target_pairs={{10,4},{11,5},{26,20},{27,21}} | collective-permute-start | bytes 1179656 | tf_op jit(solution)/shard_map/ppermute | solution.py:766
  54.9 9.5 %collective-permute-start.8 = (bf16[256,768]{1,0:T(8,128)(2,1)S(1)}, bf16[256,768]{1,0:T(8,128)(2,1)S(1)}, u32[]{:S(2)}, u32[]{:S(2)}) collective-permute-start(bf16[256,768]{1,0:T(8,128)(2,1)S(1)} %shard_map.41.refs_2_), channel_id=1, source_target_pairs={{8,4},{9,5},{24,20},{25,21}} | collective-permute-start | bytes 1179656 | tf_op jit(solution)/shard_map/ppermute | solution.py:766
  64.5 2.4 %collective-permute-start.9 = (bf16[512,768]{1,0:T(8,128)(2,1)S(1)}, bf16[512,768]{1,0:T(8,128)(2,1)S(1)}, u32[]{:S(2)}, u32[]{:S(2)}) collective-permute-start(bf16[512,768]{1,0:T(8,128)(2,1)S(1)} %shard_map.45.late), channel_id=1, source_target_pairs={{0,1},{1,0},{2,3},{3,2},{4,5},{5,4},{6,7},{7,6},{8,9},{9,8},{10,11... | collective-permute-start | bytes 2359304 | tf_op jit(solution)/shard_map/ppermute | solution.py:769
  66.9 15.7 %copy-start.1 = (bf16[1024,768]{1,0:T(8,128)(2,1)S(1)}, bf16[1024,768]{1,0:T(8,128)(2,1)}, u32[]{:S(2)}) copy-start(bf16[1024,768]{1,0:T(8,128)(2,1)} %x_hbm.1) | copy-start | bytes 4718596
  66.9 15.7 %copy-start.3 = (s32[1024]{0:T(1024)S(1)}, s32[1024]{0:T(1024)}, u32[]{:S(2)}) copy-start(s32[1024]{0:T(1024)} %param.6) | copy-start | bytes 12292
  66.9 15.7 %copy-start.5 = (s32[64]{0:T(128)S(1)}, s32[64]{0:T(128)}, u32[]{:S(2)}) copy-start(s32[64]{0:T(128)} %param.7) | copy-start | bytes 772
  67.6 15.0 %all-to-all-start.3 = ((f32[16,1,256]{2,1,0:T(1,128)}), f32[16,1,256]{2,1,0:T(1,128)S(1)}, u32[]{:S(2)}, u32[]{:S(2)}) async-start(f32[16,1,256]{2,1,0:T(1,128)} %shard_map.47), calls=%async_computation.3 | async-start | bytes 32768 | tf_op jit(solution)/shard_map/all_to_all | solution.py:825
  82.7 0.6 copy-start.4

commit v30 on v29

--- a/solution.py
+++ b/solution.py
@@ -664,7 +664,7 @@
         back[...] = jnp.zeros(back.shape, jnp.float32)
         late_back[...] = jnp.zeros(late_back.shape, jnp.float32)
         buffers = (buf_a, buf_b)
-        tiles = first_tiles(lay, rows, early, lab_sub, back, 128)
+        tiles = first_tiles(lay, rows, early, lab_sub, back, 512)
         stream((late_j, lay.n_late, 0), tiles, late_lane, buffers, setter(late_other))
         turn_sums(back, lay.n_first, total, 0)
         put = adder(total)

time: 83.6 us -> 81.9 us (0.980)
  starting transfers between devices: 23.7 us -> 22 us
    all_to_all x1, starting transfers between devices: 8.54 us -> 6.78 us  [body(): lax.all_to_all(results, ('cl', 'grp'), split_axis=0, concat_axis=0, tiled...]
where the time goes in v30:
time: 81.9 us; the launch traced here: 81.6 us
  waiting for transfers between devices  43.3 us (53%)
  starting transfers between devices  22 us (27%)
  Pallas kernels  14.9 us (18%)
  between operations  0.82 us (1%)
    ppermute x6, waiting for transfers between devices, hop(): return lax.ppermute(x, 'cl', pairs)  27.8 us
    pallas_call x4, Pallas kernels, pair_call(): pl.pallas_call(functools.partial(kernel, lay), out_shape=out_shape, in_sp...  9.5 us
    all_to_all x1, waiting for transfers between devices, body(): lax.all_to_all(packed.reshape(n_owner, main, width), 'cl', split_axis=0,...  7.44 us
    ppermute x6, starting transfers between devices, hop(): return lax.ppermute(x, 'cl', pairs)  7.3 us
    all_to_all x1, starting transfers between devices, body(): lax.all_to_all(packed.reshape(n_owner, main, width), 'cl', split_axis=0,...  7.29 us
    all_to_all x1, starting transfers between devices, body(): lax.all_to_all(results, ('cl', 'grp'), split_axis=0, concat_axis=0, tiled...  6.78 us
    all_to_all x1, waiting for transfers between devices, body(): lax.all_to_all(results, ('cl', 'grp'), split_axis=0, concat_axis=0, tiled...  5.85 us
    pallas_call x1, Pallas kernels, place_rows(): pl.pallas_call(functools.partial(place_kernel, lay), out_shape=(jax.Shape...  5.23 us
  transfers between devices with their start and end apart: 11, of which 4 were waited for; matrix products, arithmetic and copies ran while one was open for 0% of the time, Pallas kernels for 11%

profile of v30, /device:TPU:0, one launch (start us, length us, event | category | flops | bytes accessed | tf_op | source)
XLA Modules:
  0.0 81.6 jit_solution(15731882292426401908)
XLA Ops:
  0.0 5.2 %shard_map.39 = (bf16[1152,768]{1,0:T(8,128)(2,1)}, bf16[128,768]{1,0:T(8,128)(2,1)S(1)}, s32[8,128]{1,0:T(8,128)S(1)}) custom-call(bf16[1024,768]{1,0:T(8,128)(2,1)} %x_hbm.1, s32[8,128]{1,0:T(8,128)} %bitcast.23, s32[1,64]{1,0:T(1,128)} %bitcast.27), custom_call_target="tpu_custom_call" | custom-call | tf_op jit(solution)/shard_map/pallas_call | solution.py:311
  5.2 7.3 %all-to-all-start.2 = ((bf16[8,144,768]{2,1,0:T(8,128)(2,1)}), bf16[8,144,768]{2,1,0:T(8,128)(2,1)S(1)}, u32[]{:S(2)}, u32[]{:S(2)}) async-start(bf16[8,144,768]{2,1,0:T(8,128)(2,1)} %bitcast.12), calls=%async_computation.2 | async-start | bytes 3538944 | tf_op jit(solution)/shard_map/all_to_all | solution.py:774
  12.5 0.7 collective-permute-start.4
  13.2 3.9 %collective-permute-start.1 = (bf16[128,768]{1,0:T(8,128)(2,1)S(1)}, bf16[128,768]{1,0:T(8,128)(2,1)S(1)}, u32[]{:S(2)}, u32[]{:S(2)}) collective-permute-start(bf16[128,768]{1,0:T(8,128)(2,1)S(1)} %get-tuple-element.41.refs_2_.refs_0_), channel_id=1, source_target_pairs={{0,4},{1,5},{16,20},{17,21}} | collective-permute-start | bytes 589832 | tf_op jit(solution)/shard_map/ppermute | solution.py:766
  17.1 0.7 collective-permute-start.2
  17.8 0.7 collective-permute-start.3
  18.5 0.0 collective-permute-done.4.refs_1_
  18.6 27.7 %collective-permute-done.1.refs_0_ = bf16[128,768]{1,0:T(8,128)(2,1)S(1)} collective-permute-done((bf16[128,768]{1,0:T(8,128)(2,1)S(1)}, bf16[128,768]{1,0:T(8,128)(2,1)S(1)}, u32[]{:S(2)}, u32[]{:S(2)}) %collective-permute-start.1) | collective-permute-done | bytes 196640 | tf_op jit(solution)/shard_map/ppermute | solution.py:766
  46.3 0.0 collective-permute-done.2.refs_1_
  46.3 0.0 collective-permute-done.3.refs_3_
  46.3 7.4 %all-to-all-done.2 = bf16[8,144,768]{2,1,0:T(8,128)(2,1)S(1)} async-done(((bf16[8,144,768]{2,1,0:T(8,128)(2,1)}), bf16[8,144,768]{2,1,0:T(8,128)(2,1)S(1)}, u32[]{:S(2)}, u32[]{:S(2)}) %all-to-all-start.2) | async-done | bytes 1769504 | tf_op jit(solution)/shard_map/all_to_all | solution.py:774
  53.8 0.0 collective-permute-start.5
  53.8 0.5 collective-permute-start.6
  54.3 0.7 collective-permute-start.7
  54.9 0.7 collective-permute-start.8
  55.6 4.0 %shard_map.43 = (f32[1,1536]{1,0:T(1,128)S(1)}, f32[1,1536]{1,0:T(1,128)S(1)}, f32[1536,128]{1,0:T(8,128)S(1)}, bf16[1024,768]{1,0:T(8,128)(2,1)S(1)}) custom-call(bf16[1152,768]{1,0:T(8,128)(2,1)S(1)} %shard_map.42.mine, bf16[512,768]{1,0:T(8,128)(2,1)S(1)} %shard_map.40.refs_1_.early), custom_call_target="tpu_custom_call" | custom-call | bytes 1 | tf_op jit(solution)/shard_map/pallas_call | solution.py:699
  59.6 0.0 collective-permute-done.6.early_j
  59.6 0.0 collective-permute-done.5.other
  59.6 4.8 %shard_map.44 = (f32[1,1536]{1,0:T(1,128)S(1)}, f32[1,1536]{1,0:T(1,128)S(1)}, s32[1,1]{1,0:T(1,128)}, f32[512,128]{1,0:T(8,128)S(1)}, f32[512,128]{1,0:T(8,128)...) custom-call(bf16[1152,768]{1,0:T(8,128)(2,1)S(1)} %shard_map.42.mine, ...), custom_call_target="tpu_custom_call" | custom-call | bytes 1 | tf_op jit(solution)/shard_map/pallas_call | solution.py:699
  64.5 0.0 collective-permute-done.7.refs_0_
  64.5 0.0 collective-permute-done.8.refs_1_
  64.5 0.1 collective-permute-start.9
  64.6 2.2 %collective-permute-done.9.late_j = bf16[512,768]{1,0:T(8,128)(2,1)S(1)} collective-permute-done((bf16[512,768]{1,0:T(8,128)(2,1)S(1)}, bf16[512,768]{1,0:T(8,128)(2,1)S(1)}, u32[]{:S(2)}, u32[]{:S(2)}) %collective-permute-start.9) | collective-permute-done | bytes 786464 | tf_op jit(solution)/shard_map/ppermute | solution.py:769
  66.9 0.0 copy-start.1
  66.9 0.0 copy-start.3
  66.9 0.0 copy-start.5
  66.9 0.7 shard_map.47
  67.6 6.8 %all-to-all-start.3 = ((f32[16,1,256]{2,1,0:T(1,128)}), f32[16,1,256]{2,1,0:T(1,128)S(1)}, u32[]{:S(2)}, u32[]{:S(2)}) async-start(f32[16,1,256]{2,1,0:T(1,128)} %shard_map.47), calls=%async_computation.3 | async-start | bytes 32768 | tf_op jit(solution)/shard_map/all_to_all | solution.py:825
  75.0 5.8 %all-to-all-done.3 = f32[16,1,256]{2,1,0:T(1,128)S(1)} async-done(((f32[16,1,256]{2,1,0:T(1,128)}), f32[16,1,256]{2,1,0:T(1,128)S(1)}, u32[]{:S(2)}, u32[]{:S(2)}) %all-to-all-start.3) | async-done | bytes 16416 | tf_op jit(solution)/shard_map/all_to_all | solution.py:825
  80.8 0.0 copy-done.1
  80.8 0.0 copy-done.3
  80.8 0.0 copy-done.5
  80.8 0.1 conditional.1
  80.9 0.1 branch_1_fun.1
  81.0 0.0 copy-start.4
  81.0 0.6 copy-done.4
  (5 shorter events, 0.1 us)
Async XLA Ops:
  5.2 48.5 %all-to-all-start.2 = ((bf16[8,144,768]{2,1,0:T(8,128)(2,1)}), bf16[8,144,768]{2,1,0:T(8,128)(2,1)S(1)}, u32[]{:S(2)}, u32[]{:S(2)}) async-start(bf16[8,144,768]{2,1,0:T(8,128)(2,1)} %bitcast.12), calls=%async_computation.2 | async-start | bytes 3538944 | tf_op jit(solution)/shard_map/all_to_all | solution.py:774
  12.5 6.0 %collective-permute-start.4 = (bf16[128,768]{1,0:T(8,128)(2,1)S(1)}, bf16[128,768]{1,0:T(8,128)(2,1)S(1)}, u32[]{:S(2)}, u32[]{:S(2)}) collective-permute-start(bf16[128,768]{1,0:T(8,128)(2,1)S(1)} %get-tuple-element.41.refs_2_.refs_0_), channel_id=1, source_target_pairs={{12,8},{14,10},{13,9},{15,11},{28,24},{30,26},{29,25},{31,27}} | collective-permute-start | bytes 589832 | tf_op jit(solution)/shard_map/ppermute | solution.py:766
  13.2 33.1 %collective-permute-start.1 = (bf16[128,768]{1,0:T(8,128)(2,1)S(1)}, bf16[128,768]{1,0:T(8,128)(2,1)S(1)}, u32[]{:S(2)}, u32[]{:S(2)}) collective-permute-start(bf16[128,768]{1,0:T(8,128)(2,1)S(1)} %get-tuple-element.41.refs_2_.refs_0_), channel_id=1, source_target_pairs={{0,4},{1,5},{16,20},{17,21}} | collective-permute-start | bytes 589832 | tf_op jit(solution)/shard_map/ppermute | solution.py:766
  17.1 29.2 %collective-permute-start.2 = (bf16[128,768]{1,0:T(8,128)(2,1)S(1)}, bf16[128,768]{1,0:T(8,128)(2,1)S(1)}, u32[]{:S(2)}, u32[]{:S(2)}) collective-permute-start(bf16[128,768]{1,0:T(8,128)(2,1)S(1)} %get-tuple-element.41.refs_2_.refs_0_), channel_id=1, source_target_pairs={{2,4},{3,5},{18,20},{19,21}} | collective-permute-start | bytes 589832 | tf_op jit(solution)/shard_map/ppermute | solution.py:766
  17.8 28.5 %collective-permute-start.3 = (bf16[128,768]{1,0:T(8,128)(2,1)S(1)}, bf16[128,768]{1,0:T(8,128)(2,1)S(1)}, u32[]{:S(2)}, u32[]{:S(2)}) collective-permute-start(bf16[128,768]{1,0:T(8,128)(2,1)S(1)} %get-tuple-element.41.refs_2_.refs_0_), channel_id=1, source_target_pairs={{6,4},{7,5},{22,20},{23,21}} | collective-permute-start | bytes 589832 | tf_op jit(solution)/shard_map/ppermute | solution.py:766
  53.8 5.9 %collective-permute-start.5 = (bf16[1152,768]{1,0:T(8,128)(2,1)S(1)}, bf16[1152,768]{1,0:T(8,128)(2,1)S(1)}, u32[]{:S(2)}, u32[]{:S(2)}) collective-permute-start(bf16[1152,768]{1,0:T(8,128)(2,1)S(1)} %shard_map.42.mine), channel_id=1, source_target_pairs={{0,1},{1,0},{2,3},{3,2},{4,5},{5,4},{6,7},{7,6},{8,9},{9,8},{10,11... | collective-permute-start | bytes 5308424 | tf_op jit(solution)/shard_map/ppermute | solution.py:769
  53.8 5.9 %collective-permute-start.6 = (bf16[512,768]{1,0:T(8,128)(2,1)S(1)}, bf16[512,768]{1,0:T(8,128)(2,1)S(1)}, u32[]{:S(2)}, u32[]{:S(2)}) collective-permute-start(bf16[512,768]{1,0:T(8,128)(2,1)S(1)} %shard_map.40.refs_1_.early), channel_id=1, source_target_pairs={{0,1},{1,0},{2,3},{3,2},{4,5},{5,4},{6,7},{7,6},{8,9},{9,8},{10,11... | collective-permute-start | bytes 2359304 | tf_op jit(solution)/shard_map/ppermute | solution.py:769
  54.3 10.2 %collective-permute-start.7 = (bf16[256,768]{1,0:T(8,128)(2,1)S(1)}, bf16[256,768]{1,0:T(8,128)(2,1)S(1)}, u32[]{:S(2)}, u32[]{:S(2)}) collective-permute-start(bf16[256,768]{1,0:T(8,128)(2,1)S(1)} %shard_map.41.refs_2_), channel_id=1, source_target_pairs={{10,4},{11,5},{26,20},{27,21}} | collective-permute-start | bytes 1179656 | tf_op jit(solution)/shard_map/ppermute | solution.py:766
  54.9 9.5 %collective-permute-start.8 = (bf16[256,768]{1,0:T(8,128)(2,1)S(1)}, bf16[256,768]{1,0:T(8,128)(2,1)S(1)}, u32[]{:S(2)}, u32[]{:S(2)}) collective-permute-start(bf16[256,768]{1,0:T(8,128)(2,1)S(1)} %shard_map.41.refs_2_), channel_id=1, source_target_pairs={{8,4},{9,5},{24,20},{25,21}} | collective-permute-start | bytes 1179656 | tf_op jit(solution)/shard_map/ppermute | solution.py:766
  64.5 2.4 %collective-permute-start.9 = (bf16[512,768]{1,0:T(8,128)(2,1)S(1)}, bf16[512,768]{1,0:T(8,128)(2,1)S(1)}, u32[]{:S(2)}, u32[]{:S(2)}) collective-permute-start(bf16[512,768]{1,0:T(8,128)(2,1)S(1)} %shard_map.45.late), channel_id=1, source_target_pairs={{0,1},{1,0},{2,3},{3,2},{4,5},{5,4},{6,7},{7,6},{8,9},{9,8},{10,11... | collective-permute-start | bytes 2359304 | tf_op jit(solution)/shard_map/ppermute | solution.py:769
  66.9 14.0 %copy-start.1 = (bf16[1024,768]{1,0:T(8,128)(2,1)S(1)}, bf16[1024,768]{1,0:T(8,128)(2,1)}, u32[]{:S(2)}) copy-start(bf16[1024,768]{1,0:T(8,128)(2,1)} %x_hbm.1) | copy-start | bytes 4718596
  66.9 14.0 %copy-start.3 = (s32[1024]{0:T(1024)S(1)}, s32[1024]{0:T(1024)}, u32[]{:S(2)}) copy-start(s32[1024]{0:T(1024)} %param.6) | copy-start | bytes 12292
  66.9 14.0 %copy-start.5 = (s32[64]{0:T(128)S(1)}, s32[64]{0:T(128)}, u32[]{:S(2)}) copy-start(s32[64]{0:T(128)} %param.7) | copy-start | bytes 772
  67.6 13.3 %all-to-all-start.3 = ((f32[16,1,256]{2,1,0:T(1,128)}), f32[16,1,256]{2,1,0:T(1,128)S(1)}, u32[]{:S(2)}, u32[]{:S(2)}) async-start(f32[16,1,256]{2,1,0:T(1,128)} %shard_map.47), calls=%async_computation.3 | async-start | bytes 32768 | tf_op jit(solution)/shard_map/all_to_all | solution.py:825
  81.0 0.6 copy-start.4

commit v31 on v28

--- a/solution.py
+++ b/solution.py
@@ -825,9 +825,10 @@
     returned = lax.all_to_all(
         results, ("cl", "grp"), split_axis=0, concat_axis=0, tiled=True
     )
+    result = fast_unpack(returned, pos).reshape(rows)
     return lax.cond(
         unfit[0, 0] == 0,
-        lambda: fast_unpack(returned, pos).reshape(rows),
+        lambda: result,
         lambda: general(embeddings, labels, owner_map),
     )
 

time: 81.9 us -> 83.9 us (1.024)
  local copies, waits for them, and re-layouts: 0.6 us -> 1.79 us
    unnamed x8 -> x12, local copies, waits for them, and re-layouts: 0.6 us -> 1.79 us
where the time goes in v31:
time: 83.9 us; the launch traced here: 83.5 us
  waiting for transfers between devices  43.3 us (52%)
  starting transfers between devices  21.9 us (26%)
  Pallas kernels  15.6 us (19%)
  local copies, waits for them, and re-layouts  1.79 us (2%)
  between operations  0.9 us (1%)
    ppermute x6, waiting for transfers between devices, hop(): return lax.ppermute(x, 'cl', pairs)  27.8 us
    pallas_call x4, Pallas kernels, pair_call(): pl.pallas_call(functools.partial(kernel, lay), out_shape=out_shape, in_sp...  9.51 us
    all_to_all x1, waiting for transfers between devices, body(): lax.all_to_all(packed.reshape(n_owner, main, width), 'cl', split_axis=0,...  7.44 us
    ppermute x6, starting transfers between devices, hop(): return lax.ppermute(x, 'cl', pairs)  7.3 us
    all_to_all x1, starting transfers between devices, body(): lax.all_to_all(packed.reshape(n_owner, main, width), 'cl', split_axis=0,...  7.28 us
    all_to_all x1, starting transfers between devices, body(): lax.all_to_all(results, ('cl', 'grp'), split_axis=0, concat_axis=0, tiled...  6.76 us
    all_to_all x1, waiting for transfers between devices, body(): lax.all_to_all(results, ('cl', 'grp'), split_axis=0, concat_axis=0, tiled...  5.81 us
    pallas_call x1, Pallas kernels, place_rows(): pl.pallas_call(functools.partial(place_kernel, lay), out_shape=(jax.Shape...  5.23 us
  transfers between devices with their start and end apart: 11, of which 4 were waited for; matrix products, arithmetic and copies ran while one was open for 0% of the time, Pallas kernels for 11%

profile of v31, /device:TPU:0, one launch (start us, length us, event | category | flops | bytes accessed | tf_op | source)
XLA Modules:
  0.0 83.5 jit_solution(11187431988627173303)
XLA Ops:
  0.0 5.2 %shard_map.39 = (bf16[1152,768]{1,0:T(8,128)(2,1)}, bf16[128,768]{1,0:T(8,128)(2,1)S(1)}, s32[8,128]{1,0:T(8,128)S(1)}) custom-call(bf16[1024,768]{1,0:T(8,128)(2,1)} %x_hbm.1, s32[8,128]{1,0:T(8,128)} %bitcast.23, s32[1,64]{1,0:T(1,128)} %bitcast.27), custom_call_target="tpu_custom_call" | custom-call | tf_op jit(solution)/shard_map/pallas_call | solution.py:311
  5.2 0.0 copy-start
  5.2 0.6 copy-done
  5.8 7.3 %all-to-all-start.2 = ((bf16[8,144,768]{2,1,0:T(8,128)(2,1)}), bf16[8,144,768]{2,1,0:T(8,128)(2,1)S(1)}, u32[]{:S(2)}, u32[]{:S(2)}) async-start(bf16[8,144,768]{2,1,0:T(8,128)(2,1)} %bitcast.12), calls=%async_computation.2 | async-start | bytes 3538944 | tf_op jit(solution)/shard_map/all_to_all | solution.py:774
  13.1 0.7 collective-permute-start.4
  13.8 3.9 %collective-permute-start.1 = (bf16[128,768]{1,0:T(8,128)(2,1)S(1)}, bf16[128,768]{1,0:T(8,128)(2,1)S(1)}, u32[]{:S(2)}, u32[]{:S(2)}) collective-permute-start(bf16[128,768]{1,0:T(8,128)(2,1)S(1)} %get-tuple-element.38.refs_2_.refs_0_), channel_id=1, source_target_pairs={{0,4},{1,5},{16,20},{17,21}} | collective-permute-start | bytes 589832 | tf_op jit(solution)/shard_map/ppermute | solution.py:766
  17.7 0.7 collective-permute-start.2
  18.4 0.7 collective-permute-start.3
  19.1 0.0 collective-permute-done.4.refs_1_
  19.1 27.7 %collective-permute-done.1.refs_0_ = bf16[128,768]{1,0:T(8,128)(2,1)S(1)} collective-permute-done((bf16[128,768]{1,0:T(8,128)(2,1)S(1)}, bf16[128,768]{1,0:T(8,128)(2,1)S(1)}, u32[]{:S(2)}, u32[]{:S(2)}) %collective-permute-start.1) | collective-permute-done | bytes 196640 | tf_op jit(solution)/shard_map/ppermute | solution.py:766
  46.9 0.0 collective-permute-done.2.refs_1_
  46.9 0.0 collective-permute-done.3.refs_3_
  46.9 7.4 %all-to-all-done.2 = bf16[8,144,768]{2,1,0:T(8,128)(2,1)S(1)} async-done(((bf16[8,144,768]{2,1,0:T(8,128)(2,1)}), bf16[8,144,768]{2,1,0:T(8,128)(2,1)S(1)}, u32[]{:S(2)}, u32[]{:S(2)}) %all-to-all-start.2) | async-done | bytes 1769504 | tf_op jit(solution)/shard_map/all_to_all | solution.py:774
  54.3 0.0 collective-permute-start.5
  54.3 0.5 collective-permute-start.6
  54.8 0.7 collective-permute-start.7
  55.5 0.7 collective-permute-start.8
  56.2 4.0 %shard_map.43 = (f32[1,1536]{1,0:T(1,128)S(1)}, f32[1,1536]{1,0:T(1,128)S(1)}, f32[1536,128]{1,0:T(8,128)S(1)}, bf16[1024,768]{1,0:T(8,128)(2,1)S(1)}) custom-call(bf16[1152,768]{1,0:T(8,128)(2,1)S(1)} %shard_map.42.mine, bf16[512,768]{1,0:T(8,128)(2,1)S(1)} %shard_map.40.refs_1_.early), custom_call_target="tpu_custom_call" | custom-call | bytes 1 | tf_op jit(solution)/shard_map/pallas_call | solution.py:699
  60.2 0.0 collective-permute-done.6.early_j
  60.2 0.0 collective-permute-done.5.other
  60.2 4.8 %shard_map.44 = (f32[1,1536]{1,0:T(1,128)S(1)}, f32[1,1536]{1,0:T(1,128)S(1)}, s32[1,1]{1,0:T(1,128)}, f32[512,128]{1,0:T(8,128)S(1)}, f32[512,128]{1,0:T(8,128)...) custom-call(bf16[1152,768]{1,0:T(8,128)(2,1)S(1)} %shard_map.42.mine, ...), custom_call_target="tpu_custom_call" | custom-call | bytes 1 | tf_op jit(solution)/shard_map/pallas_call | solution.py:699
  65.1 0.0 collective-permute-done.7.refs_0_
  65.1 0.0 collective-permute-done.8.refs_1_
  65.1 0.1 collective-permute-start.9
  65.2 2.2 %collective-permute-done.9.late_j = bf16[512,768]{1,0:T(8,128)(2,1)S(1)} collective-permute-done((bf16[512,768]{1,0:T(8,128)(2,1)S(1)}, bf16[512,768]{1,0:T(8,128)(2,1)S(1)}, u32[]{:S(2)}, u32[]{:S(2)}) %collective-permute-start.9) | collective-permute-done | bytes 786464 | tf_op jit(solution)/shard_map/ppermute | solution.py:769
  67.5 0.0 copy-start.2
  67.5 0.0 copy-start.5
  67.5 0.0 copy-start.7
  67.5 0.7 shard_map.47
  68.1 6.8 %all-to-all-start.3 = ((f32[16,1,256]{2,1,0:T(1,128)}), f32[16,1,256]{2,1,0:T(1,128)S(1)}, u32[]{:S(2)}, u32[]{:S(2)}) async-start(f32[16,1,256]{2,1,0:T(1,128)} %shard_map.47), calls=%async_computation.3 | async-start | bytes 32768 | tf_op jit(solution)/shard_map/all_to_all | solution.py:825
  75.6 5.8 %all-to-all-done.3.values_ref = f32[16,1,256]{2,1,0:T(1,128)S(1)} async-done(((f32[16,1,256]{2,1,0:T(1,128)}), f32[16,1,256]{2,1,0:T(1,128)S(1)}, u32[]{:S(2)}, u32[]{:S(2)}) %all-to-all-start.3) | async-done | bytes 16416 | tf_op jit(solution)/shard_map/all_to_all | solution.py:825
  81.4 0.0 copy-start.4
  81.4 0.6 copy-done.4
  82.0 0.8 shard_map.48
  82.8 0.0 copy-done.2
  82.8 0.0 copy-done.5
  82.8 0.0 copy-done.7
  82.9 0.0 copy-start.6
  82.9 0.6 copy-done.6
  (6 shorter events, 0.1 us)
Async XLA Ops:
  5.2 0.6 copy-start
  5.8 48.5 %all-to-all-start.2 = ((bf16[8,144,768]{2,1,0:T(8,128)(2,1)}), bf16[8,144,768]{2,1,0:T(8,128)(2,1)S(1)}, u32[]{:S(2)}, u32[]{:S(2)}) async-start(bf16[8,144,768]{2,1,0:T(8,128)(2,1)} %bitcast.12), calls=%async_computation.2 | async-start | bytes 3538944 | tf_op jit(solution)/shard_map/all_to_all | solution.py:774
  13.1 6.0 %collective-permute-start.4 = (bf16[128,768]{1,0:T(8,128)(2,1)S(1)}, bf16[128,768]{1,0:T(8,128)(2,1)S(1)}, u32[]{:S(2)}, u32[]{:S(2)}) collective-permute-start(bf16[128,768]{1,0:T(8,128)(2,1)S(1)} %get-tuple-element.38.refs_2_.refs_0_), channel_id=1, source_target_pairs={{12,8},{14,10},{13,9},{15,11},{28,24},{30,26},{29,25},{31,27}} | collective-permute-start | bytes 589832 | tf_op jit(solution)/shard_map/ppermute | solution.py:766
  13.8 33.1 %collective-permute-start.1 = (bf16[128,768]{1,0:T(8,128)(2,1)S(1)}, bf16[128,768]{1,0:T(8,128)(2,1)S(1)}, u32[]{:S(2)}, u32[]{:S(2)}) collective-permute-start(bf16[128,768]{1,0:T(8,128)(2,1)S(1)} %get-tuple-element.38.refs_2_.refs_0_), channel_id=1, source_target_pairs={{0,4},{1,5},{16,20},{17,21}} | collective-permute-start | bytes 589832 | tf_op jit(solution)/shard_map/ppermute | solution.py:766
  17.7 29.2 %collective-permute-start.2 = (bf16[128,768]{1,0:T(8,128)(2,1)S(1)}, bf16[128,768]{1,0:T(8,128)(2,1)S(1)}, u32[]{:S(2)}, u32[]{:S(2)}) collective-permute-start(bf16[128,768]{1,0:T(8,128)(2,1)S(1)} %get-tuple-element.38.refs_2_.refs_0_), channel_id=1, source_target_pairs={{2,4},{3,5},{18,20},{19,21}} | collective-permute-start | bytes 589832 | tf_op jit(solution)/shard_map/ppermute | solution.py:766
  18.4 28.5 %collective-permute-start.3 = (bf16[128,768]{1,0:T(8,128)(2,1)S(1)}, bf16[128,768]{1,0:T(8,128)(2,1)S(1)}, u32[]{:S(2)}, u32[]{:S(2)}) collective-permute-start(bf16[128,768]{1,0:T(8,128)(2,1)S(1)} %get-tuple-element.38.refs_2_.refs_0_), channel_id=1, source_target_pairs={{6,4},{7,5},{22,20},{23,21}} | collective-permute-start | bytes 589832 | tf_op jit(solution)/shard_map/ppermute | solution.py:766
  54.3 5.9 %collective-permute-start.5 = (bf16[1152,768]{1,0:T(8,128)(2,1)S(1)}, bf16[1152,768]{1,0:T(8,128)(2,1)S(1)}, u32[]{:S(2)}, u32[]{:S(2)}) collective-permute-start(bf16[1152,768]{1,0:T(8,128)(2,1)S(1)} %shard_map.42.mine), channel_id=1, source_target_pairs={{0,1},{1,0},{2,3},{3,2},{4,5},{5,4},{6,7},{7,6},{8,9},{9,8},{10,11... | collective-permute-start | bytes 5308424 | tf_op jit(solution)/shard_map/ppermute | solution.py:769
  54.3 5.9 %collective-permute-start.6 = (bf16[512,768]{1,0:T(8,128)(2,1)S(1)}, bf16[512,768]{1,0:T(8,128)(2,1)S(1)}, u32[]{:S(2)}, u32[]{:S(2)}) collective-permute-start(bf16[512,768]{1,0:T(8,128)(2,1)S(1)} %shard_map.40.refs_1_.early), channel_id=1, source_target_pairs={{0,1},{1,0},{2,3},{3,2},{4,5},{5,4},{6,7},{7,6},{8,9},{9,8},{10,11... | collective-permute-start | bytes 2359304 | tf_op jit(solution)/shard_map/ppermute | solution.py:769
  54.8 10.2 %collective-permute-start.7 = (bf16[256,768]{1,0:T(8,128)(2,1)S(1)}, bf16[256,768]{1,0:T(8,128)(2,1)S(1)}, u32[]{:S(2)}, u32[]{:S(2)}) collective-permute-start(bf16[256,768]{1,0:T(8,128)(2,1)S(1)} %shard_map.41.refs_2_), channel_id=1, source_target_pairs={{10,4},{11,5},{26,20},{27,21}} | collective-permute-start | bytes 1179656 | tf_op jit(solution)/shard_map/ppermute | solution.py:766
  55.5 9.5 %collective-permute-start.8 = (bf16[256,768]{1,0:T(8,128)(2,1)S(1)}, bf16[256,768]{1,0:T(8,128)(2,1)S(1)}, u32[]{:S(2)}, u32[]{:S(2)}) collective-permute-start(bf16[256,768]{1,0:T(8,128)(2,1)S(1)} %shard_map.41.refs_2_), channel_id=1, source_target_pairs={{8,4},{9,5},{24,20},{25,21}} | collective-permute-start | bytes 1179656 | tf_op jit(solution)/shard_map/ppermute | solution.py:766
  65.1 2.4 %collective-permute-start.9 = (bf16[512,768]{1,0:T(8,128)(2,1)S(1)}, bf16[512,768]{1,0:T(8,128)(2,1)S(1)}, u32[]{:S(2)}, u32[]{:S(2)}) collective-permute-start(bf16[512,768]{1,0:T(8,128)(2,1)S(1)} %shard_map.45.late), channel_id=1, source_target_pairs={{0,1},{1,0},{2,3},{3,2},{4,5},{5,4},{6,7},{7,6},{8,9},{9,8},{10,11... | collective-permute-start | bytes 2359304 | tf_op jit(solution)/shard_map/ppermute | solution.py:769
  67.5 15.4 %copy-start.2 = (bf16[1024,768]{1,0:T(8,128)(2,1)S(1)}, bf16[1024,768]{1,0:T(8,128)(2,1)}, u32[]{:S(2)}) copy-start(bf16[1024,768]{1,0:T(8,128)(2,1)} %x_hbm.1) | copy-start | bytes 4718596
  67.5 15.4 %copy-start.5 = (s32[1024]{0:T(1024)S(1)}, s32[1024]{0:T(1024)}, u32[]{:S(2)}) copy-start(s32[1024]{0:T(1024)} %param.6) | copy-start | bytes 12292
  67.5 15.4 %copy-start.7 = (s32[64]{0:T(128)S(1)}, s32[64]{0:T(128)}, u32[]{:S(2)}) copy-start(s32[64]{0:T(128)} %param.7) | copy-start | bytes 772
  68.1 13.3 %all-to-all-start.3 = ((f32[16,1,256]{2,1,0:T(1,128)}), f32[16,1,256]{2,1,0:T(1,128)S(1)}, u32[]{:S(2)}, u32[]{:S(2)}) async-start(f32[16,1,256]{2,1,0:T(1,128)} %shard_map.47), calls=%async_computation.3 | async-start | bytes 32768 | tf_op jit(solution)/shard_map/all_to_all | solution.py:825
  81.4 0.6 copy-start.4
  82.9 0.6 copy-start.6
